TPU v7x, 32 devices: a whole 2x2x4 slice. The times are simulated.
32 devices in a mesh: ctx: 2 (over y), tile: 4 (over z), mp: 4 (over x, core).
Axes of the slice: x: 2, y: 2, z: 4, core: 2. Of those that a mesh axis runs over, the one named last changes fastest.
Arguments:
- text_embed: bfloat16 [2048, 4096], P('ctx', ('tile', 'mp')), may hold values from -6 to 6
- latents: bfloat16 [4, 64, 512], P('ctx', 'tile'), may hold values from -6 to 6
- down_conv: bfloat16 [72, 256], P(None, 'mp'), may hold values from -0.75 to 0.75
- patch_in: bfloat16 [4096, 4096], P(None, ('tile', 'mp')), may hold values from -0.09375 to 0.09375
- norm_gain: bfloat16 [4096], P(('tile', 'mp')), may hold values from 0.25 to 1.75
- query_weight: bfloat16 [4096, 4096], P(None, ('tile', 'mp')), may hold values from -0.09375 to 0.09375
- key_weight: bfloat16 [4096, 4096], P(None, ('tile', 'mp')), may hold values from -0.09375 to 0.09375
- value_weight: bfloat16 [4096, 4096], P(None, ('tile', 'mp')), may hold values from -0.09375 to 0.09375
- query_gain: float32 [128], replicated, may hold values from 0.5 to 6
- key_gain: float32 [128], replicated, may hold values from 0.5 to 6
- out_weight: bfloat16 [4096, 4096], P(None, ('tile', 'mp')), may hold values from -0.5 to 0.5
- patch_out: bfloat16 [4096, 4096], P(('tile', 'mp')), may hold values from -0.09375 to 0.09375
- up_conv: bfloat16 [2304, 8], replicated, may hold values from -0.125 to 0.125
- span_start: int32 [4], replicated, may hold values from 0 to 1792, as said below
- image_of_slot: int32 [4], replicated, may hold values from 0 to 3, each once
Outputs:
- layer_out: bfloat16 [2048, 4096], P('ctx', ('tile', 'mp'))
- noise_pred: float32 [4, 64, 512], P('ctx', 'tile')
Inputs may be any that keep to these rules, and one draw needn't show every extreme that they name: `span_start`: sorted ascending; each image spans 256 positions, spans do not intersect, the first image starts the document and the last one ends it; spans may cross the boundaries between indices of ctx. `image_of_slot`: each image appears in exactly one slot.
All inputs are finite; a program needn't handle non-finite values.
Results may differ from a plain program's by a relative error of at most 0.04.
Values may be sent and summed in bfloat16 or wider, within the bound.
No kernel may reach another device: no remote copies, remote signals or barrier semaphores. Data moves between devices by JAX's collectives and lax.ppermute only.
A program may use at most 128 MiB of HBM per device.

v0:
```python
import jax
import jax.numpy as jnp
from jax import lax
from jax.sharding import PartitionSpec as P

HD = 128
CH = 256
CIN = 8
WL = 64
PATCH = 4
IMG_TOK = 256


EPSILON = 1e-05
NEGATIVE_FILL = -1e30


def padded_2(block, sides, width):
    for axis, dim in sides:
        count = lax.axis_size(axis)
        forward = [(i, i + 1) for i in range(count - 1)]
        backward = [(target, source) for source, target in forward]
        low = lax.ppermute(
            lax.slice_in_dim(block, block.shape[dim] - width, None, axis=dim), axis, forward
        )
        high = lax.ppermute(lax.slice_in_dim(block, 0, width, axis=dim), axis, backward)
        block = jnp.concatenate([low, block, high], axis=dim)
    return block


def rms_scale(values):
    return lax.rsqrt(jnp.mean(values * values, axis=-1, keepdims=True) + EPSILON)


def conv_rows(padded, weight):
    images, padded_height, breadth, channels_in = padded.shape
    height = padded_height - 2
    widened = jnp.pad(padded, ((0, 0), (0, 0), (1, 1), (0, 0)))
    taps = [
        widened[:, row_shift : row_shift + height, col_shift : col_shift + breadth, :]
        for row_shift in range(3)
        for col_shift in range(3)
    ]
    stacked = jnp.concatenate(taps, axis=-1).reshape(images * height * breadth, 9 * channels_in)
    result = jnp.dot(stacked, weight, preferred_element_type=jnp.float32)
    return result.reshape(images, height, breadth, weight.shape[1])


def image_ids(positions, span_start):
    inside = (positions[:, None] >= span_start[None, :]) & (
        positions[:, None] < span_start[None, :] + IMG_TOK
    )
    numbers = jnp.arange(span_start.shape[0], dtype=jnp.int32)
    return jnp.sum(jnp.where(inside, numbers[None, :] + 1, 0), axis=1) - 1


def slot_lookup(image_of_slot):
    numbers = jnp.arange(image_of_slot.shape[0], dtype=jnp.int32)
    matches = image_of_slot[None, :] == numbers[:, None]
    return jnp.sum(jnp.where(matches, numbers[None, :], 0), axis=1)


def shards(
    text_embed,
    latents,
    down_conv,
    patch_in,
    norm_gain,
    query_weight,
    key_weight,
    value_weight,
    query_gain,
    key_gain,
    out_weight,
    patch_out,
    up_conv,
    span_start,
    image_of_slot,
):
    mp_count = lax.axis_size("mp")
    ctx_index = lax.axis_index("ctx")
    seq_rows, slice_width = text_embed.shape
    local_images, band_height, row_width = latents.shape
    image_count = span_start.shape[0]
    quarter_channels = down_conv.shape[1]
    image = latents.reshape(local_images, band_height, WL, CIN)
    padded = padded_2(image, (("tile", 1),), 1)
    activated = jax.nn.silu(conv_rows(padded, down_conv)).astype(jnp.bfloat16)
    band_patches = band_height // PATCH * (WL // PATCH)
    patches = activated.reshape(
        local_images, band_height // PATCH, PATCH, WL // PATCH, PATCH, quarter_channels
    )
    patches = patches.transpose(0, 1, 3, 2, 4, 5).reshape(
        local_images, band_patches, PATCH * PATCH * quarter_channels
    )
    split_in = patch_in.reshape(PATCH * PATCH, mp_count, quarter_channels, slice_width)
    tokens_init = jnp.zeros((local_images, IMG_TOK, slice_width), jnp.float32)
    shard_part = lax.all_gather(patches[None], ("tile", "mp"), axis=0, tiled=True)

    def one_shard(offset, inner):
        weight = lax.dynamic_index_in_dim(split_in, offset % mp_count, 1, keepdims=False)
        weight = weight.reshape(PATCH * PATCH * quarter_channels, slice_width)
        single = lax.dynamic_index_in_dim(shard_part, offset, 0, keepdims=False)
        term = jnp.einsum("ipf,fd->ipd", single, weight, preferred_element_type=jnp.float32)
        row_offset = offset // mp_count * band_patches
        current = lax.dynamic_slice_in_dim(inner, row_offset, band_patches, 1)
        return lax.dynamic_update_slice_in_dim(inner, current + term, row_offset, 1)

    image_tokens = lax.fori_loop(0, shard_part.shape[0], one_shard, tokens_init).astype(
        jnp.bfloat16
    )
    every_token = lax.all_gather(
        image_tokens.reshape(local_images * IMG_TOK, slice_width), "ctx", axis=0, tiled=True
    )
    positions = ctx_index * seq_rows + jnp.arange(seq_rows, dtype=jnp.int32)
    owners = image_ids(positions, span_start)
    safe_owner = jnp.maximum(owners, 0)
    slot_table = slot_lookup(image_of_slot)
    owner_start = jnp.take(span_start, safe_owner)
    source_rows = jnp.take(slot_table, safe_owner) * IMG_TOK + positions - owner_start
    source_rows = jnp.clip(source_rows, 0, image_count * IMG_TOK - 1)
    stream = jnp.where(
        (owners >= 0)[:, None], jnp.take(every_token, source_rows, axis=0), text_embed
    )
    gain_row = norm_gain.reshape(1, slice_width)
    work_owners = image_ids(positions, span_start)
    whole, gain_whole = (
        lax.all_gather(stream, ("tile", "mp"), axis=1, tiled=True),
        lax.all_gather(gain_row, ("tile", "mp"), axis=1, tiled=True),
    )
    widened = whole.astype(jnp.float32)
    normed = (widened * rms_scale(widened) * gain_whole.astype(jnp.float32)).astype(jnp.bfloat16)
    query_raw = jnp.dot(normed, query_weight, preferred_element_type=jnp.float32)
    key_raw = jnp.dot(normed, key_weight, preferred_element_type=jnp.float32)
    value_raw = jnp.dot(normed, value_weight, preferred_element_type=jnp.float32)
    heads_here = query_weight.shape[1] // HD

    def head_norm(raw, gain, factor):
        shaped = raw.reshape(seq_rows, heads_here, HD)
        return (shaped * rms_scale(shaped) * gain * factor).astype(jnp.bfloat16)

    queries = head_norm(query_raw, query_gain, HD ** (-0.5))
    key_rows = head_norm(key_raw, key_gain, 1.0)
    value_rows = value_raw.astype(jnp.bfloat16).reshape(seq_rows, heads_here, HD)
    fold_shard_part = (
        lax.all_gather(key_rows, "ctx", axis=0, tiled=True),
        lax.all_gather(value_rows, "ctx", axis=0, tiled=True),
    )
    key_positions = jnp.arange(fold_shard_part[0].shape[0], dtype=jnp.int32)
    key_part, value_part = fold_shard_part
    key_owners = image_ids(key_positions, span_start)
    visible = (key_positions[None, :] <= positions[:, None]) | (
        key_owners[None, :] == work_owners[:, None]
    ) & (work_owners[:, None] >= 0)
    scores = jnp.einsum("qhd,khd->qhk", queries, key_part, preferred_element_type=jnp.float32)
    scores = jnp.where(visible[:, None, :], scores, NEGATIVE_FILL)
    old_top = jnp.full((seq_rows, heads_here), NEGATIVE_FILL, jnp.float32)
    new_top = jnp.maximum(old_top, jnp.max(scores, axis=2))
    weights = jnp.where(visible[:, None, :], jnp.exp(scores - new_top[:, :, None]), 0.0)
    factor = jnp.exp(old_top - new_top)
    new_sum = jnp.sum(weights, axis=2)
    product = jnp.einsum(
        "qhk,khd->qhd", weights.astype(jnp.bfloat16), value_part, preferred_element_type=jnp.float32
    )
    attended = (
        (product / new_sum[:, :, None]).astype(jnp.bfloat16).reshape(seq_rows, heads_here * HD)
    )
    rows_used = out_weight
    mixed = jnp.dot(
        lax.all_gather(attended, ("tile", "mp"), axis=1, tiled=True),
        rows_used,
        preferred_element_type=jnp.float32,
    )
    work_out = (stream.astype(jnp.float32) + mixed).astype(jnp.bfloat16)
    every_row = lax.all_gather(work_out, "ctx", axis=0, tiled=True)
    slots = ctx_index * local_images + jnp.arange(local_images, dtype=jnp.int32)
    starts = jnp.take(span_start, jnp.take(image_of_slot, slots))
    picked = jax.vmap(
        lambda first_token: lax.dynamic_slice_in_dim(every_row, first_token, IMG_TOK, 0)
    )(starts)
    patch_major = picked.transpose(1, 0, 2).reshape(IMG_TOK * local_images, slice_width)
    rows_used = patch_major
    own_rows = lax.psum_scatter(
        jnp.dot(rows_used, patch_out, preferred_element_type=jnp.float32).astype(jnp.bfloat16),
        ("tile", "mp"),
        scatter_dimension=0,
        tiled=True,
    ).astype(jnp.float32)
    own_active = jax.nn.silu(own_rows).astype(jnp.bfloat16)
    band = lax.all_gather(own_active, "mp", axis=0, tiled=True)
    pixels = band.reshape(band_height // PATCH, WL // PATCH, local_images, PATCH, PATCH, CH)
    pixels = pixels.transpose(2, 0, 3, 1, 4, 5).reshape(local_images, band_height, WL, CH)
    padded_up = padded_2(pixels, (("tile", 1),), 1)
    noise_pred = conv_rows(padded_up, up_conv).reshape(local_images, band_height, WL * CIN)
    return (work_out, noise_pred)


def solution(mesh):
    return jax.shard_map(
        shards,
        mesh=mesh,
        in_specs=(
            P("ctx", ("tile", "mp")),
            P("ctx", "tile", None),
            P(None, "mp"),
            P(None, ("tile", "mp")),
            P(("tile", "mp")),
            P(None, ("tile", "mp")),
            P(None, ("tile", "mp")),
            P(None, ("tile", "mp")),
            P(),
            P(),
            P(None, ("tile", "mp")),
            P(("tile", "mp"), None),
            P(),
            P(),
            P(),
        ),
        out_specs=(P("ctx", ("tile", "mp")), P("ctx", "tile", None)),
        check_vma=False,
    )
```

profile of v0, /device:TPU:1, one launch (start us, length us, event | category | flops | bytes accessed | tf_op | source)
XLA Modules:
  0.0 530.7 jit_solution(11298371027246895460)
XLA Ops:
  9.3 4.0 collective-permute-start
  14.9 3.1 collective-permute-done.1
  22.3 5.7 %concatenate.49 = bf16[2,16,64,72]{3,2,1,0:T(8,128)(2,1)} concatenate(bf16[2,16,64,8]{3,2,1,0:T(8,128)(2,1)} %get-tuple-element.195, bf16[2,16,64,8]{3,2,1,0:T(8,128)(2,1)} %copy.102, bf16[2,16,64,8]{3,2,1,0:T(8,128)(2,1)} %get-tuple-element.194, bf16[2,16,64,8]{3,2,1,0:T(8,128)(2,1)} %get-tuple-element.193, bf16[2,16,64,8]{3,2,1,0:T(8,128)(2,1)S(1)} %copy.95, ...), dimensions={3} | concatenate | bytes 589824 | tf_op jit(solution)/shard_map/concatenate | solution.py:44
  32.3 4.9 compare_and_fusion.1
  37.2 46.3 %all-gather.10.cloned.1.call-done = bf16[16,2,64,1024]{3,2,1,0:T(8,128)(2,1)} async-done(((bf16[1,2,64,1024]{3,2,1,0:T(8,128)(2,1)}), bf16[16,2,64,1024]{3,2,1,0:T(8,128)(2,1)}) %all-gather.10.cloned.1.call-update) | async-done | bytes 4194320 | tf_op jit(solution)/shard_map/all_gather | solution.py:98
  83.6 37.3 %while.16 = (s32[]{:T(128)}, f32[2,256,256]{2,1,0:T(8,128)S(1)}, bf16[16,2,64,1024]{3,2,1,0:T(8,128)(2,1)}, bf16[16,4,64,256]{3,2,1,0:T(8,128)(2,1)}, s32[]{:T(1...) while((s32[]{:T(128)}, f32[2,256,256]{2,1,0:T(8,128)S(1)}, ...), condition=%wide.region_3.5_spmd, body=%wide.region_2.4_spmd.sunk | while | flops 67141648 | bytes 2097484 | solution.py:109
  120.9 8.3 %all_gather.28 = bf16[1024,256]{1,0:T(8,128)(2,1)S(1)} all-gather(bf16[512,256]{1,0:T(8,128)(2,1)S(1)} %bitcast.118), channel_id=1, replica_groups=mesh['ctx'=2,'tile'=4,'mp'=4] {'ctx'}, dimensions={0}, use_global_device_ids=true | all-gather | bytes 786432 | tf_op jit(solution)/shard_map/all_gather | solution.py:112
  129.2 3.9 gather_fusion
  135.4 20.1 %all-gather.1 = bf16[16,1,256]{2,1,0:T(2,128)(2,1)S(1)} all-gather(bf16[1,1,256]{2,1,0:T(2,128)(2,1)S(1)} %reshape.274), channel_id=2, replica_groups=mesh['ctx'=2,'tile'=4,'mp'=4] {'tile','mp'}, dimensions={0}, use_global_device_ids=true | all-gather | bytes 8704 | tf_op jit(solution)/shard_map/all_gather | solution.py:129
  155.6 3.3 fusion.12
  158.9 54.1 %all-gather.12.cloned.1.call-done = bf16[1024,4096]{1,0:T(8,128)(2,1)} async-done(((bf16[1024,256]{1,0:T(8,128)(2,1)}), bf16[1024,4096]{1,0:T(8,128)(2,1)}) %all-gather.12.cloned.1.call-update) | async-done | bytes 8388624 | tf_op jit(solution)/shard_map/all_gather | solution.py:128
  213.0 5.1 fusion.4
  218.1 10.4 %fusion.6 = bf16[1024,4096]{1,0:T(8,128)(2,1)} fusion(bf16[1024,4096]{1,0:T(8,128)(2,1)} %all-gather.12.cloned.1.call-done, f32[4096]{0:T(1024)S(1)} %bitcast.125, f32[1024]{0:T(1024)S(1)} %add_rsqrt_fusion.2), kind=kLoop, calls=%fused_computation.15 | loop fusion | flops 16777216 | bytes 16797696 | tf_op jit(solution)/shard_map/convert_element_type | solution.py:132
  228.5 7.4 %multiply_reduce_fusion.1 = (f32[1024,2]{0,1:T(2,128)S(1)}, f32[1024,256]{0,1:T(8,128)}) fusion(bf16[1024,4096]{1,0:T(8,128)(2,1)} %fusion.6, bf16[4096,256]{1,0:T(8,128)(2,1)} %param.27), kind=kOutput, calls=%fused_computation.43 | convolution fusion | flops 2148005888 | bytes 11542528 | tf_op jit(solution)/shard_map/dot_general | solution.py:134
  239.1 7.4 %multiply_reduce_fusion = (f32[1024,2]{0,1:T(2,128)S(1)}, f32[1024,256]{0,1:T(8,128)}) fusion(bf16[1024,4096]{1,0:T(8,128)(2,1)} %fusion.6, bf16[4096,256]{1,0:T(8,128)(2,1)} %param.26), kind=kOutput, calls=%fused_computation.41 | convolution fusion | flops 2148005888 | bytes 11542528 | tf_op jit(solution)/shard_map/dot_general | solution.py:133
  248.1 7.2 %convolution_convert_fusion.1 = bf16[1024,256]{0,1:T(8,128)(2,1)} fusion(bf16[1024,4096]{1,0:T(8,128)(2,1)} %fusion.6, bf16[4096,256]{1,0:T(8,128)(2,1)} %param.28), kind=kOutput, calls=%fused_computation.33 | convolution fusion | flops 2147745792 | bytes 11010048 | tf_op jit(solution)/shard_map/dot_general | solution.py:135
  257.9 5.2 fusion.7
  263.1 6.1 %copy-done.3 = f32[2,2048,1024]{2,1,0:T(8,128)} copy-done((f32[2,2048,1024]{2,1,0:T(8,128)}, f32[2,2048,1024]{2,1,0:T(8,128)S(1)}, u32[]{:S(2)}) %copy-start.3) | copy-done | bytes 16777240
  269.1 3.9 fusion.8
  273.0 7.6 %all-gather.14.cloned.1.call-done = bf16[2048,2,128]{0,2,1:T(8,128)(2,1)} async-done(((bf16[1024,2,128]{0,2,1:T(8,128)(2,1)}), bf16[2048,2,128]{0,2,1:T(8,128)(2,1)}) %all-gather.14.cloned.1.call-update) | async-done | bytes 1048592 | tf_op jit(solution)/shard_map/all_gather | solution.py:147
  280.6 12.4 %divide_convert_fusion = bf16[1024,2,128]{0,2,1:T(8,128)(2,1)} fusion(bf16[2048,2,128]{0,2,1:T(8,128)(2,1)} %all-gather.14.cloned.1.call-done, f32[2,2048,1024]{2,1,0:T(8,128)} %copy-done.3, f32[1024,2]{0,1:T(2,128)S(1)} %broadcast_maximum_fusion, pred[1024,2048]{0,1:T(8,128)(4,1)} %fusion.12, f32[1024,2]{0,1:T(2,128)S(1)} %fusion.8), kind=kOutput, calls=%fused_computation.39 | convolution fusion | flops 1091043328 | bytes 20463616 | tf_op jit(solution)/shard_map/qhk,khd->qhd/dot_general | solution.py:162
  293.1 75.4 %all-gather.18.cloned.1.call-done = bf16[1024,4096]{0,1:T(8,128)(2,1)} async-done(((bf16[1024,256]{0,1:T(8,128)(2,1)}), bf16[1024,4096]{0,1:T(8,128)(2,1)}) %all-gather.18.cloned.1.call-update) | async-done | bytes 8388624 | tf_op jit(solution)/shard_map/all_gather | solution.py:170
  368.5 7.2 %fusion.18 = bf16[1024,256]{1,0:T(8,128)(2,1)} fusion(bf16[1024,4096]{0,1:T(8,128)(2,1)} %all-gather.18.cloned.1.call-done, bf16[4096,256]{1,0:T(8,128)(2,1)} %param.31, bf16[1024,256]{1,0:T(8,128)(2,1)S(1)} %copy-done.5), kind=kOutput, calls=%fused_computation.32 | convolution fusion | flops 2148270080 | bytes 11534336 | tf_op jit(solution)/shard_map/dot_general | solution.py:169
  377.3 17.7 %all-gather.20.cloned.1.call-done = bf16[2048,256]{1,0:T(8,128)(2,1)} async-done(((bf16[1024,256]{1,0:T(8,128)(2,1)}), bf16[2048,256]{1,0:T(8,128)(2,1)}) %all-gather.20.cloned.1.call-update) | async-done | bytes 1048592 | tf_op jit(solution)/shard_map/all_gather | solution.py:175
  397.4 3.2 convolution_convert_fusion
  400.7 70.7 %reduce-scatter.2.cloned.1.call-done = bf16[32,4096]{1,0:T(8,128)(2,1)} async-done(((bf16[512,4096]{1,0:T(8,128)(2,1)}), bf16[32,4096]{1,0:T(8,128)(2,1)}) %reduce-scatter.2.cloned.1.call-update) | async-done | bytes 262160 | tf_op jit(solution)/shard_map/reduce_scatter | solution.py:183
  473.3 18.1 %all-gather.22.cloned.1.call-done = bf16[128,4096]{1,0:T(8,128)(2,1)} async-done(((bf16[32,4096]{1,0:T(8,128)(2,1)}), bf16[128,4096]{1,0:T(8,128)(2,1)}) %all-gather.22.cloned.1.call-update) | async-done | bytes 1048592 | tf_op jit(solution)/shard_map/all_gather | solution.py:190
  496.4 3.1 collective-permute-start.2
  500.8 2.8 copy.130
  505.7 2.9 pad_maximum_fusion
  511.2 6.5 %fusion.42 = (bf16[2,16,64,256]{3,0,2,1:T(2,128)(2,1)S(1)}, bf16[2,16,64,256]{3,0,2,1:T(2,128)(2,1)S(1)}, bf16[2,16,64,256]{3,0,2,1:T(2,128)(2,1)S(1)}, bf16[2,1...) fusion(bf16[2,18,66,256]{3,0,2,1:T(2,128)(2,1)S(1)} %select_maximum_fusion), kind=kLoop, calls=%fused_computation.108 | loop fusion | bytes 12582912 | tf_op jit(solution)/shard_map/slice | solution.py:40
  519.9 2.7 fusion.48
  (154 shorter events, 80.6 us)
Async XLA Ops:
  7.2 390.2 %copy-start = (bf16[256,4096]{1,0:T(8,128)(2,1)S(1)}, bf16[256,4096]{1,0:T(8,128)(2,1)}, u32[]{:S(2)}) copy-start(bf16[256,4096]{1,0:T(8,128)(2,1)} %param.32) | copy-start | bytes 6291460
  7.2 20.8 %copy-start.10 = (bf16[72,64]{0,1:T(8,128)(2,1)S(1)}, bf16[72,64]{0,1:T(8,128)(2,1)}, u32[]{:S(2)}) copy-start(bf16[72,64]{0,1:T(8,128)(2,1)} %param.23) | copy-start | bytes 27652
  7.2 76.3 %all-gather.10.cloned.1.call-start = ((), (), s32[]{:S(2)}) async-start(), calls=%async_computation.1 | async-start | bytes 4456448 | tf_op jit(solution)/shard_map/all_gather | solution.py:98
  9.3 5.6 %collective-permute-start = (bf16[2,1,64,8]{3,2,1,0:T(8,128)(2,1)S(1)}, bf16[2,1,64,8]{3,2,1,0:T(8,128)(2,1)S(1)}, u32[]{:S(2)}, u32[]{:S(2)}) collective-permute-start(bf16[2,1,64,8]{3,2,1,0:T(8,128)(2,1)S(1)} %get-tuple-element.196), channel_id=1, source_target_pairs={{0,4},{4,8},{8,12},{1,5},{5,9},{9,13},{2,6},{6,10},{10,14},{3,7},{... | collective-permute-start | bytes 6152 | tf_op jit(solution)/shard_map/ppermute | solution.py:23
  13.3 4.7 collective-permute-start.1
  20.4 10.4 %copy-start.2 = (s32[4]{0:T(128)S(1)}, s32[4]{0:T(128)}, u32[]{:S(2)}) copy-start(s32[4]{0:T(128)} %param.35) | copy-start | bytes 52
  20.4 11.1 %copy-start.1 = (s32[4]{0:T(128)S(1)}, s32[4]{0:T(128)}, u32[]{:S(2)}) copy-start(s32[4]{0:T(128)} %param.34) | copy-start | bytes 52
  30.7 182.3 %all-gather.12.cloned.1.call-start = ((), (), s32[]{:S(2)}) async-start(), calls=%async_computation.2 | async-start | bytes 8912896 | tf_op jit(solution)/shard_map/all_gather | solution.py:128
  83.5 51.9 %copy-start.11 = (bf16[256]{0:T(256)(128)(2,1)S(1)}, bf16[256]{0:T(256)(128)(2,1)}, u32[]{:S(2)}) copy-start(bf16[256]{0:T(256)(128)(2,1)} %param.25) | copy-start | bytes 1540
  135.4 122.5 %all-gather.16.cloned.1.call-start = ((), (), s32[]{:S(2)}) async-start(), calls=%async_computation.4 | async-start | bytes 1572864 | tf_op jit(solution)/shard_map/all_gather | solution.py:146
  228.5 9.0 %copy-start.8 = (f32[128]{0:T(128)S(1)}, f32[128]{0:T(128)}, u32[]{:S(2)}) copy-start(f32[128]{0:T(128)} %param.30) | copy-start | bytes 1540
  238.7 42.0 %all-gather.14.cloned.1.call-start = ((), (), s32[]{:S(2)}) async-start(), calls=%async_computation.3 | async-start | bytes 1572864 | tf_op jit(solution)/shard_map/all_gather | solution.py:147
  248.1 9.8 %copy-start.7 = (f32[128]{0:T(128)S(1)}, f32[128]{0:T(128)}, u32[]{:S(2)}) copy-start(f32[128]{0:T(128)} %param.29) | copy-start | bytes 1540
  255.3 113.2 %all-gather.18.cloned.1.call-start = ((), (), s32[]{:S(2)}) async-start(), calls=%async_computation.5 | async-start | bytes 8912896 | tf_op jit(solution)/shard_map/all_gather | solution.py:170
  257.9 11.2 %copy-start.4 = (pred[1024,2048]{0,1:T(8,128)(4,1)S(1)}, pred[1024,2048]{0,1:T(8,128)(4,1)}, u32[]{:S(2)}) copy-start(pred[1024,2048]{0,1:T(8,128)(4,1)} %fusion.12) | copy-start | bytes 6291460
  263.0 6.1 %copy-start.3 = (f32[2,2048,1024]{2,1,0:T(8,128)}, f32[2,2048,1024]{2,1,0:T(8,128)S(1)}, u32[]{:S(2)}) copy-start(f32[2,2048,1024]{2,1,0:T(8,128)S(1)} %get-tuple-element.214) | copy-start | bytes 50331652
  273.0 95.5 %copy-start.5 = (bf16[1024,256]{1,0:T(8,128)(2,1)S(1)}, bf16[1024,256]{1,0:T(8,128)(2,1)}, u32[]{:S(2)}) copy-start(bf16[1024,256]{1,0:T(8,128)(2,1)} %select_select_fusion) | copy-start | bytes 1572868
  293.0 102.0 %all-gather.20.cloned.1.call-start = ((), (), s32[]{:S(2)}) async-start(), calls=%async_computation.6 | async-start | bytes 1572864 | tf_op jit(solution)/shard_map/all_gather | solution.py:175
  375.7 95.8 %reduce-scatter.2.cloned.1.call-start = ((), (), s32[]{:S(2)}) async-start(), calls=%async_computation.7 | async-start | bytes 4456448 | tf_op jit(solution)/shard_map/reduce_scatter | solution.py:183
  400.7 90.7 %all-gather.22.cloned.1.call-start = ((), (), s32[]{:S(2)}) async-start(), calls=%async_computation.8 | async-start | bytes 1310720 | tf_op jit(solution)/shard_map/all_gather | solution.py:190
  496.4 9.3 %collective-permute-start.2 = (bf16[2,1,64,256]{3,0,2,1:T(2,128)(2,1)S(1)}, bf16[2,1,64,256]{3,0,2,1:T(2,128)(2,1)S(1)}, u32[]{:S(2)}, u32[]{:S(2)}) collective-permute-start(bf16[2,1,64,256]{3,0,2,1:T(2,128)(2,1)S(1)} %get-tuple-element.188), channel_id=1, source_target_pairs={{0,4},{4,8},{8,12},{1,5},{5,9},{9,13},{2,6},{6,10},{10,14},{3,7},{... | collective-permute-start | bytes 196616 | tf_op jit(solution)/shard_map/ppermute | solution.py:23
  499.5 6.2 %collective-permute-start.3 = (bf16[2,1,64,256]{3,0,2,1:T(2,128)(2,1)S(1)}, bf16[2,1,64,256]{3,0,2,1:T(2,128)(2,1)S(1)}, u32[]{:S(2)}, u32[]{:S(2)}) collective-permute-start(bf16[2,1,64,256]{3,0,2,1:T(2,128)(2,1)S(1)} %get-tuple-element.189), channel_id=1, source_target_pairs={{4,0},{8,4},{12,8},{5,1},{9,5},{13,9},{6,2},{10,6},{14,10},{7,3},{... | collective-permute-start | bytes 196616 | tf_op jit(solution)/shard_map/ppermute | solution.py:26
  518.2 1.2 copy-start.6
  519.0 0.8 copy-start.9
Sparse Core Ops, SparseCore 0:
  30.8 52.6 all-gather.9
  135.5 77.4 all-gather.11
  238.8 19.0 all-gather.15
  259.3 21.2 all-gather.13
  293.1 75.3 all-gather.17
  375.8 19.1 all-gather.19
  400.8 70.6 reduce-scatter.1
  473.4 17.9 all-gather.21
where the time goes:
time: 538 us; the launch traced here: 531 us
  waiting for transfers between devices  296 us (55%)
  matrix products  73.2 us (14%)
  local copies, waits for them, and re-layouts  68.8 us (13%)
  other arithmetic  38.5 us (7%)
  blocking collectives  28.4 us (5%)
  between operations  14.9 us (3%)
  starting transfers between devices  10.6 us (2%)
    all_gather x1, waiting for transfers between devices, shards(): lax.all_gather(attended, ('tile', 'mp'), axis=1, tiled=True)  75.4 us
    reduce_scatter x1, waiting for transfers between devices, shards(): lax.psum_scatter(jnp.dot(rows_used, patch_out, preferred_element_type=jnp...  70.7 us
    all_gather x1, waiting for transfers between devices, shards(): lax.all_gather(stream, ('tile', 'mp'), axis=1, tiled=True)  54.1 us
    all_gather x1, waiting for transfers between devices, shards(): lax.all_gather(patches[None], ('tile', 'mp'), axis=0, tiled=True)  46.3 us
    all_gather x1, blocking collectives, shards(): lax.all_gather(gain_row, ('tile', 'mp'), axis=1, tiled=True)  20.1 us
    dot_general x16, matrix products, one_shard(): jnp.einsum('ipf,fd->ipd', single, weight, preferred_element_type=jnp.floa...  19.2 us
    all_gather x1, waiting for transfers between devices, shards(): band = lax.all_gather(own_active, 'mp', axis=0, tiled=True)  18.1 us
    all_gather x1, waiting for transfers between devices, shards(): every_row = lax.all_gather(work_out, 'ctx', axis=0, tiled=True)  17.7 us
  transfers between devices with their start and end apart: 12, of which 9 were waited for; matrix products, arithmetic and copies ran while one was open for 8% of the time, Pallas kernels for 0%

commit v1 on v0

v1 whole, which is shorter than its diff:
```python
import functools

import jax
import jax.numpy as jnp
from jax import lax
from jax.experimental import pallas as pl
from jax.experimental.pallas import tpu as pltpu
from jax.sharding import Mesh
from jax.sharding import PartitionSpec as P

HD = 128
CH = 256
CIN = 8
WL = 64
HL = 64
PATCH = 4
PIX = PATCH * PATCH
SIDE = WL // PATCH
IMG_TOK = 256
EPSILON = 1e-05
NEGATIVE_FILL = -1e30
WINDOW = (PATCH + 2) * CIN
TAPS = 3 * WINDOW
BF16 = jnp.bfloat16
F32 = jnp.float32
VMEM_LIMIT = 48 * 1024 * 1024


def params(*semantics):
    return pltpu.CompilerParams(
        dimension_semantics=semantics or None, vmem_limit_bytes=VMEM_LIMIT
    )


def cost(flops, nbytes, transcendentals=0):
    return pl.CostEstimate(
        flops=int(flops), bytes_accessed=int(nbytes), transcendentals=int(transcendentals)
    )


def silu(values):
    return values / (1.0 + jnp.exp(-values))


def mxu(left, right):
    return jnp.dot(left, right, preferred_element_type=F32)


def swap(values):
    return lax.ppermute(values, "core", [(0, 1), (1, 0)])


def down_kernel(images, half, meta, rows_ref, conv_ref, patch_ref, text_ref, out_ref, windows, total):
    step = pl.program_id(0)
    group = images * SIDE

    @pl.when(step == 0)
    def _():
        for col in range(SIDE):
            for row in range(PATCH + 2):
                piece = rows_ref[row, :, PATCH * CIN * col : PATCH * CIN * col + WINDOW]
                for shift in range(3):
                    if 0 <= row - shift < PATCH:
                        windows[
                            row - shift,
                            group * col : group * (col + 1),
                            WINDOW * shift : WINDOW * (shift + 1),
                        ] = piece

    hidden = mxu(windows[step // PATCH], conv_ref[lax.rem(step, PATCH)])
    term = mxu(silu(hidden).astype(BF16), patch_ref[...])

    @pl.when(step == 0)
    def _():
        total[...] = term

    @pl.when(step > 0)
    def _():
        total[...] += term

    @pl.when(step == PIX - 1)
    def _():
        tokens = total[...].astype(BF16)
        first = meta[2 * images]
        core = meta[2 * images + 1]
        block = 256
        for part in range(2 * half // block):
            which = part * block // half
            base = first + jnp.where(which == 0, core, 1 - core) * half + part * block - which * half
            place = base + lax.broadcasted_iota(jnp.int32, (block, 1), 0)
            source = jnp.full((block, 1), -1, jnp.int32)
            for image in range(images):
                inner = place - meta[image]
                inside = (inner >= 0) & (inner < IMG_TOK)
                index = (inner & (SIDE - 1)) * group + meta[images + image] * SIDE + (inner >> 4)
                source = jnp.where(inside, index, source)
            choice = source == lax.broadcasted_iota(jnp.int32, (block, images * IMG_TOK), 1)
            picked = mxu(jnp.where(choice, 1.0, 0.0).astype(BF16), tokens).astype(BF16)
            at = part * block - which * half
            out_ref[which, at : at + block, :] = jnp.where(
                source >= 0, picked.astype(F32), text_ref[part * block : (part + 1) * block, :].astype(F32)
            ).astype(BF16)


def down_stream(meta, rows, conv, patch_in, text, images):
    seq_rows, width = text.shape
    half = seq_rows // 2
    count = images * IMG_TOK
    return pl.pallas_call(
        functools.partial(down_kernel, images, half),
        grid_spec=pltpu.PrefetchScalarGridSpec(
            num_scalar_prefetch=1,
            grid=(PIX,),
            in_specs=[
                pl.BlockSpec(rows.shape, lambda i, m: (0, 0, 0)),
                pl.BlockSpec(conv.shape, lambda i, m: (0, 0, 0)),
                pl.BlockSpec((CH, width), lambda i, m: (i, 0)),
                pl.BlockSpec((seq_rows, width), lambda i, m: (0, 0)),
            ],
            out_specs=pl.BlockSpec((2, half, width), lambda i, m: (0, 0, 0)),
            scratch_shapes=[
                pltpu.VMEM((PATCH, count, TAPS), BF16),
                pltpu.VMEM((count, width), F32),
            ],
        ),
        out_shape=jax.ShapeDtypeStruct((2, half, width), BF16),
        compiler_params=params("arbitrary"),
        cost_estimate=cost(2 * count * PIX * CH * (256 + width), 4 << 20, count * PIX * CH),
        name="down_stream",
    )(meta, rows, conv, patch_in, text)


def head_norm(raw, gain):
    heads = raw.shape[1] // HD
    parts = []
    for head in range(heads):
        part = raw[:, head * HD : (head + 1) * HD]
        scale = lax.rsqrt(jnp.mean(part * part, axis=-1, keepdims=True) + EPSILON)
        parts.append((part * scale * gain).astype(BF16))
    return jnp.concatenate(parts, axis=1) if heads > 1 else parts[0]


def qkv_kernel(blocks, meta, x_ref, gain_ref, weight_ref, gains_ref, kvp_ref, qp_ref, kvo_ref, qo_ref, normed):
    step = pl.program_id(0)
    core = meta[0]
    half, width = x_ref.shape[1], x_ref.shape[2]

    @pl.when(step == 0)
    def _():
        chunk = 64

        def one(index, carry):
            rows = pl.ds(pl.multiple_of(index * chunk, chunk), chunk)
            square = jnp.zeros((chunk, width), F32)
            for block in range(blocks):
                value = x_ref[block, rows, :].astype(F32)
                square = square + value * value
            scale = lax.rsqrt(
                jnp.sum(square, axis=-1, keepdims=True) * (1.0 / (blocks * width)) + EPSILON
            )
            for block in range(blocks):
                place = jnp.bitwise_xor(block, core)
                value = x_ref[block, rows, :].astype(F32) * scale
                value = value * gain_ref[place].astype(F32)
                normed[rows, pl.ds(pl.multiple_of(place * width, width), width)] = value.astype(BF16)
            return carry

        lax.fori_loop(0, half // chunk, one, 0)

    raw = mxu(normed[...], weight_ref[0])

    @pl.when(step == 0)
    def _():
        kvp_ref[0] = head_norm(raw, gains_ref[1:2, :])

    @pl.when(step == 1)
    def _():
        kvp_ref[0] = raw.astype(BF16)

    @pl.when(step == 2)
    def _():
        qp_ref[...] = head_norm(raw, gains_ref[0:1, :] * HD ** (-0.5))

    @pl.when(step == 3)
    def _():
        kvo_ref[0] = head_norm(raw, gains_ref[1:2, :])

    @pl.when(step == 4)
    def _():
        kvo_ref[0] = raw.astype(BF16)

    @pl.when(step == 5)
    def _():
        qo_ref[...] = head_norm(raw, gains_ref[0:1, :] * HD ** (-0.5))


def qkv(meta, x, gain, weights, gains):
    blocks, half, width = x.shape
    model = blocks * width
    return pl.pallas_call(
        functools.partial(qkv_kernel, blocks),
        grid_spec=pltpu.PrefetchScalarGridSpec(
            num_scalar_prefetch=1,
            grid=(6,),
            in_specs=[
                pl.BlockSpec(x.shape, lambda i, m: (0, 0, 0)),
                pl.BlockSpec(gain.shape, lambda i, m: (0, 0, 0)),
                pl.BlockSpec((1, model, width), lambda i, m: (i, 0, 0)),
                pl.BlockSpec(gains.shape, lambda i, m: (0, 0)),
            ],
            out_specs=[
                pl.BlockSpec((1, half, width), lambda i, m: (jnp.minimum(i, 1), 0, 0)),
                pl.BlockSpec((half, width), lambda i, m: (0, 0)),
                pl.BlockSpec((1, half, width), lambda i, m: (jnp.clip(i - 3, 0, 1), 0, 0)),
                pl.BlockSpec((half, width), lambda i, m: (0, 0)),
            ],
            scratch_shapes=[pltpu.VMEM((half, model), BF16)],
        ),
        out_shape=[
            jax.ShapeDtypeStruct((2, half, width), BF16),
            jax.ShapeDtypeStruct((half, width), BF16),
            jax.ShapeDtypeStruct((2, half, width), BF16),
            jax.ShapeDtypeStruct((half, width), BF16),
        ],
        compiler_params=params("arbitrary"),
        cost_estimate=cost(12 * half * model * width, 18 << 20),
        name="norm_qkv",
    )(meta, x, gain, weights, gains)


def attention_kernel(images, pieces, meta, q_ref, *refs):
    kv_refs, out_ref = refs[:pieces], refs[pieces]
    rows = q_ref.shape[0]
    place = meta[images] + pl.program_id(1) * rows + lax.broadcasted_iota(jnp.int32, (rows, 1), 0)
    limit = place
    for image in range(images):
        inner = place - meta[image]
        limit = jnp.where((inner >= 0) & (inner < IMG_TOK), meta[image] + IMG_TOK - 1, limit)
    query = q_ref[...]
    scores = []
    top = None
    for piece in range(pieces):
        key = kv_refs[piece][0]
        score = lax.dot_general(
            query, key, (((1,), (1,)), ((), ())), preferred_element_type=F32
        )
        position = meta[images + 1 + piece] + lax.broadcasted_iota(jnp.int32, score.shape, 1)
        score = jnp.where(position <= limit, score, NEGATIVE_FILL)
        scores.append(score)
        best = jnp.max(score, axis=1, keepdims=True)
        top = best if top is None else jnp.maximum(top, best)
    total = jnp.zeros((rows, 1), F32)
    product = jnp.zeros((rows, HD), F32)
    for piece in range(pieces):
        weight = jnp.exp(scores[piece] - top)
        total = total + jnp.sum(weight, axis=1, keepdims=True)
        product = product + mxu(weight.astype(BF16), kv_refs[piece][1])
    out_ref[...] = (product / total).astype(BF16)


def attention(meta, query, pieces, images):
    half, width = query.shape
    block = 256 if half % 256 == 0 else half
    keys = half * len(pieces)
    return pl.pallas_call(
        functools.partial(attention_kernel, images, len(pieces)),
        grid_spec=pltpu.PrefetchScalarGridSpec(
            num_scalar_prefetch=1,
            grid=(width // HD, half // block),
            in_specs=[pl.BlockSpec((block, HD), lambda h, i, m: (i, h))]
            + [pl.BlockSpec((2, half, HD), lambda h, i, m: (0, 0, h)) for _ in pieces],
            out_specs=pl.BlockSpec((block, HD), lambda h, i, m: (i, h)),
        ),
        out_shape=jax.ShapeDtypeStruct((half, width), BF16),
        compiler_params=params("arbitrary", "arbitrary"),
        cost_estimate=cost(4 * half * keys * width, 4 * keys * width, half * keys * width // HD),
        name="attention",
    )(meta, query, *pieces)


def out_kernel(steps, meta, att_ref, own_w, par_w, own_s, par_s, par_out, own_out, own_t, par_t):
    step = pl.program_id(0)
    core = meta[0]
    blocks, half, width = att_ref.shape
    for weight_ref, stream_ref, total in ((par_w, par_s, par_t), (own_w, own_s, own_t)):
        @pl.when(step == 0)
        def _():
            total[...] = stream_ref[...].astype(F32)

        term = None
        for block in range(blocks):
            place = jnp.bitwise_xor(block, core)
            one = mxu(
                att_ref[block], weight_ref[pl.ds(pl.multiple_of(place * width, width), width), :]
            )
            term = one if term is None else term + one
        total[...] += term

    @pl.when(step == steps - 1)
    def _():
        par_out[...] = par_t[...].astype(BF16)
        own_out[...] = own_t[...].astype(BF16)


def out_project(meta, attended, own_w, par_w, own_s, par_s):
    blocks, half, width = attended.shape
    steps = 4
    deep = blocks // steps
    shape = jax.ShapeDtypeStruct((half, width), BF16)
    whole = pl.BlockSpec((half, width), lambda i, m: (0, 0))
    weight = pl.BlockSpec((deep * width, width), lambda i, m: (i, 0))
    return pl.pallas_call(
        functools.partial(out_kernel, steps),
        grid_spec=pltpu.PrefetchScalarGridSpec(
            num_scalar_prefetch=1,
            grid=(steps,),
            in_specs=[
                pl.BlockSpec((deep, half, width), lambda i, m: (i, 0, 0)),
                weight,
                weight,
                whole,
                whole,
            ],
            out_specs=[whole, whole],
            scratch_shapes=[pltpu.VMEM((half, width), F32), pltpu.VMEM((half, width), F32)],
        ),
        out_shape=[shape, shape],
        compiler_params=params("arbitrary"),
        cost_estimate=cost(4 * half * blocks * width * width, 9 << 20),
        name="out_project",
    )(meta, attended, own_w, par_w, own_s, par_s)


def pick_kernel(targets, meta, own_ref, par_ref, out_ref):
    half = own_ref.shape[0]
    own_base, par_base = meta[targets], meta[targets + 1]
    for target in range(targets):
        place = meta[target] + lax.broadcasted_iota(jnp.int32, (IMG_TOK, half), 0)
        column = lax.broadcasted_iota(jnp.int32, (IMG_TOK, half), 1)
        own = jnp.where(place == column + own_base, 1.0, 0.0).astype(BF16)
        par = jnp.where(place == column + par_base, 1.0, 0.0).astype(BF16)
        out_ref[target] = (mxu(own, own_ref[...]) + mxu(par, par_ref[...])).astype(BF16)


def pick_rows(meta, own, par, targets):
    half, width = own.shape
    whole = pl.BlockSpec((half, width), lambda i, m: (0, 0))
    return pl.pallas_call(
        functools.partial(pick_kernel, targets),
        grid_spec=pltpu.PrefetchScalarGridSpec(
            num_scalar_prefetch=1,
            grid=(1,),
            in_specs=[whole, whole],
            out_specs=pl.BlockSpec((targets, IMG_TOK, width), lambda i, m: (0, 0, 0)),
        ),
        out_shape=jax.ShapeDtypeStruct((targets, IMG_TOK, width), BF16),
        compiler_params=params("arbitrary"),
        cost_estimate=cost(targets * 4 * IMG_TOK * half * width, 1 << 20),
        name="pick_rows",
    )(meta, own, par)


def up_kernel(count, *refs):
    own_refs, par_refs = refs[:count], refs[count : 2 * count]
    own_w, par_w, out_ref = refs[2 * count :]

    def merged(parts):
        total = parts[0][...].astype(F32)
        for part in parts[1:]:
            total = total + part[...].astype(F32)
        return total.astype(BF16)

    out_ref[0] = (mxu(merged(own_refs), own_w[...]) + mxu(merged(par_refs), par_w[...])).astype(BF16)


def up_project(own_parts, par_parts, own_w, par_w, groups):
    width, features = own_w.shape
    deep = features // groups
    part = pl.BlockSpec((IMG_TOK, width), lambda i: (0, 0))
    weight = pl.BlockSpec((width, deep), lambda i: (0, i))
    return pl.pallas_call(
        functools.partial(up_kernel, len(own_parts)),
        grid=(groups,),
        in_specs=[part] * (len(own_parts) + len(par_parts)) + [weight, weight],
        out_specs=pl.BlockSpec((1, IMG_TOK, deep), lambda i: (i, 0, 0)),
        out_shape=jax.ShapeDtypeStruct((groups, IMG_TOK, deep), BF16),
        compiler_params=params("arbitrary"),
        cost_estimate=cost(4 * IMG_TOK * width * features, 6 << 20),
        name="up_project",
    )(*own_parts, *par_parts, own_w, par_w)


def spread_kernel(rows_ref, spread_ref, out_ref):
    active = silu(rows_ref[...].astype(F32)).astype(BF16)
    row = lax.broadcasted_iota(jnp.int32, (IMG_TOK, PIX * CIN), 0)
    patch_row, patch_col = row >> 4, row & (SIDE - 1)
    total = None
    for index in range(9):
        down, right = index // 3 - 1, index % 3 - 1
        part = mxu(active, spread_ref[:, index * PIX * CIN : (index + 1) * PIX * CIN])
        offset = down * SIDE + right
        if offset:
            part = pltpu.roll(part, offset % IMG_TOK, 0)
        source_row, source_col = patch_row - down, patch_col - right
        inside = (source_row >= 0) & (source_row < SIDE) & (source_col >= 0) & (source_col < SIDE)
        part = jnp.where(inside, part, 0.0)
        total = part if total is None else total + part
    out_ref[...] = total


def spread_rows(rows, spread):
    return pl.pallas_call(
        spread_kernel,
        out_shape=jax.ShapeDtypeStruct((IMG_TOK, PIX * CIN), F32),
        compiler_params=params(),
        cost_estimate=cost(2 * IMG_TOK * rows.shape[1] * 9 * PIX * CIN, 2 << 20),
        name="spread_rows",
    )(rows, spread)


def spread_weights(up_conv, pixels):
    taps = up_conv.reshape(9, CH, CIN).transpose(1, 0, 2).reshape(CH, 9 * CIN)
    shape = (pixels.shape[0], 9 * CIN, 9 * PIX * CIN)
    row = lax.broadcasted_iota(jnp.int32, shape, 1)
    col = lax.broadcasted_iota(jnp.int32, shape, 2)
    pixel = pixels[:, None, None]
    tap, channel = row >> 3, row & 7
    patch, target, out_channel = col >> 7, (col >> 3) & 15, col & 7
    tap_row, tap_col = tap // 3, tap % 3
    down, right = patch // 3 - 1, patch % 3 - 1
    hit = (
        (channel == out_channel)
        & ((pixel >> 2) + 1 - tap_row == (target >> 2) + PATCH * down)
        & ((pixel & 3) + 1 - tap_col == (target & 3) + PATCH * right)
    )
    placed = jnp.where(hit, 1.0, 0.0).astype(BF16)
    spread = jnp.einsum("ct,ptn->pcn", taps, placed, preferred_element_type=F32)
    return spread.astype(BF16).reshape(pixels.shape[0] * CH, 9 * PIX * CIN)


def gather_small(latents, down_conv, norm_gain):
    tiles, outer, cores = (lax.axis_size(name) for name in ("tile", "mpo", "core"))
    ctxs = lax.axis_size("ctx")
    parts = outer * cores
    mp_index = lax.axis_index("mpo") * cores + lax.axis_index("core")
    local, height, breadth = latents.shape
    piece = height // parts
    own = lax.dynamic_slice_in_dim(latents, mp_index * piece, piece, 1).reshape(-1)
    taps, channels = down_conv.shape
    tap_piece = taps // tiles
    conv = lax.dynamic_slice_in_dim(down_conv, lax.axis_index("tile") * tap_piece, tap_piece, 0)
    conv = conv.reshape(-1)
    flat = jnp.concatenate([own, conv, norm_gain])
    size = -(-flat.shape[0] // 2048) * 2048
    flat = jnp.pad(flat, (0, size - flat.shape[0])).reshape(1, size // 128, 128)
    every = lax.all_gather(flat, ("ctx", "tile", "mpo", "core"), axis=0, tiled=True)
    every = every.reshape(ctxs, tiles, parts, size)
    first, second = own.shape[0], own.shape[0] + conv.shape[0]
    images = every[..., :first].reshape(ctxs, tiles, parts, local, piece, breadth)
    images = images.transpose(0, 3, 1, 2, 4, 5).reshape(ctxs * local, HL, breadth)
    conv = every[0, :, :, first:second].reshape(tiles, parts, tap_piece, channels)
    conv = conv.transpose(0, 2, 1, 3).reshape(taps, parts * channels)
    gain = every[0, :, :, second : second + norm_gain.shape[0]].reshape(tiles * parts, 1, -1)
    return images, conv, gain


def shards(
    text_embed,
    latents,
    down_conv,
    patch_in,
    norm_gain,
    query_weight,
    key_weight,
    value_weight,
    query_gain,
    key_gain,
    out_weight,
    patch_out,
    up_conv,
    span_start,
    image_of_slot,
):
    ctxs, tiles, outer = (lax.axis_size(name) for name in ("ctx", "tile", "mpo"))
    ctx, tile, mpo, core = (lax.axis_index(name) for name in ("ctx", "tile", "mpo", "core"))
    seq_rows, width = text_embed.shape
    half = seq_rows // 2
    images = span_start.shape[0]
    groups = tiles * outer
    gather_axes = ("tile", "mpo")

    weights_par = [swap(w) for w in (key_weight, value_weight, query_weight)]
    out_par = swap(out_weight)
    up_par = swap(patch_out)
    every_latent, conv, gain = gather_small(latents, down_conv, norm_gain)

    numbers = jnp.arange(images, dtype=jnp.int32)
    matches = image_of_slot[None, :] == numbers[:, None]
    slot_of_image = jnp.sum(jnp.where(matches, numbers[None, :], 0), axis=1)
    first = ctx * seq_rows
    core_meta = jnp.stack([core]).astype(jnp.int32)
    stream_meta = jnp.concatenate([span_start, slot_of_image, jnp.stack([first, core])]).astype(jnp.int32)

    padded = jnp.pad(every_latent, ((0, 0), (1, 1), (CIN, 128 - CIN)))
    rows = jnp.stack(
        [padded[:, r : r + HL - PATCH + 1 : PATCH, :].reshape(images * SIDE, -1) for r in range(PATCH + 2)]
    )
    conv = conv.reshape(3, 3 * CIN, CH)
    conv = jnp.stack(
        [
            jnp.pad(conv, ((0, 0), (CIN * c, WINDOW - 3 * CIN - CIN * c), (0, 0))).reshape(TAPS, CH)
            for c in range(PATCH)
        ]
    )
    text = jnp.roll(text_embed.reshape(2, half, width), core, axis=0).reshape(seq_rows, width)
    stream = down_stream(stream_meta, rows, conv, patch_in, text, images)
    stream_own = stream[0]
    stream_par = swap(stream[1])

    x = lax.all_gather(jnp.stack([stream_own, stream_par]), gather_axes, axis=0, tiled=True)
    weights = jnp.stack(weights_par + [key_weight, value_weight, query_weight])
    gains = jnp.stack([query_gain, key_gain])
    kv_send, q_send, kv_own, q_own = qkv(core_meta, x, gain, weights, gains)

    def shifted(values, step, cross):
        pairs = [
            (2 * c + k, 2 * ((c + step) % ctxs) + (1 - k if cross else k))
            for c in range(ctxs)
            for k in range(2)
        ]
        return lax.ppermute(values, ("ctx", "core"), pairs)

    q_par = swap(q_send)
    pieces = [kv_own, swap(kv_send)]
    bases = [first + core * half, first + (1 - core) * half]
    for step in range(1, ctxs):
        from_ctx = lax.rem(ctx + ctxs - step, ctxs) * seq_rows
        pieces += [shifted(kv_own, step, False), shifted(kv_send, step, True)]
        bases += [from_ctx + core * half, from_ctx + (1 - core) * half]
    spans = [span_start[i] for i in range(images)]

    def attend(query, base):
        meta = jnp.stack(spans + [base] + bases).astype(jnp.int32)
        return attention(meta, query, pieces, images)

    att_par = swap(attend(q_par, bases[1]))
    att_own = attend(q_own, bases[0])
    attended = lax.all_gather(jnp.stack([att_own, att_par]), gather_axes, axis=0, tiled=True)
    out_send, out_own = out_project(
        core_meta, attended, out_weight, out_par, stream_own, stream_par
    )
    out_other = swap(out_send)
    ordered = jnp.where(
        core == 0, jnp.stack([out_own, out_other]), jnp.stack([out_other, out_own])
    )
    layer_out = ordered.reshape(seq_rows, width)

    starts = jnp.take(span_start, image_of_slot)
    wanted = []
    for step in range(ctxs):
        to_ctx = lax.rem(ctx + step, ctxs)
        wanted += [starts[2 * to_ctx + core], starts[2 * to_ctx + 1 - core]]
    pick_meta = jnp.stack(wanted + bases[:2]).astype(jnp.int32)
    picks = pick_rows(pick_meta, out_own, out_other, 2 * ctxs)
    own_parts, par_parts = [picks[0]], [swap(picks[1])]
    for step in range(1, ctxs):
        own_parts.append(shifted(picks[2 * step], step, False))
        par_parts.append(shifted(picks[2 * step + 1], step, True))
    partial = up_project(own_parts, par_parts, patch_out, up_par, groups)
    deep = partial.shape[2]
    own_rows = lax.psum_scatter(partial, gather_axes, scatter_dimension=0, tiled=True)
    pixels = (tile * outer + mpo) * (deep // CH) + jnp.arange(deep // CH, dtype=jnp.int32)
    spread = spread_rows(own_rows.reshape(IMG_TOK, deep), spread_weights(up_conv, pixels))

    bands = spread.reshape(tiles, IMG_TOK // tiles, PIX * CIN)
    band = lax.dynamic_index_in_dim(bands, tile, 0, keepdims=False)
    for step in range(1, tiles):
        piece = lax.dynamic_index_in_dim(bands, lax.rem(tile + step, tiles), 0, keepdims=False)
        band = band + lax.ppermute(piece, "tile", [(t, (t + step) % tiles) for t in range(tiles)])
    summed = band
    for step in range(1, outer):
        summed = summed + lax.ppermute(band, "mpo", [(m, (m + step) % outer) for m in range(outer)])
    other = swap(summed)
    slots = jnp.where(core == 0, jnp.stack([summed, other]), jnp.stack([other, summed]))
    noise = slots.reshape(2, SIDE // tiles, SIDE, PATCH, PATCH * CIN).transpose(0, 1, 3, 2, 4)
    return layer_out, noise.reshape(2, HL // tiles, WL * CIN)


def solution(mesh):
    ctxs, tiles, parts = mesh.devices.shape
    fine = Mesh(
        mesh.devices.reshape(ctxs, tiles, parts // 2, 2), ("ctx", "tile", "mpo", "core")
    )
    features = ("tile", "mpo", "core")
    return jax.shard_map(
        shards,
        mesh=fine,
        in_specs=(
            P("ctx", features),
            P("ctx", "tile", None),
            P(None, ("mpo", "core")),
            P(None, features),
            P(features),
            P(None, features),
            P(None, features),
            P(None, features),
            P(),
            P(),
            P(None, features),
            P(features, None),
            P(),
            P(),
            P(),
        ),
        out_specs=(P("ctx", features), P("ctx", "tile", None)),
        check_vma=False,
    )
```

time: 538 us -> 396 us (0.74); the launches traced: 531 us -> 395 us
  waiting for transfers between devices: 296 us -> 214 us
  matrix products: 73.2 us -> 0.61 us
  Pallas kernels: 0 us -> 54.5 us
  other arithmetic: 38.5 us -> 5.92 us
  local copies, waits for them, and re-layouts: 68.8 us -> 42 us
  blocking collectives: 28.4 us -> 44.1 us
  starting transfers between devices: 10.6 us -> 19.3 us
    all_gather x7 -> x2, waiting for transfers between devices: 222 us -> 113 us  [the longest x1 63.5 us: shards(): lax.all_gather(jnp.stack([att_own, att_par]), gather_axes, axis=0, tiled=...]
    dot_general x25 -> x1, matrix products: 73.2 us -> 0.61 us  [spread_weights(): spread = jnp.einsum('ct,ptn->pcn', taps, placed, preferred_element_type=F32)]
    pallas_call x0 -> x8, Pallas kernels: none -> 54.5 us  [the longest x1 13.9 us: down_stream(): pl.pallas_call(functools.partial(down_kernel, images, half), grid_spec=pl...]
    ppermute x4 -> x20, waiting for transfers between devices: 3.07 us -> 38.7 us  [the longest x4 27.9 us: shifted(): return lax.ppermute(values, ('ctx', 'core'), pairs)]
    unnamed x35 -> x56, local copies, waits for them, and re-layouts: 8.05 us -> 27.7 us
    dynamic_slice x16 -> x3, local copies, waits for them, and re-layouts: 17.4 us -> 1.55 us  [the longest x2 0.89 us: gather_small(): lax.dynamic_slice_in_dim(down_conv, lax.axis_index('tile') * tap_piece, t...]
    all_gather x2 -> x1, blocking collectives: 28.4 us -> 44.1 us  [gather_small(): lax.all_gather(flat, ('ctx', 'tile', 'mpo', 'core'), axis=0, tiled=True)]
    convert_element_type x4 -> x0, other arithmetic: 13.4 us -> none  [the longest x1 10.4 us: shards(): (widened * rms_scale(widened) * gain_whole.astype(jnp.float32)).astype(jn...]
  transfers between devices with their start and end apart: 12 -> 23, of which waited for: 9 -> 14; matrix products, arithmetic and copies ran while one was open for 8% -> 9% of each run, Pallas kernels for 0% -> 7%
where the time goes in v1:
time: 396 us; the launch traced here: 395 us
  waiting for transfers between devices  214 us (54%)
  Pallas kernels  54.5 us (14%)
  blocking collectives  44.1 us (11%)
  local copies, waits for them, and re-layouts  42 us (11%)
  starting transfers between devices  19.3 us (5%)
  between operations  14.3 us (4%)
  other arithmetic  5.92 us (1%)
    all_gather x1, waiting for transfers between devices, shards(): lax.all_gather(jnp.stack([att_own, att_par]), gather_axes, axis=0, tiled=...  63.5 us
    reduce_scatter x1, waiting for transfers between devices, shards(): lax.psum_scatter(partial, gather_axes, scatter_dimension=0, tiled=True)  63 us
    all_gather x1, waiting for transfers between devices, shards(): lax.all_gather(jnp.stack([stream_own, stream_par]), gather_axes, axis=0,...  49.2 us
    all_gather x1, blocking collectives, gather_small(): lax.all_gather(flat, ('ctx', 'tile', 'mpo', 'core'), axis=0, tiled=True)  44.1 us
    ppermute x4, waiting for transfers between devices, shifted(): return lax.ppermute(values, ('ctx', 'core'), pairs)  27.9 us
    unnamed x56, local copies, waits for them, and re-layouts  27.7 us
    pallas_call x1, Pallas kernels, down_stream(): pl.pallas_call(functools.partial(down_kernel, images, half), grid_spec=pl...  13.9 us
    pallas_call x1, Pallas kernels, qkv(): pl.pallas_call(functools.partial(qkv_kernel, blocks), grid_spec=pltpu.Pre...  13.7 us
  transfers between devices with their start and end apart: 23, of which 14 were waited for; matrix products, arithmetic and copies ran while one was open for 9% of the time, Pallas kernels for 7%

profile of v1, /device:TPU:1, one launch (start us, length us, event | category | flops | bytes accessed | tf_op | source)
XLA Modules:
  0.0 395.2 jit_solution(1879135272919664045)
XLA Ops:
  9.7 44.1 %all_gather.9 = bf16[32,48,128]{2,1,0:T(8,128)(2,1)S(1)} all-gather(bf16[1,48,128]{2,1,0:T(8,128)(2,1)S(1)} %fusion.33), channel_id=1, replica_groups=mesh['ctx'=2,'tile'=4,'mpo'=2,'core'=2] {'ctx','tile','mpo','core'}, dimensions={0}, use_global_device_ids=true | all-gather | bytes 405504 | tf_op jit(solution)/shard_map/all_gather | solution.py:456
  62.7 13.9 %down_stream.1 = bf16[2,512,256]{2,1,0:T(8,128)(2,1)S(1)} custom-call(s32[10]{0:T(128)S(1)} %pad_add_fusion.meta, bf16[6,64,640]{2,1,0:T(8,128)(2,1)S(1)} %bitcast_dynamic-update-slice_fusion.6.rows_ref, bf16[4,144,256]{2,1,0:T(8,128)(2,1)S(1)} %pad_maximum_fusion.2.conv_ref, bf16[4096,256]{1,0:T(8,128)(2,1)S(1)} %copy-done.7, bf16[1024,256]{1,0:T(8,128)(2,1)S(1)} %bitcast.103), custom_call_target="tpu_custom_call" | custom-call | flops 4294967296 | bytes 4194304 | tf_op jit(solution)/shard_map/down_stream/pallas_call | solution.py:109
  76.9 1.4 collective-permute-done.par_s
  80.7 3.1 bitcast_dynamic-update-slice_fusion.5
  84.0 3.2 bitcast_dynamic-update-slice_fusion.4
  87.2 3.2 bitcast_dynamic-update-slice_fusion.3
  90.5 1.5 bitcast_dynamic-update-slice_fusion.2
  92.0 3.1 bitcast_dynamic-update-slice_fusion.1
  95.0 3.1 bitcast_dynamic-update-slice_fusion.weight_ref
  98.2 49.2 %all-gather.3.cloned.1.call-done.x_ref = bf16[16,512,256]{2,1,0:T(8,128)(2,1)} async-done(((bf16[2,512,256]{2,1,0:T(8,128)(2,1)}), bf16[16,512,256]{2,1,0:T(8,128)(2,1)}) %all-gather.3.cloned.1.call-update) | async-done | bytes 4194320 | tf_op jit(solution)/shard_map/all_gather | solution.py:520
  147.3 2.2 copy-done.6
  149.5 13.7 %norm_qkv.1 = (bf16[2,512,256]{2,1,0:T(8,128)(2,1)}, bf16[512,256]{1,0:T(8,128)(2,1)S(1)}, bf16[2,512,256]{2,1,0:T(8,128)(2,1)S(1)}, bf16[512,256]{1,0:T(8,128)(2,1)S(1)}) custom-call(s32[1]{0:T(128)} %bitcast.meta, bf16[16,512,256]{2,1,0:T(8,128)(2,1)S(1)} %copy-done.6, bf16[16,1,256]{2,1,0:T(2,128)(2,1)S(1)} %reshape_squeeze.8.gain_ref, ...), custom_call_target="tpu_custom_call" | custom-call | flops 6442450944 | bytes 18874368 | tf_op jit(solution)/shard_map/norm_qkv/pallas_call | solution.py:200
  164.0 1.9 collective-permute-start.4
  169.0 10.4 %collective-permute-done.5.refs_2_ = bf16[2,512,256]{2,1,0:T(8,128)(2,1)S(1)} collective-permute-done((bf16[2,512,256]{2,1,0:T(8,128)(2,1)S(1)}, bf16[2,512,256]{2,1,0:T(8,128)(2,1)S(1)}, u32[]{:S(2)}, u32[]{:S(2)}) %collective-permute-start.5) | collective-permute-done | bytes 524320 | tf_op jit(solution)/shard_map/ppermute | solution.py:531
  179.4 11.3 %collective-permute-done.6.refs_3_ = bf16[2,512,256]{2,1,0:T(8,128)(2,1)S(1)} collective-permute-done((bf16[2,512,256]{2,1,0:T(8,128)(2,1)}, bf16[2,512,256]{2,1,0:T(8,128)(2,1)S(1)}, u32[]{:S(2)}, u32[]{:S(2)}) %collective-permute-start.6) | collective-permute-done | bytes 524320 | tf_op jit(solution)/shard_map/ppermute | solution.py:531
  190.7 5.8 %attention.3 = bf16[512,256]{1,0:T(8,128)(2,1)} custom-call(s32[9]{0:T(128)S(1)} %stack.137.meta, bf16[512,256]{1,0:T(8,128)(2,1)S(1)} %collective-permute-done.7.q_ref, bf16[2,512,256]{2,1,0:T(8,128)(2,1)S(1)} %get-tuple-element.9.refs_0_, bf16[2,512,256]{2,1,0:T(8,128)(2,1)S(1)} %collective-permute-done.4.refs_1_, ...), custom_call_target="tpu_custom_call" | custom-call | flops 1073741824 | bytes 2097152 | tf_op jit(solution)/shard_map/attention/pallas_call | solution.py:265
  201.0 5.2 %attention.2 = bf16[512,256]{1,0:T(8,128)(2,1)S(1)} custom-call(s32[9]{0:T(128)S(1)} %stack.120.meta, bf16[512,256]{1,0:T(8,128)(2,1)S(1)} %copy-done.15, bf16[2,512,256]{2,1,0:T(8,128)(2,1)S(1)} %get-tuple-element.9.refs_0_, bf16[2,512,256]{2,1,0:T(8,128)(2,1)S(1)} %copy-done.9, bf16[2,512,256]{2,1,0:T(8,128)(2,1)S(1)} %copy-done.11, ...), custom_call_target="tpu_custom_call" | custom-call | flops 1073741824 | bytes 2097152 | tf_op jit(solution)/shard_map/attention/pallas_call | solution.py:265
  207.8 4.6 %collective-permute-done.9.par_w = bf16[4096,256]{1,0:T(8,128)(2,1)S(1)} collective-permute-done((bf16[4096,256]{1,0:T(8,128)(2,1)S(1)}, bf16[4096,256]{1,0:T(8,128)(2,1)S(1)}, u32[]{:S(2)}, u32[]{:S(2)}) %collective-permute-start.9) | collective-permute-done | bytes 2097184 | tf_op jit(solution)/shard_map/ppermute | solution.py:50
  212.4 1.4 copy-done.2
  213.8 63.5 %all-gather.5.cloned.1.call-done.att_ref = bf16[16,512,256]{2,1,0:T(8,128)(2,1)} async-done(((bf16[2,512,256]{2,1,0:T(8,128)(2,1)}), bf16[16,512,256]{2,1,0:T(8,128)(2,1)}) %all-gather.5.cloned.1.call-update) | async-done | bytes 4194320 | tf_op jit(solution)/shard_map/all_gather | solution.py:548
  277.3 1.6 copy-done.3
  278.9 6.9 %out_project.1 = (bf16[512,256]{1,0:T(8,128)(2,1)S(1)}, bf16[512,256]{1,0:T(8,128)(2,1)S(1)}) custom-call(s32[1]{0:T(128)} %bitcast.meta, bf16[16,512,256]{2,1,0:T(8,128)(2,1)} %all-gather.5.cloned.1.call-done.att_ref, bf16[4096,256]{1,0:T(8,128)(2,1)S(1)} %copy-done.1, bf16[4096,256]{1,0:T(8,128)(2,1)S(1)} %copy-done.3, ...), custom_call_target="tpu_custom_call" | custom-call | flops 2147483648 | bytes 9437184 | tf_op jit(solution)/shard_map/out_project/pallas_call | solution.py:312
  285.9 1.9 collective-permute-start.10
  289.1 2.6 stack.144.meta
  294.9 3.2 collective-permute-done.11.refs_1_
  298.1 3.0 collective-permute-done.13.refs_3_
  301.1 6.8 %up_project.1 = bf16[8,256,512]{2,1,0:T(8,128)(2,1)} custom-call(bf16[256,256]{1,0:T(8,128)(2,1)S(1)} %get-tuple-element.17.refs_0_, bf16[256,256]{1,0:T(8,128)(2,1)S(1)} %collective-permute-done.11.refs_1_, bf16[256,256]{1,0:T(8,128)(2,1)S(1)} %collective-permute-done.12.refs_2_, bf16[256,256]{1,0:T(8,128)(2,1)S(1)} %collective-permute-done.13.refs_3_, ...), custom_call_target="tpu_custom_call" | custom-call | flops 1073741824 | bytes 6291456 | tf_op jit(solution)/shard_map/up_project/pallas_call | solution.py:381
  308.7 63.0 %reduce-scatter.2.cloned.1.call-done = bf16[1,256,512]{2,1,0:T(8,128)(2,1)} async-done(((bf16[8,256,512]{2,1,0:T(8,128)(2,1)}), bf16[1,256,512]{2,1,0:T(8,128)(2,1)}) %reduce-scatter.2.cloned.1.call-update) | async-done | bytes 262160 | tf_op jit(solution)/shard_map/reduce_scatter | solution.py:571
  375.7 1.5 collective-permute-start.17
  378.8 1.3 collective-permute-start.18
  380.1 1.8 collective-permute-done.18
  382.0 4.7 %collective-permute-start.19 = (f32[64,128]{1,0:T(8,128)S(1)}, f32[64,128]{1,0:T(8,128)S(1)}, u32[]{:S(2)}, u32[]{:S(2)}) collective-permute-start(f32[64,128]{1,0:T(8,128)S(1)} %add.205), channel_id=1, source_target_pairs={{0,1},{1,0},{2,3},{3,2},{4,5},{5,4},{6,7},{7,6},{8,9},{9,8},{10,11... | collective-permute-start | bytes 98312 | tf_op jit(solution)/shard_map/ppermute | solution.py:50
  (144 shorter events, 36.8 us)
Async XLA Ops:
  7.2 300.9 %copy-start = (bf16[2304,8]{0,1:T(8,128)(2,1)S(1)}, bf16[2304,8]{0,1:T(8,128)(2,1)}, u32[]{:S(2)}) copy-start(bf16[2304,8]{0,1:T(8,128)(2,1)} %param.27) | copy-start | bytes 110596
  7.2 140.1 %all-gather.3.cloned.1.call-start = ((), (), s32[]{:S(2)}) async-start(), calls=%async_computation.1 | async-start | bytes 4718592 | tf_op jit(solution)/shard_map/all_gather | solution.py:520
  7.2 73.5 %collective-permute-start.1 = (bf16[4096,256]{1,0:T(8,128)(2,1)}, bf16[4096,256]{1,0:T(8,128)(2,1)}, u32[]{:S(2)}, u32[]{:S(2)}) collective-permute-start(bf16[4096,256]{1,0:T(8,128)(2,1)} %param.21), channel_id=1, source_target_pairs={{0,1},{1,0},{2,3},{3,2},{4,5},{5,4},{6,7},{7,6},{8,9},{9,8},{10,11... | collective-permute-start | bytes 6291464 | tf_op jit(solution)/shard_map/ppermute | solution.py:50
  54.0 5.2 %copy-start.21 = (s32[4]{0:T(128)S(1)}, s32[4]{0:T(128)}, u32[]{:S(2)}) copy-start(s32[4]{0:T(128)} %param.29) | copy-start | bytes 52
  54.7 7.9 %copy-start.16 = (s32[4]{0:T(128)S(1)}, s32[4]{0:T(128)}, u32[]{:S(2)}) copy-start(s32[4]{0:T(128)} %param.28) | copy-start | bytes 52
  54.8 7.9 %copy-start.7 = (bf16[4096,256]{1,0:T(8,128)(2,1)S(1)}, bf16[4096,256]{1,0:T(8,128)(2,1)}, u32[]{:S(2)}) copy-start(bf16[4096,256]{1,0:T(8,128)(2,1)} %patch_ref.1) | copy-start | bytes 6291460
  76.7 1.6 collective-permute-start
  79.2 198.2 %all-gather.5.cloned.1.call-start = ((), (), s32[]{:S(2)}) async-start(), calls=%async_computation.2 | async-start | bytes 4718592 | tf_op jit(solution)/shard_map/all_gather | solution.py:548
  79.4 4.6 %collective-permute-start.2 = (bf16[4096,256]{1,0:T(8,128)(2,1)}, bf16[4096,256]{1,0:T(8,128)(2,1)}, u32[]{:S(2)}, u32[]{:S(2)}) collective-permute-start(bf16[4096,256]{1,0:T(8,128)(2,1)} %param.22), channel_id=1, source_target_pairs={{0,1},{1,0},{2,3},{3,2},{4,5},{5,4},{6,7},{7,6},{8,9},{9,8},{10,11... | collective-permute-start | bytes 6291464 | tf_op jit(solution)/shard_map/ppermute | solution.py:50
  79.6 7.6 %collective-permute-start.3 = (bf16[4096,256]{1,0:T(8,128)(2,1)}, bf16[4096,256]{1,0:T(8,128)(2,1)}, u32[]{:S(2)}, u32[]{:S(2)}) collective-permute-start(bf16[4096,256]{1,0:T(8,128)(2,1)} %param.20), channel_id=1, source_target_pairs={{0,1},{1,0},{2,3},{3,2},{4,5},{5,4},{6,7},{7,6},{8,9},{9,8},{10,11... | collective-permute-start | bytes 6291464 | tf_op jit(solution)/shard_map/ppermute | solution.py:50
  164.0 5.0 %collective-permute-start.4 = (bf16[2,512,256]{2,1,0:T(8,128)(2,1)}, bf16[2,512,256]{2,1,0:T(8,128)(2,1)S(1)}, u32[]{:S(2)}, u32[]{:S(2)}) collective-permute-start(bf16[2,512,256]{2,1,0:T(8,128)(2,1)} %get-tuple-element.10), channel_id=1, source_target_pairs={{0,1},{1,0},{2,3},{3,2},{4,5},{5,4},{6,7},{7,6},{8,9},{9,8},{10,11... | collective-permute-start | bytes 1572872 | tf_op jit(solution)/shard_map/ppermute | solution.py:50
  165.8 13.6 %collective-permute-start.5 = (bf16[2,512,256]{2,1,0:T(8,128)(2,1)S(1)}, bf16[2,512,256]{2,1,0:T(8,128)(2,1)S(1)}, u32[]{:S(2)}, u32[]{:S(2)}) collective-permute-start(bf16[2,512,256]{2,1,0:T(8,128)(2,1)S(1)} %get-tuple-element.9.refs_0_), channel_id=1, source_target_pairs={{0,16},{1,17},{16,0},{17,1},{2,18},{3,19},{18,2},{19,3},{4,20},{5,... | collective-permute-start | bytes 1572872 | tf_op jit(solution)/shard_map/ppermute | solution.py:531
  167.0 23.7 %collective-permute-start.6 = (bf16[2,512,256]{2,1,0:T(8,128)(2,1)}, bf16[2,512,256]{2,1,0:T(8,128)(2,1)S(1)}, u32[]{:S(2)}, u32[]{:S(2)}) collective-permute-start(bf16[2,512,256]{2,1,0:T(8,128)(2,1)} %get-tuple-element.10), channel_id=1, source_target_pairs={{0,17},{1,16},{16,1},{17,0},{2,19},{3,18},{18,3},{19,2},{4,21},{5,... | collective-permute-start | bytes 1572872 | tf_op jit(solution)/shard_map/ppermute | solution.py:531
  167.5 1.5 collective-permute-start.7
  169.0 27.9 %copy-start.8 = (bf16[2,512,256]{2,1,0:T(8,128)(2,1)}, bf16[2,512,256]{2,1,0:T(8,128)(2,1)S(1)}, u32[]{:S(2)}) copy-start(bf16[2,512,256]{2,1,0:T(8,128)(2,1)S(1)} %collective-permute-done.4.refs_1_) | copy-start | bytes 1572868
  179.4 17.6 %copy-start.10 = (bf16[2,512,256]{2,1,0:T(8,128)(2,1)}, bf16[2,512,256]{2,1,0:T(8,128)(2,1)S(1)}, u32[]{:S(2)}) copy-start(bf16[2,512,256]{2,1,0:T(8,128)(2,1)S(1)} %collective-permute-done.5.refs_2_) | copy-start | bytes 1572868
  190.7 6.2 %copy-start.12 = (bf16[2,512,256]{2,1,0:T(8,128)(2,1)}, bf16[2,512,256]{2,1,0:T(8,128)(2,1)S(1)}, u32[]{:S(2)}) copy-start(bf16[2,512,256]{2,1,0:T(8,128)(2,1)S(1)} %collective-permute-done.6.refs_3_) | copy-start | bytes 1572868
  196.6 9.7 %collective-permute-start.8 = (bf16[512,256]{1,0:T(8,128)(2,1)}, bf16[512,256]{1,0:T(8,128)(2,1)S(1)}, u32[]{:S(2)}, u32[]{:S(2)}) collective-permute-start(bf16[512,256]{1,0:T(8,128)(2,1)} %attention.3), channel_id=1, source_target_pairs={{0,1},{1,0},{2,3},{3,2},{4,5},{5,4},{6,7},{7,6},{8,9},{9,8},{10,11... | collective-permute-start | bytes 786440 | tf_op jit(solution)/shard_map/ppermute | solution.py:50
  201.0 6.2 %copy-start.1 = (bf16[4096,256]{1,0:T(8,128)(2,1)S(1)}, bf16[4096,256]{1,0:T(8,128)(2,1)}, u32[]{:S(2)}) copy-start(bf16[4096,256]{1,0:T(8,128)(2,1)} %own_w.1) | copy-start | bytes 6291460
  207.2 164.5 %reduce-scatter.2.cloned.1.call-start = ((), (), s32[]{:S(2)}) async-start(), calls=%async_computation.3 | async-start | bytes 2359296 | tf_op jit(solution)/shard_map/reduce_scatter | solution.py:571
  207.2 5.2 %collective-permute-start.9 = (bf16[4096,256]{1,0:T(8,128)(2,1)S(1)}, bf16[4096,256]{1,0:T(8,128)(2,1)S(1)}, u32[]{:S(2)}, u32[]{:S(2)}) collective-permute-start(bf16[4096,256]{1,0:T(8,128)(2,1)S(1)} %copy-done.1), channel_id=1, source_target_pairs={{0,1},{1,0},{2,3},{3,2},{4,5},{5,4},{6,7},{7,6},{8,9},{9,8},{10,11... | collective-permute-start | bytes 6291464 | tf_op jit(solution)/shard_map/ppermute | solution.py:50
  207.5 87.4 %collective-permute-start.14 = (bf16[256,4096]{1,0:T(8,128)(2,1)}, bf16[256,4096]{1,0:T(8,128)(2,1)}, u32[]{:S(2)}, u32[]{:S(2)}) collective-permute-start(bf16[256,4096]{1,0:T(8,128)(2,1)} %refs_4_.1), channel_id=1, source_target_pairs={{0,1},{1,0},{2,3},{3,2},{4,5},{5,4},{6,7},{7,6},{8,9},{9,8},{10,11... | collective-permute-start | bytes 6291464 | tf_op jit(solution)/shard_map/ppermute | solution.py:50
  285.8 15.2 %copy-start.4 = (bf16[256,4096]{1,0:T(8,128)(2,1)S(1)}, bf16[256,4096]{1,0:T(8,128)(2,1)}, u32[]{:S(2)}) copy-start(bf16[256,4096]{1,0:T(8,128)(2,1)} %refs_4_.1) | copy-start | bytes 6291460
  285.9 5.8 %collective-permute-start.10 = (bf16[512,256]{1,0:T(8,128)(2,1)S(1)}, bf16[512,256]{1,0:T(8,128)(2,1)S(1)}, u32[]{:S(2)}, u32[]{:S(2)}) collective-permute-start(bf16[512,256]{1,0:T(8,128)(2,1)S(1)} %get-tuple-element.13), channel_id=1, source_target_pairs={{0,1},{1,0},{2,3},{3,2},{4,5},{5,4},{6,7},{7,6},{8,9},{9,8},{10,11... | collective-permute-start | bytes 786440 | tf_op jit(solution)/shard_map/ppermute | solution.py:50
  293.0 5.1 %collective-permute-start.11 = (bf16[256,256]{1,0:T(8,128)(2,1)S(1)}, bf16[256,256]{1,0:T(8,128)(2,1)S(1)}, u32[]{:S(2)}, u32[]{:S(2)}) collective-permute-start(bf16[256,256]{1,0:T(8,128)(2,1)S(1)} %get-tuple-element.16), channel_id=1, source_target_pairs={{0,16},{1,17},{16,0},{17,1},{2,18},{3,19},{18,2},{19,3},{4,20},{5,... | collective-permute-start | bytes 393224 | tf_op jit(solution)/shard_map/ppermute | solution.py:531
  294.2 3.9 collective-permute-start.12
  294.6 6.5 %collective-permute-start.13 = (bf16[256,256]{1,0:T(8,128)(2,1)S(1)}, bf16[256,256]{1,0:T(8,128)(2,1)S(1)}, u32[]{:S(2)}, u32[]{:S(2)}) collective-permute-start(bf16[256,256]{1,0:T(8,128)(2,1)S(1)} %get-tuple-element.14), channel_id=1, source_target_pairs={{0,17},{1,16},{16,1},{17,0},{2,19},{3,18},{18,3},{19,2},{4,21},{5,... | collective-permute-start | bytes 393224 | tf_op jit(solution)/shard_map/ppermute | solution.py:531
  373.5 4.6 %collective-permute-start.15 = (f32[64,128]{1,0:T(8,128)S(1)}, f32[64,128]{1,0:T(8,128)S(1)}, u32[]{:S(2)}, u32[]{:S(2)}) collective-permute-start(f32[64,128]{1,0:T(8,128)S(1)} %get-tuple-element.21), channel_id=1, source_target_pairs={{0,4},{4,8},{8,12},{12,0},{1,5},{5,9},{9,13},{13,1},{2,6},{6,10},{... | collective-permute-start | bytes 98312 | tf_op jit(solution)/shard_map/ppermute | solution.py:579
  374.5 4.3 %collective-permute-start.16 = (f32[64,128]{1,0:T(8,128)S(1)}, f32[64,128]{1,0:T(8,128)S(1)}, u32[]{:S(2)}, u32[]{:S(2)}) collective-permute-start(f32[64,128]{1,0:T(8,128)S(1)} %get-tuple-element.23), channel_id=1, source_target_pairs={{0,8},{4,12},{8,0},{12,4},{1,9},{5,13},{9,1},{13,5},{2,10},{6,14},... | collective-permute-start | bytes 98312 | tf_op jit(solution)/shard_map/ppermute | solution.py:579
  375.7 3.1 collective-permute-start.17
  378.8 3.1 collective-permute-start.18
  382.0 5.7 %collective-permute-start.19 = (f32[64,128]{1,0:T(8,128)S(1)}, f32[64,128]{1,0:T(8,128)S(1)}, u32[]{:S(2)}, u32[]{:S(2)}) collective-permute-start(f32[64,128]{1,0:T(8,128)S(1)} %add.205), channel_id=1, source_target_pairs={{0,1},{1,0},{2,3},{3,2},{4,5},{5,4},{6,7},{7,6},{8,9},{9,8},{10,11... | collective-permute-start | bytes 98312 | tf_op jit(solution)/shard_map/ppermute | solution.py:50
  (13 other events, 26.7 us)
Sparse Core Ops, SparseCore 0:
  79.3 67.9 all-gather.2
  207.3 69.9 all-gather.4
  308.0 63.6 reduce-scatter.1

commit v2 on v1

v2 whole, which is shorter than its diff:
```python
import functools

import jax
import jax.numpy as jnp
from jax import lax
from jax.experimental import pallas as pl
from jax.experimental.pallas import tpu as pltpu
from jax.sharding import Mesh
from jax.sharding import PartitionSpec as P

HD = 128
CH = 256
CIN = 8
WL = 64
HL = 64
PATCH = 4
PIX = PATCH * PATCH
SIDE = WL // PATCH
IMG_TOK = 256
EPSILON = 1e-05
NEGATIVE_FILL = -1e30
WINDOW = (PATCH + 2) * CIN
TAPS = 3 * WINDOW
BF16 = jnp.bfloat16
F32 = jnp.float32
VMEM_LIMIT = 48 * 1024 * 1024


def params(*semantics):
    return pltpu.CompilerParams(
        dimension_semantics=semantics or None, vmem_limit_bytes=VMEM_LIMIT
    )


def cost(flops, nbytes, transcendentals=0):
    return pl.CostEstimate(
        flops=int(flops), bytes_accessed=int(nbytes), transcendentals=int(transcendentals)
    )


def silu(values):
    return values / (1.0 + jnp.exp(-values))


def mxu(left, right):
    return jnp.dot(left, right, preferred_element_type=F32)


def swap(values):
    return lax.ppermute(values, "core", [(0, 1), (1, 0)])


def down_kernel(images, half, meta, rows_ref, conv_ref, patch_ref, text_ref, out_ref, windows, total):
    step = pl.program_id(0)
    group = images * SIDE

    @pl.when(step == 0)
    def _():
        for col in range(SIDE):
            for row in range(PATCH + 2):
                piece = rows_ref[row, :, PATCH * CIN * col : PATCH * CIN * col + WINDOW]
                for shift in range(3):
                    if 0 <= row - shift < PATCH:
                        windows[
                            row - shift,
                            group * col : group * (col + 1),
                            WINDOW * shift : WINDOW * (shift + 1),
                        ] = piece

    hidden = mxu(windows[step // PATCH], conv_ref[lax.rem(step, PATCH)])
    term = mxu(silu(hidden).astype(BF16), patch_ref[...])

    @pl.when(step == 0)
    def _():
        total[...] = term

    @pl.when(step > 0)
    def _():
        total[...] += term

    @pl.when(step == PIX - 1)
    def _():
        tokens = total[...].astype(BF16)
        first = meta[2 * images]
        core = meta[2 * images + 1]
        block = 256
        for part in range(2 * half // block):
            which = part * block // half
            base = first + jnp.where(which == 0, core, 1 - core) * half + part * block - which * half
            place = base + lax.broadcasted_iota(jnp.int32, (block, 1), 0)
            source = jnp.full((block, 1), -1, jnp.int32)
            for image in range(images):
                inner = place - meta[image]
                inside = (inner >= 0) & (inner < IMG_TOK)
                index = (inner & (SIDE - 1)) * group + meta[images + image] * SIDE + (inner >> 4)
                source = jnp.where(inside, index, source)
            choice = source == lax.broadcasted_iota(jnp.int32, (block, images * IMG_TOK), 1)
            picked = mxu(jnp.where(choice, 1.0, 0.0).astype(BF16), tokens).astype(BF16)
            at = part * block - which * half
            out_ref[which, at : at + block, :] = jnp.where(
                source >= 0, picked.astype(F32), text_ref[part * block : (part + 1) * block, :].astype(F32)
            ).astype(BF16)


def down_stream(meta, rows, conv, patch_in, text, images):
    seq_rows, width = text.shape
    half = seq_rows // 2
    count = images * IMG_TOK
    return pl.pallas_call(
        functools.partial(down_kernel, images, half),
        grid_spec=pltpu.PrefetchScalarGridSpec(
            num_scalar_prefetch=1,
            grid=(PIX,),
            in_specs=[
                pl.BlockSpec(rows.shape, lambda i, m: (0, 0, 0)),
                pl.BlockSpec(conv.shape, lambda i, m: (0, 0, 0)),
                pl.BlockSpec((CH, width), lambda i, m: (i, 0)),
                pl.BlockSpec((seq_rows, width), lambda i, m: (0, 0)),
            ],
            out_specs=pl.BlockSpec((2, half, width), lambda i, m: (0, 0, 0)),
            scratch_shapes=[
                pltpu.VMEM((PATCH, count, TAPS), BF16),
                pltpu.VMEM((count, width), F32),
            ],
        ),
        out_shape=jax.ShapeDtypeStruct((2, half, width), BF16),
        compiler_params=params("arbitrary"),
        cost_estimate=cost(2 * count * PIX * CH * (256 + width), 4 << 20, count * PIX * CH),
        name="down_stream",
    )(meta, rows, conv, patch_in, text)


def qkv_kernel(count, first, last, meta, *refs):
    refs = list(refs)
    x_refs = [refs.pop(0) for _ in range(count)]
    gain_refs = [refs.pop(0) for _ in range(count)]
    weight_refs = [[refs.pop(0) for _ in range(6)] for _ in range(count)]
    if not first:
        acc_in, square_in = refs.pop(0), refs.pop(0)
    if last:
        head_gains = refs.pop(0)
    scaled = refs.pop()
    half, span = x_refs[0].shape
    chunk = 64

    def scale_rows(index, carry):
        rows = pl.ds(pl.multiple_of(index * chunk, chunk), chunk)
        square = jnp.zeros((chunk, HD), F32) if first else square_in[rows, :]
        for block in range(count):
            value = x_refs[block][rows, :].astype(F32)
            scaled[block, rows, :] = (value * gain_refs[block][0].astype(F32)).astype(BF16)
            value = value * value
            for part in range(span // HD):
                square = square + value[:, part * HD : (part + 1) * HD]
        square_out[rows, :] = square
        return carry

    if last:
        square_out = refs.pop()
        outs = refs
    else:
        acc_out, square_out = refs
    lax.fori_loop(0, half // chunk, scale_rows, 0)
    width = weight_refs[0][0].shape[1]
    heads = width // HD
    if last:
        model = meta[count] * span
        mean = jnp.sum(square_out[...], axis=-1, keepdims=True) / model.astype(F32)
        scale = lax.rsqrt(mean + EPSILON)
    for part in range(6):
        total = None if first else acc_in[part]
        for block in range(count):
            term = mxu(scaled[block], weight_refs[block][part][...])
            total = term if total is None else total + term
        if not last:
            acc_out[part] = total
            continue
        total = total * scale
        side, kind = part // 3, part % 3
        kv_outs = outs[2 * heads * side : 2 * heads * side + heads]
        q_outs = outs[2 * heads * side + heads : 2 * heads * side + 2 * heads]
        for head in range(heads):
            raw = total[:, head * HD : (head + 1) * HD]
            if kind == 1:
                kv_outs[head][1] = raw.astype(BF16)
                continue
            raw = raw * lax.rsqrt(jnp.mean(raw * raw, axis=-1, keepdims=True) + EPSILON)
            if kind == 0:
                kv_outs[head][0] = (raw * head_gains[1:2, :]).astype(BF16)
            else:
                q_outs[head][...] = (raw * (head_gains[0:1, :] * HD ** (-0.5))).astype(BF16)


def full(shape):
    return pl.BlockSpec(shape, lambda i, m: (0,) * len(shape))


def qkv_step(blocks, chips, gain, weights, state, head_gains):
    half, span = blocks[0].shape
    width = weights[0].shape[1]
    heads = width // HD
    count, first, last = len(blocks), state is None, head_gains is not None
    groups = gain.shape[0]
    inputs, specs = list(blocks), [full(b.shape) for b in blocks]
    for index in range(count):
        inputs.append(gain)
        specs.append(pl.BlockSpec((1, 1, span), lambda i, m, index=index: (m[index], 0, 0)))
    for index in range(count):
        for weight in weights:
            inputs.append(weight)
            specs.append(pl.BlockSpec((span, width), lambda i, m, index=index: (m[index], 0)))
    if not first:
        inputs += list(state)
        specs += [full(s.shape) for s in state]
    scratch = [pltpu.VMEM((count, half, span), BF16)]
    if last:
        inputs.append(head_gains)
        specs.append(full(head_gains.shape))
        kv, q = jax.ShapeDtypeStruct((2, half, HD), BF16), jax.ShapeDtypeStruct((half, HD), BF16)
        outs = ([kv] * heads + [q] * heads) * 2
        scratch = [pltpu.VMEM((half, HD), F32)] + scratch
    else:
        outs = [
            jax.ShapeDtypeStruct((6, half, width), F32),
            jax.ShapeDtypeStruct((half, HD), F32),
        ]
    meta = jnp.stack(list(chips) + [jnp.int32(groups)]).astype(jnp.int32)
    return pl.pallas_call(
        functools.partial(qkv_kernel, count, first, last),
        grid_spec=pltpu.PrefetchScalarGridSpec(
            num_scalar_prefetch=1,
            grid=(1,),
            in_specs=specs,
            out_specs=[full(o.shape) for o in outs],
            scratch_shapes=scratch,
        ),
        out_shape=outs,
        compiler_params=params("arbitrary"),
        cost_estimate=cost(12 * count * half * span * width, (6 + 2 * count) << 20),
        name="qkv_last" if last else "qkv_step",
    )(meta, *inputs)


def attention_kernel(images, pieces, meta, *refs):
    q_refs, kv_refs, out_refs = refs[:2], refs[2 : 2 + pieces], refs[2 + pieces :]
    rows = q_refs[0].shape[0]
    step = pl.program_id(0)
    for side in range(2):
        place = meta[images + side] + step * rows + lax.broadcasted_iota(jnp.int32, (rows, 1), 0)
        limit = place
        for image in range(images):
            inner = place - meta[image]
            limit = jnp.where((inner >= 0) & (inner < IMG_TOK), meta[image] + IMG_TOK - 1, limit)
        query = q_refs[side][...]
        scores = []
        top = None
        for piece in range(pieces):
            score = lax.dot_general(
                query, kv_refs[piece][0], (((1,), (1,)), ((), ())), preferred_element_type=F32
            )
            position = lax.broadcasted_iota(jnp.int32, score.shape, 1)
            score = jnp.where(position <= limit - meta[images + 2 + piece], score, NEGATIVE_FILL)
            scores.append(score)
            best = jnp.max(score, axis=1, keepdims=True)
            top = best if top is None else jnp.maximum(top, best)
        total = jnp.zeros((rows, 1), F32)
        product = jnp.zeros((rows, HD), F32)
        for piece in range(pieces):
            weight = jnp.exp(scores[piece] - top)
            total = total + jnp.sum(weight, axis=1, keepdims=True)
            product = product + mxu(weight.astype(BF16), kv_refs[piece][1])
        out_refs[side][...] = (product / total).astype(BF16)


def attention(meta, queries, pieces, images):
    half = queries[0].shape[0]
    block = 256
    keys = half * len(pieces)
    rows = pl.BlockSpec((block, HD), lambda i, m: (i, 0))
    return pl.pallas_call(
        functools.partial(attention_kernel, images, len(pieces)),
        grid_spec=pltpu.PrefetchScalarGridSpec(
            num_scalar_prefetch=1,
            grid=(half // block,),
            in_specs=[rows, rows] + [full(p.shape) for p in pieces],
            out_specs=[rows, rows],
        ),
        out_shape=[jax.ShapeDtypeStruct((half, HD), BF16)] * 2,
        compiler_params=params("arbitrary"),
        cost_estimate=cost(8 * half * keys * HD, 4 * keys * HD, 2 * half * keys),
        name="attention",
    )(meta, *queries, *pieces)


def out_kernel(count, first, last, meta, *refs):
    x_refs, weight_refs = refs[:count], refs[count : 3 * count]
    if first:
        start, outs = refs[3 * count : 3 * count + 2], refs[3 * count + 2 :]
    else:
        start, outs = [refs[3 * count].at[0], refs[3 * count].at[1]], refs[3 * count + 1 :]
    for side in range(2):
        total = start[side][...].astype(F32)
        for block in range(count):
            weight = weight_refs[2 * block + side][0, :, 0]
            total = total + mxu(x_refs[block][...], weight.reshape(2 * HD, weight.shape[2]))
        if last:
            outs[side][...] = total.astype(BF16)
        else:
            outs[0][side] = total


def out_step(blocks, chips, head, weights, state, last):
    half = blocks[0].shape[0]
    width = weights[0].shape[1]
    first = isinstance(state, tuple)
    count = len(blocks)
    views = [w.reshape(-1, 2, width // HD, HD, width) for w in weights]
    inputs, specs = list(blocks), [full(b.shape) for b in blocks]
    for index in range(count):
        for view in views:
            inputs.append(view)
            specs.append(
                pl.BlockSpec((1, 2, 1, HD, width), lambda i, m, index=index: (m[index], 0, head, 0, 0))
            )
    states = list(state) if first else [state]
    inputs += states
    specs += [full(s.shape) for s in states]
    if last:
        outs = [jax.ShapeDtypeStruct((half, width), BF16)] * 2
    else:
        outs = [jax.ShapeDtypeStruct((2, half, width), F32)]
    result = pl.pallas_call(
        functools.partial(out_kernel, count, first, last),
        grid_spec=pltpu.PrefetchScalarGridSpec(
            num_scalar_prefetch=1,
            grid=(1,),
            in_specs=specs,
            out_specs=[full(o.shape) for o in outs],
        ),
        out_shape=outs,
        compiler_params=params("arbitrary"),
        cost_estimate=cost(8 * count * half * HD * width, (2 + count) << 20),
        name="out_last" if last else "out_step",
    )(jnp.stack(list(chips)).astype(jnp.int32), *inputs)
    return result if last else result[0]


def pick_kernel(targets, meta, own_ref, par_ref, out_ref):
    half = own_ref.shape[0]
    own_base, par_base = meta[targets], meta[targets + 1]
    for target in range(targets):
        place = meta[target] + lax.broadcasted_iota(jnp.int32, (IMG_TOK, half), 0)
        column = lax.broadcasted_iota(jnp.int32, (IMG_TOK, half), 1)
        own = jnp.where(place == column + own_base, 1.0, 0.0).astype(BF16)
        par = jnp.where(place == column + par_base, 1.0, 0.0).astype(BF16)
        out_ref[target] = (mxu(own, own_ref[...]) + mxu(par, par_ref[...])).astype(BF16)


def pick_rows(meta, own, par, targets):
    half, width = own.shape
    whole = pl.BlockSpec((half, width), lambda i, m: (0, 0))
    return pl.pallas_call(
        functools.partial(pick_kernel, targets),
        grid_spec=pltpu.PrefetchScalarGridSpec(
            num_scalar_prefetch=1,
            grid=(1,),
            in_specs=[whole, whole],
            out_specs=pl.BlockSpec((targets, IMG_TOK, width), lambda i, m: (0, 0, 0)),
        ),
        out_shape=jax.ShapeDtypeStruct((targets, IMG_TOK, width), BF16),
        compiler_params=params("arbitrary"),
        cost_estimate=cost(targets * 4 * IMG_TOK * half * width, 1 << 20),
        name="pick_rows",
    )(meta, own, par)


def merge_kernel(*refs):
    out_ref = refs[-1]
    sides = refs[: len(refs) // 2], refs[len(refs) // 2 : -1]
    width = sides[0][0].shape[1]
    for side in range(2):
        total = sides[side][0][...].astype(F32)
        for part in sides[side][1:]:
            total = total + part[...].astype(F32)
        out_ref[:, side * width : (side + 1) * width] = total.astype(BF16)


def merge_picks(own_parts, par_parts):
    width = own_parts[0].shape[1]
    return pl.pallas_call(
        merge_kernel,
        out_shape=jax.ShapeDtypeStruct((IMG_TOK, 2 * width), BF16),
        compiler_params=params(),
        cost_estimate=cost(1 << 20, 1 << 20),
        name="merge_picks",
    )(*own_parts, *par_parts)


def spread(active, spread_ref):
    row = lax.broadcasted_iota(jnp.int32, (IMG_TOK, PIX * CIN), 0)
    patch_row, patch_col = row >> 4, row & (SIDE - 1)
    total = None
    for index in range(9):
        down, right = index // 3 - 1, index % 3 - 1
        part = mxu(active, spread_ref[:, index * PIX * CIN : (index + 1) * PIX * CIN])
        offset = down * SIDE + right
        if offset:
            part = pltpu.roll(part, offset % IMG_TOK, 0)
        source_row, source_col = patch_row - down, patch_col - right
        inside = (source_row >= 0) & (source_row < SIDE) & (source_col >= 0) & (source_col < SIDE)
        part = jnp.where(inside, part, 0.0)
        total = part if total is None else total + part
    return total


def up_kernel(count, halves, first, last, *refs):
    refs = list(refs)
    x_refs = [refs.pop(0) for _ in range(count)]
    weight_refs = [[[refs.pop(0) for _ in range(2)] for _ in range(halves)] for _ in range(count)]
    acc_in = None if first else refs.pop(0)
    spread_ref = refs.pop(0) if last else None
    out_ref = refs[0]
    width = x_refs[0].shape[1] // 2
    totals = []
    for part in range(halves):
        total = None if first else acc_in[part]
        for block in range(count):
            for side in range(2):
                term = mxu(
                    x_refs[block][:, side * width : (side + 1) * width],
                    weight_refs[block][part][side][0],
                )
                total = term if total is None else total + term
        totals.append(total)
        if not last:
            out_ref[part] = total
    if last:
        active = [silu(total).astype(BF16) for total in totals]
        active = jnp.concatenate(active, axis=1) if halves > 1 else active[0]
        out_ref[...] = spread(active, spread_ref)


def up_step(blocks, offsets, weights, state, spread_weight):
    span = blocks[0].shape[1]
    halves, count = len(weights), len(blocks)
    first, last = state is None, spread_weight is not None
    whole = lambda shape: pl.BlockSpec(shape, lambda i: (0,) * len(shape))
    inputs, specs = list(blocks), [whole(b.shape) for b in blocks]
    for offset in offsets:
        for sides in weights:
            for weight in sides:
                inputs.append(weight)
                specs.append(pl.BlockSpec((1, span // 2, CH), lambda i, offset=offset: (offset, 0, 0)))
    if not first:
        inputs.append(state)
        specs.append(whole(state.shape))
    if last:
        inputs.append(spread_weight)
        specs.append(whole(spread_weight.shape))
        out = jax.ShapeDtypeStruct((IMG_TOK, PIX * CIN), F32)
    else:
        out = jax.ShapeDtypeStruct((halves, IMG_TOK, CH), F32)
    return pl.pallas_call(
        functools.partial(up_kernel, count, halves, first, last),
        grid=(1,),
        in_specs=specs,
        out_specs=whole(out.shape),
        out_shape=out,
        compiler_params=params("arbitrary"),
        cost_estimate=cost(2 * count * IMG_TOK * span * CH * halves, (1 + count) << 20),
        name="up_last" if last else "up_step",
    )(*inputs)


def spread_weights(up_conv, pixels):
    taps = up_conv.reshape(9, CH, CIN).transpose(1, 0, 2).reshape(CH, 9 * CIN)
    shape = (pixels.shape[0], 9 * CIN, 9 * PIX * CIN)
    row = lax.broadcasted_iota(jnp.int32, shape, 1)
    col = lax.broadcasted_iota(jnp.int32, shape, 2)
    pixel = pixels[:, None, None]
    tap, channel = row >> 3, row & 7
    patch, target, out_channel = col >> 7, (col >> 3) & 15, col & 7
    tap_row, tap_col = tap // 3, tap % 3
    down, right = patch // 3 - 1, patch % 3 - 1
    hit = (
        (channel == out_channel)
        & ((pixel >> 2) + 1 - tap_row == (target >> 2) + PATCH * down)
        & ((pixel & 3) + 1 - tap_col == (target & 3) + PATCH * right)
    )
    placed = jnp.where(hit, 1.0, 0.0).astype(BF16)
    spread = jnp.einsum("ct,ptn->pcn", taps, placed, preferred_element_type=F32)
    return spread.astype(BF16).reshape(pixels.shape[0] * CH, 9 * PIX * CIN)


def by_core(core, own, other, axis):
    return jnp.where(
        core == 0, jnp.concatenate([own, other], axis), jnp.concatenate([other, own], axis)
    )


def shift(values, axis, step):
    count = lax.axis_size(axis)
    return lax.ppermute(values, axis, [(i, (i + step) % count) for i in range(count)])


def gather_small(latents, down_conv, norm_gain):
    ctxs, tiles = lax.axis_size("ctx"), lax.axis_size("tile")
    tile, mpo, core = (lax.axis_index(name) for name in ("tile", "mpo", "core"))
    local, height, breadth = latents.shape
    taps, channels = down_conv.shape
    width = norm_gain.shape[0]
    every = jnp.concatenate([latents] + [shift(latents, "ctx", s) for s in range(1, ctxs)])
    size = -(-(taps * channels + width) // 1024) * 1024
    flat = jnp.concatenate([down_conv.reshape(-1), norm_gain])
    flat = jnp.pad(flat, (0, size - flat.shape[0])).reshape(1, size // 128, 128)
    flat = by_core(core, flat, swap(flat), 0)[None]
    flat = by_core(mpo, flat, shift(flat, "mpo", 1), 0).reshape(4, size)
    conv = flat[:, : taps * channels].reshape(4, taps, channels)
    conv = conv.transpose(1, 0, 2).reshape(taps, 4 * channels)
    gain = flat[:, taps * channels : taps * channels + width].reshape(4 * width // 128, 128)
    rows = ctxs * local * height
    sent = every.reshape(rows * breadth // 128, 128)
    lines = sent.shape[0]
    pad = -gain.shape[0] % 16
    sent = jnp.concatenate([sent, jnp.pad(gain, ((0, pad), (0, 0)))])[None]
    turned = [shift(sent, "tile", s) for s in range(tiles - 1, 0, -1)] + [sent]
    whole = jnp.concatenate(turned + turned[:-1])
    whole = lax.dynamic_slice_in_dim(whole, tiles - 1 - tile, tiles, 0)
    images = whole[:, :lines].reshape(tiles, ctxs * local, height, breadth)
    images = images.transpose(1, 0, 2, 3).reshape(ctxs * local, tiles * height, breadth)
    gain = whole[:, lines : lines + gain.shape[0]].reshape(tiles * 2, 1, 2 * width)
    return images, conv, gain


def transpose_up(patch_out):
    ctxs, tiles, outer = (lax.axis_size(name) for name in ("ctx", "tile", "mpo"))
    ctx, tile, mpo = (lax.axis_index(name) for name in ("ctx", "tile", "mpo"))
    width, features = patch_out.shape
    deep = features // (tiles * outer)
    halves = 2 if ctxs == 2 and deep == 2 * CH else 1
    blocks = []
    for down in range(tiles):
        for right in range(outer):
            chip = lax.rem(tile + down, tiles) * outer + lax.rem(mpo + right, outer)
            start = chip * deep + (ctx * CH if halves == 2 else 0)
            block = lax.dynamic_slice_in_dim(patch_out, start, deep // halves, 1)
            if down or right:
                pairs = [
                    (t * outer + m, (t + down) % tiles * outer + (m + right) % outer)
                    for t in range(tiles)
                    for m in range(outer)
                ]
                block = lax.ppermute(block, ("tile", "mpo"), pairs)
            blocks.append(block)
    own = jnp.stack(blocks)
    weights = [own] if halves == 1 else [own, shift(own, "ctx", 1)]
    return [[weight, swap(weight)] for weight in weights]


def gather_chips(block):
    tiles = lax.axis_size("tile")
    blocks = []
    for step in range(tiles):
        if step:
            block = shift(block, "tile", 1)
        blocks += [block, shift(block, "mpo", 1)]
    return blocks


def arrivals(tiles):
    steps = [[0, 1] + ([2] if tiles > 1 else [])]
    for step in range(2, tiles):
        steps.append([2 * step, 2 * step - 1])
    return steps + [[2 * tiles - 1]]


def shards(
    text_embed,
    latents,
    down_conv,
    patch_in,
    norm_gain,
    query_weight,
    key_weight,
    value_weight,
    query_gain,
    key_gain,
    out_weight,
    patch_out,
    up_conv,
    span_start,
    image_of_slot,
):
    ctxs, tiles, outer = (lax.axis_size(name) for name in ("ctx", "tile", "mpo"))
    ctx, tile, mpo, core = (lax.axis_index(name) for name in ("ctx", "tile", "mpo", "core"))
    seq_rows, width = text_embed.shape
    half = seq_rows // 2
    heads = width // HD
    images = span_start.shape[0]
    local = latents.shape[0]

    every_latent, conv, gain = gather_small(latents, down_conv, norm_gain)
    weights = [swap(w) for w in (key_weight, value_weight, query_weight)]
    weights += [key_weight, value_weight, query_weight]
    out_par = swap(out_weight)
    up_weights = transpose_up(patch_out)

    numbers = jnp.arange(images, dtype=jnp.int32)
    matches = image_of_slot[None, :] == numbers[:, None]
    slot_of_image = jnp.sum(jnp.where(matches, numbers[None, :], 0), axis=1)
    slot_place = lax.rem(ctx + ctxs - slot_of_image // local, ctxs) * local + slot_of_image % local
    first = ctx * seq_rows
    stream_meta = jnp.concatenate([span_start, slot_place, jnp.stack([first, core])]).astype(jnp.int32)

    padded = jnp.pad(every_latent, ((0, 0), (1, 1), (CIN, 128 - CIN)))
    rows = jnp.stack(
        [padded[:, r : r + HL - PATCH + 1 : PATCH, :].reshape(images * SIDE, -1) for r in range(PATCH + 2)]
    )
    conv = conv.reshape(3, 3 * CIN, CH)
    conv = jnp.stack(
        [
            jnp.pad(conv, ((0, 0), (CIN * c, WINDOW - 3 * CIN - CIN * c), (0, 0))).reshape(TAPS, CH)
            for c in range(PATCH)
        ]
    )
    text = jnp.roll(text_embed.reshape(2, half, width), core, axis=0).reshape(seq_rows, width)
    stream = down_stream(stream_meta, rows, conv, patch_in, text, images)
    stream_own = stream[0]
    stream_par = swap(stream[1])

    def chip(index):
        return lax.rem(tile + tiles - index // 2, tiles) * outer + lax.rem(mpo + index % 2, outer)

    blocks = gather_chips(by_core(core, stream_own, stream_par, 1))
    head_gains = jnp.stack([query_gain, key_gain])
    state = None
    steps = arrivals(tiles)
    for step in steps:
        state = qkv_step(
            [blocks[b] for b in step],
            [chip(b) for b in step],
            gain,
            weights,
            state,
            head_gains if step is steps[-1] else None,
        )
    kv_send, q_send = state[:heads], state[heads : 2 * heads]
    kv_own, q_own = state[2 * heads : 3 * heads], state[3 * heads :]

    def shifted(values, step, cross):
        pairs = [
            (2 * c + k, 2 * ((c + step) % ctxs) + (1 - k if cross else k))
            for c in range(ctxs)
            for k in range(2)
        ]
        return lax.ppermute(values, ("ctx", "core"), pairs)

    bases = [first + core * half, first + (1 - core) * half]
    key_bases = list(bases)
    for step in range(1, ctxs):
        from_ctx = lax.rem(ctx + ctxs - step, ctxs) * seq_rows
        key_bases += [from_ctx + core * half, from_ctx + (1 - core) * half]
    spans = [span_start[i] for i in range(images)]
    att_meta = jnp.stack(spans + bases + key_bases).astype(jnp.int32)
    gathered = []
    for head in range(heads):
        q_par = swap(q_send[head])
        pieces = [kv_own[head], swap(kv_send[head])]
        for step in range(1, ctxs):
            pieces += [shifted(kv_own[head], step, False), shifted(kv_send[head], step, True)]
        att_own, att_send = attention(att_meta, [q_own[head], q_par], pieces, images)
        gathered.append(gather_chips(by_core(core, att_own, swap(att_send), 1)))
    state = (stream_own, stream_par)
    for head in range(heads):
        for step in steps:
            last = head == heads - 1 and step is steps[-1]
            state = out_step(
                [gathered[head][b] for b in step],
                [chip(b) for b in step],
                head,
                (out_weight, out_par),
                state,
                last,
            )
    out_own, out_send = state
    out_other = swap(out_send)
    layer_out = by_core(core, out_own, out_other, 0)

    starts = jnp.take(span_start, image_of_slot)
    wanted = []
    for step in range(ctxs):
        to_ctx = lax.rem(ctx + step, ctxs)
        wanted += [starts[2 * to_ctx + core], starts[2 * to_ctx + 1 - core]]
    pick_meta = jnp.stack(wanted + bases).astype(jnp.int32)
    picks = pick_rows(pick_meta, out_own, out_other, 2 * ctxs)
    own_parts, par_parts = [picks[0]], [swap(picks[1])]
    for step in range(1, ctxs):
        own_parts.append(shifted(picks[2 * step], step, False))
        par_parts.append(shifted(picks[2 * step + 1], step, True))

    blocks = gather_chips(merge_picks(own_parts, par_parts))
    halves = len(up_weights)
    pixel = tile * outer + mpo
    pixels = jnp.stack([pixel * halves + lax.rem(ctx + h, halves) for h in range(halves)])
    spread_weight = spread_weights(up_conv, pixels)
    state = None
    for step in steps:
        state = up_step(
            [blocks[b] for b in step], step, up_weights, state, spread_weight if step is steps[-1] else None
        )

    bands = state.reshape(tiles, IMG_TOK // tiles, PIX * CIN)
    band = lax.dynamic_index_in_dim(bands, tile, 0, keepdims=False)
    for step in range(1, tiles):
        piece = lax.dynamic_index_in_dim(bands, lax.rem(tile + step, tiles), 0, keepdims=False)
        band = band + shift(piece, "tile", step)
    summed = band
    for step in range(1, outer):
        summed = summed + shift(band, "mpo", step)
    slots = by_core(core, summed[None], swap(summed)[None], 0)
    noise = slots.reshape(2, SIDE // tiles, SIDE, PATCH, PATCH * CIN).transpose(0, 1, 3, 2, 4)
    return layer_out, noise.reshape(2, HL // tiles, WL * CIN)


def solution(mesh):
    ctxs, tiles, parts = mesh.devices.shape
    fine = Mesh(
        mesh.devices.reshape(ctxs, tiles, parts // 2, 2), ("ctx", "tile", "mpo", "core")
    )
    features = ("tile", "mpo", "core")
    return jax.shard_map(
        shards,
        mesh=fine,
        in_specs=(
            P("ctx", features),
            P("ctx", "tile", None),
            P(None, ("mpo", "core")),
            P(None, features),
            P(features),
            P(None, features),
            P(None, features),
            P(None, features),
            P(),
            P(),
            P(None, features),
            P(features, None),
            P(),
            P(),
            P(),
        ),
        out_specs=(P("ctx", features), P("ctx", "tile", None)),
        check_vma=False,
    )
```

time: 396 us -> 328 us (0.83)
  waiting for transfers between devices: 214 us -> 153 us
  starting transfers between devices: 19.3 us -> 65 us
  blocking collectives: 44.1 us -> 0 us
  Pallas kernels: 54.5 us -> 76.7 us
  local copies, waits for them, and re-layouts: 42 us -> 23 us
  between operations: 14.3 us -> 1.6 us
    ppermute x4 -> x45, waiting for transfers between devices: 3.46 us -> 136 us  [the longest x38 110 us: shift(): lax.ppermute(values, axis, [(i, (i + step) % count) for i in range(count)])]
    all_gather x2 -> x0, waiting for transfers between devices: 113 us -> none  [the longest x1 63.5 us: shards(): lax.all_gather(jnp.stack([att_own, att_par]), gather_axes, axis=0, tiled=...]
    reduce_scatter x1 -> x0, waiting for transfers between devices: 63 us -> none  [shards(): lax.psum_scatter(partial, gather_axes, scatter_dimension=0, tiled=True)]
    all_gather x1 -> x0, blocking collectives: 44.1 us -> none  [gather_small(): lax.all_gather(flat, ('ctx', 'tile', 'mpo', 'core'), axis=0, tiled=True)]
    ppermute x4 -> x45, starting transfers between devices: 4.98 us -> 43 us  [the longest x38 39 us: shift(): lax.ppermute(values, axis, [(i, (i + step) % count) for i in range(count)])]
    pallas_call x4 -> x17, Pallas kernels: 28.3 us -> 50.4 us  [the longest x4 27.9 us: qkv_step(): pl.pallas_call(functools.partial(qkv_kernel, count, first, last), grid_sp...]
    unnamed x56 -> x85, local copies, waits for them, and re-layouts: 27.7 us -> 12.8 us
    ppermute x4 -> x6, waiting for transfers between devices: 27.9 us -> 15.1 us  [shifted(): return lax.ppermute(values, ('ctx', 'core'), pairs)]
  transfers between devices with their start and end apart: 23 -> 68, of which waited for: 14 -> 33; matrix products, arithmetic and copies ran while one was open for 9% -> 5% of each run, Pallas kernels for 7% -> 18%
where the time goes in v2:
time: 328 us
  waiting for transfers between devices  153 us (47%)
  Pallas kernels  76.7 us (23%)
  starting transfers between devices  65 us (20%)
  local copies, waits for them, and re-layouts  23 us (7%)
  other arithmetic  6.74 us (2%)
    ppermute x38, waiting for transfers between devices, shift(): lax.ppermute(values, axis, [(i, (i + step) % count) for i in range(count)])  110 us
    ppermute x38, starting transfers between devices, shift(): lax.ppermute(values, axis, [(i, (i + step) % count) for i in range(count)])  39 us
    pallas_call x4, Pallas kernels, qkv_step(): pl.pallas_call(functools.partial(qkv_kernel, count, first, last), grid_sp...  27.9 us
    ppermute x7, waiting for transfers between devices, transpose_up(): block = lax.ppermute(block, ('tile', 'mpo'), pairs)  25.9 us
    ppermute x17, starting transfers between devices, swap(): return lax.ppermute(values, 'core', [(0, 1), (1, 0)])  18.2 us
    pallas_call x8, Pallas kernels, out_step(): pl.pallas_call(functools.partial(out_kernel, count, first, last), grid_sp...  15.3 us
    ppermute x6, waiting for transfers between devices, shifted(): return lax.ppermute(values, ('ctx', 'core'), pairs)  15.1 us
    pallas_call x1, Pallas kernels, down_stream(): pl.pallas_call(functools.partial(down_kernel, images, half), grid_spec=pl...  13.9 us
  transfers between devices with their start and end apart: 68, of which 33 were waited for; matrix products, arithmetic and copies ran while one was open for 5% of the time, Pallas kernels for 18%

profile of v2, /device:TPU:1, one launch (start us, length us, event | category | flops | bytes accessed | tf_op | source)
XLA Modules:
  0.0 327.7 jit_solution(2463799716104402188)
XLA Ops:
  10.2 3.4 %collective-permute-start.3 = (bf16[1,272,128]{2,1,0:T(8,128)(2,1)S(1)}, bf16[1,272,128]{2,1,0:T(8,128)(2,1)S(1)}, u32[]{:S(2)}, u32[]{:S(2)}) collective-permute-start(bf16[1,272,128]{2,1,0:T(8,128)(2,1)S(1)} %fusion.28), channel_id=1, source_target_pairs={{0,12},{4,0},{8,4},{12,8},{1,13},{5,1},{9,5},{13,9},{2,14},{6,2},{... | collective-permute-start | bytes 208904 | tf_op jit(solution)/shard_map/ppermute | solution.py:503
  15.0 4.3 %collective-permute-done.4 = bf16[1,272,128]{2,1,0:T(8,128)(2,1)S(1)} collective-permute-done((bf16[1,272,128]{2,1,0:T(8,128)(2,1)S(1)}, bf16[1,272,128]{2,1,0:T(8,128)(2,1)S(1)}, u32[]{:S(2)}, u32[]{:S(2)}) %collective-permute-start.4) | collective-permute-done | bytes 69664 | tf_op jit(solution)/shard_map/ppermute | solution.py:503
  23.7 13.9 %down_stream.1 = bf16[2,512,256]{2,1,0:T(8,128)(2,1)S(1)} custom-call(s32[10]{0:T(128)S(1)} %pad_add_fusion.3.meta, bf16[6,64,640]{2,1,0:T(8,128)(2,1)S(1)} %bitcast_dynamic-update-slice_fusion.8.rows_ref, bf16[4,144,256]{2,1,0:T(8,128)(2,1)S(1)} %pad_maximum_fusion.conv_ref, bf16[4096,256]{1,0:T(8,128)(2,1)S(1)} %copy-done.8, bf16[1024,256]{1,0:T(8,128)(2,1)S(1)} %bitcast.136), custom_call_target="tpu_custom_call" | custom-call | flops 4294967296 | bytes 4194304 | tf_op jit(solution)/shard_map/down_stream/pallas_call | solution.py:109
  41.5 14.9 %collective-permute-done.7.refs_2_ = bf16[512,512]{1,0:T(8,128)(2,1)S(1)} collective-permute-done((bf16[512,512]{1,0:T(8,128)(2,1)S(1)}, bf16[512,512]{1,0:T(8,128)(2,1)S(1)}, u32[]{:S(2)}, u32[]{:S(2)}) %collective-permute-start.7) | collective-permute-done | bytes 524320 | tf_op jit(solution)/shard_map/ppermute | solution.py:503
  58.4 12.9 %collective-permute-done.8.refs_0_ = bf16[512,512]{1,0:T(8,128)(2,1)} collective-permute-done((bf16[512,512]{1,0:T(8,128)(2,1)S(1)}, bf16[512,512]{1,0:T(8,128)(2,1)}, u32[]{:S(2)}, u32[]{:S(2)}) %collective-permute-start.8) | collective-permute-done | bytes 524320 | tf_op jit(solution)/shard_map/ppermute | solution.py:503
  72.9 11.9 %collective-permute-done.9.refs_0_ = bf16[512,512]{1,0:T(8,128)(2,1)} collective-permute-done((bf16[512,512]{1,0:T(8,128)(2,1)}, bf16[512,512]{1,0:T(8,128)(2,1)}, u32[]{:S(2)}, u32[]{:S(2)}) %collective-permute-start.9) | collective-permute-done | bytes 524320 | tf_op jit(solution)/shard_map/ppermute | solution.py:503
  86.7 3.4 %collective-permute-start.26 = (bf16[4096,256]{1,0:T(8,128)(2,1)S(1)}, bf16[4096,256]{1,0:T(8,128)(2,1)}, u32[]{:S(2)}, u32[]{:S(2)}) collective-permute-start(bf16[4096,256]{1,0:T(8,128)(2,1)S(1)} %copy-done.1), channel_id=1, source_target_pairs={{0,1},{1,0},{2,3},{3,2},{4,5},{5,4},{6,7},{7,6},{8,9},{9,8},{10,11... | collective-permute-start | bytes 6291464 | tf_op jit(solution)/shard_map/ppermute | solution.py:50
  91.5 7.8 %qkv_step.3 = (f32[6,512,256]{2,1,0:T(8,128)}, f32[512,128]{1,0:T(8,128)S(1)}) custom-call(s32[4]{0:T(128)S(1)} %pad_add_fusion.4.meta, bf16[512,512]{1,0:T(8,128)(2,1)S(1)} %maximum_select_fusion.refs_0_, bf16[512,512]{1,0:T(8,128)(2,1)} %collective-permute-done.16.refs_1_, bf16[512,512]{1,0:T(8,128)(2,1)S(1)} %copy-done.5, ...), custom_call_target="tpu_custom_call" | custom-call | flops 2415919104 | bytes 12582912 | tf_op jit(solution)/shard_map/qkv_step/pallas_call | solution.py:228
  99.3 7.5 %qkv_step.4 = (f32[6,512,256]{2,1,0:T(8,128)}, f32[512,128]{1,0:T(8,128)S(1)}) custom-call(s32[3]{0:T(128)S(1)} %pad_add_fusion.meta, bf16[512,512]{1,0:T(8,128)(2,1)} %collective-permute-done.8.refs_0_, bf16[512,512]{1,0:T(8,128)(2,1)} %collective-permute-done.15.refs_1_, bf16[8,1,512]{2,1,0:T(2,128)(2,1)S(1)} %reshape.213.refs_3_.refs_4_.refs_5_.refs_2_.refs_1_, ...), custom_call_target="tpu_custom_call" | custom-call | flops 1610612736 | bytes 10485760 | tf_op jit(solution)/shard_map/qkv_step/pallas_call | solution.py:228
  106.8 7.6 %qkv_step.5 = (f32[6,512,256]{2,1,0:T(8,128)}, f32[512,128]{1,0:T(8,128)S(1)}) custom-call(s32[3]{0:T(128)S(1)} %pad_add_fusion.1.meta, bf16[512,512]{1,0:T(8,128)(2,1)} %collective-permute-done.9.refs_0_, bf16[512,512]{1,0:T(8,128)(2,1)} %collective-permute-done.14.refs_1_, bf16[8,1,512]{2,1,0:T(2,128)(2,1)S(1)} %reshape.213.refs_3_.refs_4_.refs_5_.refs_2_.refs_1_, ...), custom_call_target="tpu_custom_call" | custom-call | flops 1610612736 | bytes 10485760 | tf_op jit(solution)/shard_map/qkv_step/pallas_call | solution.py:228
  114.4 5.0 %qkv_last.1 = (bf16[2,512,128]{2,1,0:T(8,128)(2,1)}, bf16[2,512,128]{2,1,0:T(8,128)(2,1)S(1)}, bf16[512,128]{1,0:T(8,128)(2,1)S(1)}, bf16[512,128]{1,0:T(8,128)(...) custom-call(s32[2]{0:T(128)S(1)} %pad_add_fusion.2.meta, ...), custom_call_target="tpu_custom_call" | custom-call | flops 805306368 | bytes 8388608 | tf_op jit(solution)/shard_map/qkv_last/pallas_call | solution.py:228
  132.2 6.4 %collective-permute-done.33.refs_5_ = bf16[2,512,128]{2,1,0:T(8,128)(2,1)} collective-permute-done((bf16[2,512,128]{2,1,0:T(8,128)(2,1)}, bf16[2,512,128]{2,1,0:T(8,128)(2,1)}, u32[]{:S(2)}, u32[]{:S(2)}) %collective-permute-start.33) | collective-permute-done | bytes 262176 | tf_op jit(solution)/shard_map/ppermute | solution.py:656
  140.7 5.6 %attention.3 = (bf16[512,128]{1,0:T(8,128)(2,1)S(1)}, bf16[512,128]{1,0:T(8,128)(2,1)S(1)}) custom-call(s32[10]{0:T(128)S(1)} %stack.148.meta, bf16[512,128]{1,0:T(8,128)(2,1)S(1)} %copy-done.16, bf16[512,128]{1,0:T(8,128)(2,1)S(1)} %copy-done.19, bf16[2,512,128]{2,1,0:T(8,128)(2,1)} %get-tuple-element.36.refs_2_, ...), custom_call_target="tpu_custom_call" | custom-call | flops 1073741824 | bytes 1048576 | tf_op jit(solution)/shard_map/attention/pallas_call | solution.py:280
  149.8 5.6 %attention.2 = (bf16[512,128]{1,0:T(8,128)(2,1)S(1)}, bf16[512,128]{1,0:T(8,128)(2,1)S(1)}) custom-call(s32[10]{0:T(128)S(1)} %stack.148.meta, bf16[512,128]{1,0:T(8,128)(2,1)S(1)} %copy-done.13, bf16[512,128]{1,0:T(8,128)(2,1)} %collective-permute-done.17.refs_1_, bf16[2,512,128]{2,1,0:T(8,128)(2,1)S(1)} %copy-done.10, ...), custom_call_target="tpu_custom_call" | custom-call | flops 1073741824 | bytes 1048576 | tf_op jit(solution)/shard_map/attention/pallas_call | solution.py:280
  160.6 7.9 %collective-permute-done.35.refs_2_ = bf16[512,256]{1,0:T(8,128)(2,1)S(1)} collective-permute-done((bf16[512,256]{1,0:T(8,128)(2,1)S(1)}, bf16[512,256]{1,0:T(8,128)(2,1)S(1)}, u32[]{:S(2)}, u32[]{:S(2)}) %collective-permute-start.35) | collective-permute-done | bytes 262176 | tf_op jit(solution)/shard_map/ppermute | solution.py:503
  169.2 4.9 %collective-permute-done.22.refs_2_ = bf16[512,256]{1,0:T(8,128)(2,1)S(1)} collective-permute-done((bf16[512,256]{1,0:T(8,128)(2,1)S(1)}, bf16[512,256]{1,0:T(8,128)(2,1)S(1)}, u32[]{:S(2)}, u32[]{:S(2)}) %collective-permute-start.22) | collective-permute-done | bytes 262176 | tf_op jit(solution)/shard_map/ppermute | solution.py:503
  174.1 20.4 %collective-permute-done.53 = bf16[256,256]{1,0:T(8,128)(2,1)S(1)} collective-permute-done((bf16[256,256]{1,0:T(8,128)(2,1)S(1)}, bf16[256,256]{1,0:T(8,128)(2,1)S(1)}, u32[]{:S(2)}, u32[]{:S(2)}) %collective-permute-start.53) | collective-permute-done | bytes 131104 | tf_op jit(solution)/shard_map/ppermute | solution.py:553
  194.6 2.8 collective-permute-done.54
  202.7 6.8 %collective-permute-start.40 = (bf16[512,256]{1,0:T(8,128)(2,1)S(1)}, bf16[512,256]{1,0:T(8,128)(2,1)S(1)}, u32[]{:S(2)}, u32[]{:S(2)}) collective-permute-start(bf16[512,256]{1,0:T(8,128)(2,1)S(1)} %collective-permute-done.35.refs_2_), channel_id=1, source_target_pairs={{0,2},{2,0},{1,3},{3,1},{4,6},{6,4},{5,7},{7,5},{8,10},{10,8},{9,1... | collective-permute-start | bytes 786440 | tf_op jit(solution)/shard_map/ppermute | solution.py:503
  215.9 3.9 %collective-permute-done.39.refs_1_ = bf16[512,256]{1,0:T(8,128)(2,1)S(1)} collective-permute-done((bf16[512,256]{1,0:T(8,128)(2,1)S(1)}, bf16[512,256]{1,0:T(8,128)(2,1)S(1)}, u32[]{:S(2)}, u32[]{:S(2)}) %collective-permute-start.39) | collective-permute-done | bytes 262176 | tf_op jit(solution)/shard_map/ppermute | solution.py:503
  221.6 3.8 %collective-permute-done.38.refs_0_ = bf16[512,256]{1,0:T(8,128)(2,1)S(1)} collective-permute-done((bf16[512,256]{1,0:T(8,128)(2,1)S(1)}, bf16[512,256]{1,0:T(8,128)(2,1)S(1)}, u32[]{:S(2)}, u32[]{:S(2)}) %collective-permute-start.38) | collective-permute-done | bytes 262176 | tf_op jit(solution)/shard_map/ppermute | solution.py:503
  238.7 3.6 %collective-permute-done.27.refs_1_ = bf16[512,256]{1,0:T(8,128)(2,1)S(1)} collective-permute-done((bf16[512,256]{1,0:T(8,128)(2,1)S(1)}, bf16[512,256]{1,0:T(8,128)(2,1)S(1)}, u32[]{:S(2)}, u32[]{:S(2)}) %collective-permute-start.27) | collective-permute-done | bytes 262176 | tf_op jit(solution)/shard_map/ppermute | solution.py:503
  244.3 3.6 %collective-permute-done.25.refs_0_ = bf16[512,256]{1,0:T(8,128)(2,1)S(1)} collective-permute-done((bf16[512,256]{1,0:T(8,128)(2,1)S(1)}, bf16[512,256]{1,0:T(8,128)(2,1)S(1)}, u32[]{:S(2)}, u32[]{:S(2)}) %collective-permute-start.25) | collective-permute-done | bytes 262176 | tf_op jit(solution)/shard_map/ppermute | solution.py:503
  259.9 2.9 collective-permute-done.43.refs_1_
  262.8 2.9 collective-permute-done.45.refs_3_
  267.0 8.4 %collective-permute-done.46.refs_2_ = bf16[256,512]{1,0:T(8,128)(2,1)} collective-permute-done((bf16[256,512]{1,0:T(8,128)(2,1)S(1)}, bf16[256,512]{1,0:T(8,128)(2,1)}, u32[]{:S(2)}, u32[]{:S(2)}) %collective-permute-start.46) | collective-permute-done | bytes 262176 | tf_op jit(solution)/shard_map/ppermute | solution.py:503
  275.5 8.8 %collective-permute-done.47.refs_0_ = bf16[256,512]{1,0:T(8,128)(2,1)} collective-permute-done((bf16[256,512]{1,0:T(8,128)(2,1)}, bf16[256,512]{1,0:T(8,128)(2,1)}, u32[]{:S(2)}, u32[]{:S(2)}) %collective-permute-start.47) | collective-permute-done | bytes 262176 | tf_op jit(solution)/shard_map/ppermute | solution.py:503
  287.3 4.9 %collective-permute-done.48.refs_0_ = bf16[256,512]{1,0:T(8,128)(2,1)} collective-permute-done((bf16[256,512]{1,0:T(8,128)(2,1)}, bf16[256,512]{1,0:T(8,128)(2,1)}, u32[]{:S(2)}, u32[]{:S(2)}) %collective-permute-start.48) | collective-permute-done | bytes 262176 | tf_op jit(solution)/shard_map/ppermute | solution.py:503
  298.5 2.9 collective-permute-done.60.refs_1_
  302.9 4.1 %collective-permute-done.49.refs_0_ = bf16[256,512]{1,0:T(8,128)(2,1)S(1)} collective-permute-done((bf16[256,512]{1,0:T(8,128)(2,1)}, bf16[256,512]{1,0:T(8,128)(2,1)S(1)}, u32[]{:S(2)}, u32[]{:S(2)}) %collective-permute-start.49) | collective-permute-done | bytes 262176 | tf_op jit(solution)/shard_map/ppermute | solution.py:503
  309.5 3.3 collective-permute-start.64
  318.4 6.0 %collective-permute-start.67 = (f32[64,128]{1,0:T(8,128)S(1)}, f32[64,128]{1,0:T(8,128)S(1)}, u32[]{:S(2)}, u32[]{:S(2)}) collective-permute-start(f32[64,128]{1,0:T(8,128)S(1)} %add.383), channel_id=1, source_target_pairs={{0,1},{1,0},{2,3},{3,2},{4,5},{5,4},{6,7},{7,6},{8,9},{9,8},{10,11... | collective-permute-start | bytes 98312 | tf_op jit(solution)/shard_map/ppermute | solution.py:50
  (286 shorter events, 113.9 us)
Async XLA Ops:
  40.1 46.6 %collective-permute-start.11 = (bf16[4096,256]{1,0:T(8,128)(2,1)}, bf16[4096,256]{1,0:T(8,128)(2,1)}, u32[]{:S(2)}, u32[]{:S(2)}) collective-permute-start(bf16[4096,256]{1,0:T(8,128)(2,1)} %refs_5_.1), channel_id=1, source_target_pairs={{0,1},{1,0},{2,3},{3,2},{4,5},{5,4},{6,7},{7,6},{8,9},{9,8},{10,11... | collective-permute-start | bytes 6291464 | tf_op jit(solution)/shard_map/ppermute | solution.py:50
  40.2 49.9 %collective-permute-start.12 = (bf16[4096,256]{1,0:T(8,128)(2,1)}, bf16[4096,256]{1,0:T(8,128)(2,1)}, u32[]{:S(2)}, u32[]{:S(2)}) collective-permute-start(bf16[4096,256]{1,0:T(8,128)(2,1)} %refs_6_.1), channel_id=1, source_target_pairs={{0,1},{1,0},{2,3},{3,2},{4,5},{5,4},{6,7},{7,6},{8,9},{9,8},{10,11... | collective-permute-start | bytes 6291464 | tf_op jit(solution)/shard_map/ppermute | solution.py:50
  40.7 49.8 %collective-permute-start.13 = (bf16[4096,256]{1,0:T(8,128)(2,1)}, bf16[4096,256]{1,0:T(8,128)(2,1)}, u32[]{:S(2)}, u32[]{:S(2)}) collective-permute-start(bf16[4096,256]{1,0:T(8,128)(2,1)} %refs_7_.5), channel_id=1, source_target_pairs={{0,1},{1,0},{2,3},{3,2},{4,5},{5,4},{6,7},{7,6},{8,9},{9,8},{10,11... | collective-permute-start | bytes 6291464 | tf_op jit(solution)/shard_map/ppermute | solution.py:50
  41.4 15.0 %collective-permute-start.7 = (bf16[512,512]{1,0:T(8,128)(2,1)S(1)}, bf16[512,512]{1,0:T(8,128)(2,1)S(1)}, u32[]{:S(2)}, u32[]{:S(2)}) collective-permute-start(bf16[512,512]{1,0:T(8,128)(2,1)S(1)} %maximum_select_fusion.refs_0_), channel_id=1, source_target_pairs={{0,4},{4,8},{8,12},{12,0},{1,5},{5,9},{9,13},{13,1},{2,6},{6,10},{... | collective-permute-start | bytes 1572872 | tf_op jit(solution)/shard_map/ppermute | solution.py:503
  57.2 14.1 %collective-permute-start.8 = (bf16[512,512]{1,0:T(8,128)(2,1)S(1)}, bf16[512,512]{1,0:T(8,128)(2,1)}, u32[]{:S(2)}, u32[]{:S(2)}) collective-permute-start(bf16[512,512]{1,0:T(8,128)(2,1)S(1)} %collective-permute-done.7.refs_2_), channel_id=1, source_target_pairs={{0,4},{4,8},{8,12},{12,0},{1,5},{5,9},{9,13},{13,1},{2,6},{6,10},{... | collective-permute-start | bytes 1572872 | tf_op jit(solution)/shard_map/ppermute | solution.py:503
  57.2 14.3 %collective-permute-start.16 = (bf16[512,512]{1,0:T(8,128)(2,1)S(1)}, bf16[512,512]{1,0:T(8,128)(2,1)}, u32[]{:S(2)}, u32[]{:S(2)}) collective-permute-start(bf16[512,512]{1,0:T(8,128)(2,1)S(1)} %maximum_select_fusion.refs_0_), channel_id=1, source_target_pairs={{0,2},{2,0},{1,3},{3,1},{4,6},{6,4},{5,7},{7,5},{8,10},{10,8},{9,1... | collective-permute-start | bytes 1572872 | tf_op jit(solution)/shard_map/ppermute | solution.py:503
  71.3 13.4 %collective-permute-start.9 = (bf16[512,512]{1,0:T(8,128)(2,1)}, bf16[512,512]{1,0:T(8,128)(2,1)}, u32[]{:S(2)}, u32[]{:S(2)}) collective-permute-start(bf16[512,512]{1,0:T(8,128)(2,1)} %collective-permute-done.8.refs_0_), channel_id=1, source_target_pairs={{0,4},{4,8},{8,12},{12,0},{1,5},{5,9},{9,13},{13,1},{2,6},{6,10},{... | collective-permute-start | bytes 1572872 | tf_op jit(solution)/shard_map/ppermute | solution.py:503
  71.5 27.7 %collective-permute-start.15 = (bf16[512,512]{1,0:T(8,128)(2,1)}, bf16[512,512]{1,0:T(8,128)(2,1)}, u32[]{:S(2)}, u32[]{:S(2)}) collective-permute-start(bf16[512,512]{1,0:T(8,128)(2,1)} %copy-done.4), channel_id=1, source_target_pairs={{0,2},{2,0},{1,3},{3,1},{4,6},{6,4},{5,7},{7,5},{8,10},{10,8},{9,1... | collective-permute-start | bytes 1572872 | tf_op jit(solution)/shard_map/ppermute | solution.py:503
  84.7 22.1 %collective-permute-start.14 = (bf16[512,512]{1,0:T(8,128)(2,1)}, bf16[512,512]{1,0:T(8,128)(2,1)}, u32[]{:S(2)}, u32[]{:S(2)}) collective-permute-start(bf16[512,512]{1,0:T(8,128)(2,1)} %collective-permute-done.8.refs_0_), channel_id=1, source_target_pairs={{0,2},{2,0},{1,3},{3,1},{4,6},{6,4},{5,7},{7,5},{8,10},{10,8},{9,1... | collective-permute-start | bytes 1572872 | tf_op jit(solution)/shard_map/ppermute | solution.py:503
  86.7 122.8 %collective-permute-start.26 = (bf16[4096,256]{1,0:T(8,128)(2,1)S(1)}, bf16[4096,256]{1,0:T(8,128)(2,1)}, u32[]{:S(2)}, u32[]{:S(2)}) collective-permute-start(bf16[4096,256]{1,0:T(8,128)(2,1)S(1)} %copy-done.1), channel_id=1, source_target_pairs={{0,1},{1,0},{2,3},{3,2},{4,5},{5,4},{6,7},{7,6},{8,9},{9,8},{10,11... | collective-permute-start | bytes 6291464 | tf_op jit(solution)/shard_map/ppermute | solution.py:50
  90.1 24.2 %collective-permute-start.10 = (bf16[512,512]{1,0:T(8,128)(2,1)}, bf16[512,512]{1,0:T(8,128)(2,1)S(1)}, u32[]{:S(2)}, u32[]{:S(2)}) collective-permute-start(bf16[512,512]{1,0:T(8,128)(2,1)} %collective-permute-done.9.refs_0_), channel_id=1, source_target_pairs={{0,2},{2,0},{1,3},{3,1},{4,6},{6,4},{5,7},{7,5},{8,10},{10,8},{9,1... | collective-permute-start | bytes 1572872 | tf_op jit(solution)/shard_map/ppermute | solution.py:503
  124.0 14.6 %collective-permute-start.33 = (bf16[2,512,128]{2,1,0:T(8,128)(2,1)}, bf16[2,512,128]{2,1,0:T(8,128)(2,1)}, u32[]{:S(2)}, u32[]{:S(2)}) collective-permute-start(bf16[2,512,128]{2,1,0:T(8,128)(2,1)} %get-tuple-element.37), channel_id=1, source_target_pairs={{0,17},{1,16},{16,1},{17,0},{2,19},{3,18},{18,3},{19,2},{4,21},{5,... | collective-permute-start | bytes 786440 | tf_op jit(solution)/shard_map/ppermute | solution.py:656
  129.6 18.0 %collective-permute-start.18 = (bf16[2,512,128]{2,1,0:T(8,128)(2,1)}, bf16[2,512,128]{2,1,0:T(8,128)(2,1)}, u32[]{:S(2)}, u32[]{:S(2)}) collective-permute-start(bf16[2,512,128]{2,1,0:T(8,128)(2,1)} %copy-done.11), channel_id=1, source_target_pairs={{0,1},{1,0},{2,3},{3,2},{4,5},{5,4},{6,7},{7,6},{8,9},{9,8},{10,11... | collective-permute-start | bytes 786440 | tf_op jit(solution)/shard_map/ppermute | solution.py:50
  130.0 19.7 %collective-permute-start.20 = (bf16[2,512,128]{2,1,0:T(8,128)(2,1)}, bf16[2,512,128]{2,1,0:T(8,128)(2,1)}, u32[]{:S(2)}, u32[]{:S(2)}) collective-permute-start(bf16[2,512,128]{2,1,0:T(8,128)(2,1)} %copy-done.11), channel_id=1, source_target_pairs={{0,17},{1,16},{16,1},{17,0},{2,19},{3,18},{18,3},{19,2},{4,21},{5,... | collective-permute-start | bytes 786440 | tf_op jit(solution)/shard_map/ppermute | solution.py:656
  131.9 16.9 %collective-permute-start.19 = (bf16[2,512,128]{2,1,0:T(8,128)(2,1)}, bf16[2,512,128]{2,1,0:T(8,128)(2,1)}, u32[]{:S(2)}, u32[]{:S(2)}) collective-permute-start(bf16[2,512,128]{2,1,0:T(8,128)(2,1)} %copy-done.9), channel_id=1, source_target_pairs={{0,16},{1,17},{16,0},{17,1},{2,18},{3,19},{18,2},{19,3},{4,20},{5,... | collective-permute-start | bytes 786440 | tf_op jit(solution)/shard_map/ppermute | solution.py:656
  155.5 13.0 %collective-permute-start.52 = (bf16[256,256]{1,0:T(8,128)(2,1)S(1)}, bf16[256,256]{1,0:T(8,128)(2,1)S(1)}, u32[]{:S(2)}, u32[]{:S(2)}) collective-permute-start(bf16[256,256]{1,0:T(8,128)(2,1)S(1)} %copy-done.26), channel_id=1, source_target_pairs={{0,6},{2,4},{4,10},{6,8},{8,14},{10,12},{12,2},{14,0},{1,7},{3,5},... | collective-permute-start | bytes 393224 | tf_op jit(solution)/shard_map/ppermute | solution.py:553
  156.9 17.2 %collective-permute-start.22 = (bf16[512,256]{1,0:T(8,128)(2,1)S(1)}, bf16[512,256]{1,0:T(8,128)(2,1)S(1)}, u32[]{:S(2)}, u32[]{:S(2)}) collective-permute-start(bf16[512,256]{1,0:T(8,128)(2,1)S(1)} %maximum_select_fusion.2.refs_0_), channel_id=1, source_target_pairs={{0,4},{4,8},{8,12},{12,0},{1,5},{5,9},{9,13},{13,1},{2,6},{6,10},{... | collective-permute-start | bytes 786440 | tf_op jit(solution)/shard_map/ppermute | solution.py:503
  158.6 36.0 %collective-permute-start.53 = (bf16[256,256]{1,0:T(8,128)(2,1)S(1)}, bf16[256,256]{1,0:T(8,128)(2,1)S(1)}, u32[]{:S(2)}, u32[]{:S(2)}) collective-permute-start(bf16[256,256]{1,0:T(8,128)(2,1)S(1)} %copy-done.25), channel_id=1, source_target_pairs={{0,8},{2,10},{4,12},{6,14},{8,0},{10,2},{12,4},{14,6},{1,9},{3,11}... | collective-permute-start | bytes 393224 | tf_op jit(solution)/shard_map/ppermute | solution.py:553
  168.5 28.9 %collective-permute-start.36 = (bf16[512,256]{1,0:T(8,128)(2,1)S(1)}, bf16[512,256]{1,0:T(8,128)(2,1)S(1)}, u32[]{:S(2)}, u32[]{:S(2)}) collective-permute-start(bf16[512,256]{1,0:T(8,128)(2,1)S(1)} %collective-permute-done.35.refs_2_), channel_id=1, source_target_pairs={{0,4},{4,8},{8,12},{12,0},{1,5},{5,9},{9,13},{13,1},{2,6},{6,10},{... | collective-permute-start | bytes 786440 | tf_op jit(solution)/shard_map/ppermute | solution.py:503
  168.5 28.8 %collective-permute-start.54 = (bf16[256,256]{1,0:T(8,128)(2,1)S(1)}, bf16[256,256]{1,0:T(8,128)(2,1)S(1)}, u32[]{:S(2)}, u32[]{:S(2)}) collective-permute-start(bf16[256,256]{1,0:T(8,128)(2,1)S(1)} %copy-done.24), channel_id=1, source_target_pairs={{0,10},{2,8},{4,14},{6,12},{8,2},{10,0},{12,6},{14,4},{1,11},{3,9}... | collective-permute-start | bytes 393224 | tf_op jit(solution)/shard_map/ppermute | solution.py:553
  174.1 35.5 %collective-permute-start.23 = (bf16[512,256]{1,0:T(8,128)(2,1)S(1)}, bf16[512,256]{1,0:T(8,128)(2,1)S(1)}, u32[]{:S(2)}, u32[]{:S(2)}) collective-permute-start(bf16[512,256]{1,0:T(8,128)(2,1)S(1)} %collective-permute-done.22.refs_2_), channel_id=1, source_target_pairs={{0,4},{4,8},{8,12},{12,0},{1,5},{5,9},{9,13},{13,1},{2,6},{6,10},{... | collective-permute-start | bytes 786440 | tf_op jit(solution)/shard_map/ppermute | solution.py:503
  197.4 13.0 %collective-permute-start.37 = (bf16[512,256]{1,0:T(8,128)(2,1)S(1)}, bf16[512,256]{1,0:T(8,128)(2,1)S(1)}, u32[]{:S(2)}, u32[]{:S(2)}) collective-permute-start(bf16[512,256]{1,0:T(8,128)(2,1)S(1)} %collective-permute-done.36.refs_0_), channel_id=1, source_target_pairs={{0,4},{4,8},{8,12},{12,0},{1,5},{5,9},{9,13},{13,1},{2,6},{6,10},{... | collective-permute-start | bytes 786440 | tf_op jit(solution)/shard_map/ppermute | solution.py:503
  210.4 15.0 %collective-permute-start.38 = (bf16[512,256]{1,0:T(8,128)(2,1)S(1)}, bf16[512,256]{1,0:T(8,128)(2,1)S(1)}, u32[]{:S(2)}, u32[]{:S(2)}) collective-permute-start(bf16[512,256]{1,0:T(8,128)(2,1)S(1)} %collective-permute-done.37.refs_0_), channel_id=1, source_target_pairs={{0,2},{2,0},{1,3},{3,1},{4,6},{6,4},{5,7},{7,5},{8,10},{10,8},{9,1... | collective-permute-start | bytes 786440 | tf_op jit(solution)/shard_map/ppermute | solution.py:503
  211.6 21.4 %collective-permute-start.29 = (bf16[512,256]{1,0:T(8,128)(2,1)S(1)}, bf16[512,256]{1,0:T(8,128)(2,1)S(1)}, u32[]{:S(2)}, u32[]{:S(2)}) collective-permute-start(bf16[512,256]{1,0:T(8,128)(2,1)S(1)} %maximum_select_fusion.2.refs_0_), channel_id=1, source_target_pairs={{0,2},{2,0},{1,3},{3,1},{4,6},{6,4},{5,7},{7,5},{8,10},{10,8},{9,1... | collective-permute-start | bytes 786440 | tf_op jit(solution)/shard_map/ppermute | solution.py:503
  214.2 22.6 %collective-permute-start.28 = (bf16[512,256]{1,0:T(8,128)(2,1)S(1)}, bf16[512,256]{1,0:T(8,128)(2,1)S(1)}, u32[]{:S(2)}, u32[]{:S(2)}) collective-permute-start(bf16[512,256]{1,0:T(8,128)(2,1)S(1)} %collective-permute-done.22.refs_2_), channel_id=1, source_target_pairs={{0,2},{2,0},{1,3},{3,1},{4,6},{6,4},{5,7},{7,5},{8,10},{10,8},{9,1... | collective-permute-start | bytes 786440 | tf_op jit(solution)/shard_map/ppermute | solution.py:503
  219.8 22.6 %collective-permute-start.27 = (bf16[512,256]{1,0:T(8,128)(2,1)S(1)}, bf16[512,256]{1,0:T(8,128)(2,1)S(1)}, u32[]{:S(2)}, u32[]{:S(2)}) collective-permute-start(bf16[512,256]{1,0:T(8,128)(2,1)S(1)} %collective-permute-done.23.refs_0_), channel_id=1, source_target_pairs={{0,2},{2,0},{1,3},{3,1},{4,6},{6,4},{5,7},{7,5},{8,10},{10,8},{9,1... | collective-permute-start | bytes 786440 | tf_op jit(solution)/shard_map/ppermute | solution.py:503
  221.5 26.5 %collective-permute-start.25 = (bf16[512,256]{1,0:T(8,128)(2,1)S(1)}, bf16[512,256]{1,0:T(8,128)(2,1)S(1)}, u32[]{:S(2)}, u32[]{:S(2)}) collective-permute-start(bf16[512,256]{1,0:T(8,128)(2,1)S(1)} %collective-permute-done.24.refs_0_), channel_id=1, source_target_pairs={{0,2},{2,0},{1,3},{3,1},{4,6},{6,4},{5,7},{7,5},{8,10},{10,8},{9,1... | collective-permute-start | bytes 786440 | tf_op jit(solution)/shard_map/ppermute | solution.py:503
  225.4 41.0 %collective-permute-start.58 = (bf16[8,256,256]{2,1,0:T(8,128)(2,1)S(1)}, bf16[8,256,256]{2,1,0:T(8,128)(2,1)}, u32[]{:S(2)}, u32[]{:S(2)}) collective-permute-start(bf16[8,256,256]{2,1,0:T(8,128)(2,1)S(1)} %bitcast_dynamic-update-slice_fusion.refs_3_.refs_7_.refs_11_.refs_2_.refs_6_.refs_1_), channel_id=1, source_target_pairs={{0,16},{16,0},{1,17},{17,1},{2,18},{18,2},{3,19},{19,3},{4,20},{20... | collective-permute-start | bytes 3145736 | tf_op jit(solution)/shard_map/ppermute | solution.py:503
  259.6 26.4 %collective-permute-start.57 = (bf16[8,256,256]{2,1,0:T(8,128)(2,1)S(1)}, bf16[8,256,256]{2,1,0:T(8,128)(2,1)S(1)}, u32[]{:S(2)}, u32[]{:S(2)}) collective-permute-start(bf16[8,256,256]{2,1,0:T(8,128)(2,1)S(1)} %bitcast_dynamic-update-slice_fusion.refs_3_.refs_7_.refs_11_.refs_2_.refs_6_.refs_1_), channel_id=1, source_target_pairs={{0,1},{1,0},{2,3},{3,2},{4,5},{5,4},{6,7},{7,6},{8,9},{9,8},{10,11... | collective-permute-start | bytes 3145736 | tf_op jit(solution)/shard_map/ppermute | solution.py:50
  266.4 28.9 %collective-permute-start.59 = (bf16[8,256,256]{2,1,0:T(8,128)(2,1)}, bf16[8,256,256]{2,1,0:T(8,128)(2,1)S(1)}, u32[]{:S(2)}, u32[]{:S(2)}) collective-permute-start(bf16[8,256,256]{2,1,0:T(8,128)(2,1)} %collective-permute-done.58.refs_5_.refs_9_.refs_13_.refs_4_.refs_8_.refs_3_), channel_id=1, source_target_pairs={{0,1},{1,0},{2,3},{3,2},{4,5},{5,4},{6,7},{7,6},{8,9},{9,8},{10,11... | collective-permute-start | bytes 3145736 | tf_op jit(solution)/shard_map/ppermute | solution.py:50
  285.9 15.5 %collective-permute-start.60 = (bf16[256,512]{1,0:T(8,128)(2,1)}, bf16[256,512]{1,0:T(8,128)(2,1)S(1)}, u32[]{:S(2)}, u32[]{:S(2)}) collective-permute-start(bf16[256,512]{1,0:T(8,128)(2,1)} %collective-permute-done.47.refs_0_), channel_id=1, source_target_pairs={{0,2},{2,0},{1,3},{3,1},{4,6},{6,4},{5,7},{7,5},{8,10},{10,8},{9,1... | collective-permute-start | bytes 786440 | tf_op jit(solution)/shard_map/ppermute | solution.py:503
  292.1 14.8 %collective-permute-start.49 = (bf16[256,512]{1,0:T(8,128)(2,1)}, bf16[256,512]{1,0:T(8,128)(2,1)S(1)}, u32[]{:S(2)}, u32[]{:S(2)}) collective-permute-start(bf16[256,512]{1,0:T(8,128)(2,1)} %collective-permute-done.48.refs_0_), channel_id=1, source_target_pairs={{0,2},{2,0},{1,3},{3,1},{4,6},{6,4},{5,7},{7,5},{8,10},{10,8},{9,1... | collective-permute-start | bytes 786440 | tf_op jit(solution)/shard_map/ppermute | solution.py:503
  (69 other events, 1004.8 us)

commit v3 on v2

--- a/solution.py
+++ b/solution.py
@@ -23,12 +23,15 @@
 TAPS = 3 * WINDOW
 BF16 = jnp.bfloat16
 F32 = jnp.float32
-VMEM_LIMIT = 48 * 1024 * 1024
-
-
-def params(*semantics):
+
+
+def split_meta(meta, images):
+    return meta[3 * images], meta[3 * images + 1], meta[3 * images + 2], meta[3 * images + 3]
+
+
+def params(mebibytes):
     return pltpu.CompilerParams(
-        dimension_semantics=semantics or None, vmem_limit_bytes=VMEM_LIMIT
+        dimension_semantics=("arbitrary",), vmem_limit_bytes=mebibytes * 1024 * 1024
     )
 
 
@@ -39,7 +42,8 @@
 
 
 def silu(values):
-    return values / (1.0 + jnp.exp(-values))
+    half = values * 0.5
+    return half + half * jnp.tanh(half)
 
 
 def mxu(left, right):
@@ -81,8 +85,8 @@
     @pl.when(step == PIX - 1)
     def _():
         tokens = total[...].astype(BF16)
-        first = meta[2 * images]
-        core = meta[2 * images + 1]
+        ctx, core, _, _ = split_meta(meta, images)
+        first = ctx * (2 * half)
         block = 256
         for part in range(2 * half // block):
             which = part * block // half
@@ -124,15 +128,31 @@
             ],
         ),
         out_shape=jax.ShapeDtypeStruct((2, half, width), BF16),
-        compiler_params=params("arbitrary"),
+        compiler_params=params(24),
         cost_estimate=cost(2 * count * PIX * CH * (256 + width), 4 << 20, count * PIX * CH),
         name="down_stream",
     )(meta, rows, conv, patch_in, text)
 
 
-def qkv_kernel(count, first, last, meta, *refs):
+def load(pieces):
+    if len(pieces) == 1:
+        return pieces[0][...]
+    return jnp.concatenate([piece[...] for piece in pieces], axis=0)
+
+
+def take_blocks(refs, shapes):
+    return [[refs.pop(0) for _ in pieces] for pieces in shapes]
+
+
+def chip_of(meta, images, tiles, outer, entry):
+    _, _, tile, mpo = split_meta(meta, images)
+    return lax.rem(tile + tiles - entry // 2, tiles) * outer + lax.rem(mpo + entry % 2, outer)
+
+
+def qkv_kernel(shapes, groups, first, last, meta, *refs):
     refs = list(refs)
-    x_refs = [refs.pop(0) for _ in range(count)]
+    count = len(shapes)
+    x_refs = take_blocks(refs, shapes)
     gain_refs = [refs.pop(0) for _ in range(count)]
     weight_refs = [[refs.pop(0) for _ in range(6)] for _ in range(count)]
     if not first:
@@ -140,18 +160,21 @@
     if last:
         head_gains = refs.pop(0)
     scaled = refs.pop()
-    half, span = x_refs[0].shape
+    half, span = scaled.shape[1:]
     chunk = 64
 
-    def scale_rows(index, carry):
-        rows = pl.ds(pl.multiple_of(index * chunk, chunk), chunk)
-        square = jnp.zeros((chunk, HD), F32) if first else square_in[rows, :]
-        for block in range(count):
-            value = x_refs[block][rows, :].astype(F32)
-            scaled[block, rows, :] = (value * gain_refs[block][0].astype(F32)).astype(BF16)
-            value = value * value
-            for part in range(span // HD):
-                square = square + value[:, part * HD : (part + 1) * HD]
+    def scale_rows(block, piece, base, index, carry):
+        rows = pl.ds(pl.multiple_of(base + index * chunk, chunk), chunk)
+        local = pl.ds(pl.multiple_of(index * chunk, chunk), chunk)
+        if block:
+            square = square_out[rows, :]
+        else:
+            square = jnp.zeros((chunk, HD), F32) if first else square_in[rows, :]
+        value = piece[local, :].astype(F32)
+        scaled[block, rows, :] = (value * gain_refs[block][0].astype(F32)).astype(BF16)
+        value = value * value
+        for part in range(span // HD):
+            square = square + value[:, part * HD : (part + 1) * HD]
         square_out[rows, :] = square
         return carry
 
@@ -160,12 +183,16 @@
         outs = refs
     else:
         acc_out, square_out = refs
-    lax.fori_loop(0, half // chunk, scale_rows, 0)
+    for block in range(count):
+        base = 0
+        for piece in x_refs[block]:
+            body = functools.partial(scale_rows, block, piece, base)
+            lax.fori_loop(0, piece.shape[0] // chunk, body, 0)
+            base += piece.shape[0]
     width = weight_refs[0][0].shape[1]
     heads = width // HD
     if last:
-        model = meta[count] * span
-        mean = jnp.sum(square_out[...], axis=-1, keepdims=True) / model.astype(F32)
+        mean = jnp.sum(square_out[...], axis=-1, keepdims=True) * (1.0 / (groups * span))
         scale = lax.rsqrt(mean + EPSILON)
     for part in range(6):
         total = None if first else acc_in[part]
@@ -195,20 +222,27 @@
     return pl.BlockSpec(shape, lambda i, m: (0,) * len(shape))
 
 
-def qkv_step(blocks, chips, gain, weights, state, head_gains):
-    half, span = blocks[0].shape
+def qkv_step(meta, layout, blocks, entries, gain, weights, state, head_gains):
+    span = blocks[0][0].shape[1]
+    half = sum(piece.shape[0] for piece in blocks[0])
     width = weights[0].shape[1]
     heads = width // HD
     count, first, last = len(blocks), state is None, head_gains is not None
     groups = gain.shape[0]
-    inputs, specs = list(blocks), [full(b.shape) for b in blocks]
-    for index in range(count):
+    shapes = [[p.shape for p in pieces] for pieces in blocks]
+    inputs = [p for pieces in blocks for p in pieces]
+    specs = [full(p.shape) for p in inputs]
+    for entry in entries:
         inputs.append(gain)
-        specs.append(pl.BlockSpec((1, 1, span), lambda i, m, index=index: (m[index], 0, 0)))
-    for index in range(count):
+        specs.append(
+            pl.BlockSpec((1, 1, span), lambda i, m, entry=entry: (chip_of(m, *layout, entry), 0, 0))
+        )
+    for entry in entries:
         for weight in weights:
             inputs.append(weight)
-            specs.append(pl.BlockSpec((span, width), lambda i, m, index=index: (m[index], 0)))
+            specs.append(
+                pl.BlockSpec((span, width), lambda i, m, entry=entry: (chip_of(m, *layout, entry), 0))
+            )
     if not first:
         inputs += list(state)
         specs += [full(s.shape) for s in state]
@@ -224,9 +258,8 @@
             jax.ShapeDtypeStruct((6, half, width), F32),
             jax.ShapeDtypeStruct((half, HD), F32),
         ]
-    meta = jnp.stack(list(chips) + [jnp.int32(groups)]).astype(jnp.int32)
     return pl.pallas_call(
-        functools.partial(qkv_kernel, count, first, last),
+        functools.partial(qkv_kernel, shapes, groups, first, last),
         grid_spec=pltpu.PrefetchScalarGridSpec(
             num_scalar_prefetch=1,
             grid=(1,),
@@ -235,18 +268,24 @@
             scratch_shapes=scratch,
         ),
         out_shape=outs,
-        compiler_params=params("arbitrary"),
+        compiler_params=params(30),
         cost_estimate=cost(12 * count * half * span * width, (6 + 2 * count) << 20),
         name="qkv_last" if last else "qkv_step",
     )(meta, *inputs)
 
 
-def attention_kernel(images, pieces, meta, *refs):
+def attention_kernel(images, pieces, half, meta, *refs):
+    ctx, core, _, _ = split_meta(meta, images)
+    ctxs = pieces // 2
+    bases = []
+    for piece in range(pieces):
+        side = jnp.bitwise_xor(core, piece % 2)
+        bases.append(lax.rem(ctx + ctxs - piece // 2, ctxs) * (2 * half) + side * half)
     q_refs, kv_refs, out_refs = refs[:2], refs[2 : 2 + pieces], refs[2 + pieces :]
     rows = q_refs[0].shape[0]
     step = pl.program_id(0)
     for side in range(2):
-        place = meta[images + side] + step * rows + lax.broadcasted_iota(jnp.int32, (rows, 1), 0)
+        place = bases[side] + step * rows + lax.broadcasted_iota(jnp.int32, (rows, 1), 0)
         limit = place
         for image in range(images):
             inner = place - meta[image]
@@ -259,7 +298,7 @@
                 query, kv_refs[piece][0], (((1,), (1,)), ((), ())), preferred_element_type=F32
             )
             position = lax.broadcasted_iota(jnp.int32, score.shape, 1)
-            score = jnp.where(position <= limit - meta[images + 2 + piece], score, NEGATIVE_FILL)
+            score = jnp.where(position <= limit - bases[piece], score, NEGATIVE_FILL)
             scores.append(score)
             best = jnp.max(score, axis=1, keepdims=True)
             top = best if top is None else jnp.maximum(top, best)
@@ -278,7 +317,7 @@
     keys = half * len(pieces)
     rows = pl.BlockSpec((block, HD), lambda i, m: (i, 0))
     return pl.pallas_call(
-        functools.partial(attention_kernel, images, len(pieces)),
+        functools.partial(attention_kernel, images, len(pieces), half),
         grid_spec=pltpu.PrefetchScalarGridSpec(
             num_scalar_prefetch=1,
             grid=(half // block,),
@@ -286,41 +325,47 @@
             out_specs=[rows, rows],
         ),
         out_shape=[jax.ShapeDtypeStruct((half, HD), BF16)] * 2,
-        compiler_params=params("arbitrary"),
+        compiler_params=params(24),
         cost_estimate=cost(8 * half * keys * HD, 4 * keys * HD, 2 * half * keys),
         name="attention",
     )(meta, *queries, *pieces)
 
 
-def out_kernel(count, first, last, meta, *refs):
-    x_refs, weight_refs = refs[:count], refs[count : 3 * count]
-    if first:
-        start, outs = refs[3 * count : 3 * count + 2], refs[3 * count + 2 :]
-    else:
-        start, outs = [refs[3 * count].at[0], refs[3 * count].at[1]], refs[3 * count + 1 :]
+def out_kernel(shapes, first, last, meta, *refs):
+    refs = list(refs)
+    count = len(shapes)
+    x_refs = take_blocks(refs, shapes)
+    weight_refs = [refs.pop(0) for _ in range(2 * count)]
+    start = [refs.pop(0), refs.pop(0)] if first else [refs[0].at[0], refs.pop(0).at[1]]
+    outs = refs
     for side in range(2):
         total = start[side][...].astype(F32)
         for block in range(count):
             weight = weight_refs[2 * block + side][0, :, 0]
-            total = total + mxu(x_refs[block][...], weight.reshape(2 * HD, weight.shape[2]))
+            total = total + mxu(load(x_refs[block]), weight.reshape(2 * HD, weight.shape[2]))
         if last:
             outs[side][...] = total.astype(BF16)
         else:
             outs[0][side] = total
 
 
-def out_step(blocks, chips, head, weights, state, last):
-    half = blocks[0].shape[0]
+def out_step(meta, layout, blocks, entries, head, weights, state, last):
+    half = sum(piece.shape[0] for piece in blocks[0])
     width = weights[0].shape[1]
     first = isinstance(state, tuple)
     count = len(blocks)
+    shapes = [[p.shape for p in pieces] for pieces in blocks]
     views = [w.reshape(-1, 2, width // HD, HD, width) for w in weights]
-    inputs, specs = list(blocks), [full(b.shape) for b in blocks]
-    for index in range(count):
+    inputs = [p for pieces in blocks for p in pieces]
+    specs = [full(p.shape) for p in inputs]
+    for entry in entries:
         for view in views:
             inputs.append(view)
             specs.append(
-                pl.BlockSpec((1, 2, 1, HD, width), lambda i, m, index=index: (m[index], 0, head, 0, 0))
+                pl.BlockSpec(
+                    (1, 2, 1, HD, width),
+                    lambda i, m, entry=entry: (chip_of(m, *layout, entry), 0, head, 0, 0),
+                )
             )
     states = list(state) if first else [state]
     inputs += states
@@ -330,7 +375,7 @@
     else:
         outs = [jax.ShapeDtypeStruct((2, half, width), F32)]
     result = pl.pallas_call(
-        functools.partial(out_kernel, count, first, last),
+        functools.partial(out_kernel, shapes, first, last),
         grid_spec=pltpu.PrefetchScalarGridSpec(
             num_scalar_prefetch=1,
             grid=(1,),
@@ -338,37 +383,40 @@
             out_specs=[full(o.shape) for o in outs],
         ),
         out_shape=outs,
-        compiler_params=params("arbitrary"),
+        compiler_params=params(16),
         cost_estimate=cost(8 * count * half * HD * width, (2 + count) << 20),
         name="out_last" if last else "out_step",
-    )(jnp.stack(list(chips)).astype(jnp.int32), *inputs)
+    )(meta, *inputs)
     return result if last else result[0]
 
 
-def pick_kernel(targets, meta, own_ref, par_ref, out_ref):
+def pick_kernel(images, ctxs, meta, own_ref, par_ref, *out_refs):
     half = own_ref.shape[0]
-    own_base, par_base = meta[targets], meta[targets + 1]
-    for target in range(targets):
-        place = meta[target] + lax.broadcasted_iota(jnp.int32, (IMG_TOK, half), 0)
-        column = lax.broadcasted_iota(jnp.int32, (IMG_TOK, half), 1)
-        own = jnp.where(place == column + own_base, 1.0, 0.0).astype(BF16)
-        par = jnp.where(place == column + par_base, 1.0, 0.0).astype(BF16)
-        out_ref[target] = (mxu(own, own_ref[...]) + mxu(par, par_ref[...])).astype(BF16)
-
-
-def pick_rows(meta, own, par, targets):
+    ctx, core, _, _ = split_meta(meta, images)
+    for target in range(2 * ctxs):
+        to_core = jnp.bitwise_xor(core, target % 2)
+        slot = 2 * lax.rem(ctx + target // 2, ctxs) + to_core
+        start = meta[meta[2 * images + slot]]
+        place = start + lax.broadcasted_iota(jnp.int32, (IMG_TOK, half), 0)
+        column = ctx * (2 * half) + lax.broadcasted_iota(jnp.int32, (IMG_TOK, half), 1)
+        own = jnp.where(place == column + core * half, 1.0, 0.0).astype(BF16)
+        par = jnp.where(place == column + (1 - core) * half, 1.0, 0.0).astype(BF16)
+        out_refs[target][...] = (mxu(own, own_ref[...]) + mxu(par, par_ref[...])).astype(BF16)
+
+
+def pick_rows(meta, own, par, images, ctxs):
     half, width = own.shape
-    whole = pl.BlockSpec((half, width), lambda i, m: (0, 0))
+    targets = 2 * ctxs
     return pl.pallas_call(
-        functools.partial(pick_kernel, targets),
+        functools.partial(pick_kernel, images, ctxs),
         grid_spec=pltpu.PrefetchScalarGridSpec(
             num_scalar_prefetch=1,
             grid=(1,),
-            in_specs=[whole, whole],
-            out_specs=pl.BlockSpec((targets, IMG_TOK, width), lambda i, m: (0, 0, 0)),
+            in_specs=[full(own.shape), full(par.shape)],
+            out_specs=[full((IMG_TOK, width))] * targets,
         ),
-        out_shape=jax.ShapeDtypeStruct((targets, IMG_TOK, width), BF16),
-        compiler_params=params("arbitrary"),
+        out_shape=[jax.ShapeDtypeStruct((IMG_TOK, width), BF16)] * targets,
+        compiler_params=params(16),
         cost_estimate=cost(targets * 4 * IMG_TOK * half * width, 1 << 20),
         name="pick_rows",
     )(meta, own, par)
@@ -390,7 +438,7 @@
     return pl.pallas_call(
         merge_kernel,
         out_shape=jax.ShapeDtypeStruct((IMG_TOK, 2 * width), BF16),
-        compiler_params=params(),
+        compiler_params=pltpu.CompilerParams(vmem_limit_bytes=8 << 20),
         cost_estimate=cost(1 << 20, 1 << 20),
         name="merge_picks",
     )(*own_parts, *par_parts)
@@ -413,21 +461,23 @@
     return total
 
 
-def up_kernel(count, halves, first, last, *refs):
+def up_kernel(shapes, halves, first, last, *refs):
     refs = list(refs)
-    x_refs = [refs.pop(0) for _ in range(count)]
+    count = len(shapes)
+    x_refs = take_blocks(refs, shapes)
     weight_refs = [[[refs.pop(0) for _ in range(2)] for _ in range(halves)] for _ in range(count)]
     acc_in = None if first else refs.pop(0)
     spread_ref = refs.pop(0) if last else None
     out_ref = refs[0]
-    width = x_refs[0].shape[1] // 2
+    width = x_refs[0][0].shape[1] // 2
+    values = [load(pieces) for pieces in x_refs]
     totals = []
     for part in range(halves):
         total = None if first else acc_in[part]
         for block in range(count):
             for side in range(2):
                 term = mxu(
-                    x_refs[block][:, side * width : (side + 1) * width],
+                    values[block][:, side * width : (side + 1) * width],
                     weight_refs[block][part][side][0],
                 )
                 total = term if total is None else total + term
@@ -441,11 +491,13 @@
 
 
 def up_step(blocks, offsets, weights, state, spread_weight):
-    span = blocks[0].shape[1]
+    span = blocks[0][0].shape[1]
+    shapes = [[p.shape for p in pieces] for pieces in blocks]
     halves, count = len(weights), len(blocks)
     first, last = state is None, spread_weight is not None
     whole = lambda shape: pl.BlockSpec(shape, lambda i: (0,) * len(shape))
-    inputs, specs = list(blocks), [whole(b.shape) for b in blocks]
+    inputs = [p for pieces in blocks for p in pieces]
+    specs = [whole(p.shape) for p in inputs]
     for offset in offsets:
         for sides in weights:
             for weight in sides:
@@ -461,12 +513,12 @@
     else:
         out = jax.ShapeDtypeStruct((halves, IMG_TOK, CH), F32)
     return pl.pallas_call(
-        functools.partial(up_kernel, count, halves, first, last),
+        functools.partial(up_kernel, shapes, halves, first, last),
         grid=(1,),
         in_specs=specs,
         out_specs=whole(out.shape),
         out_shape=out,
-        compiler_params=params("arbitrary"),
+        compiler_params=params(16),
         cost_estimate=cost(2 * count * IMG_TOK * span * CH * halves, (1 + count) << 20),
         name="up_last" if last else "up_step",
     )(*inputs)
@@ -557,21 +609,20 @@
     return [[weight, swap(weight)] for weight in weights]
 
 
-def gather_chips(block):
+def gather_work(block, state, step):
     tiles = lax.axis_size("tile")
-    blocks = []
-    for step in range(tiles):
-        if step:
-            block = shift(block, "tile", 1)
-        blocks += [block, shift(block, "mpo", 1)]
-    return blocks
-
-
-def arrivals(tiles):
-    steps = [[0, 1] + ([2] if tiles > 1 else [])]
-    for step in range(2, tiles):
-        steps.append([2 * step, 2 * step - 1])
-    return steps + [[2 * tiles - 1]]
+    ring, cross = block, None
+    fresh, entries = [[block]], [0]
+    for index in range(tiles - 1):
+        ring_next, cross_next = shift(ring, "tile", 1), shift(ring, "mpo", 1)
+        state = step(fresh, entries, state, False)
+        ring, cross, state = lax.optimization_barrier((ring_next, cross_next, state))
+        fresh, entries = [[ring], [cross]], [2 * index + 2, 2 * index + 1]
+    middle = block.shape[0] // 2
+    upper, lower = shift(ring[:middle], "mpo", 1), shift(cross[middle:], "tile", 1)
+    state = step(fresh, entries, state, False)
+    upper, lower, state = lax.optimization_barrier((upper, lower, state))
+    return step([[upper, lower]], [2 * tiles - 1], state, True)
 
 
 def shards(
@@ -609,8 +660,10 @@
     matches = image_of_slot[None, :] == numbers[:, None]
     slot_of_image = jnp.sum(jnp.where(matches, numbers[None, :], 0), axis=1)
     slot_place = lax.rem(ctx + ctxs - slot_of_image // local, ctxs) * local + slot_of_image % local
-    first = ctx * seq_rows
-    stream_meta = jnp.concatenate([span_start, slot_place, jnp.stack([first, core])]).astype(jnp.int32)
+    meta = jnp.concatenate(
+        [span_start, slot_place, image_of_slot, jnp.stack([ctx, core, tile, mpo])]
+    ).astype(jnp.int32)
+    layout = (images, tiles, outer)
 
     padded = jnp.pad(every_latent, ((0, 0), (1, 1), (CIN, 128 - CIN)))
     rows = jnp.stack(
@@ -624,26 +677,18 @@
         ]
     )
     text = jnp.roll(text_embed.reshape(2, half, width), core, axis=0).reshape(seq_rows, width)
-    stream = down_stream(stream_meta, rows, conv, patch_in, text, images)
+    stream = down_stream(meta, rows, conv, patch_in, text, images)
     stream_own = stream[0]
     stream_par = swap(stream[1])
 
-    def chip(index):
-        return lax.rem(tile + tiles - index // 2, tiles) * outer + lax.rem(mpo + index % 2, outer)
-
-    blocks = gather_chips(by_core(core, stream_own, stream_par, 1))
     head_gains = jnp.stack([query_gain, key_gain])
-    state = None
-    steps = arrivals(tiles)
-    for step in steps:
-        state = qkv_step(
-            [blocks[b] for b in step],
-            [chip(b) for b in step],
-            gain,
-            weights,
-            state,
-            head_gains if step is steps[-1] else None,
+
+    def project(blocks, entries, state, last):
+        return qkv_step(
+            meta, layout, blocks, entries, gain, weights, state, head_gains if last else None
         )
+
+    state = gather_work(by_core(core, stream_own, stream_par, 1), None, project)
     kv_send, q_send = state[:heads], state[heads : 2 * heads]
     kv_own, q_own = state[2 * heads : 3 * heads], state[3 * heads :]
 
@@ -655,59 +700,42 @@
         ]
         return lax.ppermute(values, ("ctx", "core"), pairs)
 
-    bases = [first + core * half, first + (1 - core) * half]
-    key_bases = list(bases)
-    for step in range(1, ctxs):
-        from_ctx = lax.rem(ctx + ctxs - step, ctxs) * seq_rows
-        key_bases += [from_ctx + core * half, from_ctx + (1 - core) * half]
-    spans = [span_start[i] for i in range(images)]
-    att_meta = jnp.stack(spans + bases + key_bases).astype(jnp.int32)
-    gathered = []
+    attended = []
     for head in range(heads):
         q_par = swap(q_send[head])
         pieces = [kv_own[head], swap(kv_send[head])]
         for step in range(1, ctxs):
             pieces += [shifted(kv_own[head], step, False), shifted(kv_send[head], step, True)]
-        att_own, att_send = attention(att_meta, [q_own[head], q_par], pieces, images)
-        gathered.append(gather_chips(by_core(core, att_own, swap(att_send), 1)))
+        att_own, att_send = attention(meta, [q_own[head], q_par], pieces, images)
+        attended.append(by_core(core, att_own, swap(att_send), 1))
     state = (stream_own, stream_par)
     for head in range(heads):
-        for step in steps:
-            last = head == heads - 1 and step is steps[-1]
-            state = out_step(
-                [gathered[head][b] for b in step],
-                [chip(b) for b in step],
-                head,
-                (out_weight, out_par),
-                state,
-                last,
+
+        def project_out(blocks, entries, state, last):
+            return out_step(
+                meta, layout, blocks, entries, head, (out_weight, out_par), state, last and head == heads - 1
             )
+
+        state = gather_work(attended[head], state, project_out)
     out_own, out_send = state
     out_other = swap(out_send)
     layer_out = by_core(core, out_own, out_other, 0)
 
-    starts = jnp.take(span_start, image_of_slot)
-    wanted = []
-    for step in range(ctxs):
-        to_ctx = lax.rem(ctx + step, ctxs)
-        wanted += [starts[2 * to_ctx + core], starts[2 * to_ctx + 1 - core]]
-    pick_meta = jnp.stack(wanted + bases).astype(jnp.int32)
-    picks = pick_rows(pick_meta, out_own, out_other, 2 * ctxs)
+    picks = pick_rows(meta, out_own, out_other, images, ctxs)
     own_parts, par_parts = [picks[0]], [swap(picks[1])]
     for step in range(1, ctxs):
         own_parts.append(shifted(picks[2 * step], step, False))
         par_parts.append(shifted(picks[2 * step + 1], step, True))
 
-    blocks = gather_chips(merge_picks(own_parts, par_parts))
     halves = len(up_weights)
     pixel = tile * outer + mpo
     pixels = jnp.stack([pixel * halves + lax.rem(ctx + h, halves) for h in range(halves)])
     spread_weight = spread_weights(up_conv, pixels)
-    state = None
-    for step in steps:
-        state = up_step(
-            [blocks[b] for b in step], step, up_weights, state, spread_weight if step is steps[-1] else None
-        )
+
+    def project_up(blocks, entries, state, last):
+        return up_step(blocks, entries, up_weights, state, spread_weight if last else None)
+
+    state = gather_work(merge_picks(own_parts, par_parts), None, project_up)
 
     bands = state.reshape(tiles, IMG_TOK // tiles, PIX * CIN)
     band = lax.dynamic_index_in_dim(bands, tile, 0, keepdims=False)

time: 328 us -> 285 us (0.87)
  waiting for transfers between devices: 153 us -> 99 us
  local copies, waits for them, and re-layouts: 23 us -> 37 us
  Pallas kernels: 76.7 us -> 70.4 us
  starting transfers between devices: 65 us -> 70.2 us
    ppermute x38 -> x42, waiting for transfers between devices: 110 us -> 71 us  [shift(): lax.ppermute(values, axis, [(i, (i + step) % count) for i in range(count)])]
    ppermute x7, waiting for transfers between devices: 25.9 us -> 0.02 us  [transpose_up(): block = lax.ppermute(block, ('tile', 'mpo'), pairs)]
    ppermute x38 -> x42, starting transfers between devices: 39 us -> 26.4 us  [shift(): lax.ppermute(values, axis, [(i, (i + step) % count) for i in range(count)])]
    unnamed x85, local copies, waits for them, and re-layouts: 12.8 us -> 25.2 us
    ppermute x17, starting transfers between devices: 18.2 us -> 29.9 us  [swap(): return lax.ppermute(values, 'core', [(0, 1), (1, 0)])]
    ppermute x6, waiting for transfers between devices: 15.1 us -> 24.6 us  [shifted(): return lax.ppermute(values, ('ctx', 'core'), pairs)]
    pallas_call x19 -> x23, Pallas kernels: 62.7 us -> 56.7 us  [the longest x5 19.2 us: qkv_step(): pl.pallas_call(functools.partial(qkv_kernel, shapes, groups, first, last)...]
    ppermute x7, starting transfers between devices: 3.93 us -> 8.51 us  [transpose_up(): block = lax.ppermute(block, ('tile', 'mpo'), pairs)]
  transfers between devices with their start and end apart: 68 -> 72, of which waited for: 33 -> 31; matrix products, arithmetic and copies ran while one was open for 5% -> 7% of each run, Pallas kernels for 18% -> 24%
where the time goes in v3:
time: 285 us; the launch traced here: 284 us
  waiting for transfers between devices  99 us (35%)
  Pallas kernels  70.4 us (25%)
  starting transfers between devices  70.2 us (25%)
  local copies, waits for them, and re-layouts  37 us (13%)
  other arithmetic  4.99 us (2%)
    ppermute x42, waiting for transfers between devices, shift(): lax.ppermute(values, axis, [(i, (i + step) % count) for i in range(count)])  71 us
    ppermute x17, starting transfers between devices, swap(): return lax.ppermute(values, 'core', [(0, 1), (1, 0)])  29.9 us
    ppermute x42, starting transfers between devices, shift(): lax.ppermute(values, axis, [(i, (i + step) % count) for i in range(count)])  26.4 us
    unnamed x85, local copies, waits for them, and re-layouts  25.2 us
    ppermute x6, waiting for transfers between devices, shifted(): return lax.ppermute(values, ('ctx', 'core'), pairs)  24.6 us
    pallas_call x5, Pallas kernels, qkv_step(): pl.pallas_call(functools.partial(qkv_kernel, shapes, groups, first, last)...  19.2 us
    pallas_call x10, Pallas kernels, out_step(): pl.pallas_call(functools.partial(out_kernel, shapes, first, last), grid_s...  18.9 us
    pallas_call x1, Pallas kernels, down_stream(): pl.pallas_call(functools.partial(down_kernel, images, half), grid_spec=pl...  13.7 us
  transfers between devices with their start and end apart: 72, of which 31 were waited for; matrix products, arithmetic and copies ran while one was open for 7% of the time, Pallas kernels for 24%

profile of v3, /device:TPU:1, one launch (start us, length us, event | category | flops | bytes accessed | tf_op | source)
XLA Modules:
  0.0 283.9 jit_solution(2717860953381596431)
XLA Ops:
  2.3 2.7 collective-permute-start
  10.4 3.4 %collective-permute-start.3 = (bf16[1,272,128]{2,1,0:T(8,128)(2,1)S(1)}, bf16[1,272,128]{2,1,0:T(8,128)(2,1)S(1)}, u32[]{:S(2)}, u32[]{:S(2)}) collective-permute-start(bf16[1,272,128]{2,1,0:T(8,128)(2,1)S(1)} %fusion.28), channel_id=1, source_target_pairs={{0,12},{4,0},{8,4},{12,8},{1,13},{5,1},{9,5},{13,9},{2,14},{6,2},{... | collective-permute-start | bytes 208904 | tf_op jit(solution)/shard_map/ppermute | solution.py:555
  15.8 2.8 collective-permute-done.4
  28.2 13.7 %down_stream.1 = bf16[2,512,256]{2,1,0:T(8,128)(2,1)S(1)} custom-call(s32[16]{0:T(128)S(1)} %concatenate.93.meta, bf16[6,64,640]{2,1,0:T(8,128)(2,1)S(1)} %bitcast_dynamic-update-slice_fusion.8.rows_ref, bf16[4,144,256]{2,1,0:T(8,128)(2,1)S(1)} %pad_maximum_fusion.conv_ref, bf16[4096,256]{1,0:T(8,128)(2,1)S(1)} %copy-done.24, bf16[1024,256]{1,0:T(8,128)(2,1)S(1)} %bitcast.119), custom_call_target="tpu_custom_call" | custom-call | flops 4294967296 | bytes 4194304 | tf_op jit(solution)/shard_map/down_stream/pallas_call | solution.py:113
  41.9 3.5 %collective-permute-start.6 = (bf16[512,256]{1,0:T(8,128)(2,1)S(1)}, bf16[512,256]{1,0:T(8,128)(2,1)S(1)}, u32[]{:S(2)}, u32[]{:S(2)}) collective-permute-start(bf16[512,256]{1,0:T(8,128)(2,1)S(1)} %get-tuple-element.166), channel_id=1, source_target_pairs={{0,1},{1,0},{2,3},{3,2},{4,5},{5,4},{6,7},{7,6},{8,9},{9,8},{10,11... | collective-permute-start | bytes 786440 | tf_op jit(solution)/shard_map/ppermute | solution.py:54
  51.9 2.9 %qkv_step.4 = (f32[6,512,256]{2,1,0:T(8,128)S(1)}, f32[512,128]{1,0:T(8,128)S(1)}) custom-call(s32[16]{0:T(128)S(1)} %concatenate.93.meta, bf16[512,512]{1,0:T(8,128)(2,1)S(1)} %maximum_select_fusion.refs_0_, bf16[8,1,512]{2,1,0:T(2,128)(2,1)S(1)} %reshape.203.refs_1_.refs_2_.refs_3_, ...), custom_call_target="tpu_custom_call" | custom-call | flops 805306368 | bytes 8388608 | tf_op jit(solution)/shard_map/qkv_step/pallas_call | solution.py:261
  54.8 7.0 %collective-permute-done.7.refs_0_ = bf16[512,512]{1,0:T(8,128)(2,1)} collective-permute-done((bf16[512,512]{1,0:T(8,128)(2,1)S(1)}, bf16[512,512]{1,0:T(8,128)(2,1)}, u32[]{:S(2)}, u32[]{:S(2)}) %collective-permute-start.7) | collective-permute-done | bytes 524320 | tf_op jit(solution)/shard_map/ppermute | solution.py:555
  62.9 4.4 %qkv_step.5 = (f32[6,512,256]{2,1,0:T(8,128)S(1)}, f32[512,128]{1,0:T(8,128)S(1)}) custom-call(s32[16]{0:T(128)S(1)} %concatenate.93.meta, bf16[512,512]{1,0:T(8,128)(2,1)} %collective-permute-done.7.refs_0_, bf16[512,512]{1,0:T(8,128)(2,1)} %collective-permute-done.8.refs_1_, bf16[8,1,512]{2,1,0:T(2,128)(2,1)S(1)} %reshape.203.refs_1_.refs_2_.refs_3_, ...), custom_call_target="tpu_custom_call" | custom-call | flops 1610612736 | bytes 10485760 | tf_op jit(solution)/shard_map/qkv_step/pallas_call | solution.py:261
  69.7 6.5 %collective-permute-done.12.refs_0_ = bf16[512,512]{1,0:T(8,128)(2,1)} collective-permute-done((bf16[512,512]{1,0:T(8,128)(2,1)}, bf16[512,512]{1,0:T(8,128)(2,1)}, u32[]{:S(2)}, u32[]{:S(2)}) %collective-permute-start.12) | collective-permute-done | bytes 524320 | tf_op jit(solution)/shard_map/ppermute | solution.py:555
  92.7 4.3 %qkv_step.6 = (f32[6,512,256]{2,1,0:T(8,128)S(1)}, f32[512,128]{1,0:T(8,128)S(1)}) custom-call(s32[16]{0:T(128)S(1)} %concatenate.93.meta, bf16[512,512]{1,0:T(8,128)(2,1)} %collective-permute-done.12.refs_0_, bf16[512,512]{1,0:T(8,128)(2,1)S(1)} %copy-done.15, bf16[8,1,512]{2,1,0:T(2,128)(2,1)S(1)} %reshape.203.refs_1_.refs_2_.refs_3_, ...), custom_call_target="tpu_custom_call" | custom-call | flops 1610612736 | bytes 10485760 | tf_op jit(solution)/shard_map/qkv_step/pallas_call | solution.py:261
  97.0 2.9 %collective-permute-start.53 = (bf16[256,256]{1,0:T(8,128)(2,1)S(1)}, bf16[256,256]{1,0:T(8,128)(2,1)S(1)}, u32[]{:S(2)}, u32[]{:S(2)}) collective-permute-start(bf16[256,256]{1,0:T(8,128)(2,1)S(1)} %copy-done.29), channel_id=1, source_target_pairs={{0,6},{2,4},{4,10},{6,8},{8,14},{10,12},{12,2},{14,0},{1,7},{3,5},... | collective-permute-start | bytes 393224 | tf_op jit(solution)/shard_map/ppermute | solution.py:605
  105.5 4.4 %qkv_step.7 = (f32[6,512,256]{2,1,0:T(8,128)S(1)}, f32[512,128]{1,0:T(8,128)S(1)}) custom-call(s32[16]{0:T(128)S(1)} %concatenate.93.meta, bf16[512,512]{1,0:T(8,128)(2,1)} %collective-permute-done.14.refs_0_, bf16[512,512]{1,0:T(8,128)(2,1)} %collective-permute-done.15.refs_1_, bf16[8,1,512]{2,1,0:T(2,128)(2,1)S(1)} %reshape.203.refs_1_.refs_2_.refs_3_, ...), custom_call_target="tpu_custom_call" | custom-call | flops 1610612736 | bytes 10485760 | tf_op jit(solution)/shard_map/qkv_step/pallas_call | solution.py:261
  111.2 3.1 %qkv_last.1 = (bf16[2,512,128]{2,1,0:T(8,128)(2,1)S(1)}, bf16[2,512,128]{2,1,0:T(8,128)(2,1)S(1)}, bf16[512,128]{1,0:T(8,128)(2,1)S(1)}, bf16[512,128]{1,0:T(8,1...) custom-call(s32[16]{0:T(128)S(1)} %concatenate.93.meta, ...), custom_call_target="tpu_custom_call" | custom-call | flops 805306368 | bytes 8388608 | tf_op jit(solution)/shard_map/qkv_last/pallas_call | solution.py:261
  119.7 3.0 %collective-permute-start.55 = (bf16[256,256]{1,0:T(8,128)(2,1)S(1)}, bf16[256,256]{1,0:T(8,128)(2,1)S(1)}, u32[]{:S(2)}, u32[]{:S(2)}) collective-permute-start(bf16[256,256]{1,0:T(8,128)(2,1)S(1)} %copy-done.27), channel_id=1, source_target_pairs={{0,10},{2,8},{4,14},{6,12},{8,2},{10,0},{12,6},{14,4},{1,11},{3,9}... | collective-permute-start | bytes 393224 | tf_op jit(solution)/shard_map/ppermute | solution.py:605
  122.7 7.0 %collective-permute-done.28.refs_4_ = bf16[2,512,128]{2,1,0:T(8,128)(2,1)S(1)} collective-permute-done((bf16[2,512,128]{2,1,0:T(8,128)(2,1)S(1)}, bf16[2,512,128]{2,1,0:T(8,128)(2,1)S(1)}, u32[]{:S(2)}, u32[]{:S(2)}) %collective-permute-start.28) | collective-permute-done | bytes 262176 | tf_op jit(solution)/shard_map/ppermute | solution.py:701
  131.7 4.4 %attention.3 = (bf16[512,128]{1,0:T(8,128)(2,1)S(1)}, bf16[512,128]{1,0:T(8,128)(2,1)S(1)}) custom-call(s32[16]{0:T(128)S(1)} %concatenate.93.meta, bf16[512,128]{1,0:T(8,128)(2,1)S(1)} %get-tuple-element.110.refs_0_, bf16[512,128]{1,0:T(8,128)(2,1)S(1)} %collective-permute-done.26.refs_1_, bf16[2,512,128]{2,1,0:T(8,128)(2,1)S(1)} %get-tuple-element.112.refs_2_, ...), custom_call_target="tpu_custom_call" | custom-call | flops 1073741824 | bytes 1048576 | tf_op jit(solution)/shard_map/attention/pallas_call | solution.py:319
  142.3 5.9 %collective-permute-done.31.refs_0_ = bf16[512,256]{1,0:T(8,128)(2,1)S(1)} collective-permute-done((bf16[512,256]{1,0:T(8,128)(2,1)S(1)}, bf16[512,256]{1,0:T(8,128)(2,1)S(1)}, u32[]{:S(2)}, u32[]{:S(2)}) %collective-permute-start.31) | collective-permute-done | bytes 262176 | tf_op jit(solution)/shard_map/ppermute | solution.py:555
  151.6 11.6 %collective-permute-done.20.refs_4_ = bf16[2,512,128]{2,1,0:T(8,128)(2,1)S(1)} collective-permute-done((bf16[2,512,128]{2,1,0:T(8,128)(2,1)S(1)}, bf16[2,512,128]{2,1,0:T(8,128)(2,1)S(1)}, u32[]{:S(2)}, u32[]{:S(2)}) %collective-permute-start.20) | collective-permute-done | bytes 262176 | tf_op jit(solution)/shard_map/ppermute | solution.py:701
  163.3 4.4 %attention.2 = (bf16[512,128]{1,0:T(8,128)(2,1)S(1)}, bf16[512,128]{1,0:T(8,128)(2,1)S(1)}) custom-call(s32[16]{0:T(128)S(1)} %concatenate.93.meta, bf16[512,128]{1,0:T(8,128)(2,1)S(1)} %get-tuple-element.104.refs_0_, bf16[512,128]{1,0:T(8,128)(2,1)S(1)} %collective-permute-done.18.refs_1_, bf16[2,512,128]{2,1,0:T(8,128)(2,1)S(1)} %get-tuple-element.106.refs_2_, ...), custom_call_target="tpu_custom_call" | custom-call | flops 1073741824 | bytes 1048576 | tf_op jit(solution)/shard_map/attention/pallas_call | solution.py:319
  173.6 5.4 %collective-permute-done.35.refs_0_ = bf16[512,256]{1,0:T(8,128)(2,1)S(1)} collective-permute-done((bf16[512,256]{1,0:T(8,128)(2,1)S(1)}, bf16[512,256]{1,0:T(8,128)(2,1)S(1)}, u32[]{:S(2)}, u32[]{:S(2)}) %collective-permute-start.35) | collective-permute-done | bytes 262176 | tf_op jit(solution)/shard_map/ppermute | solution.py:555
  181.7 4.0 %collective-permute-done.37.refs_0_ = bf16[256,256]{1,0:T(8,128)(2,1)S(1)} collective-permute-done((bf16[256,256]{1,0:T(8,128)(2,1)S(1)}, bf16[256,256]{1,0:T(8,128)(2,1)S(1)}, u32[]{:S(2)}, u32[]{:S(2)}) %collective-permute-start.37) | collective-permute-done | bytes 131104 | tf_op jit(solution)/shard_map/ppermute | solution.py:555
  192.9 4.4 %collective-permute-done.39.refs_0_ = bf16[512,256]{1,0:T(8,128)(2,1)S(1)} collective-permute-done((bf16[512,256]{1,0:T(8,128)(2,1)S(1)}, bf16[512,256]{1,0:T(8,128)(2,1)S(1)}, u32[]{:S(2)}, u32[]{:S(2)}) %collective-permute-start.39) | collective-permute-done | bytes 262176 | tf_op jit(solution)/shard_map/ppermute | solution.py:555
  197.8 4.2 %collective-permute-start.58 = (bf16[8,256,256]{2,1,0:T(8,128)(2,1)S(1)}, bf16[8,256,256]{2,1,0:T(8,128)(2,1)}, u32[]{:S(2)}, u32[]{:S(2)}) collective-permute-start(bf16[8,256,256]{2,1,0:T(8,128)(2,1)S(1)} %bitcast_dynamic-update-slice_fusion.refs_1_.refs_2_.refs_6_), channel_id=1, source_target_pairs={{0,1},{1,0},{2,3},{3,2},{4,5},{5,4},{6,7},{7,6},{8,9},{9,8},{10,11... | collective-permute-start | bytes 3145736 | tf_op jit(solution)/shard_map/ppermute | solution.py:54
  212.6 6.5 %collective-permute-start.45 = (bf16[512,256]{1,0:T(8,128)(2,1)S(1)}, bf16[512,256]{1,0:T(8,128)(2,1)S(1)}, u32[]{:S(2)}, u32[]{:S(2)}) collective-permute-start(bf16[512,256]{1,0:T(8,128)(2,1)S(1)} %get-tuple-element.141), channel_id=1, source_target_pairs={{0,1},{1,0},{2,3},{3,2},{4,5},{5,4},{6,7},{7,6},{8,9},{9,8},{10,11... | collective-permute-start | bytes 786440 | tf_op jit(solution)/shard_map/ppermute | solution.py:54
  223.7 2.7 collective-permute-done.46.refs_1_
  226.4 3.3 %collective-permute-done.48.refs_3_ = bf16[256,256]{1,0:T(8,128)(2,1)S(1)} collective-permute-done((bf16[256,256]{1,0:T(8,128)(2,1)S(1)}, bf16[256,256]{1,0:T(8,128)(2,1)S(1)}, u32[]{:S(2)}, u32[]{:S(2)}) %collective-permute-start.48) | collective-permute-done | bytes 131104 | tf_op jit(solution)/shard_map/ppermute | solution.py:701
  231.8 7.7 %collective-permute-done.49.refs_0_ = bf16[256,512]{1,0:T(8,128)(2,1)S(1)} collective-permute-done((bf16[256,512]{1,0:T(8,128)(2,1)S(1)}, bf16[256,512]{1,0:T(8,128)(2,1)S(1)}, u32[]{:S(2)}, u32[]{:S(2)}) %collective-permute-start.49) | collective-permute-done | bytes 262176 | tf_op jit(solution)/shard_map/ppermute | solution.py:555
  241.9 6.6 %collective-permute-done.61.refs_0_ = bf16[256,512]{1,0:T(8,128)(2,1)S(1)} collective-permute-done((bf16[256,512]{1,0:T(8,128)(2,1)S(1)}, bf16[256,512]{1,0:T(8,128)(2,1)S(1)}, u32[]{:S(2)}, u32[]{:S(2)}) %collective-permute-start.61) | collective-permute-done | bytes 262176 | tf_op jit(solution)/shard_map/ppermute | solution.py:555
  250.7 5.7 %collective-permute-done.63.refs_0_ = bf16[256,512]{1,0:T(8,128)(2,1)S(1)} collective-permute-done((bf16[256,512]{1,0:T(8,128)(2,1)S(1)}, bf16[256,512]{1,0:T(8,128)(2,1)S(1)}, u32[]{:S(2)}, u32[]{:S(2)}) %collective-permute-start.63) | collective-permute-done | bytes 262176 | tf_op jit(solution)/shard_map/ppermute | solution.py:555
  261.8 2.5 collective-permute-done.66.refs_1_
  268.1 2.7 collective-permute-start.69
  275.5 6.2 %collective-permute-start.71 = (f32[64,128]{1,0:T(8,128)S(1)}, f32[64,128]{1,0:T(8,128)S(1)}, u32[]{:S(2)}, u32[]{:S(2)}) collective-permute-start(f32[64,128]{1,0:T(8,128)S(1)} %add.262), channel_id=1, source_target_pairs={{0,1},{1,0},{2,3},{3,2},{4,5},{5,4},{6,7},{7,6},{8,9},{9,8},{10,11... | collective-permute-start | bytes 98312 | tf_op jit(solution)/shard_map/ppermute | solution.py:54
  (291 shorter events, 122.2 us)
Async XLA Ops:
  5.0 43.5 %collective-permute-start.10 = (bf16[4096,256]{1,0:T(8,128)(2,1)}, bf16[4096,256]{1,0:T(8,128)(2,1)}, u32[]{:S(2)}, u32[]{:S(2)}) collective-permute-start(bf16[4096,256]{1,0:T(8,128)(2,1)} %refs_7_.9), channel_id=1, source_target_pairs={{0,1},{1,0},{2,3},{3,2},{4,5},{5,4},{6,7},{7,6},{8,9},{9,8},{10,11... | collective-permute-start | bytes 6291464 | tf_op jit(solution)/shard_map/ppermute | solution.py:54
  5.3 43.2 %collective-permute-start.11 = (bf16[4096,256]{1,0:T(8,128)(2,1)}, bf16[4096,256]{1,0:T(8,128)(2,1)}, u32[]{:S(2)}, u32[]{:S(2)}) collective-permute-start(bf16[4096,256]{1,0:T(8,128)(2,1)} %refs_8_.7), channel_id=1, source_target_pairs={{0,1},{1,0},{2,3},{3,2},{4,5},{5,4},{6,7},{7,6},{8,9},{9,8},{10,11... | collective-permute-start | bytes 6291464 | tf_op jit(solution)/shard_map/ppermute | solution.py:54
  5.5 43.0 %collective-permute-start.9 = (bf16[4096,256]{1,0:T(8,128)(2,1)}, bf16[4096,256]{1,0:T(8,128)(2,1)}, u32[]{:S(2)}, u32[]{:S(2)}) collective-permute-start(bf16[4096,256]{1,0:T(8,128)(2,1)} %refs_6_.3), channel_id=1, source_target_pairs={{0,1},{1,0},{2,3},{3,2},{4,5},{5,4},{6,7},{7,6},{8,9},{9,8},{10,11... | collective-permute-start | bytes 6291464 | tf_op jit(solution)/shard_map/ppermute | solution.py:54
  46.7 15.1 %collective-permute-start.7 = (bf16[512,512]{1,0:T(8,128)(2,1)S(1)}, bf16[512,512]{1,0:T(8,128)(2,1)}, u32[]{:S(2)}, u32[]{:S(2)}) collective-permute-start(bf16[512,512]{1,0:T(8,128)(2,1)S(1)} %maximum_select_fusion.refs_0_), channel_id=1, source_target_pairs={{0,4},{4,8},{8,12},{12,0},{1,5},{5,9},{9,13},{13,1},{2,6},{6,10},{... | collective-permute-start | bytes 1572872 | tf_op jit(solution)/shard_map/ppermute | solution.py:555
  46.8 15.0 %collective-permute-start.8 = (bf16[512,512]{1,0:T(8,128)(2,1)S(1)}, bf16[512,512]{1,0:T(8,128)(2,1)}, u32[]{:S(2)}, u32[]{:S(2)}) collective-permute-start(bf16[512,512]{1,0:T(8,128)(2,1)S(1)} %maximum_select_fusion.refs_0_), channel_id=1, source_target_pairs={{0,2},{2,0},{1,3},{3,1},{4,6},{6,4},{5,7},{7,5},{8,10},{10,8},{9,1... | collective-permute-start | bytes 1572872 | tf_op jit(solution)/shard_map/ppermute | solution.py:555
  61.8 14.4 %collective-permute-start.12 = (bf16[512,512]{1,0:T(8,128)(2,1)}, bf16[512,512]{1,0:T(8,128)(2,1)}, u32[]{:S(2)}, u32[]{:S(2)}) collective-permute-start(bf16[512,512]{1,0:T(8,128)(2,1)} %collective-permute-done.7.refs_0_), channel_id=1, source_target_pairs={{0,4},{4,8},{8,12},{12,0},{1,5},{5,9},{9,13},{13,1},{2,6},{6,10},{... | collective-permute-start | bytes 1572872 | tf_op jit(solution)/shard_map/ppermute | solution.py:555
  61.9 14.3 %collective-permute-start.13 = (bf16[512,512]{1,0:T(8,128)(2,1)}, bf16[512,512]{1,0:T(8,128)(2,1)S(1)}, u32[]{:S(2)}, u32[]{:S(2)}) collective-permute-start(bf16[512,512]{1,0:T(8,128)(2,1)} %collective-permute-done.7.refs_0_), channel_id=1, source_target_pairs={{0,2},{2,0},{1,3},{3,1},{4,6},{6,4},{5,7},{7,5},{8,10},{10,8},{9,1... | collective-permute-start | bytes 1572872 | tf_op jit(solution)/shard_map/ppermute | solution.py:555
  77.0 20.0 %collective-permute-start.14 = (bf16[512,512]{1,0:T(8,128)(2,1)}, bf16[512,512]{1,0:T(8,128)(2,1)}, u32[]{:S(2)}, u32[]{:S(2)}) collective-permute-start(bf16[512,512]{1,0:T(8,128)(2,1)} %collective-permute-done.12.refs_0_), channel_id=1, source_target_pairs={{0,4},{4,8},{8,12},{12,0},{1,5},{5,9},{9,13},{13,1},{2,6},{6,10},{... | collective-permute-start | bytes 1572872 | tf_op jit(solution)/shard_map/ppermute | solution.py:555
  77.0 22.9 %collective-permute-start.15 = (bf16[512,512]{1,0:T(8,128)(2,1)}, bf16[512,512]{1,0:T(8,128)(2,1)}, u32[]{:S(2)}, u32[]{:S(2)}) collective-permute-start(bf16[512,512]{1,0:T(8,128)(2,1)} %collective-permute-done.12.refs_0_), channel_id=1, source_target_pairs={{0,2},{2,0},{1,3},{3,1},{4,6},{6,4},{5,7},{7,5},{8,10},{10,8},{9,1... | collective-permute-start | bytes 1572872 | tf_op jit(solution)/shard_map/ppermute | solution.py:555
  78.0 62.5 %collective-permute-start.25 = (bf16[4096,256]{1,0:T(8,128)(2,1)S(1)}, bf16[4096,256]{1,0:T(8,128)(2,1)}, u32[]{:S(2)}, u32[]{:S(2)}) collective-permute-start(bf16[4096,256]{1,0:T(8,128)(2,1)S(1)} %copy-done.1), channel_id=1, source_target_pairs={{0,1},{1,0},{2,3},{3,2},{4,5},{5,4},{6,7},{7,6},{8,9},{9,8},{10,11... | collective-permute-start | bytes 6291464 | tf_op jit(solution)/shard_map/ppermute | solution.py:54
  82.6 19.9 %collective-permute-start.51 = (bf16[256,256]{1,0:T(8,128)(2,1)}, bf16[256,256]{1,0:T(8,128)(2,1)}, u32[]{:S(2)}, u32[]{:S(2)}) collective-permute-start(bf16[256,256]{1,0:T(8,128)(2,1)} %get-tuple-element.163), channel_id=1, source_target_pairs={{0,2},{2,0},{4,6},{6,4},{8,10},{10,8},{12,14},{14,12},{1,3},{3,1},... | collective-permute-start | bytes 393224 | tf_op jit(solution)/shard_map/ppermute | solution.py:605
  83.1 33.5 %collective-permute-start.52 = (bf16[256,256]{1,0:T(8,128)(2,1)}, bf16[256,256]{1,0:T(8,128)(2,1)}, u32[]{:S(2)}, u32[]{:S(2)}) collective-permute-start(bf16[256,256]{1,0:T(8,128)(2,1)} %get-tuple-element.162), channel_id=1, source_target_pairs={{0,4},{2,6},{4,8},{6,10},{8,12},{10,14},{12,0},{14,2},{1,5},{3,7},... | collective-permute-start | bytes 393224 | tf_op jit(solution)/shard_map/ppermute | solution.py:605
  97.0 20.8 %collective-permute-start.53 = (bf16[256,256]{1,0:T(8,128)(2,1)S(1)}, bf16[256,256]{1,0:T(8,128)(2,1)S(1)}, u32[]{:S(2)}, u32[]{:S(2)}) collective-permute-start(bf16[256,256]{1,0:T(8,128)(2,1)S(1)} %copy-done.29), channel_id=1, source_target_pairs={{0,6},{2,4},{4,10},{6,8},{8,14},{10,12},{12,2},{14,0},{1,7},{3,5},... | collective-permute-start | bytes 393224 | tf_op jit(solution)/shard_map/ppermute | solution.py:605
  100.9 10.0 %collective-permute-start.16 = (bf16[256,512]{1,0:T(8,128)(2,1)S(1)}, bf16[256,512]{1,0:T(8,128)(2,1)S(1)}, u32[]{:S(2)}, u32[]{:S(2)}) collective-permute-start(bf16[256,512]{1,0:T(8,128)(2,1)S(1)} %slice.72), channel_id=1, source_target_pairs={{0,2},{2,0},{1,3},{3,1},{4,6},{6,4},{5,7},{7,5},{8,10},{10,8},{9,1... | collective-permute-start | bytes 786440 | tf_op jit(solution)/shard_map/ppermute | solution.py:555
  116.4 13.3 %collective-permute-start.29 = (bf16[2,512,128]{2,1,0:T(8,128)(2,1)S(1)}, bf16[2,512,128]{2,1,0:T(8,128)(2,1)S(1)}, u32[]{:S(2)}, u32[]{:S(2)}) collective-permute-start(bf16[2,512,128]{2,1,0:T(8,128)(2,1)S(1)} %get-tuple-element.113), channel_id=1, source_target_pairs={{0,17},{1,16},{16,1},{17,0},{2,19},{3,18},{18,3},{19,2},{4,21},{5,... | collective-permute-start | bytes 786440 | tf_op jit(solution)/shard_map/ppermute | solution.py:701
  116.6 13.1 %collective-permute-start.28 = (bf16[2,512,128]{2,1,0:T(8,128)(2,1)S(1)}, bf16[2,512,128]{2,1,0:T(8,128)(2,1)S(1)}, u32[]{:S(2)}, u32[]{:S(2)}) collective-permute-start(bf16[2,512,128]{2,1,0:T(8,128)(2,1)S(1)} %get-tuple-element.112.refs_2_), channel_id=1, source_target_pairs={{0,16},{1,17},{16,0},{17,1},{2,18},{3,19},{18,2},{19,3},{4,20},{5,... | collective-permute-start | bytes 786440 | tf_op jit(solution)/shard_map/ppermute | solution.py:701
  119.5 16.6 %collective-permute-start.54 = (bf16[256,256]{1,0:T(8,128)(2,1)S(1)}, bf16[256,256]{1,0:T(8,128)(2,1)S(1)}, u32[]{:S(2)}, u32[]{:S(2)}) collective-permute-start(bf16[256,256]{1,0:T(8,128)(2,1)S(1)} %copy-done.28), channel_id=1, source_target_pairs={{0,8},{2,10},{4,12},{6,14},{8,0},{10,2},{12,4},{14,6},{1,9},{3,11}... | collective-permute-start | bytes 393224 | tf_op jit(solution)/shard_map/ppermute | solution.py:605
  119.7 19.2 %collective-permute-start.55 = (bf16[256,256]{1,0:T(8,128)(2,1)S(1)}, bf16[256,256]{1,0:T(8,128)(2,1)S(1)}, u32[]{:S(2)}, u32[]{:S(2)}) collective-permute-start(bf16[256,256]{1,0:T(8,128)(2,1)S(1)} %copy-done.27), channel_id=1, source_target_pairs={{0,10},{2,8},{4,14},{6,12},{8,2},{10,0},{12,6},{14,4},{1,11},{3,9}... | collective-permute-start | bytes 393224 | tf_op jit(solution)/shard_map/ppermute | solution.py:605
  129.8 21.0 %collective-permute-start.57 = (bf16[256,256]{1,0:T(8,128)(2,1)S(1)}, bf16[256,256]{1,0:T(8,128)(2,1)S(1)}, u32[]{:S(2)}, u32[]{:S(2)}) collective-permute-start(bf16[256,256]{1,0:T(8,128)(2,1)S(1)} %copy-done.25), channel_id=1, source_target_pairs={{0,14},{2,12},{4,2},{6,0},{8,6},{10,4},{12,10},{14,8},{1,15},{3,13... | collective-permute-start | bytes 393224 | tf_op jit(solution)/shard_map/ppermute | solution.py:605
  138.9 10.6 %collective-permute-start.32 = (bf16[512,256]{1,0:T(8,128)(2,1)S(1)}, bf16[512,256]{1,0:T(8,128)(2,1)S(1)}, u32[]{:S(2)}, u32[]{:S(2)}) collective-permute-start(bf16[512,256]{1,0:T(8,128)(2,1)S(1)} %maximum_select_fusion.3.refs_0_), channel_id=1, source_target_pairs={{0,2},{2,0},{1,3},{3,1},{4,6},{6,4},{5,7},{7,5},{8,10},{10,8},{9,1... | collective-permute-start | bytes 786440 | tf_op jit(solution)/shard_map/ppermute | solution.py:555
  139.5 11.9 %collective-permute-start.19 = (bf16[2,512,128]{2,1,0:T(8,128)(2,1)S(1)}, bf16[2,512,128]{2,1,0:T(8,128)(2,1)S(1)}, u32[]{:S(2)}, u32[]{:S(2)}) collective-permute-start(bf16[2,512,128]{2,1,0:T(8,128)(2,1)S(1)} %get-tuple-element.107), channel_id=1, source_target_pairs={{0,1},{1,0},{2,3},{3,2},{4,5},{5,4},{6,7},{7,6},{8,9},{9,8},{10,11... | collective-permute-start | bytes 786440 | tf_op jit(solution)/shard_map/ppermute | solution.py:54
  140.4 10.3 %collective-permute-start.18 = (bf16[512,128]{1,0:T(8,128)(2,1)S(1)}, bf16[512,128]{1,0:T(8,128)(2,1)S(1)}, u32[]{:S(2)}, u32[]{:S(2)}) collective-permute-start(bf16[512,128]{1,0:T(8,128)(2,1)S(1)} %get-tuple-element.105), channel_id=1, source_target_pairs={{0,1},{1,0},{2,3},{3,2},{4,5},{5,4},{6,7},{7,6},{8,9},{9,8},{10,11... | collective-permute-start | bytes 393224 | tf_op jit(solution)/shard_map/ppermute | solution.py:54
  148.2 15.1 %collective-permute-start.21 = (bf16[2,512,128]{2,1,0:T(8,128)(2,1)S(1)}, bf16[2,512,128]{2,1,0:T(8,128)(2,1)S(1)}, u32[]{:S(2)}, u32[]{:S(2)}) collective-permute-start(bf16[2,512,128]{2,1,0:T(8,128)(2,1)S(1)} %get-tuple-element.107), channel_id=1, source_target_pairs={{0,17},{1,16},{16,1},{17,0},{2,19},{3,18},{18,3},{19,2},{4,21},{5,... | collective-permute-start | bytes 786440 | tf_op jit(solution)/shard_map/ppermute | solution.py:701
  149.5 13.7 %collective-permute-start.20 = (bf16[2,512,128]{2,1,0:T(8,128)(2,1)S(1)}, bf16[2,512,128]{2,1,0:T(8,128)(2,1)S(1)}, u32[]{:S(2)}, u32[]{:S(2)}) collective-permute-start(bf16[2,512,128]{2,1,0:T(8,128)(2,1)S(1)} %get-tuple-element.106.refs_2_), channel_id=1, source_target_pairs={{0,16},{1,17},{16,0},{17,1},{2,18},{3,19},{18,2},{19,3},{4,20},{5,... | collective-permute-start | bytes 786440 | tf_op jit(solution)/shard_map/ppermute | solution.py:701
  150.7 19.0 %collective-permute-start.33 = (bf16[512,256]{1,0:T(8,128)(2,1)S(1)}, bf16[512,256]{1,0:T(8,128)(2,1)S(1)}, u32[]{:S(2)}, u32[]{:S(2)}) collective-permute-start(bf16[512,256]{1,0:T(8,128)(2,1)S(1)} %collective-permute-done.31.refs_0_), channel_id=1, source_target_pairs={{0,4},{4,8},{8,12},{12,0},{1,5},{5,9},{9,13},{13,1},{2,6},{6,10},{... | collective-permute-start | bytes 786440 | tf_op jit(solution)/shard_map/ppermute | solution.py:555
  150.8 19.0 %collective-permute-start.34 = (bf16[512,256]{1,0:T(8,128)(2,1)S(1)}, bf16[512,256]{1,0:T(8,128)(2,1)S(1)}, u32[]{:S(2)}, u32[]{:S(2)}) collective-permute-start(bf16[512,256]{1,0:T(8,128)(2,1)S(1)} %collective-permute-done.31.refs_0_), channel_id=1, source_target_pairs={{0,2},{2,0},{1,3},{3,1},{4,6},{6,4},{5,7},{7,5},{8,10},{10,8},{9,1... | collective-permute-start | bytes 786440 | tf_op jit(solution)/shard_map/ppermute | solution.py:555
  151.4 50.7 %collective-permute-start.59 = (bf16[8,256,256]{2,1,0:T(8,128)(2,1)S(1)}, bf16[8,256,256]{2,1,0:T(8,128)(2,1)}, u32[]{:S(2)}, u32[]{:S(2)}) collective-permute-start(bf16[8,256,256]{2,1,0:T(8,128)(2,1)S(1)} %bitcast_dynamic-update-slice_fusion.refs_1_.refs_2_.refs_6_), channel_id=1, source_target_pairs={{0,16},{16,0},{1,17},{17,1},{2,18},{18,2},{3,19},{19,3},{4,20},{20... | collective-permute-start | bytes 3145736 | tf_op jit(solution)/shard_map/ppermute | solution.py:555
  170.5 19.7 %collective-permute-start.23 = (bf16[512,256]{1,0:T(8,128)(2,1)S(1)}, bf16[512,256]{1,0:T(8,128)(2,1)S(1)}, u32[]{:S(2)}, u32[]{:S(2)}) collective-permute-start(bf16[512,256]{1,0:T(8,128)(2,1)S(1)} %maximum_select_fusion.2.refs_0_), channel_id=1, source_target_pairs={{0,4},{4,8},{8,12},{12,0},{1,5},{5,9},{9,13},{13,1},{2,6},{6,10},{... | collective-permute-start | bytes 786440 | tf_op jit(solution)/shard_map/ppermute | solution.py:555
  170.6 19.6 %collective-permute-start.24 = (bf16[512,256]{1,0:T(8,128)(2,1)S(1)}, bf16[512,256]{1,0:T(8,128)(2,1)S(1)}, u32[]{:S(2)}, u32[]{:S(2)}) collective-permute-start(bf16[512,256]{1,0:T(8,128)(2,1)S(1)} %maximum_select_fusion.2.refs_0_), channel_id=1, source_target_pairs={{0,2},{2,0},{1,3},{3,1},{4,6},{6,4},{5,7},{7,5},{8,10},{10,8},{9,1... | collective-permute-start | bytes 786440 | tf_op jit(solution)/shard_map/ppermute | solution.py:555
  197.8 32.7 %collective-permute-start.58 = (bf16[8,256,256]{2,1,0:T(8,128)(2,1)S(1)}, bf16[8,256,256]{2,1,0:T(8,128)(2,1)}, u32[]{:S(2)}, u32[]{:S(2)}) collective-permute-start(bf16[8,256,256]{2,1,0:T(8,128)(2,1)S(1)} %bitcast_dynamic-update-slice_fusion.refs_1_.refs_2_.refs_6_), channel_id=1, source_target_pairs={{0,1},{1,0},{2,3},{3,2},{4,5},{5,4},{6,7},{7,6},{8,9},{9,8},{10,11... | collective-permute-start | bytes 3145736 | tf_op jit(solution)/shard_map/ppermute | solution.py:54
  202.0 28.5 %collective-permute-start.60 = (bf16[8,256,256]{2,1,0:T(8,128)(2,1)}, bf16[8,256,256]{2,1,0:T(8,128)(2,1)}, u32[]{:S(2)}, u32[]{:S(2)}) collective-permute-start(bf16[8,256,256]{2,1,0:T(8,128)(2,1)} %collective-permute-done.59.refs_3_.refs_4_.refs_8_), channel_id=1, source_target_pairs={{0,1},{1,0},{2,3},{3,2},{4,5},{5,4},{6,7},{7,6},{8,9},{9,8},{10,11... | collective-permute-start | bytes 3145736 | tf_op jit(solution)/shard_map/ppermute | solution.py:54
  229.8 9.8 %collective-permute-start.49 = (bf16[256,512]{1,0:T(8,128)(2,1)S(1)}, bf16[256,512]{1,0:T(8,128)(2,1)S(1)}, u32[]{:S(2)}, u32[]{:S(2)}) collective-permute-start(bf16[256,512]{1,0:T(8,128)(2,1)S(1)} %merge_picks.1.refs_0_), channel_id=1, source_target_pairs={{0,4},{4,8},{8,12},{12,0},{1,5},{5,9},{9,13},{13,1},{2,6},{6,10},{... | collective-permute-start | bytes 786440 | tf_op jit(solution)/shard_map/ppermute | solution.py:555
  (73 other events, 759.2 us)

commit v4 on v3

v4 whole, which is shorter than its diff:
```python
import functools

import jax
import jax.numpy as jnp
from jax import lax
from jax.experimental import pallas as pl
from jax.experimental.pallas import tpu as pltpu
from jax.sharding import Mesh
from jax.sharding import PartitionSpec as P

HD = 128
CH = 256
CIN = 8
WL = 64
HL = 64
PATCH = 4
PIX = PATCH * PATCH
SIDE = WL // PATCH
IMG_TOK = 256
EPSILON = 1e-05
NEGATIVE_FILL = -1e30
WINDOW = (PATCH + 2) * CIN
TAPS = 3 * WINDOW
BF16 = jnp.bfloat16
F32 = jnp.float32


def split_meta(meta, images):
    return meta[3 * images], meta[3 * images + 1], meta[3 * images + 2], meta[3 * images + 3]


def params(mebibytes):
    return pltpu.CompilerParams(
        dimension_semantics=("arbitrary",), vmem_limit_bytes=mebibytes * 1024 * 1024
    )


def cost(flops, nbytes, transcendentals=0):
    return pl.CostEstimate(
        flops=int(flops), bytes_accessed=int(nbytes), transcendentals=int(transcendentals)
    )


def silu(values):
    half = values * 0.5
    return half + half * jnp.tanh(half)


def mxu(left, right):
    return jnp.dot(left, right, preferred_element_type=F32)


def swap(values):
    return lax.ppermute(values, "core", [(0, 1), (1, 0)])


GAIN_ROWS = 16
TOP = 16


def down_kernel(images, tiles, half, meta, *refs):
    lat_refs, refs = refs[:tiles], refs[tiles:]
    conv_ref, patch_ref, own_text, par_text, gain_ref, first_ref, second_ref = refs[:7]
    grid_rows, conv_wide, conv_bf16, windows, total = refs[7:]
    step = pl.program_id(0)
    group = images * SIDE
    ctx, core, tile, _ = split_meta(meta, images)

    @pl.when(step == 0)
    def _():
        grid_rows[...] = jnp.zeros_like(grid_rows)
        blocks = grid_rows.shape[1]
        for index in range(tiles):
            band = lat_refs[index].shape[1]
            at = TOP + lax.rem(tile + tiles - index, tiles) * band
            rows = pl.ds(pl.multiple_of(at, 8), band)
            latent = lat_refs[index][...].astype(F32)
            edges = [jnp.zeros((images, band, size), F32) for size in (CIN, HD - CIN)]
            wide = jnp.concatenate([edges[0], latent, edges[1]], axis=2)
            for part in range(blocks):
                grid_rows[:, part, rows, :] = wide[:, :, part * HD : (part + 1) * HD]
        conv_wide[...] = jnp.zeros_like(conv_wide)
        conv = conv_ref[...].astype(F32)
        for col in range(PATCH):
            for tap in range(3):
                at = WINDOW * tap + CIN * col
                conv_wide[at : at + 3 * CIN, CH * col : CH * (col + 1)] = conv[
                    3 * CIN * tap : 3 * CIN * (tap + 1), :
                ]
        conv_bf16[...] = conv_wide[...].astype(BF16)

        def build(image, carry):
            for row in range(PATCH + 2):
                take = pl.ds(TOP - 1 + row, SIDE, stride=PATCH)
                line = [grid_rows[image, part, take, :] for part in range(blocks)]
                line = jnp.concatenate(line, axis=1).astype(BF16)
                for col in range(SIDE):
                    piece = line[:, PATCH * CIN * col : PATCH * CIN * col + WINDOW]
                    at = pl.ds(pl.multiple_of(group * col + image * SIDE, SIDE), SIDE)
                    for shift in range(3):
                        if 0 <= row - shift < PATCH:
                            windows[row - shift, at, WINDOW * shift : WINDOW * (shift + 1)] = piece
            return carry

        lax.fori_loop(0, images, build, 0)
        total[...] = jnp.zeros_like(total)

    chunk = 256
    for part in range(images * IMG_TOK // chunk):
        rows = slice(part * chunk, (part + 1) * chunk)
        hidden = silu(mxu(windows[step, rows, :], conv_bf16[...])).astype(BF16)
        total[rows, :] += mxu(hidden, patch_ref[...])

    @pl.when(step == PATCH - 1)
    def _():
        tokens = total[...].astype(BF16)
        block = half // 2
        for side, text_ref in enumerate((own_text, par_text)):
            base = ctx * (2 * half) + jnp.bitwise_xor(core, side) * half
            for part, out_ref in enumerate((first_ref, second_ref)):
                place = base + part * block + lax.broadcasted_iota(jnp.int32, (block, 1), 0)
                source = jnp.full((block, 1), -1, jnp.int32)
                for image in range(images):
                    inner = place - meta[image]
                    inside = (inner >= 0) & (inner < IMG_TOK)
                    index = (inner & (SIDE - 1)) * group + meta[images + image] * SIDE + (inner >> 4)
                    source = jnp.where(inside, index, source)
                choice = source == lax.broadcasted_iota(jnp.int32, (block, images * IMG_TOK), 1)
                picked = mxu(jnp.where(choice, 1.0, 0.0).astype(BF16), tokens)
                text = text_ref[0, part * block : (part + 1) * block, :].astype(F32)
                out_ref[side, :block, :] = jnp.where(source >= 0, picked, text).astype(BF16)
            gain = gain_ref[...].astype(F32)
            first_ref[side, block:, :] = jnp.broadcast_to(gain, (GAIN_ROWS, gain.shape[1])).astype(BF16)


def down_stream(meta, pieces, conv, patch_in, text, gain, images):
    seq_rows, width = text.shape
    half = seq_rows // 2
    tiles = len(pieces)
    count = images * IMG_TOK
    halves = text.reshape(2, half, width)
    core_at = 3 * images + 1
    first, second = (2, half // 2 + GAIN_ROWS, width), (2, half // 2, width)
    return pl.pallas_call(
        functools.partial(down_kernel, images, tiles, half),
        grid_spec=pltpu.PrefetchScalarGridSpec(
            num_scalar_prefetch=1,
            grid=(PATCH,),
            in_specs=[full(p.shape) for p in pieces]
            + [
                full(conv.shape),
                pl.BlockSpec((PATCH * CH, width), lambda i, m: (i, 0)),
                pl.BlockSpec((1, half, width), lambda i, m: (m[core_at], 0, 0)),
                pl.BlockSpec((1, half, width), lambda i, m: (1 - m[core_at], 0, 0)),
                full((1, width)),
            ],
            out_specs=[full(first), full(second)],
            scratch_shapes=[
                pltpu.VMEM((images, WL * CIN // HD + 1, TOP + HL + 16, HD), F32),
                pltpu.VMEM((TAPS, PATCH * CH), F32),
                pltpu.VMEM((TAPS, PATCH * CH), BF16),
                pltpu.VMEM((PATCH, count, TAPS), BF16),
                pltpu.VMEM((count, width), F32),
            ],
        ),
        out_shape=[jax.ShapeDtypeStruct(first, BF16), jax.ShapeDtypeStruct(second, BF16)],
        compiler_params=params(40),
        cost_estimate=cost(2 * count * PIX * CH * (256 + width), 4 << 20, count * PIX * CH),
        name="down_stream",
    )(meta, *pieces, conv, patch_in, halves, halves, gain.reshape(1, width))


def full(shape):
    return pl.BlockSpec(shape, lambda i, m: (0,) * len(shape))


def load(pieces):
    return jnp.concatenate([piece[...] for piece in pieces], axis=0)


def take_blocks(refs, count):
    return [[refs.pop(0), refs.pop(0)] for _ in range(count)]


def chip_of(meta, images, tiles, outer, entry):
    _, _, tile, mpo = split_meta(meta, images)
    return lax.rem(tile + tiles - entry // 2, tiles) * outer + lax.rem(mpo + entry % 2, outer)


def qkv_kernel(count, groups, first, last, meta, *refs):
    refs = list(refs)
    x_refs = take_blocks(refs, count)
    weight_refs = [[refs.pop(0) for _ in range(6)] for _ in range(count)]
    if not first:
        acc_in, square_in = refs.pop(0), refs.pop(0)
    if last:
        head_gains = refs.pop(0)
    scaled = refs.pop()
    half, span = scaled.shape[1:]
    chunk = 64

    def scale_rows(block, gain, piece, base, index, carry):
        rows = pl.ds(pl.multiple_of(base + index * chunk, chunk), chunk)
        local = pl.ds(pl.multiple_of(index * chunk, chunk), chunk)
        if block:
            square = square_out[rows, :]
        else:
            square = jnp.zeros((chunk, HD), F32) if first else square_in[rows, :]
        value = piece[local, :].astype(F32)
        scaled[block, rows, :] = (value * gain).astype(BF16)
        value = value * value
        for part in range(span // HD):
            square = square + value[:, part * HD : (part + 1) * HD]
        square_out[rows, :] = square
        return carry

    if last:
        square_out = refs.pop()
        outs = refs
    else:
        acc_out, square_out = refs
    for block in range(count):
        gain = x_refs[block][0][half // 2 :, :].astype(F32)[:1]
        for part in range(2):
            body = functools.partial(scale_rows, block, gain, x_refs[block][part], part * half // 2)
            lax.fori_loop(0, half // 2 // chunk, body, 0)
    width = weight_refs[0][0].shape[1]
    heads = width // HD
    if last:
        mean = jnp.sum(square_out[...], axis=-1, keepdims=True) * (1.0 / (groups * span))
        scale = lax.rsqrt(mean + EPSILON)
    for part in range(6):
        total = None if first else acc_in[part]
        for block in range(count):
            term = mxu(scaled[block], weight_refs[block][part][...])
            total = term if total is None else total + term
        if not last:
            acc_out[part] = total
            continue
        total = total * scale
        side, kind = part // 3, part % 3
        kv_outs = outs[2 * heads * side : 2 * heads * side + heads]
        q_outs = outs[2 * heads * side + heads : 2 * heads * side + 2 * heads]
        for head in range(heads):
            raw = total[:, head * HD : (head + 1) * HD]
            if kind == 1:
                kv_outs[head][1] = raw.astype(BF16)
                continue
            raw = raw * lax.rsqrt(jnp.mean(raw * raw, axis=-1, keepdims=True) + EPSILON)
            if kind == 0:
                kv_outs[head][0] = (raw * head_gains[1:2, :]).astype(BF16)
            else:
                q_outs[head][...] = (raw * (head_gains[0:1, :] * HD ** (-0.5))).astype(BF16)


def qkv_step(meta, layout, blocks, entries, weights, state, head_gains):
    span = blocks[0][1].shape[1]
    half = 2 * blocks[0][1].shape[0]
    width = weights[0].shape[1]
    heads = width // HD
    count, first, last = len(blocks), state is None, head_gains is not None
    groups = layout[1] * layout[2]
    inputs = [p for pieces in blocks for p in pieces]
    specs = [full(p.shape) for p in inputs]
    for entry in entries:
        for weight in weights:
            inputs.append(weight)
            specs.append(
                pl.BlockSpec((span, width), lambda i, m, entry=entry: (chip_of(m, *layout, entry), 0))
            )
    if not first:
        inputs += list(state)
        specs += [full(s.shape) for s in state]
    scratch = [pltpu.VMEM((count, half, span), BF16)]
    if last:
        inputs.append(head_gains)
        specs.append(full(head_gains.shape))
        kv, q = jax.ShapeDtypeStruct((2, half, HD), BF16), jax.ShapeDtypeStruct((half, HD), BF16)
        outs = ([kv] * heads + [q] * heads) * 2
        scratch = [pltpu.VMEM((half, HD), F32)] + scratch
    else:
        outs = [
            jax.ShapeDtypeStruct((6, half, width), F32),
            jax.ShapeDtypeStruct((half, HD), F32),
        ]
    return pl.pallas_call(
        functools.partial(qkv_kernel, count, groups, first, last),
        grid_spec=pltpu.PrefetchScalarGridSpec(
            num_scalar_prefetch=1,
            grid=(1,),
            in_specs=specs,
            out_specs=[full(o.shape) for o in outs],
            scratch_shapes=scratch,
        ),
        out_shape=outs,
        compiler_params=params(48),
        cost_estimate=cost(12 * count * half * span * width, (6 + 2 * count) << 20),
        name="qkv_last" if last else "qkv_step",
    )(meta, *inputs)


def attention_kernel(images, pieces, half, meta, *refs):
    ctx, core, _, _ = split_meta(meta, images)
    ctxs = pieces // 2
    bases = []
    for piece in range(pieces):
        side = jnp.bitwise_xor(core, piece % 2)
        bases.append(lax.rem(ctx + ctxs - piece // 2, ctxs) * (2 * half) + side * half)
    q_refs, kv_refs, out_refs = refs[:2], refs[2 : 2 + pieces], refs[2 + pieces :]
    rows = q_refs[0].shape[0]
    step = pl.program_id(0)
    for side in range(2):
        place = bases[side] + step * rows + lax.broadcasted_iota(jnp.int32, (rows, 1), 0)
        limit = place
        for image in range(images):
            inner = place - meta[image]
            limit = jnp.where((inner >= 0) & (inner < IMG_TOK), meta[image] + IMG_TOK - 1, limit)
        query = q_refs[side][...]
        scores = []
        top = None
        for piece in range(pieces):
            score = lax.dot_general(
                query, kv_refs[piece][0], (((1,), (1,)), ((), ())), preferred_element_type=F32
            )
            position = lax.broadcasted_iota(jnp.int32, score.shape, 1)
            score = jnp.where(position <= limit - bases[piece], score, NEGATIVE_FILL)
            scores.append(score)
            best = jnp.max(score, axis=1, keepdims=True)
            top = best if top is None else jnp.maximum(top, best)
        total = jnp.zeros((rows, 1), F32)
        product = jnp.zeros((rows, HD), F32)
        for piece in range(pieces):
            weight = jnp.exp(scores[piece] - top)
            total = total + jnp.sum(weight, axis=1, keepdims=True)
            product = product + mxu(weight.astype(BF16), kv_refs[piece][1])
        out_refs[side][...] = (product / total).astype(BF16)


def attention(meta, queries, pieces, images):
    half = queries[0].shape[0]
    block = 256
    keys = half * len(pieces)
    rows = pl.BlockSpec((block, HD), lambda i, m: (i, 0))
    return pl.pallas_call(
        functools.partial(attention_kernel, images, len(pieces), half),
        grid_spec=pltpu.PrefetchScalarGridSpec(
            num_scalar_prefetch=1,
            grid=(half // block,),
            in_specs=[rows, rows] + [full(p.shape) for p in pieces],
            out_specs=[rows, rows],
        ),
        out_shape=[jax.ShapeDtypeStruct((half, HD), BF16)] * 2,
        compiler_params=params(24),
        cost_estimate=cost(8 * half * keys * HD, 4 * keys * HD, 2 * half * keys),
        name="attention",
    )(meta, *queries, *pieces)


def out_kernel(count, heads, first, last, meta, *refs):
    refs = list(refs)
    x_refs = take_blocks(refs, count)
    weight_refs = [[refs.pop(0), refs.pop(0)] for _ in range(count)]
    if first:
        streams = [refs.pop(0), refs.pop(0)]
        block = streams[1].shape[1]
    else:
        acc_in = refs.pop(0)
    outs = refs
    for side in range(2):
        if first:
            rows = [streams[0][side, :block, :], streams[1][side]]
            total = jnp.concatenate(rows, axis=0).astype(F32)
        else:
            total = acc_in[side]
        for index in range(count):
            weight = weight_refs[index][side]
            if heads == 2:
                for head in range(heads):
                    part = weight[0, :, head].reshape(2 * HD, weight.shape[4])
                    total = total + mxu(x_refs[index][head][...], part)
            else:
                total = total + mxu(load(x_refs[index]), weight[0, :, 0].reshape(2 * HD, weight.shape[4]))
        if last:
            outs[side][...] = total.astype(BF16)
        else:
            outs[0][side] = total


def out_step(meta, layout, blocks, entries, weights, state, last):
    width = weights[0].shape[1]
    heads = width // HD
    half = blocks[0][0].shape[0] * (1 if heads == 2 else 2)
    first = isinstance(state, list)
    count = len(blocks)
    views = [w.reshape(-1, 2, heads, HD, width) for w in weights]
    inputs = [p for pieces in blocks for p in pieces]
    specs = [full(p.shape) for p in inputs]
    for entry in entries:
        for view in views:
            inputs.append(view)
            specs.append(
                pl.BlockSpec(
                    (1, 2, heads, HD, width),
                    lambda i, m, entry=entry: (chip_of(m, *layout, entry), 0, 0, 0, 0),
                )
            )
    states = state if first else [state]
    inputs += states
    specs += [full(s.shape) for s in states]
    if last:
        outs = [jax.ShapeDtypeStruct((half, width), BF16)] * 2
    else:
        outs = [jax.ShapeDtypeStruct((2, half, width), F32)]
    result = pl.pallas_call(
        functools.partial(out_kernel, count, heads, first, last),
        grid_spec=pltpu.PrefetchScalarGridSpec(
            num_scalar_prefetch=1,
            grid=(1,),
            in_specs=specs,
            out_specs=[full(o.shape) for o in outs],
        ),
        out_shape=outs,
        compiler_params=params(40),
        cost_estimate=cost(8 * count * half * heads * HD * width, (2 + count) << 20),
        name="out_last" if last else "out_step",
    )(meta, *inputs)
    return result if last else result[0]


def pick_kernel(images, ctxs, meta, own_ref, par_ref, *out_refs):
    half = own_ref.shape[0]
    ctx, core, _, _ = split_meta(meta, images)
    for target in range(2 * ctxs):
        to_core = jnp.bitwise_xor(core, target % 2)
        slot = 2 * lax.rem(ctx + target // 2, ctxs) + to_core
        start = meta[meta[2 * images + slot]]
        place = start + lax.broadcasted_iota(jnp.int32, (IMG_TOK, half), 0)
        column = ctx * (2 * half) + lax.broadcasted_iota(jnp.int32, (IMG_TOK, half), 1)
        own = jnp.where(place == column + core * half, 1.0, 0.0).astype(BF16)
        par = jnp.where(place == column + (1 - core) * half, 1.0, 0.0).astype(BF16)
        out_refs[target][...] = (mxu(own, own_ref[...]) + mxu(par, par_ref[...])).astype(BF16)


def pick_rows(meta, own, par, images, ctxs):
    half, width = own.shape
    targets = 2 * ctxs
    return pl.pallas_call(
        functools.partial(pick_kernel, images, ctxs),
        grid_spec=pltpu.PrefetchScalarGridSpec(
            num_scalar_prefetch=1,
            grid=(1,),
            in_specs=[full(own.shape), full(par.shape)],
            out_specs=[full((IMG_TOK, width))] * targets,
        ),
        out_shape=[jax.ShapeDtypeStruct((IMG_TOK, width), BF16)] * targets,
        compiler_params=params(16),
        cost_estimate=cost(targets * 4 * IMG_TOK * half * width, 1 << 20),
        name="pick_rows",
    )(meta, own, par)


def merge_kernel(*refs):
    out_refs = refs[-2:]
    refs = refs[:-2]
    sides = refs[: len(refs) // 2], refs[len(refs) // 2 :]
    width = sides[0][0].shape[1]
    block = IMG_TOK // 2
    for side in range(2):
        total = sides[side][0][...].astype(F32)
        for part in sides[side][1:]:
            total = total + part[...].astype(F32)
        total = total.astype(BF16)
        for index in range(2):
            out_refs[index][:, side * width : (side + 1) * width] = total[index * block : (index + 1) * block]


def merge_picks(own_parts, par_parts):
    width = own_parts[0].shape[1]
    return pl.pallas_call(
        merge_kernel,
        out_shape=[jax.ShapeDtypeStruct((IMG_TOK // 2, 2 * width), BF16)] * 2,
        compiler_params=pltpu.CompilerParams(vmem_limit_bytes=8 << 20),
        cost_estimate=cost(1 << 20, 1 << 20),
        name="merge_picks",
    )(*own_parts, *par_parts)


def finish_kernel(core_ref, own_a, own_b, par_a, par_b, out_ref, sums, lines):
    core = core_ref[0]
    for side, (left, right) in enumerate(((own_a, own_b), (par_a, par_b))):
        sums[side] = left[...] + right[...]
    rows = sums.shape[1] // SIDE
    lanes = PATCH * CIN
    per = HD // lanes
    for side in range(2):
        for part in range(SIDE // per):
            cols = [sums[side, pl.ds(part * per + k, rows, stride=SIDE), :] for k in range(per)]
            for row in range(PATCH):
                pieces = [col[:, row * lanes : (row + 1) * lanes] for col in cols]
                lines[part, pl.ds(row, rows, stride=PATCH), :] = jnp.concatenate(pieces, axis=1)
        slot = jnp.bitwise_xor(core, side)
        for part in range(SIDE // per):
            out_ref[slot, :, part * HD : (part + 1) * HD] = lines[part]


def finish(core, own_a, own_b, par_a, par_b):
    count = own_a.shape[0]
    return pl.pallas_call(
        finish_kernel,
        grid_spec=pltpu.PrefetchScalarGridSpec(
            num_scalar_prefetch=1,
            grid=(1,),
            in_specs=[full(own_a.shape)] * 4,
            out_specs=full((2, count // PATCH, WL * CIN)),
            scratch_shapes=[
                pltpu.VMEM((2, count, PIX * CIN), F32),
                pltpu.VMEM((WL * CIN // HD, count // PATCH, HD), F32),
            ],
        ),
        out_shape=jax.ShapeDtypeStruct((2, count // PATCH, WL * CIN), F32),
        compiler_params=params(8),
        cost_estimate=cost(1 << 16, 1 << 18),
        name="finish",
    )(core, own_a, own_b, par_a, par_b)


def spread(active, spread_ref):
    row = lax.broadcasted_iota(jnp.int32, (IMG_TOK, PIX * CIN), 0)
    patch_row, patch_col = row >> 4, row & (SIDE - 1)
    total = None
    for index in range(9):
        down, right = index // 3 - 1, index % 3 - 1
        part = mxu(active, spread_ref[:, index * PIX * CIN : (index + 1) * PIX * CIN])
        offset = down * SIDE + right
        if offset:
            part = pltpu.roll(part, offset % IMG_TOK, 0)
        source_row, source_col = patch_row - down, patch_col - right
        inside = (source_row >= 0) & (source_row < SIDE) & (source_col >= 0) & (source_col < SIDE)
        part = jnp.where(inside, part, 0.0)
        total = part if total is None else total + part
    return total


def up_kernel(count, halves, first, last, *refs):
    refs = list(refs)
    x_refs = take_blocks(refs, count)
    weight_refs = [[[refs.pop(0) for _ in range(2)] for _ in range(halves)] for _ in range(count)]
    acc_in = None if first else refs.pop(0)
    spread_ref = refs.pop(0) if last else None
    out_ref = refs[0]
    width = x_refs[0][0].shape[1] // 2
    values = [load(pieces) for pieces in x_refs]
    totals = []
    for part in range(halves):
        total = None if first else acc_in[part]
        for block in range(count):
            for side in range(2):
                term = mxu(
                    values[block][:, side * width : (side + 1) * width],
                    weight_refs[block][part][side][0],
                )
                total = term if total is None else total + term
        totals.append(total)
        if not last:
            out_ref[part] = total
    if last:
        active = [silu(total).astype(BF16) for total in totals]
        active = jnp.concatenate(active, axis=1) if halves > 1 else active[0]
        out_ref[...] = spread(active, spread_ref)


def up_step(blocks, entries, tiles, first_weights, second_weights, state, spread_weight):
    span = blocks[0][0].shape[1]
    halves, count = len(first_weights), len(blocks)
    first, last = state is None, spread_weight is not None
    whole = lambda shape: pl.BlockSpec(shape, lambda i: (0,) * len(shape))
    inputs = [p for pieces in blocks for p in pieces]
    specs = [whole(p.shape) for p in inputs]
    for entry in entries:
        apart = entry // 2 == tiles // 2
        offset = entry % 2 if apart else entry - 2 * (entry // 2 > tiles // 2)
        for sides in second_weights if apart else first_weights:
            for weight in sides:
                inputs.append(weight)
                specs.append(pl.BlockSpec((1, span // 2, CH), lambda i, offset=offset: (offset, 0, 0)))
    if not first:
        inputs.append(state)
        specs.append(whole(state.shape))
    if last:
        inputs.append(spread_weight)
        specs.append(whole(spread_weight.shape))
        out = jax.ShapeDtypeStruct((IMG_TOK, PIX * CIN), F32)
    else:
        out = jax.ShapeDtypeStruct((halves, IMG_TOK, CH), F32)
    return pl.pallas_call(
        functools.partial(up_kernel, count, halves, first, last),
        grid=(1,),
        in_specs=specs,
        out_specs=whole(out.shape),
        out_shape=out,
        compiler_params=params(16),
        cost_estimate=cost(2 * count * IMG_TOK * span * CH * halves, (1 + count) << 20),
        name="up_last" if last else "up_step",
    )(*inputs)


def spread_weights(up_conv, pixels):
    taps = up_conv.reshape(9, CH, CIN).transpose(1, 0, 2).reshape(CH, 9 * CIN)
    shape = (pixels.shape[0], 9 * CIN, 9 * PIX * CIN)
    row = lax.broadcasted_iota(jnp.int32, shape, 1)
    col = lax.broadcasted_iota(jnp.int32, shape, 2)
    pixel = pixels[:, None, None]
    tap, channel = row >> 3, row & 7
    patch, target, out_channel = col >> 7, (col >> 3) & 15, col & 7
    tap_row, tap_col = tap // 3, tap % 3
    down, right = patch // 3 - 1, patch % 3 - 1
    hit = (
        (channel == out_channel)
        & ((pixel >> 2) + 1 - tap_row == (target >> 2) + PATCH * down)
        & ((pixel & 3) + 1 - tap_col == (target & 3) + PATCH * right)
    )
    placed = jnp.where(hit, 1.0, 0.0).astype(BF16)
    spread = jnp.einsum("ct,ptn->pcn", taps, placed, preferred_element_type=F32)
    return spread.astype(BF16).reshape(pixels.shape[0] * CH, 9 * PIX * CIN)


def by_core(core, own, other, axis):
    return jnp.where(
        core == 0, jnp.concatenate([own, other], axis), jnp.concatenate([other, own], axis)
    )


def shift(values, axis, step):
    count = lax.axis_size(axis)
    return lax.ppermute(values, axis, [(i, (i + step) % count) for i in range(count)])


def gather_small(latents, down_conv):
    ctxs, tiles = lax.axis_size("ctx"), lax.axis_size("tile")
    every = jnp.concatenate([latents] + [shift(latents, "ctx", s) for s in range(1, ctxs)])
    conv = by_core(lax.axis_index("core"), down_conv, swap(down_conv), 1)
    conv = by_core(lax.axis_index("mpo"), conv, shift(conv, "mpo", 1), 1)
    return [every] + [shift(every, "tile", s) for s in range(1, tiles)], conv


def transpose_first(patch_out):
    ctxs, tiles, outer = (lax.axis_size(name) for name in ("ctx", "tile", "mpo"))
    ctx, mpo = lax.axis_index("ctx"), lax.axis_index("mpo")
    width, features = patch_out.shape
    deep = features // (tiles * outer)
    halves = 2 if ctxs == 2 and deep == 2 * CH else 1
    view = patch_out.reshape(width, tiles, outer, halves, deep // halves)
    at = ctx if halves == 2 else 0

    def columns(which):
        size = (width, tiles, 1, 1, deep // halves)
        return lax.dynamic_slice(view, (0, 0, which, at, 0), size)[:, :, 0, 0].transpose(1, 0, 2)

    return columns(mpo), columns(1 - mpo), halves


def transpose_second(both, step):
    tiles = lax.axis_size("tile")
    place = lax.rem(lax.axis_index("tile") + step, tiles)
    block = lax.dynamic_index_in_dim(both, place, 0, keepdims=False)
    return shift(block, "tile", step) if step else block


def transposed(blocks, halves):
    own = jnp.concatenate(blocks)
    weights = [own] if halves == 1 else [own, shift(own, "ctx", 1)]
    return [[weight, swap(weight)] for weight in weights]


def gather_pair(first, second, state, step, extras=None):
    tiles = lax.axis_size("tile")
    found, moving = [{0: first}, {}], [None, None]

    def launch(which, index):
        ring = found[which][2 * index]
        if index < tiles - 1:
            moving[which] = (shift(ring, "tile", 1), shift(ring, "mpo", 1))
        elif which:
            moving[which] = shift(found[which][2 * index - 1], "tile", 1)
        else:
            moving[which] = shift(ring, "mpo", 1)

    def work(entries, state):
        return step([[found[0][e], found[1][e]] for e in entries], entries, state, False)

    launch(0, 0)
    late = callable(second)
    if late:
        events = [(0, 1), (0, 2)]
        for index in range(1, tiles - 2):
            events += [(1, index), (0, index + 2)]
        events += [(1, tiles - 2), (1, tiles - 1)]
    else:
        found[1][0] = second
        launch(1, 0)
        events = [(which, index) for index in range(1, tiles) for which in range(2)]
    seen = first
    for which, index in events:
        ring, cross = moving[which]
        ring, cross, seen, state = lax.optimization_barrier((ring, cross, seen, state))
        found[which][2 * index], found[which][2 * index - 1] = ring, cross
        seen = ring
        launch(which, index)
        if late and (which, index) == (0, 1):
            found[1][0], extras = second(cross)
            launch(1, 0)
        if (which, index) == (1, tiles - 2):
            state = work(list(range(2 * tiles - 3)), state)
    state = work([2 * tiles - 2, 2 * tiles - 3], state)
    last = lax.optimization_barrier((moving[0], moving[1], state, extras))
    return step([[last[0], last[1]]], [2 * tiles - 1], last[2], True), last[3]


def shards(
    text_embed,
    latents,
    down_conv,
    patch_in,
    norm_gain,
    query_weight,
    key_weight,
    value_weight,
    query_gain,
    key_gain,
    out_weight,
    patch_out,
    up_conv,
    span_start,
    image_of_slot,
):
    ctxs, tiles, outer = (lax.axis_size(name) for name in ("ctx", "tile", "mpo"))
    ctx, tile, mpo, core = (lax.axis_index(name) for name in ("ctx", "tile", "mpo", "core"))
    seq_rows, width = text_embed.shape
    half = seq_rows // 2
    heads = width // HD
    images = span_start.shape[0]
    local = latents.shape[0]

    pieces, conv = gather_small(latents, down_conv)
    weights = [swap(key_weight)]
    kept, sent, halves = transpose_first(patch_out)
    pieces, conv, weights, received, later = lax.optimization_barrier(
        (pieces, conv, weights, shift(sent, "mpo", 1), [value_weight, query_weight])
    )
    later = [swap(w) for w in later]
    both = jnp.stack([kept, received], axis=1)
    up_blocks = [transpose_second(both, step) for step in range(tiles) if 2 * step != tiles]

    numbers = jnp.arange(images, dtype=jnp.int32)
    matches = image_of_slot[None, :] == numbers[:, None]
    slot_of_image = jnp.sum(jnp.where(matches, numbers[None, :], 0), axis=1)
    slot_place = lax.rem(ctx + ctxs - slot_of_image // local, ctxs) * local + slot_of_image % local
    meta = jnp.concatenate(
        [span_start, slot_place, image_of_slot, jnp.stack([ctx, core, tile, mpo])]
    ).astype(jnp.int32)
    layout = (images, tiles, outer)

    streams = down_stream(meta, pieces, conv, patch_in, text_embed, norm_gain, images)
    streams, later, up_blocks = lax.optimization_barrier((streams, later, up_blocks))
    others = [swap(s[1]) for s in streams]
    weights += later + [key_weight, value_weight, query_weight]

    head_gains = jnp.stack([query_gain, key_gain])

    def project(blocks, entries, state, last):
        return qkv_step(meta, layout, blocks, entries, weights, state, head_gains if last else None)

    extras = (swap(out_weight), transposed(up_blocks, halves))
    state, (out_par, up_first) = gather_pair(
        *[by_core(core, s[0], o, 1) for s, o in zip(streams, others)], None, project, extras
    )
    state, both = lax.optimization_barrier((state, both))
    up_block = transpose_second(both, tiles // 2)
    kv_send, q_send = state[:heads], state[heads : 2 * heads]
    kv_own, q_own = state[2 * heads : 3 * heads], state[3 * heads :]

    def shifted(values, step, cross):
        pairs = [
            (2 * c + k, 2 * ((c + step) % ctxs) + (1 - k if cross else k))
            for c in range(ctxs)
            for k in range(2)
        ]
        return lax.ppermute(values, ("ctx", "core"), pairs)

    def same_core(head):
        return [shifted(kv_own[head], step, False) for step in range(1, ctxs)]

    def pieces_of(head, same):
        pieces = [swap(q_send[head]), kv_own[head], swap(kv_send[head])]
        for step in range(1, ctxs):
            pieces += [same[step - 1], shifted(kv_send[head], step, True)]
        return pieces

    def attend(head, pieces, ahead):
        result = attention(meta, [q_own[head], pieces[0]], pieces[1:], images)
        (att_own, att_send), ahead = lax.optimization_barrier((result, ahead))
        return by_core(core, att_own, swap(att_send), 1), ahead

    pieces, up_block = lax.optimization_barrier((pieces_of(0, same_core(0)), up_block))
    attended, same = attend(0, pieces, same_core(1) if heads > 1 else None)
    if heads == 1:
        attended, second = attended[: half // 2], attended[half // 2 :]
        extras = transposed([up_block], halves)
    else:
        extras = None

        def second(token):
            pieces, token = lax.optimization_barrier((pieces_of(1, same), token))
            result, block = lax.optimization_barrier((attend(1, pieces, None)[0], up_block))
            return result, transposed([block], halves)

    def project_out(blocks, entries, state, last):
        return out_step(meta, layout, blocks, entries, (out_weight, out_par), state, last)

    state = [jnp.stack([s[0], o]) for s, o in zip(streams, others)]
    state, up_second = gather_pair(attended, second, state, project_out, extras)
    out_own, out_send = state
    out_other = swap(out_send)
    layer_out = by_core(core, out_own, out_other, 0)

    picks = pick_rows(meta, out_own, out_other, images, ctxs)
    own_parts, par_parts = [picks[0]], [swap(picks[1])]
    for step in range(1, ctxs):
        own_parts.append(shifted(picks[2 * step], step, False))
        par_parts.append(shifted(picks[2 * step + 1], step, True))

    pixel = tile * outer + mpo
    pixels = jnp.stack([pixel * halves + lax.rem(ctx + h, halves) for h in range(halves)])
    spread_weight = spread_weights(up_conv, pixels)

    def project_up(blocks, entries, state, last):
        return up_step(blocks, entries, tiles, up_first, up_second, state, spread_weight if last else None)

    state, _ = gather_pair(*merge_picks(own_parts, par_parts), None, project_up)

    bands = state.reshape(tiles, IMG_TOK // tiles, PIX * CIN)
    band = lax.dynamic_index_in_dim(bands, tile, 0, keepdims=False)
    for step in range(1, tiles):
        piece = lax.dynamic_index_in_dim(bands, lax.rem(tile + step, tiles), 0, keepdims=False)
        band = band + shift(piece, "tile", step)
    quad = {}
    for name, pairs in (
        ("mpo", [(0, 2), (1, 3), (2, 0), (3, 1)]),
        ("core", [(0, 1), (1, 0), (2, 3), (3, 2)]),
        ("both", [(0, 3), (1, 2), (2, 1), (3, 0)]),
    ):
        quad[name] = lax.ppermute(band, ("mpo", "core"), pairs)
    return layer_out, finish(meta[3 * images + 1 :], band, quad["mpo"], quad["core"], quad["both"])


def solution(mesh):
    ctxs, tiles, parts = mesh.devices.shape
    fine = Mesh(
        mesh.devices.reshape(ctxs, tiles, parts // 2, 2), ("ctx", "tile", "mpo", "core")
    )
    features = ("tile", "mpo", "core")
    return jax.shard_map(
        shards,
        mesh=fine,
        in_specs=(
            P("ctx", features),
            P("ctx", "tile", None),
            P(None, ("mpo", "core")),
            P(None, features),
            P(features),
            P(None, features),
            P(None, features),
            P(None, features),
            P(),
            P(),
            P(None, features),
            P(features, None),
            P(),
            P(),
            P(),
        ),
        out_specs=(P("ctx", features), P("ctx", "tile", None)),
        check_vma=False,
    )
```

time: 285 us -> 265 us (0.930)
  Pallas kernels: 70.4 us -> 56.3 us
  starting transfers between devices: 70.2 us -> 82.1 us
  local copies, waits for them, and re-layouts: 37 us -> 25.7 us
  waiting for transfers between devices: 99 us -> 94.9 us
    ppermute x42 -> x56, starting transfers between devices: 26.4 us -> 50.2 us  [shift(): lax.ppermute(values, axis, [(i, (i + step) % count) for i in range(count)])]
    pallas_call x22 -> x12, Pallas kernels: 60.3 us -> 46.1 us  [the longest x3 21.9 us: qkv_step(): pl.pallas_call(functools.partial(qkv_kernel, count, groups, first, last),...]
    unnamed x85 -> x74, local copies, waits for them, and re-layouts: 25.2 us -> 12.7 us
    ppermute x6, waiting for transfers between devices: 24.6 us -> 14.7 us  [shifted(): return lax.ppermute(values, ('ctx', 'core'), pairs)]
    ppermute x17 -> x19, starting transfers between devices: 29.9 us -> 20.2 us  [swap(): return lax.ppermute(values, 'core', [(0, 1), (1, 0)])]
    slice x18 -> x2, local copies, waits for them, and re-layouts: 6.27 us -> 1.37 us  [shards(): s[0]]
    dynamic_slice x1 -> x3, local copies, waits for them, and re-layouts: 2.21 us -> 7.04 us  [columns(): lax.dynamic_slice(view, (0, 0, which, at, 0), size)[:, :, 0, 0]]
    ppermute x42 -> x56, waiting for transfers between devices: 71 us -> 75.4 us  [shift(): lax.ppermute(values, axis, [(i, (i + step) % count) for i in range(count)])]
  transfers between devices with their start and end apart: 72 -> 84, of which waited for: 31 -> 35; matrix products, arithmetic and copies ran while one was open for 7% -> 6% of each run, Pallas kernels for 24% -> 15%
where the time goes in v4:
time: 265 us; the launch traced here: 264 us
  waiting for transfers between devices  94.9 us (36%)
  starting transfers between devices  82.1 us (31%)
  Pallas kernels  56.3 us (21%)
  local copies, waits for them, and re-layouts  25.7 us (10%)
  other arithmetic  3.21 us (1%)
    ppermute x56, waiting for transfers between devices, shift(): lax.ppermute(values, axis, [(i, (i + step) % count) for i in range(count)])  75.4 us
    ppermute x56, starting transfers between devices, shift(): lax.ppermute(values, axis, [(i, (i + step) % count) for i in range(count)])  50.2 us
    pallas_call x3, Pallas kernels, qkv_step(): pl.pallas_call(functools.partial(qkv_kernel, count, groups, first, last),...  21.9 us
    ppermute x19, starting transfers between devices, swap(): return lax.ppermute(values, 'core', [(0, 1), (1, 0)])  20.2 us
    ppermute x6, waiting for transfers between devices, shifted(): return lax.ppermute(values, ('ctx', 'core'), pairs)  14.7 us
    unnamed x74, local copies, waits for them, and re-layouts  12.7 us
    pallas_call x1, Pallas kernels, down_stream(): pl.pallas_call(functools.partial(down_kernel, images, tiles, half), grid_...  9.35 us
    pallas_call x2, Pallas kernels, attention(): pl.pallas_call(functools.partial(attention_kernel, images, len(pieces), h...  8.92 us
  transfers between devices with their start and end apart: 84, of which 35 were waited for; matrix products, arithmetic and copies ran while one was open for 6% of the time, Pallas kernels for 15%

profile of v4, /device:TPU:1, one launch (start us, length us, event | category | flops | bytes accessed | tf_op | source)
XLA Modules:
  0.0 264.1 jit_solution(4551495687418698078)
XLA Ops:
  0.8 4.5 %reshape.76 = bf16[256,4,2,2,256]{4,3,2,1,0:T(2,128)(2,1)} reshape(bf16[256,4096]{1,0:T(8,128)(2,1)} %param.26) | data formatting | bytes 4194304 | tf_op jit(solution)/shard_map/reshape | solution.py:652
  5.2 4.7 %constant_dynamic-slice_fusion = (bf16[256,4,1,1,256]{4,3,2,1,0:T(2,128)(2,1)}, bf16[256,4,1,1,256]{4,3,2,1,0:T(2,128)(2,1)S(1)}) fusion(bf16[256,4,2,2,256]{4,3,2,1,0:T(2,128)(2,1)} %reshape.76, s32[]{:T(128)S(6)} %select_n.132, s32[]{:T(128)S(6)} %select_n.131, s32[]{:T(128)S(6)} %select_n.130), kind=kLoop, calls=%fused_computation.82 | loop fusion | bytes 2097164 | tf_op jit(solution)/shard_map/dynamic_slice | solution.py:657
  10.9 2.7 %collective-permute-start.7 = (bf16[4,256,256]{2,1,0:T(8,128)(2,1)}, bf16[4,256,256]{2,1,0:T(8,128)(2,1)S(1)}, u32[]{:S(2)}, u32[]{:S(2)}) collective-permute-start(bf16[4,256,256]{2,1,0:T(8,128)(2,1)} %bitcast.65), channel_id=1, source_target_pairs={{0,2},{2,0},{1,3},{3,1},{4,6},{6,4},{5,7},{7,5},{8,10},{10,8},{9,1... | collective-permute-start | bytes 1572872 | tf_op jit(solution)/shard_map/ppermute | solution.py:635
  20.4 6.0 %collective-permute-done.5 = bf16[72,128]{1,0:T(8,128)(2,1)S(1)} collective-permute-done((bf16[72,128]{1,0:T(8,128)(2,1)S(1)}, bf16[72,128]{1,0:T(8,128)(2,1)S(1)}, u32[]{:S(2)}, u32[]{:S(2)}) %collective-permute-start.5) | collective-permute-done | bytes 18464 | tf_op jit(solution)/shard_map/ppermute | solution.py:635
  26.4 3.4 %collective-permute-start.3 = (bf16[4,16,512]{2,1,0:T(8,128)(2,1)S(1)}, bf16[4,16,512]{2,1,0:T(8,128)(2,1)S(1)}, u32[]{:S(2)}, u32[]{:S(2)}) collective-permute-start(bf16[4,16,512]{2,1,0:T(8,128)(2,1)S(1)} %constant_dynamic-update-slice_fusion.refs_0_), channel_id=1, source_target_pairs={{0,12},{4,0},{8,4},{12,8},{1,13},{5,1},{9,5},{13,9},{2,14},{6,2},{... | collective-permute-start | bytes 196616 | tf_op jit(solution)/shard_map/ppermute | solution.py:635
  36.3 3.9 %collective-permute-start.11 = (bf16[2,256,256]{2,1,0:T(8,128)(2,1)S(1)}, bf16[2,256,256]{2,1,0:T(8,128)(2,1)S(1)}, u32[]{:S(2)}, u32[]{:S(2)}) collective-permute-start(bf16[2,256,256]{2,1,0:T(8,128)(2,1)S(1)} %get-tuple-element.282), channel_id=1, source_target_pairs={{0,12},{4,0},{8,4},{12,8},{1,13},{5,1},{9,5},{13,9},{2,14},{6,2},{... | collective-permute-start | bytes 786440 | tf_op jit(solution)/shard_map/ppermute | solution.py:635
  41.8 9.3 %down_stream.1 = (bf16[2,272,256]{2,1,0:T(8,128)(2,1)S(1)}, bf16[2,256,256]{2,1,0:T(8,128)(2,1)S(1)}) custom-call(s32[16]{0:T(128)S(1)} %concatenate.61.meta, bf16[4,16,512]{2,1,0:T(8,128)(2,1)S(1)} %constant_dynamic-update-slice_fusion.refs_0_, bf16[4,16,512]{2,1,0:T(8,128)(2,1)S(1)} %collective-permute-done.1.refs_1_, ...), custom_call_target="tpu_custom_call" | custom-call | flops 4294967296 | bytes 4194304 | tf_op jit(solution)/shard_map/down_stream/pallas_call | solution.py:144
  58.2 5.0 %collective-permute-done.13.refs_4_ = bf16[272,512]{1,0:T(8,128)(2,1)S(1)} collective-permute-done((bf16[272,512]{1,0:T(8,128)(2,1)S(1)}, bf16[272,512]{1,0:T(8,128)(2,1)S(1)}, u32[]{:S(2)}, u32[]{:S(2)}) %collective-permute-start.13) | collective-permute-done | bytes 278560 | tf_op jit(solution)/shard_map/ppermute | solution.py:635
  65.1 3.7 %collective-permute-done.18.refs_5_ = bf16[256,512]{1,0:T(8,128)(2,1)S(1)} collective-permute-done((bf16[256,512]{1,0:T(8,128)(2,1)S(1)}, bf16[256,512]{1,0:T(8,128)(2,1)S(1)}, u32[]{:S(2)}, u32[]{:S(2)}) %collective-permute-start.18) | collective-permute-done | bytes 262176 | tf_op jit(solution)/shard_map/ppermute | solution.py:635
  82.0 3.3 %collective-permute-start.29 = (bf16[6,256,256]{2,1,0:T(8,128)(2,1)S(1)}, bf16[6,256,256]{2,1,0:T(8,128)(2,1)}, u32[]{:S(2)}, u32[]{:S(2)}) collective-permute-start(bf16[6,256,256]{2,1,0:T(8,128)(2,1)S(1)} %constant_dynamic-update-slice_fusion.2.refs_10_.refs_14_.refs_18_.refs_22_.refs_4_.refs_2_), channel_id=1, source_target_pairs={{0,1},{1,0},{2,3},{3,2},{4,5},{5,4},{6,7},{7,6},{8,9},{9,8},{10,11... | collective-permute-start | bytes 2359304 | tf_op jit(solution)/shard_map/ppermute | solution.py:54
  94.8 10.4 %qkv_step.2 = (f32[6,512,256]{2,1,0:T(8,128)}, f32[512,128]{1,0:T(8,128)S(1)}) custom-call(s32[16]{0:T(128)S(1)} %concatenate.61.meta, bf16[272,512]{1,0:T(8,128)(2,1)S(1)} %maximum_select_fusion.1.refs_0_, bf16[256,512]{1,0:T(8,128)(2,1)S(1)} %maximum_select_fusion.2.refs_1_, bf16[272,512]{1,0:T(8,128)(2,1)S(1)} %copy-done.5, ...), custom_call_target="tpu_custom_call" | custom-call | flops 4026531840 | bytes 16777216 | tf_op jit(solution)/shard_map/qkv_step/pallas_call | solution.py:286
  106.0 7.3 %qkv_step.3 = (f32[6,512,256]{2,1,0:T(8,128)}, f32[512,128]{1,0:T(8,128)S(1)}) custom-call(s32[16]{0:T(128)S(1)} %concatenate.61.meta, bf16[272,512]{1,0:T(8,128)(2,1)} %collective-permute-done.20.refs_0_, bf16[256,512]{1,0:T(8,128)(2,1)S(1)} %collective-permute-done.25.refs_1_, bf16[272,512]{1,0:T(8,128)(2,1)} %collective-permute-done.21.refs_2_, ...), custom_call_target="tpu_custom_call" | custom-call | flops 1610612736 | bytes 10485760 | tf_op jit(solution)/shard_map/qkv_step/pallas_call | solution.py:286
  113.3 4.2 %qkv_last.1 = (bf16[2,512,128]{2,1,0:T(8,128)(2,1)S(1)}, bf16[2,512,128]{2,1,0:T(8,128)(2,1)S(1)}, bf16[512,128]{1,0:T(8,128)(2,1)S(1)}, bf16[512,128]{1,0:T(8,1...) custom-call(s32[16]{0:T(128)S(1)} %concatenate.61.meta, ...), custom_call_target="tpu_custom_call" | custom-call | flops 805306368 | bytes 8388608 | tf_op jit(solution)/shard_map/qkv_last/pallas_call | solution.py:286
  117.5 3.7 %collective-permute-start.33 = (bf16[2,512,128]{2,1,0:T(8,128)(2,1)S(1)}, bf16[2,512,128]{2,1,0:T(8,128)(2,1)S(1)}, u32[]{:S(2)}, u32[]{:S(2)}) collective-permute-start(bf16[2,512,128]{2,1,0:T(8,128)(2,1)S(1)} %get-tuple-element.194), channel_id=1, source_target_pairs={{0,1},{1,0},{2,3},{3,2},{4,5},{5,4},{6,7},{7,6},{8,9},{9,8},{10,11... | collective-permute-start | bytes 786440 | tf_op jit(solution)/shard_map/ppermute | solution.py:54
  126.7 7.9 %collective-permute-done.34.refs_4_ = bf16[2,512,128]{2,1,0:T(8,128)(2,1)S(1)} collective-permute-done((bf16[2,512,128]{2,1,0:T(8,128)(2,1)S(1)}, bf16[2,512,128]{2,1,0:T(8,128)(2,1)S(1)}, u32[]{:S(2)}, u32[]{:S(2)}) %collective-permute-start.34) | collective-permute-done | bytes 262176 | tf_op jit(solution)/shard_map/ppermute | solution.py:788
  134.6 3.0 %collective-permute-done.36.refs_26_.refs_8_ = bf16[2,256,256]{2,1,0:T(8,128)(2,1)S(1)} collective-permute-done((bf16[2,256,256]{2,1,0:T(8,128)(2,1)S(1)}, bf16[2,256,256]{2,1,0:T(8,128)(2,1)S(1)}, u32[]{:S(2)}, u32[]{:S(2)}) %collective-permute-start.36) | collective-permute-done | bytes 262176 | tf_op jit(solution)/shard_map/ppermute | solution.py:635
  137.6 4.5 %attention.2 = (bf16[512,128]{1,0:T(8,128)(2,1)S(1)}, bf16[512,128]{1,0:T(8,128)(2,1)S(1)}) custom-call(s32[16]{0:T(128)S(1)} %concatenate.61.meta, bf16[512,128]{1,0:T(8,128)(2,1)S(1)} %get-tuple-element.191.refs_0_, bf16[512,128]{1,0:T(8,128)(2,1)S(1)} %collective-permute-done.32.refs_1_, bf16[2,512,128]{2,1,0:T(8,128)(2,1)S(1)} %get-tuple-element.197.refs_2_, ...), custom_call_target="tpu_custom_call" | custom-call | flops 1073741824 | bytes 1048576 | tf_op jit(solution)/shard_map/attention/pallas_call | solution.py:344
  148.1 5.4 %collective-permute-done.39.refs_4_ = bf16[512,256]{1,0:T(8,128)(2,1)S(1)} collective-permute-done((bf16[512,256]{1,0:T(8,128)(2,1)S(1)}, bf16[512,256]{1,0:T(8,128)(2,1)S(1)}, u32[]{:S(2)}, u32[]{:S(2)}) %collective-permute-start.39) | collective-permute-done | bytes 262176 | tf_op jit(solution)/shard_map/ppermute | solution.py:635
  154.3 4.5 %attention.3 = (bf16[512,128]{1,0:T(8,128)(2,1)S(1)}, bf16[512,128]{1,0:T(8,128)(2,1)S(1)}) custom-call(s32[16]{0:T(128)S(1)} %concatenate.61.meta, bf16[512,128]{1,0:T(8,128)(2,1)S(1)} %get-tuple-element.210.refs_0_, bf16[512,128]{1,0:T(8,128)(2,1)S(1)} %collective-permute-done.45.refs_1_, bf16[2,512,128]{2,1,0:T(8,128)(2,1)S(1)} %get-tuple-element.216.refs_2_, ...), custom_call_target="tpu_custom_call" | custom-call | flops 1073741824 | bytes 1048576 | tf_op jit(solution)/shard_map/attention/pallas_call | solution.py:344
  163.8 5.1 %collective-permute-done.41.refs_8_ = bf16[512,256]{1,0:T(8,128)(2,1)S(1)} collective-permute-done((bf16[512,256]{1,0:T(8,128)(2,1)S(1)}, bf16[512,256]{1,0:T(8,128)(2,1)S(1)}, u32[]{:S(2)}, u32[]{:S(2)}) %collective-permute-start.41) | collective-permute-done | bytes 262176 | tf_op jit(solution)/shard_map/ppermute | solution.py:635
  170.1 4.4 %collective-permute-done.49.refs_5_ = bf16[512,256]{1,0:T(8,128)(2,1)S(1)} collective-permute-done((bf16[512,256]{1,0:T(8,128)(2,1)S(1)}, bf16[512,256]{1,0:T(8,128)(2,1)S(1)}, u32[]{:S(2)}, u32[]{:S(2)}) %collective-permute-start.49) | collective-permute-done | bytes 262176 | tf_op jit(solution)/shard_map/ppermute | solution.py:635
  177.0 3.1 %collective-permute-done.43.refs_0_ = bf16[512,256]{1,0:T(8,128)(2,1)S(1)} collective-permute-done((bf16[512,256]{1,0:T(8,128)(2,1)S(1)}, bf16[512,256]{1,0:T(8,128)(2,1)S(1)}, u32[]{:S(2)}, u32[]{:S(2)}) %collective-permute-start.43) | collective-permute-done | bytes 262176 | tf_op jit(solution)/shard_map/ppermute | solution.py:635
  180.2 5.6 %collective-permute-done.52.refs_9_ = bf16[512,256]{1,0:T(8,128)(2,1)S(1)} collective-permute-done((bf16[512,256]{1,0:T(8,128)(2,1)S(1)}, bf16[512,256]{1,0:T(8,128)(2,1)S(1)}, u32[]{:S(2)}, u32[]{:S(2)}) %collective-permute-start.52) | collective-permute-done | bytes 262176 | tf_op jit(solution)/shard_map/ppermute | solution.py:635
  189.8 3.3 %out_step.2.refs_8_ = f32[2,512,256]{2,1,0:T(8,128)S(1)} custom-call(s32[16]{0:T(128)S(1)} %concatenate.61.meta, bf16[512,256]{1,0:T(8,128)(2,1)S(1)} %maximum_select_fusion.3.refs_0_, bf16[512,256]{1,0:T(8,128)(2,1)S(1)} %maximum_select_fusion.4.refs_1_, bf16[512,256]{1,0:T(8,128)(2,1)S(1)} %collective-permute-done.40.refs_2_, ...), custom_call_target="tpu_custom_call" | custom-call | flops 1342177280 | bytes 7340032 | tf_op jit(solution)/shard_map/out_step/pallas_call | solution.py:414
  197.7 3.8 %collective-permute-done.56.refs_1_ = bf16[512,256]{1,0:T(8,128)(2,1)S(1)} collective-permute-done((bf16[512,256]{1,0:T(8,128)(2,1)S(1)}, bf16[512,256]{1,0:T(8,128)(2,1)S(1)}, u32[]{:S(2)}, u32[]{:S(2)}) %collective-permute-start.56) | collective-permute-done | bytes 262176 | tf_op jit(solution)/shard_map/ppermute | solution.py:635
  203.5 4.0 %collective-permute-start.60 = (bf16[512,256]{1,0:T(8,128)(2,1)S(1)}, bf16[512,256]{1,0:T(8,128)(2,1)S(1)}, u32[]{:S(2)}, u32[]{:S(2)}) collective-permute-start(bf16[512,256]{1,0:T(8,128)(2,1)S(1)} %get-tuple-element.248), channel_id=1, source_target_pairs={{0,1},{1,0},{2,3},{3,2},{4,5},{5,4},{6,7},{7,6},{8,9},{9,8},{10,11... | collective-permute-start | bytes 786440 | tf_op jit(solution)/shard_map/ppermute | solution.py:54
  212.0 2.7 %collective-permute-done.61.refs_1_ = bf16[256,256]{1,0:T(8,128)(2,1)S(1)} collective-permute-done((bf16[256,256]{1,0:T(8,128)(2,1)S(1)}, bf16[256,256]{1,0:T(8,128)(2,1)S(1)}, u32[]{:S(2)}, u32[]{:S(2)}) %collective-permute-start.61) | collective-permute-done | bytes 131104 | tf_op jit(solution)/shard_map/ppermute | solution.py:788
  214.7 3.3 %collective-permute-done.63.refs_3_ = bf16[256,256]{1,0:T(8,128)(2,1)S(1)} collective-permute-done((bf16[256,256]{1,0:T(8,128)(2,1)S(1)}, bf16[256,256]{1,0:T(8,128)(2,1)S(1)}, u32[]{:S(2)}, u32[]{:S(2)}) %collective-permute-start.63) | collective-permute-done | bytes 131104 | tf_op jit(solution)/shard_map/ppermute | solution.py:788
  219.7 5.4 %collective-permute-done.64.refs_4_ = bf16[128,512]{1,0:T(8,128)(2,1)S(1)} collective-permute-done((bf16[128,512]{1,0:T(8,128)(2,1)S(1)}, bf16[128,512]{1,0:T(8,128)(2,1)S(1)}, u32[]{:S(2)}, u32[]{:S(2)}) %collective-permute-start.64) | collective-permute-done | bytes 131104 | tf_op jit(solution)/shard_map/ppermute | solution.py:635
  231.5 2.7 %collective-permute-done.72.refs_9_ = bf16[128,512]{1,0:T(8,128)(2,1)S(1)} collective-permute-done((bf16[128,512]{1,0:T(8,128)(2,1)S(1)}, bf16[128,512]{1,0:T(8,128)(2,1)S(1)}, u32[]{:S(2)}, u32[]{:S(2)}) %collective-permute-start.72) | collective-permute-done | bytes 131104 | tf_op jit(solution)/shard_map/ppermute | solution.py:635
  242.7 3.5 %collective-permute-done.77.refs_1_ = bf16[128,512]{1,0:T(8,128)(2,1)S(1)} collective-permute-done((bf16[128,512]{1,0:T(8,128)(2,1)S(1)}, bf16[128,512]{1,0:T(8,128)(2,1)S(1)}, u32[]{:S(2)}, u32[]{:S(2)}) %collective-permute-start.77) | collective-permute-done | bytes 131104 | tf_op jit(solution)/shard_map/ppermute | solution.py:635
  254.4 5.0 %collective-permute-start.82 = (f32[64,128]{1,0:T(8,128)S(1)}, f32[64,128]{1,0:T(8,128)S(1)}, u32[]{:S(2)}, u32[]{:S(2)}) collective-permute-start(f32[64,128]{1,0:T(8,128)S(1)} %fusion.31.own_a), channel_id=1, source_target_pairs={{0,1},{1,0},{2,3},{3,2},{4,5},{5,4},{6,7},{7,6},{8,9},{9,8},{10,11... | collective-permute-start | bytes 98312 | tf_op jit(solution)/shard_map/ppermute | solution.py:852
  (264 shorter events, 113.6 us)
Async XLA Ops:
  0.6 30.5 %collective-permute-start.6 = (bf16[4096,256]{1,0:T(8,128)(2,1)}, bf16[4096,256]{1,0:T(8,128)(2,1)S(1)}, u32[]{:S(2)}, u32[]{:S(2)}) collective-permute-start(bf16[4096,256]{1,0:T(8,128)(2,1)} %refs_5_.3), channel_id=1, source_target_pairs={{0,1},{1,0},{2,3},{3,2},{4,5},{5,4},{6,7},{7,6},{8,9},{9,8},{10,11... | collective-permute-start | bytes 6291464 | tf_op jit(solution)/shard_map/ppermute | solution.py:54
  10.9 20.2 %collective-permute-start.7 = (bf16[4,256,256]{2,1,0:T(8,128)(2,1)}, bf16[4,256,256]{2,1,0:T(8,128)(2,1)S(1)}, u32[]{:S(2)}, u32[]{:S(2)}) collective-permute-start(bf16[4,256,256]{2,1,0:T(8,128)(2,1)} %bitcast.65), channel_id=1, source_target_pairs={{0,2},{2,0},{1,3},{3,1},{4,6},{6,4},{5,7},{7,5},{8,10},{10,8},{9,1... | collective-permute-start | bytes 1572872 | tf_op jit(solution)/shard_map/ppermute | solution.py:635
  16.5 9.9 %collective-permute-start.5 = (bf16[72,128]{1,0:T(8,128)(2,1)S(1)}, bf16[72,128]{1,0:T(8,128)(2,1)S(1)}, u32[]{:S(2)}, u32[]{:S(2)}) collective-permute-start(bf16[72,128]{1,0:T(8,128)(2,1)S(1)} %maximum_select_fusion.6), channel_id=1, source_target_pairs={{0,2},{2,0},{1,3},{3,1},{4,6},{6,4},{5,7},{7,5},{8,10},{10,8},{9,1... | collective-permute-start | bytes 55304 | tf_op jit(solution)/shard_map/ppermute | solution.py:635
  16.8 13.0 %collective-permute-start.1 = (bf16[4,16,512]{2,1,0:T(8,128)(2,1)S(1)}, bf16[4,16,512]{2,1,0:T(8,128)(2,1)S(1)}, u32[]{:S(2)}, u32[]{:S(2)}) collective-permute-start(bf16[4,16,512]{2,1,0:T(8,128)(2,1)S(1)} %constant_dynamic-update-slice_fusion.refs_0_), channel_id=1, source_target_pairs={{0,4},{4,8},{8,12},{12,0},{1,5},{5,9},{9,13},{13,1},{2,6},{6,10},{... | collective-permute-start | bytes 196616 | tf_op jit(solution)/shard_map/ppermute | solution.py:635
  18.1 11.7 %collective-permute-start.2 = (bf16[4,16,512]{2,1,0:T(8,128)(2,1)S(1)}, bf16[4,16,512]{2,1,0:T(8,128)(2,1)S(1)}, u32[]{:S(2)}, u32[]{:S(2)}) collective-permute-start(bf16[4,16,512]{2,1,0:T(8,128)(2,1)S(1)} %constant_dynamic-update-slice_fusion.refs_0_), channel_id=1, source_target_pairs={{0,8},{4,12},{8,0},{12,4},{1,9},{5,13},{9,1},{13,5},{2,10},{6,14},... | collective-permute-start | bytes 196616 | tf_op jit(solution)/shard_map/ppermute | solution.py:635
  31.2 20.0 %collective-permute-start.8 = (bf16[4096,256]{1,0:T(8,128)(2,1)}, bf16[4096,256]{1,0:T(8,128)(2,1)}, u32[]{:S(2)}, u32[]{:S(2)}) collective-permute-start(bf16[4096,256]{1,0:T(8,128)(2,1)} %refs_6_.1), channel_id=1, source_target_pairs={{0,1},{1,0},{2,3},{3,2},{4,5},{5,4},{6,7},{7,6},{8,9},{9,8},{10,11... | collective-permute-start | bytes 6291464 | tf_op jit(solution)/shard_map/ppermute | solution.py:54
  32.9 18.3 %collective-permute-start.9 = (bf16[4096,256]{1,0:T(8,128)(2,1)}, bf16[4096,256]{1,0:T(8,128)(2,1)}, u32[]{:S(2)}, u32[]{:S(2)}) collective-permute-start(bf16[4096,256]{1,0:T(8,128)(2,1)} %refs_7_.3), channel_id=1, source_target_pairs={{0,1},{1,0},{2,3},{3,2},{4,5},{5,4},{6,7},{7,6},{8,9},{9,8},{10,11... | collective-permute-start | bytes 6291464 | tf_op jit(solution)/shard_map/ppermute | solution.py:54
  33.0 80.3 %collective-permute-start.28 = (bf16[4096,256]{1,0:T(8,128)(2,1)}, bf16[4096,256]{1,0:T(8,128)(2,1)}, u32[]{:S(2)}, u32[]{:S(2)}) collective-permute-start(bf16[4096,256]{1,0:T(8,128)(2,1)} %param.25), channel_id=1, source_target_pairs={{0,1},{1,0},{2,3},{3,2},{4,5},{5,4},{6,7},{7,6},{8,9},{9,8},{10,11... | collective-permute-start | bytes 6291464 | tf_op jit(solution)/shard_map/ppermute | solution.py:54
  36.2 15.0 %collective-permute-start.10 = (bf16[2,256,256]{2,1,0:T(8,128)(2,1)S(1)}, bf16[2,256,256]{2,1,0:T(8,128)(2,1)S(1)}, u32[]{:S(2)}, u32[]{:S(2)}) collective-permute-start(bf16[2,256,256]{2,1,0:T(8,128)(2,1)S(1)} %get-tuple-element.284), channel_id=1, source_target_pairs={{0,4},{4,8},{8,12},{12,0},{1,5},{5,9},{9,13},{13,1},{2,6},{6,10},{... | collective-permute-start | bytes 786440 | tf_op jit(solution)/shard_map/ppermute | solution.py:635
  36.3 14.9 %collective-permute-start.11 = (bf16[2,256,256]{2,1,0:T(8,128)(2,1)S(1)}, bf16[2,256,256]{2,1,0:T(8,128)(2,1)S(1)}, u32[]{:S(2)}, u32[]{:S(2)}) collective-permute-start(bf16[2,256,256]{2,1,0:T(8,128)(2,1)S(1)} %get-tuple-element.282), channel_id=1, source_target_pairs={{0,12},{4,0},{8,4},{12,8},{1,13},{5,1},{9,5},{13,9},{2,14},{6,2},{... | collective-permute-start | bytes 786440 | tf_op jit(solution)/shard_map/ppermute | solution.py:635
  53.5 9.7 %collective-permute-start.13 = (bf16[272,512]{1,0:T(8,128)(2,1)S(1)}, bf16[272,512]{1,0:T(8,128)(2,1)S(1)}, u32[]{:S(2)}, u32[]{:S(2)}) collective-permute-start(bf16[272,512]{1,0:T(8,128)(2,1)S(1)} %maximum_select_fusion.1.refs_0_), channel_id=1, source_target_pairs={{0,4},{4,8},{8,12},{12,0},{1,5},{5,9},{9,13},{13,1},{2,6},{6,10},{... | collective-permute-start | bytes 835592 | tf_op jit(solution)/shard_map/ppermute | solution.py:635
  55.2 30.1 %collective-permute-start.30 = (bf16[6,256,256]{2,1,0:T(8,128)(2,1)S(1)}, bf16[6,256,256]{2,1,0:T(8,128)(2,1)}, u32[]{:S(2)}, u32[]{:S(2)}) collective-permute-start(bf16[6,256,256]{2,1,0:T(8,128)(2,1)S(1)} %constant_dynamic-update-slice_fusion.2.refs_10_.refs_14_.refs_18_.refs_22_.refs_4_.refs_2_), channel_id=1, source_target_pairs={{0,16},{16,0},{1,17},{17,1},{2,18},{18,2},{3,19},{19,3},{4,20},{20... | collective-permute-start | bytes 2359304 | tf_op jit(solution)/shard_map/ppermute | solution.py:635
  57.8 11.0 %collective-permute-start.18 = (bf16[256,512]{1,0:T(8,128)(2,1)S(1)}, bf16[256,512]{1,0:T(8,128)(2,1)S(1)}, u32[]{:S(2)}, u32[]{:S(2)}) collective-permute-start(bf16[256,512]{1,0:T(8,128)(2,1)S(1)} %maximum_select_fusion.2.refs_1_), channel_id=1, source_target_pairs={{0,4},{4,8},{8,12},{12,0},{1,5},{5,9},{9,13},{13,1},{2,6},{6,10},{... | collective-permute-start | bytes 786440 | tf_op jit(solution)/shard_map/ppermute | solution.py:635
  82.0 31.3 %collective-permute-start.29 = (bf16[6,256,256]{2,1,0:T(8,128)(2,1)S(1)}, bf16[6,256,256]{2,1,0:T(8,128)(2,1)}, u32[]{:S(2)}, u32[]{:S(2)}) collective-permute-start(bf16[6,256,256]{2,1,0:T(8,128)(2,1)S(1)} %constant_dynamic-update-slice_fusion.2.refs_10_.refs_14_.refs_18_.refs_22_.refs_4_.refs_2_), channel_id=1, source_target_pairs={{0,1},{1,0},{2,3},{3,2},{4,5},{5,4},{6,7},{7,6},{8,9},{9,8},{10,11... | collective-permute-start | bytes 2359304 | tf_op jit(solution)/shard_map/ppermute | solution.py:54
  85.3 28.0 %collective-permute-start.31 = (bf16[6,256,256]{2,1,0:T(8,128)(2,1)}, bf16[6,256,256]{2,1,0:T(8,128)(2,1)}, u32[]{:S(2)}, u32[]{:S(2)}) collective-permute-start(bf16[6,256,256]{2,1,0:T(8,128)(2,1)} %collective-permute-done.30.refs_12_.refs_16_.refs_20_.refs_24_.refs_6_.refs_4_), channel_id=1, source_target_pairs={{0,1},{1,0},{2,3},{3,2},{4,5},{5,4},{6,7},{7,6},{8,9},{9,8},{10,11... | collective-permute-start | bytes 2359304 | tf_op jit(solution)/shard_map/ppermute | solution.py:54
  85.5 19.8 %collective-permute-start.25 = (bf16[256,512]{1,0:T(8,128)(2,1)}, bf16[256,512]{1,0:T(8,128)(2,1)S(1)}, u32[]{:S(2)}, u32[]{:S(2)}) collective-permute-start(bf16[256,512]{1,0:T(8,128)(2,1)} %copy-done.12), channel_id=1, source_target_pairs={{0,4},{4,8},{8,12},{12,0},{1,5},{5,9},{9,13},{13,1},{2,6},{6,10},{... | collective-permute-start | bytes 786440 | tf_op jit(solution)/shard_map/ppermute | solution.py:635
  86.6 18.7 %collective-permute-start.26 = (bf16[256,512]{1,0:T(8,128)(2,1)}, bf16[256,512]{1,0:T(8,128)(2,1)S(1)}, u32[]{:S(2)}, u32[]{:S(2)}) collective-permute-start(bf16[256,512]{1,0:T(8,128)(2,1)} %copy-done.12), channel_id=1, source_target_pairs={{0,2},{2,0},{1,3},{3,1},{4,6},{6,4},{5,7},{7,5},{8,10},{10,8},{9,1... | collective-permute-start | bytes 786440 | tf_op jit(solution)/shard_map/ppermute | solution.py:635
  121.3 13.3 %collective-permute-start.35 = (bf16[2,512,128]{2,1,0:T(8,128)(2,1)S(1)}, bf16[2,512,128]{2,1,0:T(8,128)(2,1)S(1)}, u32[]{:S(2)}, u32[]{:S(2)}) collective-permute-start(bf16[2,512,128]{2,1,0:T(8,128)(2,1)S(1)} %get-tuple-element.194), channel_id=1, source_target_pairs={{0,17},{1,16},{16,1},{17,0},{2,19},{3,18},{18,3},{19,2},{4,21},{5,... | collective-permute-start | bytes 786440 | tf_op jit(solution)/shard_map/ppermute | solution.py:788
  122.9 11.7 %collective-permute-start.34 = (bf16[2,512,128]{2,1,0:T(8,128)(2,1)S(1)}, bf16[2,512,128]{2,1,0:T(8,128)(2,1)S(1)}, u32[]{:S(2)}, u32[]{:S(2)}) collective-permute-start(bf16[2,512,128]{2,1,0:T(8,128)(2,1)S(1)} %get-tuple-element.197.refs_2_), channel_id=1, source_target_pairs={{0,16},{1,17},{16,0},{17,1},{2,18},{3,19},{18,2},{19,3},{4,20},{5,... | collective-permute-start | bytes 786440 | tf_op jit(solution)/shard_map/ppermute | solution.py:788
  123.2 14.4 %collective-permute-start.36 = (bf16[2,256,256]{2,1,0:T(8,128)(2,1)S(1)}, bf16[2,256,256]{2,1,0:T(8,128)(2,1)S(1)}, u32[]{:S(2)}, u32[]{:S(2)}) collective-permute-start(bf16[2,256,256]{2,1,0:T(8,128)(2,1)S(1)} %dynamic-slice_bitcast_fusion), channel_id=1, source_target_pairs={{0,8},{4,12},{8,0},{12,4},{1,9},{5,13},{9,1},{13,5},{2,10},{6,14},... | collective-permute-start | bytes 786440 | tf_op jit(solution)/shard_map/ppermute | solution.py:635
  125.4 16.6 %collective-permute-start.37 = (bf16[2,512,128]{2,1,0:T(8,128)(2,1)S(1)}, bf16[2,512,128]{2,1,0:T(8,128)(2,1)S(1)}, u32[]{:S(2)}, u32[]{:S(2)}) collective-permute-start(bf16[2,512,128]{2,1,0:T(8,128)(2,1)S(1)} %get-tuple-element.216.refs_2_), channel_id=1, source_target_pairs={{0,16},{1,17},{16,0},{17,1},{2,18},{3,19},{18,2},{19,3},{4,20},{5,... | collective-permute-start | bytes 786440 | tf_op jit(solution)/shard_map/ppermute | solution.py:788
  144.1 9.4 %collective-permute-start.39 = (bf16[512,256]{1,0:T(8,128)(2,1)S(1)}, bf16[512,256]{1,0:T(8,128)(2,1)S(1)}, u32[]{:S(2)}, u32[]{:S(2)}) collective-permute-start(bf16[512,256]{1,0:T(8,128)(2,1)S(1)} %maximum_select_fusion.3.refs_0_), channel_id=1, source_target_pairs={{0,4},{4,8},{8,12},{12,0},{1,5},{5,9},{9,13},{13,1},{2,6},{6,10},{... | collective-permute-start | bytes 786440 | tf_op jit(solution)/shard_map/ppermute | solution.py:635
  159.2 9.7 %collective-permute-start.41 = (bf16[512,256]{1,0:T(8,128)(2,1)S(1)}, bf16[512,256]{1,0:T(8,128)(2,1)S(1)}, u32[]{:S(2)}, u32[]{:S(2)}) collective-permute-start(bf16[512,256]{1,0:T(8,128)(2,1)S(1)} %collective-permute-done.39.refs_4_), channel_id=1, source_target_pairs={{0,4},{4,8},{8,12},{12,0},{1,5},{5,9},{9,13},{13,1},{2,6},{6,10},{... | collective-permute-start | bytes 786440 | tf_op jit(solution)/shard_map/ppermute | solution.py:635
  159.2 9.7 %collective-permute-start.42 = (bf16[512,256]{1,0:T(8,128)(2,1)S(1)}, bf16[512,256]{1,0:T(8,128)(2,1)S(1)}, u32[]{:S(2)}, u32[]{:S(2)}) collective-permute-start(bf16[512,256]{1,0:T(8,128)(2,1)S(1)} %collective-permute-done.39.refs_4_), channel_id=1, source_target_pairs={{0,2},{2,0},{1,3},{3,1},{4,6},{6,4},{5,7},{7,5},{8,10},{10,8},{9,1... | collective-permute-start | bytes 786440 | tf_op jit(solution)/shard_map/ppermute | solution.py:635
  160.6 14.0 %collective-permute-start.49 = (bf16[512,256]{1,0:T(8,128)(2,1)S(1)}, bf16[512,256]{1,0:T(8,128)(2,1)S(1)}, u32[]{:S(2)}, u32[]{:S(2)}) collective-permute-start(bf16[512,256]{1,0:T(8,128)(2,1)S(1)} %maximum_select_fusion.4.refs_1_), channel_id=1, source_target_pairs={{0,4},{4,8},{8,12},{12,0},{1,5},{5,9},{9,13},{13,1},{2,6},{6,10},{... | collective-permute-start | bytes 786440 | tf_op jit(solution)/shard_map/ppermute | solution.py:635
  162.6 11.9 %collective-permute-start.50 = (bf16[512,256]{1,0:T(8,128)(2,1)S(1)}, bf16[512,256]{1,0:T(8,128)(2,1)S(1)}, u32[]{:S(2)}, u32[]{:S(2)}) collective-permute-start(bf16[512,256]{1,0:T(8,128)(2,1)S(1)} %maximum_select_fusion.4.refs_1_), channel_id=1, source_target_pairs={{0,2},{2,0},{1,3},{3,1},{4,6},{6,4},{5,7},{7,5},{8,10},{10,8},{9,1... | collective-permute-start | bytes 786440 | tf_op jit(solution)/shard_map/ppermute | solution.py:635
  168.9 11.2 %collective-permute-start.43 = (bf16[512,256]{1,0:T(8,128)(2,1)S(1)}, bf16[512,256]{1,0:T(8,128)(2,1)S(1)}, u32[]{:S(2)}, u32[]{:S(2)}) collective-permute-start(bf16[512,256]{1,0:T(8,128)(2,1)S(1)} %collective-permute-done.41.refs_8_), channel_id=1, source_target_pairs={{0,4},{4,8},{8,12},{12,0},{1,5},{5,9},{9,13},{13,1},{2,6},{6,10},{... | collective-permute-start | bytes 786440 | tf_op jit(solution)/shard_map/ppermute | solution.py:635
  169.3 10.8 %collective-permute-start.44 = (bf16[512,256]{1,0:T(8,128)(2,1)S(1)}, bf16[512,256]{1,0:T(8,128)(2,1)S(1)}, u32[]{:S(2)}, u32[]{:S(2)}) collective-permute-start(bf16[512,256]{1,0:T(8,128)(2,1)S(1)} %collective-permute-done.41.refs_8_), channel_id=1, source_target_pairs={{0,2},{2,0},{1,3},{3,1},{4,6},{6,4},{5,7},{7,5},{8,10},{10,8},{9,1... | collective-permute-start | bytes 786440 | tf_op jit(solution)/shard_map/ppermute | solution.py:635
  174.5 11.2 %collective-permute-start.52 = (bf16[512,256]{1,0:T(8,128)(2,1)S(1)}, bf16[512,256]{1,0:T(8,128)(2,1)S(1)}, u32[]{:S(2)}, u32[]{:S(2)}) collective-permute-start(bf16[512,256]{1,0:T(8,128)(2,1)S(1)} %collective-permute-done.49.refs_5_), channel_id=1, source_target_pairs={{0,4},{4,8},{8,12},{12,0},{1,5},{5,9},{9,13},{13,1},{2,6},{6,10},{... | collective-permute-start | bytes 786440 | tf_op jit(solution)/shard_map/ppermute | solution.py:635
  175.0 10.8 %collective-permute-start.53 = (bf16[512,256]{1,0:T(8,128)(2,1)S(1)}, bf16[512,256]{1,0:T(8,128)(2,1)S(1)}, u32[]{:S(2)}, u32[]{:S(2)}) collective-permute-start(bf16[512,256]{1,0:T(8,128)(2,1)S(1)} %collective-permute-done.49.refs_5_), channel_id=1, source_target_pairs={{0,2},{2,0},{1,3},{3,1},{4,6},{6,4},{5,7},{7,5},{8,10},{10,8},{9,1... | collective-permute-start | bytes 786440 | tf_op jit(solution)/shard_map/ppermute | solution.py:635
  175.8 12.9 %collective-permute-start.58 = (bf16[2,256,256]{2,1,0:T(8,128)(2,1)S(1)}, bf16[2,256,256]{2,1,0:T(8,128)(2,1)S(1)}, u32[]{:S(2)}, u32[]{:S(2)}) collective-permute-start(bf16[2,256,256]{2,1,0:T(8,128)(2,1)S(1)} %collective-permute-done.36.refs_26_.refs_8_), channel_id=1, source_target_pairs={{0,16},{16,0},{1,17},{17,1},{2,18},{18,2},{3,19},{19,3},{4,20},{20... | collective-permute-start | bytes 786440 | tf_op jit(solution)/shard_map/ppermute | solution.py:635
  187.0 9.8 %collective-permute-start.57 = (bf16[2,256,256]{2,1,0:T(8,128)(2,1)S(1)}, bf16[2,256,256]{2,1,0:T(8,128)(2,1)S(1)}, u32[]{:S(2)}, u32[]{:S(2)}) collective-permute-start(bf16[2,256,256]{2,1,0:T(8,128)(2,1)S(1)} %collective-permute-done.36.refs_26_.refs_8_), channel_id=1, source_target_pairs={{0,1},{1,0},{2,3},{3,2},{4,5},{5,4},{6,7},{7,6},{8,9},{9,8},{10,11... | collective-permute-start | bytes 786440 | tf_op jit(solution)/shard_map/ppermute | solution.py:54
  (87 other events, 1017.4 us)

commit v5 on v4

--- a/solution.py
+++ b/solution.py
@@ -164,7 +164,7 @@
             ],
         ),
         out_shape=[jax.ShapeDtypeStruct(first, BF16), jax.ShapeDtypeStruct(second, BF16)],
-        compiler_params=params(40),
+        compiler_params=params(32),
         cost_estimate=cost(2 * count * PIX * CH * (256 + width), 4 << 20, count * PIX * CH),
         name="down_stream",
     )(meta, *pieces, conv, patch_in, halves, halves, gain.reshape(1, width))
@@ -187,57 +187,68 @@
     return lax.rem(tile + tiles - entry // 2, tiles) * outer + lax.rem(mpo + entry % 2, outer)
 
 
-def qkv_kernel(count, groups, first, last, meta, *refs):
+def qkv_kernel(entries, layout, groups, first, last, meta, *refs):
     refs = list(refs)
+    count = len(entries)
     x_refs = take_blocks(refs, count)
-    weight_refs = [[refs.pop(0) for _ in range(6)] for _ in range(count)]
+    weight_refs = [refs.pop(0) for _ in range(6)]
     if not first:
         acc_in, square_in = refs.pop(0), refs.pop(0)
     if last:
         head_gains = refs.pop(0)
-    scaled = refs.pop()
-    half, span = scaled.shape[1:]
-    chunk = 64
-
-    def scale_rows(block, gain, piece, base, index, carry):
-        rows = pl.ds(pl.multiple_of(base + index * chunk, chunk), chunk)
-        local = pl.ds(pl.multiple_of(index * chunk, chunk), chunk)
-        if block:
-            square = square_out[rows, :]
-        else:
-            square = jnp.zeros((chunk, HD), F32) if first else square_in[rows, :]
-        value = piece[local, :].astype(F32)
-        scaled[block, rows, :] = (value * gain).astype(BF16)
+    fetched, arrived = refs.pop(-2), refs.pop(-1)
+    span, width = fetched.shape[2:]
+    half = 2 * x_refs[0][1].shape[0]
+    heads = width // HD
+
+    def fetch(index):
+        rows = pl.ds(pl.multiple_of(chip_of(meta, *layout, entries[index]) * span, span), span)
+        return [
+            pltpu.make_async_copy(
+                weight_refs[part].at[rows, :], fetched.at[index % 2, part], arrived.at[index % 2, part]
+            )
+            for part in range(6)
+        ]
+
+    copies = fetch(0)
+    for copy in copies:
+        copy.start()
+    square = None if first else square_in[...]
+    if last:
+        acc, outs = [None] * 6, refs
+    else:
+        acc_out, square_out = refs
+    for index in range(count):
+        following = fetch(index + 1) if index + 1 < count else []
+        for copy in following:
+            copy.start()
+        gain = x_refs[index][0][half // 2 :, :][:1]
+        value = jnp.concatenate([x_refs[index][0][: half // 2, :], x_refs[index][1][...]], axis=0)
+        scaled = (value * gain).astype(BF16)
+        value = value.astype(F32)
         value = value * value
         for part in range(span // HD):
-            square = square + value[:, part * HD : (part + 1) * HD]
-        square_out[rows, :] = square
-        return carry
-
-    if last:
-        square_out = refs.pop()
-        outs = refs
-    else:
-        acc_out, square_out = refs
-    for block in range(count):
-        gain = x_refs[block][0][half // 2 :, :].astype(F32)[:1]
-        for part in range(2):
-            body = functools.partial(scale_rows, block, gain, x_refs[block][part], part * half // 2)
-            lax.fori_loop(0, half // 2 // chunk, body, 0)
-    width = weight_refs[0][0].shape[1]
-    heads = width // HD
-    if last:
-        mean = jnp.sum(square_out[...], axis=-1, keepdims=True) * (1.0 / (groups * span))
-        scale = lax.rsqrt(mean + EPSILON)
+            piece = value[:, part * HD : (part + 1) * HD]
+            square = piece if square is None else square + piece
+        for part in range(6):
+            copies[part].wait()
+            term = mxu(scaled, fetched[index % 2, part])
+            if index == 0 and not first:
+                term = term + acc_in[part]
+            if last:
+                acc[part] = term if index == 0 else acc[part] + term
+            elif index == 0:
+                acc_out[part] = term
+            else:
+                acc_out[part] += term
+        copies = following
+    if not last:
+        square_out[...] = square
+        return
+    mean = jnp.sum(square, axis=-1, keepdims=True) * (1.0 / (groups * span))
+    scale = lax.rsqrt(mean + EPSILON)
     for part in range(6):
-        total = None if first else acc_in[part]
-        for block in range(count):
-            term = mxu(scaled[block], weight_refs[block][part][...])
-            total = term if total is None else total + term
-        if not last:
-            acc_out[part] = total
-            continue
-        total = total * scale
+        total = acc[part] * scale
         side, kind = part // 3, part % 3
         kv_outs = outs[2 * heads * side : 2 * heads * side + heads]
         q_outs = outs[2 * heads * side + heads : 2 * heads * side + 2 * heads]
@@ -262,38 +273,35 @@
     groups = layout[1] * layout[2]
     inputs = [p for pieces in blocks for p in pieces]
     specs = [full(p.shape) for p in inputs]
-    for entry in entries:
-        for weight in weights:
-            inputs.append(weight)
-            specs.append(
-                pl.BlockSpec((span, width), lambda i, m, entry=entry: (chip_of(m, *layout, entry), 0))
-            )
+    inputs += weights
+    specs += [pl.BlockSpec(memory_space=pl.ANY)] * 6
     if not first:
         inputs += list(state)
         specs += [full(s.shape) for s in state]
-    scratch = [pltpu.VMEM((count, half, span), BF16)]
     if last:
         inputs.append(head_gains)
         specs.append(full(head_gains.shape))
         kv, q = jax.ShapeDtypeStruct((2, half, HD), BF16), jax.ShapeDtypeStruct((half, HD), BF16)
         outs = ([kv] * heads + [q] * heads) * 2
-        scratch = [pltpu.VMEM((half, HD), F32)] + scratch
     else:
         outs = [
             jax.ShapeDtypeStruct((6, half, width), F32),
             jax.ShapeDtypeStruct((half, HD), F32),
         ]
     return pl.pallas_call(
-        functools.partial(qkv_kernel, count, groups, first, last),
+        functools.partial(qkv_kernel, entries, layout, groups, first, last),
         grid_spec=pltpu.PrefetchScalarGridSpec(
             num_scalar_prefetch=1,
             grid=(1,),
             in_specs=specs,
             out_specs=[full(o.shape) for o in outs],
-            scratch_shapes=scratch,
+            scratch_shapes=[
+                pltpu.VMEM((2, 6, span, width), BF16),
+                pltpu.SemaphoreType.DMA((2, 6)),
+            ],
         ),
         out_shape=outs,
-        compiler_params=params(48),
+        compiler_params=params(40),
         cost_estimate=cost(12 * count * half * span * width, (6 + 2 * count) << 20),
         name="qkv_last" if last else "qkv_step",
     )(meta, *inputs)
@@ -420,7 +428,7 @@
             out_specs=[full(o.shape) for o in outs],
         ),
         out_shape=outs,
-        compiler_params=params(40),
+        compiler_params=params(24),
         cost_estimate=cost(8 * count * half * heads * HD * width, (2 + count) << 20),
         name="out_last" if last else "out_step",
     )(meta, *inputs)
@@ -635,34 +643,54 @@
     return lax.ppermute(values, axis, [(i, (i + step) % count) for i in range(count)])
 
 
-def gather_small(latents, down_conv):
+def gather_small(latents, down_conv, *others):
     ctxs, tiles = lax.axis_size("ctx"), lax.axis_size("tile")
     every = jnp.concatenate([latents] + [shift(latents, "ctx", s) for s in range(1, ctxs)])
     conv = by_core(lax.axis_index("core"), down_conv, swap(down_conv), 1)
     conv = by_core(lax.axis_index("mpo"), conv, shift(conv, "mpo", 1), 1)
-    return [every] + [shift(every, "tile", s) for s in range(1, tiles)], conv
-
-
-def transpose_first(patch_out):
-    ctxs, tiles, outer = (lax.axis_size(name) for name in ("ctx", "tile", "mpo"))
-    ctx, mpo = lax.axis_index("ctx"), lax.axis_index("mpo")
+    every, conv, others = lax.optimization_barrier((every, conv, others))
+    return [every] + [shift(every, "tile", s) for s in range(1, tiles)], conv, *others
+
+
+def columns_kernel(meta, kept_in, sent_in, kept_out, sent_out):
+    kept_out[0] = kept_in[...]
+    sent_out[0] = sent_in[...]
+
+
+def transpose_first(meta, patch_out, layout, ctxs):
+    images, tiles, outer = layout
     width, features = patch_out.shape
     deep = features // (tiles * outer)
     halves = 2 if ctxs == 2 and deep == 2 * CH else 1
-    view = patch_out.reshape(width, tiles, outer, halves, deep // halves)
-    at = ctx if halves == 2 else 0
-
-    def columns(which):
-        size = (width, tiles, 1, 1, deep // halves)
-        return lax.dynamic_slice(view, (0, 0, which, at, 0), size)[:, :, 0, 0].transpose(1, 0, 2)
-
-    return columns(mpo), columns(1 - mpo), halves
-
-
-def transpose_second(both, step):
+    size = deep // halves
+
+    def place(other):
+        def index(i, m):
+            ctx, _, _, mpo = split_meta(m, images)
+            chip = i * outer + lax.rem(mpo + other, outer)
+            return 0, chip * halves + (ctx if halves == 2 else 0)
+
+        return pl.BlockSpec((width, size), index)
+
+    out = pl.BlockSpec((1, width, size), lambda i, m: (i, 0, 0))
+    kept, sent = pl.pallas_call(
+        columns_kernel,
+        grid_spec=pltpu.PrefetchScalarGridSpec(
+            num_scalar_prefetch=1, grid=(tiles,), in_specs=[place(0), place(1)], out_specs=[out, out]
+        ),
+        out_shape=[jax.ShapeDtypeStruct((tiles, width, size), BF16)] * 2,
+        compiler_params=params(8),
+        cost_estimate=cost(1 << 16, 2 << 20),
+        name="columns",
+    )(meta, patch_out, patch_out)
+    return kept, sent, halves
+
+
+def transpose_second(kept, received, step):
     tiles = lax.axis_size("tile")
     place = lax.rem(lax.axis_index("tile") + step, tiles)
-    block = lax.dynamic_index_in_dim(both, place, 0, keepdims=False)
+    block = [lax.dynamic_index_in_dim(x, place, 0, keepdims=False) for x in (kept, received)]
+    block = jnp.stack(block)
     return shift(block, "tile", step) if step else block
 
 
@@ -702,7 +730,10 @@
     seen = first
     for which, index in events:
         ring, cross = moving[which]
-        ring, cross, seen, state = lax.optimization_barrier((ring, cross, seen, state))
+        if (which, index) == (int(late), tiles - 1):
+            ring, cross, seen, state = lax.optimization_barrier((ring, cross, seen, state))
+        else:
+            ring, cross, seen = lax.optimization_barrier((ring, cross, seen))
         found[which][2 * index], found[which][2 * index - 1] = ring, cross
         seen = ring
         launch(which, index)
@@ -741,16 +772,6 @@
     images = span_start.shape[0]
     local = latents.shape[0]
 
-    pieces, conv = gather_small(latents, down_conv)
-    weights = [swap(key_weight)]
-    kept, sent, halves = transpose_first(patch_out)
-    pieces, conv, weights, received, later = lax.optimization_barrier(
-        (pieces, conv, weights, shift(sent, "mpo", 1), [value_weight, query_weight])
-    )
-    later = [swap(w) for w in later]
-    both = jnp.stack([kept, received], axis=1)
-    up_blocks = [transpose_second(both, step) for step in range(tiles) if 2 * step != tiles]
-
     numbers = jnp.arange(images, dtype=jnp.int32)
     matches = image_of_slot[None, :] == numbers[:, None]
     slot_of_image = jnp.sum(jnp.where(matches, numbers[None, :], 0), axis=1)
@@ -760,22 +781,29 @@
     ).astype(jnp.int32)
     layout = (images, tiles, outer)
 
+    weights = [swap(w) for w in (key_weight, value_weight, query_weight)]
+    pieces, conv, meta, weights[0], weights[1] = gather_small(latents, down_conv, meta, *weights[:2])
+    kept, sent, halves = transpose_first(meta, patch_out, layout, ctxs)
+    pieces, received = lax.optimization_barrier((pieces, shift(sent, "mpo", 1)))
+    up_blocks = [transpose_second(kept, received, step) for step in range(tiles) if 2 * step != tiles]
+
     streams = down_stream(meta, pieces, conv, patch_in, text_embed, norm_gain, images)
-    streams, later, up_blocks = lax.optimization_barrier((streams, later, up_blocks))
+    streams, weights[2], out_par, up_blocks = lax.optimization_barrier(
+        (streams, weights[2], swap(out_weight), up_blocks)
+    )
     others = [swap(s[1]) for s in streams]
-    weights += later + [key_weight, value_weight, query_weight]
+    weights += [key_weight, value_weight, query_weight]
 
     head_gains = jnp.stack([query_gain, key_gain])
 
     def project(blocks, entries, state, last):
         return qkv_step(meta, layout, blocks, entries, weights, state, head_gains if last else None)
 
-    extras = (swap(out_weight), transposed(up_blocks, halves))
-    state, (out_par, up_first) = gather_pair(
-        *[by_core(core, s[0], o, 1) for s, o in zip(streams, others)], None, project, extras
+    state, up_first = gather_pair(
+        *[by_core(core, s[0], o, 1) for s, o in zip(streams, others)], None, project, transposed(up_blocks, halves)
     )
-    state, both = lax.optimization_barrier((state, both))
-    up_block = transpose_second(both, tiles // 2)
+    state, kept, received = lax.optimization_barrier((state, kept, received))
+    up_block = transpose_second(kept, received, tiles // 2)
     kv_send, q_send = state[:heads], state[heads : 2 * heads]
     kv_own, q_own = state[2 * heads : 3 * heads], state[3 * heads :]
 
@@ -787,13 +815,10 @@
         ]
         return lax.ppermute(values, ("ctx", "core"), pairs)
 
-    def same_core(head):
-        return [shifted(kv_own[head], step, False) for step in range(1, ctxs)]
-
-    def pieces_of(head, same):
+    def pieces_of(head):
         pieces = [swap(q_send[head]), kv_own[head], swap(kv_send[head])]
         for step in range(1, ctxs):
-            pieces += [same[step - 1], shifted(kv_send[head], step, True)]
+            pieces += [shifted(kv_own[head], step, False), shifted(kv_send[head], step, True)]
         return pieces
 
     def attend(head, pieces, ahead):
@@ -801,8 +826,8 @@
         (att_own, att_send), ahead = lax.optimization_barrier((result, ahead))
         return by_core(core, att_own, swap(att_send), 1), ahead
 
-    pieces, up_block = lax.optimization_barrier((pieces_of(0, same_core(0)), up_block))
-    attended, same = attend(0, pieces, same_core(1) if heads > 1 else None)
+    pieces, up_block = lax.optimization_barrier((pieces_of(0), up_block))
+    attended, pieces = attend(0, pieces, pieces_of(1) if heads > 1 else None)
     if heads == 1:
         attended, second = attended[: half // 2], attended[half // 2 :]
         extras = transposed([up_block], halves)
@@ -810,8 +835,7 @@
         extras = None
 
         def second(token):
-            pieces, token = lax.optimization_barrier((pieces_of(1, same), token))
-            result, block = lax.optimization_barrier((attend(1, pieces, None)[0], up_block))
+            result, (block, _) = attend(1, pieces, (up_block, token))
             return result, transposed([block], halves)
 
     def project_out(blocks, entries, state, last):

time: 265 us -> 276 us (1.042)
  waiting for transfers between devices: 94.9 us -> 114 us
  Pallas kernels: 56.3 us -> 66.3 us
  local copies, waits for them, and re-layouts: 25.7 us -> 16.2 us
  starting transfers between devices: 82.1 us -> 74.1 us
    ppermute x56, waiting for transfers between devices: 75.4 us -> 95.6 us  [shift(): lax.ppermute(values, axis, [(i, (i + step) % count) for i in range(count)])]
    pallas_call x3 -> x4, Pallas kernels: 21.9 us -> 35.2 us  [the longest x3 33 us: qkv_step(): pl.pallas_call(functools.partial(qkv_kernel, entries, layout, groups, fir...]
    ppermute x56, starting transfers between devices: 50.2 us -> 42.2 us  [shift(): lax.ppermute(values, axis, [(i, (i + step) % count) for i in range(count)])]
    dynamic_slice x3, local copies, waits for them, and re-layouts: 7.04 us -> 2.02 us  [transpose_second(): lax.dynamic_index_in_dim(x, place, 0, keepdims=False)]
    reshape x1 -> x0, local copies, waits for them, and re-layouts: 4.47 us -> none  [transpose_first(): view = patch_out.reshape(width, tiles, outer, halves, deep // halves)]
    pallas_call x3, Pallas kernels: 7.57 us -> 4.31 us  [out_step(): pl.pallas_call(functools.partial(out_kernel, count, heads, first, last),...]
    unnamed x74 -> x67, local copies, waits for them, and re-layouts: 12.7 us -> 11.9 us
  transfers between devices with their start and end apart: 84 -> 84, of which waited for: 35 -> 38; matrix products, arithmetic and copies ran while one was open for 6% -> 3% of each run, Pallas kernels for 15% -> 20%
where the time goes in v5:
time: 276 us
  waiting for transfers between devices  114 us (41%)
  starting transfers between devices  74.1 us (27%)
  Pallas kernels  66.3 us (24%)
  local copies, waits for them, and re-layouts  16.2 us (6%)
  other arithmetic  3.47 us (1%)
    ppermute x56, waiting for transfers between devices, shift(): lax.ppermute(values, axis, [(i, (i + step) % count) for i in range(count)])  95.6 us
    ppermute x56, starting transfers between devices, shift(): lax.ppermute(values, axis, [(i, (i + step) % count) for i in range(count)])  42.2 us
    pallas_call x3, Pallas kernels, qkv_step(): pl.pallas_call(functools.partial(qkv_kernel, entries, layout, groups, fir...  33 us
    ppermute x19, starting transfers between devices, swap(): return lax.ppermute(values, 'core', [(0, 1), (1, 0)])  19.5 us
    ppermute x6, waiting for transfers between devices, shifted(): return lax.ppermute(values, ('ctx', 'core'), pairs)  12.6 us
    unnamed x67, local copies, waits for them, and re-layouts  11.9 us
    pallas_call x1, Pallas kernels, down_stream(): pl.pallas_call(functools.partial(down_kernel, images, tiles, half), grid_...  9.33 us
    pallas_call x2, Pallas kernels, attention(): pl.pallas_call(functools.partial(attention_kernel, images, len(pieces), h...  8.88 us
  transfers between devices with their start and end apart: 84, of which 38 were waited for; matrix products, arithmetic and copies ran while one was open for 3% of the time, Pallas kernels for 20%

profile of v5, /device:TPU:1, one launch (start us, length us, event | category | flops | bytes accessed | tf_op | source)
XLA Modules:
  0.0 275.7 jit_solution(5806919260740075255)
XLA Ops:
  5.0 2.4 collective-permute-start.2
  24.1 3.4 %collective-permute-done.7.refs_3_ = bf16[4,16,512]{2,1,0:T(8,128)(2,1)S(1)} collective-permute-done((bf16[4,16,512]{2,1,0:T(8,128)(2,1)S(1)}, bf16[4,16,512]{2,1,0:T(8,128)(2,1)S(1)}, u32[]{:S(2)}, u32[]{:S(2)}) %collective-permute-start.7) | collective-permute-done | bytes 65568 | tf_op jit(solution)/shard_map/ppermute | solution.py:643
  32.1 9.3 %down_stream.1 = (bf16[2,272,256]{2,1,0:T(8,128)(2,1)S(1)}, bf16[2,256,256]{2,1,0:T(8,128)(2,1)S(1)}) custom-call(s32[16]{0:T(128)S(1)} %concatenate.64.meta, bf16[4,16,512]{2,1,0:T(8,128)(2,1)S(1)} %pad_maximum_fusion.6.refs_0_, bf16[4,16,512]{2,1,0:T(8,128)(2,1)S(1)} %collective-permute-done.5.refs_1_, ...), custom_call_target="tpu_custom_call" | custom-call | flops 4294967296 | bytes 4194304 | tf_op jit(solution)/shard_map/down_stream/pallas_call | solution.py:144
  43.0 3.9 %collective-permute-start.13 = (bf16[272,256]{1,0:T(8,128)(2,1)S(1)}, bf16[272,256]{1,0:T(8,128)(2,1)S(1)}, u32[]{:S(2)}, u32[]{:S(2)}) collective-permute-start(bf16[272,256]{1,0:T(8,128)(2,1)S(1)} %get-tuple-element.268), channel_id=1, source_target_pairs={{0,1},{1,0},{2,3},{3,2},{4,5},{5,4},{6,7},{7,6},{8,9},{9,8},{10,11... | collective-permute-start | bytes 417800 | tf_op jit(solution)/shard_map/ppermute | solution.py:54
  50.9 7.9 %collective-permute-done.14.refs_4_ = bf16[272,512]{1,0:T(8,128)(2,1)S(1)} collective-permute-done((bf16[272,512]{1,0:T(8,128)(2,1)S(1)}, bf16[272,512]{1,0:T(8,128)(2,1)S(1)}, u32[]{:S(2)}, u32[]{:S(2)}) %collective-permute-start.14) | collective-permute-done | bytes 278560 | tf_op jit(solution)/shard_map/ppermute | solution.py:643
  60.6 12.7 %collective-permute-done.19.refs_5_ = bf16[256,512]{1,0:T(8,128)(2,1)S(1)} collective-permute-done((bf16[256,512]{1,0:T(8,128)(2,1)S(1)}, bf16[256,512]{1,0:T(8,128)(2,1)S(1)}, u32[]{:S(2)}, u32[]{:S(2)}) %collective-permute-start.19) | collective-permute-done | bytes 262176 | tf_op jit(solution)/shard_map/ppermute | solution.py:643
  74.1 2.7 collective-permute-start.29
  76.8 10.3 %collective-permute-done.23.refs_9_ = bf16[256,512]{1,0:T(8,128)(2,1)} collective-permute-done((bf16[256,512]{1,0:T(8,128)(2,1)S(1)}, bf16[256,512]{1,0:T(8,128)(2,1)}, u32[]{:S(2)}, u32[]{:S(2)}) %collective-permute-start.23) | collective-permute-done | bytes 262176 | tf_op jit(solution)/shard_map/ppermute | solution.py:643
  88.6 16.4 %qkv_step.2 = (f32[6,512,256]{2,1,0:T(8,128)}, f32[512,128]{1,0:T(8,128)S(1)}) custom-call(s32[16]{0:T(128)S(1)} %concatenate.64.meta, bf16[272,512]{1,0:T(8,128)(2,1)S(1)} %maximum_select_fusion.1.refs_0_, bf16[256,512]{1,0:T(8,128)(2,1)S(1)} %maximum_select_fusion.2.refs_1_, bf16[272,512]{1,0:T(8,128)(2,1)S(1)} %collective-permute-done.15.refs_2_, ...), custom_call_target="tpu_custom_call" | custom-call | flops 4026531840 | bytes 16777216 | tf_op jit(solution)/shard_map/qkv_step/pallas_call | solution.py:291
  113.7 10.3 %qkv_step.3 = (f32[6,512,256]{2,1,0:T(8,128)}, f32[512,128]{1,0:T(8,128)S(1)}) custom-call(s32[16]{0:T(128)S(1)} %concatenate.64.meta, bf16[272,512]{1,0:T(8,128)(2,1)} %collective-permute-done.21.refs_0_, bf16[256,512]{1,0:T(8,128)(2,1)} %collective-permute-done.26.refs_1_, bf16[272,512]{1,0:T(8,128)(2,1)S(1)} %copy-done.14, ...), custom_call_target="tpu_custom_call" | custom-call | flops 1610612736 | bytes 10485760 | tf_op jit(solution)/shard_map/qkv_step/pallas_call | solution.py:291
  124.0 6.4 %qkv_last.1 = (bf16[2,512,128]{2,1,0:T(8,128)(2,1)S(1)}, bf16[2,512,128]{2,1,0:T(8,128)(2,1)S(1)}, bf16[512,128]{1,0:T(8,128)(2,1)S(1)}, bf16[512,128]{1,0:T(8,1...) custom-call(s32[16]{0:T(128)S(1)} %concatenate.64.meta, ...), custom_call_target="tpu_custom_call" | custom-call | flops 805306368 | bytes 8388608 | tf_op jit(solution)/shard_map/qkv_last/pallas_call | solution.py:291
  130.4 3.9 %collective-permute-start.33 = (bf16[2,512,128]{2,1,0:T(8,128)(2,1)S(1)}, bf16[2,512,128]{2,1,0:T(8,128)(2,1)S(1)}, u32[]{:S(2)}, u32[]{:S(2)}) collective-permute-start(bf16[2,512,128]{2,1,0:T(8,128)(2,1)S(1)} %get-tuple-element.184), channel_id=1, source_target_pairs={{0,1},{1,0},{2,3},{3,2},{4,5},{5,4},{6,7},{7,6},{8,9},{9,8},{10,11... | collective-permute-start | bytes 786440 | tf_op jit(solution)/shard_map/ppermute | solution.py:54
  137.1 4.1 %collective-permute-start.36 = (bf16[2,256,256]{2,1,0:T(8,128)(2,1)S(1)}, bf16[2,256,256]{2,1,0:T(8,128)(2,1)S(1)}, u32[]{:S(2)}, u32[]{:S(2)}) collective-permute-start(bf16[2,256,256]{2,1,0:T(8,128)(2,1)S(1)} %pad_maximum_fusion.4), channel_id=1, source_target_pairs={{0,8},{4,12},{8,0},{12,4},{1,9},{5,13},{9,1},{13,5},{2,10},{6,14},... | collective-permute-start | bytes 786440 | tf_op jit(solution)/shard_map/ppermute | solution.py:643
  142.4 5.1 %collective-permute-done.34.refs_4_ = bf16[2,512,128]{2,1,0:T(8,128)(2,1)S(1)} collective-permute-done((bf16[2,512,128]{2,1,0:T(8,128)(2,1)S(1)}, bf16[2,512,128]{2,1,0:T(8,128)(2,1)S(1)}, u32[]{:S(2)}, u32[]{:S(2)}) %collective-permute-start.34) | collective-permute-done | bytes 262176 | tf_op jit(solution)/shard_map/ppermute | solution.py:816
  149.7 3.4 %collective-permute-done.36.refs_26_.refs_8_ = bf16[2,256,256]{2,1,0:T(8,128)(2,1)S(1)} collective-permute-done((bf16[2,256,256]{2,1,0:T(8,128)(2,1)S(1)}, bf16[2,256,256]{2,1,0:T(8,128)(2,1)S(1)}, u32[]{:S(2)}, u32[]{:S(2)}) %collective-permute-start.36) | collective-permute-done | bytes 262176 | tf_op jit(solution)/shard_map/ppermute | solution.py:643
  153.1 4.4 %attention.2 = (bf16[512,128]{1,0:T(8,128)(2,1)S(1)}, bf16[512,128]{1,0:T(8,128)(2,1)S(1)}) custom-call(s32[16]{0:T(128)S(1)} %concatenate.64.meta, bf16[512,128]{1,0:T(8,128)(2,1)S(1)} %get-tuple-element.181.refs_0_, bf16[512,128]{1,0:T(8,128)(2,1)S(1)} %collective-permute-done.32.refs_1_, bf16[2,512,128]{2,1,0:T(8,128)(2,1)S(1)} %get-tuple-element.188.refs_2_, ...), custom_call_target="tpu_custom_call" | custom-call | flops 1073741824 | bytes 1048576 | tf_op jit(solution)/shard_map/attention/pallas_call | solution.py:352
  161.9 4.4 %attention.3 = (bf16[512,128]{1,0:T(8,128)(2,1)S(1)}, bf16[512,128]{1,0:T(8,128)(2,1)S(1)}) custom-call(s32[16]{0:T(128)S(1)} %concatenate.64.meta, bf16[512,128]{1,0:T(8,128)(2,1)S(1)} %get-tuple-element.201.refs_0_, bf16[512,128]{1,0:T(8,128)(2,1)S(1)} %collective-permute-done.37.refs_1_, bf16[2,512,128]{2,1,0:T(8,128)(2,1)S(1)} %get-tuple-element.203.refs_2_, ...), custom_call_target="tpu_custom_call" | custom-call | flops 1073741824 | bytes 1048576 | tf_op jit(solution)/shard_map/attention/pallas_call | solution.py:352
  166.4 4.4 %collective-permute-done.42.refs_4_ = bf16[512,256]{1,0:T(8,128)(2,1)S(1)} collective-permute-done((bf16[512,256]{1,0:T(8,128)(2,1)S(1)}, bf16[512,256]{1,0:T(8,128)(2,1)S(1)}, u32[]{:S(2)}, u32[]{:S(2)}) %collective-permute-start.42) | collective-permute-done | bytes 262176 | tf_op jit(solution)/shard_map/ppermute | solution.py:643
  175.7 5.4 %collective-permute-done.44.refs_8_ = bf16[512,256]{1,0:T(8,128)(2,1)S(1)} collective-permute-done((bf16[512,256]{1,0:T(8,128)(2,1)S(1)}, bf16[512,256]{1,0:T(8,128)(2,1)S(1)}, u32[]{:S(2)}, u32[]{:S(2)}) %collective-permute-start.44) | collective-permute-done | bytes 262176 | tf_op jit(solution)/shard_map/ppermute | solution.py:643
  182.5 4.2 %collective-permute-done.49.refs_5_ = bf16[512,256]{1,0:T(8,128)(2,1)S(1)} collective-permute-done((bf16[512,256]{1,0:T(8,128)(2,1)S(1)}, bf16[512,256]{1,0:T(8,128)(2,1)S(1)}, u32[]{:S(2)}, u32[]{:S(2)}) %collective-permute-start.49) | collective-permute-done | bytes 262176 | tf_op jit(solution)/shard_map/ppermute | solution.py:643
  188.8 3.0 %collective-permute-done.46.refs_0_ = bf16[512,256]{1,0:T(8,128)(2,1)S(1)} collective-permute-done((bf16[512,256]{1,0:T(8,128)(2,1)S(1)}, bf16[512,256]{1,0:T(8,128)(2,1)S(1)}, u32[]{:S(2)}, u32[]{:S(2)}) %collective-permute-start.46) | collective-permute-done | bytes 262176 | tf_op jit(solution)/shard_map/ppermute | solution.py:643
  192.5 5.0 %collective-permute-done.52.refs_9_ = bf16[512,256]{1,0:T(8,128)(2,1)S(1)} collective-permute-done((bf16[512,256]{1,0:T(8,128)(2,1)S(1)}, bf16[512,256]{1,0:T(8,128)(2,1)S(1)}, u32[]{:S(2)}, u32[]{:S(2)}) %collective-permute-start.52) | collective-permute-done | bytes 262176 | tf_op jit(solution)/shard_map/ppermute | solution.py:643
  203.6 3.0 %collective-permute-done.54.refs_1_ = bf16[512,256]{1,0:T(8,128)(2,1)S(1)} collective-permute-done((bf16[512,256]{1,0:T(8,128)(2,1)S(1)}, bf16[512,256]{1,0:T(8,128)(2,1)S(1)}, u32[]{:S(2)}, u32[]{:S(2)}) %collective-permute-start.54) | collective-permute-done | bytes 262176 | tf_op jit(solution)/shard_map/ppermute | solution.py:643
  207.9 2.8 %collective-permute-done.51.refs_0_ = bf16[512,256]{1,0:T(8,128)(2,1)S(1)} collective-permute-done((bf16[512,256]{1,0:T(8,128)(2,1)S(1)}, bf16[512,256]{1,0:T(8,128)(2,1)S(1)}, u32[]{:S(2)}, u32[]{:S(2)}) %collective-permute-start.51) | collective-permute-done | bytes 262176 | tf_op jit(solution)/shard_map/ppermute | solution.py:643
  210.7 3.3 %collective-permute-done.56.refs_1_ = bf16[512,256]{1,0:T(8,128)(2,1)S(1)} collective-permute-done((bf16[512,256]{1,0:T(8,128)(2,1)S(1)}, bf16[512,256]{1,0:T(8,128)(2,1)S(1)}, u32[]{:S(2)}, u32[]{:S(2)}) %collective-permute-start.56) | collective-permute-done | bytes 262176 | tf_op jit(solution)/shard_map/ppermute | solution.py:643
  215.0 3.2 %collective-permute-start.60 = (bf16[512,256]{1,0:T(8,128)(2,1)S(1)}, bf16[512,256]{1,0:T(8,128)(2,1)S(1)}, u32[]{:S(2)}, u32[]{:S(2)}) collective-permute-start(bf16[512,256]{1,0:T(8,128)(2,1)S(1)} %get-tuple-element.229), channel_id=1, source_target_pairs={{0,1},{1,0},{2,3},{3,2},{4,5},{5,4},{6,7},{7,6},{8,9},{9,8},{10,11... | collective-permute-start | bytes 786440 | tf_op jit(solution)/shard_map/ppermute | solution.py:54
  223.4 2.7 collective-permute-done.61.refs_1_
  226.1 3.3 %collective-permute-done.63.refs_3_ = bf16[256,256]{1,0:T(8,128)(2,1)S(1)} collective-permute-done((bf16[256,256]{1,0:T(8,128)(2,1)S(1)}, bf16[256,256]{1,0:T(8,128)(2,1)S(1)}, u32[]{:S(2)}, u32[]{:S(2)}) %collective-permute-start.63) | collective-permute-done | bytes 131104 | tf_op jit(solution)/shard_map/ppermute | solution.py:816
  231.1 5.4 %collective-permute-done.64.refs_4_ = bf16[128,512]{1,0:T(8,128)(2,1)S(1)} collective-permute-done((bf16[128,512]{1,0:T(8,128)(2,1)S(1)}, bf16[128,512]{1,0:T(8,128)(2,1)S(1)}, u32[]{:S(2)}, u32[]{:S(2)}) %collective-permute-start.64) | collective-permute-done | bytes 131104 | tf_op jit(solution)/shard_map/ppermute | solution.py:643
  243.0 2.6 collective-permute-done.72.refs_9_
  254.0 3.5 %collective-permute-done.77.refs_1_ = bf16[128,512]{1,0:T(8,128)(2,1)S(1)} collective-permute-done((bf16[128,512]{1,0:T(8,128)(2,1)S(1)}, bf16[128,512]{1,0:T(8,128)(2,1)S(1)}, u32[]{:S(2)}, u32[]{:S(2)}) %collective-permute-start.77) | collective-permute-done | bytes 131104 | tf_op jit(solution)/shard_map/ppermute | solution.py:643
  266.0 5.0 %collective-permute-start.82 = (f32[64,128]{1,0:T(8,128)S(1)}, f32[64,128]{1,0:T(8,128)S(1)}, u32[]{:S(2)}, u32[]{:S(2)}) collective-permute-start(f32[64,128]{1,0:T(8,128)S(1)} %fusion.25.own_a), channel_id=1, source_target_pairs={{0,1},{1,0},{2,3},{3,2},{4,5},{5,4},{6,7},{7,6},{8,9},{9,8},{10,11... | collective-permute-start | bytes 98312 | tf_op jit(solution)/shard_map/ppermute | solution.py:876
  (258 shorter events, 106.6 us)
Async XLA Ops:
  0.6 11.7 %collective-permute-start.3 = (bf16[4096,256]{1,0:T(8,128)(2,1)}, bf16[4096,256]{1,0:T(8,128)(2,1)}, u32[]{:S(2)}, u32[]{:S(2)}) collective-permute-start(bf16[4096,256]{1,0:T(8,128)(2,1)} %refs_5_.3), channel_id=1, source_target_pairs={{0,1},{1,0},{2,3},{3,2},{4,5},{5,4},{6,7},{7,6},{8,9},{9,8},{10,11... | collective-permute-start | bytes 6291464 | tf_op jit(solution)/shard_map/ppermute | solution.py:54
  0.8 11.6 %collective-permute-start.4 = (bf16[4096,256]{1,0:T(8,128)(2,1)}, bf16[4096,256]{1,0:T(8,128)(2,1)}, u32[]{:S(2)}, u32[]{:S(2)}) collective-permute-start(bf16[4096,256]{1,0:T(8,128)(2,1)} %refs_6_.1), channel_id=1, source_target_pairs={{0,1},{1,0},{2,3},{3,2},{4,5},{5,4},{6,7},{7,6},{8,9},{9,8},{10,11... | collective-permute-start | bytes 6291464 | tf_op jit(solution)/shard_map/ppermute | solution.py:54
  1.2 40.2 %collective-permute-start.9 = (bf16[4096,256]{1,0:T(8,128)(2,1)}, bf16[4096,256]{1,0:T(8,128)(2,1)}, u32[]{:S(2)}, u32[]{:S(2)}) collective-permute-start(bf16[4096,256]{1,0:T(8,128)(2,1)} %refs_7_.3), channel_id=1, source_target_pairs={{0,1},{1,0},{2,3},{3,2},{4,5},{5,4},{6,7},{7,6},{8,9},{9,8},{10,11... | collective-permute-start | bytes 6291464 | tf_op jit(solution)/shard_map/ppermute | solution.py:54
  1.3 40.1 %collective-permute-start.10 = (bf16[4096,256]{1,0:T(8,128)(2,1)}, bf16[4096,256]{1,0:T(8,128)(2,1)S(1)}, u32[]{:S(2)}, u32[]{:S(2)}) collective-permute-start(bf16[4096,256]{1,0:T(8,128)(2,1)} %param.25), channel_id=1, source_target_pairs={{0,1},{1,0},{2,3},{3,2},{4,5},{5,4},{6,7},{7,6},{8,9},{9,8},{10,11... | collective-permute-start | bytes 6291464 | tf_op jit(solution)/shard_map/ppermute | solution.py:54
  16.1 11.3 %collective-permute-start.8 = (bf16[4,256,256]{2,1,0:T(8,128)(2,1)}, bf16[4,256,256]{2,1,0:T(8,128)(2,1)}, u32[]{:S(2)}, u32[]{:S(2)}) collective-permute-start(bf16[4,256,256]{2,1,0:T(8,128)(2,1)} %get-tuple-element.133), channel_id=1, source_target_pairs={{0,2},{2,0},{1,3},{3,1},{4,6},{6,4},{5,7},{7,5},{8,10},{10,8},{9,1... | collective-permute-start | bytes 1572872 | tf_op jit(solution)/shard_map/ppermute | solution.py:643
  28.6 12.8 %collective-permute-start.11 = (bf16[2,256,256]{2,1,0:T(8,128)(2,1)S(1)}, bf16[2,256,256]{2,1,0:T(8,128)(2,1)S(1)}, u32[]{:S(2)}, u32[]{:S(2)}) collective-permute-start(bf16[2,256,256]{2,1,0:T(8,128)(2,1)S(1)} %pad_maximum_fusion.2), channel_id=1, source_target_pairs={{0,4},{4,8},{8,12},{12,0},{1,5},{5,9},{9,13},{13,1},{2,6},{6,10},{... | collective-permute-start | bytes 786440 | tf_op jit(solution)/shard_map/ppermute | solution.py:643
  29.9 12.4 %collective-permute-start.12 = (bf16[2,256,256]{2,1,0:T(8,128)(2,1)S(1)}, bf16[2,256,256]{2,1,0:T(8,128)(2,1)S(1)}, u32[]{:S(2)}, u32[]{:S(2)}) collective-permute-start(bf16[2,256,256]{2,1,0:T(8,128)(2,1)S(1)} %pad_maximum_fusion.3), channel_id=1, source_target_pairs={{0,12},{4,0},{8,4},{12,8},{1,13},{5,1},{9,5},{13,9},{2,14},{6,2},{... | collective-permute-start | bytes 786440 | tf_op jit(solution)/shard_map/ppermute | solution.py:643
  47.0 29.8 %collective-permute-start.30 = (bf16[6,256,256]{2,1,0:T(8,128)(2,1)S(1)}, bf16[6,256,256]{2,1,0:T(8,128)(2,1)}, u32[]{:S(2)}, u32[]{:S(2)}) collective-permute-start(bf16[6,256,256]{2,1,0:T(8,128)(2,1)S(1)} %constant_dynamic-update-slice_fusion.refs_10_.refs_14_.refs_18_.refs_22_.refs_4_.refs_2_), channel_id=1, source_target_pairs={{0,16},{16,0},{1,17},{17,1},{2,18},{18,2},{3,19},{19,3},{4,20},{20... | collective-permute-start | bytes 2359304 | tf_op jit(solution)/shard_map/ppermute | solution.py:643
  58.9 14.5 %collective-permute-start.16 = (bf16[272,512]{1,0:T(8,128)(2,1)S(1)}, bf16[272,512]{1,0:T(8,128)(2,1)S(1)}, u32[]{:S(2)}, u32[]{:S(2)}) collective-permute-start(bf16[272,512]{1,0:T(8,128)(2,1)S(1)} %collective-permute-done.14.refs_4_), channel_id=1, source_target_pairs={{0,4},{4,8},{8,12},{12,0},{1,5},{5,9},{9,13},{13,1},{2,6},{6,10},{... | collective-permute-start | bytes 835592 | tf_op jit(solution)/shard_map/ppermute | solution.py:643
  58.9 14.5 %collective-permute-start.17 = (bf16[272,512]{1,0:T(8,128)(2,1)S(1)}, bf16[272,512]{1,0:T(8,128)(2,1)S(1)}, u32[]{:S(2)}, u32[]{:S(2)}) collective-permute-start(bf16[272,512]{1,0:T(8,128)(2,1)S(1)} %collective-permute-done.14.refs_4_), channel_id=1, source_target_pairs={{0,2},{2,0},{1,3},{3,1},{4,6},{6,4},{5,7},{7,5},{8,10},{10,8},{9,1... | collective-permute-start | bytes 835592 | tf_op jit(solution)/shard_map/ppermute | solution.py:643
  59.6 13.8 %collective-permute-start.19 = (bf16[256,512]{1,0:T(8,128)(2,1)S(1)}, bf16[256,512]{1,0:T(8,128)(2,1)S(1)}, u32[]{:S(2)}, u32[]{:S(2)}) collective-permute-start(bf16[256,512]{1,0:T(8,128)(2,1)S(1)} %maximum_select_fusion.2.refs_1_), channel_id=1, source_target_pairs={{0,4},{4,8},{8,12},{12,0},{1,5},{5,9},{9,13},{13,1},{2,6},{6,10},{... | collective-permute-start | bytes 786440 | tf_op jit(solution)/shard_map/ppermute | solution.py:643
  59.7 13.7 %collective-permute-start.20 = (bf16[256,512]{1,0:T(8,128)(2,1)S(1)}, bf16[256,512]{1,0:T(8,128)(2,1)S(1)}, u32[]{:S(2)}, u32[]{:S(2)}) collective-permute-start(bf16[256,512]{1,0:T(8,128)(2,1)S(1)} %maximum_select_fusion.2.refs_1_), channel_id=1, source_target_pairs={{0,2},{2,0},{1,3},{3,1},{4,6},{6,4},{5,7},{7,5},{8,10},{10,8},{9,1... | collective-permute-start | bytes 786440 | tf_op jit(solution)/shard_map/ppermute | solution.py:643
  73.4 14.2 %collective-permute-start.21 = (bf16[272,512]{1,0:T(8,128)(2,1)S(1)}, bf16[272,512]{1,0:T(8,128)(2,1)}, u32[]{:S(2)}, u32[]{:S(2)}) collective-permute-start(bf16[272,512]{1,0:T(8,128)(2,1)S(1)} %collective-permute-done.16.refs_8_), channel_id=1, source_target_pairs={{0,4},{4,8},{8,12},{12,0},{1,5},{5,9},{9,13},{13,1},{2,6},{6,10},{... | collective-permute-start | bytes 835592 | tf_op jit(solution)/shard_map/ppermute | solution.py:643
  73.4 13.6 %collective-permute-start.23 = (bf16[256,512]{1,0:T(8,128)(2,1)S(1)}, bf16[256,512]{1,0:T(8,128)(2,1)}, u32[]{:S(2)}, u32[]{:S(2)}) collective-permute-start(bf16[256,512]{1,0:T(8,128)(2,1)S(1)} %collective-permute-done.19.refs_5_), channel_id=1, source_target_pairs={{0,4},{4,8},{8,12},{12,0},{1,5},{5,9},{9,13},{13,1},{2,6},{6,10},{... | collective-permute-start | bytes 786440 | tf_op jit(solution)/shard_map/ppermute | solution.py:643
  73.5 14.1 %collective-permute-start.24 = (bf16[256,512]{1,0:T(8,128)(2,1)S(1)}, bf16[256,512]{1,0:T(8,128)(2,1)S(1)}, u32[]{:S(2)}, u32[]{:S(2)}) collective-permute-start(bf16[256,512]{1,0:T(8,128)(2,1)S(1)} %collective-permute-done.19.refs_5_), channel_id=1, source_target_pairs={{0,2},{2,0},{1,3},{3,1},{4,6},{6,4},{5,7},{7,5},{8,10},{10,8},{9,1... | collective-permute-start | bytes 786440 | tf_op jit(solution)/shard_map/ppermute | solution.py:643
  74.1 49.9 %collective-permute-start.29 = (bf16[6,256,256]{2,1,0:T(8,128)(2,1)S(1)}, bf16[6,256,256]{2,1,0:T(8,128)(2,1)}, u32[]{:S(2)}, u32[]{:S(2)}) collective-permute-start(bf16[6,256,256]{2,1,0:T(8,128)(2,1)S(1)} %constant_dynamic-update-slice_fusion.refs_10_.refs_14_.refs_18_.refs_22_.refs_4_.refs_2_), channel_id=1, source_target_pairs={{0,1},{1,0},{2,3},{3,2},{4,5},{5,4},{6,7},{7,6},{8,9},{9,8},{10,11... | collective-permute-start | bytes 2359304 | tf_op jit(solution)/shard_map/ppermute | solution.py:54
  76.8 47.2 %collective-permute-start.31 = (bf16[6,256,256]{2,1,0:T(8,128)(2,1)}, bf16[6,256,256]{2,1,0:T(8,128)(2,1)}, u32[]{:S(2)}, u32[]{:S(2)}) collective-permute-start(bf16[6,256,256]{2,1,0:T(8,128)(2,1)} %collective-permute-done.30.refs_12_.refs_16_.refs_20_.refs_24_.refs_6_.refs_4_), channel_id=1, source_target_pairs={{0,1},{1,0},{2,3},{3,2},{4,5},{5,4},{6,7},{7,6},{8,9},{9,8},{10,11... | collective-permute-start | bytes 2359304 | tf_op jit(solution)/shard_map/ppermute | solution.py:54
  87.1 18.6 %collective-permute-start.22 = (bf16[272,512]{1,0:T(8,128)(2,1)S(1)}, bf16[272,512]{1,0:T(8,128)(2,1)S(1)}, u32[]{:S(2)}, u32[]{:S(2)}) collective-permute-start(bf16[272,512]{1,0:T(8,128)(2,1)S(1)} %collective-permute-done.16.refs_8_), channel_id=1, source_target_pairs={{0,2},{2,0},{1,3},{3,1},{4,6},{6,4},{5,7},{7,5},{8,10},{10,8},{9,1... | collective-permute-start | bytes 835592 | tf_op jit(solution)/shard_map/ppermute | solution.py:643
  87.6 19.3 %collective-permute-start.26 = (bf16[256,512]{1,0:T(8,128)(2,1)}, bf16[256,512]{1,0:T(8,128)(2,1)}, u32[]{:S(2)}, u32[]{:S(2)}) collective-permute-start(bf16[256,512]{1,0:T(8,128)(2,1)} %collective-permute-done.23.refs_9_), channel_id=1, source_target_pairs={{0,4},{4,8},{8,12},{12,0},{1,5},{5,9},{9,13},{13,1},{2,6},{6,10},{... | collective-permute-start | bytes 786440 | tf_op jit(solution)/shard_map/ppermute | solution.py:643
  87.6 19.3 %collective-permute-start.27 = (bf16[256,512]{1,0:T(8,128)(2,1)}, bf16[256,512]{1,0:T(8,128)(2,1)}, u32[]{:S(2)}, u32[]{:S(2)}) collective-permute-start(bf16[256,512]{1,0:T(8,128)(2,1)} %collective-permute-done.23.refs_9_), channel_id=1, source_target_pairs={{0,2},{2,0},{1,3},{3,1},{4,6},{6,4},{5,7},{7,5},{8,10},{10,8},{9,1... | collective-permute-start | bytes 786440 | tf_op jit(solution)/shard_map/ppermute | solution.py:643
  106.4 17.6 %collective-permute-start.25 = (bf16[272,512]{1,0:T(8,128)(2,1)}, bf16[272,512]{1,0:T(8,128)(2,1)}, u32[]{:S(2)}, u32[]{:S(2)}) collective-permute-start(bf16[272,512]{1,0:T(8,128)(2,1)} %collective-permute-done.21.refs_0_), channel_id=1, source_target_pairs={{0,2},{2,0},{1,3},{3,1},{4,6},{6,4},{5,7},{7,5},{8,10},{10,8},{9,1... | collective-permute-start | bytes 835592 | tf_op jit(solution)/shard_map/ppermute | solution.py:643
  106.9 17.0 %collective-permute-start.28 = (bf16[256,512]{1,0:T(8,128)(2,1)}, bf16[256,512]{1,0:T(8,128)(2,1)S(1)}, u32[]{:S(2)}, u32[]{:S(2)}) collective-permute-start(bf16[256,512]{1,0:T(8,128)(2,1)} %collective-permute-done.27.refs_3_), channel_id=1, source_target_pairs={{0,4},{4,8},{8,12},{12,0},{1,5},{5,9},{9,13},{13,1},{2,6},{6,10},{... | collective-permute-start | bytes 786440 | tf_op jit(solution)/shard_map/ppermute | solution.py:643
  130.4 11.4 %collective-permute-start.33 = (bf16[2,512,128]{2,1,0:T(8,128)(2,1)S(1)}, bf16[2,512,128]{2,1,0:T(8,128)(2,1)S(1)}, u32[]{:S(2)}, u32[]{:S(2)}) collective-permute-start(bf16[2,512,128]{2,1,0:T(8,128)(2,1)S(1)} %get-tuple-element.184), channel_id=1, source_target_pairs={{0,1},{1,0},{2,3},{3,2},{4,5},{5,4},{6,7},{7,6},{8,9},{9,8},{10,11... | collective-permute-start | bytes 786440 | tf_op jit(solution)/shard_map/ppermute | solution.py:54
  134.2 15.4 %collective-permute-start.35 = (bf16[2,512,128]{2,1,0:T(8,128)(2,1)S(1)}, bf16[2,512,128]{2,1,0:T(8,128)(2,1)S(1)}, u32[]{:S(2)}, u32[]{:S(2)}) collective-permute-start(bf16[2,512,128]{2,1,0:T(8,128)(2,1)S(1)} %get-tuple-element.184), channel_id=1, source_target_pairs={{0,17},{1,16},{16,1},{17,0},{2,19},{3,18},{18,3},{19,2},{4,21},{5,... | collective-permute-start | bytes 786440 | tf_op jit(solution)/shard_map/ppermute | solution.py:816
  135.3 12.3 %collective-permute-start.34 = (bf16[2,512,128]{2,1,0:T(8,128)(2,1)S(1)}, bf16[2,512,128]{2,1,0:T(8,128)(2,1)S(1)}, u32[]{:S(2)}, u32[]{:S(2)}) collective-permute-start(bf16[2,512,128]{2,1,0:T(8,128)(2,1)S(1)} %get-tuple-element.188.refs_2_), channel_id=1, source_target_pairs={{0,16},{1,17},{16,0},{17,1},{2,18},{3,19},{18,2},{19,3},{4,20},{5,... | collective-permute-start | bytes 786440 | tf_op jit(solution)/shard_map/ppermute | solution.py:816
  137.1 16.0 %collective-permute-start.36 = (bf16[2,256,256]{2,1,0:T(8,128)(2,1)S(1)}, bf16[2,256,256]{2,1,0:T(8,128)(2,1)S(1)}, u32[]{:S(2)}, u32[]{:S(2)}) collective-permute-start(bf16[2,256,256]{2,1,0:T(8,128)(2,1)S(1)} %pad_maximum_fusion.4), channel_id=1, source_target_pairs={{0,8},{4,12},{8,0},{12,4},{1,9},{5,13},{9,1},{13,5},{2,10},{6,14},... | collective-permute-start | bytes 786440 | tf_op jit(solution)/shard_map/ppermute | solution.py:643
  141.1 16.4 %collective-permute-start.38 = (bf16[2,512,128]{2,1,0:T(8,128)(2,1)S(1)}, bf16[2,512,128]{2,1,0:T(8,128)(2,1)S(1)}, u32[]{:S(2)}, u32[]{:S(2)}) collective-permute-start(bf16[2,512,128]{2,1,0:T(8,128)(2,1)S(1)} %get-tuple-element.196), channel_id=1, source_target_pairs={{0,1},{1,0},{2,3},{3,2},{4,5},{5,4},{6,7},{7,6},{8,9},{9,8},{10,11... | collective-permute-start | bytes 786440 | tf_op jit(solution)/shard_map/ppermute | solution.py:54
  141.8 15.8 %collective-permute-start.39 = (bf16[2,512,128]{2,1,0:T(8,128)(2,1)S(1)}, bf16[2,512,128]{2,1,0:T(8,128)(2,1)S(1)}, u32[]{:S(2)}, u32[]{:S(2)}) collective-permute-start(bf16[2,512,128]{2,1,0:T(8,128)(2,1)S(1)} %get-tuple-element.203.refs_2_), channel_id=1, source_target_pairs={{0,16},{1,17},{16,0},{17,1},{2,18},{3,19},{18,2},{19,3},{4,20},{5,... | collective-permute-start | bytes 786440 | tf_op jit(solution)/shard_map/ppermute | solution.py:816
  147.6 11.5 %collective-permute-start.40 = (bf16[2,512,128]{2,1,0:T(8,128)(2,1)S(1)}, bf16[2,512,128]{2,1,0:T(8,128)(2,1)S(1)}, u32[]{:S(2)}, u32[]{:S(2)}) collective-permute-start(bf16[2,512,128]{2,1,0:T(8,128)(2,1)S(1)} %get-tuple-element.196), channel_id=1, source_target_pairs={{0,17},{1,16},{16,1},{17,0},{2,19},{3,18},{18,3},{19,2},{4,21},{5,... | collective-permute-start | bytes 786440 | tf_op jit(solution)/shard_map/ppermute | solution.py:816
  174.7 12.1 %collective-permute-start.49 = (bf16[512,256]{1,0:T(8,128)(2,1)S(1)}, bf16[512,256]{1,0:T(8,128)(2,1)S(1)}, u32[]{:S(2)}, u32[]{:S(2)}) collective-permute-start(bf16[512,256]{1,0:T(8,128)(2,1)S(1)} %maximum_select_fusion.4.refs_1_), channel_id=1, source_target_pairs={{0,4},{4,8},{8,12},{12,0},{1,5},{5,9},{9,13},{13,1},{2,6},{6,10},{... | collective-permute-start | bytes 786440 | tf_op jit(solution)/shard_map/ppermute | solution.py:643
  174.8 12.1 %collective-permute-start.50 = (bf16[512,256]{1,0:T(8,128)(2,1)S(1)}, bf16[512,256]{1,0:T(8,128)(2,1)S(1)}, u32[]{:S(2)}, u32[]{:S(2)}) collective-permute-start(bf16[512,256]{1,0:T(8,128)(2,1)S(1)} %maximum_select_fusion.4.refs_1_), channel_id=1, source_target_pairs={{0,2},{2,0},{1,3},{3,1},{4,6},{6,4},{5,7},{7,5},{8,10},{10,8},{9,1... | collective-permute-start | bytes 786440 | tf_op jit(solution)/shard_map/ppermute | solution.py:643
  188.1 12.8 %collective-permute-start.58 = (bf16[2,256,256]{2,1,0:T(8,128)(2,1)S(1)}, bf16[2,256,256]{2,1,0:T(8,128)(2,1)S(1)}, u32[]{:S(2)}, u32[]{:S(2)}) collective-permute-start(bf16[2,256,256]{2,1,0:T(8,128)(2,1)S(1)} %collective-permute-done.36.refs_26_.refs_8_), channel_id=1, source_target_pairs={{0,16},{16,0},{1,17},{17,1},{2,18},{18,2},{3,19},{19,3},{4,20},{20... | collective-permute-start | bytes 786440 | tf_op jit(solution)/shard_map/ppermute | solution.py:643
  (84 other events, 1180.8 us)

commit v6 on v5

--- a/solution.py
+++ b/solution.py
@@ -54,15 +54,29 @@
     return lax.ppermute(values, "core", [(0, 1), (1, 0)])
 
 
+HELD = pl.BlockSpec(memory_space=pltpu.VMEM)
+
+
 GAIN_ROWS = 16
 TOP = 16
 
 
 def down_kernel(images, tiles, half, meta, *refs):
     lat_refs, refs = refs[:tiles], refs[tiles:]
-    conv_ref, patch_ref, own_text, par_text, gain_ref, first_ref, second_ref = refs[:7]
-    grid_rows, conv_wide, conv_bf16, windows, total = refs[7:]
+    conv_ref, patch_ref, own_text, par_text, gain_ref = refs[:5]
+    weight_refs, (first_ref, second_ref), held_refs = refs[5:11], refs[11:13], refs[13:19]
+    grid_rows, conv_wide, conv_bf16, windows, total, arrived = refs[19:]
     step = pl.program_id(0)
+    copies = [
+        pltpu.make_async_copy(weight, held, arrived.at[index])
+        for index, (weight, held) in enumerate(zip(weight_refs, held_refs))
+    ]
+
+    @pl.when(step == 0)
+    def _():
+        for copy in copies:
+            copy.start()
+
     group = images * SIDE
     ctx, core, tile, _ = split_meta(meta, images)
 
@@ -131,9 +145,11 @@
                 out_ref[side, :block, :] = jnp.where(source >= 0, picked, text).astype(BF16)
             gain = gain_ref[...].astype(F32)
             first_ref[side, block:, :] = jnp.broadcast_to(gain, (GAIN_ROWS, gain.shape[1])).astype(BF16)
-
-
-def down_stream(meta, pieces, conv, patch_in, text, gain, images):
+        for copy in copies:
+            copy.wait()
+
+
+def down_stream(meta, pieces, conv, patch_in, text, gain, weights, images):
     seq_rows, width = text.shape
     half = seq_rows // 2
     tiles = len(pieces)
@@ -153,21 +169,24 @@
                 pl.BlockSpec((1, half, width), lambda i, m: (m[core_at], 0, 0)),
                 pl.BlockSpec((1, half, width), lambda i, m: (1 - m[core_at], 0, 0)),
                 full((1, width)),
-            ],
-            out_specs=[full(first), full(second)],
+            ]
+            + [pl.BlockSpec(memory_space=pl.ANY)] * 6,
+            out_specs=[full(first), full(second)] + [HELD] * 6,
             scratch_shapes=[
                 pltpu.VMEM((images, WL * CIN // HD + 1, TOP + HL + 16, HD), F32),
                 pltpu.VMEM((TAPS, PATCH * CH), F32),
                 pltpu.VMEM((TAPS, PATCH * CH), BF16),
                 pltpu.VMEM((PATCH, count, TAPS), BF16),
                 pltpu.VMEM((count, width), F32),
+                pltpu.SemaphoreType.DMA((6,)),
             ],
         ),
-        out_shape=[jax.ShapeDtypeStruct(first, BF16), jax.ShapeDtypeStruct(second, BF16)],
+        out_shape=[jax.ShapeDtypeStruct(first, BF16), jax.ShapeDtypeStruct(second, BF16)]
+        + [pltpu.VMEM(w.shape, w.dtype) for w in weights],
         compiler_params=params(32),
         cost_estimate=cost(2 * count * PIX * CH * (256 + width), 4 << 20, count * PIX * CH),
         name="down_stream",
-    )(meta, *pieces, conv, patch_in, halves, halves, gain.reshape(1, width))
+    )(meta, *pieces, conv, patch_in, halves, halves, gain.reshape(1, width), *weights)
 
 
 def full(shape):
@@ -196,43 +215,29 @@
         acc_in, square_in = refs.pop(0), refs.pop(0)
     if last:
         head_gains = refs.pop(0)
-    fetched, arrived = refs.pop(-2), refs.pop(-1)
-    span, width = fetched.shape[2:]
-    half = 2 * x_refs[0][1].shape[0]
+    scaled_ref = refs.pop(-1)
+    half, span = scaled_ref.shape
+    width = weight_refs[0].shape[1]
     heads = width // HD
-
-    def fetch(index):
-        rows = pl.ds(pl.multiple_of(chip_of(meta, *layout, entries[index]) * span, span), span)
-        return [
-            pltpu.make_async_copy(
-                weight_refs[part].at[rows, :], fetched.at[index % 2, part], arrived.at[index % 2, part]
-            )
-            for part in range(6)
-        ]
-
-    copies = fetch(0)
-    for copy in copies:
-        copy.start()
     square = None if first else square_in[...]
     if last:
         acc, outs = [None] * 6, refs
     else:
         acc_out, square_out = refs
     for index in range(count):
-        following = fetch(index + 1) if index + 1 < count else []
-        for copy in following:
-            copy.start()
+        rows = pl.ds(pl.multiple_of(chip_of(meta, *layout, entries[index]) * span, span), span)
         gain = x_refs[index][0][half // 2 :, :][:1]
+        for part in range(2):
+            at = slice(part * half // 2, (part + 1) * half // 2)
+            scaled_ref[at, :] = (x_refs[index][part][: half // 2, :] * gain).astype(BF16)
         value = jnp.concatenate([x_refs[index][0][: half // 2, :], x_refs[index][1][...]], axis=0)
-        scaled = (value * gain).astype(BF16)
         value = value.astype(F32)
         value = value * value
         for part in range(span // HD):
             piece = value[:, part * HD : (part + 1) * HD]
             square = piece if square is None else square + piece
         for part in range(6):
-            copies[part].wait()
-            term = mxu(scaled, fetched[index % 2, part])
+            term = mxu(scaled_ref[...], weight_refs[part][rows, :])
             if index == 0 and not first:
                 term = term + acc_in[part]
             if last:
@@ -241,7 +246,6 @@
                 acc_out[part] = term
             else:
                 acc_out[part] += term
-        copies = following
     if not last:
         square_out[...] = square
         return
@@ -274,34 +278,28 @@
     inputs = [p for pieces in blocks for p in pieces]
     specs = [full(p.shape) for p in inputs]
     inputs += weights
-    specs += [pl.BlockSpec(memory_space=pl.ANY)] * 6
+    specs += [HELD] * 6
     if not first:
         inputs += list(state)
-        specs += [full(s.shape) for s in state]
+        specs += [HELD] * 2
     if last:
         inputs.append(head_gains)
         specs.append(full(head_gains.shape))
         kv, q = jax.ShapeDtypeStruct((2, half, HD), BF16), jax.ShapeDtypeStruct((half, HD), BF16)
         outs = ([kv] * heads + [q] * heads) * 2
     else:
-        outs = [
-            jax.ShapeDtypeStruct((6, half, width), F32),
-            jax.ShapeDtypeStruct((half, HD), F32),
-        ]
+        outs = [pltpu.VMEM((6, half, width), F32), pltpu.VMEM((half, HD), F32)]
     return pl.pallas_call(
         functools.partial(qkv_kernel, entries, layout, groups, first, last),
         grid_spec=pltpu.PrefetchScalarGridSpec(
             num_scalar_prefetch=1,
             grid=(1,),
             in_specs=specs,
-            out_specs=[full(o.shape) for o in outs],
-            scratch_shapes=[
-                pltpu.VMEM((2, 6, span, width), BF16),
-                pltpu.SemaphoreType.DMA((2, 6)),
-            ],
+            out_specs=[full(o.shape) if last else HELD for o in outs],
+            scratch_shapes=[pltpu.VMEM((half, span), BF16)],
         ),
         out_shape=outs,
-        compiler_params=params(40),
+        compiler_params=params(20),
         cost_estimate=cost(12 * count * half * span * width, (6 + 2 * count) << 20),
         name="qkv_last" if last else "qkv_step",
     )(meta, *inputs)
@@ -577,17 +575,18 @@
         out_ref[...] = spread(active, spread_ref)
 
 
-def up_step(blocks, entries, tiles, first_weights, second_weights, state, spread_weight):
+def up_step(blocks, entries, tiles, weights, state, spread_weight):
     span = blocks[0][0].shape[1]
-    halves, count = len(first_weights), len(blocks)
+    halves, count = len(weights), len(blocks)
     first, last = state is None, spread_weight is not None
     whole = lambda shape: pl.BlockSpec(shape, lambda i: (0,) * len(shape))
     inputs = [p for pieces in blocks for p in pieces]
     specs = [whole(p.shape) for p in inputs]
     for entry in entries:
-        apart = entry // 2 == tiles // 2
-        offset = entry % 2 if apart else entry - 2 * (entry // 2 > tiles // 2)
-        for sides in second_weights if apart else first_weights:
+        offset = entry - 2 * (entry // 2 > tiles // 2)
+        if entry // 2 == tiles // 2:
+            offset = 2 * tiles - 2 + entry % 2
+        for sides in weights:
             for weight in sides:
                 inputs.append(weight)
                 specs.append(pl.BlockSpec((1, span // 2, CH), lambda i, offset=offset: (offset, 0, 0)))
@@ -787,20 +786,20 @@
     pieces, received = lax.optimization_barrier((pieces, shift(sent, "mpo", 1)))
     up_blocks = [transpose_second(kept, received, step) for step in range(tiles) if 2 * step != tiles]
 
-    streams = down_stream(meta, pieces, conv, patch_in, text_embed, norm_gain, images)
-    streams, weights[2], out_par, up_blocks = lax.optimization_barrier(
-        (streams, weights[2], swap(out_weight), up_blocks)
-    )
+    weights += [key_weight, value_weight, query_weight]
+    streams = down_stream(meta, pieces, conv, patch_in, text_embed, norm_gain, weights, images)
+    streams, weights = streams[:2], streams[2:]
+    streams, up_blocks = lax.optimization_barrier((streams, up_blocks))
     others = [swap(s[1]) for s in streams]
-    weights += [key_weight, value_weight, query_weight]
+    others = lax.optimization_barrier(others)
 
     head_gains = jnp.stack([query_gain, key_gain])
 
     def project(blocks, entries, state, last):
         return qkv_step(meta, layout, blocks, entries, weights, state, head_gains if last else None)
 
-    state, up_first = gather_pair(
-        *[by_core(core, s[0], o, 1) for s, o in zip(streams, others)], None, project, transposed(up_blocks, halves)
+    state, out_par = gather_pair(
+        *[by_core(core, s[0], o, 1) for s, o in zip(streams, others)], None, project, swap(out_weight)
     )
     state, kept, received = lax.optimization_barrier((state, kept, received))
     up_block = transpose_second(kept, received, tiles // 2)
@@ -830,19 +829,19 @@
     attended, pieces = attend(0, pieces, pieces_of(1) if heads > 1 else None)
     if heads == 1:
         attended, second = attended[: half // 2], attended[half // 2 :]
-        extras = transposed([up_block], halves)
+        extras = transposed(up_blocks + [up_block], halves)
     else:
         extras = None
 
         def second(token):
-            result, (block, _) = attend(1, pieces, (up_block, token))
-            return result, transposed([block], halves)
+            result, (up, _) = attend(1, pieces, (up_blocks + [up_block], token))
+            return result, transposed(up, halves)
 
     def project_out(blocks, entries, state, last):
         return out_step(meta, layout, blocks, entries, (out_weight, out_par), state, last)
 
     state = [jnp.stack([s[0], o]) for s, o in zip(streams, others)]
-    state, up_second = gather_pair(attended, second, state, project_out, extras)
+    state, up_weights = gather_pair(attended, second, state, project_out, extras)
     out_own, out_send = state
     out_other = swap(out_send)
     layer_out = by_core(core, out_own, out_other, 0)
@@ -858,7 +857,7 @@
     spread_weight = spread_weights(up_conv, pixels)
 
     def project_up(blocks, entries, state, last):
-        return up_step(blocks, entries, tiles, up_first, up_second, state, spread_weight if last else None)
+        return up_step(blocks, entries, tiles, up_weights, state, spread_weight if last else None)
 
     state, _ = gather_pair(*merge_picks(own_parts, par_parts), None, project_up)
 

time: 276 us -> 270 us (0.978)
  Pallas kernels: 66.3 us -> 47.2 us
  local copies, waits for them, and re-layouts: 16.2 us -> 24.3 us
  starting transfers between devices: 74.1 us -> 76.9 us
    pallas_call x3, Pallas kernels: 33 us -> 13 us  [qkv_step(): pl.pallas_call(functools.partial(qkv_kernel, entries, layout, groups, fir...]
    unnamed x67 -> x90, local copies, waits for them, and re-layouts: 11.9 us -> 19.4 us
    pallas_call x3, Pallas kernels: 4.31 us -> 7.57 us  [out_step(): pl.pallas_call(functools.partial(out_kernel, count, heads, first, last),...]
    ppermute x56 -> x55, waiting for transfers between devices: 95.6 us -> 93.5 us  [shift(): lax.ppermute(values, axis, [(i, (i + step) % count) for i in range(count)])]
    ppermute x19 -> x17, starting transfers between devices: 19.5 us -> 20.7 us  [swap(): return lax.ppermute(values, 'core', [(0, 1), (1, 0)])]
    ppermute x56 -> x55, starting transfers between devices: 42.2 us -> 42.8 us  [shift(): lax.ppermute(values, axis, [(i, (i + step) % count) for i in range(count)])]
  transfers between devices with their start and end apart: 84 -> 81, of which waited for: 38 -> 36; matrix products, arithmetic and copies ran while one was open for 3% -> 4% of each run, Pallas kernels for 20% -> 14%
where the time goes in v6:
time: 270 us
  waiting for transfers between devices  114 us (42%)
  starting transfers between devices  76.9 us (28%)
  Pallas kernels  47.2 us (17%)
  local copies, waits for them, and re-layouts  24.3 us (9%)
  other arithmetic  5.41 us (2%)
    ppermute x55, waiting for transfers between devices, shift(): lax.ppermute(values, axis, [(i, (i + step) % count) for i in range(count)])  93.5 us
    ppermute x55, starting transfers between devices, shift(): lax.ppermute(values, axis, [(i, (i + step) % count) for i in range(count)])  42.8 us
    ppermute x17, starting transfers between devices, swap(): return lax.ppermute(values, 'core', [(0, 1), (1, 0)])  20.7 us
    unnamed x90, local copies, waits for them, and re-layouts  19.4 us
    ppermute x6, waiting for transfers between devices, shifted(): return lax.ppermute(values, ('ctx', 'core'), pairs)  15 us
    pallas_call x3, Pallas kernels, qkv_step(): pl.pallas_call(functools.partial(qkv_kernel, entries, layout, groups, fir...  13 us
    pallas_call x1, Pallas kernels, down_stream(): pl.pallas_call(functools.partial(down_kernel, images, tiles, half), grid_...  9.47 us
    pallas_call x2, Pallas kernels, attention(): pl.pallas_call(functools.partial(attention_kernel, images, len(pieces), h...  8.92 us
  transfers between devices with their start and end apart: 81, of which 36 were waited for; matrix products, arithmetic and copies ran while one was open for 4% of the time, Pallas kernels for 14%

profile of v6, /device:TPU:1, one launch (start us, length us, event | category | flops | bytes accessed | tf_op | source)
XLA Modules:
  0.0 269.7 jit_solution(13379482336959109171)
XLA Ops:
  19.8 3.4 %collective-permute-start.28 = (bf16[4096,256]{1,0:T(8,128)(2,1)S(1)}, bf16[4096,256]{1,0:T(8,128)(2,1)}, u32[]{:S(2)}, u32[]{:S(2)}) collective-permute-start(bf16[4096,256]{1,0:T(8,128)(2,1)S(1)} %copy-done.1), channel_id=1, source_target_pairs={{0,1},{1,0},{2,3},{3,2},{4,5},{5,4},{6,7},{7,6},{8,9},{9,8},{10,11... | collective-permute-start | bytes 6291464 | tf_op jit(solution)/shard_map/ppermute | solution.py:54
  30.3 9.5 %down_stream.1 = (bf16[2,272,256]{2,1,0:T(8,128)(2,1)S(1)}, bf16[2,256,256]{2,1,0:T(8,128)(2,1)S(1)}, bf16[4096,256]{1,0:T(8,128)(2,1)S(1)}, bf16[4096,256]{1,0:...) custom-call(s32[16]{0:T(128)S(1)} %concatenate.64.meta, ...), custom_call_target="tpu_custom_call" | custom-call | flops 4294967296 | bytes 4194304 | tf_op jit(solution)/shard_map/down_stream/pallas_call | solution.py:160
  49.9 7.0 %collective-permute-done.14.refs_4_ = bf16[272,512]{1,0:T(8,128)(2,1)S(1)} collective-permute-done((bf16[272,512]{1,0:T(8,128)(2,1)S(1)}, bf16[272,512]{1,0:T(8,128)(2,1)S(1)}, u32[]{:S(2)}, u32[]{:S(2)}) %collective-permute-start.14) | collective-permute-done | bytes 278560 | tf_op jit(solution)/shard_map/ppermute | solution.py:642
  58.4 4.2 %collective-permute-done.18.refs_5_ = bf16[256,512]{1,0:T(8,128)(2,1)S(1)} collective-permute-done((bf16[256,512]{1,0:T(8,128)(2,1)S(1)}, bf16[256,512]{1,0:T(8,128)(2,1)S(1)}, u32[]{:S(2)}, u32[]{:S(2)}) %collective-permute-start.18) | collective-permute-done | bytes 262176 | tf_op jit(solution)/shard_map/ppermute | solution.py:642
  64.0 4.5 %collective-permute-done.16.refs_8_ = bf16[272,512]{1,0:T(8,128)(2,1)S(1)} collective-permute-done((bf16[272,512]{1,0:T(8,128)(2,1)S(1)}, bf16[272,512]{1,0:T(8,128)(2,1)S(1)}, u32[]{:S(2)}, u32[]{:S(2)}) %collective-permute-start.16) | collective-permute-done | bytes 278560 | tf_op jit(solution)/shard_map/ppermute | solution.py:642
  70.1 4.2 %collective-permute-done.22.refs_9_ = bf16[256,512]{1,0:T(8,128)(2,1)} collective-permute-done((bf16[256,512]{1,0:T(8,128)(2,1)S(1)}, bf16[256,512]{1,0:T(8,128)(2,1)}, u32[]{:S(2)}, u32[]{:S(2)}) %collective-permute-start.22) | collective-permute-done | bytes 262176 | tf_op jit(solution)/shard_map/ppermute | solution.py:642
  75.7 6.5 %qkv_step.2 = (f32[6,512,256]{2,1,0:T(8,128)S(1)}, f32[512,128]{1,0:T(8,128)S(1)}) custom-call(s32[16]{0:T(128)S(1)} %concatenate.64.meta, bf16[272,512]{1,0:T(8,128)(2,1)S(1)} %maximum_select_fusion.1.refs_0_, bf16[256,512]{1,0:T(8,128)(2,1)S(1)} %maximum_select_fusion.2.refs_1_, bf16[272,512]{1,0:T(8,128)(2,1)S(1)} %collective-permute-done.15.refs_2_, ...), custom_call_target="tpu_custom_call" | custom-call | flops 4026531840 | bytes 16777216 | tf_op jit(solution)/shard_map/qkv_step/pallas_call | solution.py:292
  98.3 3.8 %qkv_step.3 = (f32[6,512,256]{2,1,0:T(8,128)S(1)}, f32[512,128]{1,0:T(8,128)S(1)}) custom-call(s32[16]{0:T(128)S(1)} %concatenate.64.meta, bf16[272,512]{1,0:T(8,128)(2,1)S(1)} %collective-permute-done.20.refs_0_, bf16[256,512]{1,0:T(8,128)(2,1)} %collective-permute-done.25.refs_1_, bf16[272,512]{1,0:T(8,128)(2,1)S(1)} %collective-permute-done.21.refs_2_, ...), custom_call_target="tpu_custom_call" | custom-call | flops 1610612736 | bytes 10485760 | tf_op jit(solution)/shard_map/qkv_step/pallas_call | solution.py:292
  102.1 2.7 %qkv_last.1 = (bf16[2,512,128]{2,1,0:T(8,128)(2,1)S(1)}, bf16[2,512,128]{2,1,0:T(8,128)(2,1)S(1)}, bf16[512,128]{1,0:T(8,128)(2,1)S(1)}, bf16[512,128]{1,0:T(8,1...) custom-call(s32[16]{0:T(128)S(1)} %concatenate.64.meta, ...), custom_call_target="tpu_custom_call" | custom-call | flops 805306368 | bytes 8388608 | tf_op jit(solution)/shard_map/qkv_last/pallas_call | solution.py:292
  108.4 3.2 %collective-permute-start.30 = (bf16[2,512,128]{2,1,0:T(8,128)(2,1)S(1)}, bf16[2,512,128]{2,1,0:T(8,128)(2,1)S(1)}, u32[]{:S(2)}, u32[]{:S(2)}) collective-permute-start(bf16[2,512,128]{2,1,0:T(8,128)(2,1)S(1)} %get-tuple-element.194), channel_id=1, source_target_pairs={{0,1},{1,0},{2,3},{3,2},{4,5},{5,4},{6,7},{7,6},{8,9},{9,8},{10,11... | collective-permute-start | bytes 786440 | tf_op jit(solution)/shard_map/ppermute | solution.py:54
  113.8 6.2 %collective-permute-done.33 = bf16[2,256,256]{2,1,0:T(8,128)(2,1)S(1)} collective-permute-done((bf16[2,256,256]{2,1,0:T(8,128)(2,1)S(1)}, bf16[2,256,256]{2,1,0:T(8,128)(2,1)S(1)}, u32[]{:S(2)}, u32[]{:S(2)}) %collective-permute-start.33) | collective-permute-done | bytes 262176 | tf_op jit(solution)/shard_map/ppermute | solution.py:642
  122.9 3.3 %collective-permute-done.32.refs_5_ = bf16[2,512,128]{2,1,0:T(8,128)(2,1)S(1)} collective-permute-done((bf16[2,512,128]{2,1,0:T(8,128)(2,1)S(1)}, bf16[2,512,128]{2,1,0:T(8,128)(2,1)S(1)}, u32[]{:S(2)}, u32[]{:S(2)}) %collective-permute-start.32) | collective-permute-done | bytes 262176 | tf_op jit(solution)/shard_map/ppermute | solution.py:815
  126.2 4.4 %attention.2 = (bf16[512,128]{1,0:T(8,128)(2,1)S(1)}, bf16[512,128]{1,0:T(8,128)(2,1)S(1)}) custom-call(s32[16]{0:T(128)S(1)} %concatenate.64.meta, bf16[512,128]{1,0:T(8,128)(2,1)S(1)} %get-tuple-element.191.refs_0_, bf16[512,128]{1,0:T(8,128)(2,1)S(1)} %collective-permute-done.29.refs_1_, bf16[2,512,128]{2,1,0:T(8,128)(2,1)S(1)} %get-tuple-element.198.refs_2_, ...), custom_call_target="tpu_custom_call" | custom-call | flops 1073741824 | bytes 1048576 | tf_op jit(solution)/shard_map/attention/pallas_call | solution.py:350
  130.7 5.8 %collective-permute-done.37.refs_5_ = bf16[2,512,128]{2,1,0:T(8,128)(2,1)S(1)} collective-permute-done((bf16[2,512,128]{2,1,0:T(8,128)(2,1)S(1)}, bf16[2,512,128]{2,1,0:T(8,128)(2,1)S(1)}, u32[]{:S(2)}, u32[]{:S(2)}) %collective-permute-start.37) | collective-permute-done | bytes 262176 | tf_op jit(solution)/shard_map/ppermute | solution.py:815
  139.5 4.5 %attention.3 = (bf16[512,128]{1,0:T(8,128)(2,1)S(1)}, bf16[512,128]{1,0:T(8,128)(2,1)S(1)}) custom-call(s32[16]{0:T(128)S(1)} %concatenate.64.meta, bf16[512,128]{1,0:T(8,128)(2,1)S(1)} %get-tuple-element.211.refs_0_, bf16[512,128]{1,0:T(8,128)(2,1)S(1)} %collective-permute-done.34.refs_1_, bf16[2,512,128]{2,1,0:T(8,128)(2,1)S(1)} %get-tuple-element.213.refs_2_, ...), custom_call_target="tpu_custom_call" | custom-call | flops 1073741824 | bytes 1048576 | tf_op jit(solution)/shard_map/attention/pallas_call | solution.py:350
  144.0 3.5 %collective-permute-done.39.refs_4_ = bf16[512,256]{1,0:T(8,128)(2,1)S(1)} collective-permute-done((bf16[512,256]{1,0:T(8,128)(2,1)S(1)}, bf16[512,256]{1,0:T(8,128)(2,1)S(1)}, u32[]{:S(2)}, u32[]{:S(2)}) %collective-permute-start.39) | collective-permute-done | bytes 262176 | tf_op jit(solution)/shard_map/ppermute | solution.py:642
  153.4 4.1 %collective-permute-done.41.refs_8_ = bf16[512,256]{1,0:T(8,128)(2,1)S(1)} collective-permute-done((bf16[512,256]{1,0:T(8,128)(2,1)S(1)}, bf16[512,256]{1,0:T(8,128)(2,1)S(1)}, u32[]{:S(2)}, u32[]{:S(2)}) %collective-permute-start.41) | collective-permute-done | bytes 262176 | tf_op jit(solution)/shard_map/ppermute | solution.py:642
  157.5 3.6 %collective-permute-start.54 = (bf16[8,256,256]{2,1,0:T(8,128)(2,1)S(1)}, bf16[8,256,256]{2,1,0:T(8,128)(2,1)S(1)}, u32[]{:S(2)}, u32[]{:S(2)}) collective-permute-start(bf16[8,256,256]{2,1,0:T(8,128)(2,1)S(1)} %constant_dynamic-update-slice_fusion.refs_10_.refs_14_.refs_18_.refs_22_.refs_26_.refs_4_.refs_8_., ...), channel_id=1, source_target_pairs={{0,1},{1,0},{2,3},{3,2},{4,5},{5,4},{6,7},{7,6},{8,9},{9,8},{10,11... | collective-permute-start | bytes 3145736 | tf_op jit(solution)/shard_map/ppermute | solution.py:54
  161.1 10.3 %collective-permute-done.55.refs_12_.refs_16_.refs_20_.refs_24_.refs_28_.refs_6_.refs_10_.refs_4_ = bf16[8,256,256]{2,1,0:T(8,128)(2,1)S(1)} collective-permute-done((bf16[8,256,256]{2,1,0:T(8,128)(2,1)S(1)}, bf16[8,256,256]{2,1,0:T(8,128)(2,1)S(1)}, u32[]{:S(2)}, u32[]{:S(2)}) %collective-permute-start.55) | collective-permute-done | bytes 1048608 | tf_op jit(solution)/shard_map/ppermute | solution.py:642
  174.9 6.3 %collective-permute-done.44.refs_2_ = bf16[512,256]{1,0:T(8,128)(2,1)S(1)} collective-permute-done((bf16[512,256]{1,0:T(8,128)(2,1)S(1)}, bf16[512,256]{1,0:T(8,128)(2,1)S(1)}, u32[]{:S(2)}, u32[]{:S(2)}) %collective-permute-start.44) | collective-permute-done | bytes 262176 | tf_op jit(solution)/shard_map/ppermute | solution.py:642
  181.2 2.9 %collective-permute-done.49.refs_9_ = bf16[512,256]{1,0:T(8,128)(2,1)S(1)} collective-permute-done((bf16[512,256]{1,0:T(8,128)(2,1)S(1)}, bf16[512,256]{1,0:T(8,128)(2,1)S(1)}, u32[]{:S(2)}, u32[]{:S(2)}) %collective-permute-start.49) | collective-permute-done | bytes 262176 | tf_op jit(solution)/shard_map/ppermute | solution.py:642
  188.4 3.3 %out_step.2.refs_8_ = f32[2,512,256]{2,1,0:T(8,128)S(1)} custom-call(s32[16]{0:T(128)S(1)} %concatenate.64.meta, bf16[512,256]{1,0:T(8,128)(2,1)S(1)} %maximum_select_fusion.3.refs_0_, bf16[512,256]{1,0:T(8,128)(2,1)S(1)} %maximum_select_fusion.4.refs_1_, bf16[512,256]{1,0:T(8,128)(2,1)S(1)} %collective-permute-done.40.refs_2_, ...), custom_call_target="tpu_custom_call" | custom-call | flops 1342177280 | bytes 7340032 | tf_op jit(solution)/shard_map/out_step/pallas_call | solution.py:420
  191.8 3.8 %collective-permute-done.51.refs_1_ = bf16[512,256]{1,0:T(8,128)(2,1)S(1)} collective-permute-done((bf16[512,256]{1,0:T(8,128)(2,1)S(1)}, bf16[512,256]{1,0:T(8,128)(2,1)S(1)}, u32[]{:S(2)}, u32[]{:S(2)}) %collective-permute-start.51) | collective-permute-done | bytes 262176 | tf_op jit(solution)/shard_map/ppermute | solution.py:642
  199.4 4.0 %collective-permute-done.53.refs_1_ = bf16[512,256]{1,0:T(8,128)(2,1)S(1)} collective-permute-done((bf16[512,256]{1,0:T(8,128)(2,1)S(1)}, bf16[512,256]{1,0:T(8,128)(2,1)S(1)}, u32[]{:S(2)}, u32[]{:S(2)}) %collective-permute-start.53) | collective-permute-done | bytes 262176 | tf_op jit(solution)/shard_map/ppermute | solution.py:642
  205.4 2.7 %collective-permute-start.57 = (bf16[512,256]{1,0:T(8,128)(2,1)S(1)}, bf16[512,256]{1,0:T(8,128)(2,1)S(1)}, u32[]{:S(2)}, u32[]{:S(2)}) collective-permute-start(bf16[512,256]{1,0:T(8,128)(2,1)S(1)} %get-tuple-element.245), channel_id=1, source_target_pairs={{0,1},{1,0},{2,3},{3,2},{4,5},{5,4},{6,7},{7,6},{8,9},{9,8},{10,11... | collective-permute-start | bytes 786440 | tf_op jit(solution)/shard_map/ppermute | solution.py:54
  216.0 3.3 %collective-permute-done.60.refs_3_ = bf16[256,256]{1,0:T(8,128)(2,1)S(1)} collective-permute-done((bf16[256,256]{1,0:T(8,128)(2,1)S(1)}, bf16[256,256]{1,0:T(8,128)(2,1)S(1)}, u32[]{:S(2)}, u32[]{:S(2)}) %collective-permute-start.60) | collective-permute-done | bytes 131104 | tf_op jit(solution)/shard_map/ppermute | solution.py:815
  221.1 5.5 %collective-permute-done.61.refs_4_ = bf16[128,512]{1,0:T(8,128)(2,1)} collective-permute-done((bf16[128,512]{1,0:T(8,128)(2,1)S(1)}, bf16[128,512]{1,0:T(8,128)(2,1)}, u32[]{:S(2)}, u32[]{:S(2)}) %collective-permute-start.61) | collective-permute-done | bytes 131104 | tf_op jit(solution)/shard_map/ppermute | solution.py:642
  226.6 2.8 %collective-permute-done.65.refs_5_ = bf16[128,512]{1,0:T(8,128)(2,1)} collective-permute-done((bf16[128,512]{1,0:T(8,128)(2,1)S(1)}, bf16[128,512]{1,0:T(8,128)(2,1)}, u32[]{:S(2)}, u32[]{:S(2)}) %collective-permute-start.65) | collective-permute-done | bytes 131104 | tf_op jit(solution)/shard_map/ppermute | solution.py:642
  231.0 7.5 %collective-permute-done.63.refs_8_ = bf16[128,512]{1,0:T(8,128)(2,1)S(1)} collective-permute-done((bf16[128,512]{1,0:T(8,128)(2,1)}, bf16[128,512]{1,0:T(8,128)(2,1)S(1)}, u32[]{:S(2)}, u32[]{:S(2)}) %collective-permute-start.63) | collective-permute-done | bytes 131104 | tf_op jit(solution)/shard_map/ppermute | solution.py:642
  247.8 4.4 %collective-permute-done.74.refs_1_ = bf16[128,512]{1,0:T(8,128)(2,1)S(1)} collective-permute-done((bf16[128,512]{1,0:T(8,128)(2,1)S(1)}, bf16[128,512]{1,0:T(8,128)(2,1)S(1)}, u32[]{:S(2)}, u32[]{:S(2)}) %collective-permute-start.74) | collective-permute-done | bytes 131104 | tf_op jit(solution)/shard_map/ppermute | solution.py:642
  253.4 3.2 %collective-permute-start.77 = (f32[64,128]{1,0:T(8,128)S(1)}, f32[64,128]{1,0:T(8,128)S(1)}, u32[]{:S(2)}, u32[]{:S(2)}) collective-permute-start(f32[64,128]{1,0:T(8,128)S(1)} %get-tuple-element.285), channel_id=1, source_target_pairs={{0,12},{4,0},{8,4},{12,8},{1,13},{5,1},{9,5},{13,9},{2,14},{6,2},{... | collective-permute-start | bytes 98312 | tf_op jit(solution)/shard_map/ppermute | solution.py:642
  259.6 5.3 %collective-permute-start.79 = (f32[64,128]{1,0:T(8,128)S(1)}, f32[64,128]{1,0:T(8,128)S(1)}, u32[]{:S(2)}, u32[]{:S(2)}) collective-permute-start(f32[64,128]{1,0:T(8,128)S(1)} %fusion.25.own_a), channel_id=1, source_target_pairs={{0,1},{1,0},{2,3},{3,2},{4,5},{5,4},{6,7},{7,6},{8,9},{9,8},{10,11... | collective-permute-start | bytes 98312 | tf_op jit(solution)/shard_map/ppermute | solution.py:875
  (275 shorter events, 118.4 us)
Async XLA Ops:
  1.2 29.1 %collective-permute-start.9 = (bf16[4096,256]{1,0:T(8,128)(2,1)}, bf16[4096,256]{1,0:T(8,128)(2,1)}, u32[]{:S(2)}, u32[]{:S(2)}) collective-permute-start(bf16[4096,256]{1,0:T(8,128)(2,1)} %refs_14_.1), channel_id=1, source_target_pairs={{0,1},{1,0},{2,3},{3,2},{4,5},{5,4},{6,7},{7,6},{8,9},{9,8},{10,11... | collective-permute-start | bytes 6291464 | tf_op jit(solution)/shard_map/ppermute | solution.py:54
  13.3 12.0 %collective-permute-start.8 = (bf16[4,256,256]{2,1,0:T(8,128)(2,1)}, bf16[4,256,256]{2,1,0:T(8,128)(2,1)}, u32[]{:S(2)}, u32[]{:S(2)}) collective-permute-start(bf16[4,256,256]{2,1,0:T(8,128)(2,1)} %get-tuple-element.139), channel_id=1, source_target_pairs={{0,2},{2,0},{1,3},{3,1},{4,6},{6,4},{5,7},{7,5},{8,10},{10,8},{9,1... | collective-permute-start | bytes 1572872 | tf_op jit(solution)/shard_map/ppermute | solution.py:642
  19.8 82.2 %collective-permute-start.28 = (bf16[4096,256]{1,0:T(8,128)(2,1)S(1)}, bf16[4096,256]{1,0:T(8,128)(2,1)}, u32[]{:S(2)}, u32[]{:S(2)}) collective-permute-start(bf16[4096,256]{1,0:T(8,128)(2,1)S(1)} %copy-done.1), channel_id=1, source_target_pairs={{0,1},{1,0},{2,3},{3,2},{4,5},{5,4},{6,7},{7,6},{8,9},{9,8},{10,11... | collective-permute-start | bytes 6291464 | tf_op jit(solution)/shard_map/ppermute | solution.py:54
  26.4 14.3 %collective-permute-start.10 = (bf16[2,256,256]{2,1,0:T(8,128)(2,1)S(1)}, bf16[2,256,256]{2,1,0:T(8,128)(2,1)S(1)}, u32[]{:S(2)}, u32[]{:S(2)}) collective-permute-start(bf16[2,256,256]{2,1,0:T(8,128)(2,1)S(1)} %pad_maximum_fusion.2), channel_id=1, source_target_pairs={{0,4},{4,8},{8,12},{12,0},{1,5},{5,9},{9,13},{13,1},{2,6},{6,10},{... | collective-permute-start | bytes 786440 | tf_op jit(solution)/shard_map/ppermute | solution.py:642
  28.2 13.3 %collective-permute-start.11 = (bf16[2,256,256]{2,1,0:T(8,128)(2,1)S(1)}, bf16[2,256,256]{2,1,0:T(8,128)(2,1)S(1)}, u32[]{:S(2)}, u32[]{:S(2)}) collective-permute-start(bf16[2,256,256]{2,1,0:T(8,128)(2,1)S(1)} %pad_maximum_fusion.3), channel_id=1, source_target_pairs={{0,12},{4,0},{8,4},{12,8},{1,13},{5,1},{9,5},{13,9},{2,14},{6,2},{... | collective-permute-start | bytes 786440 | tf_op jit(solution)/shard_map/ppermute | solution.py:642
  48.9 13.7 %collective-permute-start.18 = (bf16[256,512]{1,0:T(8,128)(2,1)S(1)}, bf16[256,512]{1,0:T(8,128)(2,1)S(1)}, u32[]{:S(2)}, u32[]{:S(2)}) collective-permute-start(bf16[256,512]{1,0:T(8,128)(2,1)S(1)} %maximum_select_fusion.2.refs_1_), channel_id=1, source_target_pairs={{0,4},{4,8},{8,12},{12,0},{1,5},{5,9},{9,13},{13,1},{2,6},{6,10},{... | collective-permute-start | bytes 786440 | tf_op jit(solution)/shard_map/ppermute | solution.py:642
  49.6 12.9 %collective-permute-start.19 = (bf16[256,512]{1,0:T(8,128)(2,1)S(1)}, bf16[256,512]{1,0:T(8,128)(2,1)S(1)}, u32[]{:S(2)}, u32[]{:S(2)}) collective-permute-start(bf16[256,512]{1,0:T(8,128)(2,1)S(1)} %maximum_select_fusion.2.refs_1_), channel_id=1, source_target_pairs={{0,2},{2,0},{1,3},{3,1},{4,6},{6,4},{5,7},{7,5},{8,10},{10,8},{9,1... | collective-permute-start | bytes 786440 | tf_op jit(solution)/shard_map/ppermute | solution.py:642
  56.9 11.6 %collective-permute-start.16 = (bf16[272,512]{1,0:T(8,128)(2,1)S(1)}, bf16[272,512]{1,0:T(8,128)(2,1)S(1)}, u32[]{:S(2)}, u32[]{:S(2)}) collective-permute-start(bf16[272,512]{1,0:T(8,128)(2,1)S(1)} %collective-permute-done.14.refs_4_), channel_id=1, source_target_pairs={{0,4},{4,8},{8,12},{12,0},{1,5},{5,9},{9,13},{13,1},{2,6},{6,10},{... | collective-permute-start | bytes 835592 | tf_op jit(solution)/shard_map/ppermute | solution.py:642
  56.9 11.6 %collective-permute-start.17 = (bf16[272,512]{1,0:T(8,128)(2,1)S(1)}, bf16[272,512]{1,0:T(8,128)(2,1)S(1)}, u32[]{:S(2)}, u32[]{:S(2)}) collective-permute-start(bf16[272,512]{1,0:T(8,128)(2,1)S(1)} %collective-permute-done.14.refs_4_), channel_id=1, source_target_pairs={{0,2},{2,0},{1,3},{3,1},{4,6},{6,4},{5,7},{7,5},{8,10},{10,8},{9,1... | collective-permute-start | bytes 835592 | tf_op jit(solution)/shard_map/ppermute | solution.py:642
  62.6 11.7 %collective-permute-start.22 = (bf16[256,512]{1,0:T(8,128)(2,1)S(1)}, bf16[256,512]{1,0:T(8,128)(2,1)}, u32[]{:S(2)}, u32[]{:S(2)}) collective-permute-start(bf16[256,512]{1,0:T(8,128)(2,1)S(1)} %collective-permute-done.18.refs_5_), channel_id=1, source_target_pairs={{0,4},{4,8},{8,12},{12,0},{1,5},{5,9},{9,13},{13,1},{2,6},{6,10},{... | collective-permute-start | bytes 786440 | tf_op jit(solution)/shard_map/ppermute | solution.py:642
  62.6 11.7 %collective-permute-start.23 = (bf16[256,512]{1,0:T(8,128)(2,1)S(1)}, bf16[256,512]{1,0:T(8,128)(2,1)S(1)}, u32[]{:S(2)}, u32[]{:S(2)}) collective-permute-start(bf16[256,512]{1,0:T(8,128)(2,1)S(1)} %collective-permute-done.18.refs_5_), channel_id=1, source_target_pairs={{0,2},{2,0},{1,3},{3,1},{4,6},{6,4},{5,7},{7,5},{8,10},{10,8},{9,1... | collective-permute-start | bytes 786440 | tf_op jit(solution)/shard_map/ppermute | solution.py:642
  68.5 16.1 %collective-permute-start.20 = (bf16[272,512]{1,0:T(8,128)(2,1)S(1)}, bf16[272,512]{1,0:T(8,128)(2,1)S(1)}, u32[]{:S(2)}, u32[]{:S(2)}) collective-permute-start(bf16[272,512]{1,0:T(8,128)(2,1)S(1)} %collective-permute-done.16.refs_8_), channel_id=1, source_target_pairs={{0,4},{4,8},{8,12},{12,0},{1,5},{5,9},{9,13},{13,1},{2,6},{6,10},{... | collective-permute-start | bytes 835592 | tf_op jit(solution)/shard_map/ppermute | solution.py:642
  68.6 16.0 %collective-permute-start.21 = (bf16[272,512]{1,0:T(8,128)(2,1)S(1)}, bf16[272,512]{1,0:T(8,128)(2,1)S(1)}, u32[]{:S(2)}, u32[]{:S(2)}) collective-permute-start(bf16[272,512]{1,0:T(8,128)(2,1)S(1)} %collective-permute-done.16.refs_8_), channel_id=1, source_target_pairs={{0,2},{2,0},{1,3},{3,1},{4,6},{6,4},{5,7},{7,5},{8,10},{10,8},{9,1... | collective-permute-start | bytes 835592 | tf_op jit(solution)/shard_map/ppermute | solution.py:642
  74.2 11.6 %collective-permute-start.25 = (bf16[256,512]{1,0:T(8,128)(2,1)}, bf16[256,512]{1,0:T(8,128)(2,1)}, u32[]{:S(2)}, u32[]{:S(2)}) collective-permute-start(bf16[256,512]{1,0:T(8,128)(2,1)} %collective-permute-done.22.refs_9_), channel_id=1, source_target_pairs={{0,4},{4,8},{8,12},{12,0},{1,5},{5,9},{9,13},{13,1},{2,6},{6,10},{... | collective-permute-start | bytes 786440 | tf_op jit(solution)/shard_map/ppermute | solution.py:642
  74.3 11.6 %collective-permute-start.26 = (bf16[256,512]{1,0:T(8,128)(2,1)}, bf16[256,512]{1,0:T(8,128)(2,1)}, u32[]{:S(2)}, u32[]{:S(2)}) collective-permute-start(bf16[256,512]{1,0:T(8,128)(2,1)} %collective-permute-done.22.refs_9_), channel_id=1, source_target_pairs={{0,2},{2,0},{1,3},{3,1},{4,6},{6,4},{5,7},{7,5},{8,10},{10,8},{9,1... | collective-permute-start | bytes 786440 | tf_op jit(solution)/shard_map/ppermute | solution.py:642
  84.6 17.4 %collective-permute-start.24 = (bf16[272,512]{1,0:T(8,128)(2,1)S(1)}, bf16[272,512]{1,0:T(8,128)(2,1)}, u32[]{:S(2)}, u32[]{:S(2)}) collective-permute-start(bf16[272,512]{1,0:T(8,128)(2,1)S(1)} %collective-permute-done.20.refs_0_), channel_id=1, source_target_pairs={{0,2},{2,0},{1,3},{3,1},{4,6},{6,4},{5,7},{7,5},{8,10},{10,8},{9,1... | collective-permute-start | bytes 835592 | tf_op jit(solution)/shard_map/ppermute | solution.py:642
  85.8 16.2 %collective-permute-start.27 = (bf16[256,512]{1,0:T(8,128)(2,1)}, bf16[256,512]{1,0:T(8,128)(2,1)S(1)}, u32[]{:S(2)}, u32[]{:S(2)}) collective-permute-start(bf16[256,512]{1,0:T(8,128)(2,1)} %collective-permute-done.26.refs_3_), channel_id=1, source_target_pairs={{0,4},{4,8},{8,12},{12,0},{1,5},{5,9},{9,13},{13,1},{2,6},{6,10},{... | collective-permute-start | bytes 786440 | tf_op jit(solution)/shard_map/ppermute | solution.py:642
  105.8 14.3 %collective-permute-start.33 = (bf16[2,256,256]{2,1,0:T(8,128)(2,1)S(1)}, bf16[2,256,256]{2,1,0:T(8,128)(2,1)S(1)}, u32[]{:S(2)}, u32[]{:S(2)}) collective-permute-start(bf16[2,256,256]{2,1,0:T(8,128)(2,1)S(1)} %pad_maximum_fusion.4), channel_id=1, source_target_pairs={{0,8},{4,12},{8,0},{12,4},{1,9},{5,13},{9,1},{13,5},{2,10},{6,14},... | collective-permute-start | bytes 786440 | tf_op jit(solution)/shard_map/ppermute | solution.py:642
  108.4 12.8 %collective-permute-start.30 = (bf16[2,512,128]{2,1,0:T(8,128)(2,1)S(1)}, bf16[2,512,128]{2,1,0:T(8,128)(2,1)S(1)}, u32[]{:S(2)}, u32[]{:S(2)}) collective-permute-start(bf16[2,512,128]{2,1,0:T(8,128)(2,1)S(1)} %get-tuple-element.194), channel_id=1, source_target_pairs={{0,1},{1,0},{2,3},{3,2},{4,5},{5,4},{6,7},{7,6},{8,9},{9,8},{10,11... | collective-permute-start | bytes 786440 | tf_op jit(solution)/shard_map/ppermute | solution.py:54
  111.6 11.3 %collective-permute-start.31 = (bf16[2,512,128]{2,1,0:T(8,128)(2,1)S(1)}, bf16[2,512,128]{2,1,0:T(8,128)(2,1)S(1)}, u32[]{:S(2)}, u32[]{:S(2)}) collective-permute-start(bf16[2,512,128]{2,1,0:T(8,128)(2,1)S(1)} %get-tuple-element.198.refs_2_), channel_id=1, source_target_pairs={{0,16},{1,17},{16,0},{17,1},{2,18},{3,19},{18,2},{19,3},{4,20},{5,... | collective-permute-start | bytes 786440 | tf_op jit(solution)/shard_map/ppermute | solution.py:815
  113.0 13.2 %collective-permute-start.32 = (bf16[2,512,128]{2,1,0:T(8,128)(2,1)S(1)}, bf16[2,512,128]{2,1,0:T(8,128)(2,1)S(1)}, u32[]{:S(2)}, u32[]{:S(2)}) collective-permute-start(bf16[2,512,128]{2,1,0:T(8,128)(2,1)S(1)} %get-tuple-element.194), channel_id=1, source_target_pairs={{0,17},{1,16},{16,1},{17,0},{2,19},{3,18},{18,3},{19,2},{4,21},{5,... | collective-permute-start | bytes 786440 | tf_op jit(solution)/shard_map/ppermute | solution.py:815
  113.7 16.9 %collective-permute-start.35 = (bf16[2,512,128]{2,1,0:T(8,128)(2,1)S(1)}, bf16[2,512,128]{2,1,0:T(8,128)(2,1)S(1)}, u32[]{:S(2)}, u32[]{:S(2)}) collective-permute-start(bf16[2,512,128]{2,1,0:T(8,128)(2,1)S(1)} %get-tuple-element.206), channel_id=1, source_target_pairs={{0,1},{1,0},{2,3},{3,2},{4,5},{5,4},{6,7},{7,6},{8,9},{9,8},{10,11... | collective-permute-start | bytes 786440 | tf_op jit(solution)/shard_map/ppermute | solution.py:54
  120.1 10.6 %collective-permute-start.36 = (bf16[2,512,128]{2,1,0:T(8,128)(2,1)S(1)}, bf16[2,512,128]{2,1,0:T(8,128)(2,1)S(1)}, u32[]{:S(2)}, u32[]{:S(2)}) collective-permute-start(bf16[2,512,128]{2,1,0:T(8,128)(2,1)S(1)} %get-tuple-element.213.refs_2_), channel_id=1, source_target_pairs={{0,16},{1,17},{16,0},{17,1},{2,18},{3,19},{18,2},{19,3},{4,20},{5,... | collective-permute-start | bytes 786440 | tf_op jit(solution)/shard_map/ppermute | solution.py:815
  121.2 15.3 %collective-permute-start.37 = (bf16[2,512,128]{2,1,0:T(8,128)(2,1)S(1)}, bf16[2,512,128]{2,1,0:T(8,128)(2,1)S(1)}, u32[]{:S(2)}, u32[]{:S(2)}) collective-permute-start(bf16[2,512,128]{2,1,0:T(8,128)(2,1)S(1)} %get-tuple-element.206), channel_id=1, source_target_pairs={{0,17},{1,16},{16,1},{17,0},{2,19},{3,18},{18,3},{19,2},{4,21},{5,... | collective-permute-start | bytes 786440 | tf_op jit(solution)/shard_map/ppermute | solution.py:815
  147.7 23.8 %collective-permute-start.55 = (bf16[8,256,256]{2,1,0:T(8,128)(2,1)S(1)}, bf16[8,256,256]{2,1,0:T(8,128)(2,1)S(1)}, u32[]{:S(2)}, u32[]{:S(2)}) collective-permute-start(bf16[8,256,256]{2,1,0:T(8,128)(2,1)S(1)} %constant_dynamic-update-slice_fusion.refs_10_.refs_14_.refs_18_.refs_22_.refs_26_.refs_4_.refs_8_., ...), channel_id=1, source_target_pairs={{0,16},{16,0},{1,17},{17,1},{2,18},{18,2},{3,19},{19,3},{4,20},{20... | collective-permute-start | bytes 3145736 | tf_op jit(solution)/shard_map/ppermute | solution.py:642
  153.0 20.3 %collective-permute-start.46 = (bf16[512,256]{1,0:T(8,128)(2,1)S(1)}, bf16[512,256]{1,0:T(8,128)(2,1)S(1)}, u32[]{:S(2)}, u32[]{:S(2)}) collective-permute-start(bf16[512,256]{1,0:T(8,128)(2,1)S(1)} %maximum_select_fusion.4.refs_1_), channel_id=1, source_target_pairs={{0,4},{4,8},{8,12},{12,0},{1,5},{5,9},{9,13},{13,1},{2,6},{6,10},{... | collective-permute-start | bytes 786440 | tf_op jit(solution)/shard_map/ppermute | solution.py:642
  153.1 21.7 %collective-permute-start.47 = (bf16[512,256]{1,0:T(8,128)(2,1)S(1)}, bf16[512,256]{1,0:T(8,128)(2,1)S(1)}, u32[]{:S(2)}, u32[]{:S(2)}) collective-permute-start(bf16[512,256]{1,0:T(8,128)(2,1)S(1)} %maximum_select_fusion.4.refs_1_), channel_id=1, source_target_pairs={{0,2},{2,0},{1,3},{3,1},{4,6},{6,4},{5,7},{7,5},{8,10},{10,8},{9,1... | collective-permute-start | bytes 786440 | tf_op jit(solution)/shard_map/ppermute | solution.py:642
  157.5 17.2 %collective-permute-start.43 = (bf16[512,256]{1,0:T(8,128)(2,1)S(1)}, bf16[512,256]{1,0:T(8,128)(2,1)S(1)}, u32[]{:S(2)}, u32[]{:S(2)}) collective-permute-start(bf16[512,256]{1,0:T(8,128)(2,1)S(1)} %collective-permute-done.41.refs_8_), channel_id=1, source_target_pairs={{0,4},{4,8},{8,12},{12,0},{1,5},{5,9},{9,13},{13,1},{2,6},{6,10},{... | collective-permute-start | bytes 786440 | tf_op jit(solution)/shard_map/ppermute | solution.py:642
  157.5 41.8 %collective-permute-start.54 = (bf16[8,256,256]{2,1,0:T(8,128)(2,1)S(1)}, bf16[8,256,256]{2,1,0:T(8,128)(2,1)S(1)}, u32[]{:S(2)}, u32[]{:S(2)}) collective-permute-start(bf16[8,256,256]{2,1,0:T(8,128)(2,1)S(1)} %constant_dynamic-update-slice_fusion.refs_10_.refs_14_.refs_18_.refs_22_.refs_26_.refs_4_.refs_8_., ...), channel_id=1, source_target_pairs={{0,1},{1,0},{2,3},{3,2},{4,5},{5,4},{6,7},{7,6},{8,9},{9,8},{10,11... | collective-permute-start | bytes 3145736 | tf_op jit(solution)/shard_map/ppermute | solution.py:54
  171.4 32.0 %collective-permute-start.56 = (bf16[8,256,256]{2,1,0:T(8,128)(2,1)S(1)}, bf16[8,256,256]{2,1,0:T(8,128)(2,1)S(1)}, u32[]{:S(2)}, u32[]{:S(2)}) collective-permute-start(bf16[8,256,256]{2,1,0:T(8,128)(2,1)S(1)} %collective-permute-done.55.refs_12_.refs_16_.refs_20_.refs_24_.refs_28_.refs_6_.refs_10_.refs_4_), channel_id=1, source_target_pairs={{0,1},{1,0},{2,3},{3,2},{4,5},{5,4},{6,7},{7,6},{8,9},{9,8},{10,11... | collective-permute-start | bytes 3145736 | tf_op jit(solution)/shard_map/ppermute | solution.py:54
  174.8 12.1 %collective-permute-start.50 = (bf16[512,256]{1,0:T(8,128)(2,1)S(1)}, bf16[512,256]{1,0:T(8,128)(2,1)S(1)}, u32[]{:S(2)}, u32[]{:S(2)}) collective-permute-start(bf16[512,256]{1,0:T(8,128)(2,1)S(1)} %collective-permute-done.46.refs_5_), channel_id=1, source_target_pairs={{0,2},{2,0},{1,3},{3,1},{4,6},{6,4},{5,7},{7,5},{8,10},{10,8},{9,1... | collective-permute-start | bytes 786440 | tf_op jit(solution)/shard_map/ppermute | solution.py:642
  188.3 11.1 %collective-permute-start.48 = (bf16[512,256]{1,0:T(8,128)(2,1)S(1)}, bf16[512,256]{1,0:T(8,128)(2,1)S(1)}, u32[]{:S(2)}, u32[]{:S(2)}) collective-permute-start(bf16[512,256]{1,0:T(8,128)(2,1)S(1)} %collective-permute-done.43.refs_0_), channel_id=1, source_target_pairs={{0,2},{2,0},{1,3},{3,1},{4,6},{6,4},{5,7},{7,5},{8,10},{10,8},{9,1... | collective-permute-start | bytes 786440 | tf_op jit(solution)/shard_map/ppermute | solution.py:642
  (92 other events, 1340.4 us)

commit v7 on v6

--- a/solution.py
+++ b/solution.py
@@ -206,11 +206,11 @@
     return lax.rem(tile + tiles - entry // 2, tiles) * outer + lax.rem(mpo + entry % 2, outer)
 
 
-def qkv_kernel(entries, layout, groups, first, last, meta, *refs):
+def qkv_kernel(entries, layout, groups, held, first, last, meta, *refs):
     refs = list(refs)
     count = len(entries)
     x_refs = take_blocks(refs, count)
-    weight_refs = [refs.pop(0) for _ in range(6)]
+    weight_refs = [refs.pop(0) for _ in range(6 if held else 6 * count)]
     if not first:
         acc_in, square_in = refs.pop(0), refs.pop(0)
     if last:
@@ -237,7 +237,11 @@
             piece = value[:, part * HD : (part + 1) * HD]
             square = piece if square is None else square + piece
         for part in range(6):
-            term = mxu(scaled_ref[...], weight_refs[part][rows, :])
+            if held:
+                weight = weight_refs[part][rows, :]
+            else:
+                weight = weight_refs[6 * index + part][...]
+            term = mxu(scaled_ref[...], weight)
             if index == 0 and not first:
                 term = term + acc_in[part]
             if last:
@@ -268,7 +272,7 @@
                 q_outs[head][...] = (raw * (head_gains[0:1, :] * HD ** (-0.5))).astype(BF16)
 
 
-def qkv_step(meta, layout, blocks, entries, weights, state, head_gains):
+def qkv_step(meta, layout, blocks, entries, weights, held, state, head_gains):
     span = blocks[0][1].shape[1]
     half = 2 * blocks[0][1].shape[0]
     width = weights[0].shape[1]
@@ -277,8 +281,14 @@
     groups = layout[1] * layout[2]
     inputs = [p for pieces in blocks for p in pieces]
     specs = [full(p.shape) for p in inputs]
-    inputs += weights
-    specs += [HELD] * 6
+    if held:
+        inputs += weights
+        specs += [HELD] * 6
+    else:
+        for entry in entries:
+            inputs += weights
+            index = lambda i, m, entry=entry: (chip_of(m, *layout, entry), 0)
+            specs += [pl.BlockSpec((span, width), index)] * 6
     if not first:
         inputs += list(state)
         specs += [HELD] * 2
@@ -290,7 +300,7 @@
     else:
         outs = [pltpu.VMEM((6, half, width), F32), pltpu.VMEM((half, HD), F32)]
     return pl.pallas_call(
-        functools.partial(qkv_kernel, entries, layout, groups, first, last),
+        functools.partial(qkv_kernel, entries, layout, groups, held, first, last),
         grid_spec=pltpu.PrefetchScalarGridSpec(
             num_scalar_prefetch=1,
             grid=(1,),
@@ -575,7 +585,7 @@
         out_ref[...] = spread(active, spread_ref)
 
 
-def up_step(blocks, entries, tiles, weights, state, spread_weight):
+def up_step(blocks, entries, weights, state, spread_weight):
     span = blocks[0][0].shape[1]
     halves, count = len(weights), len(blocks)
     first, last = state is None, spread_weight is not None
@@ -583,13 +593,10 @@
     inputs = [p for pieces in blocks for p in pieces]
     specs = [whole(p.shape) for p in inputs]
     for entry in entries:
-        offset = entry - 2 * (entry // 2 > tiles // 2)
-        if entry // 2 == tiles // 2:
-            offset = 2 * tiles - 2 + entry % 2
         for sides in weights:
             for weight in sides:
                 inputs.append(weight)
-                specs.append(pl.BlockSpec((1, span // 2, CH), lambda i, offset=offset: (offset, 0, 0)))
+                specs.append(pl.BlockSpec((1, span // 2, CH), lambda i, entry=entry: (entry, 0, 0)))
     if not first:
         inputs.append(state)
         specs.append(whole(state.shape))
@@ -693,12 +700,6 @@
     return shift(block, "tile", step) if step else block
 
 
-def transposed(blocks, halves):
-    own = jnp.concatenate(blocks)
-    weights = [own] if halves == 1 else [own, shift(own, "ctx", 1)]
-    return [[weight, swap(weight)] for weight in weights]
-
-
 def gather_pair(first, second, state, step, extras=None):
     tiles = lax.axis_size("tile")
     found, moving = [{0: first}, {}], [None, None]
@@ -731,6 +732,8 @@
         ring, cross = moving[which]
         if (which, index) == (int(late), tiles - 1):
             ring, cross, seen, state = lax.optimization_barrier((ring, cross, seen, state))
+        elif late and (which, index) == (1, tiles - 2):
+            ring, cross, seen, extras = lax.optimization_barrier((ring, cross, seen, extras))
         else:
             ring, cross, seen = lax.optimization_barrier((ring, cross, seen))
         found[which][2 * index], found[which][2 * index - 1] = ring, cross
@@ -782,27 +785,30 @@
 
     weights = [swap(w) for w in (key_weight, value_weight, query_weight)]
     pieces, conv, meta, weights[0], weights[1] = gather_small(latents, down_conv, meta, *weights[:2])
-    kept, sent, halves = transpose_first(meta, patch_out, layout, ctxs)
-    pieces, received = lax.optimization_barrier((pieces, shift(sent, "mpo", 1)))
-    up_blocks = [transpose_second(kept, received, step) for step in range(tiles) if 2 * step != tiles]
-
+    later, pieces[1] = lax.optimization_barrier((meta, pieces[1]))
+    kept, sent, halves = transpose_first(later, patch_out, layout, ctxs)
+    pieces, sent = lax.optimization_barrier((pieces, sent))
+    received = shift(sent, "mpo", 1)
     weights += [key_weight, value_weight, query_weight]
     streams = down_stream(meta, pieces, conv, patch_in, text_embed, norm_gain, weights, images)
-    streams, weights = streams[:2], streams[2:]
-    streams, up_blocks = lax.optimization_barrier((streams, up_blocks))
+    streams, held_weights = streams[:2], streams[2:]
+    streams, received = lax.optimization_barrier((streams, received))
     others = [swap(s[1]) for s in streams]
     others = lax.optimization_barrier(others)
 
     head_gains = jnp.stack([query_gain, key_gain])
 
     def project(blocks, entries, state, last):
-        return qkv_step(meta, layout, blocks, entries, weights, state, head_gains if last else None)
+        held = state is None
+        return qkv_step(
+            meta, layout, blocks, entries, held_weights if held else weights, held, state, head_gains if last else None
+        )
 
     state, out_par = gather_pair(
         *[by_core(core, s[0], o, 1) for s, o in zip(streams, others)], None, project, swap(out_weight)
     )
     state, kept, received = lax.optimization_barrier((state, kept, received))
-    up_block = transpose_second(kept, received, tiles // 2)
+    up_blocks = [transpose_second(kept, received, step) for step in range(tiles)]
     kv_send, q_send = state[:heads], state[heads : 2 * heads]
     kv_own, q_own = state[2 * heads : 3 * heads], state[3 * heads :]
 
@@ -825,17 +831,21 @@
         (att_own, att_send), ahead = lax.optimization_barrier((result, ahead))
         return by_core(core, att_own, swap(att_send), 1), ahead
 
-    pieces, up_block = lax.optimization_barrier((pieces_of(0), up_block))
-    attended, pieces = attend(0, pieces, pieces_of(1) if heads > 1 else None)
+    attended, (pieces, up_blocks) = attend(
+        0, pieces_of(0), (pieces_of(1) if heads > 1 else None, up_blocks)
+    )
     if heads == 1:
         attended, second = attended[: half // 2], attended[half // 2 :]
-        extras = transposed(up_blocks + [up_block], halves)
+        own = jnp.concatenate(up_blocks)
+        extras = [own, swap(own)] + ([shift(own, "ctx", 1)] if halves == 2 else [])
     else:
         extras = None
 
         def second(token):
-            result, (up, _) = attend(1, pieces, (up_blocks + [up_block], token))
-            return result, transposed(up, halves)
+            result, (up, _) = attend(1, pieces, (up_blocks, token))
+            own = jnp.concatenate(up)
+            result, own, par = lax.optimization_barrier((result, own, swap(own)))
+            return result, [own, par] + ([shift(own, "ctx", 1)] if halves == 2 else [])
 
     def project_out(blocks, entries, state, last):
         return out_step(meta, layout, blocks, entries, (out_weight, out_par), state, last)
@@ -846,7 +856,10 @@
     out_other = swap(out_send)
     layer_out = by_core(core, out_own, out_other, 0)
 
-    picks = pick_rows(meta, out_own, out_other, images, ctxs)
+    picks, swapped = lax.optimization_barrier(
+        (pick_rows(meta, out_own, out_other, images, ctxs), [swap(other) for other in up_weights[2:]])
+    )
+    up_weights = [up_weights[:2]] + [[up_weights[2], other] for other in swapped]
     own_parts, par_parts = [picks[0]], [swap(picks[1])]
     for step in range(1, ctxs):
         own_parts.append(shifted(picks[2 * step], step, False))
@@ -857,7 +870,7 @@
     spread_weight = spread_weights(up_conv, pixels)
 
     def project_up(blocks, entries, state, last):
-        return up_step(blocks, entries, tiles, up_weights, state, spread_weight if last else None)
+        return up_step(blocks, entries, up_weights, state, spread_weight if last else None)
 
     state, _ = gather_pair(*merge_picks(own_parts, par_parts), None, project_up)
 

time: 270 us -> 245 us (0.907)
  starting transfers between devices: 76.9 us -> 62 us
  local copies, waits for them, and re-layouts: 24.3 us -> 19.1 us
  waiting for transfers between devices: 114 us -> 110 us
    ppermute x55, starting transfers between devices: 42.8 us -> 35.6 us  [shift(): lax.ppermute(values, axis, [(i, (i + step) % count) for i in range(count)])]
    ppermute x17, starting transfers between devices: 20.7 us -> 14.6 us  [swap(): return lax.ppermute(values, 'core', [(0, 1), (1, 0)])]
    ppermute x55, waiting for transfers between devices: 93.5 us -> 89.2 us  [shift(): lax.ppermute(values, axis, [(i, (i + step) % count) for i in range(count)])]
    ppermute x17, waiting for transfers between devices: 4.47 us -> 7.4 us  [swap(): return lax.ppermute(values, 'core', [(0, 1), (1, 0)])]
    unnamed x90 -> x66, local copies, waits for them, and re-layouts: 19.4 us -> 16.7 us
  transfers between devices with their start and end apart: 81 -> 81, of which waited for: 36 -> 36; matrix products, arithmetic and copies ran while one was open for 4% -> 3% of each run, Pallas kernels for 14% -> 17%
where the time goes in v7:
time: 245 us; the launch traced here: 244 us
  waiting for transfers between devices  110 us (45%)
  starting transfers between devices  62 us (25%)
  Pallas kernels  46.6 us (19%)
  local copies, waits for them, and re-layouts  19.1 us (8%)
  other arithmetic  4.55 us (2%)
    ppermute x55, waiting for transfers between devices, shift(): lax.ppermute(values, axis, [(i, (i + step) % count) for i in range(count)])  89.2 us
    ppermute x55, starting transfers between devices, shift(): lax.ppermute(values, axis, [(i, (i + step) % count) for i in range(count)])  35.6 us
    unnamed x66, local copies, waits for them, and re-layouts  16.7 us
    ppermute x17, starting transfers between devices, swap(): return lax.ppermute(values, 'core', [(0, 1), (1, 0)])  14.6 us
    pallas_call x3, Pallas kernels, qkv_step(): pl.pallas_call(functools.partial(qkv_kernel, entries, layout, groups, hel...  13.6 us
    ppermute x6, waiting for transfers between devices, shifted(): return lax.ppermute(values, ('ctx', 'core'), pairs)  13.3 us
    pallas_call x1, Pallas kernels, down_stream(): pl.pallas_call(functools.partial(down_kernel, images, tiles, half), grid_...  9.45 us
    pallas_call x2, Pallas kernels, attention(): pl.pallas_call(functools.partial(attention_kernel, images, len(pieces), h...  8.9 us
  transfers between devices with their start and end apart: 81, of which 36 were waited for; matrix products, arithmetic and copies ran while one was open for 3% of the time, Pallas kernels for 17%

profile of v7, /device:TPU:1, one launch (start us, length us, event | category | flops | bytes accessed | tf_op | source)
XLA Modules:
  0.0 244.3 jit_solution(79080204230456545)
XLA Ops:
  18.9 3.2 %collective-permute-start.26 = (bf16[4096,256]{1,0:T(8,128)(2,1)S(1)}, bf16[4096,256]{1,0:T(8,128)(2,1)}, u32[]{:S(2)}, u32[]{:S(2)}) collective-permute-start(bf16[4096,256]{1,0:T(8,128)(2,1)S(1)} %copy-done.1), channel_id=1, source_target_pairs={{0,1},{1,0},{2,3},{3,2},{4,5},{5,4},{6,7},{7,6},{8,9},{9,8},{10,11... | collective-permute-start | bytes 6291464 | tf_op jit(solution)/shard_map/ppermute | solution.py:54
  23.2 9.5 %down_stream.1 = (bf16[2,272,256]{2,1,0:T(8,128)(2,1)S(1)}, bf16[2,256,256]{2,1,0:T(8,128)(2,1)S(1)}, bf16[4096,256]{1,0:T(8,128)(2,1)S(1)}, bf16[4096,256]{1,0:...) custom-call(s32[16]{0:T(128)S(1)} %concatenate.64.meta, ...), custom_call_target="tpu_custom_call" | custom-call | flops 4294967296 | bytes 4194304 | tf_op jit(solution)/shard_map/down_stream/pallas_call | solution.py:160
  39.0 6.5 %collective-permute-done.12.refs_4_ = bf16[272,512]{1,0:T(8,128)(2,1)S(1)} collective-permute-done((bf16[272,512]{1,0:T(8,128)(2,1)S(1)}, bf16[272,512]{1,0:T(8,128)(2,1)S(1)}, u32[]{:S(2)}, u32[]{:S(2)}) %collective-permute-start.12) | collective-permute-done | bytes 278560 | tf_op jit(solution)/shard_map/ppermute | solution.py:649
  46.1 5.0 %collective-permute-done.16.refs_5_ = bf16[256,512]{1,0:T(8,128)(2,1)S(1)} collective-permute-done((bf16[256,512]{1,0:T(8,128)(2,1)S(1)}, bf16[256,512]{1,0:T(8,128)(2,1)S(1)}, u32[]{:S(2)}, u32[]{:S(2)}) %collective-permute-start.16) | collective-permute-done | bytes 262176 | tf_op jit(solution)/shard_map/ppermute | solution.py:649
  51.7 5.4 %collective-permute-done.14.refs_8_ = bf16[272,512]{1,0:T(8,128)(2,1)S(1)} collective-permute-done((bf16[272,512]{1,0:T(8,128)(2,1)S(1)}, bf16[272,512]{1,0:T(8,128)(2,1)S(1)}, u32[]{:S(2)}, u32[]{:S(2)}) %collective-permute-start.14) | collective-permute-done | bytes 278560 | tf_op jit(solution)/shard_map/ppermute | solution.py:649
  57.8 5.0 %collective-permute-done.20.refs_9_ = bf16[256,512]{1,0:T(8,128)(2,1)} collective-permute-done((bf16[256,512]{1,0:T(8,128)(2,1)S(1)}, bf16[256,512]{1,0:T(8,128)(2,1)}, u32[]{:S(2)}, u32[]{:S(2)}) %collective-permute-start.20) | collective-permute-done | bytes 262176 | tf_op jit(solution)/shard_map/ppermute | solution.py:649
  63.4 6.5 %qkv_step.2 = (f32[6,512,256]{2,1,0:T(8,128)S(1)}, f32[512,128]{1,0:T(8,128)S(1)}) custom-call(s32[16]{0:T(128)S(1)} %concatenate.64.meta, bf16[272,512]{1,0:T(8,128)(2,1)S(1)} %maximum_select_fusion.1.refs_0_, bf16[256,512]{1,0:T(8,128)(2,1)S(1)} %maximum_select_fusion.2.refs_1_, bf16[272,512]{1,0:T(8,128)(2,1)S(1)} %collective-permute-done.13.refs_2_, ...), custom_call_target="tpu_custom_call" | custom-call | flops 4026531840 | bytes 16777216 | tf_op jit(solution)/shard_map/qkv_step/pallas_call | solution.py:302
  82.0 4.2 %qkv_step.3 = (f32[6,512,256]{2,1,0:T(8,128)S(1)}, f32[512,128]{1,0:T(8,128)S(1)}) custom-call(s32[16]{0:T(128)S(1)} %concatenate.64.meta, bf16[272,512]{1,0:T(8,128)(2,1)S(1)} %collective-permute-done.18.refs_0_, bf16[256,512]{1,0:T(8,128)(2,1)} %collective-permute-done.23.refs_1_, bf16[272,512]{1,0:T(8,128)(2,1)S(1)} %collective-permute-done.19.refs_2_, ...), custom_call_target="tpu_custom_call" | custom-call | flops 1610612736 | bytes 10485760 | tf_op jit(solution)/shard_map/qkv_step/pallas_call | solution.py:302
  86.3 2.9 %qkv_last.1 = (bf16[2,512,128]{2,1,0:T(8,128)(2,1)S(1)}, bf16[2,512,128]{2,1,0:T(8,128)(2,1)S(1)}, bf16[512,128]{1,0:T(8,128)(2,1)S(1)}, bf16[512,128]{1,0:T(8,1...) custom-call(s32[16]{0:T(128)S(1)} %concatenate.64.meta, ...), custom_call_target="tpu_custom_call" | custom-call | flops 805306368 | bytes 8388608 | tf_op jit(solution)/shard_map/qkv_last/pallas_call | solution.py:302
  89.2 2.8 %collective-permute-start.27 = (bf16[512,128]{1,0:T(8,128)(2,1)S(1)}, bf16[512,128]{1,0:T(8,128)(2,1)S(1)}, u32[]{:S(2)}, u32[]{:S(2)}) collective-permute-start(bf16[512,128]{1,0:T(8,128)(2,1)S(1)} %get-tuple-element.203), channel_id=1, source_target_pairs={{0,1},{1,0},{2,3},{3,2},{4,5},{5,4},{6,7},{7,6},{8,9},{9,8},{10,11... | collective-permute-start | bytes 393224 | tf_op jit(solution)/shard_map/ppermute | solution.py:54
  103.9 5.5 %collective-permute-done.30.refs_5_ = bf16[2,512,128]{2,1,0:T(8,128)(2,1)S(1)} collective-permute-done((bf16[2,512,128]{2,1,0:T(8,128)(2,1)S(1)}, bf16[2,512,128]{2,1,0:T(8,128)(2,1)S(1)}, u32[]{:S(2)}, u32[]{:S(2)}) %collective-permute-start.30) | collective-permute-done | bytes 262176 | tf_op jit(solution)/shard_map/ppermute | solution.py:821
  109.7 4.5 %attention.2 = (bf16[512,128]{1,0:T(8,128)(2,1)S(1)}, bf16[512,128]{1,0:T(8,128)(2,1)S(1)}) custom-call(s32[16]{0:T(128)S(1)} %concatenate.64.meta, bf16[512,128]{1,0:T(8,128)(2,1)S(1)} %get-tuple-element.202.refs_0_, bf16[512,128]{1,0:T(8,128)(2,1)S(1)} %collective-permute-done.27.refs_1_, bf16[2,512,128]{2,1,0:T(8,128)(2,1)S(1)} %get-tuple-element.204.refs_2_, ...), custom_call_target="tpu_custom_call" | custom-call | flops 1073741824 | bytes 1048576 | tf_op jit(solution)/shard_map/attention/pallas_call | solution.py:360
  114.2 3.9 %collective-permute-done.36 = bf16[2,256,256]{2,1,0:T(8,128)(2,1)S(1)} collective-permute-done((bf16[2,256,256]{2,1,0:T(8,128)(2,1)S(1)}, bf16[2,256,256]{2,1,0:T(8,128)(2,1)S(1)}, u32[]{:S(2)}, u32[]{:S(2)}) %collective-permute-start.36) | collective-permute-done | bytes 262176 | tf_op jit(solution)/shard_map/ppermute | solution.py:649
  121.5 4.4 %attention.3 = (bf16[512,128]{1,0:T(8,128)(2,1)S(1)}, bf16[512,128]{1,0:T(8,128)(2,1)S(1)}) custom-call(s32[16]{0:T(128)S(1)} %concatenate.64.meta, bf16[512,128]{1,0:T(8,128)(2,1)S(1)} %get-tuple-element.217.refs_0_, bf16[512,128]{1,0:T(8,128)(2,1)S(1)} %collective-permute-done.31.refs_1_, bf16[2,512,128]{2,1,0:T(8,128)(2,1)S(1)} %get-tuple-element.219.refs_2_, ...), custom_call_target="tpu_custom_call" | custom-call | flops 1073741824 | bytes 1048576 | tf_op jit(solution)/shard_map/attention/pallas_call | solution.py:360
  126.0 4.7 %collective-permute-done.39.refs_4_ = bf16[512,256]{1,0:T(8,128)(2,1)S(1)} collective-permute-done((bf16[512,256]{1,0:T(8,128)(2,1)S(1)}, bf16[512,256]{1,0:T(8,128)(2,1)S(1)}, u32[]{:S(2)}, u32[]{:S(2)}) %collective-permute-start.39) | collective-permute-done | bytes 262176 | tf_op jit(solution)/shard_map/ppermute | solution.py:649
  132.0 2.4 collective-permute-done.45
  138.4 7.3 %collective-permute-done.41.refs_8_ = bf16[512,256]{1,0:T(8,128)(2,1)S(1)} collective-permute-done((bf16[512,256]{1,0:T(8,128)(2,1)S(1)}, bf16[512,256]{1,0:T(8,128)(2,1)S(1)}, u32[]{:S(2)}, u32[]{:S(2)}) %collective-permute-start.41) | collective-permute-done | bytes 262176 | tf_op jit(solution)/shard_map/ppermute | solution.py:649
  145.9 5.4 %collective-permute-done.47.refs_5_ = bf16[512,256]{1,0:T(8,128)(2,1)S(1)} collective-permute-done((bf16[512,256]{1,0:T(8,128)(2,1)S(1)}, bf16[512,256]{1,0:T(8,128)(2,1)S(1)}, u32[]{:S(2)}, u32[]{:S(2)}) %collective-permute-start.47) | collective-permute-done | bytes 262176 | tf_op jit(solution)/shard_map/ppermute | solution.py:649
  151.6 5.4 %collective-permute-done.43.refs_0_ = bf16[512,256]{1,0:T(8,128)(2,1)S(1)} collective-permute-done((bf16[512,256]{1,0:T(8,128)(2,1)S(1)}, bf16[512,256]{1,0:T(8,128)(2,1)S(1)}, u32[]{:S(2)}, u32[]{:S(2)}) %collective-permute-start.43) | collective-permute-done | bytes 262176 | tf_op jit(solution)/shard_map/ppermute | solution.py:649
  156.9 5.6 %collective-permute-done.50.refs_9_ = bf16[512,256]{1,0:T(8,128)(2,1)S(1)} collective-permute-done((bf16[512,256]{1,0:T(8,128)(2,1)S(1)}, bf16[512,256]{1,0:T(8,128)(2,1)S(1)}, u32[]{:S(2)}, u32[]{:S(2)}) %collective-permute-start.50) | collective-permute-done | bytes 262176 | tf_op jit(solution)/shard_map/ppermute | solution.py:649
  164.3 3.3 %out_step.2.refs_8_ = f32[2,512,256]{2,1,0:T(8,128)S(1)} custom-call(s32[16]{0:T(128)S(1)} %concatenate.64.meta, bf16[512,256]{1,0:T(8,128)(2,1)S(1)} %maximum_select_fusion.3.refs_0_, bf16[512,256]{1,0:T(8,128)(2,1)S(1)} %maximum_select_fusion.4.refs_1_, bf16[512,256]{1,0:T(8,128)(2,1)S(1)} %collective-permute-done.40.refs_2_, ...), custom_call_target="tpu_custom_call" | custom-call | flops 1342177280 | bytes 7340032 | tf_op jit(solution)/shard_map/out_step/pallas_call | solution.py:430
  167.7 3.0 %collective-permute-done.53.refs_1_ = bf16[512,256]{1,0:T(8,128)(2,1)S(1)} collective-permute-done((bf16[512,256]{1,0:T(8,128)(2,1)S(1)}, bf16[512,256]{1,0:T(8,128)(2,1)S(1)}, u32[]{:S(2)}, u32[]{:S(2)}) %collective-permute-start.53) | collective-permute-done | bytes 262176 | tf_op jit(solution)/shard_map/ppermute | solution.py:649
  174.6 3.1 %collective-permute-done.55.refs_1_ = bf16[512,256]{1,0:T(8,128)(2,1)S(1)} collective-permute-done((bf16[512,256]{1,0:T(8,128)(2,1)S(1)}, bf16[512,256]{1,0:T(8,128)(2,1)S(1)}, u32[]{:S(2)}, u32[]{:S(2)}) %collective-permute-start.55) | collective-permute-done | bytes 262176 | tf_op jit(solution)/shard_map/ppermute | solution.py:649
  177.7 3.9 %collective-permute-start.57 = (bf16[8,256,256]{2,1,0:T(8,128)(2,1)S(1)}, bf16[8,256,256]{2,1,0:T(8,128)(2,1)S(1)}, u32[]{:S(2)}, u32[]{:S(2)}) collective-permute-start(bf16[8,256,256]{2,1,0:T(8,128)(2,1)S(1)} %collective-permute-done.52.refs_12_.refs_16_.refs_20_.refs_24_.refs_28_.refs_6_.refs_10_.refs_4_), channel_id=1, source_target_pairs={{0,1},{1,0},{2,3},{3,2},{4,5},{5,4},{6,7},{7,6},{8,9},{9,8},{10,11... | collective-permute-start | bytes 3145736 | tf_op jit(solution)/shard_map/ppermute | solution.py:54
  189.3 3.1 %collective-permute-done.58.refs_1_ = bf16[256,256]{1,0:T(8,128)(2,1)S(1)} collective-permute-done((bf16[256,256]{1,0:T(8,128)(2,1)S(1)}, bf16[256,256]{1,0:T(8,128)(2,1)S(1)}, u32[]{:S(2)}, u32[]{:S(2)}) %collective-permute-start.58) | collective-permute-done | bytes 131104 | tf_op jit(solution)/shard_map/ppermute | solution.py:821
  192.4 3.1 %collective-permute-done.60.refs_3_ = bf16[256,256]{1,0:T(8,128)(2,1)S(1)} collective-permute-done((bf16[256,256]{1,0:T(8,128)(2,1)S(1)}, bf16[256,256]{1,0:T(8,128)(2,1)S(1)}, u32[]{:S(2)}, u32[]{:S(2)}) %collective-permute-start.60) | collective-permute-done | bytes 131104 | tf_op jit(solution)/shard_map/ppermute | solution.py:821
  197.5 5.0 %collective-permute-done.61.refs_4_ = bf16[128,512]{1,0:T(8,128)(2,1)} collective-permute-done((bf16[128,512]{1,0:T(8,128)(2,1)S(1)}, bf16[128,512]{1,0:T(8,128)(2,1)}, u32[]{:S(2)}, u32[]{:S(2)}) %collective-permute-start.61) | collective-permute-done | bytes 131104 | tf_op jit(solution)/shard_map/ppermute | solution.py:649
  202.5 2.8 %collective-permute-done.65.refs_5_ = bf16[128,512]{1,0:T(8,128)(2,1)} collective-permute-done((bf16[128,512]{1,0:T(8,128)(2,1)S(1)}, bf16[128,512]{1,0:T(8,128)(2,1)}, u32[]{:S(2)}, u32[]{:S(2)}) %collective-permute-start.65) | collective-permute-done | bytes 131104 | tf_op jit(solution)/shard_map/ppermute | solution.py:649
  207.0 7.2 %collective-permute-done.63.refs_8_ = bf16[128,512]{1,0:T(8,128)(2,1)S(1)} collective-permute-done((bf16[128,512]{1,0:T(8,128)(2,1)}, bf16[128,512]{1,0:T(8,128)(2,1)S(1)}, u32[]{:S(2)}, u32[]{:S(2)}) %collective-permute-start.63) | collective-permute-done | bytes 131104 | tf_op jit(solution)/shard_map/ppermute | solution.py:649
  223.0 4.5 %collective-permute-done.74.refs_1_ = bf16[128,512]{1,0:T(8,128)(2,1)S(1)} collective-permute-done((bf16[128,512]{1,0:T(8,128)(2,1)S(1)}, bf16[128,512]{1,0:T(8,128)(2,1)S(1)}, u32[]{:S(2)}, u32[]{:S(2)}) %collective-permute-start.74) | collective-permute-done | bytes 131104 | tf_op jit(solution)/shard_map/ppermute | solution.py:649
  228.8 3.2 %collective-permute-start.77 = (f32[64,128]{1,0:T(8,128)S(1)}, f32[64,128]{1,0:T(8,128)S(1)}, u32[]{:S(2)}, u32[]{:S(2)}) collective-permute-start(f32[64,128]{1,0:T(8,128)S(1)} %get-tuple-element.303), channel_id=1, source_target_pairs={{0,12},{4,0},{8,4},{12,8},{1,13},{5,1},{9,5},{13,9},{2,14},{6,2},{... | collective-permute-start | bytes 98312 | tf_op jit(solution)/shard_map/ppermute | solution.py:649
  233.9 5.7 %collective-permute-start.79 = (f32[64,128]{1,0:T(8,128)S(1)}, f32[64,128]{1,0:T(8,128)S(1)}, u32[]{:S(2)}, u32[]{:S(2)}) collective-permute-start(f32[64,128]{1,0:T(8,128)S(1)} %fusion.25.own_a), channel_id=1, source_target_pairs={{0,1},{1,0},{2,3},{3,2},{4,5},{5,4},{6,7},{7,6},{8,9},{9,8},{10,11... | collective-permute-start | bytes 98312 | tf_op jit(solution)/shard_map/ppermute | solution.py:888
  (249 shorter events, 95.1 us)
Async XLA Ops:
  1.2 20.9 %collective-permute-start.8 = (bf16[4096,256]{1,0:T(8,128)(2,1)}, bf16[4096,256]{1,0:T(8,128)(2,1)}, u32[]{:S(2)}, u32[]{:S(2)}) collective-permute-start(bf16[4096,256]{1,0:T(8,128)(2,1)} %refs_7_.3), channel_id=1, source_target_pairs={{0,1},{1,0},{2,3},{3,2},{4,5},{5,4},{6,7},{7,6},{8,9},{9,8},{10,11... | collective-permute-start | bytes 6291464 | tf_op jit(solution)/shard_map/ppermute | solution.py:54
  17.7 15.0 %collective-permute-start.9 = (bf16[4,256,256]{2,1,0:T(8,128)(2,1)S(1)}, bf16[4,256,256]{2,1,0:T(8,128)(2,1)S(1)}, u32[]{:S(2)}, u32[]{:S(2)}) collective-permute-start(bf16[4,256,256]{2,1,0:T(8,128)(2,1)S(1)} %get-tuple-element.159), channel_id=1, source_target_pairs={{0,2},{2,0},{1,3},{3,1},{4,6},{6,4},{5,7},{7,5},{8,10},{10,8},{9,1... | collective-permute-start | bytes 1572872 | tf_op jit(solution)/shard_map/ppermute | solution.py:649
  18.9 67.4 %collective-permute-start.26 = (bf16[4096,256]{1,0:T(8,128)(2,1)S(1)}, bf16[4096,256]{1,0:T(8,128)(2,1)}, u32[]{:S(2)}, u32[]{:S(2)}) collective-permute-start(bf16[4096,256]{1,0:T(8,128)(2,1)S(1)} %copy-done.1), channel_id=1, source_target_pairs={{0,1},{1,0},{2,3},{3,2},{4,5},{5,4},{6,7},{7,6},{8,9},{9,8},{10,11... | collective-permute-start | bytes 6291464 | tf_op jit(solution)/shard_map/ppermute | solution.py:54
  35.7 9.7 %collective-permute-start.12 = (bf16[272,512]{1,0:T(8,128)(2,1)S(1)}, bf16[272,512]{1,0:T(8,128)(2,1)S(1)}, u32[]{:S(2)}, u32[]{:S(2)}) collective-permute-start(bf16[272,512]{1,0:T(8,128)(2,1)S(1)} %maximum_select_fusion.1.refs_0_), channel_id=1, source_target_pairs={{0,4},{4,8},{8,12},{12,0},{1,5},{5,9},{9,13},{13,1},{2,6},{6,10},{... | collective-permute-start | bytes 835592 | tf_op jit(solution)/shard_map/ppermute | solution.py:649
  37.7 13.4 %collective-permute-start.16 = (bf16[256,512]{1,0:T(8,128)(2,1)S(1)}, bf16[256,512]{1,0:T(8,128)(2,1)S(1)}, u32[]{:S(2)}, u32[]{:S(2)}) collective-permute-start(bf16[256,512]{1,0:T(8,128)(2,1)S(1)} %maximum_select_fusion.2.refs_1_), channel_id=1, source_target_pairs={{0,4},{4,8},{8,12},{12,0},{1,5},{5,9},{9,13},{13,1},{2,6},{6,10},{... | collective-permute-start | bytes 786440 | tf_op jit(solution)/shard_map/ppermute | solution.py:649
  37.9 13.2 %collective-permute-start.17 = (bf16[256,512]{1,0:T(8,128)(2,1)S(1)}, bf16[256,512]{1,0:T(8,128)(2,1)S(1)}, u32[]{:S(2)}, u32[]{:S(2)}) collective-permute-start(bf16[256,512]{1,0:T(8,128)(2,1)S(1)} %maximum_select_fusion.2.refs_1_), channel_id=1, source_target_pairs={{0,2},{2,0},{1,3},{3,1},{4,6},{6,4},{5,7},{7,5},{8,10},{10,8},{9,1... | collective-permute-start | bytes 786440 | tf_op jit(solution)/shard_map/ppermute | solution.py:649
  45.5 11.6 %collective-permute-start.14 = (bf16[272,512]{1,0:T(8,128)(2,1)S(1)}, bf16[272,512]{1,0:T(8,128)(2,1)S(1)}, u32[]{:S(2)}, u32[]{:S(2)}) collective-permute-start(bf16[272,512]{1,0:T(8,128)(2,1)S(1)} %collective-permute-done.12.refs_4_), channel_id=1, source_target_pairs={{0,4},{4,8},{8,12},{12,0},{1,5},{5,9},{9,13},{13,1},{2,6},{6,10},{... | collective-permute-start | bytes 835592 | tf_op jit(solution)/shard_map/ppermute | solution.py:649
  45.5 11.6 %collective-permute-start.15 = (bf16[272,512]{1,0:T(8,128)(2,1)S(1)}, bf16[272,512]{1,0:T(8,128)(2,1)S(1)}, u32[]{:S(2)}, u32[]{:S(2)}) collective-permute-start(bf16[272,512]{1,0:T(8,128)(2,1)S(1)} %collective-permute-done.12.refs_4_), channel_id=1, source_target_pairs={{0,2},{2,0},{1,3},{3,1},{4,6},{6,4},{5,7},{7,5},{8,10},{10,8},{9,1... | collective-permute-start | bytes 835592 | tf_op jit(solution)/shard_map/ppermute | solution.py:649
  51.1 11.7 %collective-permute-start.20 = (bf16[256,512]{1,0:T(8,128)(2,1)S(1)}, bf16[256,512]{1,0:T(8,128)(2,1)}, u32[]{:S(2)}, u32[]{:S(2)}) collective-permute-start(bf16[256,512]{1,0:T(8,128)(2,1)S(1)} %collective-permute-done.16.refs_5_), channel_id=1, source_target_pairs={{0,4},{4,8},{8,12},{12,0},{1,5},{5,9},{9,13},{13,1},{2,6},{6,10},{... | collective-permute-start | bytes 786440 | tf_op jit(solution)/shard_map/ppermute | solution.py:649
  51.1 11.7 %collective-permute-start.21 = (bf16[256,512]{1,0:T(8,128)(2,1)S(1)}, bf16[256,512]{1,0:T(8,128)(2,1)S(1)}, u32[]{:S(2)}, u32[]{:S(2)}) collective-permute-start(bf16[256,512]{1,0:T(8,128)(2,1)S(1)} %collective-permute-done.16.refs_5_), channel_id=1, source_target_pairs={{0,2},{2,0},{1,3},{3,1},{4,6},{6,4},{5,7},{7,5},{8,10},{10,8},{9,1... | collective-permute-start | bytes 786440 | tf_op jit(solution)/shard_map/ppermute | solution.py:649
  57.1 15.2 %collective-permute-start.18 = (bf16[272,512]{1,0:T(8,128)(2,1)S(1)}, bf16[272,512]{1,0:T(8,128)(2,1)S(1)}, u32[]{:S(2)}, u32[]{:S(2)}) collective-permute-start(bf16[272,512]{1,0:T(8,128)(2,1)S(1)} %collective-permute-done.14.refs_8_), channel_id=1, source_target_pairs={{0,4},{4,8},{8,12},{12,0},{1,5},{5,9},{9,13},{13,1},{2,6},{6,10},{... | collective-permute-start | bytes 835592 | tf_op jit(solution)/shard_map/ppermute | solution.py:649
  57.1 15.1 %collective-permute-start.19 = (bf16[272,512]{1,0:T(8,128)(2,1)S(1)}, bf16[272,512]{1,0:T(8,128)(2,1)S(1)}, u32[]{:S(2)}, u32[]{:S(2)}) collective-permute-start(bf16[272,512]{1,0:T(8,128)(2,1)S(1)} %collective-permute-done.14.refs_8_), channel_id=1, source_target_pairs={{0,2},{2,0},{1,3},{3,1},{4,6},{6,4},{5,7},{7,5},{8,10},{10,8},{9,1... | collective-permute-start | bytes 835592 | tf_op jit(solution)/shard_map/ppermute | solution.py:649
  62.8 11.6 %collective-permute-start.23 = (bf16[256,512]{1,0:T(8,128)(2,1)}, bf16[256,512]{1,0:T(8,128)(2,1)}, u32[]{:S(2)}, u32[]{:S(2)}) collective-permute-start(bf16[256,512]{1,0:T(8,128)(2,1)} %collective-permute-done.20.refs_9_), channel_id=1, source_target_pairs={{0,4},{4,8},{8,12},{12,0},{1,5},{5,9},{9,13},{13,1},{2,6},{6,10},{... | collective-permute-start | bytes 786440 | tf_op jit(solution)/shard_map/ppermute | solution.py:649
  62.8 11.6 %collective-permute-start.24 = (bf16[256,512]{1,0:T(8,128)(2,1)}, bf16[256,512]{1,0:T(8,128)(2,1)}, u32[]{:S(2)}, u32[]{:S(2)}) collective-permute-start(bf16[256,512]{1,0:T(8,128)(2,1)} %collective-permute-done.20.refs_9_), channel_id=1, source_target_pairs={{0,2},{2,0},{1,3},{3,1},{4,6},{6,4},{5,7},{7,5},{8,10},{10,8},{9,1... | collective-permute-start | bytes 786440 | tf_op jit(solution)/shard_map/ppermute | solution.py:649
  72.2 14.1 %collective-permute-start.22 = (bf16[272,512]{1,0:T(8,128)(2,1)S(1)}, bf16[272,512]{1,0:T(8,128)(2,1)S(1)}, u32[]{:S(2)}, u32[]{:S(2)}) collective-permute-start(bf16[272,512]{1,0:T(8,128)(2,1)S(1)} %collective-permute-done.18.refs_0_), channel_id=1, source_target_pairs={{0,2},{2,0},{1,3},{3,1},{4,6},{6,4},{5,7},{7,5},{8,10},{10,8},{9,1... | collective-permute-start | bytes 835592 | tf_op jit(solution)/shard_map/ppermute | solution.py:649
  74.4 11.9 %collective-permute-start.25 = (bf16[256,512]{1,0:T(8,128)(2,1)}, bf16[256,512]{1,0:T(8,128)(2,1)S(1)}, u32[]{:S(2)}, u32[]{:S(2)}) collective-permute-start(bf16[256,512]{1,0:T(8,128)(2,1)} %collective-permute-done.24.refs_3_), channel_id=1, source_target_pairs={{0,4},{4,8},{8,12},{12,0},{1,5},{5,9},{9,13},{13,1},{2,6},{6,10},{... | collective-permute-start | bytes 786440 | tf_op jit(solution)/shard_map/ppermute | solution.py:649
  96.1 13.3 %collective-permute-start.30 = (bf16[2,512,128]{2,1,0:T(8,128)(2,1)S(1)}, bf16[2,512,128]{2,1,0:T(8,128)(2,1)S(1)}, u32[]{:S(2)}, u32[]{:S(2)}) collective-permute-start(bf16[2,512,128]{2,1,0:T(8,128)(2,1)S(1)} %get-tuple-element.205), channel_id=1, source_target_pairs={{0,17},{1,16},{16,1},{17,0},{2,19},{3,18},{18,3},{19,2},{4,21},{5,... | collective-permute-start | bytes 786440 | tf_op jit(solution)/shard_map/ppermute | solution.py:821
  98.0 20.0 %collective-permute-start.36 = (bf16[2,256,256]{2,1,0:T(8,128)(2,1)S(1)}, bf16[2,256,256]{2,1,0:T(8,128)(2,1)S(1)}, u32[]{:S(2)}, u32[]{:S(2)}) collective-permute-start(bf16[2,256,256]{2,1,0:T(8,128)(2,1)S(1)} %pad_maximum_fusion.3), channel_id=1, source_target_pairs={{0,8},{4,12},{8,0},{12,4},{1,9},{5,13},{9,1},{13,5},{2,10},{6,14},... | collective-permute-start | bytes 786440 | tf_op jit(solution)/shard_map/ppermute | solution.py:649
  100.2 17.8 %collective-permute-start.35 = (bf16[2,256,256]{2,1,0:T(8,128)(2,1)S(1)}, bf16[2,256,256]{2,1,0:T(8,128)(2,1)S(1)}, u32[]{:S(2)}, u32[]{:S(2)}) collective-permute-start(bf16[2,256,256]{2,1,0:T(8,128)(2,1)S(1)} %pad_maximum_fusion.2), channel_id=1, source_target_pairs={{0,4},{4,8},{8,12},{12,0},{1,5},{5,9},{9,13},{13,1},{2,6},{6,10},{... | collective-permute-start | bytes 786440 | tf_op jit(solution)/shard_map/ppermute | solution.py:649
  101.7 16.4 %collective-permute-start.32 = (bf16[2,512,128]{2,1,0:T(8,128)(2,1)S(1)}, bf16[2,512,128]{2,1,0:T(8,128)(2,1)S(1)}, u32[]{:S(2)}, u32[]{:S(2)}) collective-permute-start(bf16[2,512,128]{2,1,0:T(8,128)(2,1)S(1)} %get-tuple-element.210), channel_id=1, source_target_pairs={{0,1},{1,0},{2,3},{3,2},{4,5},{5,4},{6,7},{7,6},{8,9},{9,8},{10,11... | collective-permute-start | bytes 786440 | tf_op jit(solution)/shard_map/ppermute | solution.py:54
  102.7 15.4 %collective-permute-start.33 = (bf16[2,512,128]{2,1,0:T(8,128)(2,1)S(1)}, bf16[2,512,128]{2,1,0:T(8,128)(2,1)S(1)}, u32[]{:S(2)}, u32[]{:S(2)}) collective-permute-start(bf16[2,512,128]{2,1,0:T(8,128)(2,1)S(1)} %get-tuple-element.219.refs_2_), channel_id=1, source_target_pairs={{0,16},{1,17},{16,0},{17,1},{2,18},{3,19},{18,2},{19,3},{4,20},{5,... | collective-permute-start | bytes 786440 | tf_op jit(solution)/shard_map/ppermute | solution.py:821
  109.4 10.3 %collective-permute-start.34 = (bf16[2,512,128]{2,1,0:T(8,128)(2,1)S(1)}, bf16[2,512,128]{2,1,0:T(8,128)(2,1)S(1)}, u32[]{:S(2)}, u32[]{:S(2)}) collective-permute-start(bf16[2,512,128]{2,1,0:T(8,128)(2,1)S(1)} %get-tuple-element.210), channel_id=1, source_target_pairs={{0,17},{1,16},{16,1},{17,0},{2,19},{3,18},{18,3},{19,2},{4,21},{5,... | collective-permute-start | bytes 786440 | tf_op jit(solution)/shard_map/ppermute | solution.py:821
  121.1 9.6 %collective-permute-start.39 = (bf16[512,256]{1,0:T(8,128)(2,1)S(1)}, bf16[512,256]{1,0:T(8,128)(2,1)S(1)}, u32[]{:S(2)}, u32[]{:S(2)}) collective-permute-start(bf16[512,256]{1,0:T(8,128)(2,1)S(1)} %maximum_select_fusion.3.refs_0_), channel_id=1, source_target_pairs={{0,4},{4,8},{8,12},{12,0},{1,5},{5,9},{9,13},{13,1},{2,6},{6,10},{... | collective-permute-start | bytes 786440 | tf_op jit(solution)/shard_map/ppermute | solution.py:649
  121.2 9.5 %collective-permute-start.40 = (bf16[512,256]{1,0:T(8,128)(2,1)S(1)}, bf16[512,256]{1,0:T(8,128)(2,1)S(1)}, u32[]{:S(2)}, u32[]{:S(2)}) collective-permute-start(bf16[512,256]{1,0:T(8,128)(2,1)S(1)} %maximum_select_fusion.3.refs_0_), channel_id=1, source_target_pairs={{0,2},{2,0},{1,3},{3,1},{4,6},{6,4},{5,7},{7,5},{8,10},{10,8},{9,1... | collective-permute-start | bytes 786440 | tf_op jit(solution)/shard_map/ppermute | solution.py:649
  135.5 27.1 %collective-permute-start.52 = (bf16[8,256,256]{2,1,0:T(8,128)(2,1)S(1)}, bf16[8,256,256]{2,1,0:T(8,128)(2,1)S(1)}, u32[]{:S(2)}, u32[]{:S(2)}) collective-permute-start(bf16[8,256,256]{2,1,0:T(8,128)(2,1)S(1)} %constant_dynamic-update-slice_fusion.refs_10_.refs_14_.refs_18_.refs_22_.refs_26_.refs_4_.refs_8_., ...), channel_id=1, source_target_pairs={{0,16},{16,0},{1,17},{17,1},{2,18},{18,2},{3,19},{19,3},{4,20},{20... | collective-permute-start | bytes 3145736 | tf_op jit(solution)/shard_map/ppermute | solution.py:649
  136.9 14.4 %collective-permute-start.47 = (bf16[512,256]{1,0:T(8,128)(2,1)S(1)}, bf16[512,256]{1,0:T(8,128)(2,1)S(1)}, u32[]{:S(2)}, u32[]{:S(2)}) collective-permute-start(bf16[512,256]{1,0:T(8,128)(2,1)S(1)} %maximum_select_fusion.4.refs_1_), channel_id=1, source_target_pairs={{0,4},{4,8},{8,12},{12,0},{1,5},{5,9},{9,13},{13,1},{2,6},{6,10},{... | collective-permute-start | bytes 786440 | tf_op jit(solution)/shard_map/ppermute | solution.py:649
  137.2 14.1 %collective-permute-start.48 = (bf16[512,256]{1,0:T(8,128)(2,1)S(1)}, bf16[512,256]{1,0:T(8,128)(2,1)S(1)}, u32[]{:S(2)}, u32[]{:S(2)}) collective-permute-start(bf16[512,256]{1,0:T(8,128)(2,1)S(1)} %maximum_select_fusion.4.refs_1_), channel_id=1, source_target_pairs={{0,2},{2,0},{1,3},{3,1},{4,6},{6,4},{5,7},{7,5},{8,10},{10,8},{9,1... | collective-permute-start | bytes 786440 | tf_op jit(solution)/shard_map/ppermute | solution.py:649
  145.7 11.2 %collective-permute-start.43 = (bf16[512,256]{1,0:T(8,128)(2,1)S(1)}, bf16[512,256]{1,0:T(8,128)(2,1)S(1)}, u32[]{:S(2)}, u32[]{:S(2)}) collective-permute-start(bf16[512,256]{1,0:T(8,128)(2,1)S(1)} %collective-permute-done.41.refs_8_), channel_id=1, source_target_pairs={{0,4},{4,8},{8,12},{12,0},{1,5},{5,9},{9,13},{13,1},{2,6},{6,10},{... | collective-permute-start | bytes 786440 | tf_op jit(solution)/shard_map/ppermute | solution.py:649
  145.7 11.2 %collective-permute-start.44 = (bf16[512,256]{1,0:T(8,128)(2,1)S(1)}, bf16[512,256]{1,0:T(8,128)(2,1)S(1)}, u32[]{:S(2)}, u32[]{:S(2)}) collective-permute-start(bf16[512,256]{1,0:T(8,128)(2,1)S(1)} %collective-permute-done.41.refs_8_), channel_id=1, source_target_pairs={{0,2},{2,0},{1,3},{3,1},{4,6},{6,4},{5,7},{7,5},{8,10},{10,8},{9,1... | collective-permute-start | bytes 786440 | tf_op jit(solution)/shard_map/ppermute | solution.py:649
  151.3 11.2 %collective-permute-start.50 = (bf16[512,256]{1,0:T(8,128)(2,1)S(1)}, bf16[512,256]{1,0:T(8,128)(2,1)S(1)}, u32[]{:S(2)}, u32[]{:S(2)}) collective-permute-start(bf16[512,256]{1,0:T(8,128)(2,1)S(1)} %collective-permute-done.47.refs_5_), channel_id=1, source_target_pairs={{0,4},{4,8},{8,12},{12,0},{1,5},{5,9},{9,13},{13,1},{2,6},{6,10},{... | collective-permute-start | bytes 786440 | tf_op jit(solution)/shard_map/ppermute | solution.py:649
  151.3 11.2 %collective-permute-start.51 = (bf16[512,256]{1,0:T(8,128)(2,1)S(1)}, bf16[512,256]{1,0:T(8,128)(2,1)S(1)}, u32[]{:S(2)}, u32[]{:S(2)}) collective-permute-start(bf16[512,256]{1,0:T(8,128)(2,1)S(1)} %collective-permute-done.47.refs_5_), channel_id=1, source_target_pairs={{0,2},{2,0},{1,3},{3,1},{4,6},{6,4},{5,7},{7,5},{8,10},{10,8},{9,1... | collective-permute-start | bytes 786440 | tf_op jit(solution)/shard_map/ppermute | solution.py:649
  163.0 11.6 %collective-permute-start.49 = (bf16[512,256]{1,0:T(8,128)(2,1)S(1)}, bf16[512,256]{1,0:T(8,128)(2,1)S(1)}, u32[]{:S(2)}, u32[]{:S(2)}) collective-permute-start(bf16[512,256]{1,0:T(8,128)(2,1)S(1)} %collective-permute-done.43.refs_0_), channel_id=1, source_target_pairs={{0,2},{2,0},{1,3},{3,1},{4,6},{6,4},{5,7},{7,5},{8,10},{10,8},{9,1... | collective-permute-start | bytes 786440 | tf_op jit(solution)/shard_map/ppermute | solution.py:649
  (80 other events, 915.5 us)

commit v8 on v7

--- a/solution.py
+++ b/solution.py
@@ -206,20 +206,27 @@
     return lax.rem(tile + tiles - entry // 2, tiles) * outer + lax.rem(mpo + entry % 2, outer)
 
 
-def qkv_kernel(entries, layout, groups, held, first, last, meta, *refs):
+def qkv_kernel(entries, layout, groups, last, meta, *refs):
     refs = list(refs)
     count = len(entries)
     x_refs = take_blocks(refs, count)
-    weight_refs = [refs.pop(0) for _ in range(6 if held else 6 * count)]
-    if not first:
-        acc_in, square_in = refs.pop(0), refs.pop(0)
+    weight_refs = [refs.pop(0) for _ in range(6)]
     if last:
-        head_gains = refs.pop(0)
+        acc_in, square_in, head_gains = refs.pop(0), refs.pop(0), refs.pop(0)
+        fetched, arrived = refs.pop(-3), refs.pop(-2)
+        span = fetched.shape[1]
+        rows = pl.ds(pl.multiple_of(chip_of(meta, *layout, entries[0]) * span, span), span)
+        copies = [
+            pltpu.make_async_copy(weight.at[rows, :], fetched.at[part], arrived.at[part])
+            for part, weight in enumerate(weight_refs)
+        ]
+        for copy in copies:
+            copy.start()
     scaled_ref = refs.pop(-1)
     half, span = scaled_ref.shape
     width = weight_refs[0].shape[1]
     heads = width // HD
-    square = None if first else square_in[...]
+    square = square_in[...] if last else None
     if last:
         acc, outs = [None] * 6, refs
     else:
@@ -237,16 +244,12 @@
             piece = value[:, part * HD : (part + 1) * HD]
             square = piece if square is None else square + piece
         for part in range(6):
-            if held:
-                weight = weight_refs[part][rows, :]
-            else:
-                weight = weight_refs[6 * index + part][...]
-            term = mxu(scaled_ref[...], weight)
-            if index == 0 and not first:
-                term = term + acc_in[part]
             if last:
-                acc[part] = term if index == 0 else acc[part] + term
-            elif index == 0:
+                copies[part].wait()
+                acc[part] = acc_in[part] + mxu(scaled_ref[...], fetched[part])
+                continue
+            term = mxu(scaled_ref[...], weight_refs[part][rows, :])
+            if index == 0:
                 acc_out[part] = term
             else:
                 acc_out[part] += term
@@ -272,41 +275,33 @@
                 q_outs[head][...] = (raw * (head_gains[0:1, :] * HD ** (-0.5))).astype(BF16)
 
 
-def qkv_step(meta, layout, blocks, entries, weights, held, state, head_gains):
+def qkv_step(meta, layout, blocks, entries, weights, state, head_gains):
     span = blocks[0][1].shape[1]
     half = 2 * blocks[0][1].shape[0]
     width = weights[0].shape[1]
     heads = width // HD
-    count, first, last = len(blocks), state is None, head_gains is not None
+    count, last = len(blocks), state is not None
     groups = layout[1] * layout[2]
-    inputs = [p for pieces in blocks for p in pieces]
-    specs = [full(p.shape) for p in inputs]
-    if held:
-        inputs += weights
-        specs += [HELD] * 6
-    else:
-        for entry in entries:
-            inputs += weights
-            index = lambda i, m, entry=entry: (chip_of(m, *layout, entry), 0)
-            specs += [pl.BlockSpec((span, width), index)] * 6
-    if not first:
-        inputs += list(state)
-        specs += [HELD] * 2
+    inputs = [p for pieces in blocks for p in pieces] + list(weights)
+    specs = [full(p.shape) for pieces in blocks for p in pieces]
+    scratch = [pltpu.VMEM((half, span), BF16)]
     if last:
-        inputs.append(head_gains)
-        specs.append(full(head_gains.shape))
+        specs += [pl.BlockSpec(memory_space=pltpu.HBM)] * 6 + [HELD] * 2 + [full(head_gains.shape)]
+        inputs += list(state) + [head_gains]
         kv, q = jax.ShapeDtypeStruct((2, half, HD), BF16), jax.ShapeDtypeStruct((half, HD), BF16)
         outs = ([kv] * heads + [q] * heads) * 2
+        scratch = [pltpu.VMEM((6, span, width), BF16), pltpu.SemaphoreType.DMA((6,))] + scratch
     else:
+        specs += [HELD] * 6
         outs = [pltpu.VMEM((6, half, width), F32), pltpu.VMEM((half, HD), F32)]
     return pl.pallas_call(
-        functools.partial(qkv_kernel, entries, layout, groups, held, first, last),
+        functools.partial(qkv_kernel, entries, layout, groups, last),
         grid_spec=pltpu.PrefetchScalarGridSpec(
             num_scalar_prefetch=1,
             grid=(1,),
             in_specs=specs,
             out_specs=[full(o.shape) if last else HELD for o in outs],
-            scratch_shapes=[pltpu.VMEM((half, span), BF16)],
+            scratch_shapes=scratch,
         ),
         out_shape=outs,
         compiler_params=params(20),
@@ -654,7 +649,7 @@
     every = jnp.concatenate([latents] + [shift(latents, "ctx", s) for s in range(1, ctxs)])
     conv = by_core(lax.axis_index("core"), down_conv, swap(down_conv), 1)
     conv = by_core(lax.axis_index("mpo"), conv, shift(conv, "mpo", 1), 1)
-    every, conv, others = lax.optimization_barrier((every, conv, others))
+    every, others = lax.optimization_barrier((every, others))
     return [every] + [shift(every, "tile", s) for s in range(1, tiles)], conv, *others
 
 
@@ -713,25 +708,24 @@
         else:
             moving[which] = shift(ring, "mpo", 1)
 
-    def work(entries, state):
-        return step([[found[0][e], found[1][e]] for e in entries], entries, state, False)
-
     launch(0, 0)
     late = callable(second)
     if late:
+        second, extras = second()
         events = [(0, 1), (0, 2)]
         for index in range(1, tiles - 2):
             events += [(1, index), (0, index + 2)]
         events += [(1, tiles - 2), (1, tiles - 1)]
     else:
-        found[1][0] = second
+        events = [(which, index) for index in range(1, tiles) for which in range(2)]
+    found[1][0] = second
+    if not late:
         launch(1, 0)
-        events = [(which, index) for index in range(1, tiles) for which in range(2)]
     seen = first
     for which, index in events:
         ring, cross = moving[which]
-        if (which, index) == (int(late), tiles - 1):
-            ring, cross, seen, state = lax.optimization_barrier((ring, cross, seen, state))
+        if late and (which, index) == (0, 1):
+            ring, cross, found[1][0] = lax.optimization_barrier((ring, cross, second))
         elif late and (which, index) == (1, tiles - 2):
             ring, cross, seen, extras = lax.optimization_barrier((ring, cross, seen, extras))
         else:
@@ -740,11 +734,9 @@
         seen = ring
         launch(which, index)
         if late and (which, index) == (0, 1):
-            found[1][0], extras = second(cross)
             launch(1, 0)
-        if (which, index) == (1, tiles - 2):
-            state = work(list(range(2 * tiles - 3)), state)
-    state = work([2 * tiles - 2, 2 * tiles - 3], state)
+    entries = list(range(2 * tiles - 1))
+    state = step([[found[0][e], found[1][e]] for e in entries], entries, state, False)
     last = lax.optimization_barrier((moving[0], moving[1], state, extras))
     return step([[last[0], last[1]]], [2 * tiles - 1], last[2], True), last[3]
 
@@ -799,16 +791,13 @@
     head_gains = jnp.stack([query_gain, key_gain])
 
     def project(blocks, entries, state, last):
-        held = state is None
         return qkv_step(
-            meta, layout, blocks, entries, held_weights if held else weights, held, state, head_gains if last else None
+            meta, layout, blocks, entries, weights if last else held_weights, state, head_gains
         )
 
     state, out_par = gather_pair(
         *[by_core(core, s[0], o, 1) for s, o in zip(streams, others)], None, project, swap(out_weight)
     )
-    state, kept, received = lax.optimization_barrier((state, kept, received))
-    up_blocks = [transpose_second(kept, received, step) for step in range(tiles)]
     kv_send, q_send = state[:heads], state[heads : 2 * heads]
     kv_own, q_own = state[2 * heads : 3 * heads], state[3 * heads :]
 
@@ -831,8 +820,14 @@
         (att_own, att_send), ahead = lax.optimization_barrier((result, ahead))
         return by_core(core, att_own, swap(att_send), 1), ahead
 
-    attended, (pieces, up_blocks) = attend(
-        0, pieces_of(0), (pieces_of(1) if heads > 1 else None, up_blocks)
+    pieces = pieces_of(0)
+    pieces[0], q_send, kv_own, kv_send, kept, received = lax.optimization_barrier(
+        (pieces[0], q_send, kv_own, kv_send, kept, received)
+    )
+    up_blocks = [transpose_second(kept, received, step) for step in range(tiles)]
+    pieces, up_blocks[tiles // 2] = lax.optimization_barrier((pieces, up_blocks[tiles // 2]))
+    attended, (other_pieces, up_blocks) = attend(
+        0, pieces, (pieces_of(1) if heads > 1 else None, up_blocks)
     )
     if heads == 1:
         attended, second = attended[: half // 2], attended[half // 2 :]
@@ -841,11 +836,11 @@
     else:
         extras = None
 
-        def second(token):
-            result, (up, _) = attend(1, pieces, (up_blocks, token))
+        def second():
+            pieces, _ = lax.optimization_barrier((other_pieces, attended))
+            result, up = attend(1, pieces, up_blocks)
             own = jnp.concatenate(up)
-            result, own, par = lax.optimization_barrier((result, own, swap(own)))
-            return result, [own, par] + ([shift(own, "ctx", 1)] if halves == 2 else [])
+            return result, [own, swap(own)] + ([shift(own, "ctx", 1)] if halves == 2 else [])
 
     def project_out(blocks, entries, state, last):
         return out_step(meta, layout, blocks, entries, (out_weight, out_par), state, last)

time: 245 us -> 250 us (1.020)
  starting transfers between devices: 62 us -> 73.5 us
  local copies, waits for them, and re-layouts: 19.1 us -> 16 us
  waiting for transfers between devices: 110 us -> 107 us
    ppermute x55, starting transfers between devices: 35.6 us -> 45.1 us  [shift(): lax.ppermute(values, axis, [(i, (i + step) % count) for i in range(count)])]
    ppermute x55, waiting for transfers between devices: 89.2 us -> 83.6 us  [shift(): lax.ppermute(values, axis, [(i, (i + step) % count) for i in range(count)])]
    ppermute x6, waiting for transfers between devices: 13.3 us -> 18.2 us  [shifted(): return lax.ppermute(values, ('ctx', 'core'), pairs)]
    unnamed x66 -> x74, local copies, waits for them, and re-layouts: 16.7 us -> 12.5 us
    pallas_call x3 -> x2, Pallas kernels: 7.57 us -> 6.02 us  [out_step(): pl.pallas_call(functools.partial(out_kernel, count, heads, first, last),...]
    pallas_call x3 -> x2, Pallas kernels: 13.6 us -> 12.2 us  [qkv_step(): pl.pallas_call(functools.partial(qkv_kernel, entries, layout, groups, las...]
  transfers between devices with their start and end apart: 81 -> 81, of which waited for: 36 -> 32; matrix products, arithmetic and copies ran while one was open for 3% -> 4% of each run, Pallas kernels for 17% -> 16%
where the time goes in v8:
time: 250 us; the launch traced here: 249 us
  waiting for transfers between devices  107 us (43%)
  starting transfers between devices  73.5 us (29%)
  Pallas kernels  45.7 us (18%)
  local copies, waits for them, and re-layouts  16 us (6%)
  other arithmetic  4.55 us (2%)
    ppermute x55, waiting for transfers between devices, shift(): lax.ppermute(values, axis, [(i, (i + step) % count) for i in range(count)])  83.6 us
    ppermute x55, starting transfers between devices, shift(): lax.ppermute(values, axis, [(i, (i + step) % count) for i in range(count)])  45.1 us
    ppermute x6, waiting for transfers between devices, shifted(): return lax.ppermute(values, ('ctx', 'core'), pairs)  18.2 us
    ppermute x17, starting transfers between devices, swap(): return lax.ppermute(values, 'core', [(0, 1), (1, 0)])  14.5 us
    unnamed x74, local copies, waits for them, and re-layouts  12.5 us
    pallas_call x2, Pallas kernels, qkv_step(): pl.pallas_call(functools.partial(qkv_kernel, entries, layout, groups, las...  12.2 us
    pallas_call x2, Pallas kernels, attention(): pl.pallas_call(functools.partial(attention_kernel, images, len(pieces), h...  9.73 us
    pallas_call x1, Pallas kernels, down_stream(): pl.pallas_call(functools.partial(down_kernel, images, tiles, half), grid_...  9.57 us
  transfers between devices with their start and end apart: 81, of which 32 were waited for; matrix products, arithmetic and copies ran while one was open for 4% of the time, Pallas kernels for 16%

profile of v8, /device:TPU:1, one launch (start us, length us, event | category | flops | bytes accessed | tf_op | source)
XLA Modules:
  0.0 248.8 jit_solution(12038322661335420525)
XLA Ops:
  1.3 2.7 %collective-permute-start = (bf16[2,16,512]{2,1,0:T(8,128)(2,1)}, bf16[2,16,512]{2,1,0:T(8,128)(2,1)S(1)}, u32[]{:S(2)}, u32[]{:S(2)}) collective-permute-start(bf16[2,16,512]{2,1,0:T(8,128)(2,1)} %param.16), channel_id=1, source_target_pairs={{0,16},{16,0},{1,17},{17,1},{2,18},{18,2},{3,19},{19,3},{4,20},{20... | collective-permute-start | bytes 98312 | tf_op jit(solution)/shard_map/ppermute | solution.py:644
  25.1 9.6 %down_stream.1 = (bf16[2,272,256]{2,1,0:T(8,128)(2,1)S(1)}, bf16[2,256,256]{2,1,0:T(8,128)(2,1)S(1)}, bf16[4096,256]{1,0:T(8,128)(2,1)S(1)}, bf16[4096,256]{1,0:...) custom-call(s32[16]{0:T(128)S(1)} %concatenate.60.meta, ...), custom_call_target="tpu_custom_call" | custom-call | flops 4294967296 | bytes 4194304 | tf_op jit(solution)/shard_map/down_stream/pallas_call | solution.py:160
  41.0 7.1 %collective-permute-done.12.refs_4_ = bf16[272,512]{1,0:T(8,128)(2,1)S(1)} collective-permute-done((bf16[272,512]{1,0:T(8,128)(2,1)S(1)}, bf16[272,512]{1,0:T(8,128)(2,1)S(1)}, u32[]{:S(2)}, u32[]{:S(2)}) %collective-permute-start.12) | collective-permute-done | bytes 278560 | tf_op jit(solution)/shard_map/ppermute | solution.py:644
  49.2 4.5 %collective-permute-done.16.refs_5_ = bf16[256,512]{1,0:T(8,128)(2,1)S(1)} collective-permute-done((bf16[256,512]{1,0:T(8,128)(2,1)S(1)}, bf16[256,512]{1,0:T(8,128)(2,1)S(1)}, u32[]{:S(2)}, u32[]{:S(2)}) %collective-permute-start.16) | collective-permute-done | bytes 262176 | tf_op jit(solution)/shard_map/ppermute | solution.py:644
  54.7 4.9 %collective-permute-done.14.refs_8_ = bf16[272,512]{1,0:T(8,128)(2,1)S(1)} collective-permute-done((bf16[272,512]{1,0:T(8,128)(2,1)S(1)}, bf16[272,512]{1,0:T(8,128)(2,1)S(1)}, u32[]{:S(2)}, u32[]{:S(2)}) %collective-permute-start.14) | collective-permute-done | bytes 278560 | tf_op jit(solution)/shard_map/ppermute | solution.py:644
  60.7 4.6 %collective-permute-done.20.refs_9_ = bf16[256,512]{1,0:T(8,128)(2,1)S(1)} collective-permute-done((bf16[256,512]{1,0:T(8,128)(2,1)S(1)}, bf16[256,512]{1,0:T(8,128)(2,1)S(1)}, u32[]{:S(2)}, u32[]{:S(2)}) %collective-permute-start.20) | collective-permute-done | bytes 262176 | tf_op jit(solution)/shard_map/ppermute | solution.py:644
  66.3 4.9 %collective-permute-done.18.refs_12_ = bf16[272,512]{1,0:T(8,128)(2,1)S(1)} collective-permute-done((bf16[272,512]{1,0:T(8,128)(2,1)S(1)}, bf16[272,512]{1,0:T(8,128)(2,1)S(1)}, u32[]{:S(2)}, u32[]{:S(2)}) %collective-permute-start.18) | collective-permute-done | bytes 278560 | tf_op jit(solution)/shard_map/ppermute | solution.py:644
  72.3 4.6 %collective-permute-done.23.refs_13_ = bf16[256,512]{1,0:T(8,128)(2,1)S(1)} collective-permute-done((bf16[256,512]{1,0:T(8,128)(2,1)S(1)}, bf16[256,512]{1,0:T(8,128)(2,1)S(1)}, u32[]{:S(2)}, u32[]{:S(2)}) %collective-permute-start.23) | collective-permute-done | bytes 262176 | tf_op jit(solution)/shard_map/ppermute | solution.py:644
  76.9 7.6 %qkv_step.1 = (f32[6,512,256]{2,1,0:T(8,128)S(1)}, f32[512,128]{1,0:T(8,128)S(1)}) custom-call(s32[16]{0:T(128)S(1)} %concatenate.60.meta, bf16[272,512]{1,0:T(8,128)(2,1)S(1)} %maximum_select_fusion.1.refs_0_, bf16[256,512]{1,0:T(8,128)(2,1)S(1)} %maximum_select_fusion.2.refs_1_, bf16[272,512]{1,0:T(8,128)(2,1)S(1)} %collective-permute-done.13.refs_2_, ...), custom_call_target="tpu_custom_call" | custom-call | flops 5637144576 | bytes 20971520 | tf_op jit(solution)/shard_map/qkv_step/pallas_call | solution.py:297
  85.3 4.6 %qkv_last.1 = (bf16[2,512,128]{2,1,0:T(8,128)(2,1)S(1)}, bf16[2,512,128]{2,1,0:T(8,128)(2,1)S(1)}, bf16[512,128]{1,0:T(8,128)(2,1)}, bf16[512,128]{1,0:T(8,128)(...) custom-call(s32[16]{0:T(128)S(1)} %concatenate.60.meta, ...), custom_call_target="tpu_custom_call" | custom-call | flops 805306368 | bytes 8388608 | tf_op jit(solution)/shard_map/qkv_last/pallas_call | solution.py:297
  101.2 8.0 %collective-permute-done.29.refs_4_ = bf16[2,512,128]{2,1,0:T(8,128)(2,1)S(1)} collective-permute-done((bf16[2,512,128]{2,1,0:T(8,128)(2,1)}, bf16[2,512,128]{2,1,0:T(8,128)(2,1)S(1)}, u32[]{:S(2)}, u32[]{:S(2)}) %collective-permute-start.29) | collective-permute-done | bytes 262176 | tf_op jit(solution)/shard_map/ppermute | solution.py:810
  114.7 5.3 %attention.2 = (bf16[512,128]{1,0:T(8,128)(2,1)S(1)}, bf16[512,128]{1,0:T(8,128)(2,1)S(1)}) custom-call(s32[16]{0:T(128)S(1)} %concatenate.60.meta, bf16[512,128]{1,0:T(8,128)(2,1)S(1)} %copy-done.23, bf16[512,128]{1,0:T(8,128)(2,1)} %collective-permute-done.27.refs_1_, bf16[2,512,128]{2,1,0:T(8,128)(2,1)S(1)} %copy-done.20, ...), custom_call_target="tpu_custom_call" | custom-call | flops 1073741824 | bytes 1048576 | tf_op jit(solution)/shard_map/attention/pallas_call | solution.py:355
  120.0 4.1 %collective-permute-done.35.refs_5_ = bf16[2,512,128]{2,1,0:T(8,128)(2,1)S(1)} collective-permute-done((bf16[2,512,128]{2,1,0:T(8,128)(2,1)S(1)}, bf16[2,512,128]{2,1,0:T(8,128)(2,1)S(1)}, u32[]{:S(2)}, u32[]{:S(2)}) %collective-permute-start.35) | collective-permute-done | bytes 262176 | tf_op jit(solution)/shard_map/ppermute | solution.py:810
  125.6 2.8 %collective-permute-start.39 = (bf16[512,256]{1,0:T(8,128)(2,1)S(1)}, bf16[512,256]{1,0:T(8,128)(2,1)S(1)}, u32[]{:S(2)}, u32[]{:S(2)}) collective-permute-start(bf16[512,256]{1,0:T(8,128)(2,1)S(1)} %maximum_select_fusion.3.refs_0_), channel_id=1, source_target_pairs={{0,4},{4,8},{8,12},{12,0},{1,5},{5,9},{9,13},{13,1},{2,6},{6,10},{... | collective-permute-start | bytes 786440 | tf_op jit(solution)/shard_map/ppermute | solution.py:644
  129.4 4.5 %attention.3 = (bf16[512,128]{1,0:T(8,128)(2,1)S(1)}, bf16[512,128]{1,0:T(8,128)(2,1)S(1)}) custom-call(s32[16]{0:T(128)S(1)} %concatenate.60.meta, bf16[512,128]{1,0:T(8,128)(2,1)S(1)} %get-tuple-element.210.refs_0_, bf16[512,128]{1,0:T(8,128)(2,1)S(1)} %collective-permute-done.32.refs_1_, bf16[2,512,128]{2,1,0:T(8,128)(2,1)S(1)} %get-tuple-element.217.refs_2_, ...), custom_call_target="tpu_custom_call" | custom-call | flops 1073741824 | bytes 1048576 | tf_op jit(solution)/shard_map/attention/pallas_call | solution.py:355
  138.6 2.9 %collective-permute-start.46 = (bf16[512,256]{1,0:T(8,128)(2,1)S(1)}, bf16[512,256]{1,0:T(8,128)(2,1)S(1)}, u32[]{:S(2)}, u32[]{:S(2)}) collective-permute-start(bf16[512,256]{1,0:T(8,128)(2,1)S(1)} %maximum_select_fusion.4.refs_1_), channel_id=1, source_target_pairs={{0,4},{4,8},{8,12},{12,0},{1,5},{5,9},{9,13},{13,1},{2,6},{6,10},{... | collective-permute-start | bytes 786440 | tf_op jit(solution)/shard_map/ppermute | solution.py:644
  141.5 5.0 %collective-permute-done.42.refs_8_ = bf16[512,256]{1,0:T(8,128)(2,1)S(1)} collective-permute-done((bf16[512,256]{1,0:T(8,128)(2,1)S(1)}, bf16[512,256]{1,0:T(8,128)(2,1)S(1)}, u32[]{:S(2)}, u32[]{:S(2)}) %collective-permute-start.42) | collective-permute-done | bytes 262176 | tf_op jit(solution)/shard_map/ppermute | solution.py:644
  148.3 3.9 %collective-permute-done.46.refs_5_ = bf16[512,256]{1,0:T(8,128)(2,1)S(1)} collective-permute-done((bf16[512,256]{1,0:T(8,128)(2,1)S(1)}, bf16[512,256]{1,0:T(8,128)(2,1)S(1)}, u32[]{:S(2)}, u32[]{:S(2)}) %collective-permute-start.46) | collective-permute-done | bytes 262176 | tf_op jit(solution)/shard_map/ppermute | solution.py:644
  153.0 3.6 %collective-permute-done.44.refs_12_ = bf16[512,256]{1,0:T(8,128)(2,1)S(1)} collective-permute-done((bf16[512,256]{1,0:T(8,128)(2,1)S(1)}, bf16[512,256]{1,0:T(8,128)(2,1)S(1)}, u32[]{:S(2)}, u32[]{:S(2)}) %collective-permute-start.44) | collective-permute-done | bytes 262176 | tf_op jit(solution)/shard_map/ppermute | solution.py:644
  158.3 4.0 %collective-permute-done.49.refs_9_ = bf16[512,256]{1,0:T(8,128)(2,1)S(1)} collective-permute-done((bf16[512,256]{1,0:T(8,128)(2,1)S(1)}, bf16[512,256]{1,0:T(8,128)(2,1)S(1)}, u32[]{:S(2)}, u32[]{:S(2)}) %collective-permute-start.49) | collective-permute-done | bytes 262176 | tf_op jit(solution)/shard_map/ppermute | solution.py:644
  166.6 5.3 %collective-permute-done.53.refs_13_ = bf16[512,256]{1,0:T(8,128)(2,1)S(1)} collective-permute-done((bf16[512,256]{1,0:T(8,128)(2,1)S(1)}, bf16[512,256]{1,0:T(8,128)(2,1)S(1)}, u32[]{:S(2)}, u32[]{:S(2)}) %collective-permute-start.53) | collective-permute-done | bytes 262176 | tf_op jit(solution)/shard_map/ppermute | solution.py:644
  172.1 4.1 %out_step.1.refs_4_ = f32[2,512,256]{2,1,0:T(8,128)S(1)} custom-call(s32[16]{0:T(128)S(1)} %concatenate.60.meta, bf16[512,256]{1,0:T(8,128)(2,1)S(1)} %maximum_select_fusion.3.refs_0_, bf16[512,256]{1,0:T(8,128)(2,1)S(1)} %maximum_select_fusion.4.refs_1_, bf16[512,256]{1,0:T(8,128)(2,1)S(1)} %collective-permute-done.40.refs_2_, ...), custom_call_target="tpu_custom_call" | custom-call | flops 1879048192 | bytes 9437184 | tf_op jit(solution)/shard_map/out_step/pallas_call | solution.py:425
  176.2 2.7 %collective-permute-done.55.refs_1_ = bf16[512,256]{1,0:T(8,128)(2,1)S(1)} collective-permute-done((bf16[512,256]{1,0:T(8,128)(2,1)S(1)}, bf16[512,256]{1,0:T(8,128)(2,1)S(1)}, u32[]{:S(2)}, u32[]{:S(2)}) %collective-permute-start.55) | collective-permute-done | bytes 262176 | tf_op jit(solution)/shard_map/ppermute | solution.py:644
  178.9 5.8 %collective-permute-start.57 = (bf16[8,256,256]{2,1,0:T(8,128)(2,1)S(1)}, bf16[8,256,256]{2,1,0:T(8,128)(2,1)S(1)}, u32[]{:S(2)}, u32[]{:S(2)}) collective-permute-start(bf16[8,256,256]{2,1,0:T(8,128)(2,1)S(1)} %collective-permute-done.52.refs_16_.refs_20_.refs_24_.refs_28_.refs_32_.refs_36_.refs_40_.refs_4_), channel_id=1, source_target_pairs={{0,1},{1,0},{2,3},{3,2},{4,5},{5,4},{6,7},{7,6},{8,9},{9,8},{10,11... | collective-permute-start | bytes 3145736 | tf_op jit(solution)/shard_map/ppermute | solution.py:54
  192.4 3.1 %collective-permute-done.58.refs_1_ = bf16[256,256]{1,0:T(8,128)(2,1)S(1)} collective-permute-done((bf16[256,256]{1,0:T(8,128)(2,1)S(1)}, bf16[256,256]{1,0:T(8,128)(2,1)S(1)}, u32[]{:S(2)}, u32[]{:S(2)}) %collective-permute-start.58) | collective-permute-done | bytes 131104 | tf_op jit(solution)/shard_map/ppermute | solution.py:810
  195.5 3.1 %collective-permute-done.60.refs_3_ = bf16[256,256]{1,0:T(8,128)(2,1)S(1)} collective-permute-done((bf16[256,256]{1,0:T(8,128)(2,1)S(1)}, bf16[256,256]{1,0:T(8,128)(2,1)S(1)}, u32[]{:S(2)}, u32[]{:S(2)}) %collective-permute-start.60) | collective-permute-done | bytes 131104 | tf_op jit(solution)/shard_map/ppermute | solution.py:810
  200.7 4.8 %collective-permute-done.61.refs_4_ = bf16[128,512]{1,0:T(8,128)(2,1)} collective-permute-done((bf16[128,512]{1,0:T(8,128)(2,1)S(1)}, bf16[128,512]{1,0:T(8,128)(2,1)}, u32[]{:S(2)}, u32[]{:S(2)}) %collective-permute-start.61) | collective-permute-done | bytes 131104 | tf_op jit(solution)/shard_map/ppermute | solution.py:644
  205.5 2.8 %collective-permute-done.65.refs_5_ = bf16[128,512]{1,0:T(8,128)(2,1)} collective-permute-done((bf16[128,512]{1,0:T(8,128)(2,1)S(1)}, bf16[128,512]{1,0:T(8,128)(2,1)}, u32[]{:S(2)}, u32[]{:S(2)}) %collective-permute-start.65) | collective-permute-done | bytes 131104 | tf_op jit(solution)/shard_map/ppermute | solution.py:644
  209.9 7.3 %collective-permute-done.63.refs_8_ = bf16[128,512]{1,0:T(8,128)(2,1)S(1)} collective-permute-done((bf16[128,512]{1,0:T(8,128)(2,1)}, bf16[128,512]{1,0:T(8,128)(2,1)S(1)}, u32[]{:S(2)}, u32[]{:S(2)}) %collective-permute-start.63) | collective-permute-done | bytes 131104 | tf_op jit(solution)/shard_map/ppermute | solution.py:644
  219.3 5.7 %collective-permute-done.67.refs_12_ = bf16[128,512]{1,0:T(8,128)(2,1)S(1)} collective-permute-done((bf16[128,512]{1,0:T(8,128)(2,1)S(1)}, bf16[128,512]{1,0:T(8,128)(2,1)S(1)}, u32[]{:S(2)}, u32[]{:S(2)}) %collective-permute-start.67) | collective-permute-done | bytes 131104 | tf_op jit(solution)/shard_map/ppermute | solution.py:644
  229.2 2.7 %collective-permute-done.74.refs_1_ = bf16[128,512]{1,0:T(8,128)(2,1)S(1)} collective-permute-done((bf16[128,512]{1,0:T(8,128)(2,1)S(1)}, bf16[128,512]{1,0:T(8,128)(2,1)S(1)}, u32[]{:S(2)}, u32[]{:S(2)}) %collective-permute-start.74) | collective-permute-done | bytes 131104 | tf_op jit(solution)/shard_map/ppermute | solution.py:644
  238.3 5.9 %collective-permute-start.79 = (f32[64,128]{1,0:T(8,128)S(1)}, f32[64,128]{1,0:T(8,128)S(1)}, u32[]{:S(2)}, u32[]{:S(2)}) collective-permute-start(f32[64,128]{1,0:T(8,128)S(1)} %fusion.25.own_a), channel_id=1, source_target_pairs={{0,1},{1,0},{2,3},{3,2},{4,5},{5,4},{6,7},{7,6},{8,9},{9,8},{10,11... | collective-permute-start | bytes 98312 | tf_op jit(solution)/shard_map/ppermute | solution.py:883
  (254 shorter events, 95.2 us)
Async XLA Ops:
  1.2 20.7 %collective-permute-start.8 = (bf16[4096,256]{1,0:T(8,128)(2,1)}, bf16[4096,256]{1,0:T(8,128)(2,1)}, u32[]{:S(2)}, u32[]{:S(2)}) collective-permute-start(bf16[4096,256]{1,0:T(8,128)(2,1)} %refs_7_.1), channel_id=1, source_target_pairs={{0,1},{1,0},{2,3},{3,2},{4,5},{5,4},{6,7},{7,6},{8,9},{9,8},{10,11... | collective-permute-start | bytes 6291464 | tf_op jit(solution)/shard_map/ppermute | solution.py:54
  4.8 9.7 %collective-permute-start.6 = (bf16[72,64]{1,0:T(8,128)(2,1)S(1)}, bf16[72,64]{1,0:T(8,128)(2,1)S(1)}, u32[]{:S(2)}, u32[]{:S(2)}) collective-permute-start(bf16[72,64]{1,0:T(8,128)(2,1)S(1)} %copy.21), channel_id=1, source_target_pairs={{0,1},{1,0},{2,3},{3,2},{4,5},{5,4},{6,7},{7,6},{8,9},{9,8},{10,11... | collective-permute-start | bytes 27656 | tf_op jit(solution)/shard_map/ppermute | solution.py:54
  19.6 15.0 %collective-permute-start.9 = (bf16[4,256,256]{2,1,0:T(8,128)(2,1)}, bf16[4,256,256]{2,1,0:T(8,128)(2,1)}, u32[]{:S(2)}, u32[]{:S(2)}) collective-permute-start(bf16[4,256,256]{2,1,0:T(8,128)(2,1)} %get-tuple-element.156), channel_id=1, source_target_pairs={{0,2},{2,0},{1,3},{3,1},{4,6},{6,4},{5,7},{7,5},{8,10},{10,8},{9,1... | collective-permute-start | bytes 1572872 | tf_op jit(solution)/shard_map/ppermute | solution.py:644
  20.2 64.3 %collective-permute-start.26 = (bf16[4096,256]{1,0:T(8,128)(2,1)S(1)}, bf16[4096,256]{1,0:T(8,128)(2,1)}, u32[]{:S(2)}, u32[]{:S(2)}) collective-permute-start(bf16[4096,256]{1,0:T(8,128)(2,1)S(1)} %copy-done.1), channel_id=1, source_target_pairs={{0,1},{1,0},{2,3},{3,2},{4,5},{5,4},{6,7},{7,6},{8,9},{9,8},{10,11... | collective-permute-start | bytes 6291464 | tf_op jit(solution)/shard_map/ppermute | solution.py:54
  38.4 9.7 %collective-permute-start.12 = (bf16[272,512]{1,0:T(8,128)(2,1)S(1)}, bf16[272,512]{1,0:T(8,128)(2,1)S(1)}, u32[]{:S(2)}, u32[]{:S(2)}) collective-permute-start(bf16[272,512]{1,0:T(8,128)(2,1)S(1)} %maximum_select_fusion.1.refs_0_), channel_id=1, source_target_pairs={{0,4},{4,8},{8,12},{12,0},{1,5},{5,9},{9,13},{13,1},{2,6},{6,10},{... | collective-permute-start | bytes 835592 | tf_op jit(solution)/shard_map/ppermute | solution.py:644
  40.0 13.8 %collective-permute-start.16 = (bf16[256,512]{1,0:T(8,128)(2,1)S(1)}, bf16[256,512]{1,0:T(8,128)(2,1)S(1)}, u32[]{:S(2)}, u32[]{:S(2)}) collective-permute-start(bf16[256,512]{1,0:T(8,128)(2,1)S(1)} %maximum_select_fusion.2.refs_1_), channel_id=1, source_target_pairs={{0,4},{4,8},{8,12},{12,0},{1,5},{5,9},{9,13},{13,1},{2,6},{6,10},{... | collective-permute-start | bytes 786440 | tf_op jit(solution)/shard_map/ppermute | solution.py:644
  40.1 13.6 %collective-permute-start.17 = (bf16[256,512]{1,0:T(8,128)(2,1)S(1)}, bf16[256,512]{1,0:T(8,128)(2,1)S(1)}, u32[]{:S(2)}, u32[]{:S(2)}) collective-permute-start(bf16[256,512]{1,0:T(8,128)(2,1)S(1)} %maximum_select_fusion.2.refs_1_), channel_id=1, source_target_pairs={{0,2},{2,0},{1,3},{3,1},{4,6},{6,4},{5,7},{7,5},{8,10},{10,8},{9,1... | collective-permute-start | bytes 786440 | tf_op jit(solution)/shard_map/ppermute | solution.py:644
  48.1 11.6 %collective-permute-start.14 = (bf16[272,512]{1,0:T(8,128)(2,1)S(1)}, bf16[272,512]{1,0:T(8,128)(2,1)S(1)}, u32[]{:S(2)}, u32[]{:S(2)}) collective-permute-start(bf16[272,512]{1,0:T(8,128)(2,1)S(1)} %collective-permute-done.12.refs_4_), channel_id=1, source_target_pairs={{0,4},{4,8},{8,12},{12,0},{1,5},{5,9},{9,13},{13,1},{2,6},{6,10},{... | collective-permute-start | bytes 835592 | tf_op jit(solution)/shard_map/ppermute | solution.py:644
  48.1 11.6 %collective-permute-start.15 = (bf16[272,512]{1,0:T(8,128)(2,1)S(1)}, bf16[272,512]{1,0:T(8,128)(2,1)S(1)}, u32[]{:S(2)}, u32[]{:S(2)}) collective-permute-start(bf16[272,512]{1,0:T(8,128)(2,1)S(1)} %collective-permute-done.12.refs_4_), channel_id=1, source_target_pairs={{0,2},{2,0},{1,3},{3,1},{4,6},{6,4},{5,7},{7,5},{8,10},{10,8},{9,1... | collective-permute-start | bytes 835592 | tf_op jit(solution)/shard_map/ppermute | solution.py:644
  53.7 11.6 %collective-permute-start.20 = (bf16[256,512]{1,0:T(8,128)(2,1)S(1)}, bf16[256,512]{1,0:T(8,128)(2,1)S(1)}, u32[]{:S(2)}, u32[]{:S(2)}) collective-permute-start(bf16[256,512]{1,0:T(8,128)(2,1)S(1)} %collective-permute-done.16.refs_5_), channel_id=1, source_target_pairs={{0,4},{4,8},{8,12},{12,0},{1,5},{5,9},{9,13},{13,1},{2,6},{6,10},{... | collective-permute-start | bytes 786440 | tf_op jit(solution)/shard_map/ppermute | solution.py:644
  53.7 11.6 %collective-permute-start.21 = (bf16[256,512]{1,0:T(8,128)(2,1)S(1)}, bf16[256,512]{1,0:T(8,128)(2,1)S(1)}, u32[]{:S(2)}, u32[]{:S(2)}) collective-permute-start(bf16[256,512]{1,0:T(8,128)(2,1)S(1)} %collective-permute-done.16.refs_5_), channel_id=1, source_target_pairs={{0,2},{2,0},{1,3},{3,1},{4,6},{6,4},{5,7},{7,5},{8,10},{10,8},{9,1... | collective-permute-start | bytes 786440 | tf_op jit(solution)/shard_map/ppermute | solution.py:644
  59.7 11.6 %collective-permute-start.18 = (bf16[272,512]{1,0:T(8,128)(2,1)S(1)}, bf16[272,512]{1,0:T(8,128)(2,1)S(1)}, u32[]{:S(2)}, u32[]{:S(2)}) collective-permute-start(bf16[272,512]{1,0:T(8,128)(2,1)S(1)} %collective-permute-done.14.refs_8_), channel_id=1, source_target_pairs={{0,4},{4,8},{8,12},{12,0},{1,5},{5,9},{9,13},{13,1},{2,6},{6,10},{... | collective-permute-start | bytes 835592 | tf_op jit(solution)/shard_map/ppermute | solution.py:644
  59.7 11.6 %collective-permute-start.19 = (bf16[272,512]{1,0:T(8,128)(2,1)S(1)}, bf16[272,512]{1,0:T(8,128)(2,1)S(1)}, u32[]{:S(2)}, u32[]{:S(2)}) collective-permute-start(bf16[272,512]{1,0:T(8,128)(2,1)S(1)} %collective-permute-done.14.refs_8_), channel_id=1, source_target_pairs={{0,2},{2,0},{1,3},{3,1},{4,6},{6,4},{5,7},{7,5},{8,10},{10,8},{9,1... | collective-permute-start | bytes 835592 | tf_op jit(solution)/shard_map/ppermute | solution.py:644
  65.3 11.6 %collective-permute-start.23 = (bf16[256,512]{1,0:T(8,128)(2,1)S(1)}, bf16[256,512]{1,0:T(8,128)(2,1)S(1)}, u32[]{:S(2)}, u32[]{:S(2)}) collective-permute-start(bf16[256,512]{1,0:T(8,128)(2,1)S(1)} %collective-permute-done.20.refs_9_), channel_id=1, source_target_pairs={{0,4},{4,8},{8,12},{12,0},{1,5},{5,9},{9,13},{13,1},{2,6},{6,10},{... | collective-permute-start | bytes 786440 | tf_op jit(solution)/shard_map/ppermute | solution.py:644
  65.3 11.6 %collective-permute-start.24 = (bf16[256,512]{1,0:T(8,128)(2,1)S(1)}, bf16[256,512]{1,0:T(8,128)(2,1)S(1)}, u32[]{:S(2)}, u32[]{:S(2)}) collective-permute-start(bf16[256,512]{1,0:T(8,128)(2,1)S(1)} %collective-permute-done.20.refs_9_), channel_id=1, source_target_pairs={{0,2},{2,0},{1,3},{3,1},{4,6},{6,4},{5,7},{7,5},{8,10},{10,8},{9,1... | collective-permute-start | bytes 786440 | tf_op jit(solution)/shard_map/ppermute | solution.py:644
  71.3 14.0 %collective-permute-start.22 = (bf16[272,512]{1,0:T(8,128)(2,1)S(1)}, bf16[272,512]{1,0:T(8,128)(2,1)S(1)}, u32[]{:S(2)}, u32[]{:S(2)}) collective-permute-start(bf16[272,512]{1,0:T(8,128)(2,1)S(1)} %collective-permute-done.18.refs_12_), channel_id=1, source_target_pairs={{0,2},{2,0},{1,3},{3,1},{4,6},{6,4},{5,7},{7,5},{8,10},{10,8},{9,1... | collective-permute-start | bytes 835592 | tf_op jit(solution)/shard_map/ppermute | solution.py:644
  94.8 14.8 %collective-permute-start.30 = (bf16[2,512,128]{2,1,0:T(8,128)(2,1)}, bf16[2,512,128]{2,1,0:T(8,128)(2,1)S(1)}, u32[]{:S(2)}, u32[]{:S(2)}) collective-permute-start(bf16[2,512,128]{2,1,0:T(8,128)(2,1)} %copy-done.21), channel_id=1, source_target_pairs={{0,17},{1,16},{16,1},{17,0},{2,19},{3,18},{18,3},{19,2},{4,21},{5,... | collective-permute-start | bytes 786440 | tf_op jit(solution)/shard_map/ppermute | solution.py:810
  96.4 12.7 %collective-permute-start.29 = (bf16[2,512,128]{2,1,0:T(8,128)(2,1)}, bf16[2,512,128]{2,1,0:T(8,128)(2,1)S(1)}, u32[]{:S(2)}, u32[]{:S(2)}) collective-permute-start(bf16[2,512,128]{2,1,0:T(8,128)(2,1)} %copy-done.19), channel_id=1, source_target_pairs={{0,16},{1,17},{16,0},{17,1},{2,18},{3,19},{18,2},{19,3},{4,20},{5,... | collective-permute-start | bytes 786440 | tf_op jit(solution)/shard_map/ppermute | solution.py:810
  97.9 14.7 %collective-permute-start.31 = (bf16[2,256,256]{2,1,0:T(8,128)(2,1)S(1)}, bf16[2,256,256]{2,1,0:T(8,128)(2,1)S(1)}, u32[]{:S(2)}, u32[]{:S(2)}) collective-permute-start(bf16[2,256,256]{2,1,0:T(8,128)(2,1)S(1)} %pad_maximum_fusion.1), channel_id=1, source_target_pairs={{0,8},{4,12},{8,0},{12,4},{1,9},{5,13},{9,1},{13,5},{2,10},{6,14},... | collective-permute-start | bytes 786440 | tf_op jit(solution)/shard_map/ppermute | solution.py:644
  99.5 11.0 %collective-permute-start.32 = (bf16[512,128]{1,0:T(8,128)(2,1)S(1)}, bf16[512,128]{1,0:T(8,128)(2,1)S(1)}, u32[]{:S(2)}, u32[]{:S(2)}) collective-permute-start(bf16[512,128]{1,0:T(8,128)(2,1)S(1)} %copy-done.25), channel_id=1, source_target_pairs={{0,1},{1,0},{2,3},{3,2},{4,5},{5,4},{6,7},{7,6},{8,9},{9,8},{10,11... | collective-permute-start | bytes 393224 | tf_op jit(solution)/shard_map/ppermute | solution.py:54
  100.1 19.8 %collective-permute-start.37 = (bf16[2,256,256]{2,1,0:T(8,128)(2,1)S(1)}, bf16[2,256,256]{2,1,0:T(8,128)(2,1)S(1)}, u32[]{:S(2)}, u32[]{:S(2)}) collective-permute-start(bf16[2,256,256]{2,1,0:T(8,128)(2,1)S(1)} %pad_maximum_fusion.4), channel_id=1, source_target_pairs={{0,12},{4,0},{8,4},{12,8},{1,13},{5,1},{9,5},{13,9},{2,14},{6,2},{... | collective-permute-start | bytes 786440 | tf_op jit(solution)/shard_map/ppermute | solution.py:644
  109.2 10.8 %collective-permute-start.36 = (bf16[2,256,256]{2,1,0:T(8,128)(2,1)S(1)}, bf16[2,256,256]{2,1,0:T(8,128)(2,1)S(1)}, u32[]{:S(2)}, u32[]{:S(2)}) collective-permute-start(bf16[2,256,256]{2,1,0:T(8,128)(2,1)S(1)} %pad_maximum_fusion.3), channel_id=1, source_target_pairs={{0,4},{4,8},{8,12},{12,0},{1,5},{5,9},{9,13},{13,1},{2,6},{6,10},{... | collective-permute-start | bytes 786440 | tf_op jit(solution)/shard_map/ppermute | solution.py:644
  109.6 10.4 %collective-permute-start.33 = (bf16[2,512,128]{2,1,0:T(8,128)(2,1)S(1)}, bf16[2,512,128]{2,1,0:T(8,128)(2,1)S(1)}, u32[]{:S(2)}, u32[]{:S(2)}) collective-permute-start(bf16[2,512,128]{2,1,0:T(8,128)(2,1)S(1)} %get-tuple-element.206), channel_id=1, source_target_pairs={{0,1},{1,0},{2,3},{3,2},{4,5},{5,4},{6,7},{7,6},{8,9},{9,8},{10,11... | collective-permute-start | bytes 786440 | tf_op jit(solution)/shard_map/ppermute | solution.py:54
  110.5 9.5 %collective-permute-start.34 = (bf16[2,512,128]{2,1,0:T(8,128)(2,1)S(1)}, bf16[2,512,128]{2,1,0:T(8,128)(2,1)S(1)}, u32[]{:S(2)}, u32[]{:S(2)}) collective-permute-start(bf16[2,512,128]{2,1,0:T(8,128)(2,1)S(1)} %get-tuple-element.217.refs_2_), channel_id=1, source_target_pairs={{0,16},{1,17},{16,0},{17,1},{2,18},{3,19},{18,2},{19,3},{4,20},{5,... | collective-permute-start | bytes 786440 | tf_op jit(solution)/shard_map/ppermute | solution.py:810
  112.6 11.5 %collective-permute-start.35 = (bf16[2,512,128]{2,1,0:T(8,128)(2,1)S(1)}, bf16[2,512,128]{2,1,0:T(8,128)(2,1)S(1)}, u32[]{:S(2)}, u32[]{:S(2)}) collective-permute-start(bf16[2,512,128]{2,1,0:T(8,128)(2,1)S(1)} %get-tuple-element.206), channel_id=1, source_target_pairs={{0,17},{1,16},{16,1},{17,0},{2,19},{3,18},{18,3},{19,2},{4,21},{5,... | collective-permute-start | bytes 786440 | tf_op jit(solution)/shard_map/ppermute | solution.py:810
  125.6 12.1 %collective-permute-start.39 = (bf16[512,256]{1,0:T(8,128)(2,1)S(1)}, bf16[512,256]{1,0:T(8,128)(2,1)S(1)}, u32[]{:S(2)}, u32[]{:S(2)}) collective-permute-start(bf16[512,256]{1,0:T(8,128)(2,1)S(1)} %maximum_select_fusion.3.refs_0_), channel_id=1, source_target_pairs={{0,4},{4,8},{8,12},{12,0},{1,5},{5,9},{9,13},{13,1},{2,6},{6,10},{... | collective-permute-start | bytes 786440 | tf_op jit(solution)/shard_map/ppermute | solution.py:644
  134.0 29.8 %collective-permute-start.51 = (bf16[8,256,256]{2,1,0:T(8,128)(2,1)S(1)}, bf16[8,256,256]{2,1,0:T(8,128)(2,1)S(1)}, u32[]{:S(2)}, u32[]{:S(2)}) collective-permute-start(bf16[8,256,256]{2,1,0:T(8,128)(2,1)S(1)} %constant_dynamic-update-slice_fusion.refs_14_.refs_18_.refs_22_.refs_26_.refs_30_.refs_34_.refs_38, ...), channel_id=1, source_target_pairs={{0,1},{1,0},{2,3},{3,2},{4,5},{5,4},{6,7},{7,6},{8,9},{9,8},{10,11... | collective-permute-start | bytes 3145736 | tf_op jit(solution)/shard_map/ppermute | solution.py:54
  135.0 29.8 %collective-permute-start.52 = (bf16[8,256,256]{2,1,0:T(8,128)(2,1)S(1)}, bf16[8,256,256]{2,1,0:T(8,128)(2,1)S(1)}, u32[]{:S(2)}, u32[]{:S(2)}) collective-permute-start(bf16[8,256,256]{2,1,0:T(8,128)(2,1)S(1)} %constant_dynamic-update-slice_fusion.refs_14_.refs_18_.refs_22_.refs_26_.refs_30_.refs_34_.refs_38, ...), channel_id=1, source_target_pairs={{0,16},{16,0},{1,17},{17,1},{2,18},{18,2},{3,19},{19,3},{4,20},{20... | collective-permute-start | bytes 3145736 | tf_op jit(solution)/shard_map/ppermute | solution.py:644
  137.7 9.7 %collective-permute-start.43 = (bf16[512,256]{1,0:T(8,128)(2,1)S(1)}, bf16[512,256]{1,0:T(8,128)(2,1)S(1)}, u32[]{:S(2)}, u32[]{:S(2)}) collective-permute-start(bf16[512,256]{1,0:T(8,128)(2,1)S(1)} %collective-permute-done.39.refs_4_), channel_id=1, source_target_pairs={{0,2},{2,0},{1,3},{3,1},{4,6},{6,4},{5,7},{7,5},{8,10},{10,8},{9,1... | collective-permute-start | bytes 786440 | tf_op jit(solution)/shard_map/ppermute | solution.py:644
  138.6 13.5 %collective-permute-start.46 = (bf16[512,256]{1,0:T(8,128)(2,1)S(1)}, bf16[512,256]{1,0:T(8,128)(2,1)S(1)}, u32[]{:S(2)}, u32[]{:S(2)}) collective-permute-start(bf16[512,256]{1,0:T(8,128)(2,1)S(1)} %maximum_select_fusion.4.refs_1_), channel_id=1, source_target_pairs={{0,4},{4,8},{8,12},{12,0},{1,5},{5,9},{9,13},{13,1},{2,6},{6,10},{... | collective-permute-start | bytes 786440 | tf_op jit(solution)/shard_map/ppermute | solution.py:644
  166.0 10.2 %collective-permute-start.48 = (bf16[512,256]{1,0:T(8,128)(2,1)S(1)}, bf16[512,256]{1,0:T(8,128)(2,1)S(1)}, u32[]{:S(2)}, u32[]{:S(2)}) collective-permute-start(bf16[512,256]{1,0:T(8,128)(2,1)S(1)} %collective-permute-done.44.refs_12_), channel_id=1, source_target_pairs={{0,2},{2,0},{1,3},{3,1},{4,6},{6,4},{5,7},{7,5},{8,10},{10,8},{9,1... | collective-permute-start | bytes 786440 | tf_op jit(solution)/shard_map/ppermute | solution.py:644
  178.9 10.6 %collective-permute-start.57 = (bf16[8,256,256]{2,1,0:T(8,128)(2,1)S(1)}, bf16[8,256,256]{2,1,0:T(8,128)(2,1)S(1)}, u32[]{:S(2)}, u32[]{:S(2)}) collective-permute-start(bf16[8,256,256]{2,1,0:T(8,128)(2,1)S(1)} %collective-permute-done.52.refs_16_.refs_20_.refs_24_.refs_28_.refs_32_.refs_36_.refs_40_.refs_4_), channel_id=1, source_target_pairs={{0,1},{1,0},{2,3},{3,2},{4,5},{5,4},{6,7},{7,6},{8,9},{9,8},{10,11... | collective-permute-start | bytes 3145736 | tf_op jit(solution)/shard_map/ppermute | solution.py:54
  (84 other events, 971.9 us)

commit v9 on v8

--- a/solution.py
+++ b/solution.py
@@ -261,25 +261,24 @@
     for part in range(6):
         total = acc[part] * scale
         side, kind = part // 3, part % 3
-        kv_outs = outs[2 * heads * side : 2 * heads * side + heads]
-        q_outs = outs[2 * heads * side + heads : 2 * heads * side + 2 * heads]
+        kv_out, q_out = outs[2 * side : 2 * side + 2]
         for head in range(heads):
-            raw = total[:, head * HD : (head + 1) * HD]
+            lanes = slice(head * HD, (head + 1) * HD)
+            raw = total[:, lanes]
             if kind == 1:
-                kv_outs[head][1] = raw.astype(BF16)
+                kv_out[1, :, lanes] = raw.astype(BF16)
                 continue
             raw = raw * lax.rsqrt(jnp.mean(raw * raw, axis=-1, keepdims=True) + EPSILON)
             if kind == 0:
-                kv_outs[head][0] = (raw * head_gains[1:2, :]).astype(BF16)
+                kv_out[0, :, lanes] = (raw * head_gains[1:2, :]).astype(BF16)
             else:
-                q_outs[head][...] = (raw * (head_gains[0:1, :] * HD ** (-0.5))).astype(BF16)
+                q_out[:, lanes] = (raw * (head_gains[0:1, :] * HD ** (-0.5))).astype(BF16)
 
 
 def qkv_step(meta, layout, blocks, entries, weights, state, head_gains):
     span = blocks[0][1].shape[1]
     half = 2 * blocks[0][1].shape[0]
     width = weights[0].shape[1]
-    heads = width // HD
     count, last = len(blocks), state is not None
     groups = layout[1] * layout[2]
     inputs = [p for pieces in blocks for p in pieces] + list(weights)
@@ -288,8 +287,7 @@
     if last:
         specs += [pl.BlockSpec(memory_space=pltpu.HBM)] * 6 + [HELD] * 2 + [full(head_gains.shape)]
         inputs += list(state) + [head_gains]
-        kv, q = jax.ShapeDtypeStruct((2, half, HD), BF16), jax.ShapeDtypeStruct((half, HD), BF16)
-        outs = ([kv] * heads + [q] * heads) * 2
+        outs = [pltpu.HBM((2, half, width), BF16), pltpu.HBM((half, width), BF16)] * 2
         scratch = [pltpu.VMEM((6, span, width), BF16), pltpu.SemaphoreType.DMA((6,))] + scratch
     else:
         specs += [HELD] * 6
@@ -326,32 +324,34 @@
         for image in range(images):
             inner = place - meta[image]
             limit = jnp.where((inner >= 0) & (inner < IMG_TOK), meta[image] + IMG_TOK - 1, limit)
-        query = q_refs[side][...]
-        scores = []
-        top = None
-        for piece in range(pieces):
-            score = lax.dot_general(
-                query, kv_refs[piece][0], (((1,), (1,)), ((), ())), preferred_element_type=F32
-            )
-            position = lax.broadcasted_iota(jnp.int32, score.shape, 1)
-            score = jnp.where(position <= limit - bases[piece], score, NEGATIVE_FILL)
-            scores.append(score)
-            best = jnp.max(score, axis=1, keepdims=True)
-            top = best if top is None else jnp.maximum(top, best)
-        total = jnp.zeros((rows, 1), F32)
-        product = jnp.zeros((rows, HD), F32)
-        for piece in range(pieces):
-            weight = jnp.exp(scores[piece] - top)
-            total = total + jnp.sum(weight, axis=1, keepdims=True)
-            product = product + mxu(weight.astype(BF16), kv_refs[piece][1])
-        out_refs[side][...] = (product / total).astype(BF16)
+        for head in range(q_refs[0].shape[1] // HD):
+            lanes = slice(head * HD, (head + 1) * HD)
+            query = q_refs[side][:, lanes]
+            scores = []
+            top = None
+            for piece in range(pieces):
+                score = lax.dot_general(
+                    query, kv_refs[piece][0, :, lanes], (((1,), (1,)), ((), ())), preferred_element_type=F32
+                )
+                position = lax.broadcasted_iota(jnp.int32, score.shape, 1)
+                score = jnp.where(position <= limit - bases[piece], score, NEGATIVE_FILL)
+                scores.append(score)
+                best = jnp.max(score, axis=1, keepdims=True)
+                top = best if top is None else jnp.maximum(top, best)
+            total = jnp.zeros((rows, 1), F32)
+            product = jnp.zeros((rows, HD), F32)
+            for piece in range(pieces):
+                weight = jnp.exp(scores[piece] - top)
+                total = total + jnp.sum(weight, axis=1, keepdims=True)
+                product = product + mxu(weight.astype(BF16), kv_refs[piece][1, :, lanes])
+            out_refs[side][:, lanes] = (product / total).astype(BF16)
 
 
 def attention(meta, queries, pieces, images):
-    half = queries[0].shape[0]
+    half, width = queries[0].shape
     block = 256
     keys = half * len(pieces)
-    rows = pl.BlockSpec((block, HD), lambda i, m: (i, 0))
+    rows = pl.BlockSpec((block, width), lambda i, m: (i, 0))
     return pl.pallas_call(
         functools.partial(attention_kernel, images, len(pieces), half),
         grid_spec=pltpu.PrefetchScalarGridSpec(
@@ -360,14 +360,14 @@
             in_specs=[rows, rows] + [full(p.shape) for p in pieces],
             out_specs=[rows, rows],
         ),
-        out_shape=[jax.ShapeDtypeStruct((half, HD), BF16)] * 2,
-        compiler_params=params(24),
-        cost_estimate=cost(8 * half * keys * HD, 4 * keys * HD, 2 * half * keys),
+        out_shape=[jax.ShapeDtypeStruct((half, width), BF16)] * 2,
+        compiler_params=params(32),
+        cost_estimate=cost(8 * half * keys * width, 4 * keys * width, 2 * half * keys * width // HD),
         name="attention",
     )(meta, *queries, *pieces)
 
 
-def out_kernel(count, heads, first, last, meta, *refs):
+def out_kernel(count, first, last, meta, *refs):
     refs = list(refs)
     x_refs = take_blocks(refs, count)
     weight_refs = [[refs.pop(0), refs.pop(0)] for _ in range(count)]
@@ -384,13 +384,7 @@
         else:
             total = acc_in[side]
         for index in range(count):
-            weight = weight_refs[index][side]
-            if heads == 2:
-                for head in range(heads):
-                    part = weight[0, :, head].reshape(2 * HD, weight.shape[4])
-                    total = total + mxu(x_refs[index][head][...], part)
-            else:
-                total = total + mxu(load(x_refs[index]), weight[0, :, 0].reshape(2 * HD, weight.shape[4]))
+            total = total + mxu(load(x_refs[index]), weight_refs[index][side][...])
         if last:
             outs[side][...] = total.astype(BF16)
         else:
@@ -398,23 +392,16 @@
 
 
 def out_step(meta, layout, blocks, entries, weights, state, last):
-    width = weights[0].shape[1]
-    heads = width // HD
-    half = blocks[0][0].shape[0] * (1 if heads == 2 else 2)
+    span, width = blocks[0][0].shape[1], weights[0].shape[1]
+    half = 2 * blocks[0][0].shape[0]
     first = isinstance(state, list)
     count = len(blocks)
-    views = [w.reshape(-1, 2, heads, HD, width) for w in weights]
     inputs = [p for pieces in blocks for p in pieces]
     specs = [full(p.shape) for p in inputs]
     for entry in entries:
-        for view in views:
-            inputs.append(view)
-            specs.append(
-                pl.BlockSpec(
-                    (1, 2, heads, HD, width),
-                    lambda i, m, entry=entry: (chip_of(m, *layout, entry), 0, 0, 0, 0),
-                )
-            )
+        index = lambda i, m, entry=entry: (chip_of(m, *layout, entry), 0)
+        inputs += weights
+        specs += [pl.BlockSpec((span, width), index)] * 2
     states = state if first else [state]
     inputs += states
     specs += [full(s.shape) for s in states]
@@ -423,7 +410,7 @@
     else:
         outs = [jax.ShapeDtypeStruct((2, half, width), F32)]
     result = pl.pallas_call(
-        functools.partial(out_kernel, count, heads, first, last),
+        functools.partial(out_kernel, count, first, last),
         grid_spec=pltpu.PrefetchScalarGridSpec(
             num_scalar_prefetch=1,
             grid=(1,),
@@ -432,7 +419,7 @@
         ),
         out_shape=outs,
         compiler_params=params(24),
-        cost_estimate=cost(8 * count * half * heads * HD * width, (2 + count) << 20),
+        cost_estimate=cost(4 * count * half * span * width, (2 + count) << 20),
         name="out_last" if last else "out_step",
     )(meta, *inputs)
     return result if last else result[0]
@@ -653,9 +640,24 @@
     return [every] + [shift(every, "tile", s) for s in range(1, tiles)], conv, *others
 
 
-def columns_kernel(meta, kept_in, sent_in, kept_out, sent_out):
-    kept_out[0] = kept_in[...]
-    sent_out[0] = sent_in[...]
+def columns_kernel(layout, halves, meta, patch_ref, kept_ref, sent_ref, arrived):
+    images, tiles, outer = layout
+    ctx, _, _, mpo = split_meta(meta, images)
+    size = kept_ref.shape[2]
+    copies = []
+    for other, out_ref in enumerate((kept_ref, sent_ref)):
+        for tile in range(tiles):
+            chip = tile * outer + lax.rem(mpo + other, outer)
+            at = pl.multiple_of((chip * halves + (ctx if halves == 2 else 0)) * size, size)
+            copies.append(
+                pltpu.make_async_copy(
+                    patch_ref.at[:, pl.ds(at, size)], out_ref.at[tile], arrived.at[other, tile]
+                )
+            )
+    for copy in copies:
+        copy.start()
+    for copy in copies:
+        copy.wait()
 
 
 def transpose_first(meta, patch_out, layout, ctxs):
@@ -665,25 +667,21 @@
     halves = 2 if ctxs == 2 and deep == 2 * CH else 1
     size = deep // halves
 
-    def place(other):
-        def index(i, m):
-            ctx, _, _, mpo = split_meta(m, images)
-            chip = i * outer + lax.rem(mpo + other, outer)
-            return 0, chip * halves + (ctx if halves == 2 else 0)
-
-        return pl.BlockSpec((width, size), index)
-
-    out = pl.BlockSpec((1, width, size), lambda i, m: (i, 0, 0))
+    place = pl.BlockSpec(memory_space=pltpu.HBM)
     kept, sent = pl.pallas_call(
-        columns_kernel,
+        functools.partial(columns_kernel, layout, halves),
         grid_spec=pltpu.PrefetchScalarGridSpec(
-            num_scalar_prefetch=1, grid=(tiles,), in_specs=[place(0), place(1)], out_specs=[out, out]
+            num_scalar_prefetch=1,
+            grid=(1,),
+            in_specs=[place],
+            out_specs=[place, place],
+            scratch_shapes=[pltpu.SemaphoreType.DMA((2, tiles))],
         ),
-        out_shape=[jax.ShapeDtypeStruct((tiles, width, size), BF16)] * 2,
+        out_shape=[pltpu.HBM((tiles, width, size), BF16)] * 2,
         compiler_params=params(8),
         cost_estimate=cost(1 << 16, 2 << 20),
         name="columns",
-    )(meta, patch_out, patch_out)
+    )(meta, patch_out)
     return kept, sent, halves
 
 
@@ -697,7 +695,7 @@
 
 def gather_pair(first, second, state, step, extras=None):
     tiles = lax.axis_size("tile")
-    found, moving = [{0: first}, {}], [None, None]
+    found, moving = [{0: first}, {0: second}], [None, None]
 
     def launch(which, index):
         ring = found[which][2 * index]
@@ -709,32 +707,15 @@
             moving[which] = shift(ring, "mpo", 1)
 
     launch(0, 0)
-    late = callable(second)
-    if late:
-        second, extras = second()
-        events = [(0, 1), (0, 2)]
-        for index in range(1, tiles - 2):
-            events += [(1, index), (0, index + 2)]
-        events += [(1, tiles - 2), (1, tiles - 1)]
-    else:
-        events = [(which, index) for index in range(1, tiles) for which in range(2)]
-    found[1][0] = second
-    if not late:
-        launch(1, 0)
+    launch(1, 0)
     seen = first
-    for which, index in events:
-        ring, cross = moving[which]
-        if late and (which, index) == (0, 1):
-            ring, cross, found[1][0] = lax.optimization_barrier((ring, cross, second))
-        elif late and (which, index) == (1, tiles - 2):
-            ring, cross, seen, extras = lax.optimization_barrier((ring, cross, seen, extras))
-        else:
+    for index in range(1, tiles):
+        for which in range(2):
+            ring, cross = moving[which]
             ring, cross, seen = lax.optimization_barrier((ring, cross, seen))
-        found[which][2 * index], found[which][2 * index - 1] = ring, cross
-        seen = ring
-        launch(which, index)
-        if late and (which, index) == (0, 1):
-            launch(1, 0)
+            found[which][2 * index], found[which][2 * index - 1] = ring, cross
+            seen = ring
+            launch(which, index)
     entries = list(range(2 * tiles - 1))
     state = step([[found[0][e], found[1][e]] for e in entries], entries, state, False)
     last = lax.optimization_barrier((moving[0], moving[1], state, extras))
@@ -762,7 +743,6 @@
     ctx, tile, mpo, core = (lax.axis_index(name) for name in ("ctx", "tile", "mpo", "core"))
     seq_rows, width = text_embed.shape
     half = seq_rows // 2
-    heads = width // HD
     images = span_start.shape[0]
     local = latents.shape[0]
 
@@ -798,8 +778,7 @@
     state, out_par = gather_pair(
         *[by_core(core, s[0], o, 1) for s, o in zip(streams, others)], None, project, swap(out_weight)
     )
-    kv_send, q_send = state[:heads], state[heads : 2 * heads]
-    kv_own, q_own = state[2 * heads : 3 * heads], state[3 * heads :]
+    kv_send, q_send, kv_own, q_own = state
 
     def shifted(values, step, cross):
         pairs = [
@@ -809,44 +788,27 @@
         ]
         return lax.ppermute(values, ("ctx", "core"), pairs)
 
-    def pieces_of(head):
-        pieces = [swap(q_send[head]), kv_own[head], swap(kv_send[head])]
-        for step in range(1, ctxs):
-            pieces += [shifted(kv_own[head], step, False), shifted(kv_send[head], step, True)]
-        return pieces
-
-    def attend(head, pieces, ahead):
-        result = attention(meta, [q_own[head], pieces[0]], pieces[1:], images)
-        (att_own, att_send), ahead = lax.optimization_barrier((result, ahead))
-        return by_core(core, att_own, swap(att_send), 1), ahead
-
-    pieces = pieces_of(0)
-    pieces[0], q_send, kv_own, kv_send, kept, received = lax.optimization_barrier(
-        (pieces[0], q_send, kv_own, kv_send, kept, received)
-    )
+    q_par = swap(q_send)
+    q_par, kept, received = lax.optimization_barrier((q_par, kept, received))
     up_blocks = [transpose_second(kept, received, step) for step in range(tiles)]
-    pieces, up_blocks[tiles // 2] = lax.optimization_barrier((pieces, up_blocks[tiles // 2]))
-    attended, (other_pieces, up_blocks) = attend(
-        0, pieces, (pieces_of(1) if heads > 1 else None, up_blocks)
-    )
-    if heads == 1:
-        attended, second = attended[: half // 2], attended[half // 2 :]
-        own = jnp.concatenate(up_blocks)
-        extras = [own, swap(own)] + ([shift(own, "ctx", 1)] if halves == 2 else [])
-    else:
-        extras = None
-
-        def second():
-            pieces, _ = lax.optimization_barrier((other_pieces, attended))
-            result, up = attend(1, pieces, up_blocks)
-            own = jnp.concatenate(up)
-            return result, [own, swap(own)] + ([shift(own, "ctx", 1)] if halves == 2 else [])
+    pieces = [kv_own, swap(kv_send)]
+    for step in range(1, ctxs):
+        pieces += [shifted(kv_own, step, False), shifted(kv_send, step, True)]
+    pieces, up_blocks = lax.optimization_barrier((pieces, up_blocks))
+    att_own, att_send = attention(meta, [q_own, q_par], pieces, images)
+    att_par = swap(att_send)
+    rows = half // 2
+    attended = [
+        by_core(core, att_own[at : at + rows], att_par[at : at + rows], 1) for at in (0, rows)
+    ]
+    up_own = jnp.concatenate(up_blocks)
+    extras = [up_own, swap(up_own)] + ([shift(up_own, "ctx", 1)] if halves == 2 else [])
 
     def project_out(blocks, entries, state, last):
         return out_step(meta, layout, blocks, entries, (out_weight, out_par), state, last)
 
     state = [jnp.stack([s[0], o]) for s, o in zip(streams, others)]
-    state, up_weights = gather_pair(attended, second, state, project_out, extras)
+    state, up_weights = gather_pair(*attended, state, project_out, extras)
     out_own, out_send = state
     out_other = swap(out_send)
     layer_out = by_core(core, out_own, out_other, 0)

time: 250 us -> 247 us (0.988)
  waiting for transfers between devices: 107 us -> 117 us
  starting transfers between devices: 73.5 us -> 66.8 us
  local copies, waits for them, and re-layouts: 16 us -> 12.2 us
    ppermute x6 -> x4, waiting for transfers between devices: 18.2 us -> 23.9 us  [shifted(): return lax.ppermute(values, ('ctx', 'core'), pairs)]
    ppermute x55, starting transfers between devices: 45.1 us -> 39.6 us  [shift(): lax.ppermute(values, axis, [(i, (i + step) % count) for i in range(count)])]
    ppermute x55, waiting for transfers between devices: 83.6 us -> 87.7 us  [shift(): lax.ppermute(values, axis, [(i, (i + step) % count) for i in range(count)])]
    unnamed x74 -> x64, local copies, waits for them, and re-layouts: 12.5 us -> 8.71 us
    ppermute x6 -> x4, starting transfers between devices: 6.55 us -> 3.23 us  [shifted(): return lax.ppermute(values, ('ctx', 'core'), pairs)]
    ppermute x17 -> x14, starting transfers between devices: 14.5 us -> 16.7 us  [swap(): return lax.ppermute(values, 'core', [(0, 1), (1, 0)])]
    pallas_call x2 -> x1, Pallas kernels: 9.73 us -> 8.54 us  [attention(): pl.pallas_call(functools.partial(attention_kernel, images, len(pieces), h...]
    ppermute x17 -> x14, waiting for transfers between devices: 5.24 us -> 4.63 us  [swap(): return lax.ppermute(values, 'core', [(0, 1), (1, 0)])]
  transfers between devices with their start and end apart: 81 -> 76, of which waited for: 32 -> 31; matrix products, arithmetic and copies ran while one was open for 4% -> 4% of each run, Pallas kernels for 16% -> 11%
where the time goes in v9:
time: 247 us
  waiting for transfers between devices  117 us (47%)
  starting transfers between devices  66.8 us (27%)
  Pallas kernels  44.6 us (18%)
  local copies, waits for them, and re-layouts  12.2 us (5%)
  other arithmetic  4.62 us (2%)
    ppermute x55, waiting for transfers between devices, shift(): lax.ppermute(values, axis, [(i, (i + step) % count) for i in range(count)])  87.7 us
    ppermute x55, starting transfers between devices, shift(): lax.ppermute(values, axis, [(i, (i + step) % count) for i in range(count)])  39.6 us
    ppermute x4, waiting for transfers between devices, shifted(): return lax.ppermute(values, ('ctx', 'core'), pairs)  23.9 us
    ppermute x14, starting transfers between devices, swap(): return lax.ppermute(values, 'core', [(0, 1), (1, 0)])  16.7 us
    pallas_call x2, Pallas kernels, qkv_step(): pl.pallas_call(functools.partial(qkv_kernel, entries, layout, groups, las...  13 us
    pallas_call x1, Pallas kernels, down_stream(): pl.pallas_call(functools.partial(down_kernel, images, tiles, half), grid_...  9.45 us
    unnamed x64, local copies, waits for them, and re-layouts  8.71 us
    pallas_call x1, Pallas kernels, attention(): pl.pallas_call(functools.partial(attention_kernel, images, len(pieces), h...  8.54 us
  transfers between devices with their start and end apart: 76, of which 31 were waited for; matrix products, arithmetic and copies ran while one was open for 4% of the time, Pallas kernels for 11%

profile of v9, /device:TPU:1, one launch (start us, length us, event | category | flops | bytes accessed | tf_op | source)
XLA Modules:
  0.0 246.9 jit_solution(7148316188126961018)
XLA Ops:
  1.3 2.7 %collective-permute-start = (bf16[2,16,512]{2,1,0:T(8,128)(2,1)}, bf16[2,16,512]{2,1,0:T(8,128)(2,1)S(1)}, u32[]{:S(2)}, u32[]{:S(2)}) collective-permute-start(bf16[2,16,512]{2,1,0:T(8,128)(2,1)} %param.16), channel_id=1, source_target_pairs={{0,16},{16,0},{1,17},{17,1},{2,18},{18,2},{3,19},{19,3},{4,20},{20... | collective-permute-start | bytes 98312 | tf_op jit(solution)/shard_map/ppermute | solution.py:631
  8.2 2.5 collective-permute-start.3
  23.5 9.5 %down_stream.1 = (bf16[2,272,256]{2,1,0:T(8,128)(2,1)S(1)}, bf16[2,256,256]{2,1,0:T(8,128)(2,1)S(1)}, bf16[4096,256]{1,0:T(8,128)(2,1)S(1)}, bf16[4096,256]{1,0:...) custom-call(s32[16]{0:T(128)S(1)} %concatenate.60.meta, ...), custom_call_target="tpu_custom_call" | custom-call | flops 4294967296 | bytes 4194304 | tf_op jit(solution)/shard_map/down_stream/pallas_call | solution.py:160
  39.2 7.2 %collective-permute-done.12.refs_4_ = bf16[272,512]{1,0:T(8,128)(2,1)S(1)} collective-permute-done((bf16[272,512]{1,0:T(8,128)(2,1)S(1)}, bf16[272,512]{1,0:T(8,128)(2,1)S(1)}, u32[]{:S(2)}, u32[]{:S(2)}) %collective-permute-start.12) | collective-permute-done | bytes 278560 | tf_op jit(solution)/shard_map/ppermute | solution.py:631
  46.9 5.1 %collective-permute-done.16.refs_5_ = bf16[256,512]{1,0:T(8,128)(2,1)S(1)} collective-permute-done((bf16[256,512]{1,0:T(8,128)(2,1)S(1)}, bf16[256,512]{1,0:T(8,128)(2,1)S(1)}, u32[]{:S(2)}, u32[]{:S(2)}) %collective-permute-start.16) | collective-permute-done | bytes 262176 | tf_op jit(solution)/shard_map/ppermute | solution.py:631
  52.5 5.5 %collective-permute-done.14.refs_8_ = bf16[272,512]{1,0:T(8,128)(2,1)S(1)} collective-permute-done((bf16[272,512]{1,0:T(8,128)(2,1)S(1)}, bf16[272,512]{1,0:T(8,128)(2,1)S(1)}, u32[]{:S(2)}, u32[]{:S(2)}) %collective-permute-start.14) | collective-permute-done | bytes 278560 | tf_op jit(solution)/shard_map/ppermute | solution.py:631
  58.4 5.2 %collective-permute-done.20.refs_9_ = bf16[256,512]{1,0:T(8,128)(2,1)S(1)} collective-permute-done((bf16[256,512]{1,0:T(8,128)(2,1)S(1)}, bf16[256,512]{1,0:T(8,128)(2,1)S(1)}, u32[]{:S(2)}, u32[]{:S(2)}) %collective-permute-start.20) | collective-permute-done | bytes 262176 | tf_op jit(solution)/shard_map/ppermute | solution.py:631
  64.1 5.5 %collective-permute-done.18.refs_12_ = bf16[272,512]{1,0:T(8,128)(2,1)S(1)} collective-permute-done((bf16[272,512]{1,0:T(8,128)(2,1)S(1)}, bf16[272,512]{1,0:T(8,128)(2,1)S(1)}, u32[]{:S(2)}, u32[]{:S(2)}) %collective-permute-start.18) | collective-permute-done | bytes 278560 | tf_op jit(solution)/shard_map/ppermute | solution.py:631
  70.0 5.2 %collective-permute-done.23.refs_13_ = bf16[256,512]{1,0:T(8,128)(2,1)S(1)} collective-permute-done((bf16[256,512]{1,0:T(8,128)(2,1)S(1)}, bf16[256,512]{1,0:T(8,128)(2,1)S(1)}, u32[]{:S(2)}, u32[]{:S(2)}) %collective-permute-start.23) | collective-permute-done | bytes 262176 | tf_op jit(solution)/shard_map/ppermute | solution.py:631
  76.8 7.7 %qkv_step.1 = (f32[6,512,256]{2,1,0:T(8,128)S(1)}, f32[512,128]{1,0:T(8,128)S(1)}) custom-call(s32[16]{0:T(128)S(1)} %concatenate.60.meta, bf16[272,512]{1,0:T(8,128)(2,1)S(1)} %maximum_select_fusion.1.refs_0_, bf16[256,512]{1,0:T(8,128)(2,1)S(1)} %maximum_select_fusion.2.refs_1_, bf16[272,512]{1,0:T(8,128)(2,1)S(1)} %collective-permute-done.13.refs_2_, ...), custom_call_target="tpu_custom_call" | custom-call | flops 5637144576 | bytes 20971520 | tf_op jit(solution)/shard_map/qkv_step/pallas_call | solution.py:295
  84.5 5.4 %qkv_last.1 = (bf16[2,512,256]{2,1,0:T(8,128)(2,1)}, bf16[512,256]{1,0:T(8,128)(2,1)}, bf16[2,512,256]{2,1,0:T(8,128)(2,1)}, bf16[512,256]{1,0:T(8,128)(2,1)}) custom-call(s32[16]{0:T(128)S(1)} %concatenate.60.meta, bf16[272,512]{1,0:T(8,128)(2,1)S(1)} %collective-permute-done.22.refs_0_, bf16[256,512]{1,0:T(8,128)(2,1)S(1)} %collective-permute-done.25.refs_1_, ...), custom_call_target="tpu_custom_call" | custom-call | flops 805306368 | bytes 8388608 | tf_op jit(solution)/shard_map/qkv_last/pallas_call | solution.py:295
  94.4 3.4 %collective-permute-start.33 = (bf16[2,256,256]{2,1,0:T(8,128)(2,1)S(1)}, bf16[2,256,256]{2,1,0:T(8,128)(2,1)S(1)}, u32[]{:S(2)}, u32[]{:S(2)}) collective-permute-start(bf16[2,256,256]{2,1,0:T(8,128)(2,1)S(1)} %pad_maximum_fusion.4), channel_id=1, source_target_pairs={{0,12},{4,0},{8,4},{12,8},{1,13},{5,1},{9,5},{13,9},{2,14},{6,2},{... | collective-permute-start | bytes 786440 | tf_op jit(solution)/shard_map/ppermute | solution.py:631
  99.0 17.7 %collective-permute-done.29.refs_4_ = bf16[2,512,256]{2,1,0:T(8,128)(2,1)S(1)} collective-permute-done((bf16[2,512,256]{2,1,0:T(8,128)(2,1)}, bf16[2,512,256]{2,1,0:T(8,128)(2,1)S(1)}, u32[]{:S(2)}, u32[]{:S(2)}) %collective-permute-start.29) | collective-permute-done | bytes 524320 | tf_op jit(solution)/shard_map/ppermute | solution.py:789
  116.7 3.4 %collective-permute-done.32 = bf16[2,256,256]{2,1,0:T(8,128)(2,1)S(1)} collective-permute-done((bf16[2,256,256]{2,1,0:T(8,128)(2,1)S(1)}, bf16[2,256,256]{2,1,0:T(8,128)(2,1)S(1)}, u32[]{:S(2)}, u32[]{:S(2)}) %collective-permute-start.32) | collective-permute-done | bytes 262176 | tf_op jit(solution)/shard_map/ppermute | solution.py:631
  120.1 8.5 %attention.1 = (bf16[512,256]{1,0:T(8,128)(2,1)S(1)}, bf16[512,256]{1,0:T(8,128)(2,1)S(1)}) custom-call(s32[16]{0:T(128)S(1)} %concatenate.60.meta, bf16[512,256]{1,0:T(8,128)(2,1)S(1)} %copy-done.19, bf16[512,256]{1,0:T(8,128)(2,1)S(1)} %collective-permute-done.27.refs_1_, bf16[2,512,256]{2,1,0:T(8,128)(2,1)S(1)} %copy-done.18, ...), custom_call_target="tpu_custom_call" | custom-call | flops 2147483648 | bytes 2097152 | tf_op jit(solution)/shard_map/attention/pallas_call | solution.py:355
  136.0 4.6 %collective-permute-done.35.refs_4_ = bf16[256,512]{1,0:T(8,128)(2,1)S(1)} collective-permute-done((bf16[256,512]{1,0:T(8,128)(2,1)S(1)}, bf16[256,512]{1,0:T(8,128)(2,1)S(1)}, u32[]{:S(2)}, u32[]{:S(2)}) %collective-permute-start.35) | collective-permute-done | bytes 262176 | tf_op jit(solution)/shard_map/ppermute | solution.py:631
  142.3 3.3 %collective-permute-start.49 = (bf16[8,256,256]{2,1,0:T(8,128)(2,1)S(1)}, bf16[8,256,256]{2,1,0:T(8,128)(2,1)S(1)}, u32[]{:S(2)}, u32[]{:S(2)}) collective-permute-start(bf16[8,256,256]{2,1,0:T(8,128)(2,1)S(1)} %constant_dynamic-update-slice_fusion.refs_14_.refs_18_.refs_22_.refs_26_.refs_30_.refs_34_.refs_38, ...), channel_id=1, source_target_pairs={{0,1},{1,0},{2,3},{3,2},{4,5},{5,4},{6,7},{7,6},{8,9},{9,8},{10,11... | collective-permute-start | bytes 3145736 | tf_op jit(solution)/shard_map/ppermute | solution.py:54
  147.5 4.4 %collective-permute-done.37.refs_8_ = bf16[256,512]{1,0:T(8,128)(2,1)S(1)} collective-permute-done((bf16[256,512]{1,0:T(8,128)(2,1)S(1)}, bf16[256,512]{1,0:T(8,128)(2,1)S(1)}, u32[]{:S(2)}, u32[]{:S(2)}) %collective-permute-start.37) | collective-permute-done | bytes 262176 | tf_op jit(solution)/shard_map/ppermute | solution.py:631
  152.7 3.4 %collective-permute-done.43.refs_9_ = bf16[256,512]{1,0:T(8,128)(2,1)S(1)} collective-permute-done((bf16[256,512]{1,0:T(8,128)(2,1)S(1)}, bf16[256,512]{1,0:T(8,128)(2,1)S(1)}, u32[]{:S(2)}, u32[]{:S(2)}) %collective-permute-start.43) | collective-permute-done | bytes 262176 | tf_op jit(solution)/shard_map/ppermute | solution.py:631
  157.8 4.5 %collective-permute-done.41.refs_12_ = bf16[256,512]{1,0:T(8,128)(2,1)S(1)} collective-permute-done((bf16[256,512]{1,0:T(8,128)(2,1)S(1)}, bf16[256,512]{1,0:T(8,128)(2,1)S(1)}, u32[]{:S(2)}, u32[]{:S(2)}) %collective-permute-start.41) | collective-permute-done | bytes 262176 | tf_op jit(solution)/shard_map/ppermute | solution.py:631
  163.9 2.4 collective-permute-done.46.refs_13_
  168.6 4.1 %out_step.1.refs_4_ = f32[2,512,256]{2,1,0:T(8,128)S(1)} custom-call(s32[16]{0:T(128)S(1)} %concatenate.60.meta, bf16[256,512]{1,0:T(8,128)(2,1)S(1)} %maximum_select_fusion.3.refs_0_, bf16[256,512]{1,0:T(8,128)(2,1)S(1)} %maximum_select_fusion.4.refs_1_, bf16[256,512]{1,0:T(8,128)(2,1)S(1)} %collective-permute-done.36.refs_2_, ...), custom_call_target="tpu_custom_call" | custom-call | flops 1879048192 | bytes 9437184 | tf_op jit(solution)/shard_map/out_step/pallas_call | solution.py:412
  175.6 7.2 %collective-permute-start.52 = (bf16[8,256,256]{2,1,0:T(8,128)(2,1)S(1)}, bf16[8,256,256]{2,1,0:T(8,128)(2,1)S(1)}, u32[]{:S(2)}, u32[]{:S(2)}) collective-permute-start(bf16[8,256,256]{2,1,0:T(8,128)(2,1)S(1)} %collective-permute-done.50.refs_16_.refs_20_.refs_24_.refs_28_.refs_32_.refs_36_.refs_40_.refs_4_), channel_id=1, source_target_pairs={{0,1},{1,0},{2,3},{3,2},{4,5},{5,4},{6,7},{7,6},{8,9},{9,8},{10,11... | collective-permute-start | bytes 3145736 | tf_op jit(solution)/shard_map/ppermute | solution.py:54
  190.5 3.1 %collective-permute-done.53.refs_1_ = bf16[256,256]{1,0:T(8,128)(2,1)S(1)} collective-permute-done((bf16[256,256]{1,0:T(8,128)(2,1)S(1)}, bf16[256,256]{1,0:T(8,128)(2,1)S(1)}, u32[]{:S(2)}, u32[]{:S(2)}) %collective-permute-start.53) | collective-permute-done | bytes 131104 | tf_op jit(solution)/shard_map/ppermute | solution.py:789
  193.6 3.1 %collective-permute-done.55.refs_3_ = bf16[256,256]{1,0:T(8,128)(2,1)S(1)} collective-permute-done((bf16[256,256]{1,0:T(8,128)(2,1)S(1)}, bf16[256,256]{1,0:T(8,128)(2,1)S(1)}, u32[]{:S(2)}, u32[]{:S(2)}) %collective-permute-start.55) | collective-permute-done | bytes 131104 | tf_op jit(solution)/shard_map/ppermute | solution.py:789
  198.4 5.3 %collective-permute-done.56.refs_4_ = bf16[128,512]{1,0:T(8,128)(2,1)} collective-permute-done((bf16[128,512]{1,0:T(8,128)(2,1)S(1)}, bf16[128,512]{1,0:T(8,128)(2,1)}, u32[]{:S(2)}, u32[]{:S(2)}) %collective-permute-start.56) | collective-permute-done | bytes 131104 | tf_op jit(solution)/shard_map/ppermute | solution.py:631
  203.6 2.8 %collective-permute-done.60.refs_5_ = bf16[128,512]{1,0:T(8,128)(2,1)} collective-permute-done((bf16[128,512]{1,0:T(8,128)(2,1)S(1)}, bf16[128,512]{1,0:T(8,128)(2,1)}, u32[]{:S(2)}, u32[]{:S(2)}) %collective-permute-start.60) | collective-permute-done | bytes 131104 | tf_op jit(solution)/shard_map/ppermute | solution.py:631
  208.0 7.3 %collective-permute-done.58.refs_8_ = bf16[128,512]{1,0:T(8,128)(2,1)S(1)} collective-permute-done((bf16[128,512]{1,0:T(8,128)(2,1)}, bf16[128,512]{1,0:T(8,128)(2,1)S(1)}, u32[]{:S(2)}, u32[]{:S(2)}) %collective-permute-start.58) | collective-permute-done | bytes 131104 | tf_op jit(solution)/shard_map/ppermute | solution.py:631
  217.1 6.0 %collective-permute-done.62.refs_12_ = bf16[128,512]{1,0:T(8,128)(2,1)S(1)} collective-permute-done((bf16[128,512]{1,0:T(8,128)(2,1)S(1)}, bf16[128,512]{1,0:T(8,128)(2,1)S(1)}, u32[]{:S(2)}, u32[]{:S(2)}) %collective-permute-start.62) | collective-permute-done | bytes 131104 | tf_op jit(solution)/shard_map/ppermute | solution.py:631
  226.9 2.7 %collective-permute-done.69.refs_1_ = bf16[128,512]{1,0:T(8,128)(2,1)S(1)} collective-permute-done((bf16[128,512]{1,0:T(8,128)(2,1)S(1)}, bf16[128,512]{1,0:T(8,128)(2,1)S(1)}, u32[]{:S(2)}, u32[]{:S(2)}) %collective-permute-start.69) | collective-permute-done | bytes 131104 | tf_op jit(solution)/shard_map/ppermute | solution.py:631
  231.6 2.4 collective-permute-start.72
  236.3 5.9 %collective-permute-start.74 = (f32[64,128]{1,0:T(8,128)S(1)}, f32[64,128]{1,0:T(8,128)S(1)}, u32[]{:S(2)}, u32[]{:S(2)}) collective-permute-start(f32[64,128]{1,0:T(8,128)S(1)} %fusion.25.own_a), channel_id=1, source_target_pairs={{0,1},{1,0},{2,3},{3,2},{4,5},{5,4},{6,7},{7,6},{8,9},{9,8},{10,11... | collective-permute-start | bytes 98312 | tf_op jit(solution)/shard_map/ppermute | solution.py:845
  (235 shorter events, 78.9 us)
Async XLA Ops:
  1.2 19.6 %collective-permute-start.8 = (bf16[4096,256]{1,0:T(8,128)(2,1)}, bf16[4096,256]{1,0:T(8,128)(2,1)}, u32[]{:S(2)}, u32[]{:S(2)}) collective-permute-start(bf16[4096,256]{1,0:T(8,128)(2,1)} %refs_7_.1), channel_id=1, source_target_pairs={{0,1},{1,0},{2,3},{3,2},{4,5},{5,4},{6,7},{7,6},{8,9},{9,8},{10,11... | collective-permute-start | bytes 6291464 | tf_op jit(solution)/shard_map/ppermute | solution.py:54
  18.6 14.3 %collective-permute-start.9 = (bf16[4,256,256]{2,1,0:T(8,128)(2,1)}, bf16[4,256,256]{2,1,0:T(8,128)(2,1)}, u32[]{:S(2)}, u32[]{:S(2)}) collective-permute-start(bf16[4,256,256]{2,1,0:T(8,128)(2,1)} %get-tuple-element.123), channel_id=1, source_target_pairs={{0,2},{2,0},{1,3},{3,1},{4,6},{6,4},{5,7},{7,5},{8,10},{10,8},{9,1... | collective-permute-start | bytes 1572872 | tf_op jit(solution)/shard_map/ppermute | solution.py:631
  19.3 65.2 %collective-permute-start.26 = (bf16[4096,256]{1,0:T(8,128)(2,1)S(1)}, bf16[4096,256]{1,0:T(8,128)(2,1)}, u32[]{:S(2)}, u32[]{:S(2)}) collective-permute-start(bf16[4096,256]{1,0:T(8,128)(2,1)S(1)} %copy-done.1), channel_id=1, source_target_pairs={{0,1},{1,0},{2,3},{3,2},{4,5},{5,4},{6,7},{7,6},{8,9},{9,8},{10,11... | collective-permute-start | bytes 6291464 | tf_op jit(solution)/shard_map/ppermute | solution.py:54
  36.4 10.0 %collective-permute-start.12 = (bf16[272,512]{1,0:T(8,128)(2,1)S(1)}, bf16[272,512]{1,0:T(8,128)(2,1)S(1)}, u32[]{:S(2)}, u32[]{:S(2)}) collective-permute-start(bf16[272,512]{1,0:T(8,128)(2,1)S(1)} %maximum_select_fusion.1.refs_0_), channel_id=1, source_target_pairs={{0,4},{4,8},{8,12},{12,0},{1,5},{5,9},{9,13},{13,1},{2,6},{6,10},{... | collective-permute-start | bytes 835592 | tf_op jit(solution)/shard_map/ppermute | solution.py:631
  38.6 13.4 %collective-permute-start.16 = (bf16[256,512]{1,0:T(8,128)(2,1)S(1)}, bf16[256,512]{1,0:T(8,128)(2,1)S(1)}, u32[]{:S(2)}, u32[]{:S(2)}) collective-permute-start(bf16[256,512]{1,0:T(8,128)(2,1)S(1)} %maximum_select_fusion.2.refs_1_), channel_id=1, source_target_pairs={{0,4},{4,8},{8,12},{12,0},{1,5},{5,9},{9,13},{13,1},{2,6},{6,10},{... | collective-permute-start | bytes 786440 | tf_op jit(solution)/shard_map/ppermute | solution.py:631
  38.8 13.3 %collective-permute-start.17 = (bf16[256,512]{1,0:T(8,128)(2,1)S(1)}, bf16[256,512]{1,0:T(8,128)(2,1)S(1)}, u32[]{:S(2)}, u32[]{:S(2)}) collective-permute-start(bf16[256,512]{1,0:T(8,128)(2,1)S(1)} %maximum_select_fusion.2.refs_1_), channel_id=1, source_target_pairs={{0,2},{2,0},{1,3},{3,1},{4,6},{6,4},{5,7},{7,5},{8,10},{10,8},{9,1... | collective-permute-start | bytes 786440 | tf_op jit(solution)/shard_map/ppermute | solution.py:631
  46.4 11.6 %collective-permute-start.14 = (bf16[272,512]{1,0:T(8,128)(2,1)S(1)}, bf16[272,512]{1,0:T(8,128)(2,1)S(1)}, u32[]{:S(2)}, u32[]{:S(2)}) collective-permute-start(bf16[272,512]{1,0:T(8,128)(2,1)S(1)} %collective-permute-done.12.refs_4_), channel_id=1, source_target_pairs={{0,4},{4,8},{8,12},{12,0},{1,5},{5,9},{9,13},{13,1},{2,6},{6,10},{... | collective-permute-start | bytes 835592 | tf_op jit(solution)/shard_map/ppermute | solution.py:631
  46.4 11.6 %collective-permute-start.15 = (bf16[272,512]{1,0:T(8,128)(2,1)S(1)}, bf16[272,512]{1,0:T(8,128)(2,1)S(1)}, u32[]{:S(2)}, u32[]{:S(2)}) collective-permute-start(bf16[272,512]{1,0:T(8,128)(2,1)S(1)} %collective-permute-done.12.refs_4_), channel_id=1, source_target_pairs={{0,2},{2,0},{1,3},{3,1},{4,6},{6,4},{5,7},{7,5},{8,10},{10,8},{9,1... | collective-permute-start | bytes 835592 | tf_op jit(solution)/shard_map/ppermute | solution.py:631
  52.0 11.6 %collective-permute-start.20 = (bf16[256,512]{1,0:T(8,128)(2,1)S(1)}, bf16[256,512]{1,0:T(8,128)(2,1)S(1)}, u32[]{:S(2)}, u32[]{:S(2)}) collective-permute-start(bf16[256,512]{1,0:T(8,128)(2,1)S(1)} %collective-permute-done.16.refs_5_), channel_id=1, source_target_pairs={{0,4},{4,8},{8,12},{12,0},{1,5},{5,9},{9,13},{13,1},{2,6},{6,10},{... | collective-permute-start | bytes 786440 | tf_op jit(solution)/shard_map/ppermute | solution.py:631
  52.0 11.6 %collective-permute-start.21 = (bf16[256,512]{1,0:T(8,128)(2,1)S(1)}, bf16[256,512]{1,0:T(8,128)(2,1)S(1)}, u32[]{:S(2)}, u32[]{:S(2)}) collective-permute-start(bf16[256,512]{1,0:T(8,128)(2,1)S(1)} %collective-permute-done.16.refs_5_), channel_id=1, source_target_pairs={{0,2},{2,0},{1,3},{3,1},{4,6},{6,4},{5,7},{7,5},{8,10},{10,8},{9,1... | collective-permute-start | bytes 786440 | tf_op jit(solution)/shard_map/ppermute | solution.py:631
  58.0 11.6 %collective-permute-start.18 = (bf16[272,512]{1,0:T(8,128)(2,1)S(1)}, bf16[272,512]{1,0:T(8,128)(2,1)S(1)}, u32[]{:S(2)}, u32[]{:S(2)}) collective-permute-start(bf16[272,512]{1,0:T(8,128)(2,1)S(1)} %collective-permute-done.14.refs_8_), channel_id=1, source_target_pairs={{0,4},{4,8},{8,12},{12,0},{1,5},{5,9},{9,13},{13,1},{2,6},{6,10},{... | collective-permute-start | bytes 835592 | tf_op jit(solution)/shard_map/ppermute | solution.py:631
  58.0 11.6 %collective-permute-start.19 = (bf16[272,512]{1,0:T(8,128)(2,1)S(1)}, bf16[272,512]{1,0:T(8,128)(2,1)S(1)}, u32[]{:S(2)}, u32[]{:S(2)}) collective-permute-start(bf16[272,512]{1,0:T(8,128)(2,1)S(1)} %collective-permute-done.14.refs_8_), channel_id=1, source_target_pairs={{0,2},{2,0},{1,3},{3,1},{4,6},{6,4},{5,7},{7,5},{8,10},{10,8},{9,1... | collective-permute-start | bytes 835592 | tf_op jit(solution)/shard_map/ppermute | solution.py:631
  63.6 11.6 %collective-permute-start.23 = (bf16[256,512]{1,0:T(8,128)(2,1)S(1)}, bf16[256,512]{1,0:T(8,128)(2,1)S(1)}, u32[]{:S(2)}, u32[]{:S(2)}) collective-permute-start(bf16[256,512]{1,0:T(8,128)(2,1)S(1)} %collective-permute-done.20.refs_9_), channel_id=1, source_target_pairs={{0,4},{4,8},{8,12},{12,0},{1,5},{5,9},{9,13},{13,1},{2,6},{6,10},{... | collective-permute-start | bytes 786440 | tf_op jit(solution)/shard_map/ppermute | solution.py:631
  63.6 11.6 %collective-permute-start.24 = (bf16[256,512]{1,0:T(8,128)(2,1)S(1)}, bf16[256,512]{1,0:T(8,128)(2,1)S(1)}, u32[]{:S(2)}, u32[]{:S(2)}) collective-permute-start(bf16[256,512]{1,0:T(8,128)(2,1)S(1)} %collective-permute-done.20.refs_9_), channel_id=1, source_target_pairs={{0,2},{2,0},{1,3},{3,1},{4,6},{6,4},{5,7},{7,5},{8,10},{10,8},{9,1... | collective-permute-start | bytes 786440 | tf_op jit(solution)/shard_map/ppermute | solution.py:631
  69.6 14.9 %collective-permute-start.22 = (bf16[272,512]{1,0:T(8,128)(2,1)S(1)}, bf16[272,512]{1,0:T(8,128)(2,1)S(1)}, u32[]{:S(2)}, u32[]{:S(2)}) collective-permute-start(bf16[272,512]{1,0:T(8,128)(2,1)S(1)} %collective-permute-done.18.refs_12_), channel_id=1, source_target_pairs={{0,2},{2,0},{1,3},{3,1},{4,6},{6,4},{5,7},{7,5},{8,10},{10,8},{9,1... | collective-permute-start | bytes 835592 | tf_op jit(solution)/shard_map/ppermute | solution.py:631
  75.2 9.3 %collective-permute-start.25 = (bf16[256,512]{1,0:T(8,128)(2,1)S(1)}, bf16[256,512]{1,0:T(8,128)(2,1)S(1)}, u32[]{:S(2)}, u32[]{:S(2)}) collective-permute-start(bf16[256,512]{1,0:T(8,128)(2,1)S(1)} %collective-permute-done.24.refs_11_), channel_id=1, source_target_pairs={{0,4},{4,8},{8,12},{12,0},{1,5},{5,9},{9,13},{13,1},{2,6},{6,10},{... | collective-permute-start | bytes 786440 | tf_op jit(solution)/shard_map/ppermute | solution.py:631
  91.3 25.5 %collective-permute-start.30 = (bf16[2,512,256]{2,1,0:T(8,128)(2,1)}, bf16[2,512,256]{2,1,0:T(8,128)(2,1)S(1)}, u32[]{:S(2)}, u32[]{:S(2)}) collective-permute-start(bf16[2,512,256]{2,1,0:T(8,128)(2,1)} %get-tuple-element.158), channel_id=1, source_target_pairs={{0,17},{1,16},{16,1},{17,0},{2,19},{3,18},{18,3},{19,2},{4,21},{5,... | collective-permute-start | bytes 1572872 | tf_op jit(solution)/shard_map/ppermute | solution.py:789
  92.8 23.9 %collective-permute-start.29 = (bf16[2,512,256]{2,1,0:T(8,128)(2,1)}, bf16[2,512,256]{2,1,0:T(8,128)(2,1)S(1)}, u32[]{:S(2)}, u32[]{:S(2)}) collective-permute-start(bf16[2,512,256]{2,1,0:T(8,128)(2,1)} %get-tuple-element.161.refs_2_), channel_id=1, source_target_pairs={{0,16},{1,17},{16,0},{17,1},{2,18},{3,19},{18,2},{19,3},{4,20},{5,... | collective-permute-start | bytes 1572872 | tf_op jit(solution)/shard_map/ppermute | solution.py:789
  94.4 22.4 %collective-permute-start.33 = (bf16[2,256,256]{2,1,0:T(8,128)(2,1)S(1)}, bf16[2,256,256]{2,1,0:T(8,128)(2,1)S(1)}, u32[]{:S(2)}, u32[]{:S(2)}) collective-permute-start(bf16[2,256,256]{2,1,0:T(8,128)(2,1)S(1)} %pad_maximum_fusion.4), channel_id=1, source_target_pairs={{0,12},{4,0},{8,4},{12,8},{1,13},{5,1},{9,5},{13,9},{2,14},{6,2},{... | collective-permute-start | bytes 786440 | tf_op jit(solution)/shard_map/ppermute | solution.py:631
  97.8 22.3 %collective-permute-start.32 = (bf16[2,256,256]{2,1,0:T(8,128)(2,1)S(1)}, bf16[2,256,256]{2,1,0:T(8,128)(2,1)S(1)}, u32[]{:S(2)}, u32[]{:S(2)}) collective-permute-start(bf16[2,256,256]{2,1,0:T(8,128)(2,1)S(1)} %pad_maximum_fusion.3), channel_id=1, source_target_pairs={{0,8},{4,12},{8,0},{12,4},{1,9},{5,13},{9,1},{13,5},{2,10},{6,14},... | collective-permute-start | bytes 786440 | tf_op jit(solution)/shard_map/ppermute | solution.py:631
  97.9 22.2 %collective-permute-start.31 = (bf16[2,256,256]{2,1,0:T(8,128)(2,1)S(1)}, bf16[2,256,256]{2,1,0:T(8,128)(2,1)S(1)}, u32[]{:S(2)}, u32[]{:S(2)}) collective-permute-start(bf16[2,256,256]{2,1,0:T(8,128)(2,1)S(1)} %pad_maximum_fusion.2), channel_id=1, source_target_pairs={{0,4},{4,8},{8,12},{12,0},{1,5},{5,9},{9,13},{13,1},{2,6},{6,10},{... | collective-permute-start | bytes 786440 | tf_op jit(solution)/shard_map/ppermute | solution.py:631
  131.2 9.4 %collective-permute-start.35 = (bf16[256,512]{1,0:T(8,128)(2,1)S(1)}, bf16[256,512]{1,0:T(8,128)(2,1)S(1)}, u32[]{:S(2)}, u32[]{:S(2)}) collective-permute-start(bf16[256,512]{1,0:T(8,128)(2,1)S(1)} %maximum_select_fusion.3.refs_0_), channel_id=1, source_target_pairs={{0,4},{4,8},{8,12},{12,0},{1,5},{5,9},{9,13},{13,1},{2,6},{6,10},{... | collective-permute-start | bytes 786440 | tf_op jit(solution)/shard_map/ppermute | solution.py:631
  133.1 13.2 %collective-permute-start.39 = (bf16[256,512]{1,0:T(8,128)(2,1)S(1)}, bf16[256,512]{1,0:T(8,128)(2,1)S(1)}, u32[]{:S(2)}, u32[]{:S(2)}) collective-permute-start(bf16[256,512]{1,0:T(8,128)(2,1)S(1)} %maximum_select_fusion.4.refs_1_), channel_id=1, source_target_pairs={{0,4},{4,8},{8,12},{12,0},{1,5},{5,9},{9,13},{13,1},{2,6},{6,10},{... | collective-permute-start | bytes 786440 | tf_op jit(solution)/shard_map/ppermute | solution.py:631
  135.4 12.1 %collective-permute-start.40 = (bf16[256,512]{1,0:T(8,128)(2,1)S(1)}, bf16[256,512]{1,0:T(8,128)(2,1)S(1)}, u32[]{:S(2)}, u32[]{:S(2)}) collective-permute-start(bf16[256,512]{1,0:T(8,128)(2,1)S(1)} %maximum_select_fusion.4.refs_1_), channel_id=1, source_target_pairs={{0,2},{2,0},{1,3},{3,1},{4,6},{6,4},{5,7},{7,5},{8,10},{10,8},{9,1... | collective-permute-start | bytes 786440 | tf_op jit(solution)/shard_map/ppermute | solution.py:631
  140.6 11.2 %collective-permute-start.37 = (bf16[256,512]{1,0:T(8,128)(2,1)S(1)}, bf16[256,512]{1,0:T(8,128)(2,1)S(1)}, u32[]{:S(2)}, u32[]{:S(2)}) collective-permute-start(bf16[256,512]{1,0:T(8,128)(2,1)S(1)} %collective-permute-done.35.refs_4_), channel_id=1, source_target_pairs={{0,4},{4,8},{8,12},{12,0},{1,5},{5,9},{9,13},{13,1},{2,6},{6,10},{... | collective-permute-start | bytes 786440 | tf_op jit(solution)/shard_map/ppermute | solution.py:631
  141.4 11.2 %collective-permute-start.38 = (bf16[256,512]{1,0:T(8,128)(2,1)S(1)}, bf16[256,512]{1,0:T(8,128)(2,1)S(1)}, u32[]{:S(2)}, u32[]{:S(2)}) collective-permute-start(bf16[256,512]{1,0:T(8,128)(2,1)S(1)} %collective-permute-done.35.refs_4_), channel_id=1, source_target_pairs={{0,2},{2,0},{1,3},{3,1},{4,6},{6,4},{5,7},{7,5},{8,10},{10,8},{9,1... | collective-permute-start | bytes 786440 | tf_op jit(solution)/shard_map/ppermute | solution.py:631
  142.3 30.4 %collective-permute-start.49 = (bf16[8,256,256]{2,1,0:T(8,128)(2,1)S(1)}, bf16[8,256,256]{2,1,0:T(8,128)(2,1)S(1)}, u32[]{:S(2)}, u32[]{:S(2)}) collective-permute-start(bf16[8,256,256]{2,1,0:T(8,128)(2,1)S(1)} %constant_dynamic-update-slice_fusion.refs_14_.refs_18_.refs_22_.refs_26_.refs_30_.refs_34_.refs_38, ...), channel_id=1, source_target_pairs={{0,1},{1,0},{2,3},{3,2},{4,5},{5,4},{6,7},{7,6},{8,9},{9,8},{10,11... | collective-permute-start | bytes 3145736 | tf_op jit(solution)/shard_map/ppermute | solution.py:54
  146.2 27.5 %collective-permute-start.50 = (bf16[8,256,256]{2,1,0:T(8,128)(2,1)S(1)}, bf16[8,256,256]{2,1,0:T(8,128)(2,1)S(1)}, u32[]{:S(2)}, u32[]{:S(2)}) collective-permute-start(bf16[8,256,256]{2,1,0:T(8,128)(2,1)S(1)} %constant_dynamic-update-slice_fusion.refs_14_.refs_18_.refs_22_.refs_26_.refs_30_.refs_34_.refs_38, ...), channel_id=1, source_target_pairs={{0,16},{16,0},{1,17},{17,1},{2,18},{18,2},{3,19},{19,3},{4,20},{20... | collective-permute-start | bytes 3145736 | tf_op jit(solution)/shard_map/ppermute | solution.py:631
  152.6 9.7 %collective-permute-start.41 = (bf16[256,512]{1,0:T(8,128)(2,1)S(1)}, bf16[256,512]{1,0:T(8,128)(2,1)S(1)}, u32[]{:S(2)}, u32[]{:S(2)}) collective-permute-start(bf16[256,512]{1,0:T(8,128)(2,1)S(1)} %collective-permute-done.37.refs_8_), channel_id=1, source_target_pairs={{0,4},{4,8},{8,12},{12,0},{1,5},{5,9},{9,13},{13,1},{2,6},{6,10},{... | collective-permute-start | bytes 786440 | tf_op jit(solution)/shard_map/ppermute | solution.py:631
  163.4 12.2 %collective-permute-start.45 = (bf16[256,512]{1,0:T(8,128)(2,1)S(1)}, bf16[256,512]{1,0:T(8,128)(2,1)S(1)}, u32[]{:S(2)}, u32[]{:S(2)}) collective-permute-start(bf16[256,512]{1,0:T(8,128)(2,1)S(1)} %collective-permute-done.41.refs_12_), channel_id=1, source_target_pairs={{0,2},{2,0},{1,3},{3,1},{4,6},{6,4},{5,7},{7,5},{8,10},{10,8},{9,1... | collective-permute-start | bytes 786440 | tf_op jit(solution)/shard_map/ppermute | solution.py:631
  175.6 12.0 %collective-permute-start.52 = (bf16[8,256,256]{2,1,0:T(8,128)(2,1)S(1)}, bf16[8,256,256]{2,1,0:T(8,128)(2,1)S(1)}, u32[]{:S(2)}, u32[]{:S(2)}) collective-permute-start(bf16[8,256,256]{2,1,0:T(8,128)(2,1)S(1)} %collective-permute-done.50.refs_16_.refs_20_.refs_24_.refs_28_.refs_32_.refs_36_.refs_40_.refs_4_), channel_id=1, source_target_pairs={{0,1},{1,0},{2,3},{3,2},{4,5},{5,4},{6,7},{7,6},{8,9},{9,8},{10,11... | collective-permute-start | bytes 3145736 | tf_op jit(solution)/shard_map/ppermute | solution.py:54
  235.7 9.4 %collective-permute-start.73 = (f32[64,128]{1,0:T(8,128)S(1)}, f32[64,128]{1,0:T(8,128)S(1)}, u32[]{:S(2)}, u32[]{:S(2)}) collective-permute-start(f32[64,128]{1,0:T(8,128)S(1)} %fusion.25.own_a), channel_id=1, source_target_pairs={{0,2},{1,3},{2,0},{3,1},{4,6},{5,7},{6,4},{7,5},{8,10},{9,11},{10,... | collective-permute-start | bytes 98312 | tf_op jit(solution)/shard_map/ppermute | solution.py:845
  (74 other events, 1018.2 us)

commit v10 on v9

--- a/solution.py
+++ b/solution.py
@@ -63,10 +63,27 @@
 
 def down_kernel(images, tiles, half, meta, *refs):
     lat_refs, refs = refs[:tiles], refs[tiles:]
-    conv_ref, patch_ref, own_text, par_text, gain_ref = refs[:5]
-    weight_refs, (first_ref, second_ref), held_refs = refs[5:11], refs[11:13], refs[13:19]
-    grid_rows, conv_wide, conv_bf16, windows, total, arrived = refs[19:]
+    conv_ref, gain_ref, patch_hbm, text_hbm = refs[:4]
+    weight_refs, (first_ref, second_ref), held_refs = refs[4:10], refs[10:12], refs[12:18]
+    grid_rows, conv_wide, conv_bf16, windows, total, patch_ref, text_ref = refs[18:25]
+    arrived, patch_arrived, text_arrived = refs[25:]
     step = pl.program_id(0)
+    deep = PATCH * CH
+    patch_copies = [
+        pltpu.make_async_copy(
+            patch_hbm.at[index * deep : (index + 1) * deep, :], patch_ref.at[index], patch_arrived.at[index]
+        )
+        for index in range(PATCH)
+    ]
+    side_rows = [jnp.bitwise_xor(meta[3 * images + 1], side) * half for side in range(2)]
+    text_copies = [
+        pltpu.make_async_copy(
+            text_hbm.at[pl.ds(pl.multiple_of(side_rows[side], half), half), :],
+            text_ref.at[side],
+            text_arrived.at[side],
+        )
+        for side in range(2)
+    ]
     copies = [
         pltpu.make_async_copy(weight, held, arrived.at[index])
         for index, (weight, held) in enumerate(zip(weight_refs, held_refs))
@@ -74,7 +91,7 @@
 
     @pl.when(step == 0)
     def _():
-        for copy in copies:
+        for copy in patch_copies + text_copies + copies:
             copy.start()
 
     group = images * SIDE
@@ -119,17 +136,22 @@
         lax.fori_loop(0, images, build, 0)
         total[...] = jnp.zeros_like(total)
 
+    for index in range(PATCH):
+        pl.when(step == index)(patch_copies[index].wait)
+
     chunk = 256
     for part in range(images * IMG_TOK // chunk):
         rows = slice(part * chunk, (part + 1) * chunk)
         hidden = silu(mxu(windows[step, rows, :], conv_bf16[...])).astype(BF16)
-        total[rows, :] += mxu(hidden, patch_ref[...])
+        total[rows, :] += mxu(hidden, patch_ref[step])
 
     @pl.when(step == PATCH - 1)
     def _():
         tokens = total[...].astype(BF16)
         block = half // 2
-        for side, text_ref in enumerate((own_text, par_text)):
+        for copy in text_copies:
+            copy.wait()
+        for side in range(2):
             base = ctx * (2 * half) + jnp.bitwise_xor(core, side) * half
             for part, out_ref in enumerate((first_ref, second_ref)):
                 place = base + part * block + lax.broadcasted_iota(jnp.int32, (block, 1), 0)
@@ -141,7 +163,7 @@
                     source = jnp.where(inside, index, source)
                 choice = source == lax.broadcasted_iota(jnp.int32, (block, images * IMG_TOK), 1)
                 picked = mxu(jnp.where(choice, 1.0, 0.0).astype(BF16), tokens)
-                text = text_ref[0, part * block : (part + 1) * block, :].astype(F32)
+                text = text_ref[side, part * block : (part + 1) * block, :].astype(F32)
                 out_ref[side, :block, :] = jnp.where(source >= 0, picked, text).astype(BF16)
             gain = gain_ref[...].astype(F32)
             first_ref[side, block:, :] = jnp.broadcast_to(gain, (GAIN_ROWS, gain.shape[1])).astype(BF16)
@@ -154,8 +176,6 @@
     half = seq_rows // 2
     tiles = len(pieces)
     count = images * IMG_TOK
-    halves = text.reshape(2, half, width)
-    core_at = 3 * images + 1
     first, second = (2, half // 2 + GAIN_ROWS, width), (2, half // 2, width)
     return pl.pallas_call(
         functools.partial(down_kernel, images, tiles, half),
@@ -165,12 +185,9 @@
             in_specs=[full(p.shape) for p in pieces]
             + [
                 full(conv.shape),
-                pl.BlockSpec((PATCH * CH, width), lambda i, m: (i, 0)),
-                pl.BlockSpec((1, half, width), lambda i, m: (m[core_at], 0, 0)),
-                pl.BlockSpec((1, half, width), lambda i, m: (1 - m[core_at], 0, 0)),
                 full((1, width)),
             ]
-            + [pl.BlockSpec(memory_space=pl.ANY)] * 6,
+            + [pl.BlockSpec(memory_space=pltpu.HBM)] * 8,
             out_specs=[full(first), full(second)] + [HELD] * 6,
             scratch_shapes=[
                 pltpu.VMEM((images, WL * CIN // HD + 1, TOP + HL + 16, HD), F32),
@@ -178,7 +195,11 @@
                 pltpu.VMEM((TAPS, PATCH * CH), BF16),
                 pltpu.VMEM((PATCH, count, TAPS), BF16),
                 pltpu.VMEM((count, width), F32),
+                pltpu.VMEM((PATCH, PATCH * CH, width), BF16),
+                pltpu.VMEM((2, half, width), BF16),
                 pltpu.SemaphoreType.DMA((6,)),
+                pltpu.SemaphoreType.DMA((PATCH,)),
+                pltpu.SemaphoreType.DMA((2,)),
             ],
         ),
         out_shape=[jax.ShapeDtypeStruct(first, BF16), jax.ShapeDtypeStruct(second, BF16)]
@@ -186,7 +207,7 @@
         compiler_params=params(32),
         cost_estimate=cost(2 * count * PIX * CH * (256 + width), 4 << 20, count * PIX * CH),
         name="down_stream",
-    )(meta, *pieces, conv, patch_in, halves, halves, gain.reshape(1, width), *weights)
+    )(meta, *pieces, conv, gain.reshape(1, width), patch_in, text, *weights)
 
 
 def full(shape):
@@ -210,27 +231,19 @@
     refs = list(refs)
     count = len(entries)
     x_refs = take_blocks(refs, count)
-    weight_refs = [refs.pop(0) for _ in range(6)]
+    scaled_ref = refs.pop(-1)
     if last:
-        acc_in, square_in, head_gains = refs.pop(0), refs.pop(0), refs.pop(0)
-        fetched, arrived = refs.pop(-3), refs.pop(-2)
-        span = fetched.shape[1]
-        rows = pl.ds(pl.multiple_of(chip_of(meta, *layout, entries[0]) * span, span), span)
-        copies = [
-            pltpu.make_async_copy(weight.at[rows, :], fetched.at[part], arrived.at[part])
-            for part, weight in enumerate(weight_refs)
-        ]
-        for copy in copies:
-            copy.start()
-    scaled_ref = refs.pop(-1)
+        weights_ref, acc_in, square_in, head_gains = [refs.pop(0) for _ in range(4)]
+    else:
+        weight_refs = [refs.pop(0) for _ in range(6)]
     half, span = scaled_ref.shape
-    width = weight_refs[0].shape[1]
+    width = weights_ref.shape[2] if last else weight_refs[0].shape[1]
     heads = width // HD
     square = square_in[...] if last else None
     if last:
         acc, outs = [None] * 6, refs
     else:
-        acc_out, square_out = refs
+        weights_out, acc_out, square_out = refs
     for index in range(count):
         rows = pl.ds(pl.multiple_of(chip_of(meta, *layout, entries[index]) * span, span), span)
         gain = x_refs[index][0][half // 2 :, :][:1]
@@ -245,8 +258,7 @@
             square = piece if square is None else square + piece
         for part in range(6):
             if last:
-                copies[part].wait()
-                acc[part] = acc_in[part] + mxu(scaled_ref[...], fetched[part])
+                acc[part] = acc_in[part] + mxu(scaled_ref[...], weights_ref[part])
                 continue
             term = mxu(scaled_ref[...], weight_refs[part][rows, :])
             if index == 0:
@@ -255,43 +267,52 @@
                 acc_out[part] += term
     if not last:
         square_out[...] = square
+        rows = pl.ds(pl.multiple_of(chip_of(meta, *layout, len(entries)) * span, span), span)
+        for part in range(6):
+            weights_out[part] = weight_refs[part][rows, :]
         return
     mean = jnp.sum(square, axis=-1, keepdims=True) * (1.0 / (groups * span))
     scale = lax.rsqrt(mean + EPSILON)
     for part in range(6):
         total = acc[part] * scale
         side, kind = part // 3, part % 3
-        kv_out, q_out = outs[2 * side : 2 * side + 2]
+        kv_outs = outs[2 * heads * side : 2 * heads * side + heads]
+        q_outs = outs[2 * heads * side + heads : 2 * heads * (side + 1)]
         for head in range(heads):
-            lanes = slice(head * HD, (head + 1) * HD)
-            raw = total[:, lanes]
+            raw = total[:, head * HD : (head + 1) * HD]
             if kind == 1:
-                kv_out[1, :, lanes] = raw.astype(BF16)
+                kv_outs[head][1] = raw.astype(BF16)
                 continue
             raw = raw * lax.rsqrt(jnp.mean(raw * raw, axis=-1, keepdims=True) + EPSILON)
             if kind == 0:
-                kv_out[0, :, lanes] = (raw * head_gains[1:2, :]).astype(BF16)
+                kv_outs[head][0] = (raw * head_gains[1:2, :]).astype(BF16)
             else:
-                q_out[:, lanes] = (raw * (head_gains[0:1, :] * HD ** (-0.5))).astype(BF16)
+                q_outs[head][...] = (raw * (head_gains[0:1, :] * HD ** (-0.5))).astype(BF16)
 
 
 def qkv_step(meta, layout, blocks, entries, weights, state, head_gains):
     span = blocks[0][1].shape[1]
     half = 2 * blocks[0][1].shape[0]
-    width = weights[0].shape[1]
     count, last = len(blocks), state is not None
+    width = state[0].shape[2] if last else weights[0].shape[1]
     groups = layout[1] * layout[2]
-    inputs = [p for pieces in blocks for p in pieces] + list(weights)
+    inputs = [p for pieces in blocks for p in pieces]
     specs = [full(p.shape) for pieces in blocks for p in pieces]
     scratch = [pltpu.VMEM((half, span), BF16)]
     if last:
-        specs += [pl.BlockSpec(memory_space=pltpu.HBM)] * 6 + [HELD] * 2 + [full(head_gains.shape)]
+        specs += [HELD] * 3 + [full(head_gains.shape)]
         inputs += list(state) + [head_gains]
-        outs = [pltpu.HBM((2, half, width), BF16), pltpu.HBM((half, width), BF16)] * 2
-        scratch = [pltpu.VMEM((6, span, width), BF16), pltpu.SemaphoreType.DMA((6,))] + scratch
+        heads = width // HD
+        outs = [pltpu.HBM((2, half, HD), BF16)] * heads + [pltpu.HBM((half, HD), BF16)] * heads
+        outs = outs * 2
     else:
         specs += [HELD] * 6
-        outs = [pltpu.VMEM((6, half, width), F32), pltpu.VMEM((half, HD), F32)]
+        inputs += list(weights)
+        outs = [
+            pltpu.VMEM((6, span, width), BF16),
+            pltpu.VMEM((6, half, width), F32),
+            pltpu.VMEM((half, HD), F32),
+        ]
     return pl.pallas_call(
         functools.partial(qkv_kernel, entries, layout, groups, last),
         grid_spec=pltpu.PrefetchScalarGridSpec(
@@ -361,7 +382,7 @@
             out_specs=[rows, rows],
         ),
         out_shape=[jax.ShapeDtypeStruct((half, width), BF16)] * 2,
-        compiler_params=params(32),
+        compiler_params=params(24),
         cost_estimate=cost(8 * half * keys * width, 4 * keys * width, 2 * half * keys * width // HD),
         name="attention",
     )(meta, *queries, *pieces)
@@ -772,13 +793,15 @@
 
     def project(blocks, entries, state, last):
         return qkv_step(
-            meta, layout, blocks, entries, weights if last else held_weights, state, head_gains
+            meta, layout, blocks, entries, held_weights, state, head_gains
         )
 
     state, out_par = gather_pair(
         *[by_core(core, s[0], o, 1) for s, o in zip(streams, others)], None, project, swap(out_weight)
     )
-    kv_send, q_send, kv_own, q_own = state
+    heads = width // HD
+    kv_send, q_send = state[:heads], state[heads : 2 * heads]
+    kv_own, q_own = state[2 * heads : 3 * heads], state[3 * heads :]
 
     def shifted(values, step, cross):
         pairs = [
@@ -788,19 +811,27 @@
         ]
         return lax.ppermute(values, ("ctx", "core"), pairs)
 
-    q_par = swap(q_send)
-    q_par, kept, received = lax.optimization_barrier((q_par, kept, received))
+    results = []
+    for head in range(heads):
+        q_par = swap(q_send[head])
+        pieces = [kv_own[head], swap(kv_send[head])]
+        for step in range(1, ctxs):
+            pieces += [shifted(kv_own[head], step, False), shifted(kv_send[head], step, True)]
+        q_par, q_send, kv_send, kv_own, kept, received = lax.optimization_barrier(
+            (q_par, q_send, kv_send, kv_own, kept, received)
+        )
+        results.append(attention(meta, [q_own[head], q_par], pieces, images))
     up_blocks = [transpose_second(kept, received, step) for step in range(tiles)]
-    pieces = [kv_own, swap(kv_send)]
-    for step in range(1, ctxs):
-        pieces += [shifted(kv_own, step, False), shifted(kv_send, step, True)]
-    pieces, up_blocks = lax.optimization_barrier((pieces, up_blocks))
-    att_own, att_send = attention(meta, [q_own, q_par], pieces, images)
-    att_par = swap(att_send)
+    att_own = [result[0] for result in results]
+    att_par = [swap(result[1]) for result in results]
     rows = half // 2
-    attended = [
-        by_core(core, att_own[at : at + rows], att_par[at : at + rows], 1) for at in (0, rows)
-    ]
+    attended = []
+    for at in (0, rows):
+        own, par = (
+            jnp.concatenate([x[at : at + rows] for x in side], axis=1) for side in (att_own, att_par)
+        )
+        attended.append(by_core(core, own, par, 1))
+    attended, up_blocks = lax.optimization_barrier((attended, up_blocks))
     up_own = jnp.concatenate(up_blocks)
     extras = [up_own, swap(up_own)] + ([shift(up_own, "ctx", 1)] if halves == 2 else [])
 

time: 247 us -> 242 us (0.980)
  waiting for transfers between devices: 117 us -> 110 us
  starting transfers between devices: 66.8 us -> 72 us
  local copies, waits for them, and re-layouts: 12.2 us -> 9.5 us
    ppermute x4 -> x6, waiting for transfers between devices: 23.9 us -> 17.5 us  [shifted(): return lax.ppermute(values, ('ctx', 'core'), pairs)]
    ppermute x55, starting transfers between devices: 39.6 us -> 42.5 us  [shift(): lax.ppermute(values, axis, [(i, (i + step) % count) for i in range(count)])]
    pallas_call x2, Pallas kernels: 13 us -> 10.5 us  [qkv_step(): pl.pallas_call(functools.partial(qkv_kernel, entries, layout, groups, las...]
    ppermute x4 -> x6, starting transfers between devices: 3.23 us -> 5.63 us  [shifted(): return lax.ppermute(values, ('ctx', 'core'), pairs)]
    unnamed x64 -> x60, local copies, waits for them, and re-layouts: 8.71 us -> 7.14 us
    ppermute x14 -> x17, waiting for transfers between devices: 4.63 us -> 5.64 us  [swap(): return lax.ppermute(values, 'core', [(0, 1), (1, 0)])]
    pallas_call x1 -> x2, Pallas kernels: 8.54 us -> 8.91 us  [attention(): pl.pallas_call(functools.partial(attention_kernel, images, len(pieces), h...]
    ppermute x14 -> x17, starting transfers between devices: 16.7 us -> 16.6 us  [swap(): return lax.ppermute(values, 'core', [(0, 1), (1, 0)])]
  transfers between devices with their start and end apart: 76 -> 81, of which waited for: 31 -> 33; matrix products, arithmetic and copies ran while one was open for 4% -> 3% of each run, Pallas kernels for 11% -> 16%
where the time goes in v10:
time: 242 us; the launch traced here: 241 us
  waiting for transfers between devices  110 us (45%)
  starting transfers between devices  72 us (30%)
  Pallas kernels  42.7 us (18%)
  local copies, waits for them, and re-layouts  9.5 us (4%)
  other arithmetic  4.57 us (2%)
    ppermute x55, waiting for transfers between devices, shift(): lax.ppermute(values, axis, [(i, (i + step) % count) for i in range(count)])  86.9 us
    ppermute x55, starting transfers between devices, shift(): lax.ppermute(values, axis, [(i, (i + step) % count) for i in range(count)])  42.5 us
    ppermute x6, waiting for transfers between devices, shifted(): return lax.ppermute(values, ('ctx', 'core'), pairs)  17.5 us
    ppermute x17, starting transfers between devices, swap(): return lax.ppermute(values, 'core', [(0, 1), (1, 0)])  16.6 us
    pallas_call x2, Pallas kernels, qkv_step(): pl.pallas_call(functools.partial(qkv_kernel, entries, layout, groups, las...  10.5 us
    pallas_call x1, Pallas kernels, down_stream(): pl.pallas_call(functools.partial(down_kernel, images, tiles, half), grid_...  9.72 us
    pallas_call x2, Pallas kernels, attention(): pl.pallas_call(functools.partial(attention_kernel, images, len(pieces), h...  8.91 us
    ppermute x3, starting transfers between devices, shards(): quad[name] = lax.ppermute(band, ('mpo', 'core'), pairs)  7.28 us
  transfers between devices with their start and end apart: 81, of which 33 were waited for; matrix products, arithmetic and copies ran while one was open for 3% of the time, Pallas kernels for 16%

profile of v10, /device:TPU:1, one launch (start us, length us, event | category | flops | bytes accessed | tf_op | source)
XLA Modules:
  0.0 240.7 jit_solution(13399335395976515944)
XLA Ops:
  1.3 2.7 %collective-permute-start = (bf16[2,16,512]{2,1,0:T(8,128)(2,1)}, bf16[2,16,512]{2,1,0:T(8,128)(2,1)S(1)}, u32[]{:S(2)}, u32[]{:S(2)}) collective-permute-start(bf16[2,16,512]{2,1,0:T(8,128)(2,1)} %param.16), channel_id=1, source_target_pairs={{0,16},{16,0},{1,17},{17,1},{2,18},{18,2},{3,19},{19,3},{4,20},{20... | collective-permute-start | bytes 98312 | tf_op jit(solution)/shard_map/ppermute | solution.py:652
  23.5 9.7 %down_stream.1 = (bf16[2,272,256]{2,1,0:T(8,128)(2,1)S(1)}, bf16[2,256,256]{2,1,0:T(8,128)(2,1)S(1)}, bf16[4096,256]{1,0:T(8,128)(2,1)S(1)}, bf16[4096,256]{1,0:...) custom-call(s32[16]{0:T(128)S(1)} %concatenate.68.meta, ...), custom_call_target="tpu_custom_call" | custom-call | flops 4294967296 | bytes 4194304 | tf_op jit(solution)/shard_map/down_stream/pallas_call | solution.py:180
  39.0 6.9 %collective-permute-done.12.refs_4_ = bf16[272,512]{1,0:T(8,128)(2,1)S(1)} collective-permute-done((bf16[272,512]{1,0:T(8,128)(2,1)S(1)}, bf16[272,512]{1,0:T(8,128)(2,1)S(1)}, u32[]{:S(2)}, u32[]{:S(2)}) %collective-permute-start.12) | collective-permute-done | bytes 278560 | tf_op jit(solution)/shard_map/ppermute | solution.py:652
  47.1 4.5 %collective-permute-done.16.refs_5_ = bf16[256,512]{1,0:T(8,128)(2,1)S(1)} collective-permute-done((bf16[256,512]{1,0:T(8,128)(2,1)S(1)}, bf16[256,512]{1,0:T(8,128)(2,1)S(1)}, u32[]{:S(2)}, u32[]{:S(2)}) %collective-permute-start.16) | collective-permute-done | bytes 262176 | tf_op jit(solution)/shard_map/ppermute | solution.py:652
  52.8 4.8 %collective-permute-done.14.refs_8_ = bf16[272,512]{1,0:T(8,128)(2,1)S(1)} collective-permute-done((bf16[272,512]{1,0:T(8,128)(2,1)S(1)}, bf16[272,512]{1,0:T(8,128)(2,1)S(1)}, u32[]{:S(2)}, u32[]{:S(2)}) %collective-permute-start.14) | collective-permute-done | bytes 278560 | tf_op jit(solution)/shard_map/ppermute | solution.py:652
  58.7 4.5 %collective-permute-done.20.refs_9_ = bf16[256,512]{1,0:T(8,128)(2,1)S(1)} collective-permute-done((bf16[256,512]{1,0:T(8,128)(2,1)S(1)}, bf16[256,512]{1,0:T(8,128)(2,1)S(1)}, u32[]{:S(2)}, u32[]{:S(2)}) %collective-permute-start.20) | collective-permute-done | bytes 262176 | tf_op jit(solution)/shard_map/ppermute | solution.py:652
  64.4 4.8 %collective-permute-done.18.refs_12_ = bf16[272,512]{1,0:T(8,128)(2,1)S(1)} collective-permute-done((bf16[272,512]{1,0:T(8,128)(2,1)S(1)}, bf16[272,512]{1,0:T(8,128)(2,1)S(1)}, u32[]{:S(2)}, u32[]{:S(2)}) %collective-permute-start.18) | collective-permute-done | bytes 278560 | tf_op jit(solution)/shard_map/ppermute | solution.py:652
  70.3 4.5 %collective-permute-done.23.refs_13_ = bf16[256,512]{1,0:T(8,128)(2,1)S(1)} collective-permute-done((bf16[256,512]{1,0:T(8,128)(2,1)S(1)}, bf16[256,512]{1,0:T(8,128)(2,1)S(1)}, u32[]{:S(2)}, u32[]{:S(2)}) %collective-permute-start.23) | collective-permute-done | bytes 262176 | tf_op jit(solution)/shard_map/ppermute | solution.py:652
  74.8 7.8 %qkv_step.1 = (bf16[6,512,256]{2,1,0:T(8,128)(2,1)S(1)}, f32[6,512,256]{2,1,0:T(8,128)S(1)}, f32[512,128]{1,0:T(8,128)S(1)}) custom-call(s32[16]{0:T(128)S(1)} %concatenate.68.meta, bf16[272,512]{1,0:T(8,128)(2,1)S(1)} %maximum_select_fusion.1.refs_0_, bf16[256,512]{1,0:T(8,128)(2,1)S(1)} %maximum_select_fusion.2.refs_1_, ...), custom_call_target="tpu_custom_call" | custom-call | flops 5637144576 | bytes 20971520 | tf_op jit(solution)/shard_map/qkv_step/pallas_call | solution.py:316
  82.9 2.7 %qkv_last.1 = (bf16[2,512,128]{2,1,0:T(8,128)(2,1)}, bf16[2,512,128]{2,1,0:T(8,128)(2,1)}, bf16[512,128]{1,0:T(8,128)(2,1)}, bf16[512,128]{1,0:T(8,128)(2,1)}, b...) custom-call(s32[16]{0:T(128)S(1)} %concatenate.68.meta, ...), custom_call_target="tpu_custom_call" | custom-call | flops 805306368 | bytes 8388608 | tf_op jit(solution)/shard_map/qkv_last/pallas_call | solution.py:316
  94.2 3.3 %collective-permute-done.29.refs_4_ = bf16[2,512,128]{2,1,0:T(8,128)(2,1)S(1)} collective-permute-done((bf16[2,512,128]{2,1,0:T(8,128)(2,1)}, bf16[2,512,128]{2,1,0:T(8,128)(2,1)S(1)}, u32[]{:S(2)}, u32[]{:S(2)}) %collective-permute-start.29) | collective-permute-done | bytes 262176 | tf_op jit(solution)/shard_map/ppermute | solution.py:812
  99.8 4.9 %collective-permute-done.30.refs_5_ = bf16[2,512,128]{2,1,0:T(8,128)(2,1)S(1)} collective-permute-done((bf16[2,512,128]{2,1,0:T(8,128)(2,1)}, bf16[2,512,128]{2,1,0:T(8,128)(2,1)S(1)}, u32[]{:S(2)}, u32[]{:S(2)}) %collective-permute-start.30) | collective-permute-done | bytes 262176 | tf_op jit(solution)/shard_map/ppermute | solution.py:812
  106.3 4.5 %attention.2 = (bf16[512,128]{1,0:T(8,128)(2,1)S(1)}, bf16[512,128]{1,0:T(8,128)(2,1)S(1)}) custom-call(s32[16]{0:T(128)S(1)} %concatenate.68.meta, bf16[512,128]{1,0:T(8,128)(2,1)S(1)} %copy-done.16, bf16[512,128]{1,0:T(8,128)(2,1)S(1)} %collective-permute-done.27.refs_1_, bf16[2,512,128]{2,1,0:T(8,128)(2,1)S(1)} %copy-done.14, ...), custom_call_target="tpu_custom_call" | custom-call | flops 1073741824 | bytes 1048576 | tf_op jit(solution)/shard_map/attention/pallas_call | solution.py:376
  112.0 3.1 %collective-permute-done.34.refs_5_ = bf16[2,512,128]{2,1,0:T(8,128)(2,1)S(1)} collective-permute-done((bf16[2,512,128]{2,1,0:T(8,128)(2,1)S(1)}, bf16[2,512,128]{2,1,0:T(8,128)(2,1)S(1)}, u32[]{:S(2)}, u32[]{:S(2)}) %collective-permute-start.34) | collective-permute-done | bytes 262176 | tf_op jit(solution)/shard_map/ppermute | solution.py:812
  115.1 4.5 %attention.3 = (bf16[512,128]{1,0:T(8,128)(2,1)S(1)}, bf16[512,128]{1,0:T(8,128)(2,1)S(1)}) custom-call(s32[16]{0:T(128)S(1)} %concatenate.68.meta, bf16[512,128]{1,0:T(8,128)(2,1)S(1)} %copy-done.15, bf16[512,128]{1,0:T(8,128)(2,1)S(1)} %collective-permute-done.31.refs_1_, bf16[2,512,128]{2,1,0:T(8,128)(2,1)S(1)} %copy-done.13, ...), custom_call_target="tpu_custom_call" | custom-call | flops 1073741824 | bytes 1048576 | tf_op jit(solution)/shard_map/attention/pallas_call | solution.py:376
  121.2 3.9 %collective-permute-done.38 = bf16[2,256,256]{2,1,0:T(8,128)(2,1)S(1)} collective-permute-done((bf16[2,256,256]{2,1,0:T(8,128)(2,1)S(1)}, bf16[2,256,256]{2,1,0:T(8,128)(2,1)S(1)}, u32[]{:S(2)}, u32[]{:S(2)}) %collective-permute-start.38) | collective-permute-done | bytes 262176 | tf_op jit(solution)/shard_map/ppermute | solution.py:652
  128.4 6.0 %collective-permute-done.40.refs_4_ = bf16[256,512]{1,0:T(8,128)(2,1)S(1)} collective-permute-done((bf16[256,512]{1,0:T(8,128)(2,1)S(1)}, bf16[256,512]{1,0:T(8,128)(2,1)S(1)}, u32[]{:S(2)}, u32[]{:S(2)}) %collective-permute-start.40) | collective-permute-done | bytes 262176 | tf_op jit(solution)/shard_map/ppermute | solution.py:652
  135.5 2.8 %collective-permute-start.54 = (bf16[8,256,256]{2,1,0:T(8,128)(2,1)S(1)}, bf16[8,256,256]{2,1,0:T(8,128)(2,1)S(1)}, u32[]{:S(2)}, u32[]{:S(2)}) collective-permute-start(bf16[8,256,256]{2,1,0:T(8,128)(2,1)S(1)} %constant_dynamic-update-slice_fusion.refs_14_.refs_18_.refs_22_.refs_26_.refs_30_.refs_34_.refs_38, ...), channel_id=1, source_target_pairs={{0,1},{1,0},{2,3},{3,2},{4,5},{5,4},{6,7},{7,6},{8,9},{9,8},{10,11... | collective-permute-start | bytes 3145736 | tf_op jit(solution)/shard_map/ppermute | solution.py:54
  140.6 5.0 %collective-permute-done.42.refs_8_ = bf16[256,512]{1,0:T(8,128)(2,1)S(1)} collective-permute-done((bf16[256,512]{1,0:T(8,128)(2,1)S(1)}, bf16[256,512]{1,0:T(8,128)(2,1)S(1)}, u32[]{:S(2)}, u32[]{:S(2)}) %collective-permute-start.42) | collective-permute-done | bytes 262176 | tf_op jit(solution)/shard_map/ppermute | solution.py:652
  146.7 4.5 %collective-permute-done.48.refs_9_ = bf16[256,512]{1,0:T(8,128)(2,1)S(1)} collective-permute-done((bf16[256,512]{1,0:T(8,128)(2,1)S(1)}, bf16[256,512]{1,0:T(8,128)(2,1)S(1)}, u32[]{:S(2)}, u32[]{:S(2)}) %collective-permute-start.48) | collective-permute-done | bytes 262176 | tf_op jit(solution)/shard_map/ppermute | solution.py:652
  151.8 3.8 %collective-permute-done.46.refs_12_ = bf16[256,512]{1,0:T(8,128)(2,1)S(1)} collective-permute-done((bf16[256,512]{1,0:T(8,128)(2,1)S(1)}, bf16[256,512]{1,0:T(8,128)(2,1)S(1)}, u32[]{:S(2)}, u32[]{:S(2)}) %collective-permute-start.46) | collective-permute-done | bytes 262176 | tf_op jit(solution)/shard_map/ppermute | solution.py:652
  157.9 2.9 %collective-permute-done.51.refs_13_ = bf16[256,512]{1,0:T(8,128)(2,1)S(1)} collective-permute-done((bf16[256,512]{1,0:T(8,128)(2,1)S(1)}, bf16[256,512]{1,0:T(8,128)(2,1)S(1)}, u32[]{:S(2)}, u32[]{:S(2)}) %collective-permute-start.51) | collective-permute-done | bytes 262176 | tf_op jit(solution)/shard_map/ppermute | solution.py:652
  162.4 4.1 %out_step.1.refs_4_ = f32[2,512,256]{2,1,0:T(8,128)S(1)} custom-call(s32[16]{0:T(128)S(1)} %concatenate.68.meta, bf16[256,512]{1,0:T(8,128)(2,1)S(1)} %get-tuple-element.189.refs_0_, bf16[256,512]{1,0:T(8,128)(2,1)S(1)} %get-tuple-element.191.refs_1_, bf16[256,512]{1,0:T(8,128)(2,1)S(1)} %collective-permute-done.41.refs_2_, ...), custom_call_target="tpu_custom_call" | custom-call | flops 1879048192 | bytes 9437184 | tf_op jit(solution)/shard_map/out_step/pallas_call | solution.py:433
  169.4 7.2 %collective-permute-start.57 = (bf16[8,256,256]{2,1,0:T(8,128)(2,1)S(1)}, bf16[8,256,256]{2,1,0:T(8,128)(2,1)S(1)}, u32[]{:S(2)}, u32[]{:S(2)}) collective-permute-start(bf16[8,256,256]{2,1,0:T(8,128)(2,1)S(1)} %collective-permute-done.55.refs_16_.refs_20_.refs_24_.refs_28_.refs_32_.refs_36_.refs_40_.refs_4_), channel_id=1, source_target_pairs={{0,1},{1,0},{2,3},{3,2},{4,5},{5,4},{6,7},{7,6},{8,9},{9,8},{10,11... | collective-permute-start | bytes 3145736 | tf_op jit(solution)/shard_map/ppermute | solution.py:54
  184.3 3.1 %collective-permute-done.58.refs_1_ = bf16[256,256]{1,0:T(8,128)(2,1)S(1)} collective-permute-done((bf16[256,256]{1,0:T(8,128)(2,1)S(1)}, bf16[256,256]{1,0:T(8,128)(2,1)S(1)}, u32[]{:S(2)}, u32[]{:S(2)}) %collective-permute-start.58) | collective-permute-done | bytes 131104 | tf_op jit(solution)/shard_map/ppermute | solution.py:812
  187.3 3.1 %collective-permute-done.60.refs_3_ = bf16[256,256]{1,0:T(8,128)(2,1)S(1)} collective-permute-done((bf16[256,256]{1,0:T(8,128)(2,1)S(1)}, bf16[256,256]{1,0:T(8,128)(2,1)S(1)}, u32[]{:S(2)}, u32[]{:S(2)}) %collective-permute-start.60) | collective-permute-done | bytes 131104 | tf_op jit(solution)/shard_map/ppermute | solution.py:812
  192.2 5.2 %collective-permute-done.61.refs_4_ = bf16[128,512]{1,0:T(8,128)(2,1)} collective-permute-done((bf16[128,512]{1,0:T(8,128)(2,1)S(1)}, bf16[128,512]{1,0:T(8,128)(2,1)}, u32[]{:S(2)}, u32[]{:S(2)}) %collective-permute-start.61) | collective-permute-done | bytes 131104 | tf_op jit(solution)/shard_map/ppermute | solution.py:652
  197.4 2.8 %collective-permute-done.65.refs_5_ = bf16[128,512]{1,0:T(8,128)(2,1)} collective-permute-done((bf16[128,512]{1,0:T(8,128)(2,1)S(1)}, bf16[128,512]{1,0:T(8,128)(2,1)}, u32[]{:S(2)}, u32[]{:S(2)}) %collective-permute-start.65) | collective-permute-done | bytes 131104 | tf_op jit(solution)/shard_map/ppermute | solution.py:652
  201.8 7.3 %collective-permute-done.63.refs_8_ = bf16[128,512]{1,0:T(8,128)(2,1)S(1)} collective-permute-done((bf16[128,512]{1,0:T(8,128)(2,1)}, bf16[128,512]{1,0:T(8,128)(2,1)S(1)}, u32[]{:S(2)}, u32[]{:S(2)}) %collective-permute-start.63) | collective-permute-done | bytes 131104 | tf_op jit(solution)/shard_map/ppermute | solution.py:652
  211.3 5.7 %collective-permute-done.67.refs_12_ = bf16[128,512]{1,0:T(8,128)(2,1)S(1)} collective-permute-done((bf16[128,512]{1,0:T(8,128)(2,1)S(1)}, bf16[128,512]{1,0:T(8,128)(2,1)S(1)}, u32[]{:S(2)}, u32[]{:S(2)}) %collective-permute-start.67) | collective-permute-done | bytes 131104 | tf_op jit(solution)/shard_map/ppermute | solution.py:652
  221.2 2.7 %collective-permute-done.74.refs_1_ = bf16[128,512]{1,0:T(8,128)(2,1)S(1)} collective-permute-done((bf16[128,512]{1,0:T(8,128)(2,1)S(1)}, bf16[128,512]{1,0:T(8,128)(2,1)S(1)}, u32[]{:S(2)}, u32[]{:S(2)}) %collective-permute-start.74) | collective-permute-done | bytes 131104 | tf_op jit(solution)/shard_map/ppermute | solution.py:652
  230.2 5.8 %collective-permute-start.79 = (f32[64,128]{1,0:T(8,128)S(1)}, f32[64,128]{1,0:T(8,128)S(1)}, u32[]{:S(2)}, u32[]{:S(2)}) collective-permute-start(f32[64,128]{1,0:T(8,128)S(1)} %fusion.25.own_a), channel_id=1, source_target_pairs={{0,1},{1,0},{2,3},{3,2},{4,5},{5,4},{6,7},{7,6},{8,9},{9,8},{10,11... | collective-permute-start | bytes 98312 | tf_op jit(solution)/shard_map/ppermute | solution.py:876
  (243 shorter events, 90.6 us)
Async XLA Ops:
  1.2 19.6 %collective-permute-start.8 = (bf16[4096,256]{1,0:T(8,128)(2,1)}, bf16[4096,256]{1,0:T(8,128)(2,1)}, u32[]{:S(2)}, u32[]{:S(2)}) collective-permute-start(bf16[4096,256]{1,0:T(8,128)(2,1)} %refs_13_.1), channel_id=1, source_target_pairs={{0,1},{1,0},{2,3},{3,2},{4,5},{5,4},{6,7},{7,6},{8,9},{9,8},{10,11... | collective-permute-start | bytes 6291464 | tf_op jit(solution)/shard_map/ppermute | solution.py:54
  18.6 14.6 %collective-permute-start.9 = (bf16[4,256,256]{2,1,0:T(8,128)(2,1)}, bf16[4,256,256]{2,1,0:T(8,128)(2,1)S(1)}, u32[]{:S(2)}, u32[]{:S(2)}) collective-permute-start(bf16[4,256,256]{2,1,0:T(8,128)(2,1)} %get-tuple-element.135), channel_id=1, source_target_pairs={{0,2},{2,0},{1,3},{3,1},{4,6},{6,4},{5,7},{7,5},{8,10},{10,8},{9,1... | collective-permute-start | bytes 1572872 | tf_op jit(solution)/shard_map/ppermute | solution.py:652
  19.3 63.3 %collective-permute-start.26 = (bf16[4096,256]{1,0:T(8,128)(2,1)S(1)}, bf16[4096,256]{1,0:T(8,128)(2,1)}, u32[]{:S(2)}, u32[]{:S(2)}) collective-permute-start(bf16[4096,256]{1,0:T(8,128)(2,1)S(1)} %copy-done.1), channel_id=1, source_target_pairs={{0,1},{1,0},{2,3},{3,2},{4,5},{5,4},{6,7},{7,6},{8,9},{9,8},{10,11... | collective-permute-start | bytes 6291464 | tf_op jit(solution)/shard_map/ppermute | solution.py:54
  36.2 9.7 %collective-permute-start.12 = (bf16[272,512]{1,0:T(8,128)(2,1)S(1)}, bf16[272,512]{1,0:T(8,128)(2,1)S(1)}, u32[]{:S(2)}, u32[]{:S(2)}) collective-permute-start(bf16[272,512]{1,0:T(8,128)(2,1)S(1)} %maximum_select_fusion.1.refs_0_), channel_id=1, source_target_pairs={{0,4},{4,8},{8,12},{12,0},{1,5},{5,9},{9,13},{13,1},{2,6},{6,10},{... | collective-permute-start | bytes 835592 | tf_op jit(solution)/shard_map/ppermute | solution.py:652
  38.6 13.0 %collective-permute-start.16 = (bf16[256,512]{1,0:T(8,128)(2,1)S(1)}, bf16[256,512]{1,0:T(8,128)(2,1)S(1)}, u32[]{:S(2)}, u32[]{:S(2)}) collective-permute-start(bf16[256,512]{1,0:T(8,128)(2,1)S(1)} %maximum_select_fusion.2.refs_1_), channel_id=1, source_target_pairs={{0,4},{4,8},{8,12},{12,0},{1,5},{5,9},{9,13},{13,1},{2,6},{6,10},{... | collective-permute-start | bytes 786440 | tf_op jit(solution)/shard_map/ppermute | solution.py:652
  38.7 12.9 %collective-permute-start.17 = (bf16[256,512]{1,0:T(8,128)(2,1)S(1)}, bf16[256,512]{1,0:T(8,128)(2,1)S(1)}, u32[]{:S(2)}, u32[]{:S(2)}) collective-permute-start(bf16[256,512]{1,0:T(8,128)(2,1)S(1)} %maximum_select_fusion.2.refs_1_), channel_id=1, source_target_pairs={{0,2},{2,0},{1,3},{3,1},{4,6},{6,4},{5,7},{7,5},{8,10},{10,8},{9,1... | collective-permute-start | bytes 786440 | tf_op jit(solution)/shard_map/ppermute | solution.py:652
  46.0 11.6 %collective-permute-start.14 = (bf16[272,512]{1,0:T(8,128)(2,1)S(1)}, bf16[272,512]{1,0:T(8,128)(2,1)S(1)}, u32[]{:S(2)}, u32[]{:S(2)}) collective-permute-start(bf16[272,512]{1,0:T(8,128)(2,1)S(1)} %collective-permute-done.12.refs_4_), channel_id=1, source_target_pairs={{0,4},{4,8},{8,12},{12,0},{1,5},{5,9},{9,13},{13,1},{2,6},{6,10},{... | collective-permute-start | bytes 835592 | tf_op jit(solution)/shard_map/ppermute | solution.py:652
  46.0 11.6 %collective-permute-start.15 = (bf16[272,512]{1,0:T(8,128)(2,1)S(1)}, bf16[272,512]{1,0:T(8,128)(2,1)S(1)}, u32[]{:S(2)}, u32[]{:S(2)}) collective-permute-start(bf16[272,512]{1,0:T(8,128)(2,1)S(1)} %collective-permute-done.12.refs_4_), channel_id=1, source_target_pairs={{0,2},{2,0},{1,3},{3,1},{4,6},{6,4},{5,7},{7,5},{8,10},{10,8},{9,1... | collective-permute-start | bytes 835592 | tf_op jit(solution)/shard_map/ppermute | solution.py:652
  51.6 11.6 %collective-permute-start.20 = (bf16[256,512]{1,0:T(8,128)(2,1)S(1)}, bf16[256,512]{1,0:T(8,128)(2,1)S(1)}, u32[]{:S(2)}, u32[]{:S(2)}) collective-permute-start(bf16[256,512]{1,0:T(8,128)(2,1)S(1)} %collective-permute-done.16.refs_5_), channel_id=1, source_target_pairs={{0,4},{4,8},{8,12},{12,0},{1,5},{5,9},{9,13},{13,1},{2,6},{6,10},{... | collective-permute-start | bytes 786440 | tf_op jit(solution)/shard_map/ppermute | solution.py:652
  51.6 11.6 %collective-permute-start.21 = (bf16[256,512]{1,0:T(8,128)(2,1)S(1)}, bf16[256,512]{1,0:T(8,128)(2,1)S(1)}, u32[]{:S(2)}, u32[]{:S(2)}) collective-permute-start(bf16[256,512]{1,0:T(8,128)(2,1)S(1)} %collective-permute-done.16.refs_5_), channel_id=1, source_target_pairs={{0,2},{2,0},{1,3},{3,1},{4,6},{6,4},{5,7},{7,5},{8,10},{10,8},{9,1... | collective-permute-start | bytes 786440 | tf_op jit(solution)/shard_map/ppermute | solution.py:652
  57.6 11.6 %collective-permute-start.18 = (bf16[272,512]{1,0:T(8,128)(2,1)S(1)}, bf16[272,512]{1,0:T(8,128)(2,1)S(1)}, u32[]{:S(2)}, u32[]{:S(2)}) collective-permute-start(bf16[272,512]{1,0:T(8,128)(2,1)S(1)} %collective-permute-done.14.refs_8_), channel_id=1, source_target_pairs={{0,4},{4,8},{8,12},{12,0},{1,5},{5,9},{9,13},{13,1},{2,6},{6,10},{... | collective-permute-start | bytes 835592 | tf_op jit(solution)/shard_map/ppermute | solution.py:652
  57.6 11.6 %collective-permute-start.19 = (bf16[272,512]{1,0:T(8,128)(2,1)S(1)}, bf16[272,512]{1,0:T(8,128)(2,1)S(1)}, u32[]{:S(2)}, u32[]{:S(2)}) collective-permute-start(bf16[272,512]{1,0:T(8,128)(2,1)S(1)} %collective-permute-done.14.refs_8_), channel_id=1, source_target_pairs={{0,2},{2,0},{1,3},{3,1},{4,6},{6,4},{5,7},{7,5},{8,10},{10,8},{9,1... | collective-permute-start | bytes 835592 | tf_op jit(solution)/shard_map/ppermute | solution.py:652
  63.2 11.6 %collective-permute-start.23 = (bf16[256,512]{1,0:T(8,128)(2,1)S(1)}, bf16[256,512]{1,0:T(8,128)(2,1)S(1)}, u32[]{:S(2)}, u32[]{:S(2)}) collective-permute-start(bf16[256,512]{1,0:T(8,128)(2,1)S(1)} %collective-permute-done.20.refs_9_), channel_id=1, source_target_pairs={{0,4},{4,8},{8,12},{12,0},{1,5},{5,9},{9,13},{13,1},{2,6},{6,10},{... | collective-permute-start | bytes 786440 | tf_op jit(solution)/shard_map/ppermute | solution.py:652
  63.2 11.6 %collective-permute-start.24 = (bf16[256,512]{1,0:T(8,128)(2,1)S(1)}, bf16[256,512]{1,0:T(8,128)(2,1)S(1)}, u32[]{:S(2)}, u32[]{:S(2)}) collective-permute-start(bf16[256,512]{1,0:T(8,128)(2,1)S(1)} %collective-permute-done.20.refs_9_), channel_id=1, source_target_pairs={{0,2},{2,0},{1,3},{3,1},{4,6},{6,4},{5,7},{7,5},{8,10},{10,8},{9,1... | collective-permute-start | bytes 786440 | tf_op jit(solution)/shard_map/ppermute | solution.py:652
  69.2 13.8 %collective-permute-start.22 = (bf16[272,512]{1,0:T(8,128)(2,1)S(1)}, bf16[272,512]{1,0:T(8,128)(2,1)S(1)}, u32[]{:S(2)}, u32[]{:S(2)}) collective-permute-start(bf16[272,512]{1,0:T(8,128)(2,1)S(1)} %collective-permute-done.18.refs_12_), channel_id=1, source_target_pairs={{0,2},{2,0},{1,3},{3,1},{4,6},{6,4},{5,7},{7,5},{8,10},{10,8},{9,1... | collective-permute-start | bytes 835592 | tf_op jit(solution)/shard_map/ppermute | solution.py:652
  90.9 13.7 %collective-permute-start.30 = (bf16[2,512,128]{2,1,0:T(8,128)(2,1)}, bf16[2,512,128]{2,1,0:T(8,128)(2,1)S(1)}, u32[]{:S(2)}, u32[]{:S(2)}) collective-permute-start(bf16[2,512,128]{2,1,0:T(8,128)(2,1)} %get-tuple-element.169), channel_id=1, source_target_pairs={{0,17},{1,16},{16,1},{17,0},{2,19},{3,18},{18,3},{19,2},{4,21},{5,... | collective-permute-start | bytes 786440 | tf_op jit(solution)/shard_map/ppermute | solution.py:812
  91.7 19.1 %collective-permute-start.32 = (bf16[2,512,128]{2,1,0:T(8,128)(2,1)}, bf16[2,512,128]{2,1,0:T(8,128)(2,1)S(1)}, u32[]{:S(2)}, u32[]{:S(2)}) collective-permute-start(bf16[2,512,128]{2,1,0:T(8,128)(2,1)} %get-tuple-element.179), channel_id=1, source_target_pairs={{0,1},{1,0},{2,3},{3,2},{4,5},{5,4},{6,7},{7,6},{8,9},{9,8},{10,11... | collective-permute-start | bytes 786440 | tf_op jit(solution)/shard_map/ppermute | solution.py:54
  91.7 20.1 %collective-permute-start.33 = (bf16[2,512,128]{2,1,0:T(8,128)(2,1)}, bf16[2,512,128]{2,1,0:T(8,128)(2,1)S(1)}, u32[]{:S(2)}, u32[]{:S(2)}) collective-permute-start(bf16[2,512,128]{2,1,0:T(8,128)(2,1)} %get-tuple-element.180.refs_2_), channel_id=1, source_target_pairs={{0,16},{1,17},{16,0},{17,1},{2,18},{3,19},{18,2},{19,3},{4,20},{5,... | collective-permute-start | bytes 786440 | tf_op jit(solution)/shard_map/ppermute | solution.py:812
  93.2 21.9 %collective-permute-start.34 = (bf16[2,512,128]{2,1,0:T(8,128)(2,1)S(1)}, bf16[2,512,128]{2,1,0:T(8,128)(2,1)S(1)}, u32[]{:S(2)}, u32[]{:S(2)}) collective-permute-start(bf16[2,512,128]{2,1,0:T(8,128)(2,1)S(1)} %copy-done.26), channel_id=1, source_target_pairs={{0,17},{1,16},{16,1},{17,0},{2,19},{3,18},{18,3},{19,2},{4,21},{5,... | collective-permute-start | bytes 786440 | tf_op jit(solution)/shard_map/ppermute | solution.py:812
  97.5 23.8 %collective-permute-start.39 = (bf16[2,256,256]{2,1,0:T(8,128)(2,1)S(1)}, bf16[2,256,256]{2,1,0:T(8,128)(2,1)S(1)}, u32[]{:S(2)}, u32[]{:S(2)}) collective-permute-start(bf16[2,256,256]{2,1,0:T(8,128)(2,1)S(1)} %pad_maximum_fusion.4), channel_id=1, source_target_pairs={{0,12},{4,0},{8,4},{12,8},{1,13},{5,1},{9,5},{13,9},{2,14},{6,2},{... | collective-permute-start | bytes 786440 | tf_op jit(solution)/shard_map/ppermute | solution.py:652
  104.7 20.4 %collective-permute-start.38 = (bf16[2,256,256]{2,1,0:T(8,128)(2,1)S(1)}, bf16[2,256,256]{2,1,0:T(8,128)(2,1)S(1)}, u32[]{:S(2)}, u32[]{:S(2)}) collective-permute-start(bf16[2,256,256]{2,1,0:T(8,128)(2,1)S(1)} %pad_maximum_fusion.3), channel_id=1, source_target_pairs={{0,8},{4,12},{8,0},{12,4},{1,9},{5,13},{9,1},{13,5},{2,10},{6,14},... | collective-permute-start | bytes 786440 | tf_op jit(solution)/shard_map/ppermute | solution.py:652
  110.8 14.3 %collective-permute-start.37 = (bf16[2,256,256]{2,1,0:T(8,128)(2,1)S(1)}, bf16[2,256,256]{2,1,0:T(8,128)(2,1)S(1)}, u32[]{:S(2)}, u32[]{:S(2)}) collective-permute-start(bf16[2,256,256]{2,1,0:T(8,128)(2,1)S(1)} %pad_maximum_fusion.2), channel_id=1, source_target_pairs={{0,4},{4,8},{8,12},{12,0},{1,5},{5,9},{9,13},{13,1},{2,6},{6,10},{... | collective-permute-start | bytes 786440 | tf_op jit(solution)/shard_map/ppermute | solution.py:652
  126.2 13.8 %collective-permute-start.44 = (bf16[256,512]{1,0:T(8,128)(2,1)S(1)}, bf16[256,512]{1,0:T(8,128)(2,1)S(1)}, u32[]{:S(2)}, u32[]{:S(2)}) collective-permute-start(bf16[256,512]{1,0:T(8,128)(2,1)S(1)} %get-tuple-element.191.refs_1_), channel_id=1, source_target_pairs={{0,4},{4,8},{8,12},{12,0},{1,5},{5,9},{9,13},{13,1},{2,6},{6,10},{... | collective-permute-start | bytes 786440 | tf_op jit(solution)/shard_map/ppermute | solution.py:652
  127.8 12.8 %collective-permute-start.45 = (bf16[256,512]{1,0:T(8,128)(2,1)S(1)}, bf16[256,512]{1,0:T(8,128)(2,1)S(1)}, u32[]{:S(2)}, u32[]{:S(2)}) collective-permute-start(bf16[256,512]{1,0:T(8,128)(2,1)S(1)} %get-tuple-element.191.refs_1_), channel_id=1, source_target_pairs={{0,2},{2,0},{1,3},{3,1},{4,6},{6,4},{5,7},{7,5},{8,10},{10,8},{9,1... | collective-permute-start | bytes 786440 | tf_op jit(solution)/shard_map/ppermute | solution.py:652
  134.4 11.2 %collective-permute-start.42 = (bf16[256,512]{1,0:T(8,128)(2,1)S(1)}, bf16[256,512]{1,0:T(8,128)(2,1)S(1)}, u32[]{:S(2)}, u32[]{:S(2)}) collective-permute-start(bf16[256,512]{1,0:T(8,128)(2,1)S(1)} %collective-permute-done.40.refs_4_), channel_id=1, source_target_pairs={{0,4},{4,8},{8,12},{12,0},{1,5},{5,9},{9,13},{13,1},{2,6},{6,10},{... | collective-permute-start | bytes 786440 | tf_op jit(solution)/shard_map/ppermute | solution.py:652
  134.4 12.3 %collective-permute-start.43 = (bf16[256,512]{1,0:T(8,128)(2,1)S(1)}, bf16[256,512]{1,0:T(8,128)(2,1)S(1)}, u32[]{:S(2)}, u32[]{:S(2)}) collective-permute-start(bf16[256,512]{1,0:T(8,128)(2,1)S(1)} %collective-permute-done.40.refs_4_), channel_id=1, source_target_pairs={{0,2},{2,0},{1,3},{3,1},{4,6},{6,4},{5,7},{7,5},{8,10},{10,8},{9,1... | collective-permute-start | bytes 786440 | tf_op jit(solution)/shard_map/ppermute | solution.py:652
  135.5 31.0 %collective-permute-start.54 = (bf16[8,256,256]{2,1,0:T(8,128)(2,1)S(1)}, bf16[8,256,256]{2,1,0:T(8,128)(2,1)S(1)}, u32[]{:S(2)}, u32[]{:S(2)}) collective-permute-start(bf16[8,256,256]{2,1,0:T(8,128)(2,1)S(1)} %constant_dynamic-update-slice_fusion.refs_14_.refs_18_.refs_22_.refs_26_.refs_30_.refs_34_.refs_38, ...), channel_id=1, source_target_pairs={{0,1},{1,0},{2,3},{3,2},{4,5},{5,4},{6,7},{7,6},{8,9},{9,8},{10,11... | collective-permute-start | bytes 3145736 | tf_op jit(solution)/shard_map/ppermute | solution.py:54
  140.0 27.5 %collective-permute-start.55 = (bf16[8,256,256]{2,1,0:T(8,128)(2,1)S(1)}, bf16[8,256,256]{2,1,0:T(8,128)(2,1)S(1)}, u32[]{:S(2)}, u32[]{:S(2)}) collective-permute-start(bf16[8,256,256]{2,1,0:T(8,128)(2,1)S(1)} %constant_dynamic-update-slice_fusion.refs_14_.refs_18_.refs_22_.refs_26_.refs_30_.refs_34_.refs_38, ...), channel_id=1, source_target_pairs={{0,16},{16,0},{1,17},{17,1},{2,18},{18,2},{3,19},{19,3},{4,20},{20... | collective-permute-start | bytes 3145736 | tf_op jit(solution)/shard_map/ppermute | solution.py:652
  140.6 10.6 %collective-permute-start.48 = (bf16[256,512]{1,0:T(8,128)(2,1)S(1)}, bf16[256,512]{1,0:T(8,128)(2,1)S(1)}, u32[]{:S(2)}, u32[]{:S(2)}) collective-permute-start(bf16[256,512]{1,0:T(8,128)(2,1)S(1)} %collective-permute-done.44.refs_5_), channel_id=1, source_target_pairs={{0,4},{4,8},{8,12},{12,0},{1,5},{5,9},{9,13},{13,1},{2,6},{6,10},{... | collective-permute-start | bytes 786440 | tf_op jit(solution)/shard_map/ppermute | solution.py:652
  157.5 11.9 %collective-permute-start.50 = (bf16[256,512]{1,0:T(8,128)(2,1)S(1)}, bf16[256,512]{1,0:T(8,128)(2,1)S(1)}, u32[]{:S(2)}, u32[]{:S(2)}) collective-permute-start(bf16[256,512]{1,0:T(8,128)(2,1)S(1)} %collective-permute-done.46.refs_12_), channel_id=1, source_target_pairs={{0,2},{2,0},{1,3},{3,1},{4,6},{6,4},{5,7},{7,5},{8,10},{10,8},{9,1... | collective-permute-start | bytes 786440 | tf_op jit(solution)/shard_map/ppermute | solution.py:652
  169.4 12.0 %collective-permute-start.57 = (bf16[8,256,256]{2,1,0:T(8,128)(2,1)S(1)}, bf16[8,256,256]{2,1,0:T(8,128)(2,1)S(1)}, u32[]{:S(2)}, u32[]{:S(2)}) collective-permute-start(bf16[8,256,256]{2,1,0:T(8,128)(2,1)S(1)} %collective-permute-done.55.refs_16_.refs_20_.refs_24_.refs_28_.refs_32_.refs_36_.refs_40_.refs_4_), channel_id=1, source_target_pairs={{0,1},{1,0},{2,3},{3,2},{4,5},{5,4},{6,7},{7,6},{8,9},{9,8},{10,11... | collective-permute-start | bytes 3145736 | tf_op jit(solution)/shard_map/ppermute | solution.py:54
  229.9 9.4 %collective-permute-start.78 = (f32[64,128]{1,0:T(8,128)S(1)}, f32[64,128]{1,0:T(8,128)S(1)}, u32[]{:S(2)}, u32[]{:S(2)}) collective-permute-start(f32[64,128]{1,0:T(8,128)S(1)} %fusion.25.own_a), channel_id=1, source_target_pairs={{0,2},{1,3},{2,0},{3,1},{4,6},{5,7},{6,4},{7,5},{8,10},{9,11},{10,... | collective-permute-start | bytes 98312 | tf_op jit(solution)/shard_map/ppermute | solution.py:876
  (77 other events, 1040.7 us)

commit v11 on v10

--- a/solution.py
+++ b/solution.py
@@ -57,6 +57,10 @@
 HELD = pl.BlockSpec(memory_space=pltpu.VMEM)
 
 
+def in_hbm(values):
+    return pltpu.with_memory_space_constraint(values, pltpu.HBM)
+
+
 GAIN_ROWS = 16
 TOP = 16
 
@@ -64,9 +68,9 @@
 def down_kernel(images, tiles, half, meta, *refs):
     lat_refs, refs = refs[:tiles], refs[tiles:]
     conv_ref, gain_ref, patch_hbm, text_hbm = refs[:4]
-    weight_refs, (first_ref, second_ref), held_refs = refs[4:10], refs[10:12], refs[12:18]
-    grid_rows, conv_wide, conv_bf16, windows, total, patch_ref, text_ref = refs[18:25]
-    arrived, patch_arrived, text_arrived = refs[25:]
+    weight_refs, first_refs, second_refs, held_refs = refs[4:10], refs[10:12], refs[12:14], refs[14:20]
+    grid_rows, conv_wide, conv_bf16, windows, total, patch_ref, text_ref = refs[20:27]
+    arrived, patch_arrived, text_arrived = refs[27:]
     step = pl.program_id(0)
     deep = PATCH * CH
     patch_copies = [
@@ -153,7 +157,7 @@
             copy.wait()
         for side in range(2):
             base = ctx * (2 * half) + jnp.bitwise_xor(core, side) * half
-            for part, out_ref in enumerate((first_ref, second_ref)):
+            for part, out_ref in enumerate((first_refs[side], second_refs[side])):
                 place = base + part * block + lax.broadcasted_iota(jnp.int32, (block, 1), 0)
                 source = jnp.full((block, 1), -1, jnp.int32)
                 for image in range(images):
@@ -164,9 +168,9 @@
                 choice = source == lax.broadcasted_iota(jnp.int32, (block, images * IMG_TOK), 1)
                 picked = mxu(jnp.where(choice, 1.0, 0.0).astype(BF16), tokens)
                 text = text_ref[side, part * block : (part + 1) * block, :].astype(F32)
-                out_ref[side, :block, :] = jnp.where(source >= 0, picked, text).astype(BF16)
+                out_ref[:block, :] = jnp.where(source >= 0, picked, text).astype(BF16)
             gain = gain_ref[...].astype(F32)
-            first_ref[side, block:, :] = jnp.broadcast_to(gain, (GAIN_ROWS, gain.shape[1])).astype(BF16)
+            first_refs[side][block:, :] = jnp.broadcast_to(gain, (GAIN_ROWS, gain.shape[1])).astype(BF16)
         for copy in copies:
             copy.wait()
 
@@ -176,7 +180,8 @@
     half = seq_rows // 2
     tiles = len(pieces)
     count = images * IMG_TOK
-    first, second = (2, half // 2 + GAIN_ROWS, width), (2, half // 2, width)
+    first, second = (half // 2 + GAIN_ROWS, width), (half // 2, width)
+    pieces_out = [first, first, second, second]
     return pl.pallas_call(
         functools.partial(down_kernel, images, tiles, half),
         grid_spec=pltpu.PrefetchScalarGridSpec(
@@ -188,7 +193,7 @@
                 full((1, width)),
             ]
             + [pl.BlockSpec(memory_space=pltpu.HBM)] * 8,
-            out_specs=[full(first), full(second)] + [HELD] * 6,
+            out_specs=[full(shape) for shape in pieces_out] + [HELD] * 6,
             scratch_shapes=[
                 pltpu.VMEM((images, WL * CIN // HD + 1, TOP + HL + 16, HD), F32),
                 pltpu.VMEM((TAPS, PATCH * CH), F32),
@@ -202,12 +207,12 @@
                 pltpu.SemaphoreType.DMA((2,)),
             ],
         ),
-        out_shape=[jax.ShapeDtypeStruct(first, BF16), jax.ShapeDtypeStruct(second, BF16)]
+        out_shape=[jax.ShapeDtypeStruct(shape, BF16) for shape in pieces_out]
         + [pltpu.VMEM(w.shape, w.dtype) for w in weights],
         compiler_params=params(32),
         cost_estimate=cost(2 * count * PIX * CH * (256 + width), 4 << 20, count * PIX * CH),
         name="down_stream",
-    )(meta, *pieces, conv, gain.reshape(1, width), patch_in, text, *weights)
+    )(meta, *pieces, conv, gain.reshape(1, width), in_hbm(patch_in), in_hbm(text), *[in_hbm(w) for w in weights])
 
 
 def full(shape):
@@ -393,14 +398,14 @@
     x_refs = take_blocks(refs, count)
     weight_refs = [[refs.pop(0), refs.pop(0)] for _ in range(count)]
     if first:
-        streams = [refs.pop(0), refs.pop(0)]
-        block = streams[1].shape[1]
+        streams = [refs.pop(0) for _ in range(4)]
+        block = streams[1].shape[0]
     else:
         acc_in = refs.pop(0)
     outs = refs
     for side in range(2):
         if first:
-            rows = [streams[0][side, :block, :], streams[1][side]]
+            rows = [streams[2 * side][:block, :], streams[2 * side + 1][...]]
             total = jnp.concatenate(rows, axis=0).astype(F32)
         else:
             total = acc_in[side]
@@ -702,7 +707,7 @@
         compiler_params=params(8),
         cost_estimate=cost(1 << 16, 2 << 20),
         name="columns",
-    )(meta, patch_out)
+    )(meta, in_hbm(patch_out))
     return kept, sent, halves
 
 
@@ -784,7 +789,7 @@
     received = shift(sent, "mpo", 1)
     weights += [key_weight, value_weight, query_weight]
     streams = down_stream(meta, pieces, conv, patch_in, text_embed, norm_gain, weights, images)
-    streams, held_weights = streams[:2], streams[2:]
+    streams, held_weights = [streams[:2], streams[2:4]], streams[4:]
     streams, received = lax.optimization_barrier((streams, received))
     others = [swap(s[1]) for s in streams]
     others = lax.optimization_barrier(others)
@@ -838,7 +843,7 @@
     def project_out(blocks, entries, state, last):
         return out_step(meta, layout, blocks, entries, (out_weight, out_par), state, last)
 
-    state = [jnp.stack([s[0], o]) for s, o in zip(streams, others)]
+    state = [streams[0][0], streams[1][0], others[0], others[1]]
     state, up_weights = gather_pair(*attended, state, project_out, extras)
     out_own, out_send = state
     out_other = swap(out_send)

time: 242 us -> 268 us (1.11)
  Pallas kernels: 42.7 us -> 76.4 us
  starting transfers between devices: 72 us -> 61.9 us
  waiting for transfers between devices: 110 us -> 118 us
  local copies, waits for them, and re-layouts: 9.5 us -> 5.68 us
    pallas_call x1, Pallas kernels: 1.56 us -> 33.5 us  [transpose_first(): pl.pallas_call(functools.partial(columns_kernel, layout, halves), grid_sp...]
    ppermute x55, starting transfers between devices: 42.5 us -> 34.5 us  [shift(): lax.ppermute(values, axis, [(i, (i + step) % count) for i in range(count)])]
    ppermute x55, waiting for transfers between devices: 86.9 us -> 93.8 us  [shift(): lax.ppermute(values, axis, [(i, (i + step) % count) for i in range(count)])]
    unnamed x60, local copies, waits for them, and re-layouts: 7.14 us -> 3.58 us
  transfers between devices with their start and end apart: 81 -> 81, of which waited for: 33 -> 35; matrix products, arithmetic and copies ran while one was open for 3% -> 3% of each run, Pallas kernels for 16% -> 27%
where the time goes in v11:
time: 268 us
  waiting for transfers between devices  118 us (44%)
  Pallas kernels  76.4 us (29%)
  starting transfers between devices  61.9 us (23%)
  local copies, waits for them, and re-layouts  5.68 us (2%)
  other arithmetic  4.52 us (2%)
    ppermute x55, waiting for transfers between devices, shift(): lax.ppermute(values, axis, [(i, (i + step) % count) for i in range(count)])  93.8 us
    ppermute x55, starting transfers between devices, shift(): lax.ppermute(values, axis, [(i, (i + step) % count) for i in range(count)])  34.5 us
    pallas_call x1, Pallas kernels, transpose_first(): pl.pallas_call(functools.partial(columns_kernel, layout, halves), grid_sp...  33.5 us
    ppermute x6, waiting for transfers between devices, shifted(): return lax.ppermute(values, ('ctx', 'core'), pairs)  17.2 us
    ppermute x17, starting transfers between devices, swap(): return lax.ppermute(values, 'core', [(0, 1), (1, 0)])  14.6 us
    pallas_call x1, Pallas kernels, down_stream(): pl.pallas_call(functools.partial(down_kernel, images, tiles, half), grid_...  11.7 us
    pallas_call x2, Pallas kernels, qkv_step(): pl.pallas_call(functools.partial(qkv_kernel, entries, layout, groups, las...  10.4 us
    pallas_call x2, Pallas kernels, attention(): pl.pallas_call(functools.partial(attention_kernel, images, len(pieces), h...  8.91 us
  transfers between devices with their start and end apart: 81, of which 35 were waited for; matrix products, arithmetic and copies ran while one was open for 3% of the time, Pallas kernels for 27%

profile of v11, /device:TPU:1, one launch (start us, length us, event | category | flops | bytes accessed | tf_op | source)
XLA Modules:
  0.0 268.1 jit_solution(11314420452059970506)
XLA Ops:
  1.3 2.7 collective-permute-start
  15.4 33.5 %columns.1 = (bf16[4,256,256]{2,1,0:T(8,128)(2,1)}, bf16[4,256,256]{2,1,0:T(8,128)(2,1)}) custom-call(s32[16]{0:T(128)S(1)} %concatenate.68.meta, bf16[256,4096]{1,0:T(8,128)(2,1)} %patch_ref.1), custom_call_target="tpu_custom_call" | custom-call | flops 65536 | bytes 2097152 | tf_op jit(solution)/shard_map/columns/pallas_call | solution.py:697
  51.2 11.7 %down_stream.1 = (bf16[272,256]{1,0:T(8,128)(2,1)S(1)}, bf16[272,256]{1,0:T(8,128)(2,1)S(1)}, bf16[256,256]{1,0:T(8,128)(2,1)S(1)}, bf16[256,256]{1,0:T(8,128)(2...) custom-call(s32[16]{0:T(128)S(1)} %concatenate.68.meta, ...), custom_call_target="tpu_custom_call" | custom-call | flops 4294967296 | bytes 4194304 | tf_op jit(solution)/shard_map/down_stream/pallas_call | solution.py:185
  67.4 7.6 %collective-permute-done.12.refs_4_ = bf16[272,512]{1,0:T(8,128)(2,1)S(1)} collective-permute-done((bf16[272,512]{1,0:T(8,128)(2,1)S(1)}, bf16[272,512]{1,0:T(8,128)(2,1)S(1)}, u32[]{:S(2)}, u32[]{:S(2)}) %collective-permute-start.12) | collective-permute-done | bytes 278560 | tf_op jit(solution)/shard_map/ppermute | solution.py:657
  75.6 5.0 %collective-permute-done.16.refs_5_ = bf16[256,512]{1,0:T(8,128)(2,1)S(1)} collective-permute-done((bf16[256,512]{1,0:T(8,128)(2,1)S(1)}, bf16[256,512]{1,0:T(8,128)(2,1)S(1)}, u32[]{:S(2)}, u32[]{:S(2)}) %collective-permute-start.16) | collective-permute-done | bytes 262176 | tf_op jit(solution)/shard_map/ppermute | solution.py:657
  81.2 5.4 %collective-permute-done.14.refs_8_ = bf16[272,512]{1,0:T(8,128)(2,1)S(1)} collective-permute-done((bf16[272,512]{1,0:T(8,128)(2,1)S(1)}, bf16[272,512]{1,0:T(8,128)(2,1)S(1)}, u32[]{:S(2)}, u32[]{:S(2)}) %collective-permute-start.14) | collective-permute-done | bytes 278560 | tf_op jit(solution)/shard_map/ppermute | solution.py:657
  87.2 5.0 %collective-permute-done.20.refs_9_ = bf16[256,512]{1,0:T(8,128)(2,1)S(1)} collective-permute-done((bf16[256,512]{1,0:T(8,128)(2,1)S(1)}, bf16[256,512]{1,0:T(8,128)(2,1)S(1)}, u32[]{:S(2)}, u32[]{:S(2)}) %collective-permute-start.20) | collective-permute-done | bytes 262176 | tf_op jit(solution)/shard_map/ppermute | solution.py:657
  92.8 5.4 %collective-permute-done.18.refs_12_ = bf16[272,512]{1,0:T(8,128)(2,1)S(1)} collective-permute-done((bf16[272,512]{1,0:T(8,128)(2,1)S(1)}, bf16[272,512]{1,0:T(8,128)(2,1)S(1)}, u32[]{:S(2)}, u32[]{:S(2)}) %collective-permute-start.18) | collective-permute-done | bytes 278560 | tf_op jit(solution)/shard_map/ppermute | solution.py:657
  98.7 5.0 %collective-permute-done.23.refs_13_ = bf16[256,512]{1,0:T(8,128)(2,1)S(1)} collective-permute-done((bf16[256,512]{1,0:T(8,128)(2,1)S(1)}, bf16[256,512]{1,0:T(8,128)(2,1)S(1)}, u32[]{:S(2)}, u32[]{:S(2)}) %collective-permute-start.23) | collective-permute-done | bytes 262176 | tf_op jit(solution)/shard_map/ppermute | solution.py:657
  103.8 7.7 %qkv_step.1 = (bf16[6,512,256]{2,1,0:T(8,128)(2,1)S(1)}, f32[6,512,256]{2,1,0:T(8,128)S(1)}, f32[512,128]{1,0:T(8,128)S(1)}) custom-call(s32[16]{0:T(128)S(1)} %concatenate.68.meta, bf16[272,512]{1,0:T(8,128)(2,1)S(1)} %maximum_select_fusion.1.refs_0_, bf16[256,512]{1,0:T(8,128)(2,1)S(1)} %maximum_select_fusion.2.refs_1_, ...), custom_call_target="tpu_custom_call" | custom-call | flops 5637144576 | bytes 20971520 | tf_op jit(solution)/shard_map/qkv_step/pallas_call | solution.py:321
  112.4 2.7 %qkv_last.1 = (bf16[2,512,128]{2,1,0:T(8,128)(2,1)}, bf16[2,512,128]{2,1,0:T(8,128)(2,1)}, bf16[512,128]{1,0:T(8,128)(2,1)}, bf16[512,128]{1,0:T(8,128)(2,1)}, b...) custom-call(s32[16]{0:T(128)S(1)} %concatenate.68.meta, ...), custom_call_target="tpu_custom_call" | custom-call | flops 805306368 | bytes 8388608 | tf_op jit(solution)/shard_map/qkv_last/pallas_call | solution.py:321
  129.0 5.4 %collective-permute-done.30.refs_5_ = bf16[2,512,128]{2,1,0:T(8,128)(2,1)S(1)} collective-permute-done((bf16[2,512,128]{2,1,0:T(8,128)(2,1)}, bf16[2,512,128]{2,1,0:T(8,128)(2,1)S(1)}, u32[]{:S(2)}, u32[]{:S(2)}) %collective-permute-start.30) | collective-permute-done | bytes 262176 | tf_op jit(solution)/shard_map/ppermute | solution.py:817
  135.6 4.5 %attention.2 = (bf16[512,128]{1,0:T(8,128)(2,1)S(1)}, bf16[512,128]{1,0:T(8,128)(2,1)S(1)}) custom-call(s32[16]{0:T(128)S(1)} %concatenate.68.meta, bf16[512,128]{1,0:T(8,128)(2,1)S(1)} %copy-done.19, bf16[512,128]{1,0:T(8,128)(2,1)S(1)} %copy-done.21, bf16[2,512,128]{2,1,0:T(8,128)(2,1)S(1)} %copy-done.15, ...), custom_call_target="tpu_custom_call" | custom-call | flops 1073741824 | bytes 1048576 | tf_op jit(solution)/shard_map/attention/pallas_call | solution.py:381
  141.4 3.5 %collective-permute-done.34.refs_5_ = bf16[2,512,128]{2,1,0:T(8,128)(2,1)S(1)} collective-permute-done((bf16[2,512,128]{2,1,0:T(8,128)(2,1)S(1)}, bf16[2,512,128]{2,1,0:T(8,128)(2,1)S(1)}, u32[]{:S(2)}, u32[]{:S(2)}) %collective-permute-start.34) | collective-permute-done | bytes 262176 | tf_op jit(solution)/shard_map/ppermute | solution.py:817
  144.9 4.5 %attention.3 = (bf16[512,128]{1,0:T(8,128)(2,1)S(1)}, bf16[512,128]{1,0:T(8,128)(2,1)S(1)}) custom-call(s32[16]{0:T(128)S(1)} %concatenate.68.meta, bf16[512,128]{1,0:T(8,128)(2,1)S(1)} %copy-done.16, bf16[512,128]{1,0:T(8,128)(2,1)S(1)} %copy-done.18, bf16[2,512,128]{2,1,0:T(8,128)(2,1)S(1)} %copy-done.14, ...), custom_call_target="tpu_custom_call" | custom-call | flops 1073741824 | bytes 1048576 | tf_op jit(solution)/shard_map/attention/pallas_call | solution.py:381
  151.0 3.6 %collective-permute-done.38 = bf16[2,256,256]{2,1,0:T(8,128)(2,1)S(1)} collective-permute-done((bf16[2,256,256]{2,1,0:T(8,128)(2,1)S(1)}, bf16[2,256,256]{2,1,0:T(8,128)(2,1)S(1)}, u32[]{:S(2)}, u32[]{:S(2)}) %collective-permute-start.38) | collective-permute-done | bytes 262176 | tf_op jit(solution)/shard_map/ppermute | solution.py:657
  157.6 6.2 %collective-permute-done.40.refs_4_ = bf16[256,512]{1,0:T(8,128)(2,1)S(1)} collective-permute-done((bf16[256,512]{1,0:T(8,128)(2,1)S(1)}, bf16[256,512]{1,0:T(8,128)(2,1)S(1)}, u32[]{:S(2)}, u32[]{:S(2)}) %collective-permute-start.40) | collective-permute-done | bytes 262176 | tf_op jit(solution)/shard_map/ppermute | solution.py:657
  164.5 2.8 %collective-permute-start.54 = (bf16[8,256,256]{2,1,0:T(8,128)(2,1)S(1)}, bf16[8,256,256]{2,1,0:T(8,128)(2,1)S(1)}, u32[]{:S(2)}, u32[]{:S(2)}) collective-permute-start(bf16[8,256,256]{2,1,0:T(8,128)(2,1)S(1)} %constant_dynamic-update-slice_fusion.refs_14_.refs_18_.refs_22_.refs_26_.refs_30_.refs_34_.refs_38, ...), channel_id=1, source_target_pairs={{0,1},{1,0},{2,3},{3,2},{4,5},{5,4},{6,7},{7,6},{8,9},{9,8},{10,11... | collective-permute-start | bytes 3145736 | tf_op jit(solution)/shard_map/ppermute | solution.py:54
  169.9 5.2 %collective-permute-done.42.refs_8_ = bf16[256,512]{1,0:T(8,128)(2,1)S(1)} collective-permute-done((bf16[256,512]{1,0:T(8,128)(2,1)S(1)}, bf16[256,512]{1,0:T(8,128)(2,1)S(1)}, u32[]{:S(2)}, u32[]{:S(2)}) %collective-permute-start.42) | collective-permute-done | bytes 262176 | tf_op jit(solution)/shard_map/ppermute | solution.py:657
  175.7 4.5 %collective-permute-done.48.refs_9_ = bf16[256,512]{1,0:T(8,128)(2,1)S(1)} collective-permute-done((bf16[256,512]{1,0:T(8,128)(2,1)S(1)}, bf16[256,512]{1,0:T(8,128)(2,1)S(1)}, u32[]{:S(2)}, u32[]{:S(2)}) %collective-permute-start.48) | collective-permute-done | bytes 262176 | tf_op jit(solution)/shard_map/ppermute | solution.py:657
  180.8 4.8 %collective-permute-done.46.refs_12_ = bf16[256,512]{1,0:T(8,128)(2,1)S(1)} collective-permute-done((bf16[256,512]{1,0:T(8,128)(2,1)S(1)}, bf16[256,512]{1,0:T(8,128)(2,1)S(1)}, u32[]{:S(2)}, u32[]{:S(2)}) %collective-permute-start.46) | collective-permute-done | bytes 262176 | tf_op jit(solution)/shard_map/ppermute | solution.py:657
  186.2 4.4 %collective-permute-done.51.refs_13_ = bf16[256,512]{1,0:T(8,128)(2,1)S(1)} collective-permute-done((bf16[256,512]{1,0:T(8,128)(2,1)S(1)}, bf16[256,512]{1,0:T(8,128)(2,1)S(1)}, u32[]{:S(2)}, u32[]{:S(2)}) %collective-permute-start.51) | collective-permute-done | bytes 262176 | tf_op jit(solution)/shard_map/ppermute | solution.py:657
  192.5 4.0 %out_step.1.refs_4_ = f32[2,512,256]{2,1,0:T(8,128)S(1)} custom-call(s32[16]{0:T(128)S(1)} %concatenate.68.meta, bf16[256,512]{1,0:T(8,128)(2,1)S(1)} %get-tuple-element.197.refs_0_, bf16[256,512]{1,0:T(8,128)(2,1)S(1)} %get-tuple-element.199.refs_1_, bf16[256,512]{1,0:T(8,128)(2,1)S(1)} %collective-permute-done.41.refs_2_, ...), custom_call_target="tpu_custom_call" | custom-call | flops 1879048192 | bytes 9437184 | tf_op jit(solution)/shard_map/out_step/pallas_call | solution.py:438
  199.0 5.0 %collective-permute-start.57 = (bf16[8,256,256]{2,1,0:T(8,128)(2,1)S(1)}, bf16[8,256,256]{2,1,0:T(8,128)(2,1)S(1)}, u32[]{:S(2)}, u32[]{:S(2)}) collective-permute-start(bf16[8,256,256]{2,1,0:T(8,128)(2,1)S(1)} %collective-permute-done.55.refs_16_.refs_20_.refs_24_.refs_28_.refs_32_.refs_36_.refs_40_.refs_4_), channel_id=1, source_target_pairs={{0,1},{1,0},{2,3},{3,2},{4,5},{5,4},{6,7},{7,6},{8,9},{9,8},{10,11... | collective-permute-start | bytes 3145736 | tf_op jit(solution)/shard_map/ppermute | solution.py:54
  211.7 3.1 %collective-permute-done.58.refs_1_ = bf16[256,256]{1,0:T(8,128)(2,1)S(1)} collective-permute-done((bf16[256,256]{1,0:T(8,128)(2,1)S(1)}, bf16[256,256]{1,0:T(8,128)(2,1)S(1)}, u32[]{:S(2)}, u32[]{:S(2)}) %collective-permute-start.58) | collective-permute-done | bytes 131104 | tf_op jit(solution)/shard_map/ppermute | solution.py:817
  214.8 3.1 %collective-permute-done.60.refs_3_ = bf16[256,256]{1,0:T(8,128)(2,1)S(1)} collective-permute-done((bf16[256,256]{1,0:T(8,128)(2,1)S(1)}, bf16[256,256]{1,0:T(8,128)(2,1)S(1)}, u32[]{:S(2)}, u32[]{:S(2)}) %collective-permute-start.60) | collective-permute-done | bytes 131104 | tf_op jit(solution)/shard_map/ppermute | solution.py:817
  219.5 5.3 %collective-permute-done.61.refs_4_ = bf16[128,512]{1,0:T(8,128)(2,1)} collective-permute-done((bf16[128,512]{1,0:T(8,128)(2,1)S(1)}, bf16[128,512]{1,0:T(8,128)(2,1)}, u32[]{:S(2)}, u32[]{:S(2)}) %collective-permute-start.61) | collective-permute-done | bytes 131104 | tf_op jit(solution)/shard_map/ppermute | solution.py:657
  224.8 2.8 %collective-permute-done.65.refs_5_ = bf16[128,512]{1,0:T(8,128)(2,1)} collective-permute-done((bf16[128,512]{1,0:T(8,128)(2,1)S(1)}, bf16[128,512]{1,0:T(8,128)(2,1)}, u32[]{:S(2)}, u32[]{:S(2)}) %collective-permute-start.65) | collective-permute-done | bytes 131104 | tf_op jit(solution)/shard_map/ppermute | solution.py:657
  229.2 7.3 %collective-permute-done.63.refs_8_ = bf16[128,512]{1,0:T(8,128)(2,1)S(1)} collective-permute-done((bf16[128,512]{1,0:T(8,128)(2,1)}, bf16[128,512]{1,0:T(8,128)(2,1)S(1)}, u32[]{:S(2)}, u32[]{:S(2)}) %collective-permute-start.63) | collective-permute-done | bytes 131104 | tf_op jit(solution)/shard_map/ppermute | solution.py:657
  238.3 6.0 %collective-permute-done.67.refs_12_ = bf16[128,512]{1,0:T(8,128)(2,1)S(1)} collective-permute-done((bf16[128,512]{1,0:T(8,128)(2,1)S(1)}, bf16[128,512]{1,0:T(8,128)(2,1)S(1)}, u32[]{:S(2)}, u32[]{:S(2)}) %collective-permute-start.67) | collective-permute-done | bytes 131104 | tf_op jit(solution)/shard_map/ppermute | solution.py:657
  248.0 2.7 collective-permute-done.74.refs_1_
  257.5 5.9 %collective-permute-start.79 = (f32[64,128]{1,0:T(8,128)S(1)}, f32[64,128]{1,0:T(8,128)S(1)}, u32[]{:S(2)}, u32[]{:S(2)}) collective-permute-start(f32[64,128]{1,0:T(8,128)S(1)} %fusion.25.own_a), channel_id=1, source_target_pairs={{0,1},{1,0},{2,3},{3,2},{4,5},{5,4},{6,7},{7,6},{8,9},{9,8},{10,11... | collective-permute-start | bytes 98312 | tf_op jit(solution)/shard_map/ppermute | solution.py:881
  (239 shorter events, 80.9 us)
Async XLA Ops:
  1.2 49.9 %collective-permute-start.8 = (bf16[4096,256]{1,0:T(8,128)(2,1)}, bf16[4096,256]{1,0:T(8,128)(2,1)}, u32[]{:S(2)}, u32[]{:S(2)}) collective-permute-start(bf16[4096,256]{1,0:T(8,128)(2,1)} %refs_13_.1), channel_id=1, source_target_pairs={{0,1},{1,0},{2,3},{3,2},{4,5},{5,4},{6,7},{7,6},{8,9},{9,8},{10,11... | collective-permute-start | bytes 6291464 | tf_op jit(solution)/shard_map/ppermute | solution.py:54
  10.7 38.2 %collective-permute-start.4 = (bf16[4,16,512]{2,1,0:T(8,128)(2,1)S(1)}, bf16[4,16,512]{2,1,0:T(8,128)(2,1)S(1)}, u32[]{:S(2)}, u32[]{:S(2)}) collective-permute-start(bf16[4,16,512]{2,1,0:T(8,128)(2,1)S(1)} %pad_maximum_fusion.4.refs_0_), channel_id=1, source_target_pairs={{0,8},{4,12},{8,0},{12,4},{1,9},{5,13},{9,1},{13,5},{2,10},{6,14},... | collective-permute-start | bytes 196616 | tf_op jit(solution)/shard_map/ppermute | solution.py:657
  13.0 35.9 %collective-permute-start.5 = (bf16[4,16,512]{2,1,0:T(8,128)(2,1)S(1)}, bf16[4,16,512]{2,1,0:T(8,128)(2,1)S(1)}, u32[]{:S(2)}, u32[]{:S(2)}) collective-permute-start(bf16[4,16,512]{2,1,0:T(8,128)(2,1)S(1)} %pad_maximum_fusion.4.refs_0_), channel_id=1, source_target_pairs={{0,12},{4,0},{8,4},{12,8},{1,13},{5,1},{9,5},{13,9},{2,14},{6,2},{... | collective-permute-start | bytes 196616 | tf_op jit(solution)/shard_map/ppermute | solution.py:657
  14.2 37.0 %collective-permute-start.7 = (bf16[72,128]{1,0:T(8,128)(2,1)S(1)}, bf16[72,128]{1,0:T(8,128)(2,1)S(1)}, u32[]{:S(2)}, u32[]{:S(2)}) collective-permute-start(bf16[72,128]{1,0:T(8,128)(2,1)S(1)} %maximum_select_fusion.6), channel_id=1, source_target_pairs={{0,2},{2,0},{1,3},{3,1},{4,6},{6,4},{5,7},{7,5},{8,10},{10,8},{9,1... | collective-permute-start | bytes 55304 | tf_op jit(solution)/shard_map/ppermute | solution.py:657
  49.0 13.9 %collective-permute-start.9 = (bf16[4,256,256]{2,1,0:T(8,128)(2,1)}, bf16[4,256,256]{2,1,0:T(8,128)(2,1)S(1)}, u32[]{:S(2)}, u32[]{:S(2)}) collective-permute-start(bf16[4,256,256]{2,1,0:T(8,128)(2,1)} %get-tuple-element.141), channel_id=1, source_target_pairs={{0,2},{2,0},{1,3},{3,1},{4,6},{6,4},{5,7},{7,5},{8,10},{10,8},{9,1... | collective-permute-start | bytes 1572872 | tf_op jit(solution)/shard_map/ppermute | solution.py:657
  49.3 62.2 %collective-permute-start.26 = (bf16[4096,256]{1,0:T(8,128)(2,1)S(1)}, bf16[4096,256]{1,0:T(8,128)(2,1)}, u32[]{:S(2)}, u32[]{:S(2)}) collective-permute-start(bf16[4096,256]{1,0:T(8,128)(2,1)S(1)} %copy-done.1), channel_id=1, source_target_pairs={{0,1},{1,0},{2,3},{3,2},{4,5},{5,4},{6,7},{7,6},{8,9},{9,8},{10,11... | collective-permute-start | bytes 6291464 | tf_op jit(solution)/shard_map/ppermute | solution.py:54
  65.1 9.9 %collective-permute-start.12 = (bf16[272,512]{1,0:T(8,128)(2,1)S(1)}, bf16[272,512]{1,0:T(8,128)(2,1)S(1)}, u32[]{:S(2)}, u32[]{:S(2)}) collective-permute-start(bf16[272,512]{1,0:T(8,128)(2,1)S(1)} %maximum_select_fusion.1.refs_0_), channel_id=1, source_target_pairs={{0,4},{4,8},{8,12},{12,0},{1,5},{5,9},{9,13},{13,1},{2,6},{6,10},{... | collective-permute-start | bytes 835592 | tf_op jit(solution)/shard_map/ppermute | solution.py:657
  66.3 14.2 %collective-permute-start.16 = (bf16[256,512]{1,0:T(8,128)(2,1)S(1)}, bf16[256,512]{1,0:T(8,128)(2,1)S(1)}, u32[]{:S(2)}, u32[]{:S(2)}) collective-permute-start(bf16[256,512]{1,0:T(8,128)(2,1)S(1)} %maximum_select_fusion.2.refs_1_), channel_id=1, source_target_pairs={{0,4},{4,8},{8,12},{12,0},{1,5},{5,9},{9,13},{13,1},{2,6},{6,10},{... | collective-permute-start | bytes 786440 | tf_op jit(solution)/shard_map/ppermute | solution.py:657
  66.5 14.1 %collective-permute-start.17 = (bf16[256,512]{1,0:T(8,128)(2,1)S(1)}, bf16[256,512]{1,0:T(8,128)(2,1)S(1)}, u32[]{:S(2)}, u32[]{:S(2)}) collective-permute-start(bf16[256,512]{1,0:T(8,128)(2,1)S(1)} %maximum_select_fusion.2.refs_1_), channel_id=1, source_target_pairs={{0,2},{2,0},{1,3},{3,1},{4,6},{6,4},{5,7},{7,5},{8,10},{10,8},{9,1... | collective-permute-start | bytes 786440 | tf_op jit(solution)/shard_map/ppermute | solution.py:657
  75.0 11.6 %collective-permute-start.14 = (bf16[272,512]{1,0:T(8,128)(2,1)S(1)}, bf16[272,512]{1,0:T(8,128)(2,1)S(1)}, u32[]{:S(2)}, u32[]{:S(2)}) collective-permute-start(bf16[272,512]{1,0:T(8,128)(2,1)S(1)} %collective-permute-done.12.refs_4_), channel_id=1, source_target_pairs={{0,4},{4,8},{8,12},{12,0},{1,5},{5,9},{9,13},{13,1},{2,6},{6,10},{... | collective-permute-start | bytes 835592 | tf_op jit(solution)/shard_map/ppermute | solution.py:657
  75.0 11.6 %collective-permute-start.15 = (bf16[272,512]{1,0:T(8,128)(2,1)S(1)}, bf16[272,512]{1,0:T(8,128)(2,1)S(1)}, u32[]{:S(2)}, u32[]{:S(2)}) collective-permute-start(bf16[272,512]{1,0:T(8,128)(2,1)S(1)} %collective-permute-done.12.refs_4_), channel_id=1, source_target_pairs={{0,2},{2,0},{1,3},{3,1},{4,6},{6,4},{5,7},{7,5},{8,10},{10,8},{9,1... | collective-permute-start | bytes 835592 | tf_op jit(solution)/shard_map/ppermute | solution.py:657
  80.6 11.6 %collective-permute-start.20 = (bf16[256,512]{1,0:T(8,128)(2,1)S(1)}, bf16[256,512]{1,0:T(8,128)(2,1)S(1)}, u32[]{:S(2)}, u32[]{:S(2)}) collective-permute-start(bf16[256,512]{1,0:T(8,128)(2,1)S(1)} %collective-permute-done.16.refs_5_), channel_id=1, source_target_pairs={{0,4},{4,8},{8,12},{12,0},{1,5},{5,9},{9,13},{13,1},{2,6},{6,10},{... | collective-permute-start | bytes 786440 | tf_op jit(solution)/shard_map/ppermute | solution.py:657
  80.6 11.6 %collective-permute-start.21 = (bf16[256,512]{1,0:T(8,128)(2,1)S(1)}, bf16[256,512]{1,0:T(8,128)(2,1)S(1)}, u32[]{:S(2)}, u32[]{:S(2)}) collective-permute-start(bf16[256,512]{1,0:T(8,128)(2,1)S(1)} %collective-permute-done.16.refs_5_), channel_id=1, source_target_pairs={{0,2},{2,0},{1,3},{3,1},{4,6},{6,4},{5,7},{7,5},{8,10},{10,8},{9,1... | collective-permute-start | bytes 786440 | tf_op jit(solution)/shard_map/ppermute | solution.py:657
  86.6 11.6 %collective-permute-start.18 = (bf16[272,512]{1,0:T(8,128)(2,1)S(1)}, bf16[272,512]{1,0:T(8,128)(2,1)S(1)}, u32[]{:S(2)}, u32[]{:S(2)}) collective-permute-start(bf16[272,512]{1,0:T(8,128)(2,1)S(1)} %collective-permute-done.14.refs_8_), channel_id=1, source_target_pairs={{0,4},{4,8},{8,12},{12,0},{1,5},{5,9},{9,13},{13,1},{2,6},{6,10},{... | collective-permute-start | bytes 835592 | tf_op jit(solution)/shard_map/ppermute | solution.py:657
  86.6 11.6 %collective-permute-start.19 = (bf16[272,512]{1,0:T(8,128)(2,1)S(1)}, bf16[272,512]{1,0:T(8,128)(2,1)S(1)}, u32[]{:S(2)}, u32[]{:S(2)}) collective-permute-start(bf16[272,512]{1,0:T(8,128)(2,1)S(1)} %collective-permute-done.14.refs_8_), channel_id=1, source_target_pairs={{0,2},{2,0},{1,3},{3,1},{4,6},{6,4},{5,7},{7,5},{8,10},{10,8},{9,1... | collective-permute-start | bytes 835592 | tf_op jit(solution)/shard_map/ppermute | solution.py:657
  92.2 11.6 %collective-permute-start.23 = (bf16[256,512]{1,0:T(8,128)(2,1)S(1)}, bf16[256,512]{1,0:T(8,128)(2,1)S(1)}, u32[]{:S(2)}, u32[]{:S(2)}) collective-permute-start(bf16[256,512]{1,0:T(8,128)(2,1)S(1)} %collective-permute-done.20.refs_9_), channel_id=1, source_target_pairs={{0,4},{4,8},{8,12},{12,0},{1,5},{5,9},{9,13},{13,1},{2,6},{6,10},{... | collective-permute-start | bytes 786440 | tf_op jit(solution)/shard_map/ppermute | solution.py:657
  92.2 11.6 %collective-permute-start.24 = (bf16[256,512]{1,0:T(8,128)(2,1)S(1)}, bf16[256,512]{1,0:T(8,128)(2,1)S(1)}, u32[]{:S(2)}, u32[]{:S(2)}) collective-permute-start(bf16[256,512]{1,0:T(8,128)(2,1)S(1)} %collective-permute-done.20.refs_9_), channel_id=1, source_target_pairs={{0,2},{2,0},{1,3},{3,1},{4,6},{6,4},{5,7},{7,5},{8,10},{10,8},{9,1... | collective-permute-start | bytes 786440 | tf_op jit(solution)/shard_map/ppermute | solution.py:657
  98.2 14.2 %collective-permute-start.22 = (bf16[272,512]{1,0:T(8,128)(2,1)S(1)}, bf16[272,512]{1,0:T(8,128)(2,1)S(1)}, u32[]{:S(2)}, u32[]{:S(2)}) collective-permute-start(bf16[272,512]{1,0:T(8,128)(2,1)S(1)} %collective-permute-done.18.refs_12_), channel_id=1, source_target_pairs={{0,2},{2,0},{1,3},{3,1},{4,6},{6,4},{5,7},{7,5},{8,10},{10,8},{9,1... | collective-permute-start | bytes 835592 | tf_op jit(solution)/shard_map/ppermute | solution.py:657
  120.7 13.7 %collective-permute-start.30 = (bf16[2,512,128]{2,1,0:T(8,128)(2,1)}, bf16[2,512,128]{2,1,0:T(8,128)(2,1)S(1)}, u32[]{:S(2)}, u32[]{:S(2)}) collective-permute-start(bf16[2,512,128]{2,1,0:T(8,128)(2,1)} %get-tuple-element.177), channel_id=1, source_target_pairs={{0,17},{1,16},{16,1},{17,0},{2,19},{3,18},{18,3},{19,2},{4,21},{5,... | collective-permute-start | bytes 786440 | tf_op jit(solution)/shard_map/ppermute | solution.py:817
  121.5 18.6 %collective-permute-start.32 = (bf16[2,512,128]{2,1,0:T(8,128)(2,1)}, bf16[2,512,128]{2,1,0:T(8,128)(2,1)S(1)}, u32[]{:S(2)}, u32[]{:S(2)}) collective-permute-start(bf16[2,512,128]{2,1,0:T(8,128)(2,1)} %get-tuple-element.187), channel_id=1, source_target_pairs={{0,1},{1,0},{2,3},{3,2},{4,5},{5,4},{6,7},{7,6},{8,9},{9,8},{10,11... | collective-permute-start | bytes 786440 | tf_op jit(solution)/shard_map/ppermute | solution.py:54
  121.5 19.8 %collective-permute-start.33 = (bf16[2,512,128]{2,1,0:T(8,128)(2,1)}, bf16[2,512,128]{2,1,0:T(8,128)(2,1)S(1)}, u32[]{:S(2)}, u32[]{:S(2)}) collective-permute-start(bf16[2,512,128]{2,1,0:T(8,128)(2,1)} %get-tuple-element.188.refs_2_), channel_id=1, source_target_pairs={{0,16},{1,17},{16,0},{17,1},{2,18},{3,19},{18,2},{19,3},{4,20},{5,... | collective-permute-start | bytes 786440 | tf_op jit(solution)/shard_map/ppermute | solution.py:817
  124.2 20.7 %collective-permute-start.34 = (bf16[2,512,128]{2,1,0:T(8,128)(2,1)S(1)}, bf16[2,512,128]{2,1,0:T(8,128)(2,1)S(1)}, u32[]{:S(2)}, u32[]{:S(2)}) collective-permute-start(bf16[2,512,128]{2,1,0:T(8,128)(2,1)S(1)} %copy-done.26), channel_id=1, source_target_pairs={{0,17},{1,16},{16,1},{17,0},{2,19},{3,18},{18,3},{19,2},{4,21},{5,... | collective-permute-start | bytes 786440 | tf_op jit(solution)/shard_map/ppermute | solution.py:817
  127.2 23.8 %collective-permute-start.39 = (bf16[2,256,256]{2,1,0:T(8,128)(2,1)S(1)}, bf16[2,256,256]{2,1,0:T(8,128)(2,1)S(1)}, u32[]{:S(2)}, u32[]{:S(2)}) collective-permute-start(bf16[2,256,256]{2,1,0:T(8,128)(2,1)S(1)} %pad_maximum_fusion.3), channel_id=1, source_target_pairs={{0,12},{4,0},{8,4},{12,8},{1,13},{5,1},{9,5},{13,9},{2,14},{6,2},{... | collective-permute-start | bytes 786440 | tf_op jit(solution)/shard_map/ppermute | solution.py:657
  134.4 20.1 %collective-permute-start.38 = (bf16[2,256,256]{2,1,0:T(8,128)(2,1)S(1)}, bf16[2,256,256]{2,1,0:T(8,128)(2,1)S(1)}, u32[]{:S(2)}, u32[]{:S(2)}) collective-permute-start(bf16[2,256,256]{2,1,0:T(8,128)(2,1)S(1)} %pad_maximum_fusion.2), channel_id=1, source_target_pairs={{0,8},{4,12},{8,0},{12,4},{1,9},{5,13},{9,1},{13,5},{2,10},{6,14},... | collective-permute-start | bytes 786440 | tf_op jit(solution)/shard_map/ppermute | solution.py:657
  140.1 14.4 %collective-permute-start.37 = (bf16[2,256,256]{2,1,0:T(8,128)(2,1)S(1)}, bf16[2,256,256]{2,1,0:T(8,128)(2,1)S(1)}, u32[]{:S(2)}, u32[]{:S(2)}) collective-permute-start(bf16[2,256,256]{2,1,0:T(8,128)(2,1)S(1)} %pad_maximum_fusion.1), channel_id=1, source_target_pairs={{0,4},{4,8},{8,12},{12,0},{1,5},{5,9},{9,13},{13,1},{2,6},{6,10},{... | collective-permute-start | bytes 786440 | tf_op jit(solution)/shard_map/ppermute | solution.py:657
  155.2 14.3 %collective-permute-start.44 = (bf16[256,512]{1,0:T(8,128)(2,1)S(1)}, bf16[256,512]{1,0:T(8,128)(2,1)S(1)}, u32[]{:S(2)}, u32[]{:S(2)}) collective-permute-start(bf16[256,512]{1,0:T(8,128)(2,1)S(1)} %get-tuple-element.199.refs_1_), channel_id=1, source_target_pairs={{0,4},{4,8},{8,12},{12,0},{1,5},{5,9},{9,13},{13,1},{2,6},{6,10},{... | collective-permute-start | bytes 786440 | tf_op jit(solution)/shard_map/ppermute | solution.py:657
  156.8 13.1 %collective-permute-start.45 = (bf16[256,512]{1,0:T(8,128)(2,1)S(1)}, bf16[256,512]{1,0:T(8,128)(2,1)S(1)}, u32[]{:S(2)}, u32[]{:S(2)}) collective-permute-start(bf16[256,512]{1,0:T(8,128)(2,1)S(1)} %get-tuple-element.199.refs_1_), channel_id=1, source_target_pairs={{0,2},{2,0},{1,3},{3,1},{4,6},{6,4},{5,7},{7,5},{8,10},{10,8},{9,1... | collective-permute-start | bytes 786440 | tf_op jit(solution)/shard_map/ppermute | solution.py:657
  163.8 11.2 %collective-permute-start.42 = (bf16[256,512]{1,0:T(8,128)(2,1)S(1)}, bf16[256,512]{1,0:T(8,128)(2,1)S(1)}, u32[]{:S(2)}, u32[]{:S(2)}) collective-permute-start(bf16[256,512]{1,0:T(8,128)(2,1)S(1)} %collective-permute-done.40.refs_4_), channel_id=1, source_target_pairs={{0,4},{4,8},{8,12},{12,0},{1,5},{5,9},{9,13},{13,1},{2,6},{6,10},{... | collective-permute-start | bytes 786440 | tf_op jit(solution)/shard_map/ppermute | solution.py:657
  163.8 11.9 %collective-permute-start.43 = (bf16[256,512]{1,0:T(8,128)(2,1)S(1)}, bf16[256,512]{1,0:T(8,128)(2,1)S(1)}, u32[]{:S(2)}, u32[]{:S(2)}) collective-permute-start(bf16[256,512]{1,0:T(8,128)(2,1)S(1)} %collective-permute-done.40.refs_4_), channel_id=1, source_target_pairs={{0,2},{2,0},{1,3},{3,1},{4,6},{6,4},{5,7},{7,5},{8,10},{10,8},{9,1... | collective-permute-start | bytes 786440 | tf_op jit(solution)/shard_map/ppermute | solution.py:657
  164.5 32.0 %collective-permute-start.54 = (bf16[8,256,256]{2,1,0:T(8,128)(2,1)S(1)}, bf16[8,256,256]{2,1,0:T(8,128)(2,1)S(1)}, u32[]{:S(2)}, u32[]{:S(2)}) collective-permute-start(bf16[8,256,256]{2,1,0:T(8,128)(2,1)S(1)} %constant_dynamic-update-slice_fusion.refs_14_.refs_18_.refs_22_.refs_26_.refs_30_.refs_34_.refs_38, ...), channel_id=1, source_target_pairs={{0,1},{1,0},{2,3},{3,2},{4,5},{5,4},{6,7},{7,6},{8,9},{9,8},{10,11... | collective-permute-start | bytes 3145736 | tf_op jit(solution)/shard_map/ppermute | solution.py:54
  169.5 28.0 %collective-permute-start.55 = (bf16[8,256,256]{2,1,0:T(8,128)(2,1)S(1)}, bf16[8,256,256]{2,1,0:T(8,128)(2,1)S(1)}, u32[]{:S(2)}, u32[]{:S(2)}) collective-permute-start(bf16[8,256,256]{2,1,0:T(8,128)(2,1)S(1)} %constant_dynamic-update-slice_fusion.refs_14_.refs_18_.refs_22_.refs_26_.refs_30_.refs_34_.refs_38, ...), channel_id=1, source_target_pairs={{0,16},{16,0},{1,17},{17,1},{2,18},{18,2},{3,19},{19,3},{4,20},{20... | collective-permute-start | bytes 3145736 | tf_op jit(solution)/shard_map/ppermute | solution.py:657
  169.9 10.3 %collective-permute-start.48 = (bf16[256,512]{1,0:T(8,128)(2,1)S(1)}, bf16[256,512]{1,0:T(8,128)(2,1)S(1)}, u32[]{:S(2)}, u32[]{:S(2)}) collective-permute-start(bf16[256,512]{1,0:T(8,128)(2,1)S(1)} %collective-permute-done.44.refs_5_), channel_id=1, source_target_pairs={{0,4},{4,8},{8,12},{12,0},{1,5},{5,9},{9,13},{13,1},{2,6},{6,10},{... | collective-permute-start | bytes 786440 | tf_op jit(solution)/shard_map/ppermute | solution.py:657
  (77 other events, 1165.4 us)

commit v12 on v11

--- a/solution.py
+++ b/solution.py
@@ -666,24 +666,9 @@
     return [every] + [shift(every, "tile", s) for s in range(1, tiles)], conv, *others
 
 
-def columns_kernel(layout, halves, meta, patch_ref, kept_ref, sent_ref, arrived):
-    images, tiles, outer = layout
-    ctx, _, _, mpo = split_meta(meta, images)
-    size = kept_ref.shape[2]
-    copies = []
-    for other, out_ref in enumerate((kept_ref, sent_ref)):
-        for tile in range(tiles):
-            chip = tile * outer + lax.rem(mpo + other, outer)
-            at = pl.multiple_of((chip * halves + (ctx if halves == 2 else 0)) * size, size)
-            copies.append(
-                pltpu.make_async_copy(
-                    patch_ref.at[:, pl.ds(at, size)], out_ref.at[tile], arrived.at[other, tile]
-                )
-            )
-    for copy in copies:
-        copy.start()
-    for copy in copies:
-        copy.wait()
+def columns_kernel(meta, kept_in, sent_in, kept_out, sent_out):
+    kept_out[0] = kept_in[...]
+    sent_out[0] = sent_in[...]
 
 
 def transpose_first(meta, patch_out, layout, ctxs):
@@ -693,21 +678,26 @@
     halves = 2 if ctxs == 2 and deep == 2 * CH else 1
     size = deep // halves
 
-    place = pl.BlockSpec(memory_space=pltpu.HBM)
+    def place(other):
+        def index(i, m):
+            ctx, _, _, mpo = split_meta(m, images)
+            chip = i * outer + lax.rem(mpo + other, outer)
+            return 0, chip * halves + (ctx if halves == 2 else 0)
+
+        return pl.BlockSpec((width, size), index)
+
+    out = pl.BlockSpec((1, width, size), lambda i, m: (i, 0, 0))
+    patch_out = in_hbm(patch_out)
     kept, sent = pl.pallas_call(
-        functools.partial(columns_kernel, layout, halves),
+        columns_kernel,
         grid_spec=pltpu.PrefetchScalarGridSpec(
-            num_scalar_prefetch=1,
-            grid=(1,),
-            in_specs=[place],
-            out_specs=[place, place],
-            scratch_shapes=[pltpu.SemaphoreType.DMA((2, tiles))],
+            num_scalar_prefetch=1, grid=(tiles,), in_specs=[place(0), place(1)], out_specs=[out, out]
         ),
-        out_shape=[pltpu.HBM((tiles, width, size), BF16)] * 2,
+        out_shape=[jax.ShapeDtypeStruct((tiles, width, size), BF16)] * 2,
         compiler_params=params(8),
         cost_estimate=cost(1 << 16, 2 << 20),
         name="columns",
-    )(meta, in_hbm(patch_out))
+    )(meta, patch_out, patch_out)
     return kept, sent, halves
 
 

time: 268 us -> 239 us (0.89)
  Pallas kernels: 76.4 us -> 46.9 us
    pallas_call x1, Pallas kernels: 33.5 us -> 3.88 us  [transpose_first(): pl.pallas_call(columns_kernel, grid_spec=pltpu.PrefetchScalarGridSpec(num...]
  transfers between devices with their start and end apart: 81 -> 81, of which waited for: 35 -> 35; matrix products, arithmetic and copies ran while one was open for 3% -> 3% of each run, Pallas kernels for 27% -> 17%
where the time goes in v12:
time: 239 us
  waiting for transfers between devices  117 us (49%)
  starting transfers between devices  62.2 us (26%)
  Pallas kernels  46.9 us (20%)
  local copies, waits for them, and re-layouts  6.33 us (3%)
  other arithmetic  4.52 us (2%)
    ppermute x55, waiting for transfers between devices, shift(): lax.ppermute(values, axis, [(i, (i + step) % count) for i in range(count)])  93.7 us
    ppermute x55, starting transfers between devices, shift(): lax.ppermute(values, axis, [(i, (i + step) % count) for i in range(count)])  34.4 us
    ppermute x6, waiting for transfers between devices, shifted(): return lax.ppermute(values, ('ctx', 'core'), pairs)  16.4 us
    ppermute x17, starting transfers between devices, swap(): return lax.ppermute(values, 'core', [(0, 1), (1, 0)])  14.9 us
    pallas_call x1, Pallas kernels, down_stream(): pl.pallas_call(functools.partial(down_kernel, images, tiles, half), grid_...  11.7 us
    pallas_call x2, Pallas kernels, qkv_step(): pl.pallas_call(functools.partial(qkv_kernel, entries, layout, groups, las...  10.4 us
    pallas_call x2, Pallas kernels, attention(): pl.pallas_call(functools.partial(attention_kernel, images, len(pieces), h...  8.91 us
    ppermute x3, starting transfers between devices, shards(): quad[name] = lax.ppermute(band, ('mpo', 'core'), pairs)  7.28 us
  transfers between devices with their start and end apart: 81, of which 35 were waited for; matrix products, arithmetic and copies ran while one was open for 3% of the time, Pallas kernels for 17%

profile of v12, /device:TPU:1, one launch (start us, length us, event | category | flops | bytes accessed | tf_op | source)
XLA Modules:
  0.0 238.6 jit_solution(9635844812451153765)
XLA Ops:
  1.3 2.7 %collective-permute-start = (bf16[2,16,512]{2,1,0:T(8,128)(2,1)}, bf16[2,16,512]{2,1,0:T(8,128)(2,1)S(1)}, u32[]{:S(2)}, u32[]{:S(2)}) collective-permute-start(bf16[2,16,512]{2,1,0:T(8,128)(2,1)} %param.16), channel_id=1, source_target_pairs={{0,16},{16,0},{1,17},{17,1},{2,18},{18,2},{3,19},{19,3},{4,20},{20... | collective-permute-start | bytes 98312 | tf_op jit(solution)/shard_map/ppermute | solution.py:657
  15.4 3.9 %columns.1 = (bf16[4,256,256]{2,1,0:T(8,128)(2,1)S(1)}, bf16[4,256,256]{2,1,0:T(8,128)(2,1)}) custom-call(s32[16]{0:T(128)S(1)} %concatenate.68.meta, bf16[256,4096]{1,0:T(8,128)(2,1)} %sent_in.1, bf16[256,4096]{1,0:T(8,128)(2,1)} %sent_in.1), custom_call_target="tpu_custom_call" | custom-call | flops 65536 | bytes 2097152 | tf_op jit(solution)/shard_map/columns/pallas_call | solution.py:691
  21.5 11.7 %down_stream.1 = (bf16[272,256]{1,0:T(8,128)(2,1)S(1)}, bf16[272,256]{1,0:T(8,128)(2,1)S(1)}, bf16[256,256]{1,0:T(8,128)(2,1)S(1)}, bf16[256,256]{1,0:T(8,128)(2...) custom-call(s32[16]{0:T(128)S(1)} %concatenate.68.meta, ...), custom_call_target="tpu_custom_call" | custom-call | flops 4294967296 | bytes 4194304 | tf_op jit(solution)/shard_map/down_stream/pallas_call | solution.py:185
  37.8 7.7 %collective-permute-done.12.refs_4_ = bf16[272,512]{1,0:T(8,128)(2,1)S(1)} collective-permute-done((bf16[272,512]{1,0:T(8,128)(2,1)S(1)}, bf16[272,512]{1,0:T(8,128)(2,1)S(1)}, u32[]{:S(2)}, u32[]{:S(2)}) %collective-permute-start.12) | collective-permute-done | bytes 278560 | tf_op jit(solution)/shard_map/ppermute | solution.py:657
  46.0 5.1 %collective-permute-done.16.refs_5_ = bf16[256,512]{1,0:T(8,128)(2,1)S(1)} collective-permute-done((bf16[256,512]{1,0:T(8,128)(2,1)S(1)}, bf16[256,512]{1,0:T(8,128)(2,1)S(1)}, u32[]{:S(2)}, u32[]{:S(2)}) %collective-permute-start.16) | collective-permute-done | bytes 262176 | tf_op jit(solution)/shard_map/ppermute | solution.py:657
  51.6 5.5 %collective-permute-done.14.refs_8_ = bf16[272,512]{1,0:T(8,128)(2,1)S(1)} collective-permute-done((bf16[272,512]{1,0:T(8,128)(2,1)S(1)}, bf16[272,512]{1,0:T(8,128)(2,1)S(1)}, u32[]{:S(2)}, u32[]{:S(2)}) %collective-permute-start.14) | collective-permute-done | bytes 278560 | tf_op jit(solution)/shard_map/ppermute | solution.py:657
  57.5 5.1 %collective-permute-done.20.refs_9_ = bf16[256,512]{1,0:T(8,128)(2,1)S(1)} collective-permute-done((bf16[256,512]{1,0:T(8,128)(2,1)S(1)}, bf16[256,512]{1,0:T(8,128)(2,1)S(1)}, u32[]{:S(2)}, u32[]{:S(2)}) %collective-permute-start.20) | collective-permute-done | bytes 262176 | tf_op jit(solution)/shard_map/ppermute | solution.py:657
  63.2 5.5 %collective-permute-done.18.refs_12_ = bf16[272,512]{1,0:T(8,128)(2,1)S(1)} collective-permute-done((bf16[272,512]{1,0:T(8,128)(2,1)S(1)}, bf16[272,512]{1,0:T(8,128)(2,1)S(1)}, u32[]{:S(2)}, u32[]{:S(2)}) %collective-permute-start.18) | collective-permute-done | bytes 278560 | tf_op jit(solution)/shard_map/ppermute | solution.py:657
  69.1 5.1 %collective-permute-done.23.refs_13_ = bf16[256,512]{1,0:T(8,128)(2,1)S(1)} collective-permute-done((bf16[256,512]{1,0:T(8,128)(2,1)S(1)}, bf16[256,512]{1,0:T(8,128)(2,1)S(1)}, u32[]{:S(2)}, u32[]{:S(2)}) %collective-permute-start.23) | collective-permute-done | bytes 262176 | tf_op jit(solution)/shard_map/ppermute | solution.py:657
  74.3 7.8 %qkv_step.1 = (bf16[6,512,256]{2,1,0:T(8,128)(2,1)S(1)}, f32[6,512,256]{2,1,0:T(8,128)S(1)}, f32[512,128]{1,0:T(8,128)S(1)}) custom-call(s32[16]{0:T(128)S(1)} %concatenate.68.meta, bf16[272,512]{1,0:T(8,128)(2,1)S(1)} %maximum_select_fusion.1.refs_0_, bf16[256,512]{1,0:T(8,128)(2,1)S(1)} %maximum_select_fusion.2.refs_1_, ...), custom_call_target="tpu_custom_call" | custom-call | flops 5637144576 | bytes 20971520 | tf_op jit(solution)/shard_map/qkv_step/pallas_call | solution.py:321
  82.8 2.7 %qkv_last.1 = (bf16[2,512,128]{2,1,0:T(8,128)(2,1)}, bf16[2,512,128]{2,1,0:T(8,128)(2,1)}, bf16[512,128]{1,0:T(8,128)(2,1)}, bf16[512,128]{1,0:T(8,128)(2,1)}, b...) custom-call(s32[16]{0:T(128)S(1)} %concatenate.68.meta, ...), custom_call_target="tpu_custom_call" | custom-call | flops 805306368 | bytes 8388608 | tf_op jit(solution)/shard_map/qkv_last/pallas_call | solution.py:321
  99.5 5.4 %collective-permute-done.30.refs_5_ = bf16[2,512,128]{2,1,0:T(8,128)(2,1)S(1)} collective-permute-done((bf16[2,512,128]{2,1,0:T(8,128)(2,1)}, bf16[2,512,128]{2,1,0:T(8,128)(2,1)S(1)}, u32[]{:S(2)}, u32[]{:S(2)}) %collective-permute-start.30) | collective-permute-done | bytes 262176 | tf_op jit(solution)/shard_map/ppermute | solution.py:807
  106.1 4.5 %attention.2 = (bf16[512,128]{1,0:T(8,128)(2,1)S(1)}, bf16[512,128]{1,0:T(8,128)(2,1)S(1)}) custom-call(s32[16]{0:T(128)S(1)} %concatenate.68.meta, bf16[512,128]{1,0:T(8,128)(2,1)S(1)} %copy-done.19, bf16[512,128]{1,0:T(8,128)(2,1)S(1)} %copy-done.21, bf16[2,512,128]{2,1,0:T(8,128)(2,1)S(1)} %copy-done.15, ...), custom_call_target="tpu_custom_call" | custom-call | flops 1073741824 | bytes 1048576 | tf_op jit(solution)/shard_map/attention/pallas_call | solution.py:381
  111.9 3.4 %collective-permute-done.34.refs_5_ = bf16[2,512,128]{2,1,0:T(8,128)(2,1)S(1)} collective-permute-done((bf16[2,512,128]{2,1,0:T(8,128)(2,1)S(1)}, bf16[2,512,128]{2,1,0:T(8,128)(2,1)S(1)}, u32[]{:S(2)}, u32[]{:S(2)}) %collective-permute-start.34) | collective-permute-done | bytes 262176 | tf_op jit(solution)/shard_map/ppermute | solution.py:807
  115.3 4.5 %attention.3 = (bf16[512,128]{1,0:T(8,128)(2,1)S(1)}, bf16[512,128]{1,0:T(8,128)(2,1)S(1)}) custom-call(s32[16]{0:T(128)S(1)} %concatenate.68.meta, bf16[512,128]{1,0:T(8,128)(2,1)S(1)} %copy-done.16, bf16[512,128]{1,0:T(8,128)(2,1)S(1)} %copy-done.18, bf16[2,512,128]{2,1,0:T(8,128)(2,1)S(1)} %copy-done.14, ...), custom_call_target="tpu_custom_call" | custom-call | flops 1073741824 | bytes 1048576 | tf_op jit(solution)/shard_map/attention/pallas_call | solution.py:381
  121.4 3.5 %collective-permute-done.38 = bf16[2,256,256]{2,1,0:T(8,128)(2,1)S(1)} collective-permute-done((bf16[2,256,256]{2,1,0:T(8,128)(2,1)S(1)}, bf16[2,256,256]{2,1,0:T(8,128)(2,1)S(1)}, u32[]{:S(2)}, u32[]{:S(2)}) %collective-permute-start.38) | collective-permute-done | bytes 262176 | tf_op jit(solution)/shard_map/ppermute | solution.py:657
  128.1 6.1 %collective-permute-done.40.refs_4_ = bf16[256,512]{1,0:T(8,128)(2,1)S(1)} collective-permute-done((bf16[256,512]{1,0:T(8,128)(2,1)S(1)}, bf16[256,512]{1,0:T(8,128)(2,1)S(1)}, u32[]{:S(2)}, u32[]{:S(2)}) %collective-permute-start.40) | collective-permute-done | bytes 262176 | tf_op jit(solution)/shard_map/ppermute | solution.py:657
  134.9 2.9 %collective-permute-start.54 = (bf16[8,256,256]{2,1,0:T(8,128)(2,1)S(1)}, bf16[8,256,256]{2,1,0:T(8,128)(2,1)S(1)}, u32[]{:S(2)}, u32[]{:S(2)}) collective-permute-start(bf16[8,256,256]{2,1,0:T(8,128)(2,1)S(1)} %constant_dynamic-update-slice_fusion.refs_14_.refs_18_.refs_22_.refs_26_.refs_30_.refs_34_.refs_38, ...), channel_id=1, source_target_pairs={{0,1},{1,0},{2,3},{3,2},{4,5},{5,4},{6,7},{7,6},{8,9},{9,8},{10,11... | collective-permute-start | bytes 3145736 | tf_op jit(solution)/shard_map/ppermute | solution.py:54
  140.3 5.2 %collective-permute-done.42.refs_8_ = bf16[256,512]{1,0:T(8,128)(2,1)S(1)} collective-permute-done((bf16[256,512]{1,0:T(8,128)(2,1)S(1)}, bf16[256,512]{1,0:T(8,128)(2,1)S(1)}, u32[]{:S(2)}, u32[]{:S(2)}) %collective-permute-start.42) | collective-permute-done | bytes 262176 | tf_op jit(solution)/shard_map/ppermute | solution.py:657
  146.1 4.4 %collective-permute-done.48.refs_9_ = bf16[256,512]{1,0:T(8,128)(2,1)S(1)} collective-permute-done((bf16[256,512]{1,0:T(8,128)(2,1)S(1)}, bf16[256,512]{1,0:T(8,128)(2,1)S(1)}, u32[]{:S(2)}, u32[]{:S(2)}) %collective-permute-start.48) | collective-permute-done | bytes 262176 | tf_op jit(solution)/shard_map/ppermute | solution.py:657
  151.2 4.7 %collective-permute-done.46.refs_12_ = bf16[256,512]{1,0:T(8,128)(2,1)S(1)} collective-permute-done((bf16[256,512]{1,0:T(8,128)(2,1)S(1)}, bf16[256,512]{1,0:T(8,128)(2,1)S(1)}, u32[]{:S(2)}, u32[]{:S(2)}) %collective-permute-start.46) | collective-permute-done | bytes 262176 | tf_op jit(solution)/shard_map/ppermute | solution.py:657
  156.6 4.4 %collective-permute-done.51.refs_13_ = bf16[256,512]{1,0:T(8,128)(2,1)S(1)} collective-permute-done((bf16[256,512]{1,0:T(8,128)(2,1)S(1)}, bf16[256,512]{1,0:T(8,128)(2,1)S(1)}, u32[]{:S(2)}, u32[]{:S(2)}) %collective-permute-start.51) | collective-permute-done | bytes 262176 | tf_op jit(solution)/shard_map/ppermute | solution.py:657
  162.9 4.0 %out_step.1.refs_4_ = f32[2,512,256]{2,1,0:T(8,128)S(1)} custom-call(s32[16]{0:T(128)S(1)} %concatenate.68.meta, bf16[256,512]{1,0:T(8,128)(2,1)S(1)} %get-tuple-element.197.refs_0_, bf16[256,512]{1,0:T(8,128)(2,1)S(1)} %get-tuple-element.199.refs_1_, bf16[256,512]{1,0:T(8,128)(2,1)S(1)} %collective-permute-done.41.refs_2_, ...), custom_call_target="tpu_custom_call" | custom-call | flops 1879048192 | bytes 9437184 | tf_op jit(solution)/shard_map/out_step/pallas_call | solution.py:438
  169.3 5.1 %collective-permute-start.57 = (bf16[8,256,256]{2,1,0:T(8,128)(2,1)S(1)}, bf16[8,256,256]{2,1,0:T(8,128)(2,1)S(1)}, u32[]{:S(2)}, u32[]{:S(2)}) collective-permute-start(bf16[8,256,256]{2,1,0:T(8,128)(2,1)S(1)} %collective-permute-done.55.refs_16_.refs_20_.refs_24_.refs_28_.refs_32_.refs_36_.refs_40_.refs_4_), channel_id=1, source_target_pairs={{0,1},{1,0},{2,3},{3,2},{4,5},{5,4},{6,7},{7,6},{8,9},{9,8},{10,11... | collective-permute-start | bytes 3145736 | tf_op jit(solution)/shard_map/ppermute | solution.py:54
  182.1 3.1 %collective-permute-done.58.refs_1_ = bf16[256,256]{1,0:T(8,128)(2,1)S(1)} collective-permute-done((bf16[256,256]{1,0:T(8,128)(2,1)S(1)}, bf16[256,256]{1,0:T(8,128)(2,1)S(1)}, u32[]{:S(2)}, u32[]{:S(2)}) %collective-permute-start.58) | collective-permute-done | bytes 131104 | tf_op jit(solution)/shard_map/ppermute | solution.py:807
  185.2 3.1 %collective-permute-done.60.refs_3_ = bf16[256,256]{1,0:T(8,128)(2,1)S(1)} collective-permute-done((bf16[256,256]{1,0:T(8,128)(2,1)S(1)}, bf16[256,256]{1,0:T(8,128)(2,1)S(1)}, u32[]{:S(2)}, u32[]{:S(2)}) %collective-permute-start.60) | collective-permute-done | bytes 131104 | tf_op jit(solution)/shard_map/ppermute | solution.py:807
  190.0 5.3 %collective-permute-done.61.refs_4_ = bf16[128,512]{1,0:T(8,128)(2,1)} collective-permute-done((bf16[128,512]{1,0:T(8,128)(2,1)S(1)}, bf16[128,512]{1,0:T(8,128)(2,1)}, u32[]{:S(2)}, u32[]{:S(2)}) %collective-permute-start.61) | collective-permute-done | bytes 131104 | tf_op jit(solution)/shard_map/ppermute | solution.py:657
  195.3 2.8 %collective-permute-done.65.refs_5_ = bf16[128,512]{1,0:T(8,128)(2,1)} collective-permute-done((bf16[128,512]{1,0:T(8,128)(2,1)S(1)}, bf16[128,512]{1,0:T(8,128)(2,1)}, u32[]{:S(2)}, u32[]{:S(2)}) %collective-permute-start.65) | collective-permute-done | bytes 131104 | tf_op jit(solution)/shard_map/ppermute | solution.py:657
  199.8 7.2 %collective-permute-done.63.refs_8_ = bf16[128,512]{1,0:T(8,128)(2,1)S(1)} collective-permute-done((bf16[128,512]{1,0:T(8,128)(2,1)}, bf16[128,512]{1,0:T(8,128)(2,1)S(1)}, u32[]{:S(2)}, u32[]{:S(2)}) %collective-permute-start.63) | collective-permute-done | bytes 131104 | tf_op jit(solution)/shard_map/ppermute | solution.py:657
  208.7 6.0 %collective-permute-done.67.refs_12_ = bf16[128,512]{1,0:T(8,128)(2,1)S(1)} collective-permute-done((bf16[128,512]{1,0:T(8,128)(2,1)S(1)}, bf16[128,512]{1,0:T(8,128)(2,1)S(1)}, u32[]{:S(2)}, u32[]{:S(2)}) %collective-permute-start.67) | collective-permute-done | bytes 131104 | tf_op jit(solution)/shard_map/ppermute | solution.py:657
  218.5 2.7 %collective-permute-done.74.refs_1_ = bf16[128,512]{1,0:T(8,128)(2,1)S(1)} collective-permute-done((bf16[128,512]{1,0:T(8,128)(2,1)S(1)}, bf16[128,512]{1,0:T(8,128)(2,1)S(1)}, u32[]{:S(2)}, u32[]{:S(2)}) %collective-permute-start.74) | collective-permute-done | bytes 131104 | tf_op jit(solution)/shard_map/ppermute | solution.py:657
  228.0 5.9 %collective-permute-start.79 = (f32[64,128]{1,0:T(8,128)S(1)}, f32[64,128]{1,0:T(8,128)S(1)}, u32[]{:S(2)}, u32[]{:S(2)}) collective-permute-start(f32[64,128]{1,0:T(8,128)S(1)} %fusion.25.own_a), channel_id=1, source_target_pairs={{0,1},{1,0},{2,3},{3,2},{4,5},{5,4},{6,7},{7,6},{8,9},{9,8},{10,11... | collective-permute-start | bytes 98312 | tf_op jit(solution)/shard_map/ppermute | solution.py:871
  (237 shorter events, 80.6 us)
Async XLA Ops:
  1.2 20.3 %collective-permute-start.8 = (bf16[4096,256]{1,0:T(8,128)(2,1)}, bf16[4096,256]{1,0:T(8,128)(2,1)}, u32[]{:S(2)}, u32[]{:S(2)}) collective-permute-start(bf16[4096,256]{1,0:T(8,128)(2,1)} %refs_13_.1), channel_id=1, source_target_pairs={{0,1},{1,0},{2,3},{3,2},{4,5},{5,4},{6,7},{7,6},{8,9},{9,8},{10,11... | collective-permute-start | bytes 6291464 | tf_op jit(solution)/shard_map/ppermute | solution.py:54
  19.3 13.9 %collective-permute-start.9 = (bf16[4,256,256]{2,1,0:T(8,128)(2,1)}, bf16[4,256,256]{2,1,0:T(8,128)(2,1)}, u32[]{:S(2)}, u32[]{:S(2)}) collective-permute-start(bf16[4,256,256]{2,1,0:T(8,128)(2,1)} %get-tuple-element.141), channel_id=1, source_target_pairs={{0,2},{2,0},{1,3},{3,1},{4,6},{6,4},{5,7},{7,5},{8,10},{10,8},{9,1... | collective-permute-start | bytes 1572872 | tf_op jit(solution)/shard_map/ppermute | solution.py:657
  19.7 62.4 %collective-permute-start.26 = (bf16[4096,256]{1,0:T(8,128)(2,1)S(1)}, bf16[4096,256]{1,0:T(8,128)(2,1)}, u32[]{:S(2)}, u32[]{:S(2)}) collective-permute-start(bf16[4096,256]{1,0:T(8,128)(2,1)S(1)} %copy-done.1), channel_id=1, source_target_pairs={{0,1},{1,0},{2,3},{3,2},{4,5},{5,4},{6,7},{7,6},{8,9},{9,8},{10,11... | collective-permute-start | bytes 6291464 | tf_op jit(solution)/shard_map/ppermute | solution.py:54
  35.5 9.9 %collective-permute-start.12 = (bf16[272,512]{1,0:T(8,128)(2,1)S(1)}, bf16[272,512]{1,0:T(8,128)(2,1)S(1)}, u32[]{:S(2)}, u32[]{:S(2)}) collective-permute-start(bf16[272,512]{1,0:T(8,128)(2,1)S(1)} %maximum_select_fusion.1.refs_0_), channel_id=1, source_target_pairs={{0,4},{4,8},{8,12},{12,0},{1,5},{5,9},{9,13},{13,1},{2,6},{6,10},{... | collective-permute-start | bytes 835592 | tf_op jit(solution)/shard_map/ppermute | solution.py:657
  37.3 13.8 %collective-permute-start.16 = (bf16[256,512]{1,0:T(8,128)(2,1)S(1)}, bf16[256,512]{1,0:T(8,128)(2,1)S(1)}, u32[]{:S(2)}, u32[]{:S(2)}) collective-permute-start(bf16[256,512]{1,0:T(8,128)(2,1)S(1)} %maximum_select_fusion.2.refs_1_), channel_id=1, source_target_pairs={{0,4},{4,8},{8,12},{12,0},{1,5},{5,9},{9,13},{13,1},{2,6},{6,10},{... | collective-permute-start | bytes 786440 | tf_op jit(solution)/shard_map/ppermute | solution.py:657
  37.4 13.7 %collective-permute-start.17 = (bf16[256,512]{1,0:T(8,128)(2,1)S(1)}, bf16[256,512]{1,0:T(8,128)(2,1)S(1)}, u32[]{:S(2)}, u32[]{:S(2)}) collective-permute-start(bf16[256,512]{1,0:T(8,128)(2,1)S(1)} %maximum_select_fusion.2.refs_1_), channel_id=1, source_target_pairs={{0,2},{2,0},{1,3},{3,1},{4,6},{6,4},{5,7},{7,5},{8,10},{10,8},{9,1... | collective-permute-start | bytes 786440 | tf_op jit(solution)/shard_map/ppermute | solution.py:657
  45.5 11.6 %collective-permute-start.14 = (bf16[272,512]{1,0:T(8,128)(2,1)S(1)}, bf16[272,512]{1,0:T(8,128)(2,1)S(1)}, u32[]{:S(2)}, u32[]{:S(2)}) collective-permute-start(bf16[272,512]{1,0:T(8,128)(2,1)S(1)} %collective-permute-done.12.refs_4_), channel_id=1, source_target_pairs={{0,4},{4,8},{8,12},{12,0},{1,5},{5,9},{9,13},{13,1},{2,6},{6,10},{... | collective-permute-start | bytes 835592 | tf_op jit(solution)/shard_map/ppermute | solution.py:657
  45.5 11.6 %collective-permute-start.15 = (bf16[272,512]{1,0:T(8,128)(2,1)S(1)}, bf16[272,512]{1,0:T(8,128)(2,1)S(1)}, u32[]{:S(2)}, u32[]{:S(2)}) collective-permute-start(bf16[272,512]{1,0:T(8,128)(2,1)S(1)} %collective-permute-done.12.refs_4_), channel_id=1, source_target_pairs={{0,2},{2,0},{1,3},{3,1},{4,6},{6,4},{5,7},{7,5},{8,10},{10,8},{9,1... | collective-permute-start | bytes 835592 | tf_op jit(solution)/shard_map/ppermute | solution.py:657
  51.1 11.6 %collective-permute-start.20 = (bf16[256,512]{1,0:T(8,128)(2,1)S(1)}, bf16[256,512]{1,0:T(8,128)(2,1)S(1)}, u32[]{:S(2)}, u32[]{:S(2)}) collective-permute-start(bf16[256,512]{1,0:T(8,128)(2,1)S(1)} %collective-permute-done.16.refs_5_), channel_id=1, source_target_pairs={{0,4},{4,8},{8,12},{12,0},{1,5},{5,9},{9,13},{13,1},{2,6},{6,10},{... | collective-permute-start | bytes 786440 | tf_op jit(solution)/shard_map/ppermute | solution.py:657
  51.1 11.6 %collective-permute-start.21 = (bf16[256,512]{1,0:T(8,128)(2,1)S(1)}, bf16[256,512]{1,0:T(8,128)(2,1)S(1)}, u32[]{:S(2)}, u32[]{:S(2)}) collective-permute-start(bf16[256,512]{1,0:T(8,128)(2,1)S(1)} %collective-permute-done.16.refs_5_), channel_id=1, source_target_pairs={{0,2},{2,0},{1,3},{3,1},{4,6},{6,4},{5,7},{7,5},{8,10},{10,8},{9,1... | collective-permute-start | bytes 786440 | tf_op jit(solution)/shard_map/ppermute | solution.py:657
  57.0 11.6 %collective-permute-start.18 = (bf16[272,512]{1,0:T(8,128)(2,1)S(1)}, bf16[272,512]{1,0:T(8,128)(2,1)S(1)}, u32[]{:S(2)}, u32[]{:S(2)}) collective-permute-start(bf16[272,512]{1,0:T(8,128)(2,1)S(1)} %collective-permute-done.14.refs_8_), channel_id=1, source_target_pairs={{0,4},{4,8},{8,12},{12,0},{1,5},{5,9},{9,13},{13,1},{2,6},{6,10},{... | collective-permute-start | bytes 835592 | tf_op jit(solution)/shard_map/ppermute | solution.py:657
  57.1 11.6 %collective-permute-start.19 = (bf16[272,512]{1,0:T(8,128)(2,1)S(1)}, bf16[272,512]{1,0:T(8,128)(2,1)S(1)}, u32[]{:S(2)}, u32[]{:S(2)}) collective-permute-start(bf16[272,512]{1,0:T(8,128)(2,1)S(1)} %collective-permute-done.14.refs_8_), channel_id=1, source_target_pairs={{0,2},{2,0},{1,3},{3,1},{4,6},{6,4},{5,7},{7,5},{8,10},{10,8},{9,1... | collective-permute-start | bytes 835592 | tf_op jit(solution)/shard_map/ppermute | solution.py:657
  62.7 11.6 %collective-permute-start.23 = (bf16[256,512]{1,0:T(8,128)(2,1)S(1)}, bf16[256,512]{1,0:T(8,128)(2,1)S(1)}, u32[]{:S(2)}, u32[]{:S(2)}) collective-permute-start(bf16[256,512]{1,0:T(8,128)(2,1)S(1)} %collective-permute-done.20.refs_9_), channel_id=1, source_target_pairs={{0,4},{4,8},{8,12},{12,0},{1,5},{5,9},{9,13},{13,1},{2,6},{6,10},{... | collective-permute-start | bytes 786440 | tf_op jit(solution)/shard_map/ppermute | solution.py:657
  62.7 11.6 %collective-permute-start.24 = (bf16[256,512]{1,0:T(8,128)(2,1)S(1)}, bf16[256,512]{1,0:T(8,128)(2,1)S(1)}, u32[]{:S(2)}, u32[]{:S(2)}) collective-permute-start(bf16[256,512]{1,0:T(8,128)(2,1)S(1)} %collective-permute-done.20.refs_9_), channel_id=1, source_target_pairs={{0,2},{2,0},{1,3},{3,1},{4,6},{6,4},{5,7},{7,5},{8,10},{10,8},{9,1... | collective-permute-start | bytes 786440 | tf_op jit(solution)/shard_map/ppermute | solution.py:657
  68.6 14.2 %collective-permute-start.22 = (bf16[272,512]{1,0:T(8,128)(2,1)S(1)}, bf16[272,512]{1,0:T(8,128)(2,1)S(1)}, u32[]{:S(2)}, u32[]{:S(2)}) collective-permute-start(bf16[272,512]{1,0:T(8,128)(2,1)S(1)} %collective-permute-done.18.refs_12_), channel_id=1, source_target_pairs={{0,2},{2,0},{1,3},{3,1},{4,6},{6,4},{5,7},{7,5},{8,10},{10,8},{9,1... | collective-permute-start | bytes 835592 | tf_op jit(solution)/shard_map/ppermute | solution.py:657
  91.1 13.7 %collective-permute-start.30 = (bf16[2,512,128]{2,1,0:T(8,128)(2,1)}, bf16[2,512,128]{2,1,0:T(8,128)(2,1)S(1)}, u32[]{:S(2)}, u32[]{:S(2)}) collective-permute-start(bf16[2,512,128]{2,1,0:T(8,128)(2,1)} %get-tuple-element.177), channel_id=1, source_target_pairs={{0,17},{1,16},{16,1},{17,0},{2,19},{3,18},{18,3},{19,2},{4,21},{5,... | collective-permute-start | bytes 786440 | tf_op jit(solution)/shard_map/ppermute | solution.py:807
  91.9 18.7 %collective-permute-start.32 = (bf16[2,512,128]{2,1,0:T(8,128)(2,1)}, bf16[2,512,128]{2,1,0:T(8,128)(2,1)S(1)}, u32[]{:S(2)}, u32[]{:S(2)}) collective-permute-start(bf16[2,512,128]{2,1,0:T(8,128)(2,1)} %get-tuple-element.187), channel_id=1, source_target_pairs={{0,1},{1,0},{2,3},{3,2},{4,5},{5,4},{6,7},{7,6},{8,9},{9,8},{10,11... | collective-permute-start | bytes 786440 | tf_op jit(solution)/shard_map/ppermute | solution.py:54
  92.6 19.2 %collective-permute-start.33 = (bf16[2,512,128]{2,1,0:T(8,128)(2,1)}, bf16[2,512,128]{2,1,0:T(8,128)(2,1)S(1)}, u32[]{:S(2)}, u32[]{:S(2)}) collective-permute-start(bf16[2,512,128]{2,1,0:T(8,128)(2,1)} %get-tuple-element.188.refs_2_), channel_id=1, source_target_pairs={{0,16},{1,17},{16,0},{17,1},{2,18},{3,19},{18,2},{19,3},{4,20},{5,... | collective-permute-start | bytes 786440 | tf_op jit(solution)/shard_map/ppermute | solution.py:807
  95.2 20.1 %collective-permute-start.34 = (bf16[2,512,128]{2,1,0:T(8,128)(2,1)S(1)}, bf16[2,512,128]{2,1,0:T(8,128)(2,1)S(1)}, u32[]{:S(2)}, u32[]{:S(2)}) collective-permute-start(bf16[2,512,128]{2,1,0:T(8,128)(2,1)S(1)} %copy-done.25), channel_id=1, source_target_pairs={{0,17},{1,16},{16,1},{17,0},{2,19},{3,18},{18,3},{19,2},{4,21},{5,... | collective-permute-start | bytes 786440 | tf_op jit(solution)/shard_map/ppermute | solution.py:807
  97.6 23.8 %collective-permute-start.39 = (bf16[2,256,256]{2,1,0:T(8,128)(2,1)S(1)}, bf16[2,256,256]{2,1,0:T(8,128)(2,1)S(1)}, u32[]{:S(2)}, u32[]{:S(2)}) collective-permute-start(bf16[2,256,256]{2,1,0:T(8,128)(2,1)S(1)} %pad_maximum_fusion.3), channel_id=1, source_target_pairs={{0,12},{4,0},{8,4},{12,8},{1,13},{5,1},{9,5},{13,9},{2,14},{6,2},{... | collective-permute-start | bytes 786440 | tf_op jit(solution)/shard_map/ppermute | solution.py:657
  104.8 20.1 %collective-permute-start.38 = (bf16[2,256,256]{2,1,0:T(8,128)(2,1)S(1)}, bf16[2,256,256]{2,1,0:T(8,128)(2,1)S(1)}, u32[]{:S(2)}, u32[]{:S(2)}) collective-permute-start(bf16[2,256,256]{2,1,0:T(8,128)(2,1)S(1)} %pad_maximum_fusion.2), channel_id=1, source_target_pairs={{0,8},{4,12},{8,0},{12,4},{1,9},{5,13},{9,1},{13,5},{2,10},{6,14},... | collective-permute-start | bytes 786440 | tf_op jit(solution)/shard_map/ppermute | solution.py:657
  110.6 14.3 %collective-permute-start.37 = (bf16[2,256,256]{2,1,0:T(8,128)(2,1)S(1)}, bf16[2,256,256]{2,1,0:T(8,128)(2,1)S(1)}, u32[]{:S(2)}, u32[]{:S(2)}) collective-permute-start(bf16[2,256,256]{2,1,0:T(8,128)(2,1)S(1)} %pad_maximum_fusion.1), channel_id=1, source_target_pairs={{0,4},{4,8},{8,12},{12,0},{1,5},{5,9},{9,13},{13,1},{2,6},{6,10},{... | collective-permute-start | bytes 786440 | tf_op jit(solution)/shard_map/ppermute | solution.py:657
  125.6 14.3 %collective-permute-start.44 = (bf16[256,512]{1,0:T(8,128)(2,1)S(1)}, bf16[256,512]{1,0:T(8,128)(2,1)S(1)}, u32[]{:S(2)}, u32[]{:S(2)}) collective-permute-start(bf16[256,512]{1,0:T(8,128)(2,1)S(1)} %get-tuple-element.199.refs_1_), channel_id=1, source_target_pairs={{0,4},{4,8},{8,12},{12,0},{1,5},{5,9},{9,13},{13,1},{2,6},{6,10},{... | collective-permute-start | bytes 786440 | tf_op jit(solution)/shard_map/ppermute | solution.py:657
  127.2 13.0 %collective-permute-start.45 = (bf16[256,512]{1,0:T(8,128)(2,1)S(1)}, bf16[256,512]{1,0:T(8,128)(2,1)S(1)}, u32[]{:S(2)}, u32[]{:S(2)}) collective-permute-start(bf16[256,512]{1,0:T(8,128)(2,1)S(1)} %get-tuple-element.199.refs_1_), channel_id=1, source_target_pairs={{0,2},{2,0},{1,3},{3,1},{4,6},{6,4},{5,7},{7,5},{8,10},{10,8},{9,1... | collective-permute-start | bytes 786440 | tf_op jit(solution)/shard_map/ppermute | solution.py:657
  134.2 11.2 %collective-permute-start.42 = (bf16[256,512]{1,0:T(8,128)(2,1)S(1)}, bf16[256,512]{1,0:T(8,128)(2,1)S(1)}, u32[]{:S(2)}, u32[]{:S(2)}) collective-permute-start(bf16[256,512]{1,0:T(8,128)(2,1)S(1)} %collective-permute-done.40.refs_4_), channel_id=1, source_target_pairs={{0,4},{4,8},{8,12},{12,0},{1,5},{5,9},{9,13},{13,1},{2,6},{6,10},{... | collective-permute-start | bytes 786440 | tf_op jit(solution)/shard_map/ppermute | solution.py:657
  134.2 11.9 %collective-permute-start.43 = (bf16[256,512]{1,0:T(8,128)(2,1)S(1)}, bf16[256,512]{1,0:T(8,128)(2,1)S(1)}, u32[]{:S(2)}, u32[]{:S(2)}) collective-permute-start(bf16[256,512]{1,0:T(8,128)(2,1)S(1)} %collective-permute-done.40.refs_4_), channel_id=1, source_target_pairs={{0,2},{2,0},{1,3},{3,1},{4,6},{6,4},{5,7},{7,5},{8,10},{10,8},{9,1... | collective-permute-start | bytes 786440 | tf_op jit(solution)/shard_map/ppermute | solution.py:657
  134.9 32.0 %collective-permute-start.54 = (bf16[8,256,256]{2,1,0:T(8,128)(2,1)S(1)}, bf16[8,256,256]{2,1,0:T(8,128)(2,1)S(1)}, u32[]{:S(2)}, u32[]{:S(2)}) collective-permute-start(bf16[8,256,256]{2,1,0:T(8,128)(2,1)S(1)} %constant_dynamic-update-slice_fusion.refs_14_.refs_18_.refs_22_.refs_26_.refs_30_.refs_34_.refs_38, ...), channel_id=1, source_target_pairs={{0,1},{1,0},{2,3},{3,2},{4,5},{5,4},{6,7},{7,6},{8,9},{9,8},{10,11... | collective-permute-start | bytes 3145736 | tf_op jit(solution)/shard_map/ppermute | solution.py:54
  139.8 28.1 %collective-permute-start.55 = (bf16[8,256,256]{2,1,0:T(8,128)(2,1)S(1)}, bf16[8,256,256]{2,1,0:T(8,128)(2,1)S(1)}, u32[]{:S(2)}, u32[]{:S(2)}) collective-permute-start(bf16[8,256,256]{2,1,0:T(8,128)(2,1)S(1)} %constant_dynamic-update-slice_fusion.refs_14_.refs_18_.refs_22_.refs_26_.refs_30_.refs_34_.refs_38, ...), channel_id=1, source_target_pairs={{0,16},{16,0},{1,17},{17,1},{2,18},{18,2},{3,19},{19,3},{4,20},{20... | collective-permute-start | bytes 3145736 | tf_op jit(solution)/shard_map/ppermute | solution.py:657
  140.3 10.3 %collective-permute-start.48 = (bf16[256,512]{1,0:T(8,128)(2,1)S(1)}, bf16[256,512]{1,0:T(8,128)(2,1)S(1)}, u32[]{:S(2)}, u32[]{:S(2)}) collective-permute-start(bf16[256,512]{1,0:T(8,128)(2,1)S(1)} %collective-permute-done.44.refs_5_), channel_id=1, source_target_pairs={{0,4},{4,8},{8,12},{12,0},{1,5},{5,9},{9,13},{13,1},{2,6},{6,10},{... | collective-permute-start | bytes 786440 | tf_op jit(solution)/shard_map/ppermute | solution.py:657
  146.1 9.8 %collective-permute-start.46 = (bf16[256,512]{1,0:T(8,128)(2,1)S(1)}, bf16[256,512]{1,0:T(8,128)(2,1)S(1)}, u32[]{:S(2)}, u32[]{:S(2)}) collective-permute-start(bf16[256,512]{1,0:T(8,128)(2,1)S(1)} %collective-permute-done.42.refs_8_), channel_id=1, source_target_pairs={{0,4},{4,8},{8,12},{12,0},{1,5},{5,9},{9,13},{13,1},{2,6},{6,10},{... | collective-permute-start | bytes 786440 | tf_op jit(solution)/shard_map/ppermute | solution.py:657
  151.2 9.8 %collective-permute-start.51 = (bf16[256,512]{1,0:T(8,128)(2,1)S(1)}, bf16[256,512]{1,0:T(8,128)(2,1)S(1)}, u32[]{:S(2)}, u32[]{:S(2)}) collective-permute-start(bf16[256,512]{1,0:T(8,128)(2,1)S(1)} %collective-permute-done.48.refs_9_), channel_id=1, source_target_pairs={{0,4},{4,8},{8,12},{12,0},{1,5},{5,9},{9,13},{13,1},{2,6},{6,10},{... | collective-permute-start | bytes 786440 | tf_op jit(solution)/shard_map/ppermute | solution.py:657
  169.3 9.9 %collective-permute-start.57 = (bf16[8,256,256]{2,1,0:T(8,128)(2,1)S(1)}, bf16[8,256,256]{2,1,0:T(8,128)(2,1)S(1)}, u32[]{:S(2)}, u32[]{:S(2)}) collective-permute-start(bf16[8,256,256]{2,1,0:T(8,128)(2,1)S(1)} %collective-permute-done.55.refs_16_.refs_20_.refs_24_.refs_28_.refs_32_.refs_36_.refs_40_.refs_4_), channel_id=1, source_target_pairs={{0,1},{1,0},{2,3},{3,2},{4,5},{5,4},{6,7},{7,6},{8,9},{9,8},{10,11... | collective-permute-start | bytes 3145736 | tf_op jit(solution)/shard_map/ppermute | solution.py:54
  (76 other events, 989.6 us)

commit v13 on v12

--- a/solution.py
+++ b/solution.py
@@ -795,6 +795,7 @@
         *[by_core(core, s[0], o, 1) for s, o in zip(streams, others)], None, project, swap(out_weight)
     )
     heads = width // HD
+    state, kept, received = lax.optimization_barrier((state, kept, received))
     kv_send, q_send = state[:heads], state[heads : 2 * heads]
     kv_own, q_own = state[2 * heads : 3 * heads], state[3 * heads :]
 
@@ -812,11 +813,11 @@
         pieces = [kv_own[head], swap(kv_send[head])]
         for step in range(1, ctxs):
             pieces += [shifted(kv_own[head], step, False), shifted(kv_send[head], step, True)]
-        q_par, q_send, kv_send, kv_own, kept, received = lax.optimization_barrier(
-            (q_par, q_send, kv_send, kv_own, kept, received)
-        )
+        q_par, q_send, kv_send, kv_own = lax.optimization_barrier((q_par, q_send, kv_send, kv_own))
+        if head == 0:
+            up_blocks = [transpose_second(kept, received, step) for step in range(tiles)]
+            pieces, up_blocks[tiles // 2] = lax.optimization_barrier((pieces, up_blocks[tiles // 2]))
         results.append(attention(meta, [q_own[head], q_par], pieces, images))
-    up_blocks = [transpose_second(kept, received, step) for step in range(tiles)]
     att_own = [result[0] for result in results]
     att_par = [swap(result[1]) for result in results]
     rows = half // 2

time: 239 us -> 268 us (1.12)
  local copies, waits for them, and re-layouts: 6.33 us -> 35.3 us
  waiting for transfers between devices: 117 us -> 105 us
  starting transfers between devices: 62.2 us -> 72.3 us
    unnamed x58 -> x110, local copies, waits for them, and re-layouts: 4.23 us -> 33.2 us
    ppermute x55, starting transfers between devices: 34.4 us -> 41.9 us  [shift(): lax.ppermute(values, axis, [(i, (i + step) % count) for i in range(count)])]
    ppermute x55, waiting for transfers between devices: 93.7 us -> 86.8 us  [shift(): lax.ppermute(values, axis, [(i, (i + step) % count) for i in range(count)])]
    ppermute x17, starting transfers between devices: 14.9 us -> 18.9 us  [swap(): return lax.ppermute(values, 'core', [(0, 1), (1, 0)])]
    ppermute x6, waiting for transfers between devices: 16.4 us -> 12.5 us  [shifted(): return lax.ppermute(values, ('ctx', 'core'), pairs)]
  transfers between devices with their start and end apart: 81 -> 81, of which waited for: 35 -> 31; matrix products, arithmetic and copies ran while one was open for 3% -> 3% of each run, Pallas kernels for 17% -> 16%
where the time goes in v13:
time: 268 us; the launch traced here: 266 us
  waiting for transfers between devices  105 us (39%)
  starting transfers between devices  72.3 us (27%)
  Pallas kernels  47.8 us (18%)
  local copies, waits for them, and re-layouts  35.3 us (13%)
  other arithmetic  4.52 us (2%)
    ppermute x55, waiting for transfers between devices, shift(): lax.ppermute(values, axis, [(i, (i + step) % count) for i in range(count)])  86.8 us
    ppermute x55, starting transfers between devices, shift(): lax.ppermute(values, axis, [(i, (i + step) % count) for i in range(count)])  41.9 us
    unnamed x110, local copies, waits for them, and re-layouts  33.2 us
    ppermute x17, starting transfers between devices, swap(): return lax.ppermute(values, 'core', [(0, 1), (1, 0)])  18.9 us
    ppermute x6, waiting for transfers between devices, shifted(): return lax.ppermute(values, ('ctx', 'core'), pairs)  12.5 us
    pallas_call x2, Pallas kernels, qkv_step(): pl.pallas_call(functools.partial(qkv_kernel, entries, layout, groups, las...  11.6 us
    pallas_call x1, Pallas kernels, down_stream(): pl.pallas_call(functools.partial(down_kernel, images, tiles, half), grid_...  11.4 us
    pallas_call x2, Pallas kernels, attention(): pl.pallas_call(functools.partial(attention_kernel, images, len(pieces), h...  8.9 us
  transfers between devices with their start and end apart: 81, of which 31 were waited for; matrix products, arithmetic and copies ran while one was open for 3% of the time, Pallas kernels for 16%

profile of v13, /device:TPU:1, one launch (start us, length us, event | category | flops | bytes accessed | tf_op | source)
XLA Modules:
  0.0 266.4 jit_solution(5539293147215836294)
XLA Ops:
  1.3 2.7 %collective-permute-start = (bf16[2,16,512]{2,1,0:T(8,128)(2,1)}, bf16[2,16,512]{2,1,0:T(8,128)(2,1)S(1)}, u32[]{:S(2)}, u32[]{:S(2)}) collective-permute-start(bf16[2,16,512]{2,1,0:T(8,128)(2,1)} %param.16), channel_id=1, source_target_pairs={{0,16},{16,0},{1,17},{17,1},{2,18},{18,2},{3,19},{19,3},{4,20},{20... | collective-permute-start | bytes 98312 | tf_op jit(solution)/shard_map/ppermute | solution.py:657
  15.4 3.9 %columns.1 = (bf16[4,256,256]{2,1,0:T(8,128)(2,1)S(1)}, bf16[4,256,256]{2,1,0:T(8,128)(2,1)}) custom-call(s32[16]{0:T(128)S(1)} %concatenate.68.meta, bf16[256,4096]{1,0:T(8,128)(2,1)} %sent_in.1, bf16[256,4096]{1,0:T(8,128)(2,1)} %sent_in.1), custom_call_target="tpu_custom_call" | custom-call | flops 65536 | bytes 2097152 | tf_op jit(solution)/shard_map/columns/pallas_call | solution.py:691
  21.5 11.4 %down_stream.1 = (bf16[272,256]{1,0:T(8,128)(2,1)S(1)}, bf16[272,256]{1,0:T(8,128)(2,1)S(1)}, bf16[256,256]{1,0:T(8,128)(2,1)S(1)}, bf16[256,256]{1,0:T(8,128)(2...) custom-call(s32[16]{0:T(128)S(1)} %concatenate.68.meta, ...), custom_call_target="tpu_custom_call" | custom-call | flops 4294967296 | bytes 4194304 | tf_op jit(solution)/shard_map/down_stream/pallas_call | solution.py:185
  46.3 6.3 %collective-permute-done.12.refs_4_ = bf16[272,512]{1,0:T(8,128)(2,1)S(1)} collective-permute-done((bf16[272,512]{1,0:T(8,128)(2,1)S(1)}, bf16[272,512]{1,0:T(8,128)(2,1)S(1)}, u32[]{:S(2)}, u32[]{:S(2)}) %collective-permute-start.12) | collective-permute-done | bytes 278560 | tf_op jit(solution)/shard_map/ppermute | solution.py:657
  55.2 3.0 %collective-permute-done.16.refs_5_ = bf16[256,512]{1,0:T(8,128)(2,1)S(1)} collective-permute-done((bf16[256,512]{1,0:T(8,128)(2,1)S(1)}, bf16[256,512]{1,0:T(8,128)(2,1)S(1)}, u32[]{:S(2)}, u32[]{:S(2)}) %collective-permute-start.16) | collective-permute-done | bytes 262176 | tf_op jit(solution)/shard_map/ppermute | solution.py:657
  60.8 2.9 %collective-permute-done.14.refs_8_ = bf16[272,512]{1,0:T(8,128)(2,1)} collective-permute-done((bf16[272,512]{1,0:T(8,128)(2,1)S(1)}, bf16[272,512]{1,0:T(8,128)(2,1)}, u32[]{:S(2)}, u32[]{:S(2)}) %collective-permute-start.14) | collective-permute-done | bytes 278560 | tf_op jit(solution)/shard_map/ppermute | solution.py:657
  65.6 3.7 %collective-permute-done.20.refs_9_ = bf16[256,512]{1,0:T(8,128)(2,1)} collective-permute-done((bf16[256,512]{1,0:T(8,128)(2,1)S(1)}, bf16[256,512]{1,0:T(8,128)(2,1)}, u32[]{:S(2)}, u32[]{:S(2)}) %collective-permute-start.20) | collective-permute-done | bytes 262176 | tf_op jit(solution)/shard_map/ppermute | solution.py:657
  71.3 3.2 %collective-permute-done.18.refs_12_ = bf16[272,512]{1,0:T(8,128)(2,1)} collective-permute-done((bf16[272,512]{1,0:T(8,128)(2,1)}, bf16[272,512]{1,0:T(8,128)(2,1)}, u32[]{:S(2)}, u32[]{:S(2)}) %collective-permute-start.18) | collective-permute-done | bytes 278560 | tf_op jit(solution)/shard_map/ppermute | solution.py:657
  75.7 4.8 %collective-permute-done.23.refs_13_ = bf16[256,512]{1,0:T(8,128)(2,1)} collective-permute-done((bf16[256,512]{1,0:T(8,128)(2,1)}, bf16[256,512]{1,0:T(8,128)(2,1)}, u32[]{:S(2)}, u32[]{:S(2)}) %collective-permute-start.23) | collective-permute-done | bytes 262176 | tf_op jit(solution)/shard_map/ppermute | solution.py:657
  97.7 8.9 %qkv_step.1 = (bf16[6,512,256]{2,1,0:T(8,128)(2,1)S(1)}, f32[6,512,256]{2,1,0:T(8,128)S(1)}, f32[512,128]{1,0:T(8,128)S(1)}) custom-call(s32[16]{0:T(128)S(1)} %concatenate.68.meta, bf16[272,512]{1,0:T(8,128)(2,1)S(1)} %copy-done.13, bf16[256,512]{1,0:T(8,128)(2,1)S(1)} %copy-done.15, bf16[272,512]{1,0:T(8,128)(2,1)S(1)} %copy-done.21, ...), custom_call_target="tpu_custom_call" | custom-call | flops 5637144576 | bytes 20971520 | tf_op jit(solution)/shard_map/qkv_step/pallas_call | solution.py:321
  106.6 2.7 %qkv_last.1 = (bf16[2,512,128]{2,1,0:T(8,128)(2,1)}, bf16[2,512,128]{2,1,0:T(8,128)(2,1)}, bf16[512,128]{1,0:T(8,128)(2,1)}, bf16[512,128]{1,0:T(8,128)(2,1)}, b...) custom-call(s32[16]{0:T(128)S(1)} %concatenate.68.meta, ...), custom_call_target="tpu_custom_call" | custom-call | flops 805306368 | bytes 8388608 | tf_op jit(solution)/shard_map/qkv_last/pallas_call | solution.py:321
  109.4 3.7 %collective-permute-start.28 = (bf16[2,512,128]{2,1,0:T(8,128)(2,1)}, bf16[2,512,128]{2,1,0:T(8,128)(2,1)S(1)}, u32[]{:S(2)}, u32[]{:S(2)}) collective-permute-start(bf16[2,512,128]{2,1,0:T(8,128)(2,1)} %get-tuple-element.198), channel_id=1, source_target_pairs={{0,1},{1,0},{2,3},{3,2},{4,5},{5,4},{6,7},{7,6},{8,9},{9,8},{10,11... | collective-permute-start | bytes 786440 | tf_op jit(solution)/shard_map/ppermute | solution.py:54
  115.4 2.6 collective-permute-start.31
  120.7 9.2 %collective-permute-done.31 = bf16[2,256,256]{2,1,0:T(8,128)(2,1)S(1)} collective-permute-done((bf16[2,256,256]{2,1,0:T(8,128)(2,1)S(1)}, bf16[2,256,256]{2,1,0:T(8,128)(2,1)S(1)}, u32[]{:S(2)}, u32[]{:S(2)}) %collective-permute-start.31) | collective-permute-done | bytes 262176 | tf_op jit(solution)/shard_map/ppermute | solution.py:657
  134.8 4.5 %attention.2 = (bf16[512,128]{1,0:T(8,128)(2,1)S(1)}, bf16[512,128]{1,0:T(8,128)(2,1)S(1)}) custom-call(s32[16]{0:T(128)S(1)} %concatenate.68.meta, bf16[512,128]{1,0:T(8,128)(2,1)S(1)} %copy-done.33, bf16[512,128]{1,0:T(8,128)(2,1)S(1)} %collective-permute-done.27.refs_1_, bf16[2,512,128]{2,1,0:T(8,128)(2,1)S(1)} %copy-done.31, ...), custom_call_target="tpu_custom_call" | custom-call | flops 1073741824 | bytes 1048576 | tf_op jit(solution)/shard_map/attention/pallas_call | solution.py:381
  140.4 6.3 %collective-permute-done.34.refs_4_ = bf16[2,512,128]{2,1,0:T(8,128)(2,1)S(1)} collective-permute-done((bf16[2,512,128]{2,1,0:T(8,128)(2,1)S(1)}, bf16[2,512,128]{2,1,0:T(8,128)(2,1)S(1)}, u32[]{:S(2)}, u32[]{:S(2)}) %collective-permute-start.34) | collective-permute-done | bytes 262176 | tf_op jit(solution)/shard_map/ppermute | solution.py:808
  146.7 4.5 %attention.3 = (bf16[512,128]{1,0:T(8,128)(2,1)S(1)}, bf16[512,128]{1,0:T(8,128)(2,1)S(1)}) custom-call(s32[16]{0:T(128)S(1)} %concatenate.68.meta, bf16[512,128]{1,0:T(8,128)(2,1)S(1)} %copy-done.32, bf16[512,128]{1,0:T(8,128)(2,1)S(1)} %collective-permute-done.32.refs_1_, bf16[2,512,128]{2,1,0:T(8,128)(2,1)S(1)} %copy-done.30, ...), custom_call_target="tpu_custom_call" | custom-call | flops 1073741824 | bytes 1048576 | tf_op jit(solution)/shard_map/attention/pallas_call | solution.py:381
  155.2 7.7 %collective-permute-done.40.refs_4_ = bf16[256,512]{1,0:T(8,128)(2,1)S(1)} collective-permute-done((bf16[256,512]{1,0:T(8,128)(2,1)S(1)}, bf16[256,512]{1,0:T(8,128)(2,1)S(1)}, u32[]{:S(2)}, u32[]{:S(2)}) %collective-permute-start.40) | collective-permute-done | bytes 262176 | tf_op jit(solution)/shard_map/ppermute | solution.py:657
  168.7 5.4 %collective-permute-done.42.refs_8_ = bf16[256,512]{1,0:T(8,128)(2,1)S(1)} collective-permute-done((bf16[256,512]{1,0:T(8,128)(2,1)S(1)}, bf16[256,512]{1,0:T(8,128)(2,1)S(1)}, u32[]{:S(2)}, u32[]{:S(2)}) %collective-permute-start.42) | collective-permute-done | bytes 262176 | tf_op jit(solution)/shard_map/ppermute | solution.py:657
  175.3 4.1 %collective-permute-done.48.refs_9_ = bf16[256,512]{1,0:T(8,128)(2,1)S(1)} collective-permute-done((bf16[256,512]{1,0:T(8,128)(2,1)S(1)}, bf16[256,512]{1,0:T(8,128)(2,1)S(1)}, u32[]{:S(2)}, u32[]{:S(2)}) %collective-permute-start.48) | collective-permute-done | bytes 262176 | tf_op jit(solution)/shard_map/ppermute | solution.py:657
  180.6 3.5 %collective-permute-done.46.refs_12_ = bf16[256,512]{1,0:T(8,128)(2,1)S(1)} collective-permute-done((bf16[256,512]{1,0:T(8,128)(2,1)S(1)}, bf16[256,512]{1,0:T(8,128)(2,1)S(1)}, u32[]{:S(2)}, u32[]{:S(2)}) %collective-permute-start.46) | collective-permute-done | bytes 262176 | tf_op jit(solution)/shard_map/ppermute | solution.py:657
  186.2 3.2 %collective-permute-done.51.refs_13_ = bf16[256,512]{1,0:T(8,128)(2,1)S(1)} collective-permute-done((bf16[256,512]{1,0:T(8,128)(2,1)S(1)}, bf16[256,512]{1,0:T(8,128)(2,1)S(1)}, u32[]{:S(2)}, u32[]{:S(2)}) %collective-permute-start.51) | collective-permute-done | bytes 262176 | tf_op jit(solution)/shard_map/ppermute | solution.py:657
  192.0 4.0 %out_step.1.refs_4_ = f32[2,512,256]{2,1,0:T(8,128)S(1)} custom-call(s32[16]{0:T(128)S(1)} %concatenate.68.meta, bf16[256,512]{1,0:T(8,128)(2,1)S(1)} %get-tuple-element.219.refs_0_, bf16[256,512]{1,0:T(8,128)(2,1)S(1)} %get-tuple-element.221.refs_1_, bf16[256,512]{1,0:T(8,128)(2,1)S(1)} %collective-permute-done.41.refs_2_, ...), custom_call_target="tpu_custom_call" | custom-call | flops 1879048192 | bytes 9437184 | tf_op jit(solution)/shard_map/out_step/pallas_call | solution.py:438
  198.0 4.2 %collective-permute-start.57 = (bf16[8,256,256]{2,1,0:T(8,128)(2,1)S(1)}, bf16[8,256,256]{2,1,0:T(8,128)(2,1)S(1)}, u32[]{:S(2)}, u32[]{:S(2)}) collective-permute-start(bf16[8,256,256]{2,1,0:T(8,128)(2,1)S(1)} %collective-permute-done.55.refs_16_.refs_20_.refs_24_.refs_28_.refs_32_.refs_36_.refs_40_.refs_4_), channel_id=1, source_target_pairs={{0,1},{1,0},{2,3},{3,2},{4,5},{5,4},{6,7},{7,6},{8,9},{9,8},{10,11... | collective-permute-start | bytes 3145736 | tf_op jit(solution)/shard_map/ppermute | solution.py:54
  209.9 3.1 %collective-permute-done.58.refs_1_ = bf16[256,256]{1,0:T(8,128)(2,1)S(1)} collective-permute-done((bf16[256,256]{1,0:T(8,128)(2,1)S(1)}, bf16[256,256]{1,0:T(8,128)(2,1)S(1)}, u32[]{:S(2)}, u32[]{:S(2)}) %collective-permute-start.58) | collective-permute-done | bytes 131104 | tf_op jit(solution)/shard_map/ppermute | solution.py:808
  213.0 3.1 %collective-permute-done.60.refs_3_ = bf16[256,256]{1,0:T(8,128)(2,1)S(1)} collective-permute-done((bf16[256,256]{1,0:T(8,128)(2,1)S(1)}, bf16[256,256]{1,0:T(8,128)(2,1)S(1)}, u32[]{:S(2)}, u32[]{:S(2)}) %collective-permute-start.60) | collective-permute-done | bytes 131104 | tf_op jit(solution)/shard_map/ppermute | solution.py:808
  217.8 5.3 %collective-permute-done.61.refs_4_ = bf16[128,512]{1,0:T(8,128)(2,1)} collective-permute-done((bf16[128,512]{1,0:T(8,128)(2,1)S(1)}, bf16[128,512]{1,0:T(8,128)(2,1)}, u32[]{:S(2)}, u32[]{:S(2)}) %collective-permute-start.61) | collective-permute-done | bytes 131104 | tf_op jit(solution)/shard_map/ppermute | solution.py:657
  223.1 2.8 %collective-permute-done.65.refs_5_ = bf16[128,512]{1,0:T(8,128)(2,1)} collective-permute-done((bf16[128,512]{1,0:T(8,128)(2,1)S(1)}, bf16[128,512]{1,0:T(8,128)(2,1)}, u32[]{:S(2)}, u32[]{:S(2)}) %collective-permute-start.65) | collective-permute-done | bytes 131104 | tf_op jit(solution)/shard_map/ppermute | solution.py:657
  227.6 7.1 %collective-permute-done.63.refs_8_ = bf16[128,512]{1,0:T(8,128)(2,1)S(1)} collective-permute-done((bf16[128,512]{1,0:T(8,128)(2,1)}, bf16[128,512]{1,0:T(8,128)(2,1)S(1)}, u32[]{:S(2)}, u32[]{:S(2)}) %collective-permute-start.63) | collective-permute-done | bytes 131104 | tf_op jit(solution)/shard_map/ppermute | solution.py:657
  236.8 5.7 %collective-permute-done.67.refs_12_ = bf16[128,512]{1,0:T(8,128)(2,1)S(1)} collective-permute-done((bf16[128,512]{1,0:T(8,128)(2,1)S(1)}, bf16[128,512]{1,0:T(8,128)(2,1)S(1)}, u32[]{:S(2)}, u32[]{:S(2)}) %collective-permute-start.67) | collective-permute-done | bytes 131104 | tf_op jit(solution)/shard_map/ppermute | solution.py:657
  246.7 2.7 %collective-permute-done.74.refs_1_ = bf16[128,512]{1,0:T(8,128)(2,1)S(1)} collective-permute-done((bf16[128,512]{1,0:T(8,128)(2,1)S(1)}, bf16[128,512]{1,0:T(8,128)(2,1)S(1)}, u32[]{:S(2)}, u32[]{:S(2)}) %collective-permute-start.74) | collective-permute-done | bytes 131104 | tf_op jit(solution)/shard_map/ppermute | solution.py:657
  255.8 5.9 %collective-permute-start.79 = (f32[64,128]{1,0:T(8,128)S(1)}, f32[64,128]{1,0:T(8,128)S(1)}, u32[]{:S(2)}, u32[]{:S(2)}) collective-permute-start(f32[64,128]{1,0:T(8,128)S(1)} %fusion.25.own_a), channel_id=1, source_target_pairs={{0,1},{1,0},{2,3},{3,2},{4,5},{5,4},{6,7},{7,6},{8,9},{9,8},{10,11... | collective-permute-start | bytes 98312 | tf_op jit(solution)/shard_map/ppermute | solution.py:872
  (290 shorter events, 113.1 us)
Async XLA Ops:
  1.2 20.3 %collective-permute-start.8 = (bf16[4096,256]{1,0:T(8,128)(2,1)}, bf16[4096,256]{1,0:T(8,128)(2,1)}, u32[]{:S(2)}, u32[]{:S(2)}) collective-permute-start(bf16[4096,256]{1,0:T(8,128)(2,1)} %refs_13_.1), channel_id=1, source_target_pairs={{0,1},{1,0},{2,3},{3,2},{4,5},{5,4},{6,7},{7,6},{8,9},{9,8},{10,11... | collective-permute-start | bytes 6291464 | tf_op jit(solution)/shard_map/ppermute | solution.py:54
  19.3 21.7 %collective-permute-start.9 = (bf16[4,256,256]{2,1,0:T(8,128)(2,1)}, bf16[4,256,256]{2,1,0:T(8,128)(2,1)}, u32[]{:S(2)}, u32[]{:S(2)}) collective-permute-start(bf16[4,256,256]{2,1,0:T(8,128)(2,1)} %get-tuple-element.152), channel_id=1, source_target_pairs={{0,2},{2,0},{1,3},{3,1},{4,6},{6,4},{5,7},{7,5},{8,10},{10,8},{9,1... | collective-permute-start | bytes 1572872 | tf_op jit(solution)/shard_map/ppermute | solution.py:657
  19.7 87.0 %collective-permute-start.26 = (bf16[4096,256]{1,0:T(8,128)(2,1)S(1)}, bf16[4096,256]{1,0:T(8,128)(2,1)}, u32[]{:S(2)}, u32[]{:S(2)}) collective-permute-start(bf16[4096,256]{1,0:T(8,128)(2,1)S(1)} %copy-done.1), channel_id=1, source_target_pairs={{0,1},{1,0},{2,3},{3,2},{4,5},{5,4},{6,7},{7,6},{8,9},{9,8},{10,11... | collective-permute-start | bytes 6291464 | tf_op jit(solution)/shard_map/ppermute | solution.py:54
  44.5 13.7 %collective-permute-start.16 = (bf16[256,512]{1,0:T(8,128)(2,1)S(1)}, bf16[256,512]{1,0:T(8,128)(2,1)S(1)}, u32[]{:S(2)}, u32[]{:S(2)}) collective-permute-start(bf16[256,512]{1,0:T(8,128)(2,1)S(1)} %maximum_select_fusion.2.refs_1_), channel_id=1, source_target_pairs={{0,4},{4,8},{8,12},{12,0},{1,5},{5,9},{9,13},{13,1},{2,6},{6,10},{... | collective-permute-start | bytes 786440 | tf_op jit(solution)/shard_map/ppermute | solution.py:657
  44.7 13.5 %collective-permute-start.17 = (bf16[256,512]{1,0:T(8,128)(2,1)S(1)}, bf16[256,512]{1,0:T(8,128)(2,1)S(1)}, u32[]{:S(2)}, u32[]{:S(2)}) collective-permute-start(bf16[256,512]{1,0:T(8,128)(2,1)S(1)} %maximum_select_fusion.2.refs_1_), channel_id=1, source_target_pairs={{0,2},{2,0},{1,3},{3,1},{4,6},{6,4},{5,7},{7,5},{8,10},{10,8},{9,1... | collective-permute-start | bytes 786440 | tf_op jit(solution)/shard_map/ppermute | solution.py:657
  53.3 10.5 %collective-permute-start.14 = (bf16[272,512]{1,0:T(8,128)(2,1)S(1)}, bf16[272,512]{1,0:T(8,128)(2,1)}, u32[]{:S(2)}, u32[]{:S(2)}) collective-permute-start(bf16[272,512]{1,0:T(8,128)(2,1)S(1)} %collective-permute-done.12.refs_4_), channel_id=1, source_target_pairs={{0,4},{4,8},{8,12},{12,0},{1,5},{5,9},{9,13},{13,1},{2,6},{6,10},{... | collective-permute-start | bytes 835592 | tf_op jit(solution)/shard_map/ppermute | solution.py:657
  53.3 10.5 %collective-permute-start.15 = (bf16[272,512]{1,0:T(8,128)(2,1)S(1)}, bf16[272,512]{1,0:T(8,128)(2,1)S(1)}, u32[]{:S(2)}, u32[]{:S(2)}) collective-permute-start(bf16[272,512]{1,0:T(8,128)(2,1)S(1)} %collective-permute-done.12.refs_4_), channel_id=1, source_target_pairs={{0,2},{2,0},{1,3},{3,1},{4,6},{6,4},{5,7},{7,5},{8,10},{10,8},{9,1... | collective-permute-start | bytes 835592 | tf_op jit(solution)/shard_map/ppermute | solution.py:657
  58.9 10.5 %collective-permute-start.20 = (bf16[256,512]{1,0:T(8,128)(2,1)S(1)}, bf16[256,512]{1,0:T(8,128)(2,1)}, u32[]{:S(2)}, u32[]{:S(2)}) collective-permute-start(bf16[256,512]{1,0:T(8,128)(2,1)S(1)} %collective-permute-done.16.refs_5_), channel_id=1, source_target_pairs={{0,4},{4,8},{8,12},{12,0},{1,5},{5,9},{9,13},{13,1},{2,6},{6,10},{... | collective-permute-start | bytes 786440 | tf_op jit(solution)/shard_map/ppermute | solution.py:657
  58.9 10.5 %collective-permute-start.21 = (bf16[256,512]{1,0:T(8,128)(2,1)S(1)}, bf16[256,512]{1,0:T(8,128)(2,1)S(1)}, u32[]{:S(2)}, u32[]{:S(2)}) collective-permute-start(bf16[256,512]{1,0:T(8,128)(2,1)S(1)} %collective-permute-done.16.refs_5_), channel_id=1, source_target_pairs={{0,2},{2,0},{1,3},{3,1},{4,6},{6,4},{5,7},{7,5},{8,10},{10,8},{9,1... | collective-permute-start | bytes 786440 | tf_op jit(solution)/shard_map/ppermute | solution.py:657
  64.5 10.0 %collective-permute-start.18 = (bf16[272,512]{1,0:T(8,128)(2,1)}, bf16[272,512]{1,0:T(8,128)(2,1)}, u32[]{:S(2)}, u32[]{:S(2)}) collective-permute-start(bf16[272,512]{1,0:T(8,128)(2,1)} %collective-permute-done.14.refs_8_), channel_id=1, source_target_pairs={{0,4},{4,8},{8,12},{12,0},{1,5},{5,9},{9,13},{13,1},{2,6},{6,10},{... | collective-permute-start | bytes 835592 | tf_op jit(solution)/shard_map/ppermute | solution.py:657
  64.5 10.0 %collective-permute-start.19 = (bf16[272,512]{1,0:T(8,128)(2,1)}, bf16[272,512]{1,0:T(8,128)(2,1)}, u32[]{:S(2)}, u32[]{:S(2)}) collective-permute-start(bf16[272,512]{1,0:T(8,128)(2,1)} %collective-permute-done.14.refs_8_), channel_id=1, source_target_pairs={{0,2},{2,0},{1,3},{3,1},{4,6},{6,4},{5,7},{7,5},{8,10},{10,8},{9,1... | collective-permute-start | bytes 835592 | tf_op jit(solution)/shard_map/ppermute | solution.py:657
  70.1 10.4 %collective-permute-start.23 = (bf16[256,512]{1,0:T(8,128)(2,1)}, bf16[256,512]{1,0:T(8,128)(2,1)}, u32[]{:S(2)}, u32[]{:S(2)}) collective-permute-start(bf16[256,512]{1,0:T(8,128)(2,1)} %collective-permute-done.20.refs_9_), channel_id=1, source_target_pairs={{0,4},{4,8},{8,12},{12,0},{1,5},{5,9},{9,13},{13,1},{2,6},{6,10},{... | collective-permute-start | bytes 786440 | tf_op jit(solution)/shard_map/ppermute | solution.py:657
  70.1 10.4 %collective-permute-start.24 = (bf16[256,512]{1,0:T(8,128)(2,1)}, bf16[256,512]{1,0:T(8,128)(2,1)}, u32[]{:S(2)}, u32[]{:S(2)}) collective-permute-start(bf16[256,512]{1,0:T(8,128)(2,1)} %collective-permute-done.20.refs_9_), channel_id=1, source_target_pairs={{0,2},{2,0},{1,3},{3,1},{4,6},{6,4},{5,7},{7,5},{8,10},{10,8},{9,1... | collective-permute-start | bytes 786440 | tf_op jit(solution)/shard_map/ppermute | solution.py:657
  74.5 32.1 %collective-permute-start.22 = (bf16[272,512]{1,0:T(8,128)(2,1)}, bf16[272,512]{1,0:T(8,128)(2,1)S(1)}, u32[]{:S(2)}, u32[]{:S(2)}) collective-permute-start(bf16[272,512]{1,0:T(8,128)(2,1)} %collective-permute-done.18.refs_12_), channel_id=1, source_target_pairs={{0,2},{2,0},{1,3},{3,1},{4,6},{6,4},{5,7},{7,5},{8,10},{10,8},{9,1... | collective-permute-start | bytes 835592 | tf_op jit(solution)/shard_map/ppermute | solution.py:657
  80.5 26.1 %collective-permute-start.25 = (bf16[256,512]{1,0:T(8,128)(2,1)}, bf16[256,512]{1,0:T(8,128)(2,1)S(1)}, u32[]{:S(2)}, u32[]{:S(2)}) collective-permute-start(bf16[256,512]{1,0:T(8,128)(2,1)} %collective-permute-done.24.refs_11_), channel_id=1, source_target_pairs={{0,4},{4,8},{8,12},{12,0},{1,5},{5,9},{9,13},{13,1},{2,6},{6,10},{... | collective-permute-start | bytes 786440 | tf_op jit(solution)/shard_map/ppermute | solution.py:657
  109.4 22.5 %collective-permute-start.28 = (bf16[2,512,128]{2,1,0:T(8,128)(2,1)}, bf16[2,512,128]{2,1,0:T(8,128)(2,1)S(1)}, u32[]{:S(2)}, u32[]{:S(2)}) collective-permute-start(bf16[2,512,128]{2,1,0:T(8,128)(2,1)} %get-tuple-element.198), channel_id=1, source_target_pairs={{0,1},{1,0},{2,3},{3,2},{4,5},{5,4},{6,7},{7,6},{8,9},{9,8},{10,11... | collective-permute-start | bytes 786440 | tf_op jit(solution)/shard_map/ppermute | solution.py:54
  113.0 20.6 %collective-permute-start.30 = (bf16[2,512,128]{2,1,0:T(8,128)(2,1)}, bf16[2,512,128]{2,1,0:T(8,128)(2,1)S(1)}, u32[]{:S(2)}, u32[]{:S(2)}) collective-permute-start(bf16[2,512,128]{2,1,0:T(8,128)(2,1)} %get-tuple-element.198), channel_id=1, source_target_pairs={{0,17},{1,16},{16,1},{17,0},{2,19},{3,18},{18,3},{19,2},{4,21},{5,... | collective-permute-start | bytes 786440 | tf_op jit(solution)/shard_map/ppermute | solution.py:808
  115.4 14.5 %collective-permute-start.31 = (bf16[2,256,256]{2,1,0:T(8,128)(2,1)S(1)}, bf16[2,256,256]{2,1,0:T(8,128)(2,1)S(1)}, u32[]{:S(2)}, u32[]{:S(2)}) collective-permute-start(bf16[2,256,256]{2,1,0:T(8,128)(2,1)S(1)} %pad_maximum_fusion), channel_id=1, source_target_pairs={{0,8},{4,12},{8,0},{12,4},{1,9},{5,13},{9,1},{13,5},{2,10},{6,14},... | collective-permute-start | bytes 786440 | tf_op jit(solution)/shard_map/ppermute | solution.py:657
  118.1 15.3 %collective-permute-start.29 = (bf16[2,512,128]{2,1,0:T(8,128)(2,1)S(1)}, bf16[2,512,128]{2,1,0:T(8,128)(2,1)S(1)}, u32[]{:S(2)}, u32[]{:S(2)}) collective-permute-start(bf16[2,512,128]{2,1,0:T(8,128)(2,1)S(1)} %copy-done.31), channel_id=1, source_target_pairs={{0,16},{1,17},{16,0},{17,1},{2,18},{3,19},{18,2},{19,3},{4,20},{5,... | collective-permute-start | bytes 786440 | tf_op jit(solution)/shard_map/ppermute | solution.py:808
  120.3 19.0 %collective-permute-start.32 = (bf16[512,128]{1,0:T(8,128)(2,1)S(1)}, bf16[512,128]{1,0:T(8,128)(2,1)S(1)}, u32[]{:S(2)}, u32[]{:S(2)}) collective-permute-start(bf16[512,128]{1,0:T(8,128)(2,1)S(1)} %copy-done.50), channel_id=1, source_target_pairs={{0,1},{1,0},{2,3},{3,2},{4,5},{5,4},{6,7},{7,6},{8,9},{9,8},{10,11... | collective-permute-start | bytes 393224 | tf_op jit(solution)/shard_map/ppermute | solution.py:54
  129.9 23.6 %collective-permute-start.39 = (bf16[2,256,256]{2,1,0:T(8,128)(2,1)S(1)}, bf16[2,256,256]{2,1,0:T(8,128)(2,1)S(1)}, u32[]{:S(2)}, u32[]{:S(2)}) collective-permute-start(bf16[2,256,256]{2,1,0:T(8,128)(2,1)S(1)} %pad_maximum_fusion.3), channel_id=1, source_target_pairs={{0,12},{4,0},{8,4},{12,8},{1,13},{5,1},{9,5},{13,9},{2,14},{6,2},{... | collective-permute-start | bytes 786440 | tf_op jit(solution)/shard_map/ppermute | solution.py:657
  133.4 13.3 %collective-permute-start.35 = (bf16[2,512,128]{2,1,0:T(8,128)(2,1)S(1)}, bf16[2,512,128]{2,1,0:T(8,128)(2,1)S(1)}, u32[]{:S(2)}, u32[]{:S(2)}) collective-permute-start(bf16[2,512,128]{2,1,0:T(8,128)(2,1)S(1)} %copy-done.49), channel_id=1, source_target_pairs={{0,17},{1,16},{16,1},{17,0},{2,19},{3,18},{18,3},{19,2},{4,21},{5,... | collective-permute-start | bytes 786440 | tf_op jit(solution)/shard_map/ppermute | solution.py:808
  133.6 13.1 %collective-permute-start.34 = (bf16[2,512,128]{2,1,0:T(8,128)(2,1)S(1)}, bf16[2,512,128]{2,1,0:T(8,128)(2,1)S(1)}, u32[]{:S(2)}, u32[]{:S(2)}) collective-permute-start(bf16[2,512,128]{2,1,0:T(8,128)(2,1)S(1)} %copy-done.30), channel_id=1, source_target_pairs={{0,16},{1,17},{16,0},{17,1},{2,18},{3,19},{18,2},{19,3},{4,20},{5,... | collective-permute-start | bytes 786440 | tf_op jit(solution)/shard_map/ppermute | solution.py:808
  139.3 14.2 %collective-permute-start.38 = (bf16[2,256,256]{2,1,0:T(8,128)(2,1)S(1)}, bf16[2,256,256]{2,1,0:T(8,128)(2,1)S(1)}, u32[]{:S(2)}, u32[]{:S(2)}) collective-permute-start(bf16[2,256,256]{2,1,0:T(8,128)(2,1)S(1)} %pad_maximum_fusion.2), channel_id=1, source_target_pairs={{0,4},{4,8},{8,12},{12,0},{1,5},{5,9},{9,13},{13,1},{2,6},{6,10},{... | collective-permute-start | bytes 786440 | tf_op jit(solution)/shard_map/ppermute | solution.py:657
  139.6 12.7 %collective-permute-start.36 = (bf16[512,128]{1,0:T(8,128)(2,1)S(1)}, bf16[512,128]{1,0:T(8,128)(2,1)S(1)}, u32[]{:S(2)}, u32[]{:S(2)}) collective-permute-start(bf16[512,128]{1,0:T(8,128)(2,1)S(1)} %get-tuple-element.216), channel_id=1, source_target_pairs={{0,1},{1,0},{2,3},{3,2},{4,5},{5,4},{6,7},{7,6},{8,9},{9,8},{10,11... | collective-permute-start | bytes 393224 | tf_op jit(solution)/shard_map/ppermute | solution.py:54
  154.8 13.7 %collective-permute-start.44 = (bf16[256,512]{1,0:T(8,128)(2,1)S(1)}, bf16[256,512]{1,0:T(8,128)(2,1)S(1)}, u32[]{:S(2)}, u32[]{:S(2)}) collective-permute-start(bf16[256,512]{1,0:T(8,128)(2,1)S(1)} %get-tuple-element.221.refs_1_), channel_id=1, source_target_pairs={{0,4},{4,8},{8,12},{12,0},{1,5},{5,9},{9,13},{13,1},{2,6},{6,10},{... | collective-permute-start | bytes 786440 | tf_op jit(solution)/shard_map/ppermute | solution.py:657
  154.8 13.9 %collective-permute-start.45 = (bf16[256,512]{1,0:T(8,128)(2,1)S(1)}, bf16[256,512]{1,0:T(8,128)(2,1)S(1)}, u32[]{:S(2)}, u32[]{:S(2)}) collective-permute-start(bf16[256,512]{1,0:T(8,128)(2,1)S(1)} %get-tuple-element.221.refs_1_), channel_id=1, source_target_pairs={{0,2},{2,0},{1,3},{3,1},{4,6},{6,4},{5,7},{7,5},{8,10},{10,8},{9,1... | collective-permute-start | bytes 786440 | tf_op jit(solution)/shard_map/ppermute | solution.py:657
  162.9 11.2 %collective-permute-start.42 = (bf16[256,512]{1,0:T(8,128)(2,1)S(1)}, bf16[256,512]{1,0:T(8,128)(2,1)S(1)}, u32[]{:S(2)}, u32[]{:S(2)}) collective-permute-start(bf16[256,512]{1,0:T(8,128)(2,1)S(1)} %collective-permute-done.40.refs_4_), channel_id=1, source_target_pairs={{0,4},{4,8},{8,12},{12,0},{1,5},{5,9},{9,13},{13,1},{2,6},{6,10},{... | collective-permute-start | bytes 786440 | tf_op jit(solution)/shard_map/ppermute | solution.py:657
  162.9 12.4 %collective-permute-start.43 = (bf16[256,512]{1,0:T(8,128)(2,1)S(1)}, bf16[256,512]{1,0:T(8,128)(2,1)S(1)}, u32[]{:S(2)}, u32[]{:S(2)}) collective-permute-start(bf16[256,512]{1,0:T(8,128)(2,1)S(1)} %collective-permute-done.40.refs_4_), channel_id=1, source_target_pairs={{0,2},{2,0},{1,3},{3,1},{4,6},{6,4},{5,7},{7,5},{8,10},{10,8},{9,1... | collective-permute-start | bytes 786440 | tf_op jit(solution)/shard_map/ppermute | solution.py:657
  164.1 32.0 %collective-permute-start.54 = (bf16[8,256,256]{2,1,0:T(8,128)(2,1)S(1)}, bf16[8,256,256]{2,1,0:T(8,128)(2,1)S(1)}, u32[]{:S(2)}, u32[]{:S(2)}) collective-permute-start(bf16[8,256,256]{2,1,0:T(8,128)(2,1)S(1)} %constant_dynamic-update-slice_fusion.refs_14_.refs_18_.refs_22_.refs_26_.refs_30_.refs_34_.refs_38, ...), channel_id=1, source_target_pairs={{0,1},{1,0},{2,3},{3,2},{4,5},{5,4},{6,7},{7,6},{8,9},{9,8},{10,11... | collective-permute-start | bytes 3145736 | tf_op jit(solution)/shard_map/ppermute | solution.py:54
  168.5 28.6 %collective-permute-start.55 = (bf16[8,256,256]{2,1,0:T(8,128)(2,1)S(1)}, bf16[8,256,256]{2,1,0:T(8,128)(2,1)S(1)}, u32[]{:S(2)}, u32[]{:S(2)}) collective-permute-start(bf16[8,256,256]{2,1,0:T(8,128)(2,1)S(1)} %constant_dynamic-update-slice_fusion.refs_14_.refs_18_.refs_22_.refs_26_.refs_30_.refs_34_.refs_38, ...), channel_id=1, source_target_pairs={{0,16},{16,0},{1,17},{17,1},{2,18},{18,2},{3,19},{19,3},{4,20},{20... | collective-permute-start | bytes 3145736 | tf_op jit(solution)/shard_map/ppermute | solution.py:657
  168.7 10.7 %collective-permute-start.48 = (bf16[256,512]{1,0:T(8,128)(2,1)S(1)}, bf16[256,512]{1,0:T(8,128)(2,1)S(1)}, u32[]{:S(2)}, u32[]{:S(2)}) collective-permute-start(bf16[256,512]{1,0:T(8,128)(2,1)S(1)} %collective-permute-done.44.refs_5_), channel_id=1, source_target_pairs={{0,4},{4,8},{8,12},{12,0},{1,5},{5,9},{9,13},{13,1},{2,6},{6,10},{... | collective-permute-start | bytes 786440 | tf_op jit(solution)/shard_map/ppermute | solution.py:657
  (102 other events, 1125.1 us)

commit v14 on v12

--- a/solution.py
+++ b/solution.py
@@ -241,7 +241,7 @@
         weights_ref, acc_in, square_in, head_gains = [refs.pop(0) for _ in range(4)]
     else:
         weight_refs = [refs.pop(0) for _ in range(6)]
-    half, span = scaled_ref.shape
+    half, span = scaled_ref.shape[1:]
     width = weights_ref.shape[2] if last else weight_refs[0].shape[1]
     heads = width // HD
     square = square_in[...] if last else None
@@ -254,22 +254,23 @@
         gain = x_refs[index][0][half // 2 :, :][:1]
         for part in range(2):
             at = slice(part * half // 2, (part + 1) * half // 2)
-            scaled_ref[at, :] = (x_refs[index][part][: half // 2, :] * gain).astype(BF16)
+            scaled_ref[index, at, :] = (x_refs[index][part][: half // 2, :] * gain).astype(BF16)
         value = jnp.concatenate([x_refs[index][0][: half // 2, :], x_refs[index][1][...]], axis=0)
         value = value.astype(F32)
         value = value * value
         for part in range(span // HD):
             piece = value[:, part * HD : (part + 1) * HD]
             square = piece if square is None else square + piece
-        for part in range(6):
-            if last:
-                acc[part] = acc_in[part] + mxu(scaled_ref[...], weights_ref[part])
-                continue
-            term = mxu(scaled_ref[...], weight_refs[part][rows, :])
-            if index == 0:
-                acc_out[part] = term
-            else:
-                acc_out[part] += term
+    for part in range(6):
+        if last:
+            acc[part] = acc_in[part] + mxu(scaled_ref[0], weights_ref[part])
+            continue
+        total = None
+        for index in range(count):
+            rows = pl.ds(pl.multiple_of(chip_of(meta, *layout, entries[index]) * span, span), span)
+            term = mxu(scaled_ref[index], weight_refs[part][rows, :])
+            total = term if total is None else total + term
+        acc_out[part] = total
     if not last:
         square_out[...] = square
         rows = pl.ds(pl.multiple_of(chip_of(meta, *layout, len(entries)) * span, span), span)
@@ -303,7 +304,7 @@
     groups = layout[1] * layout[2]
     inputs = [p for pieces in blocks for p in pieces]
     specs = [full(p.shape) for pieces in blocks for p in pieces]
-    scratch = [pltpu.VMEM((half, span), BF16)]
+    scratch = [pltpu.VMEM((count, half, span), BF16)]
     if last:
         specs += [HELD] * 3 + [full(head_gains.shape)]
         inputs += list(state) + [head_gains]

time: 239 us -> 239 us (level)
  no operation moved by 1% of the time
where the time goes in v14:
time: 239 us; the launch traced here: 238 us
  waiting for transfers between devices  117 us (49%)
  starting transfers between devices  61.6 us (26%)
  Pallas kernels  46.7 us (20%)
  local copies, waits for them, and re-layouts  6.33 us (3%)
  other arithmetic  4.52 us (2%)
    ppermute x55, waiting for transfers between devices, shift(): lax.ppermute(values, axis, [(i, (i + step) % count) for i in range(count)])  93.8 us
    ppermute x55, starting transfers between devices, shift(): lax.ppermute(values, axis, [(i, (i + step) % count) for i in range(count)])  33.9 us
    ppermute x6, waiting for transfers between devices, shifted(): return lax.ppermute(values, ('ctx', 'core'), pairs)  16.9 us
    ppermute x17, starting transfers between devices, swap(): return lax.ppermute(values, 'core', [(0, 1), (1, 0)])  14.8 us
    pallas_call x1, Pallas kernels, down_stream(): pl.pallas_call(functools.partial(down_kernel, images, tiles, half), grid_...  11.7 us
    pallas_call x2, Pallas kernels, qkv_step(): pl.pallas_call(functools.partial(qkv_kernel, entries, layout, groups, las...  10.3 us
    pallas_call x2, Pallas kernels, attention(): pl.pallas_call(functools.partial(attention_kernel, images, len(pieces), h...  8.91 us
    ppermute x3, starting transfers between devices, shards(): quad[name] = lax.ppermute(band, ('mpo', 'core'), pairs)  7.28 us
  transfers between devices with their start and end apart: 81, of which 35 were waited for; matrix products, arithmetic and copies ran while one was open for 3% of the time, Pallas kernels for 17%

profile of v14, /device:TPU:1, one launch (start us, length us, event | category | flops | bytes accessed | tf_op | source)
XLA Modules:
  0.0 238.4 jit_solution(3548503950936789766)
XLA Ops:
  1.3 2.7 %collective-permute-start = (bf16[2,16,512]{2,1,0:T(8,128)(2,1)}, bf16[2,16,512]{2,1,0:T(8,128)(2,1)S(1)}, u32[]{:S(2)}, u32[]{:S(2)}) collective-permute-start(bf16[2,16,512]{2,1,0:T(8,128)(2,1)} %param.16), channel_id=1, source_target_pairs={{0,16},{16,0},{1,17},{17,1},{2,18},{18,2},{3,19},{19,3},{4,20},{20... | collective-permute-start | bytes 98312 | tf_op jit(solution)/shard_map/ppermute | solution.py:658
  15.4 3.9 %columns.1 = (bf16[4,256,256]{2,1,0:T(8,128)(2,1)S(1)}, bf16[4,256,256]{2,1,0:T(8,128)(2,1)}) custom-call(s32[16]{0:T(128)S(1)} %concatenate.68.meta, bf16[256,4096]{1,0:T(8,128)(2,1)} %sent_in.1, bf16[256,4096]{1,0:T(8,128)(2,1)} %sent_in.1), custom_call_target="tpu_custom_call" | custom-call | flops 65536 | bytes 2097152 | tf_op jit(solution)/shard_map/columns/pallas_call | solution.py:692
  21.5 11.7 %down_stream.1 = (bf16[272,256]{1,0:T(8,128)(2,1)S(1)}, bf16[272,256]{1,0:T(8,128)(2,1)S(1)}, bf16[256,256]{1,0:T(8,128)(2,1)S(1)}, bf16[256,256]{1,0:T(8,128)(2...) custom-call(s32[16]{0:T(128)S(1)} %concatenate.68.meta, ...), custom_call_target="tpu_custom_call" | custom-call | flops 4294967296 | bytes 4194304 | tf_op jit(solution)/shard_map/down_stream/pallas_call | solution.py:185
  37.8 7.7 %collective-permute-done.12.refs_4_ = bf16[272,512]{1,0:T(8,128)(2,1)S(1)} collective-permute-done((bf16[272,512]{1,0:T(8,128)(2,1)S(1)}, bf16[272,512]{1,0:T(8,128)(2,1)S(1)}, u32[]{:S(2)}, u32[]{:S(2)}) %collective-permute-start.12) | collective-permute-done | bytes 278560 | tf_op jit(solution)/shard_map/ppermute | solution.py:658
  46.0 5.1 %collective-permute-done.16.refs_5_ = bf16[256,512]{1,0:T(8,128)(2,1)S(1)} collective-permute-done((bf16[256,512]{1,0:T(8,128)(2,1)S(1)}, bf16[256,512]{1,0:T(8,128)(2,1)S(1)}, u32[]{:S(2)}, u32[]{:S(2)}) %collective-permute-start.16) | collective-permute-done | bytes 262176 | tf_op jit(solution)/shard_map/ppermute | solution.py:658
  51.6 5.5 %collective-permute-done.14.refs_8_ = bf16[272,512]{1,0:T(8,128)(2,1)S(1)} collective-permute-done((bf16[272,512]{1,0:T(8,128)(2,1)S(1)}, bf16[272,512]{1,0:T(8,128)(2,1)S(1)}, u32[]{:S(2)}, u32[]{:S(2)}) %collective-permute-start.14) | collective-permute-done | bytes 278560 | tf_op jit(solution)/shard_map/ppermute | solution.py:658
  57.5 5.1 %collective-permute-done.20.refs_9_ = bf16[256,512]{1,0:T(8,128)(2,1)S(1)} collective-permute-done((bf16[256,512]{1,0:T(8,128)(2,1)S(1)}, bf16[256,512]{1,0:T(8,128)(2,1)S(1)}, u32[]{:S(2)}, u32[]{:S(2)}) %collective-permute-start.20) | collective-permute-done | bytes 262176 | tf_op jit(solution)/shard_map/ppermute | solution.py:658
  63.2 5.5 %collective-permute-done.18.refs_12_ = bf16[272,512]{1,0:T(8,128)(2,1)S(1)} collective-permute-done((bf16[272,512]{1,0:T(8,128)(2,1)S(1)}, bf16[272,512]{1,0:T(8,128)(2,1)S(1)}, u32[]{:S(2)}, u32[]{:S(2)}) %collective-permute-start.18) | collective-permute-done | bytes 278560 | tf_op jit(solution)/shard_map/ppermute | solution.py:658
  69.1 5.1 %collective-permute-done.23.refs_13_ = bf16[256,512]{1,0:T(8,128)(2,1)S(1)} collective-permute-done((bf16[256,512]{1,0:T(8,128)(2,1)S(1)}, bf16[256,512]{1,0:T(8,128)(2,1)S(1)}, u32[]{:S(2)}, u32[]{:S(2)}) %collective-permute-start.23) | collective-permute-done | bytes 262176 | tf_op jit(solution)/shard_map/ppermute | solution.py:658
  74.3 7.6 %qkv_step.1 = (bf16[6,512,256]{2,1,0:T(8,128)(2,1)S(1)}, f32[6,512,256]{2,1,0:T(8,128)S(1)}, f32[512,128]{1,0:T(8,128)S(1)}) custom-call(s32[16]{0:T(128)S(1)} %concatenate.68.meta, bf16[272,512]{1,0:T(8,128)(2,1)S(1)} %maximum_select_fusion.1.refs_0_, bf16[256,512]{1,0:T(8,128)(2,1)S(1)} %maximum_select_fusion.2.refs_1_, ...), custom_call_target="tpu_custom_call" | custom-call | flops 5637144576 | bytes 20971520 | tf_op jit(solution)/shard_map/qkv_step/pallas_call | solution.py:322
  82.8 2.7 %qkv_last.1 = (bf16[2,512,128]{2,1,0:T(8,128)(2,1)}, bf16[2,512,128]{2,1,0:T(8,128)(2,1)}, bf16[512,128]{1,0:T(8,128)(2,1)}, bf16[512,128]{1,0:T(8,128)(2,1)}, b...) custom-call(s32[16]{0:T(128)S(1)} %concatenate.68.meta, ...), custom_call_target="tpu_custom_call" | custom-call | flops 805306368 | bytes 8388608 | tf_op jit(solution)/shard_map/qkv_last/pallas_call | solution.py:322
  99.3 5.5 %collective-permute-done.30.refs_5_ = bf16[2,512,128]{2,1,0:T(8,128)(2,1)S(1)} collective-permute-done((bf16[2,512,128]{2,1,0:T(8,128)(2,1)}, bf16[2,512,128]{2,1,0:T(8,128)(2,1)S(1)}, u32[]{:S(2)}, u32[]{:S(2)}) %collective-permute-start.30) | collective-permute-done | bytes 262176 | tf_op jit(solution)/shard_map/ppermute | solution.py:808
  106.0 4.5 %attention.2 = (bf16[512,128]{1,0:T(8,128)(2,1)S(1)}, bf16[512,128]{1,0:T(8,128)(2,1)S(1)}) custom-call(s32[16]{0:T(128)S(1)} %concatenate.68.meta, bf16[512,128]{1,0:T(8,128)(2,1)S(1)} %copy-done.19, bf16[512,128]{1,0:T(8,128)(2,1)S(1)} %copy-done.21, bf16[2,512,128]{2,1,0:T(8,128)(2,1)S(1)} %copy-done.15, ...), custom_call_target="tpu_custom_call" | custom-call | flops 1073741824 | bytes 1048576 | tf_op jit(solution)/shard_map/attention/pallas_call | solution.py:382
  111.5 3.8 %collective-permute-done.34.refs_5_ = bf16[2,512,128]{2,1,0:T(8,128)(2,1)S(1)} collective-permute-done((bf16[2,512,128]{2,1,0:T(8,128)(2,1)S(1)}, bf16[2,512,128]{2,1,0:T(8,128)(2,1)S(1)}, u32[]{:S(2)}, u32[]{:S(2)}) %collective-permute-start.34) | collective-permute-done | bytes 262176 | tf_op jit(solution)/shard_map/ppermute | solution.py:808
  115.3 4.5 %attention.3 = (bf16[512,128]{1,0:T(8,128)(2,1)S(1)}, bf16[512,128]{1,0:T(8,128)(2,1)S(1)}) custom-call(s32[16]{0:T(128)S(1)} %concatenate.68.meta, bf16[512,128]{1,0:T(8,128)(2,1)S(1)} %copy-done.16, bf16[512,128]{1,0:T(8,128)(2,1)S(1)} %copy-done.18, bf16[2,512,128]{2,1,0:T(8,128)(2,1)S(1)} %copy-done.14, ...), custom_call_target="tpu_custom_call" | custom-call | flops 1073741824 | bytes 1048576 | tf_op jit(solution)/shard_map/attention/pallas_call | solution.py:382
  121.4 3.4 %collective-permute-done.38 = bf16[2,256,256]{2,1,0:T(8,128)(2,1)S(1)} collective-permute-done((bf16[2,256,256]{2,1,0:T(8,128)(2,1)S(1)}, bf16[2,256,256]{2,1,0:T(8,128)(2,1)S(1)}, u32[]{:S(2)}, u32[]{:S(2)}) %collective-permute-start.38) | collective-permute-done | bytes 262176 | tf_op jit(solution)/shard_map/ppermute | solution.py:658
  127.9 6.1 %collective-permute-done.40.refs_4_ = bf16[256,512]{1,0:T(8,128)(2,1)S(1)} collective-permute-done((bf16[256,512]{1,0:T(8,128)(2,1)S(1)}, bf16[256,512]{1,0:T(8,128)(2,1)S(1)}, u32[]{:S(2)}, u32[]{:S(2)}) %collective-permute-start.40) | collective-permute-done | bytes 262176 | tf_op jit(solution)/shard_map/ppermute | solution.py:658
  134.7 2.9 %collective-permute-start.54 = (bf16[8,256,256]{2,1,0:T(8,128)(2,1)S(1)}, bf16[8,256,256]{2,1,0:T(8,128)(2,1)S(1)}, u32[]{:S(2)}, u32[]{:S(2)}) collective-permute-start(bf16[8,256,256]{2,1,0:T(8,128)(2,1)S(1)} %constant_dynamic-update-slice_fusion.refs_14_.refs_18_.refs_22_.refs_26_.refs_30_.refs_34_.refs_38, ...), channel_id=1, source_target_pairs={{0,1},{1,0},{2,3},{3,2},{4,5},{5,4},{6,7},{7,6},{8,9},{9,8},{10,11... | collective-permute-start | bytes 3145736 | tf_op jit(solution)/shard_map/ppermute | solution.py:54
  140.1 5.2 %collective-permute-done.42.refs_8_ = bf16[256,512]{1,0:T(8,128)(2,1)S(1)} collective-permute-done((bf16[256,512]{1,0:T(8,128)(2,1)S(1)}, bf16[256,512]{1,0:T(8,128)(2,1)S(1)}, u32[]{:S(2)}, u32[]{:S(2)}) %collective-permute-start.42) | collective-permute-done | bytes 262176 | tf_op jit(solution)/shard_map/ppermute | solution.py:658
  146.0 4.4 %collective-permute-done.48.refs_9_ = bf16[256,512]{1,0:T(8,128)(2,1)S(1)} collective-permute-done((bf16[256,512]{1,0:T(8,128)(2,1)S(1)}, bf16[256,512]{1,0:T(8,128)(2,1)S(1)}, u32[]{:S(2)}, u32[]{:S(2)}) %collective-permute-start.48) | collective-permute-done | bytes 262176 | tf_op jit(solution)/shard_map/ppermute | solution.py:658
  151.1 4.7 %collective-permute-done.46.refs_12_ = bf16[256,512]{1,0:T(8,128)(2,1)S(1)} collective-permute-done((bf16[256,512]{1,0:T(8,128)(2,1)S(1)}, bf16[256,512]{1,0:T(8,128)(2,1)S(1)}, u32[]{:S(2)}, u32[]{:S(2)}) %collective-permute-start.46) | collective-permute-done | bytes 262176 | tf_op jit(solution)/shard_map/ppermute | solution.py:658
  156.4 4.4 %collective-permute-done.51.refs_13_ = bf16[256,512]{1,0:T(8,128)(2,1)S(1)} collective-permute-done((bf16[256,512]{1,0:T(8,128)(2,1)S(1)}, bf16[256,512]{1,0:T(8,128)(2,1)S(1)}, u32[]{:S(2)}, u32[]{:S(2)}) %collective-permute-start.51) | collective-permute-done | bytes 262176 | tf_op jit(solution)/shard_map/ppermute | solution.py:658
  162.7 4.0 %out_step.1.refs_4_ = f32[2,512,256]{2,1,0:T(8,128)S(1)} custom-call(s32[16]{0:T(128)S(1)} %concatenate.68.meta, bf16[256,512]{1,0:T(8,128)(2,1)S(1)} %get-tuple-element.197.refs_0_, bf16[256,512]{1,0:T(8,128)(2,1)S(1)} %get-tuple-element.199.refs_1_, bf16[256,512]{1,0:T(8,128)(2,1)S(1)} %collective-permute-done.41.refs_2_, ...), custom_call_target="tpu_custom_call" | custom-call | flops 1879048192 | bytes 9437184 | tf_op jit(solution)/shard_map/out_step/pallas_call | solution.py:439
  169.2 5.1 %collective-permute-start.57 = (bf16[8,256,256]{2,1,0:T(8,128)(2,1)S(1)}, bf16[8,256,256]{2,1,0:T(8,128)(2,1)S(1)}, u32[]{:S(2)}, u32[]{:S(2)}) collective-permute-start(bf16[8,256,256]{2,1,0:T(8,128)(2,1)S(1)} %collective-permute-done.55.refs_16_.refs_20_.refs_24_.refs_28_.refs_32_.refs_36_.refs_40_.refs_4_), channel_id=1, source_target_pairs={{0,1},{1,0},{2,3},{3,2},{4,5},{5,4},{6,7},{7,6},{8,9},{9,8},{10,11... | collective-permute-start | bytes 3145736 | tf_op jit(solution)/shard_map/ppermute | solution.py:54
  182.0 3.1 %collective-permute-done.58.refs_1_ = bf16[256,256]{1,0:T(8,128)(2,1)S(1)} collective-permute-done((bf16[256,256]{1,0:T(8,128)(2,1)S(1)}, bf16[256,256]{1,0:T(8,128)(2,1)S(1)}, u32[]{:S(2)}, u32[]{:S(2)}) %collective-permute-start.58) | collective-permute-done | bytes 131104 | tf_op jit(solution)/shard_map/ppermute | solution.py:808
  185.1 3.1 %collective-permute-done.60.refs_3_ = bf16[256,256]{1,0:T(8,128)(2,1)S(1)} collective-permute-done((bf16[256,256]{1,0:T(8,128)(2,1)S(1)}, bf16[256,256]{1,0:T(8,128)(2,1)S(1)}, u32[]{:S(2)}, u32[]{:S(2)}) %collective-permute-start.60) | collective-permute-done | bytes 131104 | tf_op jit(solution)/shard_map/ppermute | solution.py:808
  189.8 5.3 %collective-permute-done.61.refs_4_ = bf16[128,512]{1,0:T(8,128)(2,1)} collective-permute-done((bf16[128,512]{1,0:T(8,128)(2,1)S(1)}, bf16[128,512]{1,0:T(8,128)(2,1)}, u32[]{:S(2)}, u32[]{:S(2)}) %collective-permute-start.61) | collective-permute-done | bytes 131104 | tf_op jit(solution)/shard_map/ppermute | solution.py:658
  195.1 2.8 %collective-permute-done.65.refs_5_ = bf16[128,512]{1,0:T(8,128)(2,1)} collective-permute-done((bf16[128,512]{1,0:T(8,128)(2,1)S(1)}, bf16[128,512]{1,0:T(8,128)(2,1)}, u32[]{:S(2)}, u32[]{:S(2)}) %collective-permute-start.65) | collective-permute-done | bytes 131104 | tf_op jit(solution)/shard_map/ppermute | solution.py:658
  199.6 7.2 %collective-permute-done.63.refs_8_ = bf16[128,512]{1,0:T(8,128)(2,1)S(1)} collective-permute-done((bf16[128,512]{1,0:T(8,128)(2,1)}, bf16[128,512]{1,0:T(8,128)(2,1)S(1)}, u32[]{:S(2)}, u32[]{:S(2)}) %collective-permute-start.63) | collective-permute-done | bytes 131104 | tf_op jit(solution)/shard_map/ppermute | solution.py:658
  208.6 6.0 %collective-permute-done.67.refs_12_ = bf16[128,512]{1,0:T(8,128)(2,1)S(1)} collective-permute-done((bf16[128,512]{1,0:T(8,128)(2,1)S(1)}, bf16[128,512]{1,0:T(8,128)(2,1)S(1)}, u32[]{:S(2)}, u32[]{:S(2)}) %collective-permute-start.67) | collective-permute-done | bytes 131104 | tf_op jit(solution)/shard_map/ppermute | solution.py:658
  218.3 2.7 %collective-permute-done.74.refs_1_ = bf16[128,512]{1,0:T(8,128)(2,1)S(1)} collective-permute-done((bf16[128,512]{1,0:T(8,128)(2,1)S(1)}, bf16[128,512]{1,0:T(8,128)(2,1)S(1)}, u32[]{:S(2)}, u32[]{:S(2)}) %collective-permute-start.74) | collective-permute-done | bytes 131104 | tf_op jit(solution)/shard_map/ppermute | solution.py:658
  227.8 5.9 %collective-permute-start.79 = (f32[64,128]{1,0:T(8,128)S(1)}, f32[64,128]{1,0:T(8,128)S(1)}, u32[]{:S(2)}, u32[]{:S(2)}) collective-permute-start(f32[64,128]{1,0:T(8,128)S(1)} %fusion.25.own_a), channel_id=1, source_target_pairs={{0,1},{1,0},{2,3},{3,2},{4,5},{5,4},{6,7},{7,6},{8,9},{9,8},{10,11... | collective-permute-start | bytes 98312 | tf_op jit(solution)/shard_map/ppermute | solution.py:872
  (237 shorter events, 80.2 us)
Async XLA Ops:
  1.2 20.3 %collective-permute-start.8 = (bf16[4096,256]{1,0:T(8,128)(2,1)}, bf16[4096,256]{1,0:T(8,128)(2,1)}, u32[]{:S(2)}, u32[]{:S(2)}) collective-permute-start(bf16[4096,256]{1,0:T(8,128)(2,1)} %refs_13_.1), channel_id=1, source_target_pairs={{0,1},{1,0},{2,3},{3,2},{4,5},{5,4},{6,7},{7,6},{8,9},{9,8},{10,11... | collective-permute-start | bytes 6291464 | tf_op jit(solution)/shard_map/ppermute | solution.py:54
  19.3 13.9 %collective-permute-start.9 = (bf16[4,256,256]{2,1,0:T(8,128)(2,1)}, bf16[4,256,256]{2,1,0:T(8,128)(2,1)}, u32[]{:S(2)}, u32[]{:S(2)}) collective-permute-start(bf16[4,256,256]{2,1,0:T(8,128)(2,1)} %get-tuple-element.141), channel_id=1, source_target_pairs={{0,2},{2,0},{1,3},{3,1},{4,6},{6,4},{5,7},{7,5},{8,10},{10,8},{9,1... | collective-permute-start | bytes 1572872 | tf_op jit(solution)/shard_map/ppermute | solution.py:658
  19.7 62.2 %collective-permute-start.26 = (bf16[4096,256]{1,0:T(8,128)(2,1)S(1)}, bf16[4096,256]{1,0:T(8,128)(2,1)}, u32[]{:S(2)}, u32[]{:S(2)}) collective-permute-start(bf16[4096,256]{1,0:T(8,128)(2,1)S(1)} %copy-done.1), channel_id=1, source_target_pairs={{0,1},{1,0},{2,3},{3,2},{4,5},{5,4},{6,7},{7,6},{8,9},{9,8},{10,11... | collective-permute-start | bytes 6291464 | tf_op jit(solution)/shard_map/ppermute | solution.py:54
  35.5 9.9 %collective-permute-start.12 = (bf16[272,512]{1,0:T(8,128)(2,1)S(1)}, bf16[272,512]{1,0:T(8,128)(2,1)S(1)}, u32[]{:S(2)}, u32[]{:S(2)}) collective-permute-start(bf16[272,512]{1,0:T(8,128)(2,1)S(1)} %maximum_select_fusion.1.refs_0_), channel_id=1, source_target_pairs={{0,4},{4,8},{8,12},{12,0},{1,5},{5,9},{9,13},{13,1},{2,6},{6,10},{... | collective-permute-start | bytes 835592 | tf_op jit(solution)/shard_map/ppermute | solution.py:658
  37.3 13.8 %collective-permute-start.16 = (bf16[256,512]{1,0:T(8,128)(2,1)S(1)}, bf16[256,512]{1,0:T(8,128)(2,1)S(1)}, u32[]{:S(2)}, u32[]{:S(2)}) collective-permute-start(bf16[256,512]{1,0:T(8,128)(2,1)S(1)} %maximum_select_fusion.2.refs_1_), channel_id=1, source_target_pairs={{0,4},{4,8},{8,12},{12,0},{1,5},{5,9},{9,13},{13,1},{2,6},{6,10},{... | collective-permute-start | bytes 786440 | tf_op jit(solution)/shard_map/ppermute | solution.py:658
  37.4 13.7 %collective-permute-start.17 = (bf16[256,512]{1,0:T(8,128)(2,1)S(1)}, bf16[256,512]{1,0:T(8,128)(2,1)S(1)}, u32[]{:S(2)}, u32[]{:S(2)}) collective-permute-start(bf16[256,512]{1,0:T(8,128)(2,1)S(1)} %maximum_select_fusion.2.refs_1_), channel_id=1, source_target_pairs={{0,2},{2,0},{1,3},{3,1},{4,6},{6,4},{5,7},{7,5},{8,10},{10,8},{9,1... | collective-permute-start | bytes 786440 | tf_op jit(solution)/shard_map/ppermute | solution.py:658
  45.5 11.6 %collective-permute-start.14 = (bf16[272,512]{1,0:T(8,128)(2,1)S(1)}, bf16[272,512]{1,0:T(8,128)(2,1)S(1)}, u32[]{:S(2)}, u32[]{:S(2)}) collective-permute-start(bf16[272,512]{1,0:T(8,128)(2,1)S(1)} %collective-permute-done.12.refs_4_), channel_id=1, source_target_pairs={{0,4},{4,8},{8,12},{12,0},{1,5},{5,9},{9,13},{13,1},{2,6},{6,10},{... | collective-permute-start | bytes 835592 | tf_op jit(solution)/shard_map/ppermute | solution.py:658
  45.5 11.6 %collective-permute-start.15 = (bf16[272,512]{1,0:T(8,128)(2,1)S(1)}, bf16[272,512]{1,0:T(8,128)(2,1)S(1)}, u32[]{:S(2)}, u32[]{:S(2)}) collective-permute-start(bf16[272,512]{1,0:T(8,128)(2,1)S(1)} %collective-permute-done.12.refs_4_), channel_id=1, source_target_pairs={{0,2},{2,0},{1,3},{3,1},{4,6},{6,4},{5,7},{7,5},{8,10},{10,8},{9,1... | collective-permute-start | bytes 835592 | tf_op jit(solution)/shard_map/ppermute | solution.py:658
  51.1 11.6 %collective-permute-start.20 = (bf16[256,512]{1,0:T(8,128)(2,1)S(1)}, bf16[256,512]{1,0:T(8,128)(2,1)S(1)}, u32[]{:S(2)}, u32[]{:S(2)}) collective-permute-start(bf16[256,512]{1,0:T(8,128)(2,1)S(1)} %collective-permute-done.16.refs_5_), channel_id=1, source_target_pairs={{0,4},{4,8},{8,12},{12,0},{1,5},{5,9},{9,13},{13,1},{2,6},{6,10},{... | collective-permute-start | bytes 786440 | tf_op jit(solution)/shard_map/ppermute | solution.py:658
  51.1 11.6 %collective-permute-start.21 = (bf16[256,512]{1,0:T(8,128)(2,1)S(1)}, bf16[256,512]{1,0:T(8,128)(2,1)S(1)}, u32[]{:S(2)}, u32[]{:S(2)}) collective-permute-start(bf16[256,512]{1,0:T(8,128)(2,1)S(1)} %collective-permute-done.16.refs_5_), channel_id=1, source_target_pairs={{0,2},{2,0},{1,3},{3,1},{4,6},{6,4},{5,7},{7,5},{8,10},{10,8},{9,1... | collective-permute-start | bytes 786440 | tf_op jit(solution)/shard_map/ppermute | solution.py:658
  57.0 11.6 %collective-permute-start.18 = (bf16[272,512]{1,0:T(8,128)(2,1)S(1)}, bf16[272,512]{1,0:T(8,128)(2,1)S(1)}, u32[]{:S(2)}, u32[]{:S(2)}) collective-permute-start(bf16[272,512]{1,0:T(8,128)(2,1)S(1)} %collective-permute-done.14.refs_8_), channel_id=1, source_target_pairs={{0,4},{4,8},{8,12},{12,0},{1,5},{5,9},{9,13},{13,1},{2,6},{6,10},{... | collective-permute-start | bytes 835592 | tf_op jit(solution)/shard_map/ppermute | solution.py:658
  57.1 11.6 %collective-permute-start.19 = (bf16[272,512]{1,0:T(8,128)(2,1)S(1)}, bf16[272,512]{1,0:T(8,128)(2,1)S(1)}, u32[]{:S(2)}, u32[]{:S(2)}) collective-permute-start(bf16[272,512]{1,0:T(8,128)(2,1)S(1)} %collective-permute-done.14.refs_8_), channel_id=1, source_target_pairs={{0,2},{2,0},{1,3},{3,1},{4,6},{6,4},{5,7},{7,5},{8,10},{10,8},{9,1... | collective-permute-start | bytes 835592 | tf_op jit(solution)/shard_map/ppermute | solution.py:658
  62.7 11.6 %collective-permute-start.23 = (bf16[256,512]{1,0:T(8,128)(2,1)S(1)}, bf16[256,512]{1,0:T(8,128)(2,1)S(1)}, u32[]{:S(2)}, u32[]{:S(2)}) collective-permute-start(bf16[256,512]{1,0:T(8,128)(2,1)S(1)} %collective-permute-done.20.refs_9_), channel_id=1, source_target_pairs={{0,4},{4,8},{8,12},{12,0},{1,5},{5,9},{9,13},{13,1},{2,6},{6,10},{... | collective-permute-start | bytes 786440 | tf_op jit(solution)/shard_map/ppermute | solution.py:658
  62.7 11.6 %collective-permute-start.24 = (bf16[256,512]{1,0:T(8,128)(2,1)S(1)}, bf16[256,512]{1,0:T(8,128)(2,1)S(1)}, u32[]{:S(2)}, u32[]{:S(2)}) collective-permute-start(bf16[256,512]{1,0:T(8,128)(2,1)S(1)} %collective-permute-done.20.refs_9_), channel_id=1, source_target_pairs={{0,2},{2,0},{1,3},{3,1},{4,6},{6,4},{5,7},{7,5},{8,10},{10,8},{9,1... | collective-permute-start | bytes 786440 | tf_op jit(solution)/shard_map/ppermute | solution.py:658
  68.6 14.2 %collective-permute-start.22 = (bf16[272,512]{1,0:T(8,128)(2,1)S(1)}, bf16[272,512]{1,0:T(8,128)(2,1)S(1)}, u32[]{:S(2)}, u32[]{:S(2)}) collective-permute-start(bf16[272,512]{1,0:T(8,128)(2,1)S(1)} %collective-permute-done.18.refs_12_), channel_id=1, source_target_pairs={{0,2},{2,0},{1,3},{3,1},{4,6},{6,4},{5,7},{7,5},{8,10},{10,8},{9,1... | collective-permute-start | bytes 835592 | tf_op jit(solution)/shard_map/ppermute | solution.py:658
  91.1 13.7 %collective-permute-start.30 = (bf16[2,512,128]{2,1,0:T(8,128)(2,1)}, bf16[2,512,128]{2,1,0:T(8,128)(2,1)S(1)}, u32[]{:S(2)}, u32[]{:S(2)}) collective-permute-start(bf16[2,512,128]{2,1,0:T(8,128)(2,1)} %get-tuple-element.177), channel_id=1, source_target_pairs={{0,17},{1,16},{16,1},{17,0},{2,19},{3,18},{18,3},{19,2},{4,21},{5,... | collective-permute-start | bytes 786440 | tf_op jit(solution)/shard_map/ppermute | solution.py:808
  91.9 18.6 %collective-permute-start.32 = (bf16[2,512,128]{2,1,0:T(8,128)(2,1)}, bf16[2,512,128]{2,1,0:T(8,128)(2,1)S(1)}, u32[]{:S(2)}, u32[]{:S(2)}) collective-permute-start(bf16[2,512,128]{2,1,0:T(8,128)(2,1)} %get-tuple-element.187), channel_id=1, source_target_pairs={{0,1},{1,0},{2,3},{3,2},{4,5},{5,4},{6,7},{7,6},{8,9},{9,8},{10,11... | collective-permute-start | bytes 786440 | tf_op jit(solution)/shard_map/ppermute | solution.py:54
  92.6 18.8 %collective-permute-start.33 = (bf16[2,512,128]{2,1,0:T(8,128)(2,1)}, bf16[2,512,128]{2,1,0:T(8,128)(2,1)S(1)}, u32[]{:S(2)}, u32[]{:S(2)}) collective-permute-start(bf16[2,512,128]{2,1,0:T(8,128)(2,1)} %get-tuple-element.188.refs_2_), channel_id=1, source_target_pairs={{0,16},{1,17},{16,0},{17,1},{2,18},{3,19},{18,2},{19,3},{4,20},{5,... | collective-permute-start | bytes 786440 | tf_op jit(solution)/shard_map/ppermute | solution.py:808
  95.2 20.1 %collective-permute-start.34 = (bf16[2,512,128]{2,1,0:T(8,128)(2,1)S(1)}, bf16[2,512,128]{2,1,0:T(8,128)(2,1)S(1)}, u32[]{:S(2)}, u32[]{:S(2)}) collective-permute-start(bf16[2,512,128]{2,1,0:T(8,128)(2,1)S(1)} %copy-done.25), channel_id=1, source_target_pairs={{0,17},{1,16},{16,1},{17,0},{2,19},{3,18},{18,3},{19,2},{4,21},{5,... | collective-permute-start | bytes 786440 | tf_op jit(solution)/shard_map/ppermute | solution.py:808
  97.6 23.8 %collective-permute-start.39 = (bf16[2,256,256]{2,1,0:T(8,128)(2,1)S(1)}, bf16[2,256,256]{2,1,0:T(8,128)(2,1)S(1)}, u32[]{:S(2)}, u32[]{:S(2)}) collective-permute-start(bf16[2,256,256]{2,1,0:T(8,128)(2,1)S(1)} %pad_maximum_fusion.3), channel_id=1, source_target_pairs={{0,12},{4,0},{8,4},{12,8},{1,13},{5,1},{9,5},{13,9},{2,14},{6,2},{... | collective-permute-start | bytes 786440 | tf_op jit(solution)/shard_map/ppermute | solution.py:658
  104.8 19.9 %collective-permute-start.38 = (bf16[2,256,256]{2,1,0:T(8,128)(2,1)S(1)}, bf16[2,256,256]{2,1,0:T(8,128)(2,1)S(1)}, u32[]{:S(2)}, u32[]{:S(2)}) collective-permute-start(bf16[2,256,256]{2,1,0:T(8,128)(2,1)S(1)} %pad_maximum_fusion.2), channel_id=1, source_target_pairs={{0,8},{4,12},{8,0},{12,4},{1,9},{5,13},{9,1},{13,5},{2,10},{6,14},... | collective-permute-start | bytes 786440 | tf_op jit(solution)/shard_map/ppermute | solution.py:658
  110.5 14.3 %collective-permute-start.37 = (bf16[2,256,256]{2,1,0:T(8,128)(2,1)S(1)}, bf16[2,256,256]{2,1,0:T(8,128)(2,1)S(1)}, u32[]{:S(2)}, u32[]{:S(2)}) collective-permute-start(bf16[2,256,256]{2,1,0:T(8,128)(2,1)S(1)} %pad_maximum_fusion.1), channel_id=1, source_target_pairs={{0,4},{4,8},{8,12},{12,0},{1,5},{5,9},{9,13},{13,1},{2,6},{6,10},{... | collective-permute-start | bytes 786440 | tf_op jit(solution)/shard_map/ppermute | solution.py:658
  125.4 14.3 %collective-permute-start.44 = (bf16[256,512]{1,0:T(8,128)(2,1)S(1)}, bf16[256,512]{1,0:T(8,128)(2,1)S(1)}, u32[]{:S(2)}, u32[]{:S(2)}) collective-permute-start(bf16[256,512]{1,0:T(8,128)(2,1)S(1)} %get-tuple-element.199.refs_1_), channel_id=1, source_target_pairs={{0,4},{4,8},{8,12},{12,0},{1,5},{5,9},{9,13},{13,1},{2,6},{6,10},{... | collective-permute-start | bytes 786440 | tf_op jit(solution)/shard_map/ppermute | solution.py:658
  127.1 13.0 %collective-permute-start.45 = (bf16[256,512]{1,0:T(8,128)(2,1)S(1)}, bf16[256,512]{1,0:T(8,128)(2,1)S(1)}, u32[]{:S(2)}, u32[]{:S(2)}) collective-permute-start(bf16[256,512]{1,0:T(8,128)(2,1)S(1)} %get-tuple-element.199.refs_1_), channel_id=1, source_target_pairs={{0,2},{2,0},{1,3},{3,1},{4,6},{6,4},{5,7},{7,5},{8,10},{10,8},{9,1... | collective-permute-start | bytes 786440 | tf_op jit(solution)/shard_map/ppermute | solution.py:658
  134.1 11.2 %collective-permute-start.42 = (bf16[256,512]{1,0:T(8,128)(2,1)S(1)}, bf16[256,512]{1,0:T(8,128)(2,1)S(1)}, u32[]{:S(2)}, u32[]{:S(2)}) collective-permute-start(bf16[256,512]{1,0:T(8,128)(2,1)S(1)} %collective-permute-done.40.refs_4_), channel_id=1, source_target_pairs={{0,4},{4,8},{8,12},{12,0},{1,5},{5,9},{9,13},{13,1},{2,6},{6,10},{... | collective-permute-start | bytes 786440 | tf_op jit(solution)/shard_map/ppermute | solution.py:658
  134.1 11.9 %collective-permute-start.43 = (bf16[256,512]{1,0:T(8,128)(2,1)S(1)}, bf16[256,512]{1,0:T(8,128)(2,1)S(1)}, u32[]{:S(2)}, u32[]{:S(2)}) collective-permute-start(bf16[256,512]{1,0:T(8,128)(2,1)S(1)} %collective-permute-done.40.refs_4_), channel_id=1, source_target_pairs={{0,2},{2,0},{1,3},{3,1},{4,6},{6,4},{5,7},{7,5},{8,10},{10,8},{9,1... | collective-permute-start | bytes 786440 | tf_op jit(solution)/shard_map/ppermute | solution.py:658
  134.7 32.0 %collective-permute-start.54 = (bf16[8,256,256]{2,1,0:T(8,128)(2,1)S(1)}, bf16[8,256,256]{2,1,0:T(8,128)(2,1)S(1)}, u32[]{:S(2)}, u32[]{:S(2)}) collective-permute-start(bf16[8,256,256]{2,1,0:T(8,128)(2,1)S(1)} %constant_dynamic-update-slice_fusion.refs_14_.refs_18_.refs_22_.refs_26_.refs_30_.refs_34_.refs_38, ...), channel_id=1, source_target_pairs={{0,1},{1,0},{2,3},{3,2},{4,5},{5,4},{6,7},{7,6},{8,9},{9,8},{10,11... | collective-permute-start | bytes 3145736 | tf_op jit(solution)/shard_map/ppermute | solution.py:54
  139.7 28.1 %collective-permute-start.55 = (bf16[8,256,256]{2,1,0:T(8,128)(2,1)S(1)}, bf16[8,256,256]{2,1,0:T(8,128)(2,1)S(1)}, u32[]{:S(2)}, u32[]{:S(2)}) collective-permute-start(bf16[8,256,256]{2,1,0:T(8,128)(2,1)S(1)} %constant_dynamic-update-slice_fusion.refs_14_.refs_18_.refs_22_.refs_26_.refs_30_.refs_34_.refs_38, ...), channel_id=1, source_target_pairs={{0,16},{16,0},{1,17},{17,1},{2,18},{18,2},{3,19},{19,3},{4,20},{20... | collective-permute-start | bytes 3145736 | tf_op jit(solution)/shard_map/ppermute | solution.py:658
  140.1 10.3 %collective-permute-start.48 = (bf16[256,512]{1,0:T(8,128)(2,1)S(1)}, bf16[256,512]{1,0:T(8,128)(2,1)S(1)}, u32[]{:S(2)}, u32[]{:S(2)}) collective-permute-start(bf16[256,512]{1,0:T(8,128)(2,1)S(1)} %collective-permute-done.44.refs_5_), channel_id=1, source_target_pairs={{0,4},{4,8},{8,12},{12,0},{1,5},{5,9},{9,13},{13,1},{2,6},{6,10},{... | collective-permute-start | bytes 786440 | tf_op jit(solution)/shard_map/ppermute | solution.py:658
  146.0 9.8 %collective-permute-start.46 = (bf16[256,512]{1,0:T(8,128)(2,1)S(1)}, bf16[256,512]{1,0:T(8,128)(2,1)S(1)}, u32[]{:S(2)}, u32[]{:S(2)}) collective-permute-start(bf16[256,512]{1,0:T(8,128)(2,1)S(1)} %collective-permute-done.42.refs_8_), channel_id=1, source_target_pairs={{0,4},{4,8},{8,12},{12,0},{1,5},{5,9},{9,13},{13,1},{2,6},{6,10},{... | collective-permute-start | bytes 786440 | tf_op jit(solution)/shard_map/ppermute | solution.py:658
  151.1 9.8 %collective-permute-start.51 = (bf16[256,512]{1,0:T(8,128)(2,1)S(1)}, bf16[256,512]{1,0:T(8,128)(2,1)S(1)}, u32[]{:S(2)}, u32[]{:S(2)}) collective-permute-start(bf16[256,512]{1,0:T(8,128)(2,1)S(1)} %collective-permute-done.48.refs_9_), channel_id=1, source_target_pairs={{0,4},{4,8},{8,12},{12,0},{1,5},{5,9},{9,13},{13,1},{2,6},{6,10},{... | collective-permute-start | bytes 786440 | tf_op jit(solution)/shard_map/ppermute | solution.py:658
  169.2 9.9 %collective-permute-start.57 = (bf16[8,256,256]{2,1,0:T(8,128)(2,1)S(1)}, bf16[8,256,256]{2,1,0:T(8,128)(2,1)S(1)}, u32[]{:S(2)}, u32[]{:S(2)}) collective-permute-start(bf16[8,256,256]{2,1,0:T(8,128)(2,1)S(1)} %collective-permute-done.55.refs_16_.refs_20_.refs_24_.refs_28_.refs_32_.refs_36_.refs_40_.refs_4_), channel_id=1, source_target_pairs={{0,1},{1,0},{2,3},{3,2},{4,5},{5,4},{6,7},{7,6},{8,9},{9,8},{10,11... | collective-permute-start | bytes 3145736 | tf_op jit(solution)/shard_map/ppermute | solution.py:54
  (76 other events, 989.3 us)
